TPU v7x, 32 devices: a whole 2x2x4 slice. The times are simulated.
32 devices in a mesh: groups: 2 (over x), req: 2 (over core), tp: 8 (over z, y).
Axes of the slice: x: 2, y: 2, z: 4, core: 2. Of those that a mesh axis runs over, the one named last changes fastest.
Arguments:
- hidden_in: bfloat16 [1024, 8192], P(('groups', 'req', 'tp')), parts along dimension 0, may hold values from -6 to 6
- norm_gain: float32 [8192], replicated, may hold values from 0.5 to 1.5
- w_query: bfloat16 [8192, 8192], P(None, 'tp'), may hold values from -0.0625 to 0.0625
- w_keyval: bfloat16 [8192, 2048], P(None, 'tp'), may hold values from -0.15625 to 0.15625
- w_out: bfloat16 [8192, 8192], P('tp'), may hold values from -0.1875 to 0.1875
- pool_cache: bfloat16 [16, 2048, 2, 1024], P(('groups', 'req'), 'tp'), parts along dimension 0
- doc_slot: int32 [16], P(('groups', 'req')), parts along dimension 0, may hold values from 0 to 7, each once
- doc_blocks: int32 [4, 4], P(('groups', 'req')), parts along dimension 0, may hold values from 4 to 16, as said below
- sel_pos: int32 [4, 256], P(('groups', 'req')), parts along dimension 0, may hold values from 0 to 8191, as said below
Outputs:
- attn_out: bfloat16 [1024, 8192], P(('groups', 'req', 'tp')), parts along dimension 0
There are 2 independent parts, one for each index of `groups`. A program takes and returns all parts, laid end to end along the dimension named above; an argument that names none is the same for every part. Nothing has to cross between parts.
Inputs may be any that keep to these rules, and one draw needn't show every extreme that they name: `sel_pos`: each request's positions are distinct and ascending, below the total length of its documents, and include that total minus one. `doc_slot`: every slot of the pool is used by exactly one document. `doc_blocks`: request 0's documents fill their slots.
All inputs are finite; a program needn't handle non-finite values.
Results may differ from a plain program's by a relative error of at most 0.02.
The roundings to bfloat16 on the way count: a program that leaves them out, or rounds other values in their place, can miss the bound.
Values may be sent and summed in bfloat16 or wider, within the bound.
No kernel may reach another device: no remote copies, remote signals or barrier semaphores. Data moves between devices by JAX's collectives and lax.ppermute only.
A program may use at most 256 MiB of HBM per device.

v0:
```python
import math

import jax
import jax.numpy as jnp
from jax import lax
from jax.sharding import PartitionSpec as P

HEADS = 64
KVH = 8
HD = 128
DOCS = 4
BLOCK = 128
SEL = 256


EPSILON = 1e-05
ROPE_BASE = 500000.0
MASKED = -1e30


def rotate(values, positions):
    half_dim = values.shape[-1] // 2
    inverse = ROPE_BASE ** (-(jnp.arange(half_dim, dtype=jnp.float32) * (2.0 / values.shape[-1])))
    angles = positions.astype(jnp.float32)[:, None] * inverse[None, :]
    cosine = jnp.cos(angles)[:, None, :]
    sine_part = jnp.sin(angles)[:, None, :]
    front_half = values[..., :half_dim]
    back_half = values[..., half_dim:]
    return jnp.concatenate(
        [front_half * cosine - back_half * sine_part, back_half * cosine + front_half * sine_part],
        axis=-1,
    )


def cache_layout(lengths, first_token, token_count, selected):
    offsets = jnp.cumsum(lengths) - lengths
    slot_tokens = first_token + jnp.arange(token_count, dtype=jnp.int32)
    cache_pos = offsets[:, None] + slot_tokens[None, :]
    is_valid = slot_tokens[None, :] < lengths[:, None]
    replaced = jnp.any(cache_pos[:, :, None] == selected[None, None, :], axis=-1)
    return (cache_pos.reshape(-1), (is_valid & jnp.logical_not(replaced)).reshape(-1))


def per_device(
    hidden_in, norm_gain, w_query, w_keyval, w_out, pool_cache, doc_slot, doc_blocks, sel_pos
):
    tp_size = lax.axis_size("tp")
    my_index = lax.axis_index("tp")
    selected = sel_pos[0]
    lengths = doc_blocks[0] * BLOCK
    widened = hidden_in.astype(jnp.float32)
    normed = (
        widened
        * lax.rsqrt(jnp.mean(widened * widened, axis=-1, keepdims=True) + EPSILON)
        * norm_gain
    ).astype(jnp.bfloat16)
    query_cols = w_query.shape[1]
    heads_here = query_cols // HD
    group_size = HEADS // KVH
    scale = 1.0 / math.sqrt(HD)
    piece_rows = lax.all_gather(normed, "tp", axis=0, tiled=True)
    projected = jnp.concatenate(
        [
            jnp.dot(piece_rows, w_query, preferred_element_type=jnp.float32),
            jnp.dot(piece_rows, w_keyval, preferred_element_type=jnp.float32),
        ],
        axis=1,
    )
    queries = rotate(projected[:, :query_cols].reshape(SEL, heads_here, HD), selected).astype(
        jnp.bfloat16
    )
    fresh_kv = projected[:, query_cols:].astype(jnp.bfloat16)
    fetched = lax.all_gather(pool_cache, "req", axis=0, tiled=True)
    my_docs = jnp.take(fetched, doc_slot, axis=0)
    local_tokens = my_docs.shape[1]
    all_queries = lax.all_gather(queries, "tp", axis=1, tiled=True)
    fresh_rows = lax.all_to_all(fresh_kv, "tp", split_axis=0, concat_axis=1, tiled=True)
    row_count = SEL // tp_size
    my_selected = lax.dynamic_slice_in_dim(selected, my_index * row_count, row_count)
    new_keys = rotate(
        fresh_rows[:, : KVH * HD].reshape(row_count, KVH, HD).astype(jnp.float32), my_selected
    ).astype(jnp.bfloat16)
    new_vals = fresh_rows[:, KVH * HD :].reshape(row_count, KVH, HD)
    old_keys = my_docs[:, :, 0].reshape(DOCS * local_tokens, KVH, HD)
    old_vals = my_docs[:, :, 1].reshape(DOCS * local_tokens, KVH, HD)
    cache_pos, cache_live = cache_layout(lengths, my_index * local_tokens, local_tokens, selected)
    key_pos = jnp.concatenate([cache_pos, my_selected])
    key_live = jnp.concatenate([cache_live, jnp.ones((row_count,), dtype=bool)])
    allowed = key_live[None, :] & (key_pos[None, :] <= selected[:, None])
    all_keys = jnp.concatenate([old_keys, new_keys], axis=0)
    all_vals = jnp.concatenate([old_vals, new_vals], axis=0)
    grouped = all_queries.reshape(SEL, KVH, group_size, HD)
    scores = (
        jnp.einsum("qkgd,nkd->kgqn", grouped, all_keys, preferred_element_type=jnp.float32) * scale
    )
    scores = jnp.where(allowed[None, None], scores, MASKED)
    row_top = lax.pmax(jnp.max(scores, axis=-1).astype(jnp.bfloat16), "tp").astype(jnp.float32)
    weights = jnp.exp(scores - row_top[..., None])
    totals = jnp.sum(weights, axis=-1).reshape(HEADS, SEL).T
    summed = jnp.einsum(
        "kgqn,nkd->qkgd", weights.astype(jnp.bfloat16), all_vals, preferred_element_type=jnp.float32
    ).reshape(SEL, HEADS, HD)
    summed, totals = (
        lax.psum_scatter(summed.astype(jnp.bfloat16), "tp", scatter_dimension=1, tiled=True).astype(
            jnp.float32
        ),
        lax.psum_scatter(totals.astype(jnp.bfloat16), "tp", scatter_dimension=1, tiled=True).astype(
            jnp.float32
        ),
    )
    attention = (summed / totals[:, :, None]).astype(jnp.bfloat16).reshape(SEL, heads_here * HD)
    return lax.psum_scatter(
        jnp.dot(attention, w_out, preferred_element_type=jnp.float32).astype(jnp.bfloat16),
        "tp",
        scatter_dimension=0,
        tiled=True,
    )


def solution(mesh):
    placed = (
        P(("groups", "req", "tp"), None),
        P(),
        P(None, "tp"),
        P(None, "tp"),
        P("tp", None),
        P(("groups", "req"), "tp", None, None),
        P(("groups", "req")),
        P(("groups", "req"), None),
        P(("groups", "req"), None),
    )
    return jax.shard_map(
        per_device,
        mesh=mesh,
        in_specs=placed,
        out_specs=P(("groups", "req", "tp"), None),
        check_vma=False,
    )
```

profile of v0, /device:TPU:0, one launch (start us, length us, event | category | flops | bytes accessed | tf_op | source)
XLA Modules:
  0.0 521.9 jit_solution(9844657630753365439)
XLA Ops:
  6.5 0.0 all-gather.6.cloned.1.call-start
  6.5 1.2 fusion.14
  7.8 2.0 fusion.16
  9.8 0.0 all-gather.6.cloned.1.call-update
  9.9 0.0 all-gather.4.cloned.1.call-start
  9.9 5.4 %copy.26 = bf16[4,256,2,1024]{3,1,2,0:T(8,128)(2,1)} copy(bf16[4,256,2,1024]{3,2,1,0:T(2,128)(2,1)} %param.14) | data formatting | bytes 8388608 | tf_op args[5]
  15.3 0.0 copy-start.1
  15.4 0.0 all-gather.4.cloned.1.call-update
  15.4 0.0 all-gather.8.cloned.1.call-start
  15.4 0.6 copy-done.1
  16.0 0.5 multiply_cosine_fusion
  16.6 69.5 %all-gather.6.cloned.1.call-done = bf16[256,8192]{1,0:T(8,128)(2,1)} async-done(((bf16[32,8192]{1,0:T(8,128)(2,1)}), bf16[256,8192]{1,0:T(8,128)(2,1)}) %all-gather.6.cloned.1.call-update) | async-done | bytes 4194320 | tf_op jit(solution)/shard_map/all_gather | solution.py:61
  86.1 10.0 %convolution_bitcast_fusion = f32[32,8,8,128]{3,1,2,0:T(8,128)S(1)} fusion(bf16[256,8192]{1,0:T(8,128)(2,1)} %all-gather.6.cloned.1.call-done, bf16[8192,1024]{1,0:T(8,128)(2,1)} %param.11), kind=kOutput, calls=%fused_computation.18 | convolution fusion | flops 4294967296 | bytes 22020096 | tf_op jit(solution)/shard_map/dot_general | solution.py:64
  96.1 0.0 copy-start.2
  96.1 0.0 copy-start.3
  96.1 0.2 copy.44
  96.4 0.5 subtract_convert_fusion
  96.9 1.1 pad_maximum_fusion
  97.9 0.0 all-gather.8.cloned.1.call-update
  98.0 0.0 copy-done.2
  98.0 0.2 reduce-window.8
  98.2 0.1 broadcast_add_fusion
  98.3 0.4 compare_reduce_fusion
  98.6 0.1 not_and_fusion
  98.8 0.1 fusion.20
  98.8 0.0 copy-done.3
  98.9 0.8 compare_and_fusion
  99.7 6.3 %convolution_convert_fusion.1 = bf16[256,256]{1,0:T(8,128)(2,1)} fusion(bf16[256,8192]{1,0:T(8,128)(2,1)} %all-gather.6.cloned.1.call-done, bf16[8192,256]{1,0:T(8,128)(2,1)} %param.12), kind=kOutput, calls=%fused_computation.21 | convolution fusion | flops 1073807360 | bytes 8519680 | tf_op jit(solution)/shard_map/dot_general | solution.py:65
  106.0 3.4 all-to-all-start
  109.4 0.2 reduce-scatter.6.cloned.1.call-start
  109.6 0.1 multiply_cosine_fusion.1
  109.8 6.9 %all-to-all-done = bf16[8,32,256]{2,1,0:T(8,128)(2,1)S(1)} async-done(((bf16[8,32,256]{2,1,0:T(8,128)(2,1)}), bf16[8,32,256]{2,1,0:T(8,128)(2,1)S(1)}, u32[]{:S(2)}, u32[]{:S(2)}) %all-to-all-start) | async-done | bytes 131104 | tf_op jit(solution)/shard_map/all_to_all | solution.py:77
  116.7 0.1 fusion.22
  116.8 0.1 subtract_convert_fusion.1
  116.9 0.0 all-gather.4.cloned.1.call-done
  116.9 6.3 %gather_fusion = bf16[4,256,2,1024]{3,1,2,0:T(8,128)(2,1)} fusion(bf16[8,256,2,1024]{3,1,2,0:T(8,128)(2,1)} %all-gather.4.cloned.1.call-done, s32[1024]{0:T(1024)S(1)} %pad_clamp_fusion), kind=kCustom, calls=%fused_computation | custom fusion | bytes 8388624 | tf_op jit(solution)/shard_map/jit(_take)/gather | solution.py:74
  123.3 2.7 broadcast_select_fusion
  125.9 0.4 fusion.21
  126.4 0.6 copy.40
  127.0 1.7 copy.28
  128.7 0.6 copy.42
  129.3 1.7 copy.32
  131.0 53.1 %all-gather.8.cloned.1.call-done = bf16[256,64,128]{2,1,0:T(8,128)(2,1)} async-done(((bf16[256,8,128]{2,1,0:T(8,128)(2,1)}), bf16[256,64,128]{2,1,0:T(8,128)(2,1)}) %all-gather.8.cloned.1.call-update) | async-done | bytes 4194320 | tf_op jit(solution)/shard_map/all_gather | solution.py:76
  184.1 4.9 copy.33
  189.0 26.2 %fusion.23 = (bf16[8,8,256]{2,1,0:T(8,128)(2,1)S(1)}, f32[8,8,256,1056]{2,3,1,0:T(8,128)}) fusion(bf16[256,8,8,128]{3,0,2,1:T(8,128)(2,1)S(1)} %bitcast.72, bf16[32,8,64]{2,0,1:T(8,128)(2,1)S(1)} %get-tuple-element.12, bf16[32,8,64]{2,0,1:T(8,128)(2,1)S(1)} %get-tuple-element.11, bf16[1024,8,128]{2,0,1:T(8,128)(2,1)} %copy.32, ...), kind=kOutput, calls=%fused_computation.60 | convolution fusion | flops 4487561216 | bytes 75866112 | tf_op jit(solution)/shard_map/qkgd,nkd->kgqn/dot_general | solution.py:94
  215.1 34.3 %pmax.7 = bf16[8,8,256]{2,1,0:T(8,128)(2,1)S(1)} all-reduce(bf16[8,8,256]{2,1,0:T(8,128)(2,1)S(1)} %get-tuple-element.25), channel_id=1, replica_groups=mesh['groups'=2,'req'=2,'tp'=8] {'tp'}, use_global_device_ids=true, to_apply=%region_4.5 | all-reduce | flops 16384 | bytes 65536 | tf_op jit(solution)/shard_map/pmax | solution.py:97
  249.5 0.0 copy-start
  249.5 22.4 %fusion = bf16[8,8,256]{2,1,0:T(8,128)(2,1)} fusion(f32[8,8,256,1056]{2,3,1,0:T(8,128)} %get-tuple-element.26, f32[8,8,256]{2,1,0:T(8,128)S(1)} %convert_element_type.78), kind=kLoop, calls=%fused_computation.3 | loop fusion | flops 34586624 | bytes 69304320 | tf_op jit(solution)/shard_map/reduce_sum | solution.py:99
  271.8 0.0 reduce-scatter.6.cloned.1.call-update
  271.8 0.3 reduce-scatter.4.cloned.1.call-start
  272.1 0.0 copy-done
  272.1 26.8 %fusion.5 = bf16[8,128,8,256]{3,1,2,0:T(8,128)(2,1)} fusion(f32[8,8,256,1056]{2,3,1,0:T(8,128)} %get-tuple-element.26, f32[8,8,256]{2,1,0:T(8,128)S(1)} %convert_element_type.78, bf16[32,8,128]{2,0,1:T(8,128)(2,1)S(1)} %bitcast.82, bf16[1024,8,128]{2,0,1:T(8,128)(2,1)S(1)} %copy-done), kind=kOutput, calls=%fused_computation.9 | convolution fusion | flops 4470210560 | bytes 75628544 | tf_op jit(solution)/shard_map/kgqn,nkd->qkgd/dot_general | solution.py:100
  298.9 0.0 reduce-scatter.4.cloned.1.call-update
  298.9 0.0 reduce-scatter.8.cloned.1.call-start
  299.0 23.8 %reduce-scatter.6.cloned.1.call-done = bf16[256,8]{0,1:T(8,128)(2,1)} async-done(((bf16[256,64]{0,1:T(8,128)(2,1)}), bf16[256,8]{0,1:T(8,128)(2,1)}) %reduce-scatter.6.cloned.1.call-update) | async-done | bytes 4112 | tf_op jit(solution)/shard_map/reduce_scatter | solution.py:107
  322.8 0.7 convert_element_type.87
  323.5 89.9 %reduce-scatter.4.cloned.1.call-done = bf16[256,8,128]{0,2,1:T(8,128)(2,1)} async-done(((bf16[256,64,128]{0,2,1:T(8,128)(2,1)}), bf16[256,8,128]{0,2,1:T(8,128)(2,1)}) %reduce-scatter.4.cloned.1.call-update) | async-done | bytes 524304 | tf_op jit(solution)/shard_map/reduce_scatter | solution.py:104
  413.4 1.1 divide_convert_fusion
  414.5 12.1 %convolution_convert_fusion = bf16[256,8192]{1,0:T(8,128)(2,1)} fusion(bf16[256,1024]{0,1:T(8,128)(2,1)S(1)} %bitcast.78, bf16[1024,8192]{1,0:T(8,128)(2,1)} %param.13), kind=kOutput, calls=%fused_computation.7 | convolution fusion | flops 4297064448 | bytes 21495808 | tf_op jit(solution)/shard_map/dot_general | solution.py:113
  426.6 0.0 reduce-scatter.8.cloned.1.call-update
  426.6 88.4 %reduce-scatter.8.cloned.1.call-done = bf16[32,8192]{1,0:T(8,128)(2,1)} async-done(((bf16[256,8192]{1,0:T(8,128)(2,1)}), bf16[32,8192]{1,0:T(8,128)(2,1)}) %reduce-scatter.8.cloned.1.call-update) | async-done | bytes 524304 | tf_op jit(solution)/shard_map/reduce_scatter | solution.py:112
  (18 shorter events, 0.2 us)
Async XLA Ops:
  6.5 79.6 %all-gather.6.cloned.1.call-start = ((), (), s32[]{:S(2)}) async-start(), calls=%async_computation.5 | async-start | bytes 4718592 | tf_op jit(solution)/shard_map/all_gather | solution.py:61
  9.9 107.1 %all-gather.4.cloned.1.call-start = ((), (), s32[]{:S(2)}) async-start(), calls=%async_computation.4 | async-start | bytes 12582912 | tf_op jit(solution)/shard_map/all_gather | solution.py:73
  15.3 0.7 copy-start.1
  15.4 168.7 %all-gather.8.cloned.1.call-start = ((), (), s32[]{:S(2)}) async-start(), calls=%async_computation.6 | async-start | bytes 4718592 | tf_op jit(solution)/shard_map/all_gather | solution.py:76
  96.1 1.9 copy-start.2
  96.1 2.7 copy-start.3
  106.0 10.7 %all-to-all-start = ((bf16[8,32,256]{2,1,0:T(8,128)(2,1)}), bf16[8,32,256]{2,1,0:T(8,128)(2,1)S(1)}, u32[]{:S(2)}, u32[]{:S(2)}) async-start(bf16[8,32,256]{2,1,0:T(8,128)(2,1)} %bitcast), calls=%async_computation | async-start | bytes 262144 | tf_op jit(solution)/shard_map/all_to_all | solution.py:77
  109.4 213.4 %reduce-scatter.6.cloned.1.call-start = ((), (), s32[]{:S(2)}) async-start(), calls=%async_computation.8 | async-start | bytes 36864 | tf_op jit(solution)/shard_map/reduce_scatter | solution.py:107
  249.5 22.7 %copy-start = (bf16[1024,8,128]{2,0,1:T(8,128)(2,1)S(1)}, bf16[1024,8,128]{2,0,1:T(8,128)(2,1)}, u32[]{:S(2)}) copy-start(bf16[1024,8,128]{2,0,1:T(8,128)(2,1)} %copy.28) | copy-start | bytes 6291460
  271.8 141.5 %reduce-scatter.4.cloned.1.call-start = ((), (), s32[]{:S(2)}) async-start(), calls=%async_computation.7 | async-start | bytes 4718592 | tf_op jit(solution)/shard_map/reduce_scatter | solution.py:104
  298.9 216.1 %reduce-scatter.8.cloned.1.call-start = ((), (), s32[]{:S(2)}) async-start(), calls=%async_computation.9 | async-start | bytes 4718592 | tf_op jit(solution)/shard_map/reduce_scatter | solution.py:112
Sparse Core Ops, SparseCore 0:
  10.0 76.0 all-gather.5
  87.6 18.1 all-gather.3
  107.8 76.1 all-gather.7
  272.0 50.7 reduce-scatter.5
  326.2 87.0 reduce-scatter.3
  426.7 88.2 reduce-scatter.7
where the time goes:
time: 522 us
  waiting for transfers between devices  332 us (64%)
  matrix products  81.3 us (16%)
  blocking collectives  34.3 us (7%)
  other arithmetic  34.1 us (7%)
  local copies, waits for them, and re-layouts  22.7 us (4%)
  between operations  13.7 us (3%)
    reduce_scatter x1, waiting for transfers between devices, per_device(): lax.psum_scatter(summed.astype(jnp.bfloat16), 'tp', scatter_dimension=1,...  89.9 us
    reduce_scatter x1, waiting for transfers between devices, per_device(): lax.psum_scatter(jnp.dot(attention, w_out, preferred_element_type=jnp.flo...  88.4 us
    all_gather x1, waiting for transfers between devices, per_device(): piece_rows = lax.all_gather(normed, 'tp', axis=0, tiled=True)  69.5 us
    all_gather x1, waiting for transfers between devices, per_device(): all_queries = lax.all_gather(queries, 'tp', axis=1, tiled=True)  53.1 us
    pmax x1, blocking collectives, per_device(): lax.pmax(jnp.max(scores, axis=-1).astype(jnp.bfloat16), 'tp')  34.3 us
    dot_general x1, matrix products, per_device(): jnp.einsum('kgqn,nkd->qkgd', weights.astype(jnp.bfloat16), all_vals, pref...  26.8 us
    dot_general x1, matrix products, per_device(): jnp.einsum('qkgd,nkd->kgqn', grouped, all_keys, preferred_element_type=jn...  26.2 us
    reduce_scatter x1, waiting for transfers between devices, per_device(): lax.psum_scatter(totals.astype(jnp.bfloat16), 'tp', scatter_dimension=1,...  23.8 us
  transfers between devices with their start and end apart: 7, of which 6 were waited for; matrix products, arithmetic and copies ran while one was open for 13% of the time, Pallas kernels for 0%

commit v1 on v0

v1 whole, which is shorter than its diff:
```python
import functools
import math

import jax
import jax.numpy as jnp
from jax import lax
from jax.experimental import pallas as pl
from jax.experimental.pallas import tpu as pltpu
from jax.sharding import PartitionSpec as P

HEADS = 64
KVH = 8
HD = 128
DOCS = 4
BLOCK = 128
SEL = 256


EPSILON = 1e-05
ROPE_BASE = 500000.0
MASKED = -1e30
FAR = 1 << 30
GATHER_CHUNKS = 2
REDUCE_CHUNKS = 4
TILE_Q = 64
KEY_CHUNKS = 2
VMEM_BYTES = 40 * 1024 * 1024


def rotation_tables(positions):
    half_dim = HD // 2
    inverse = ROPE_BASE ** (-(jnp.arange(half_dim, dtype=jnp.float32) * (2.0 / HD)))
    angles = positions.astype(jnp.float32)[:, None] * inverse[None, :]
    cosine = jnp.cos(angles)
    sine_part = jnp.sin(angles)
    return (
        jnp.concatenate([cosine, cosine], axis=-1),
        jnp.concatenate([-sine_part, sine_part], axis=-1),
    )


def rotate(values, cosine, sine_part):
    swapped = jnp.concatenate([values[:, HD // 2 :], values[:, : HD // 2]], axis=-1)
    return values * cosine + swapped * sine_part


def project_kernel(n_blocks, has_prev, *refs):
    blocks = refs[:n_blocks]
    wq_ref, wkv_ref = refs[n_blocks : n_blocks + 2]
    rest = refs[n_blocks + 2 :]
    if has_prev:
        prev_q, prev_kv = rest[:2]
        rest = rest[2:]
    out_q, out_kv, total_q, total_kv = rest
    step = pl.program_id(0)

    @pl.when(step == 0)
    def _():
        if has_prev:
            total_q[...] = prev_q[...]
            total_kv[...] = prev_kv[...]
        else:
            total_q[...] = jnp.zeros_like(total_q)
            total_kv[...] = jnp.zeros_like(total_kv)

    rows = jnp.concatenate([b[...] for b in blocks], axis=0) if n_blocks > 1 else blocks[0][...]
    total_q[...] += jnp.dot(rows, wq_ref[...], preferred_element_type=jnp.float32)
    total_kv[...] += jnp.dot(rows, wkv_ref[...], preferred_element_type=jnp.float32)

    @pl.when(step == pl.num_programs(0) - 1)
    def _():
        out_q[...] = total_q[...]
        out_kv[...] = total_kv[...].astype(out_kv.dtype)


def project(blocks, w_query, w_keyval, prev, chunk, last):
    depth = blocks[0].shape[1]
    tile = min(1024, depth)
    steps = depth // tile
    q_cols, kv_cols = w_query.shape[1], w_keyval.shape[1]
    whole = lambda k: (0, 0)
    specs = [pl.BlockSpec((b.shape[0], tile), lambda k: (0, k)) for b in blocks]
    specs += [
        pl.BlockSpec((tile, q_cols), lambda k: (chunk * steps + k, 0)),
        pl.BlockSpec((tile, kv_cols), lambda k: (chunk * steps + k, 0)),
    ]
    operands = list(blocks) + [w_query, w_keyval]
    if prev is not None:
        specs += [pl.BlockSpec((SEL, q_cols), whole), pl.BlockSpec((SEL, kv_cols), whole)]
        operands += list(prev)
    return pl.pallas_call(
        functools.partial(project_kernel, len(blocks), prev is not None),
        grid=(steps,),
        in_specs=specs,
        out_specs=[pl.BlockSpec((SEL, q_cols), whole), pl.BlockSpec((SEL, kv_cols), whole)],
        out_shape=[
            jax.ShapeDtypeStruct((SEL, q_cols), jnp.float32),
            jax.ShapeDtypeStruct((SEL, kv_cols), jnp.bfloat16 if last else jnp.float32),
        ],
        scratch_shapes=[
            pltpu.VMEM((SEL, q_cols), jnp.float32),
            pltpu.VMEM((SEL, kv_cols), jnp.float32),
        ],
        compiler_params=pltpu.CompilerParams(vmem_limit_bytes=VMEM_BYTES),
        cost_estimate=pl.CostEstimate(
            flops=2 * SEL * depth * (q_cols + kv_cols),
            bytes_accessed=2 * depth * (q_cols + kv_cols + SEL) + 8 * SEL * (q_cols + kv_cols),
            transcendentals=0,
        ),
        name="project",
    )(*operands)


def select_kernel(n_dest, n_src, place_ref, slot_ref, head_ref, *refs):
    sources = refs[:n_src]
    outs = refs[n_src : n_src + n_dest]
    sems = refs[n_src + n_dest]
    for doc in range(DOCS):
        for src in range(n_src):

            @pl.when(place_ref[doc] == src)
            def _():
                for dest in range(n_dest):
                    pltpu.make_async_copy(
                        sources[src].at[head_ref[dest], :, slot_ref[doc]],
                        outs[dest].at[:, doc],
                        sems.at[dest, doc],
                    ).start()

    for dest in range(n_dest):
        for doc in range(DOCS):
            pltpu.make_async_copy(
                sources[0].at[0, :, 0], outs[dest].at[:, doc], sems.at[dest, doc]
            ).wait()


def select_docs(sources, place, slot, heads, n_dest):
    tokens = sources[0].shape[3]
    shape = (2, DOCS, tokens, HD)
    smem = pl.BlockSpec(memory_space=pltpu.SMEM)
    anywhere = pl.BlockSpec(memory_space=pl.ANY)
    return pl.pallas_call(
        functools.partial(select_kernel, n_dest, len(sources)),
        in_specs=[smem] * 3 + [anywhere] * len(sources),
        out_specs=[anywhere] * n_dest,
        out_shape=[jax.ShapeDtypeStruct(shape, jnp.bfloat16)] * n_dest,
        scratch_shapes=[pltpu.SemaphoreType.DMA((n_dest, DOCS))],
        cost_estimate=pl.CostEstimate(
            flops=0, bytes_accessed=4 * n_dest * math.prod(shape), transcendentals=0
        ),
        name="select_docs",
    )(place, slot, heads, *sources)


def attend_kernel(
    n_chunks,
    tokens,
    heads_here,
    qmax_ref,
    first_ref,
    q_ref,
    qcos_ref,
    qsin_ref,
    qpos_ref,
    kpos_ref,
    newk_ref,
    newv_ref,
    ncos_ref,
    nsin_ref,
    npos_ref,
    *refs,
):
    chunks = refs[:n_chunks]
    out_ref = refs[n_chunks]
    stored, new_key, q_tile, top, total, summed, sems = refs[n_chunks + 1 :]
    rows = heads_here * TILE_Q
    key_block = KEY_CHUNKS * tokens
    n_blocks = n_chunks // KEY_CHUNKS
    scale = math.log2(math.e) / math.sqrt(HD)

    def fill(chunk):
        return pltpu.make_async_copy(
            chunks[chunk], stored.at[:, :, pl.ds(chunk * tokens, tokens)], sems.at[chunk]
        )

    for chunk in range(n_chunks):
        fill(chunk).start()
    new_key[...] = rotate(newk_ref[...].astype(jnp.float32), ncos_ref[...], nsin_ref[...]).astype(
        jnp.bfloat16
    )

    def visit(keys, values, key_pos, token_pos):
        scores = lax.dot_general(
            q_tile[...], keys, (((1,), (1,)), ((), ())), preferred_element_type=jnp.float32
        )
        allowed = key_pos <= token_pos
        scores = jnp.where(
            allowed[None], scores.reshape(heads_here, TILE_Q, keys.shape[0]) * scale, MASKED
        ).reshape(rows, keys.shape[0])
        old_top = top[:, :1]
        new_top = jnp.maximum(old_top, jnp.max(scores, axis=-1, keepdims=True))
        weights = jnp.exp2(scores - new_top)
        shrink = jnp.exp2(old_top - new_top)
        total[...] = jnp.broadcast_to(
            total[:, :1] * shrink + jnp.sum(weights, axis=-1, keepdims=True), total.shape
        )
        summed[...] = summed[...] * shrink + jnp.dot(
            weights.astype(jnp.bfloat16), values, preferred_element_type=jnp.float32
        )
        top[...] = jnp.broadcast_to(new_top, top.shape)

    for chunk in range(n_chunks):
        fill(chunk).wait()

    @pl.loop(0, SEL // TILE_Q)
    def _(tile):
        start = pl.multiple_of(tile * TILE_Q, TILE_Q)
        here = pl.ds(start, TILE_Q)
        for head in range(heads_here):
            q_tile[head * TILE_Q : (head + 1) * TILE_Q, :] = rotate(
                q_ref[here, head * HD : (head + 1) * HD], qcos_ref[here, :], qsin_ref[here, :]
            ).astype(jnp.bfloat16)
        token_pos = qpos_ref[here, :][:, :1]
        top[...] = jnp.full_like(top, MASKED)
        total[...] = jnp.zeros_like(total)
        summed[...] = jnp.zeros_like(summed)
        visit(new_key[...], newv_ref[...], npos_ref[...], token_pos)

        @pl.loop(0, DOCS * n_blocks)
        def _(index):
            doc = index // n_blocks
            block = index % n_blocks

            @pl.when(first_ref[index] <= qmax_ref[tile])
            def _():
                span = pl.ds(pl.multiple_of(block * key_block, key_block), key_block)
                visit(
                    stored[0, doc, span, :],
                    stored[1, doc, span, :],
                    kpos_ref[pl.ds(index, 1), :],
                    token_pos,
                )

        for head in range(heads_here):
            part = slice(head * TILE_Q, (head + 1) * TILE_Q)
            out_ref[here, head * HD : (head + 1) * HD] = (
                summed[part, :] / total[part, :]
            ).astype(jnp.bfloat16)


def attend(chunks, q_raw, q_pos, key_pos, first_pos, new_k, new_v, selected):
    n_chunks = len(chunks)
    tokens = chunks[0].shape[2]
    heads_here = q_raw.shape[1] // HD
    rows = heads_here * TILE_Q
    q_cos, q_sin = rotation_tables(q_pos)
    n_cos, n_sin = rotation_tables(selected)
    q_max = jnp.max(q_pos.reshape(SEL // TILE_Q, TILE_Q), axis=1)
    smem = pl.BlockSpec(memory_space=pltpu.SMEM)
    vmem = pl.BlockSpec(memory_space=pltpu.VMEM)
    anywhere = pl.BlockSpec(memory_space=pl.ANY)
    pairs = HEADS // KVH * SEL * (DOCS * n_chunks * tokens + SEL) * heads_here // (HEADS // KVH)
    return pl.pallas_call(
        functools.partial(attend_kernel, n_chunks, tokens, heads_here),
        in_specs=[smem] * 2 + [vmem] * 10 + [anywhere] * n_chunks,
        out_specs=vmem,
        out_shape=jax.ShapeDtypeStruct((SEL, heads_here * HD), jnp.bfloat16),
        scratch_shapes=[
            pltpu.VMEM((2, DOCS, n_chunks * tokens, HD), jnp.bfloat16),
            pltpu.VMEM((SEL, HD), jnp.bfloat16),
            pltpu.VMEM((rows, HD), jnp.bfloat16),
            pltpu.VMEM((rows, HD), jnp.float32),
            pltpu.VMEM((rows, HD), jnp.float32),
            pltpu.VMEM((rows, HD), jnp.float32),
            pltpu.SemaphoreType.DMA((n_chunks,)),
        ],
        compiler_params=pltpu.CompilerParams(vmem_limit_bytes=VMEM_BYTES),
        cost_estimate=pl.CostEstimate(
            flops=4 * pairs * HD,
            bytes_accessed=4 * DOCS * n_chunks * tokens * HD,
            transcendentals=pairs,
        ),
        name="attend",
    )(
        q_max,
        first_pos,
        q_raw,
        q_cos,
        q_sin,
        jnp.broadcast_to(q_pos[:, None], (SEL, HD)),
        key_pos,
        new_k,
        new_v,
        n_cos,
        n_sin,
        selected[None, :],
        *chunks,
    )


def out_kernel(rows, x_ref, w_ref, own_ref, other_ref):
    product = jnp.dot(x_ref[...], w_ref[...], preferred_element_type=jnp.float32)
    cols = product.shape[1]
    split = product.reshape(SEL // (2 * rows), 2, rows, cols)
    own_ref[...] = split[:, 0].reshape(SEL // 2, cols)
    other_ref[...] = split[:, 1].reshape(SEL // 2, cols).astype(jnp.bfloat16)


def project_out(attention, w_out, chunk, n_chunks, rows):
    depth = w_out.shape[0]
    width = w_out.shape[1] // n_chunks
    tile = min(512, width)
    steps = width // tile
    return pl.pallas_call(
        functools.partial(out_kernel, rows),
        grid=(steps,),
        in_specs=[
            pl.BlockSpec((SEL, depth), lambda n: (0, 0)),
            pl.BlockSpec((depth, tile), lambda n: (0, chunk * steps + n)),
        ],
        out_specs=[
            pl.BlockSpec((SEL // 2, tile), lambda n: (0, n)),
            pl.BlockSpec((SEL // 2, tile), lambda n: (0, n)),
        ],
        out_shape=[
            jax.ShapeDtypeStruct((SEL // 2, width), jnp.float32),
            jax.ShapeDtypeStruct((SEL // 2, width), jnp.bfloat16),
        ],
        compiler_params=pltpu.CompilerParams(vmem_limit_bytes=VMEM_BYTES),
        cost_estimate=pl.CostEstimate(
            flops=2 * SEL * depth * width,
            bytes_accessed=2 * depth * (width + SEL) + 3 * SEL * width,
            transcendentals=0,
        ),
        name="project_out",
    )(attention, w_out)


def per_device(
    hidden_in, norm_gain, w_query, w_keyval, w_out, pool_cache, doc_slot, doc_blocks, sel_pos
):
    tp_size = lax.axis_size("tp")
    req_size = lax.axis_size("req")
    me = lax.axis_index("tp")
    ring = tp_size // 2
    my_z, my_y = me // 2, me % 2
    rows = hidden_in.shape[0]
    width = hidden_in.shape[1]
    tokens = pool_cache.shape[1]
    slots = pool_cache.shape[0]
    selected = sel_pos[0]
    lengths = doc_blocks[0] * BLOCK
    up = [(((z + 1) % ring) * 2 + y, z * 2 + y) for z in range(ring) for y in range(2)]
    down = [(z * 2 + y, ((z + 1) % ring) * 2 + y) for z in range(ring) for y in range(2)]
    across = [(i, i ^ 1) for i in range(tp_size)]

    widened = hidden_in.astype(jnp.float32)
    normed = (
        widened
        * lax.rsqrt(jnp.mean(widened * widened, axis=-1, keepdims=True) + EPSILON)
        * norm_gain
    ).astype(jnp.bfloat16)

    part = width // GATHER_CHUNKS
    prev = None
    for chunk in range(GATHER_CHUNKS):
        held = normed[:, chunk * part : (chunk + 1) * part]
        blocks = []
        for step in range(ring):
            blocks += [held, lax.ppermute(held, "tp", across)]
            if step + 1 < ring:
                held = lax.ppermute(held, "tp", up)
        if rows % 16:
            blocks = [jnp.concatenate(blocks, axis=0)]
        prev = project(blocks, w_query, w_keyval, prev, chunk, chunk + 1 == GATHER_CHUNKS)
    q_raw, keyval = prev

    by_owner = selected.reshape(ring, 2, rows)
    q_pos = jnp.roll(by_owner, (-my_z, -my_y), axis=(0, 1)).reshape(SEL)

    packed = pool_cache.reshape(slots, tokens, 2, KVH, HD).transpose(3, 2, 0, 1, 4)
    sources = [packed]
    for shift in range(1, req_size):
        sources.append(
            lax.ppermute(packed, "req", [((i + shift) % req_size, i) for i in range(req_size)])
        )
    place = (doc_slot // slots - lax.axis_index("req")) % req_size
    order = jnp.arange(tp_size, dtype=jnp.int32)
    sent = select_docs(
        sources, place, doc_slot % slots, (me ^ order) * KVH // tp_size, tp_size
    )
    chunks = [sent[0]] + [
        lax.ppermute(sent[j], "tp", [(i, i ^ j) for i in range(tp_size)])
        for j in range(1, tp_size)
    ]

    offsets = jnp.cumsum(lengths) - lengths
    slot_tokens = ((me ^ order) * tokens)[:, None] + jnp.arange(tokens, dtype=jnp.int32)[None, :]
    cache_pos = offsets[:, None, None] + slot_tokens[None]
    is_valid = slot_tokens[None] < lengths[:, None, None]
    replaced = jnp.any(cache_pos[..., None] == selected, axis=-1)
    key_pos = jnp.where(is_valid & jnp.logical_not(replaced), cache_pos, FAR)
    key_pos = key_pos.reshape(DOCS * tp_size // KEY_CHUNKS, KEY_CHUNKS * tokens)
    first_pos = jnp.min(key_pos, axis=1)

    natural = jnp.roll(keyval.reshape(ring, 2, rows, -1), (my_z, my_y), axis=(0, 1)).reshape(
        SEL, -1
    )
    if tp_size == KVH:
        half = tp_size // 2
        is_key = me < half
        first, second = natural[:, :HD], natural[:, HD:]
        one = lax.ppermute(
            jnp.where(is_key, first, second),
            "tp",
            [(i, 2 * i if i < half else 2 * (i - half) + 1) for i in range(tp_size)],
        )
        two = lax.ppermute(
            jnp.where(is_key, second, first),
            "tp",
            [(i, 2 * i + 1 if i < half else 2 * (i - half)) for i in range(tp_size)],
        )
        even = my_y == 0
        new_k, new_v = jnp.where(even, one, two), jnp.where(even, two, one)
    else:
        everyone = lax.all_gather(natural, "tp", axis=1, tiled=True)
        my_head = me * KVH // tp_size
        new_k = lax.dynamic_slice_in_dim(everyone, my_head * HD, HD, axis=1)
        new_v = lax.dynamic_slice_in_dim(everyone, (KVH + my_head) * HD, HD, axis=1)

    attention = attend(chunks, q_raw, q_pos, key_pos, first_pos, new_k, new_v, selected)

    finished = []
    for chunk in range(REDUCE_CHUNKS):
        own, other = project_out(attention, w_out, chunk, REDUCE_CHUNKS, rows)
        theirs = lax.ppermute(other, "tp", across)
        held = None
        for step in range(ring - 1, -1, -1):
            here = slice(step * rows, (step + 1) * rows)
            mine = own[here] + theirs[here].astype(jnp.float32)
            if held is not None:
                mine = mine + held.astype(jnp.float32)
            mine = mine.astype(jnp.bfloat16)
            if step:
                held = lax.ppermute(mine, "tp", down)
        finished.append(mine)
    return jnp.concatenate(finished, axis=1)


def solution(mesh):
    placed = (
        P(("groups", "req", "tp"), None),
        P(),
        P(None, "tp"),
        P(None, "tp"),
        P("tp", None),
        P(("groups", "req"), "tp", None, None),
        P(("groups", "req")),
        P(("groups", "req"), None),
        P(("groups", "req"), None),
    )
    return jax.shard_map(
        per_device,
        mesh=mesh,
        in_specs=placed,
        out_specs=P(("groups", "req", "tp"), None),
        check_vma=False,
    )
```

time: 522 us -> 463 us (0.89)
  Pallas kernels: 0 us -> 238 us
  waiting for transfers between devices: 332 us -> 105 us
  matrix products: 81.3 us -> 0 us
  starting transfers between devices: 3.98 us -> 81.3 us
  blocking collectives: 34.3 us -> 0 us
  other arithmetic: 34.1 us -> 14.2 us
  between operations: 13.7 us -> 0.41 us
    pallas_call x0 -> x8, Pallas kernels: none -> 238 us  [the longest x1 129 us: select_docs(): pl.pallas_call(functools.partial(select_kernel, n_dest, len(sources)), in...]
    reduce_scatter x3 -> x0, waiting for transfers between devices: 202 us -> none  [the longest x1 89.9 us: per_device(): lax.psum_scatter(summed.astype(jnp.bfloat16), 'tp', scatter_dimension=1,...]
    all_gather x3 -> x0, waiting for transfers between devices: 123 us -> none  [the longest x1 69.5 us: per_device(): piece_rows = lax.all_gather(normed, 'tp', axis=0, tiled=True)]
    ppermute x0 -> x40, waiting for transfers between devices: none -> 105 us  [the longest x7 64.1 us: per_device(): lax.ppermute(sent[j], 'tp', [(i, i ^ j) for i in range(tp_size)])]
    dot_general x5 -> x0, matrix products: 81.3 us -> none  [the longest x1 26.8 us: per_device(): jnp.einsum('kgqn,nkd->qkgd', weights.astype(jnp.bfloat16), all_vals, pref...]
    ppermute x0 -> x40, starting transfers between devices: none -> 81.3 us  [the longest x12 33.4 us: per_device(): held = lax.ppermute(mine, 'tp', down)]
    pmax x1 -> x0, blocking collectives: 34.3 us -> none  [per_device(): lax.pmax(jnp.max(scores, axis=-1).astype(jnp.bfloat16), 'tp')]
    reduce_sum x1 -> x0, other arithmetic: 22.4 us -> none  [per_device(): totals = jnp.sum(weights, axis=-1).reshape(HEADS, SEL).T]
  transfers between devices with their start and end apart: 7 -> 40, of which waited for: 6 -> 22; matrix products, arithmetic and copies ran while one was open for 13% -> 3% of each run, Pallas kernels for 0% -> 5%
where the time goes in v1:
time: 463 us
  Pallas kernels  238 us (51%)
  waiting for transfers between devices  105 us (23%)
  starting transfers between devices  81.3 us (18%)
  local copies, waits for them, and re-layouts  23.9 us (5%)
  other arithmetic  14.2 us (3%)
    pallas_call x1, Pallas kernels, select_docs(): pl.pallas_call(functools.partial(select_kernel, n_dest, len(sources)), in...  129 us
    pallas_call x1, Pallas kernels, attend(): pl.pallas_call(functools.partial(attend_kernel, n_chunks, tokens, heads_h...  80.3 us
    ppermute x7, waiting for transfers between devices, per_device(): lax.ppermute(sent[j], 'tp', [(i, i ^ j) for i in range(tp_size)])  64.1 us
    ppermute x12, starting transfers between devices, per_device(): held = lax.ppermute(mine, 'tp', down)  33.4 us
    ppermute x6, starting transfers between devices, per_device(): held = lax.ppermute(held, 'tp', up)  20.7 us
    ppermute x8, waiting for transfers between devices, per_device(): blocks += [held, lax.ppermute(held, 'tp', across)]  17.5 us
    unnamed x32, local copies, waits for them, and re-layouts  16.3 us
    pallas_call x4, Pallas kernels, project_out(): pl.pallas_call(functools.partial(out_kernel, rows), grid=(steps,), in_spe...  15.8 us
  transfers between devices with their start and end apart: 40, of which 22 were waited for; matrix products, arithmetic and copies ran while one was open for 3% of the time, Pallas kernels for 5%

profile of v1, /device:TPU:0, one launch (start us, length us, event | category | flops | bytes accessed | tf_op | source)
XLA Modules:
  0.0 462.6 jit_solution(17702036523085501859)
XLA Ops:
  0.0 11.1 %copy.12 = bf16[4,256,2,1024]{1,3,2,0:T(8,128)(2,1)} copy(bf16[4,256,2,1024]{3,2,1,0:T(2,128)(2,1)} %param.14) | data formatting | bytes 8388608 | tf_op args[5]
  11.1 6.5 %copy.13 = bf16[4,256,2,8,128]{4,1,0,2,3:T(8,128)(2,1)} copy(bf16[4,256,2,8,128]{1,4,3,2,0:T(8,128)(2,1)} %bitcast.18) | data formatting | bytes 8388608 | tf_op jit(solution)/shard_map/reshape | solution.py:381
  18.6 4.7 %collective-permute-start.8 = (bf16[32,4096]{1,0:T(8,128)(2,1)S(1)}, bf16[32,4096]{1,0:T(8,128)(2,1)S(1)}, u32[]{:S(2)}, u32[]{:S(2)}) collective-permute-start(bf16[32,4096]{1,0:T(8,128)(2,1)S(1)} %get-tuple-element.47.refs_0_), channel_id=1, source_target_pairs={{2,0},{3,1},{4,2},{5,3},{6,4},{7,5},{0,6},{1,7},{10,8},{11,9},{12,... | collective-permute-start | bytes 786440 | tf_op jit(solution)/shard_map/ppermute | solution.py:372
  23.2 1.5 collective-permute-start.7
  27.8 2.0 collective-permute-done.8.refs_2_
  29.8 4.3 collective-permute-start.10
  34.2 1.3 collective-permute-done.1.refs_2_
  35.5 4.3 collective-permute-start.3
  39.7 1.3 collective-permute-done.10.refs_4_
  41.1 4.3 collective-permute-start.12
  46.2 1.5 collective-permute-start.9
  48.3 2.7 collective-permute-start.5
  51.0 1.3 collective-permute-done.12.refs_6_
  52.3 1.5 collective-permute-start.13
  54.5 1.8 fusion.6
  56.2 0.7 collective-permute-start
  57.0 4.1 collective-permute-done.11.refs_5_
  61.1 1.5 collective-permute-start.2
  63.1 3.6 collective-permute-done.13.refs_7_
  66.7 1.5 collective-permute-start.6
  68.8 2.2 copy-done
  71.0 6.5 %project.2 = (f32[256,1024]{1,0:T(8,128)S(1)}, f32[256,256]{1,0:T(8,128)S(1)}) custom-call(bf16[32,4096]{1,0:T(8,128)(2,1)S(1)} %get-tuple-element.47.refs_0_, bf16[32,4096]{1,0:T(8,128)(2,1)S(1)} %collective-permute-done.7.refs_1_, bf16[32,4096]{1,0:T(8,128)(2,1)S(1)} %collective-permute-done.8.refs_2_, ...), custom_call_target="tpu_custom_call" | custom-call | flops 2684354560 | bytes 15204352 | tf_op jit(solution)/shard_map/project/pallas_call | solution.py:91
  78.0 5.6 %collective-permute-done.4.refs_5_ = bf16[32,4096]{1,0:T(8,128)(2,1)} collective-permute-done((bf16[32,4096]{1,0:T(8,128)(2,1)S(1)}, bf16[32,4096]{1,0:T(8,128)(2,1)}, u32[]{:S(2)}, u32[]{:S(2)}) %collective-permute-start.4) | collective-permute-done | bytes 262176 | tf_op jit(solution)/shard_map/ppermute | solution.py:370
  83.7 3.6 collective-permute-done.6.refs_7_
  87.3 6.5 %project.3 = (f32[256,1024]{1,0:T(8,128)S(1)}, bf16[256,256]{1,0:T(8,128)(2,1)S(1)}) custom-call(bf16[32,4096]{1,0:T(8,128)(2,1)S(1)} %get-tuple-element.48.refs_0_, bf16[32,4096]{1,0:T(8,128)(2,1)S(1)} %collective-permute-done.refs_1_, bf16[32,4096]{1,0:T(8,128)(2,1)S(1)} %collective-permute-done.1.refs_2_, ...), custom_call_target="tpu_custom_call" | custom-call | flops 2684354560 | bytes 15204352 | tf_op jit(solution)/shard_map/project/pallas_call | solution.py:91
  93.8 1.0 copy-done.3
  94.8 129.3 %select_docs.1 = (bf16[2,4,256,128]{3,2,1,0:T(8,128)(2,1)}, bf16[2,4,256,128]{3,2,1,0:T(8,128)(2,1)}, bf16[2,4,256,128]{3,2,1,0:T(8,128)(2,1)}, bf16[2,4,256,128...) custom-call(s32[4]{0:T(128)} %get-tuple-element.62.place_ref, ...), custom_call_target="tpu_custom_call" | custom-call | bytes 8388608 | tf_op jit(solution)/shard_map/select_docs/pallas_call | solution.py:142
  224.1 1.6 collective-permute-start.17
  227.0 2.6 compare_reduce_fusion
  229.6 4.6 collective-permute-start.19
  234.1 4.7 %collective-permute-done.15 = bf16[256,128]{1,0:T(8,128)(2,1)S(1)} collective-permute-done((bf16[256,128]{1,0:T(8,128)(2,1)S(1)}, bf16[256,128]{1,0:T(8,128)(2,1)S(1)}, u32[]{:S(2)}, u32[]{:S(2)}) %collective-permute-start.15) | collective-permute-done | bytes 65568 | tf_op jit(solution)/shard_map/ppermute | solution.py:418
  238.8 2.1 collective-permute-start.20
  241.0 2.7 collective-permute-start.21
  243.7 0.9 collective-permute-start.22
  244.6 10.6 %collective-permute-done.18.refs_2_ = bf16[2,4,256,128]{3,2,1,0:T(8,128)(2,1)S(1)} collective-permute-done((bf16[2,4,256,128]{3,2,1,0:T(8,128)(2,1)}, bf16[2,4,256,128]{3,2,1,0:T(8,128)(2,1)S(1)}, u32[]{:S(2)}, u32[]{:S(2)}) %collective-permute-start.18) | collective-permute-done | bytes 524320 | tf_op jit(solution)/shard_map/ppermute | solution.py:393
  255.2 0.9 and_select_fusion
  256.3 1.2 pad_maximum_fusion.3
  257.5 1.1 pad_maximum_fusion.1
  258.6 0.9 broadcast_select_fusion.2
  259.5 40.2 %collective-permute-done.20.refs_4_ = bf16[2,4,256,128]{3,2,1,0:T(8,128)(2,1)S(1)} collective-permute-done((bf16[2,4,256,128]{3,2,1,0:T(8,128)(2,1)}, bf16[2,4,256,128]{3,2,1,0:T(8,128)(2,1)S(1)}, u32[]{:S(2)}, u32[]{:S(2)}) %collective-permute-start.20) | collective-permute-done | bytes 524320 | tf_op jit(solution)/shard_map/ppermute | solution.py:393
  299.7 13.3 %collective-permute-done.21.refs_5_ = bf16[2,4,256,128]{3,2,1,0:T(8,128)(2,1)} collective-permute-done((bf16[2,4,256,128]{3,2,1,0:T(8,128)(2,1)}, bf16[2,4,256,128]{3,2,1,0:T(8,128)(2,1)}, u32[]{:S(2)}, u32[]{:S(2)}) %collective-permute-start.21) | collective-permute-done | bytes 524320 | tf_op jit(solution)/shard_map/ppermute | solution.py:393
  313.7 1.0 copy-done.5
  314.8 80.3 %attend.1.x_ref = bf16[256,1024]{1,0:T(8,128)(2,1)S(1)} custom-call(s32[4]{0:T(128)S(1)} %get-tuple-element.45.qmax_ref, s32[16]{0:T(128)S(1)} %reduce_min.18.first_ref, f32[256,1024]{1,0:T(8,128)S(1)} %copy-done.4, f32[256,128]{1,0:T(8,128)S(1)} %get-tuple-element.68.qcos_ref, f32[256,128]{1,0:T(8,128)S(1)} %get-tuple-element.69.qsin_ref, ...), custom_call_target="tpu_custom_call" | custom-call | flops 8858370048 | bytes 4194304 | tf_op jit(solution)/shard_map/attend/pallas_call | solution.py:263
  395.1 4.0 project_out.7
  399.1 4.0 project_out.6
  403.1 2.1 collective-permute-start.32
  405.1 3.9 project_out.5
  409.2 3.9 project_out.4
  413.1 2.1 collective-permute-start.24
  415.2 18.6 %collective-permute-start.37 = (bf16[32,2048]{1,0:T(8,128)(2,1)S(1)}, bf16[32,2048]{1,0:T(8,128)(2,1)S(1)}, u32[]{:S(2)}, u32[]{:S(2)}) collective-permute-start(bf16[32,2048]{1,0:T(8,128)(2,1)S(1)} %add_convert_fusion.3), channel_id=1, source_target_pairs={{0,2},{1,3},{2,4},{3,5},{4,6},{5,7},{6,0},{7,1},{8,10},{9,11},{10,... | collective-permute-start | bytes 393224 | tf_op jit(solution)/shard_map/ppermute | solution.py:445
  434.2 3.9 collective-permute-start.29
  438.2 5.6 %collective-permute-start.25 = (bf16[32,2048]{1,0:T(8,128)(2,1)S(1)}, bf16[32,2048]{1,0:T(8,128)(2,1)S(1)}, u32[]{:S(2)}, u32[]{:S(2)}) collective-permute-start(bf16[32,2048]{1,0:T(8,128)(2,1)S(1)} %add_convert_fusion.15), channel_id=1, source_target_pairs={{0,2},{1,3},{2,4},{3,5},{4,6},{5,7},{6,0},{7,1},{8,10},{9,11},{10,... | collective-permute-start | bytes 393224 | tf_op jit(solution)/shard_map/ppermute | solution.py:445
  444.8 1.5 collective-permute-done.25
  446.4 2.8 collective-permute-start.26
  449.2 1.5 collective-permute-done.38
  450.8 1.3 collective-permute-done.34
  452.2 1.3 collective-permute-done.30
  453.6 1.3 collective-permute-done.26
  454.9 1.1 collective-permute-start.27
  456.0 1.5 collective-permute-done.39
  457.6 1.4 collective-permute-done.35
  459.0 1.4 collective-permute-done.31
  460.4 1.4 collective-permute-done.27
  461.8 0.8 pad_maximum_fusion
  (107 shorter events, 12.2 us)
Async XLA Ops:
  11.1 7.0 %copy-start.6 = (bf16[32,8192]{1,0:T(8,128)(2,1)S(1)}, bf16[32,8192]{1,0:T(8,128)(2,1)}, u32[]{:S(2)}) copy-start(bf16[32,8192]{1,0:T(8,128)(2,1)} %param.9) | copy-start | bytes 1572868
  11.1 7.3 %copy-start.10 = (f32[8192]{0:T(1024)S(1)}, f32[8192]{0:T(1024)}, u32[]{:S(2)}) copy-start(f32[8192]{0:T(1024)} %param.10) | copy-start | bytes 98308
  11.1 14.1 %copy-start.14 = (s32[1,4]{1,0:T(1,128)S(1)}, s32[1,4]{1,0:T(1,128)}, u32[]{:S(2)}) copy-start(s32[1,4]{1,0:T(1,128)} %param.16) | copy-start | bytes 52
  11.1 15.3 %copy-start.2 = (s32[1,256]{1,0:T(1,128)S(1)}, s32[1,256]{1,0:T(1,128)}, u32[]{:S(2)}) copy-start(s32[1,256]{1,0:T(1,128)} %npos_ref.1) | copy-start | bytes 3076
  11.1 16.1 %copy-start.13 = (s32[4]{0:T(128)S(1)}, s32[4]{0:T(128)}, u32[]{:S(2)}) copy-start(s32[4]{0:T(128)} %param.15) | copy-start | bytes 52
  17.6 77.2 %collective-permute-start.16 = (bf16[8,2,4,256,128]{4,3,2,1,0:T(8,128)(2,1)}, bf16[8,2,4,256,128]{4,3,2,1,0:T(8,128)(2,1)}, u32[]{:S(2)}, u32[]{:S(2)}) collective-permute-start(bf16[8,2,4,256,128]{4,3,2,1,0:T(8,128)(2,1)} %bitcast.16), channel_id=1, source_target_pairs={{8,0},{0,8},{9,1},{1,9},{10,2},{2,10},{11,3},{3,11},{12,4},{4,12},... | collective-permute-start | bytes 12582920 | tf_op jit(solution)/shard_map/ppermute | solution.py:385
  18.6 11.3 %collective-permute-start.8 = (bf16[32,4096]{1,0:T(8,128)(2,1)S(1)}, bf16[32,4096]{1,0:T(8,128)(2,1)S(1)}, u32[]{:S(2)}, u32[]{:S(2)}) collective-permute-start(bf16[32,4096]{1,0:T(8,128)(2,1)S(1)} %get-tuple-element.47.refs_0_), channel_id=1, source_target_pairs={{2,0},{3,1},{4,2},{5,3},{6,4},{7,5},{0,6},{1,7},{10,8},{11,9},{12,... | collective-permute-start | bytes 786440 | tf_op jit(solution)/shard_map/ppermute | solution.py:372
  23.2 24.5 %collective-permute-start.7 = (bf16[32,4096]{1,0:T(8,128)(2,1)S(1)}, bf16[32,4096]{1,0:T(8,128)(2,1)S(1)}, u32[]{:S(2)}, u32[]{:S(2)}) collective-permute-start(bf16[32,4096]{1,0:T(8,128)(2,1)S(1)} %get-tuple-element.47.refs_0_), channel_id=1, source_target_pairs={{0,1},{1,0},{2,3},{3,2},{4,5},{5,4},{6,7},{7,6},{8,9},{9,8},{10,11... | collective-permute-start | bytes 786440 | tf_op jit(solution)/shard_map/ppermute | solution.py:370
  24.7 10.7 %collective-permute-start.1 = (bf16[32,4096]{1,0:T(8,128)(2,1)S(1)}, bf16[32,4096]{1,0:T(8,128)(2,1)S(1)}, u32[]{:S(2)}, u32[]{:S(2)}) collective-permute-start(bf16[32,4096]{1,0:T(8,128)(2,1)S(1)} %get-tuple-element.48.refs_0_), channel_id=1, source_target_pairs={{2,0},{3,1},{4,2},{5,3},{6,4},{7,5},{0,6},{1,7},{10,8},{11,9},{12,... | collective-permute-start | bytes 786440 | tf_op jit(solution)/shard_map/ppermute | solution.py:372
  27.2 26.8 %copy-start.12 = (s32[4]{0:T(128)}, s32[4]{0:T(128)S(1)}, u32[]{:S(2)}) copy-start(s32[4]{0:T(128)S(1)} %bitcast_subtract_fusion) | copy-start | bytes 52
  29.8 11.2 %collective-permute-start.10 = (bf16[32,4096]{1,0:T(8,128)(2,1)S(1)}, bf16[32,4096]{1,0:T(8,128)(2,1)S(1)}, u32[]{:S(2)}, u32[]{:S(2)}) collective-permute-start(bf16[32,4096]{1,0:T(8,128)(2,1)S(1)} %collective-permute-done.8.refs_2_), channel_id=1, source_target_pairs={{2,0},{3,1},{4,2},{5,3},{6,4},{7,5},{0,6},{1,7},{10,8},{11,9},{12,... | collective-permute-start | bytes 786440 | tf_op jit(solution)/shard_map/ppermute | solution.py:372
  35.5 12.8 %collective-permute-start.3 = (bf16[32,4096]{1,0:T(8,128)(2,1)S(1)}, bf16[32,4096]{1,0:T(8,128)(2,1)S(1)}, u32[]{:S(2)}, u32[]{:S(2)}) collective-permute-start(bf16[32,4096]{1,0:T(8,128)(2,1)S(1)} %collective-permute-done.1.refs_2_), channel_id=1, source_target_pairs={{2,0},{3,1},{4,2},{5,3},{6,4},{7,5},{0,6},{1,7},{10,8},{11,9},{12,... | collective-permute-start | bytes 786440 | tf_op jit(solution)/shard_map/ppermute | solution.py:372
  41.1 11.2 %collective-permute-start.12 = (bf16[32,4096]{1,0:T(8,128)(2,1)S(1)}, bf16[32,4096]{1,0:T(8,128)(2,1)S(1)}, u32[]{:S(2)}, u32[]{:S(2)}) collective-permute-start(bf16[32,4096]{1,0:T(8,128)(2,1)S(1)} %collective-permute-done.10.refs_4_), channel_id=1, source_target_pairs={{2,0},{3,1},{4,2},{5,3},{6,4},{7,5},{0,6},{1,7},{10,8},{11,9},{12,... | collective-permute-start | bytes 786440 | tf_op jit(solution)/shard_map/ppermute | solution.py:372
  46.2 10.0 %collective-permute-start.9 = (bf16[32,4096]{1,0:T(8,128)(2,1)S(1)}, bf16[32,4096]{1,0:T(8,128)(2,1)S(1)}, u32[]{:S(2)}, u32[]{:S(2)}) collective-permute-start(bf16[32,4096]{1,0:T(8,128)(2,1)S(1)} %collective-permute-done.8.refs_2_), channel_id=1, source_target_pairs={{0,1},{1,0},{2,3},{3,2},{4,5},{5,4},{6,7},{7,6},{8,9},{9,8},{10,11... | collective-permute-start | bytes 786440 | tf_op jit(solution)/shard_map/ppermute | solution.py:370
  47.7 13.3 %collective-permute-start.11 = (bf16[32,4096]{1,0:T(8,128)(2,1)S(1)}, bf16[32,4096]{1,0:T(8,128)(2,1)S(1)}, u32[]{:S(2)}, u32[]{:S(2)}) collective-permute-start(bf16[32,4096]{1,0:T(8,128)(2,1)S(1)} %collective-permute-done.10.refs_4_), channel_id=1, source_target_pairs={{0,1},{1,0},{2,3},{3,2},{4,5},{5,4},{6,7},{7,6},{8,9},{9,8},{10,11... | collective-permute-start | bytes 786440 | tf_op jit(solution)/shard_map/ppermute | solution.py:370
  48.3 14.3 %collective-permute-start.5 = (bf16[32,4096]{1,0:T(8,128)(2,1)S(1)}, bf16[32,4096]{1,0:T(8,128)(2,1)S(1)}, u32[]{:S(2)}, u32[]{:S(2)}) collective-permute-start(bf16[32,4096]{1,0:T(8,128)(2,1)S(1)} %collective-permute-done.3.refs_4_), channel_id=1, source_target_pairs={{2,0},{3,1},{4,2},{5,3},{6,4},{7,5},{0,6},{1,7},{10,8},{11,9},{12,... | collective-permute-start | bytes 786440 | tf_op jit(solution)/shard_map/ppermute | solution.py:372
  52.3 14.4 %collective-permute-start.13 = (bf16[32,4096]{1,0:T(8,128)(2,1)S(1)}, bf16[32,4096]{1,0:T(8,128)(2,1)S(1)}, u32[]{:S(2)}, u32[]{:S(2)}) collective-permute-start(bf16[32,4096]{1,0:T(8,128)(2,1)S(1)} %collective-permute-done.12.refs_6_), channel_id=1, source_target_pairs={{0,1},{1,0},{2,3},{3,2},{4,5},{5,4},{6,7},{7,6},{8,9},{9,8},{10,11... | collective-permute-start | bytes 786440 | tf_op jit(solution)/shard_map/ppermute | solution.py:370
  53.9 0.5 copy-start.11
  56.2 21.3 %collective-permute-start = (bf16[32,4096]{1,0:T(8,128)(2,1)S(1)}, bf16[32,4096]{1,0:T(8,128)(2,1)S(1)}, u32[]{:S(2)}, u32[]{:S(2)}) collective-permute-start(bf16[32,4096]{1,0:T(8,128)(2,1)S(1)} %get-tuple-element.48.refs_0_), channel_id=1, source_target_pairs={{0,1},{1,0},{2,3},{3,2},{4,5},{5,4},{6,7},{7,6},{8,9},{9,8},{10,11... | collective-permute-start | bytes 786440 | tf_op jit(solution)/shard_map/ppermute | solution.py:370
  61.1 17.0 %collective-permute-start.2 = (bf16[32,4096]{1,0:T(8,128)(2,1)S(1)}, bf16[32,4096]{1,0:T(8,128)(2,1)}, u32[]{:S(2)}, u32[]{:S(2)}) collective-permute-start(bf16[32,4096]{1,0:T(8,128)(2,1)S(1)} %collective-permute-done.1.refs_2_), channel_id=1, source_target_pairs={{0,1},{1,0},{2,3},{3,2},{4,5},{5,4},{6,7},{7,6},{8,9},{9,8},{10,11... | collective-permute-start | bytes 786440 | tf_op jit(solution)/shard_map/ppermute | solution.py:370
  62.6 21.1 %collective-permute-start.4 = (bf16[32,4096]{1,0:T(8,128)(2,1)S(1)}, bf16[32,4096]{1,0:T(8,128)(2,1)}, u32[]{:S(2)}, u32[]{:S(2)}) collective-permute-start(bf16[32,4096]{1,0:T(8,128)(2,1)S(1)} %collective-permute-done.3.refs_4_), channel_id=1, source_target_pairs={{0,1},{1,0},{2,3},{3,2},{4,5},{5,4},{6,7},{7,6},{8,9},{9,8},{10,11... | collective-permute-start | bytes 786440 | tf_op jit(solution)/shard_map/ppermute | solution.py:370
  66.7 20.6 %collective-permute-start.6 = (bf16[32,4096]{1,0:T(8,128)(2,1)S(1)}, bf16[32,4096]{1,0:T(8,128)(2,1)}, u32[]{:S(2)}, u32[]{:S(2)}) collective-permute-start(bf16[32,4096]{1,0:T(8,128)(2,1)S(1)} %collective-permute-done.5.refs_6_), channel_id=1, source_target_pairs={{0,1},{1,0},{2,3},{3,2},{4,5},{5,4},{6,7},{7,6},{8,9},{9,8},{10,11... | collective-permute-start | bytes 786440 | tf_op jit(solution)/shard_map/ppermute | solution.py:370
  68.8 2.2 copy-start
  71.0 16.3 %copy-start.1 = (bf16[8192,256]{1,0:T(8,128)(2,1)S(1)}, bf16[8192,256]{1,0:T(8,128)(2,1)}, u32[]{:S(2)}) copy-start(bf16[8192,256]{1,0:T(8,128)(2,1)} %refs_9_.3) | copy-start | bytes 12582916
  93.8 1.0 copy-start.3
  94.8 132.2 %copy-start.7 = (s32[4,8,256]{2,1,0:T(8,128)S(1)}, s32[4,8,256]{2,1,0:T(8,128)}, u32[]{:S(2)}) copy-start(s32[4,8,256]{2,1,0:T(8,128)} %broadcast_add_fusion) | copy-start | bytes 98308
  94.8 218.9 %copy-start.4 = (f32[256,1024]{1,0:T(8,128)S(1)}, f32[256,1024]{1,0:T(8,128)}, u32[]{:S(2)}) copy-start(f32[256,1024]{1,0:T(8,128)} %copy-done.3) | copy-start | bytes 3145732
  224.1 19.6 %collective-permute-start.17 = (bf16[2,4,256,128]{3,2,1,0:T(8,128)(2,1)}, bf16[2,4,256,128]{3,2,1,0:T(8,128)(2,1)S(1)}, u32[]{:S(2)}, u32[]{:S(2)}) collective-permute-start(bf16[2,4,256,128]{3,2,1,0:T(8,128)(2,1)} %get-tuple-element.30), channel_id=1, source_target_pairs={{0,1},{1,0},{2,3},{3,2},{4,5},{5,4},{6,7},{7,6},{8,9},{9,8},{10,11... | collective-permute-start | bytes 1572872 | tf_op jit(solution)/shard_map/ppermute | solution.py:393
  225.7 29.5 %collective-permute-start.18 = (bf16[2,4,256,128]{3,2,1,0:T(8,128)(2,1)}, bf16[2,4,256,128]{3,2,1,0:T(8,128)(2,1)S(1)}, u32[]{:S(2)}, u32[]{:S(2)}) collective-permute-start(bf16[2,4,256,128]{3,2,1,0:T(8,128)(2,1)} %get-tuple-element.31), channel_id=1, source_target_pairs={{0,2},{1,3},{2,0},{3,1},{4,6},{5,7},{6,4},{7,5},{8,10},{9,11},{10,... | collective-permute-start | bytes 1572872 | tf_op jit(solution)/shard_map/ppermute | solution.py:393
  225.8 13.1 %collective-permute-start.15 = (bf16[256,128]{1,0:T(8,128)(2,1)S(1)}, bf16[256,128]{1,0:T(8,128)(2,1)S(1)}, u32[]{:S(2)}, u32[]{:S(2)}) collective-permute-start(bf16[256,128]{1,0:T(8,128)(2,1)S(1)} %get-tuple-element.51), channel_id=1, source_target_pairs={{0,1},{1,3},{2,5},{3,7},{4,0},{5,2},{6,4},{7,6},{8,9},{9,11},{10,1... | collective-permute-start | bytes 196616 | tf_op jit(solution)/shard_map/ppermute | solution.py:418
  226.3 14.7 %collective-permute-start.14 = (bf16[256,128]{1,0:T(8,128)(2,1)S(1)}, bf16[256,128]{1,0:T(8,128)(2,1)S(1)}, u32[]{:S(2)}, u32[]{:S(2)}) collective-permute-start(bf16[256,128]{1,0:T(8,128)(2,1)S(1)} %get-tuple-element.52), channel_id=1, source_target_pairs={{0,0},{1,2},{2,4},{3,6},{4,1},{5,3},{6,5},{7,7},{8,8},{9,10},{10,1... | collective-permute-start | bytes 196616 | tf_op jit(solution)/shard_map/ppermute | solution.py:413
  229.6 30.0 %collective-permute-start.19 = (bf16[2,4,256,128]{3,2,1,0:T(8,128)(2,1)}, bf16[2,4,256,128]{3,2,1,0:T(8,128)(2,1)S(1)}, u32[]{:S(2)}, u32[]{:S(2)}) collective-permute-start(bf16[2,4,256,128]{3,2,1,0:T(8,128)(2,1)} %get-tuple-element.32), channel_id=1, source_target_pairs={{0,3},{1,2},{2,1},{3,0},{4,7},{5,6},{6,5},{7,4},{8,11},{9,10},{10,... | collective-permute-start | bytes 1572872 | tf_op jit(solution)/shard_map/ppermute | solution.py:393
  238.8 16.3 %copy-start.8 = (bf16[256,128]{1,0:T(8,128)(2,1)}, bf16[256,128]{1,0:T(8,128)(2,1)S(1)}, u32[]{:S(2)}) copy-start(bf16[256,128]{1,0:T(8,128)(2,1)S(1)} %collective-permute-done.15) | copy-start | bytes 196612
  238.8 60.9 %collective-permute-start.20 = (bf16[2,4,256,128]{3,2,1,0:T(8,128)(2,1)}, bf16[2,4,256,128]{3,2,1,0:T(8,128)(2,1)S(1)}, u32[]{:S(2)}, u32[]{:S(2)}) collective-permute-start(bf16[2,4,256,128]{3,2,1,0:T(8,128)(2,1)} %get-tuple-element.33), channel_id=1, source_target_pairs={{0,4},{1,5},{2,6},{3,7},{4,0},{5,1},{6,2},{7,3},{8,12},{9,13},{10,... | collective-permute-start | bytes 1572872 | tf_op jit(solution)/shard_map/ppermute | solution.py:393
  241.0 15.3 %copy-start.9 = (bf16[256,128]{1,0:T(8,128)(2,1)}, bf16[256,128]{1,0:T(8,128)(2,1)S(1)}, u32[]{:S(2)}) copy-start(bf16[256,128]{1,0:T(8,128)(2,1)S(1)} %collective-permute-done.14) | copy-start | bytes 196612
  241.0 72.0 %collective-permute-start.21 = (bf16[2,4,256,128]{3,2,1,0:T(8,128)(2,1)}, bf16[2,4,256,128]{3,2,1,0:T(8,128)(2,1)}, u32[]{:S(2)}, u32[]{:S(2)}) collective-permute-start(bf16[2,4,256,128]{3,2,1,0:T(8,128)(2,1)} %get-tuple-element.34), channel_id=1, source_target_pairs={{0,5},{1,4},{2,7},{3,6},{4,1},{5,0},{6,3},{7,2},{8,13},{9,12},{10,... | collective-permute-start | bytes 1572872 | tf_op jit(solution)/shard_map/ppermute | solution.py:393
  243.7 69.3 %collective-permute-start.22 = (bf16[2,4,256,128]{3,2,1,0:T(8,128)(2,1)}, bf16[2,4,256,128]{3,2,1,0:T(8,128)(2,1)}, u32[]{:S(2)}, u32[]{:S(2)}) collective-permute-start(bf16[2,4,256,128]{3,2,1,0:T(8,128)(2,1)} %get-tuple-element.35), channel_id=1, source_target_pairs={{0,6},{1,7},{2,4},{3,5},{4,2},{5,3},{6,0},{7,1},{8,14},{9,15},{10,... | collective-permute-start | bytes 1572872 | tf_op jit(solution)/shard_map/ppermute | solution.py:393
  255.2 57.8 %collective-permute-start.23 = (bf16[2,4,256,128]{3,2,1,0:T(8,128)(2,1)}, bf16[2,4,256,128]{3,2,1,0:T(8,128)(2,1)}, u32[]{:S(2)}, u32[]{:S(2)}) collective-permute-start(bf16[2,4,256,128]{3,2,1,0:T(8,128)(2,1)} %get-tuple-element.36), channel_id=1, source_target_pairs={{0,7},{1,6},{2,5},{3,4},{4,3},{5,2},{6,1},{7,0},{8,15},{9,14},{10,... | collective-permute-start | bytes 1572872 | tf_op jit(solution)/shard_map/ppermute | solution.py:393
  313.7 1.0 copy-start.5
  399.0 16.2 %collective-permute-start.36 = (bf16[128,2048]{1,0:T(8,128)(2,1)S(1)}, bf16[128,2048]{1,0:T(8,128)(2,1)S(1)}, u32[]{:S(2)}, u32[]{:S(2)}) collective-permute-start(bf16[128,2048]{1,0:T(8,128)(2,1)S(1)} %get-tuple-element.44), channel_id=1, source_target_pairs={{0,1},{1,0},{2,3},{3,2},{4,5},{5,4},{6,7},{7,6},{8,9},{9,8},{10,11... | collective-permute-start | bytes 1572872 | tf_op jit(solution)/shard_map/ppermute | solution.py:436
  403.1 30.8 %collective-permute-start.32 = (bf16[128,2048]{1,0:T(8,128)(2,1)S(1)}, bf16[128,2048]{1,0:T(8,128)(2,1)S(1)}, u32[]{:S(2)}, u32[]{:S(2)}) collective-permute-start(bf16[128,2048]{1,0:T(8,128)(2,1)S(1)} %get-tuple-element.42), channel_id=1, source_target_pairs={{0,1},{1,0},{2,3},{3,2},{4,5},{5,4},{6,7},{7,6},{8,9},{9,8},{10,11... | collective-permute-start | bytes 1572872 | tf_op jit(solution)/shard_map/ppermute | solution.py:436
  409.1 25.1 %collective-permute-start.28 = (bf16[128,2048]{1,0:T(8,128)(2,1)S(1)}, bf16[128,2048]{1,0:T(8,128)(2,1)S(1)}, u32[]{:S(2)}, u32[]{:S(2)}) collective-permute-start(bf16[128,2048]{1,0:T(8,128)(2,1)S(1)} %get-tuple-element.40), channel_id=1, source_target_pairs={{0,1},{1,0},{2,3},{3,2},{4,5},{5,4},{6,7},{7,6},{8,9},{9,8},{10,11... | collective-permute-start | bytes 1572872 | tf_op jit(solution)/shard_map/ppermute | solution.py:436
  413.1 25.0 %collective-permute-start.24 = (bf16[128,2048]{1,0:T(8,128)(2,1)S(1)}, bf16[128,2048]{1,0:T(8,128)(2,1)S(1)}, u32[]{:S(2)}, u32[]{:S(2)}) collective-permute-start(bf16[128,2048]{1,0:T(8,128)(2,1)S(1)} %get-tuple-element.38), channel_id=1, source_target_pairs={{0,1},{1,0},{2,3},{3,2},{4,5},{5,4},{6,7},{7,6},{8,9},{9,8},{10,11... | collective-permute-start | bytes 1572872 | tf_op jit(solution)/shard_map/ppermute | solution.py:436
  415.2 28.6 %collective-permute-start.37 = (bf16[32,2048]{1,0:T(8,128)(2,1)S(1)}, bf16[32,2048]{1,0:T(8,128)(2,1)S(1)}, u32[]{:S(2)}, u32[]{:S(2)}) collective-permute-start(bf16[32,2048]{1,0:T(8,128)(2,1)S(1)} %add_convert_fusion.3), channel_id=1, source_target_pairs={{0,2},{1,3},{2,4},{3,5},{4,6},{5,7},{6,0},{7,1},{8,10},{9,11},{10,... | collective-permute-start | bytes 393224 | tf_op jit(solution)/shard_map/ppermute | solution.py:445
  433.9 10.7 %collective-permute-start.33 = (bf16[32,2048]{1,0:T(8,128)(2,1)S(1)}, bf16[32,2048]{1,0:T(8,128)(2,1)S(1)}, u32[]{:S(2)}, u32[]{:S(2)}) collective-permute-start(bf16[32,2048]{1,0:T(8,128)(2,1)S(1)} %add_convert_fusion.7), channel_id=1, source_target_pairs={{0,2},{1,3},{2,4},{3,5},{4,6},{5,7},{6,0},{7,1},{8,10},{9,11},{10,... | collective-permute-start | bytes 393224 | tf_op jit(solution)/shard_map/ppermute | solution.py:445
  434.2 10.5 %collective-permute-start.29 = (bf16[32,2048]{1,0:T(8,128)(2,1)S(1)}, bf16[32,2048]{1,0:T(8,128)(2,1)S(1)}, u32[]{:S(2)}, u32[]{:S(2)}) collective-permute-start(bf16[32,2048]{1,0:T(8,128)(2,1)S(1)} %add_convert_fusion.11), channel_id=1, source_target_pairs={{0,2},{1,3},{2,4},{3,5},{4,6},{5,7},{6,0},{7,1},{8,10},{9,11},{10,... | collective-permute-start | bytes 393224 | tf_op jit(solution)/shard_map/ppermute | solution.py:445
  438.2 8.1 %collective-permute-start.25 = (bf16[32,2048]{1,0:T(8,128)(2,1)S(1)}, bf16[32,2048]{1,0:T(8,128)(2,1)S(1)}, u32[]{:S(2)}, u32[]{:S(2)}) collective-permute-start(bf16[32,2048]{1,0:T(8,128)(2,1)S(1)} %add_convert_fusion.15), channel_id=1, source_target_pairs={{0,2},{1,3},{2,4},{3,5},{4,6},{5,7},{6,0},{7,1},{8,10},{9,11},{10,... | collective-permute-start | bytes 393224 | tf_op jit(solution)/shard_map/ppermute | solution.py:445
  443.8 6.8 %collective-permute-start.38 = (bf16[32,2048]{1,0:T(8,128)(2,1)S(1)}, bf16[32,2048]{1,0:T(8,128)(2,1)S(1)}, u32[]{:S(2)}, u32[]{:S(2)}) collective-permute-start(bf16[32,2048]{1,0:T(8,128)(2,1)S(1)} %add_convert_fusion.2), channel_id=1, source_target_pairs={{0,2},{1,3},{2,4},{3,5},{4,6},{5,7},{6,0},{7,1},{8,10},{9,11},{10,... | collective-permute-start | bytes 393224 | tf_op jit(solution)/shard_map/ppermute | solution.py:445
  444.6 7.4 %collective-permute-start.34 = (bf16[32,2048]{1,0:T(8,128)(2,1)S(1)}, bf16[32,2048]{1,0:T(8,128)(2,1)S(1)}, u32[]{:S(2)}, u32[]{:S(2)}) collective-permute-start(bf16[32,2048]{1,0:T(8,128)(2,1)S(1)} %add_convert_fusion.6), channel_id=1, source_target_pairs={{0,2},{1,3},{2,4},{3,5},{4,6},{5,7},{6,0},{7,1},{8,10},{9,11},{10,... | collective-permute-start | bytes 393224 | tf_op jit(solution)/shard_map/ppermute | solution.py:445
  444.8 8.7 %collective-permute-start.30 = (bf16[32,2048]{1,0:T(8,128)(2,1)S(1)}, bf16[32,2048]{1,0:T(8,128)(2,1)S(1)}, u32[]{:S(2)}, u32[]{:S(2)}) collective-permute-start(bf16[32,2048]{1,0:T(8,128)(2,1)S(1)} %add_convert_fusion.10), channel_id=1, source_target_pairs={{0,2},{1,3},{2,4},{3,5},{4,6},{5,7},{6,0},{7,1},{8,10},{9,11},{10,... | collective-permute-start | bytes 393224 | tf_op jit(solution)/shard_map/ppermute | solution.py:445
  446.4 8.5 %collective-permute-start.26 = (bf16[32,2048]{1,0:T(8,128)(2,1)S(1)}, bf16[32,2048]{1,0:T(8,128)(2,1)S(1)}, u32[]{:S(2)}, u32[]{:S(2)}) collective-permute-start(bf16[32,2048]{1,0:T(8,128)(2,1)S(1)} %add_convert_fusion.14), channel_id=1, source_target_pairs={{0,2},{1,3},{2,4},{3,5},{4,6},{5,7},{6,0},{7,1},{8,10},{9,11},{10,... | collective-permute-start | bytes 393224 | tf_op jit(solution)/shard_map/ppermute | solution.py:445
  450.7 6.8 %collective-permute-start.39 = (bf16[32,2048]{1,0:T(8,128)(2,1)S(1)}, bf16[32,2048]{1,0:T(8,128)(2,1)S(1)}, u32[]{:S(2)}, u32[]{:S(2)}) collective-permute-start(bf16[32,2048]{1,0:T(8,128)(2,1)S(1)} %add_convert_fusion.1), channel_id=1, source_target_pairs={{0,2},{1,3},{2,4},{3,5},{4,6},{5,7},{6,0},{7,1},{8,10},{9,11},{10,... | collective-permute-start | bytes 393224 | tf_op jit(solution)/shard_map/ppermute | solution.py:445
  452.1 6.8 %collective-permute-start.35 = (bf16[32,2048]{1,0:T(8,128)(2,1)S(1)}, bf16[32,2048]{1,0:T(8,128)(2,1)S(1)}, u32[]{:S(2)}, u32[]{:S(2)}) collective-permute-start(bf16[32,2048]{1,0:T(8,128)(2,1)S(1)} %add_convert_fusion.5), channel_id=1, source_target_pairs={{0,2},{1,3},{2,4},{3,5},{4,6},{5,7},{6,0},{7,1},{8,10},{9,11},{10,... | collective-permute-start | bytes 393224 | tf_op jit(solution)/shard_map/ppermute | solution.py:445
  453.5 6.8 %collective-permute-start.31 = (bf16[32,2048]{1,0:T(8,128)(2,1)S(1)}, bf16[32,2048]{1,0:T(8,128)(2,1)S(1)}, u32[]{:S(2)}, u32[]{:S(2)}) collective-permute-start(bf16[32,2048]{1,0:T(8,128)(2,1)S(1)} %add_convert_fusion.9), channel_id=1, source_target_pairs={{0,2},{1,3},{2,4},{3,5},{4,6},{5,7},{6,0},{7,1},{8,10},{9,11},{10,... | collective-permute-start | bytes 393224 | tf_op jit(solution)/shard_map/ppermute | solution.py:445
  454.9 6.8 %collective-permute-start.27 = (bf16[32,2048]{1,0:T(8,128)(2,1)S(1)}, bf16[32,2048]{1,0:T(8,128)(2,1)S(1)}, u32[]{:S(2)}, u32[]{:S(2)}) collective-permute-start(bf16[32,2048]{1,0:T(8,128)(2,1)S(1)} %add_convert_fusion.13), channel_id=1, source_target_pairs={{0,2},{1,3},{2,4},{3,5},{4,6},{5,7},{6,0},{7,1},{8,10},{9,11},{10,... | collective-permute-start | bytes 393224 | tf_op jit(solution)/shard_map/ppermute | solution.py:445

commit v2 on v1

v2 whole, which is shorter than its diff:
```python
import functools
import math

import jax
import jax.numpy as jnp
from jax import lax
from jax.experimental import pallas as pl
from jax.experimental.pallas import tpu as pltpu
from jax.sharding import PartitionSpec as P

HEADS = 64
KVH = 8
HD = 128
DOCS = 4
BLOCK = 128
SEL = 256


EPSILON = 1e-05
ROPE_BASE = 500000.0
MASKED = -1e30
FAR = 1 << 30
GATHER_CHUNKS = 2
REDUCE_CHUNKS = 2
TILE_COLS = 256
GROUPS = 2


def rotation_tables(positions):
    half_dim = HD // 2
    inverse = ROPE_BASE ** (-(jnp.arange(half_dim, dtype=jnp.float32) * (2.0 / HD)))
    angles = positions.astype(jnp.float32)[:, None] * inverse[None, :]
    cosine = jnp.cos(angles)
    sine_part = jnp.sin(angles)
    return (
        jnp.concatenate([cosine, cosine], axis=-1),
        jnp.concatenate([-sine_part, sine_part], axis=-1),
    )


def rotate(values, cosine, sine_part):
    swapped = jnp.concatenate([values[:, HD // 2 :], values[:, : HD // 2]], axis=-1)
    return values * cosine + swapped * sine_part


def megabytes(count):
    return pltpu.CompilerParams(vmem_limit_bytes=count * 1024 * 1024)


def project_kernel(n_blocks, has_prev, place_ref, *refs):
    blocks = refs[:n_blocks]
    left_ref, right_ref, wq_ref, wkv_ref = refs[n_blocks : n_blocks + 4]
    rest = refs[n_blocks + 4 :]
    if has_prev:
        prev_q, prev_kv = rest[:2]
        rest = rest[2:]
    out_q, out_kv, total_q, total_kv = rest
    step = pl.program_id(0)

    @pl.when(step == 0)
    def _():
        if has_prev:
            total_q[...] = prev_q[...]
            total_kv[...] = prev_kv[...]
        else:
            total_q[...] = jnp.zeros_like(total_q)
            total_kv[...] = jnp.zeros_like(total_kv)

    far = jnp.where(step == 0, left_ref[...], right_ref[...])
    rows = jnp.concatenate([b[...] for b in blocks] + [far], axis=0)
    total_q[...] += jnp.dot(rows, wq_ref[...], preferred_element_type=jnp.float32)
    total_kv[...] += jnp.dot(rows, wkv_ref[...], preferred_element_type=jnp.float32)

    @pl.when(step == 1)
    def _():
        if has_prev:
            count = left_ref.shape[0]
            for block in range(SEL // count):
                here = slice(block * count, (block + 1) * count)
                there = pl.ds(pl.multiple_of(place_ref[block] * count, count), count)
                out_q[there, :] = total_q[here, :]
                out_kv[there, :] = total_kv[here, :]
        else:
            out_q[...] = total_q[...]
            out_kv[...] = total_kv[...]


def project(place, blocks, left, right, w_query, w_keyval, prev, chunk):
    depth = 2 * left.shape[1]
    tile = left.shape[1]
    q_cols, kv_cols = w_query.shape[1], w_keyval.shape[1]
    whole = lambda k: (0, 0)
    specs = [pl.BlockSpec(memory_space=pltpu.SMEM)]
    specs += [pl.BlockSpec((b.shape[0], tile), lambda k: (0, k)) for b in blocks]
    specs += [pl.BlockSpec(left.shape, whole)] * 2
    specs += [
        pl.BlockSpec((tile, q_cols), lambda k: (chunk * 2 + k, 0)),
        pl.BlockSpec((tile, kv_cols), lambda k: (chunk * 2 + k, 0)),
    ]
    operands = [place, *blocks, left, right, w_query, w_keyval]
    if prev is not None:
        specs += [pl.BlockSpec((SEL, q_cols), whole), pl.BlockSpec((SEL, kv_cols), whole)]
        operands += list(prev)
    return pl.pallas_call(
        functools.partial(project_kernel, len(blocks), prev is not None),
        grid=(2,),
        in_specs=specs,
        out_specs=[pl.BlockSpec((SEL, q_cols), whole), pl.BlockSpec((SEL, kv_cols), whole)],
        out_shape=[
            jax.ShapeDtypeStruct((SEL, q_cols), jnp.float32),
            jax.ShapeDtypeStruct((SEL, kv_cols), jnp.float32),
        ],
        scratch_shapes=[
            pltpu.VMEM((SEL, q_cols), jnp.float32),
            pltpu.VMEM((SEL, kv_cols), jnp.float32),
        ],
        compiler_params=megabytes(32),
        cost_estimate=pl.CostEstimate(
            flops=2 * SEL * depth * (q_cols + kv_cols),
            bytes_accessed=2 * depth * (q_cols + kv_cols + SEL) + 8 * SEL * (q_cols + kv_cols),
            transcendentals=0,
        ),
        name="project",
    )(*operands)


def select_kernel(n_dest, n_src, place_ref, slot_ref, head_ref, *refs):
    sources = refs[:n_src]
    outs = refs[n_src : n_src + n_dest]
    sems = refs[n_src + n_dest]
    for doc in range(DOCS):
        for src in range(n_src):

            @pl.when(place_ref[doc] == src)
            def _():
                for dest in range(n_dest):
                    cols = pl.ds(pl.multiple_of(head_ref[dest] * HD, HD), HD)
                    pltpu.make_async_copy(
                        sources[src].at[slot_ref[doc], :, :, cols],
                        outs[dest].at[:, doc],
                        sems.at[dest, doc],
                    ).start()

    for dest in range(n_dest):
        for doc in range(DOCS):
            pltpu.make_async_copy(
                sources[0].at[0, :, :, 0:HD], outs[dest].at[:, doc], sems.at[dest, doc]
            ).wait()


def select_docs(sources, place, slot, heads, n_dest):
    tokens = sources[0].shape[2]
    shape = (2, DOCS, tokens, HD)
    smem = pl.BlockSpec(memory_space=pltpu.SMEM)
    return pl.pallas_call(
        functools.partial(select_kernel, n_dest, len(sources)),
        in_specs=[smem] * 3 + [pl.BlockSpec(memory_space=pl.ANY)] * len(sources),
        out_specs=[pl.BlockSpec(memory_space=pltpu.VMEM)] * n_dest,
        out_shape=[jax.ShapeDtypeStruct(shape, jnp.bfloat16)] * n_dest,
        scratch_shapes=[pltpu.SemaphoreType.DMA((n_dest, DOCS))],
        compiler_params=megabytes(16),
        cost_estimate=pl.CostEstimate(
            flops=0, bytes_accessed=4 * n_dest * math.prod(shape), transcendentals=0
        ),
        name="select_docs",
    )(place, slot, heads, *sources)


def attend_kernel(n_chunks, is_first, is_last, heads_here, first_ref, qmin_ref, qmax_ref, *refs):
    refs = list(refs)
    take = lambda count: [refs.pop(0) for _ in range(count)]
    chunks = take(n_chunks)
    dead_ref, qpos_ref = take(2)
    if is_first:
        q_ref, cos_ref, sin_ref, newk_ref, newv_ref = take(5)
    else:
        queries, old_top, old_total, old_summed = take(4)
    if is_last:
        (out_ref,) = take(1)
        if is_first:
            (queries,) = take(1)
        top, total, summed = take(3)
    else:
        queries, top, total, summed = take(4)
    values = take(1)[0]
    if is_first:
        new_key, new_value = take(2)
    n_tiles = SEL * heads_here // TILE_COLS
    tile_q = TILE_COLS // heads_here
    tokens = chunks[0].shape[2]
    scale = math.log2(math.e) / math.sqrt(HD)

    for chunk in range(n_chunks):
        for doc in range(DOCS):
            values[doc, :, chunk * tokens : (chunk + 1) * tokens] = chunks[chunk][1, doc].T
    if is_first:
        new_key[...] = rotate(
            newk_ref[...].astype(jnp.float32), cos_ref[...], sin_ref[...]
        ).astype(jnp.bfloat16)
        new_value[...] = newv_ref[...].T

    one_row = jnp.where(
        lax.broadcasted_iota(jnp.int32, (HD, TILE_COLS), 0) == 0, 1.0, 0.0
    ).astype(jnp.bfloat16)

    def update(tile, parts):
        best = functools.reduce(
            jnp.maximum, [jnp.max(scores, axis=0, keepdims=True) for scores, _ in parts]
        )
        old = top[tile]
        new = jnp.maximum(old, best)
        shrink = jnp.exp2((old - new) * scale)
        running = total[tile] * shrink
        mixed = summed[tile] * shrink
        for scores, value in parts:
            weights = jnp.exp2((scores - new) * scale)
            running += jnp.sum(weights, axis=0, keepdims=True)
            mixed += jnp.dot(
                value, weights.astype(jnp.bfloat16), preferred_element_type=jnp.float32
            )
        top[tile] = new
        total[tile] = running
        summed[tile] = mixed

    @pl.loop(0, n_tiles)
    def _(tile):
        here = pl.ds(pl.multiple_of(tile * tile_q, tile_q), tile_q)
        if is_first:
            stacked = jnp.concatenate(
                [
                    rotate(
                        q_ref[here, head * HD : (head + 1) * HD], cos_ref[here, :], sin_ref[here, :]
                    )
                    for head in range(heads_here)
                ],
                axis=0,
            )
            queries[tile] = stacked.T.astype(jnp.bfloat16)
            top[tile] = jnp.full(top.shape[1:], MASKED, jnp.float32)
            total[tile] = jnp.zeros(total.shape[1:], jnp.float32)
            summed[tile] = jnp.zeros(summed.shape[1:], jnp.float32)
            scores = jnp.dot(new_key[...], queries[tile], preferred_element_type=jnp.float32)
            key_index = lax.broadcasted_iota(jnp.int32, scores.shape, 0)
            q_index = tile * tile_q + lax.broadcasted_iota(jnp.int32, scores.shape, 1) % tile_q
            scores = jnp.where(key_index <= q_index, scores, MASKED)
            update(tile, [(scores, new_value[...])])
        else:
            top[tile] = old_top[tile]
            total[tile] = old_total[tile]
            summed[tile] = old_summed[tile]

        extended = jnp.concatenate([queries[tile], one_row], axis=0)

        @pl.loop(0, DOCS)
        def _(doc):
            firsts = [first_ref[doc * n_chunks + chunk] for chunk in range(n_chunks)]
            lowest = functools.reduce(jnp.minimum, firsts)
            reach = functools.reduce(jnp.maximum, firsts) + tokens - 1

            def visit(masked):
                parts = []
                for chunk in range(n_chunks):
                    span = slice(chunk * tokens, (chunk + 1) * tokens)
                    keys = jnp.concatenate([chunks[chunk][0, doc], dead_ref[doc, span, :]], axis=1)
                    scores = jnp.dot(keys, extended, preferred_element_type=jnp.float32)
                    if masked:
                        key_pos = firsts[chunk] + lax.broadcasted_iota(jnp.int32, scores.shape, 0)
                        scores = jnp.where(key_pos <= qpos_ref[tile], scores, MASKED)
                    parts.append((scores, values[doc, :, span]))
                update(tile, parts)

            live = lowest <= qmax_ref[tile]
            whole = reach <= qmin_ref[tile]

            @pl.when(live & whole)
            def _():
                visit(False)

            @pl.when(live & jnp.logical_not(whole))
            def _():
                visit(True)

        if is_last:
            finished = (summed[tile] / total[tile]).T.astype(jnp.bfloat16)
            for head in range(heads_here):
                out_ref[here, head * HD : (head + 1) * HD] = finished[
                    head * tile_q : (head + 1) * tile_q, :
                ]


def attend(chunks, dead, first_pos, selected, heads_here, fresh, state, is_last):
    n_chunks = len(chunks)
    tokens = chunks[0].shape[2]
    n_tiles = SEL * heads_here // TILE_COLS
    tile_q = TILE_COLS // heads_here
    is_first = state is None
    by_tile = selected.reshape(n_tiles, tile_q)
    q_pos = jnp.tile(by_tile, (1, heads_here)).reshape(n_tiles, 1, TILE_COLS)
    smem = pl.BlockSpec(memory_space=pltpu.SMEM)
    vmem = pl.BlockSpec(memory_space=pltpu.VMEM)
    operands = [first_pos, by_tile[:, 0], by_tile[:, -1], *chunks, dead, q_pos]
    operands += list(fresh) if is_first else list(state)
    shapes = [
        ((n_tiles, HD, TILE_COLS), jnp.bfloat16),
        ((n_tiles, 1, TILE_COLS), jnp.float32),
        ((n_tiles, 1, TILE_COLS), jnp.float32),
        ((n_tiles, HD, TILE_COLS), jnp.float32),
    ]
    if is_last:
        outs = [((SEL, heads_here * HD), jnp.bfloat16)]
        scratch = shapes if is_first else shapes[1:]
    else:
        outs, scratch = shapes, []
    scratch = scratch + [((DOCS, HD, n_chunks * tokens), jnp.bfloat16)]
    if is_first:
        scratch = scratch + [((SEL, HD), jnp.bfloat16), ((HD, SEL), jnp.bfloat16)]
    pairs = SEL * heads_here * DOCS * n_chunks * tokens // 2
    return pl.pallas_call(
        functools.partial(attend_kernel, n_chunks, is_first, is_last, heads_here),
        in_specs=[smem] * 3 + [vmem] * (len(operands) - 3),
        out_specs=[vmem] * len(outs),
        out_shape=[jax.ShapeDtypeStruct(*s) for s in outs],
        scratch_shapes=[pltpu.VMEM(*s) for s in scratch],
        compiler_params=megabytes(32),
        cost_estimate=pl.CostEstimate(
            flops=4 * pairs * HD,
            bytes_accessed=4 * DOCS * n_chunks * tokens * HD,
            transcendentals=pairs,
        ),
        name="attend",
    )(*operands)


def out_kernel(n_blocks, place_ref, x_ref, w_ref, *refs):
    outs, ordered = refs[:-1], refs[-1]
    rows = SEL // n_blocks
    tiles = pl.num_programs(0)
    step = pl.program_id(0)

    @pl.when(step == 0)
    def _():
        for block in range(n_blocks):
            there = pl.ds(pl.multiple_of(place_ref[block] * rows, rows), rows)
            ordered[block * rows : (block + 1) * rows, :] = x_ref[there, :]

    product = jnp.dot(
        ordered[...].astype(jnp.bfloat16), w_ref[...], preferred_element_type=jnp.float32
    )
    for block in range(n_blocks - 1):
        outs[block][...] = product[block * rows : (block + 1) * rows, :]
    far = product[(n_blocks - 1) * rows :, :].astype(jnp.bfloat16)

    @pl.when(step < tiles // 2)
    def _():
        outs[n_blocks - 1][...] = far

    @pl.when(step >= tiles // 2)
    def _():
        outs[n_blocks][...] = far


def project_out(place, attention, w_out, chunk, n_chunks, n_blocks):
    depth = w_out.shape[0]
    width = w_out.shape[1] // n_chunks
    rows = SEL // n_blocks
    tile = 512
    steps = width // tile
    half = steps // 2
    if rows % 16:
        attention = attention.astype(jnp.float32)
    return pl.pallas_call(
        functools.partial(out_kernel, n_blocks),
        grid=(steps,),
        in_specs=[
            pl.BlockSpec(memory_space=pltpu.SMEM),
            pl.BlockSpec((SEL, depth), lambda n: (0, 0)),
            pl.BlockSpec((depth, tile), lambda n: (0, chunk * steps + n)),
        ],
        out_specs=[pl.BlockSpec((rows, tile), lambda n: (0, n))] * (n_blocks - 1)
        + [
            pl.BlockSpec((rows, tile), lambda n: (0, jnp.minimum(n, half - 1))),
            pl.BlockSpec((rows, tile), lambda n: (0, jnp.maximum(n - half, 0))),
        ],
        out_shape=[jax.ShapeDtypeStruct((rows, width), jnp.float32)] * (n_blocks - 1)
        + [jax.ShapeDtypeStruct((rows, width // 2), jnp.bfloat16)] * 2,
        scratch_shapes=[pltpu.VMEM((SEL, depth), attention.dtype)],
        compiler_params=megabytes(32),
        cost_estimate=pl.CostEstimate(
            flops=2 * SEL * depth * width,
            bytes_accessed=2 * depth * (width + SEL) + 4 * SEL * width,
            transcendentals=0,
        ),
        name="project_out",
    )(place, attention, w_out)


def per_device(
    hidden_in, norm_gain, w_query, w_keyval, w_out, pool_cache, doc_slot, doc_blocks, sel_pos
):
    tp_size = lax.axis_size("tp")
    req_size = lax.axis_size("req")
    me = lax.axis_index("tp")
    rows, width = hidden_in.shape
    slots, tokens = pool_cache.shape[:2]
    heads_here = w_query.shape[1] // HD
    selected = sel_pos[0]
    lengths = doc_blocks[0] * BLOCK

    if tp_size == KVH:
        ring = [*range(0, tp_size, 2), *range(tp_size - 1, 0, -2)]
    else:
        ring = list(range(tp_size))
    far = tp_size // 2
    forth = [(ring[p], ring[(p + 1) % tp_size]) for p in range(tp_size)]
    back = [(dst, src) for src, dst in forth]
    steps = [0] + [sign * k for k in range(1, far) for sign in (-1, 1)] + [far]
    table = [[ring[(ring.index(i) + s) % tp_size] for s in steps] for i in range(tp_size)]
    place = jnp.array(table, jnp.int32)[me]

    widened = hidden_in.astype(jnp.float32)
    normed = (
        widened
        * lax.rsqrt(jnp.mean(widened * widened, axis=-1, keepdims=True) + EPSILON)
        * norm_gain
    ).astype(jnp.bfloat16)
    normed, pool_cache = lax.optimization_barrier((normed, pool_cache))

    part = width // GATHER_CHUNKS
    half = part // 2
    prev = None
    for chunk in range(GATHER_CHUNKS):
        own = normed[:, chunk * part : (chunk + 1) * part]
        before = behind = own
        blocks = [own]
        for _ in range(1, far):
            before = lax.ppermute(before, "tp", forth)
            behind = lax.ppermute(behind, "tp", back)
            blocks += [before, behind]
        left = lax.ppermute(before[:, :half], "tp", forth)
        right = lax.ppermute(behind[:, half:], "tp", back)
        if rows % 16:
            blocks = [jnp.concatenate(blocks, axis=0)]
        prev = project(place, blocks, left, right, w_query, w_keyval, prev, chunk)
    q_raw, keyval = prev

    by_kind = pool_cache.transpose(0, 2, 1, 3)
    sources = [by_kind]
    for shift in range(1, req_size):
        sources.append(
            lax.ppermute(by_kind, "req", [((i + shift) % req_size, i) for i in range(req_size)])
        )
    holder = (doc_slot // slots - lax.axis_index("req")) % req_size
    order = jnp.arange(tp_size, dtype=jnp.int32)
    sent = select_docs(sources, holder, doc_slot % slots, (me ^ order) * KVH // tp_size, tp_size)
    chunks = [sent[0]] + [
        lax.ppermute(sent[j], "tp", [(i, i ^ j) for i in range(tp_size)])
        for j in range(1, tp_size)
    ]

    offsets = jnp.cumsum(lengths) - lengths
    first_slot = (me ^ order) * tokens
    slot_tokens = first_slot[:, None] + jnp.arange(tokens, dtype=jnp.int32)[None, :]
    cache_pos = offsets[:, None, None] + slot_tokens[None]
    is_valid = slot_tokens[None] < lengths[:, None, None]
    replaced = jnp.any(cache_pos[..., None] == selected, axis=-1)
    dead = jnp.where(is_valid & jnp.logical_not(replaced), 0.0, MASKED).astype(jnp.bfloat16)
    dead = jnp.broadcast_to(dead[..., None], (DOCS, tp_size, tokens, HD))
    first_pos = jnp.where(
        first_slot[None] < lengths[:, None], offsets[:, None] + first_slot[None], FAR
    )

    keyval = keyval.astype(jnp.bfloat16)
    if tp_size == KVH:
        middle = tp_size // 2
        is_key = me < middle
        first, second = keyval[:, :HD], keyval[:, HD:]
        one = lax.ppermute(
            jnp.where(is_key, first, second),
            "tp",
            [(i, 2 * i if i < middle else 2 * (i - middle) + 1) for i in range(tp_size)],
        )
        two = lax.ppermute(
            jnp.where(is_key, second, first),
            "tp",
            [(i, 2 * i + 1 if i < middle else 2 * (i - middle)) for i in range(tp_size)],
        )
        even = me % 2 == 0
        new_k, new_v = jnp.where(even, one, two), jnp.where(even, two, one)
    else:
        everyone = lax.all_gather(keyval, "tp", axis=1, tiled=True)
        my_head = me * KVH // tp_size
        new_k = lax.dynamic_slice_in_dim(everyone, my_head * HD, HD, axis=1)
        new_v = lax.dynamic_slice_in_dim(everyone, (KVH + my_head) * HD, HD, axis=1)

    cosine, sine_part = rotation_tables(selected)
    state = None
    size = tp_size // GROUPS
    for group in range(GROUPS):
        span = slice(group * size, (group + 1) * size)
        state = attend(
            chunks[span],
            dead[:, span].reshape(DOCS, size * tokens, HD),
            first_pos[:, span].reshape(-1),
            selected,
            heads_here,
            (q_raw, cosine, sine_part, new_k, new_v),
            state,
            group + 1 == GROUPS,
        )
    (attention,) = state

    finished = []
    for chunk in range(REDUCE_CHUNKS):
        pieces = project_out(place, attention, w_out, chunk, REDUCE_CHUNKS, tp_size)
        total = pieces[0]
        to_forth, to_back = pieces[2 : tp_size - 1 : 2], pieces[1 : tp_size - 1 : 2]
        cut = pieces[-1].shape[1]
        ahead = lax.ppermute(pieces[-2], "tp", forth).astype(jnp.float32)
        astern = lax.ppermute(pieces[-1], "tp", back).astype(jnp.float32)
        for k in range(far - 1, 0, -1):
            up, down = to_forth[k - 1], to_back[k - 1]
            if k == far - 1:
                up = jnp.concatenate([up[:, :cut] + ahead, up[:, cut:]], axis=1)
                down = jnp.concatenate([down[:, :cut], down[:, cut:] + astern], axis=1)
            else:
                up, down = up + ahead, down + astern
            ahead = lax.ppermute(up.astype(jnp.bfloat16), "tp", forth).astype(jnp.float32)
            astern = lax.ppermute(down.astype(jnp.bfloat16), "tp", back).astype(jnp.float32)
        finished.append((total + ahead + astern).astype(jnp.bfloat16))
    return jnp.concatenate(finished, axis=1)


def solution(mesh):
    placed = (
        P(("groups", "req", "tp"), None),
        P(),
        P(None, "tp"),
        P(None, "tp"),
        P("tp", None),
        P(("groups", "req"), "tp", None, None),
        P(("groups", "req")),
        P(("groups", "req"), None),
        P(("groups", "req"), None),
    )
    return jax.shard_map(
        per_device,
        mesh=mesh,
        in_specs=placed,
        out_specs=P(("groups", "req", "tp"), None),
        check_vma=False,
    )
```

time: 463 us -> 252 us (0.54)
  Pallas kernels: 238 us -> 67.2 us
  waiting for transfers between devices: 105 us -> 80.7 us
  starting transfers between devices: 81.3 us -> 70.5 us
    pallas_call x1, Pallas kernels: 129 us -> 4.61 us  [select_docs(): pl.pallas_call(functools.partial(select_kernel, n_dest, len(sources)), in...]
    pallas_call x5 -> x4, Pallas kernels: 96.1 us -> 51.3 us  [the longest x2 40.4 us: attend(): pl.pallas_call(functools.partial(attend_kernel, n_chunks, is_first, is_la...]
    ppermute x7, waiting for transfers between devices: 64.1 us -> 34.5 us  [per_device(): lax.ppermute(sent[j], 'tp', [(i, i ^ j) for i in range(tp_size)])]
    ppermute x32 -> x34, starting transfers between devices: 68.8 us -> 51.2 us  [the longest x2 18.3 us: per_device(): ahead = lax.ppermute(pieces[-2], 'tp', forth).astype(jnp.float32)]
    ppermute x32 -> x34, waiting for transfers between devices: 35.8 us -> 46.2 us  [the longest x6 19.6 us: per_device(): lax.ppermute(down.astype(jnp.bfloat16), 'tp', back).astype(jnp.float32)]
    reshape x2, local copies, waits for them, and re-layouts: 6.61 us -> 0.17 us  [per_device(): first_pos[:, span].reshape(-1)]
    ppermute x7, starting transfers between devices: 11.9 us -> 17.7 us  [per_device(): lax.ppermute(sent[j], 'tp', [(i, i ^ j) for i in range(tp_size)])]
    optimization_barrier x0 -> x1, local copies, waits for them, and re-layouts: none -> 5.51 us  [per_device(): normed, pool_cache = lax.optimization_barrier((normed, pool_cache))]
  transfers between devices with their start and end apart: 40 -> 42, of which waited for: 22 -> 25; matrix products, arithmetic and copies ran while one was open for 3% -> 5% of each run, Pallas kernels for 5% -> 18%
where the time goes in v2:
time: 252 us
  waiting for transfers between devices  80.7 us (32%)
  starting transfers between devices  70.5 us (28%)
  Pallas kernels  67.2 us (27%)
  local copies, waits for them, and re-layouts  23.3 us (9%)
  other arithmetic  9.88 us (4%)
    pallas_call x2, Pallas kernels, attend(): pl.pallas_call(functools.partial(attend_kernel, n_chunks, is_first, is_la...  40.4 us
    ppermute x7, waiting for transfers between devices, per_device(): lax.ppermute(sent[j], 'tp', [(i, i ^ j) for i in range(tp_size)])  34.5 us
    ppermute x6, waiting for transfers between devices, per_device(): lax.ppermute(down.astype(jnp.bfloat16), 'tp', back).astype(jnp.float32)  19.6 us
    ppermute x2, starting transfers between devices, per_device(): ahead = lax.ppermute(pieces[-2], 'tp', forth).astype(jnp.float32)  18.3 us
    ppermute x7, starting transfers between devices, per_device(): lax.ppermute(sent[j], 'tp', [(i, i ^ j) for i in range(tp_size)])  17.7 us
    ppermute x6, waiting for transfers between devices, per_device(): before = lax.ppermute(before, 'tp', forth)  16.6 us
    unnamed x50, local copies, waits for them, and re-layouts  13.4 us
    ppermute x6, starting transfers between devices, per_device(): before = lax.ppermute(before, 'tp', forth)  11.9 us
  transfers between devices with their start and end apart: 42, of which 25 were waited for; matrix products, arithmetic and copies ran while one was open for 5% of the time, Pallas kernels for 18%

profile of v2, /device:TPU:0, one launch (start us, length us, event | category | flops | bytes accessed | tf_op | source)
XLA Modules:
  0.0 252.1 jit_solution(8058063785338809241)
XLA Ops:
  0.0 1.2 fusion
  1.3 1.2 fusion.2
  2.5 5.5 %copy.22 = bf16[4,256,2,1024]{3,1,2,0:T(8,128)(2,1)} copy(bf16[4,256,2,1024]{3,2,1,0:T(2,128)(2,1)} %param.15) | data formatting | bytes 8388608 | tf_op jit(solution)/shard_map/optimization_barrier | solution.py:426
  8.5 2.6 %collective-permute-start.8 = (bf16[32,4096]{1,0:T(8,128)(2,1)S(1)}, bf16[32,4096]{1,0:T(8,128)(2,1)S(1)}, u32[]{:S(2)}, u32[]{:S(2)}) collective-permute-start(bf16[32,4096]{1,0:T(8,128)(2,1)S(1)} %get-tuple-element.78.refs_0_), channel_id=1, source_target_pairs={{0,2},{2,4},{4,6},{6,7},{7,5},{5,3},{3,1},{1,0},{8,10},{10,12},{12... | collective-permute-start | bytes 786440 | tf_op jit(solution)/shard_map/ppermute | solution.py:436
  11.2 2.0 collective-permute-start.16
  13.6 1.3 fusion.3
  14.9 2.6 %compare_reduce_fusion = pred[4,8,256]{2,1,0:T(8,128)(4,1)S(1)} fusion(s32[256]{0:T(256)S(1)} %bitcast.29, s32[4,8,256]{2,1,0:T(8,128)S(1)} %broadcast_add_fusion), kind=kLoop, calls=%fused_computation | loop fusion | flops 4186112 | bytes 41984 | tf_op jit(solution)/shard_map/reduce_or | solution.py:465
  17.5 6.2 %collective-permute-done.16.refs_1_ = bf16[32,4096]{1,0:T(8,128)(2,1)S(1)} collective-permute-done((bf16[32,4096]{1,0:T(8,128)(2,1)S(1)}, bf16[32,4096]{1,0:T(8,128)(2,1)S(1)}, u32[]{:S(2)}, u32[]{:S(2)}) %collective-permute-start.16) | collective-permute-done | bytes 262176 | tf_op jit(solution)/shard_map/ppermute | solution.py:436
  23.7 1.8 collective-permute-start.18
  27.6 1.8 collective-permute-start.10
  30.3 2.6 %collective-permute-done.18.refs_3_ = bf16[32,4096]{1,0:T(8,128)(2,1)S(1)} collective-permute-done((bf16[32,4096]{1,0:T(8,128)(2,1)S(1)}, bf16[32,4096]{1,0:T(8,128)(2,1)S(1)}, u32[]{:S(2)}, u32[]{:S(2)}) %collective-permute-start.18) | collective-permute-done | bytes 262176 | tf_op jit(solution)/shard_map/ppermute | solution.py:436
  32.9 1.8 collective-permute-start.20
  35.7 2.8 %collective-permute-done.10.refs_3_ = bf16[32,4096]{1,0:T(8,128)(2,1)S(1)} collective-permute-done((bf16[32,4096]{1,0:T(8,128)(2,1)S(1)}, bf16[32,4096]{1,0:T(8,128)(2,1)S(1)}, u32[]{:S(2)}, u32[]{:S(2)}) %collective-permute-start.10) | collective-permute-done | bytes 262176 | tf_op jit(solution)/shard_map/ppermute | solution.py:436
  38.5 1.8 collective-permute-start.12
  40.6 3.5 %collective-permute-done.20.refs_5_ = bf16[32,4096]{1,0:T(8,128)(2,1)S(1)} collective-permute-done((bf16[32,4096]{1,0:T(8,128)(2,1)S(1)}, bf16[32,4096]{1,0:T(8,128)(2,1)S(1)}, u32[]{:S(2)}, u32[]{:S(2)}) %collective-permute-start.20) | collective-permute-done | bytes 262176 | tf_op jit(solution)/shard_map/ppermute | solution.py:436
  44.1 0.7 slice.100
  44.8 1.8 collective-permute-start.22
  47.5 0.7 dynamic-slice_bitcast_fusion.place_ref
  48.2 1.5 collective-permute-done.12.refs_5_
  49.8 1.9 collective-permute-start.14
  52.5 1.6 collective-permute-done.23.refs_8_
  54.1 2.2 copy-done.1
  56.3 5.6 %project.2 = (f32[256,1024]{1,0:T(8,128)S(1)}, f32[256,256]{1,0:T(8,128)S(1)}) custom-call(s32[8]{0:T(128)S(1)} %dynamic-slice_bitcast_fusion.place_ref, bf16[32,4096]{1,0:T(8,128)(2,1)S(1)} %get-tuple-element.77.refs_0_, bf16[32,4096]{1,0:T(8,128)(2,1)S(1)} %collective-permute-done.16.refs_1_, bf16[32,4096]{1,0:T(8,128)(2,1)S(1)} %collective-permute-done.17.refs_2_, ...), custom_call_target="tpu_custom_call" | custom-call | flops 2684354560 | bytes 15204352 | tf_op jit(solution)/shard_map/project/pallas_call | solution.py:104
  62.0 4.6 %select_docs.1 = (bf16[2,4,256,128]{3,2,1,0:T(8,128)(2,1)S(1)}, bf16[2,4,256,128]{3,2,1,0:T(8,128)(2,1)}, bf16[2,4,256,128]{3,2,1,0:T(8,128)(2,1)}, bf16[2,4,256...) custom-call(s32[4]{0:T(128)S(1)} %get-tuple-element.93.place_ref, ...), custom_call_target="tpu_custom_call" | custom-call | bytes 8388608 | tf_op jit(solution)/shard_map/select_docs/pallas_call | solution.py:155
  66.6 0.8 copy-done.7
  67.6 1.8 collective-permute-start.6
  69.5 5.7 %project.3 = (f32[256,1024]{1,0:T(8,128)S(1)}, f32[256,256]{1,0:T(8,128)S(1)}) custom-call(s32[8]{0:T(128)S(1)} %dynamic-slice_bitcast_fusion.place_ref, bf16[32,4096]{1,0:T(8,128)(2,1)S(1)} %get-tuple-element.78.refs_0_, bf16[32,4096]{1,0:T(8,128)(2,1)S(1)} %collective-permute-done.8.refs_1_, bf16[32,4096]{1,0:T(8,128)(2,1)S(1)} %collective-permute-done.9.refs_2_, ...), custom_call_target="tpu_custom_call" | custom-call | flops 2684354560 | bytes 15204352 | tf_op jit(solution)/shard_map/project/pallas_call | solution.py:104
  75.2 1.0 copy-done.3
  76.2 1.7 collective-permute-start.25
  77.9 0.8 collective-permute-start.24
  78.8 5.2 %collective-permute-start.7 = (bf16[2,4,256,128]{3,2,1,0:T(8,128)(2,1)}, bf16[2,4,256,128]{3,2,1,0:T(8,128)(2,1)S(1)}, u32[]{:S(2)}, u32[]{:S(2)}) collective-permute-start(bf16[2,4,256,128]{3,2,1,0:T(8,128)(2,1)} %get-tuple-element.49), channel_id=1, source_target_pairs={{0,3},{1,2},{2,1},{3,0},{4,7},{5,6},{6,5},{7,4},{8,11},{9,10},{10,... | collective-permute-start | bytes 1572872 | tf_op jit(solution)/shard_map/ppermute | solution.py:456
  84.6 3.2 %collective-permute-start.2 = (bf16[2,4,256,128]{3,2,1,0:T(8,128)(2,1)}, bf16[2,4,256,128]{3,2,1,0:T(8,128)(2,1)S(1)}, u32[]{:S(2)}, u32[]{:S(2)}) collective-permute-start(bf16[2,4,256,128]{3,2,1,0:T(8,128)(2,1)} %copy-done.5), channel_id=1, source_target_pairs={{0,5},{1,4},{2,7},{3,6},{4,1},{5,0},{6,3},{7,2},{8,13},{9,12},{10,... | collective-permute-start | bytes 1572872 | tf_op jit(solution)/shard_map/ppermute | solution.py:456
  87.8 1.8 collective-permute-start.3
  89.7 5.4 %collective-permute-start.4 = (bf16[2,4,256,128]{3,2,1,0:T(8,128)(2,1)S(1)}, bf16[2,4,256,128]{3,2,1,0:T(8,128)(2,1)S(1)}, u32[]{:S(2)}, u32[]{:S(2)}) collective-permute-start(bf16[2,4,256,128]{3,2,1,0:T(8,128)(2,1)S(1)} %get-tuple-element.45), channel_id=1, source_target_pairs={{0,7},{1,6},{2,5},{3,4},{4,3},{5,2},{6,1},{7,0},{8,15},{9,14},{10,... | collective-permute-start | bytes 1572872 | tf_op jit(solution)/shard_map/ppermute | solution.py:456
  95.2 6.0 %collective-permute-done.7.refs_3_ = bf16[2,4,256,128]{3,2,1,0:T(8,128)(2,1)S(1)} collective-permute-done((bf16[2,4,256,128]{3,2,1,0:T(8,128)(2,1)}, bf16[2,4,256,128]{3,2,1,0:T(8,128)(2,1)S(1)}, u32[]{:S(2)}, u32[]{:S(2)}) %collective-permute-start.7) | collective-permute-done | bytes 524320 | tf_op jit(solution)/shard_map/ppermute | solution.py:456
  101.9 1.2 copy-done.4
  103.1 1.0 copy-done.8
  104.2 23.5 %attend.2 = (bf16[8,128,256]{2,1,0:T(8,128)(2,1)S(1)}, f32[8,1,256]{2,1,0:T(1,128)S(1)}, f32[8,1,256]{2,1,0:T(1,128)S(1)}, f32[8,128,256]{2,1,0:T(8,128)S(1)}) custom-call(s32[16]{0:T(128)S(1)} %reshape.123.first_ref, s32[8]{0:T(128)S(1)} %bitcast.22, s32[8]{0:T(128)S(1)} %bitcast.24, bf16[2,4,256,128]{3,2,1,0:T(8,128)(2,1)S(1)} %copy-done.8, ...), custom_call_target="tpu_custom_call" | custom-call | flops 2147483648 | bytes 2097152 | tf_op jit(solution)/shard_map/attend/pallas_call | solution.py:318
  127.7 17.8 %collective-permute-done.1.refs_0_ = bf16[2,4,256,128]{3,2,1,0:T(8,128)(2,1)S(1)} collective-permute-done((bf16[2,4,256,128]{3,2,1,0:T(8,128)(2,1)}, bf16[2,4,256,128]{3,2,1,0:T(8,128)(2,1)S(1)}, u32[]{:S(2)}, u32[]{:S(2)}) %collective-permute-start.1) | collective-permute-done | bytes 524320 | tf_op jit(solution)/shard_map/ppermute | solution.py:456
  145.5 10.6 %collective-permute-done.2.refs_1_ = bf16[2,4,256,128]{3,2,1,0:T(8,128)(2,1)S(1)} collective-permute-done((bf16[2,4,256,128]{3,2,1,0:T(8,128)(2,1)}, bf16[2,4,256,128]{3,2,1,0:T(8,128)(2,1)S(1)}, u32[]{:S(2)}, u32[]{:S(2)}) %collective-permute-start.2) | collective-permute-done | bytes 524320 | tf_op jit(solution)/shard_map/ppermute | solution.py:456
  156.7 16.9 %attend.3.x_ref = bf16[256,1024]{1,0:T(8,128)(2,1)S(1)} custom-call(s32[16]{0:T(128)S(1)} %reshape.122.first_ref, s32[8]{0:T(128)S(1)} %bitcast.23, s32[8]{0:T(128)S(1)} %bitcast.25, bf16[2,4,256,128]{3,2,1,0:T(8,128)(2,1)S(1)} %collective-permute-done.1.refs_0_, bf16[2,4,256,128]{3,2,1,0:T(8,128)(2,1)S(1)} %collective-permute-done.2.refs_1_, ...), custom_call_target="tpu_custom_call" | custom-call | flops 2147483648 | bytes 2097152 | tf_op jit(solution)/shard_map/attend/pallas_call | solution.py:318
  173.6 5.8 %copy-done = bf16[1024,8192]{1,0:T(8,128)(2,1)S(1)} copy-done((bf16[1024,8192]{1,0:T(8,128)(2,1)S(1)}, bf16[1024,8192]{1,0:T(8,128)(2,1)}, u32[]{:S(2)}) %copy-start) | copy-done | bytes 16777240
  179.4 5.4 %project_out.3 = (f32[32,4096]{1,0:T(8,128)S(1)}, f32[32,4096]{1,0:T(8,128)S(1)}, f32[32,4096]{1,0:T(8,128)S(1)}, f32[32,4096]{1,0:T(8,128)S(1)}, f32[32,4096]{1...) custom-call(s32[8]{0:T(128)S(1)} %dynamic-slice_bitcast_fusion.place, ...), custom_call_target="tpu_custom_call" | custom-call | flops 2147483648 | bytes 13107200 | tf_op jit(solution)/shard_map/project_out/pallas_call | solution.py:371
  184.8 2.1 collective-permute-start.38
  187.0 17.0 %collective-permute-start.34 = (bf16[32,2048]{1,0:T(8,128)(2,1)S(1)}, bf16[32,2048]{1,0:T(8,128)(2,1)S(1)}, u32[]{:S(2)}, u32[]{:S(2)}) collective-permute-start(bf16[32,2048]{1,0:T(8,128)(2,1)S(1)} %get-tuple-element.72), channel_id=1, source_target_pairs={{0,2},{2,4},{4,6},{6,7},{7,5},{5,3},{3,1},{1,0},{8,10},{10,12},{12... | collective-permute-start | bytes 393224 | tf_op jit(solution)/shard_map/ppermute | solution.py:518
  204.0 5.4 %project_out.2 = (f32[32,4096]{1,0:T(8,128)S(1)}, f32[32,4096]{1,0:T(8,128)S(1)}, f32[32,4096]{1,0:T(8,128)S(1)}, f32[32,4096]{1,0:T(8,128)S(1)}, f32[32,4096]{1...) custom-call(s32[8]{0:T(128)S(1)} %dynamic-slice_bitcast_fusion.place, ...), custom_call_target="tpu_custom_call" | custom-call | flops 2147483648 | bytes 13107200 | tf_op jit(solution)/shard_map/project_out/pallas_call | solution.py:371
  209.4 1.7 collective-permute-start.30
  211.2 1.2 collective-permute-start.26
  212.5 1.8 collective-permute-start.39
  214.7 1.9 collective-permute-done.30
  216.7 1.4 collective-permute-start.31
  219.0 3.3 %collective-permute-done.39 = bf16[32,4096]{1,0:T(8,128)(2,1)S(1)} collective-permute-done((bf16[32,4096]{1,0:T(8,128)(2,1)S(1)}, bf16[32,4096]{1,0:T(8,128)(2,1)S(1)}, u32[]{:S(2)}, u32[]{:S(2)}) %collective-permute-start.39) | collective-permute-done | bytes 262176 | tf_op jit(solution)/shard_map/ppermute | solution.py:528
  222.3 1.4 collective-permute-start.40
  224.6 3.3 %collective-permute-done.31 = bf16[32,4096]{1,0:T(8,128)(2,1)S(1)} collective-permute-done((bf16[32,4096]{1,0:T(8,128)(2,1)S(1)}, bf16[32,4096]{1,0:T(8,128)(2,1)S(1)}, u32[]{:S(2)}, u32[]{:S(2)}) %collective-permute-start.31) | collective-permute-done | bytes 262176 | tf_op jit(solution)/shard_map/ppermute | solution.py:528
  227.9 1.4 collective-permute-start.32
  230.2 3.3 %collective-permute-done.40 = bf16[32,4096]{1,0:T(8,128)(2,1)S(1)} collective-permute-done((bf16[32,4096]{1,0:T(8,128)(2,1)S(1)}, bf16[32,4096]{1,0:T(8,128)(2,1)S(1)}, u32[]{:S(2)}, u32[]{:S(2)}) %collective-permute-start.40) | collective-permute-done | bytes 262176 | tf_op jit(solution)/shard_map/ppermute | solution.py:528
  233.6 1.4 collective-permute-start.41
  235.8 3.3 %collective-permute-done.32 = bf16[32,4096]{1,0:T(8,128)(2,1)S(1)} collective-permute-done((bf16[32,4096]{1,0:T(8,128)(2,1)S(1)}, bf16[32,4096]{1,0:T(8,128)(2,1)S(1)}, u32[]{:S(2)}, u32[]{:S(2)}) %collective-permute-start.32) | collective-permute-done | bytes 262176 | tf_op jit(solution)/shard_map/ppermute | solution.py:528
  239.2 1.4 collective-permute-start.33
  241.4 3.3 %collective-permute-done.41 = bf16[32,4096]{1,0:T(8,128)(2,1)S(1)} collective-permute-done((bf16[32,4096]{1,0:T(8,128)(2,1)S(1)}, bf16[32,4096]{1,0:T(8,128)(2,1)S(1)}, u32[]{:S(2)}, u32[]{:S(2)}) %collective-permute-start.41) | collective-permute-done | bytes 262176 | tf_op jit(solution)/shard_map/ppermute | solution.py:528
  244.7 1.9 collective-permute-done.37
  246.7 3.0 %collective-permute-done.33 = bf16[32,4096]{1,0:T(8,128)(2,1)S(1)} collective-permute-done((bf16[32,4096]{1,0:T(8,128)(2,1)S(1)}, bf16[32,4096]{1,0:T(8,128)(2,1)S(1)}, u32[]{:S(2)}, u32[]{:S(2)}) %collective-permute-start.33) | collective-permute-done | bytes 262176 | tf_op jit(solution)/shard_map/ppermute | solution.py:528
  249.7 1.5 collective-permute-done.29
  251.3 0.8 pad_maximum_fusion
  (138 shorter events, 14.4 us)
Async XLA Ops:
  2.5 10.7 %copy-start.19 = (s32[1,256]{1,0:T(1,128)S(1)}, s32[1,256]{1,0:T(1,128)}, u32[]{:S(2)}) copy-start(s32[1,256]{1,0:T(1,128)} %param.18) | copy-start | bytes 3076
  2.5 10.7 %copy-start.21 = (s32[1,4]{1,0:T(1,128)S(1)}, s32[1,4]{1,0:T(1,128)}, u32[]{:S(2)}) copy-start(s32[1,4]{1,0:T(1,128)} %param.17) | copy-start | bytes 52
  2.5 38.0 %copy-start.20 = (s32[4]{0:T(128)S(1)}, s32[4]{0:T(128)}, u32[]{:S(2)}) copy-start(s32[4]{0:T(128)} %param.16) | copy-start | bytes 52
  8.0 53.9 %collective-permute-start = (bf16[4,2,256,1024]{3,2,1,0:T(8,128)(2,1)}, bf16[4,2,256,1024]{3,2,1,0:T(8,128)(2,1)}, u32[]{:S(2)}, u32[]{:S(2)}) collective-permute-start(bf16[4,2,256,1024]{3,2,1,0:T(8,128)(2,1)} %bitcast.21.refs_0_), channel_id=1, source_target_pairs={{8,0},{0,8},{9,1},{1,9},{10,2},{2,10},{11,3},{3,11},{12,4},{4,12},... | collective-permute-start | bytes 12582920 | tf_op jit(solution)/shard_map/ppermute | solution.py:450
  8.5 19.1 %collective-permute-start.8 = (bf16[32,4096]{1,0:T(8,128)(2,1)S(1)}, bf16[32,4096]{1,0:T(8,128)(2,1)S(1)}, u32[]{:S(2)}, u32[]{:S(2)}) collective-permute-start(bf16[32,4096]{1,0:T(8,128)(2,1)S(1)} %get-tuple-element.78.refs_0_), channel_id=1, source_target_pairs={{0,2},{2,4},{4,6},{6,7},{7,5},{5,3},{3,1},{1,0},{8,10},{10,12},{12... | collective-permute-start | bytes 786440 | tf_op jit(solution)/shard_map/ppermute | solution.py:436
  11.2 18.2 %collective-permute-start.9 = (bf16[32,4096]{1,0:T(8,128)(2,1)S(1)}, bf16[32,4096]{1,0:T(8,128)(2,1)S(1)}, u32[]{:S(2)}, u32[]{:S(2)}) collective-permute-start(bf16[32,4096]{1,0:T(8,128)(2,1)S(1)} %get-tuple-element.78.refs_0_), channel_id=1, source_target_pairs={{2,0},{4,2},{6,4},{7,6},{5,7},{3,5},{1,3},{0,1},{10,8},{12,10},{14... | collective-permute-start | bytes 786440 | tf_op jit(solution)/shard_map/ppermute | solution.py:437
  11.2 12.5 %collective-permute-start.16 = (bf16[32,4096]{1,0:T(8,128)(2,1)S(1)}, bf16[32,4096]{1,0:T(8,128)(2,1)S(1)}, u32[]{:S(2)}, u32[]{:S(2)}) collective-permute-start(bf16[32,4096]{1,0:T(8,128)(2,1)S(1)} %get-tuple-element.77.refs_0_), channel_id=1, source_target_pairs={{0,2},{2,4},{4,6},{6,7},{7,5},{5,3},{3,1},{1,0},{8,10},{10,12},{12... | collective-permute-start | bytes 786440 | tf_op jit(solution)/shard_map/ppermute | solution.py:436
  13.2 12.3 %collective-permute-start.17 = (bf16[32,4096]{1,0:T(8,128)(2,1)S(1)}, bf16[32,4096]{1,0:T(8,128)(2,1)S(1)}, u32[]{:S(2)}, u32[]{:S(2)}) collective-permute-start(bf16[32,4096]{1,0:T(8,128)(2,1)S(1)} %get-tuple-element.77.refs_0_), channel_id=1, source_target_pairs={{2,0},{4,2},{6,4},{7,6},{5,7},{3,5},{1,3},{0,1},{10,8},{12,10},{14... | collective-permute-start | bytes 786440 | tf_op jit(solution)/shard_map/ppermute | solution.py:437
  23.7 9.2 %collective-permute-start.18 = (bf16[32,4096]{1,0:T(8,128)(2,1)S(1)}, bf16[32,4096]{1,0:T(8,128)(2,1)S(1)}, u32[]{:S(2)}, u32[]{:S(2)}) collective-permute-start(bf16[32,4096]{1,0:T(8,128)(2,1)S(1)} %collective-permute-done.16.refs_1_), channel_id=1, source_target_pairs={{0,2},{2,4},{4,6},{6,7},{7,5},{5,3},{3,1},{1,0},{8,10},{10,12},{12... | collective-permute-start | bytes 786440 | tf_op jit(solution)/shard_map/ppermute | solution.py:436
  25.5 9.3 %collective-permute-start.19 = (bf16[32,4096]{1,0:T(8,128)(2,1)S(1)}, bf16[32,4096]{1,0:T(8,128)(2,1)}, u32[]{:S(2)}, u32[]{:S(2)}) collective-permute-start(bf16[32,4096]{1,0:T(8,128)(2,1)S(1)} %collective-permute-done.17.refs_2_), channel_id=1, source_target_pairs={{2,0},{4,2},{6,4},{7,6},{5,7},{3,5},{1,3},{0,1},{10,8},{12,10},{14... | collective-permute-start | bytes 786440 | tf_op jit(solution)/shard_map/ppermute | solution.py:437
  27.6 8.1 %copy-start.12 = (s32[8,32]{1,0:T(8,128)}, s32[8,32]{1,0:T(8,128)S(1)}, u32[]{:S(2)}) copy-start(s32[8,32]{1,0:T(8,128)S(1)} %reshape_squeeze.4) | copy-start | bytes 3076
  27.6 10.9 %collective-permute-start.10 = (bf16[32,4096]{1,0:T(8,128)(2,1)S(1)}, bf16[32,4096]{1,0:T(8,128)(2,1)S(1)}, u32[]{:S(2)}, u32[]{:S(2)}) collective-permute-start(bf16[32,4096]{1,0:T(8,128)(2,1)S(1)} %collective-permute-done.8.refs_1_), channel_id=1, source_target_pairs={{0,2},{2,4},{4,6},{6,7},{7,5},{5,3},{3,1},{1,0},{8,10},{10,12},{12... | collective-permute-start | bytes 786440 | tf_op jit(solution)/shard_map/ppermute | solution.py:436
  29.4 11.0 %collective-permute-start.11 = (bf16[32,4096]{1,0:T(8,128)(2,1)S(1)}, bf16[32,4096]{1,0:T(8,128)(2,1)S(1)}, u32[]{:S(2)}, u32[]{:S(2)}) collective-permute-start(bf16[32,4096]{1,0:T(8,128)(2,1)S(1)} %collective-permute-done.9.refs_2_), channel_id=1, source_target_pairs={{2,0},{4,2},{6,4},{7,6},{5,7},{3,5},{1,3},{0,1},{10,8},{12,10},{14... | collective-permute-start | bytes 786440 | tf_op jit(solution)/shard_map/ppermute | solution.py:437
  32.9 11.2 %collective-permute-start.20 = (bf16[32,4096]{1,0:T(8,128)(2,1)S(1)}, bf16[32,4096]{1,0:T(8,128)(2,1)S(1)}, u32[]{:S(2)}, u32[]{:S(2)}) collective-permute-start(bf16[32,4096]{1,0:T(8,128)(2,1)S(1)} %collective-permute-done.18.refs_3_), channel_id=1, source_target_pairs={{0,2},{2,4},{4,6},{6,7},{7,5},{5,3},{3,1},{1,0},{8,10},{10,12},{12... | collective-permute-start | bytes 786440 | tf_op jit(solution)/shard_map/ppermute | solution.py:436
  34.9 11.8 %collective-permute-start.21 = (bf16[32,4096]{1,0:T(8,128)(2,1)}, bf16[32,4096]{1,0:T(8,128)(2,1)S(1)}, u32[]{:S(2)}, u32[]{:S(2)}) collective-permute-start(bf16[32,4096]{1,0:T(8,128)(2,1)} %collective-permute-done.19.refs_4_), channel_id=1, source_target_pairs={{2,0},{4,2},{6,4},{7,6},{5,7},{3,5},{1,3},{0,1},{10,8},{12,10},{14... | collective-permute-start | bytes 786440 | tf_op jit(solution)/shard_map/ppermute | solution.py:437
  38.5 11.2 %collective-permute-start.12 = (bf16[32,4096]{1,0:T(8,128)(2,1)S(1)}, bf16[32,4096]{1,0:T(8,128)(2,1)S(1)}, u32[]{:S(2)}, u32[]{:S(2)}) collective-permute-start(bf16[32,4096]{1,0:T(8,128)(2,1)S(1)} %collective-permute-done.10.refs_3_), channel_id=1, source_target_pairs={{0,2},{2,4},{4,6},{6,7},{7,5},{5,3},{3,1},{1,0},{8,10},{10,12},{12... | collective-permute-start | bytes 786440 | tf_op jit(solution)/shard_map/ppermute | solution.py:436
  40.4 11.3 %collective-permute-start.13 = (bf16[32,4096]{1,0:T(8,128)(2,1)S(1)}, bf16[32,4096]{1,0:T(8,128)(2,1)S(1)}, u32[]{:S(2)}, u32[]{:S(2)}) collective-permute-start(bf16[32,4096]{1,0:T(8,128)(2,1)S(1)} %collective-permute-done.11.refs_4_), channel_id=1, source_target_pairs={{2,0},{4,2},{6,4},{7,6},{5,7},{3,5},{1,3},{0,1},{10,8},{12,10},{14... | collective-permute-start | bytes 786440 | tf_op jit(solution)/shard_map/ppermute | solution.py:437
  44.8 7.8 %collective-permute-start.22 = (bf16[32,2048]{1,0:T(8,128)(2,1)}, bf16[32,2048]{1,0:T(8,128)(2,1)S(1)}, u32[]{:S(2)}, u32[]{:S(2)}) collective-permute-start(bf16[32,2048]{1,0:T(8,128)(2,1)} %slice.100), channel_id=1, source_target_pairs={{0,2},{2,4},{4,6},{6,7},{7,5},{5,3},{3,1},{1,0},{8,10},{10,12},{12... | collective-permute-start | bytes 393224 | tf_op jit(solution)/shard_map/ppermute | solution.py:439
  47.3 6.8 %collective-permute-start.23 = (bf16[32,2048]{1,0:T(8,128)(2,1)}, bf16[32,2048]{1,0:T(8,128)(2,1)}, u32[]{:S(2)}, u32[]{:S(2)}) collective-permute-start(bf16[32,2048]{1,0:T(8,128)(2,1)} %slice.101), channel_id=1, source_target_pairs={{2,0},{4,2},{6,4},{7,6},{5,7},{3,5},{1,3},{0,1},{10,8},{12,10},{14... | collective-permute-start | bytes 393224 | tf_op jit(solution)/shard_map/ppermute | solution.py:440
  49.8 19.6 %collective-permute-start.14 = (bf16[32,2048]{1,0:T(8,128)(2,1)S(1)}, bf16[32,2048]{1,0:T(8,128)(2,1)S(1)}, u32[]{:S(2)}, u32[]{:S(2)}) collective-permute-start(bf16[32,2048]{1,0:T(8,128)(2,1)S(1)} %slice.98), channel_id=1, source_target_pairs={{0,2},{2,4},{4,6},{6,7},{7,5},{5,3},{3,1},{1,0},{8,10},{10,12},{12... | collective-permute-start | bytes 393224 | tf_op jit(solution)/shard_map/ppermute | solution.py:439
  51.6 17.7 %collective-permute-start.15 = (bf16[32,2048]{1,0:T(8,128)(2,1)S(1)}, bf16[32,2048]{1,0:T(8,128)(2,1)S(1)}, u32[]{:S(2)}, u32[]{:S(2)}) collective-permute-start(bf16[32,2048]{1,0:T(8,128)(2,1)S(1)} %slice.99), channel_id=1, source_target_pairs={{2,0},{4,2},{6,4},{7,6},{5,7},{3,5},{1,3},{0,1},{10,8},{12,10},{14... | collective-permute-start | bytes 393224 | tf_op jit(solution)/shard_map/ppermute | solution.py:440
  54.1 2.2 copy-start.1
  62.0 7.4 %copy-start.2 = (bf16[8192,256]{1,0:T(8,128)(2,1)S(1)}, bf16[8192,256]{1,0:T(8,128)(2,1)}, u32[]{:S(2)}) copy-start(bf16[8192,256]{1,0:T(8,128)(2,1)} %refs_10_.3) | copy-start | bytes 12582916
  66.6 0.8 copy-start.7
  67.4 7.8 %copy-start.5 = (bf16[2,4,256,128]{3,2,1,0:T(8,128)(2,1)}, bf16[2,4,256,128]{3,2,1,0:T(8,128)(2,1)S(1)}, u32[]{:S(2)}) copy-start(bf16[2,4,256,128]{3,2,1,0:T(8,128)(2,1)S(1)} %get-tuple-element.43) | copy-start | bytes 1572868
  67.4 7.8 %copy-start.6 = (bf16[2,4,256,128]{3,2,1,0:T(8,128)(2,1)}, bf16[2,4,256,128]{3,2,1,0:T(8,128)(2,1)S(1)}, u32[]{:S(2)}) copy-start(bf16[2,4,256,128]{3,2,1,0:T(8,128)(2,1)S(1)} %get-tuple-element.42) | copy-start | bytes 1572868
  67.4 20.4 %collective-permute-start.5 = (bf16[2,4,256,128]{3,2,1,0:T(8,128)(2,1)}, bf16[2,4,256,128]{3,2,1,0:T(8,128)(2,1)}, u32[]{:S(2)}, u32[]{:S(2)}) collective-permute-start(bf16[2,4,256,128]{3,2,1,0:T(8,128)(2,1)} %get-tuple-element.47), channel_id=1, source_target_pairs={{0,1},{1,0},{2,3},{3,2},{4,5},{5,4},{6,7},{7,6},{8,9},{9,8},{10,11... | collective-permute-start | bytes 1572872 | tf_op jit(solution)/shard_map/ppermute | solution.py:456
  67.6 22.1 %collective-permute-start.6 = (bf16[2,4,256,128]{3,2,1,0:T(8,128)(2,1)}, bf16[2,4,256,128]{3,2,1,0:T(8,128)(2,1)}, u32[]{:S(2)}, u32[]{:S(2)}) collective-permute-start(bf16[2,4,256,128]{3,2,1,0:T(8,128)(2,1)} %get-tuple-element.48), channel_id=1, source_target_pairs={{0,2},{1,3},{2,0},{3,1},{4,6},{5,7},{6,4},{7,5},{8,10},{9,11},{10,... | collective-permute-start | bytes 1572872 | tf_op jit(solution)/shard_map/ppermute | solution.py:456
  69.4 14.6 %copy-start.16 = (s32[4,8]{1,0:T(4,128)S(1)}, s32[4,8]{1,0:T(4,128)}, u32[]{:S(2)}) copy-start(s32[4,8]{1,0:T(4,128)} %add_select_fusion) | copy-start | bytes 388
  69.4 14.7 %copy-start.18 = (s32[8,1]{1,0:T(8,128)S(1)}, s32[8,1]{1,0:T(8,128)}, u32[]{:S(2)}) copy-start(s32[8,1]{1,0:T(8,128)} %get-tuple-element.86) | copy-start | bytes 100
  69.4 14.8 %copy-start.17 = (s32[8,1]{1,0:T(8,128)S(1)}, s32[8,1]{1,0:T(8,128)}, u32[]{:S(2)}) copy-start(s32[8,1]{1,0:T(8,128)} %get-tuple-element.85) | copy-start | bytes 100
  69.4 14.9 %copy-start.15 = (bf16[1,4,4,256]{3,2,1,0:T(4,128)(2,1)S(1)}, bf16[1,4,4,256]{3,2,1,0:T(4,128)(2,1)}, u32[]{:S(2)}) copy-start(bf16[1,4,4,256]{3,2,1,0:T(4,128)(2,1)} %get-tuple-element.84) | copy-start | bytes 24580
  69.4 14.9 %copy-start.13 = (s32[8,32]{1,0:T(8,128)S(1)}, s32[8,32]{1,0:T(8,128)}, u32[]{:S(2)}) copy-start(s32[8,32]{1,0:T(8,128)} %copy-done.12) | copy-start | bytes 3076
  69.4 15.1 %copy-start.14 = (bf16[1,4,4,256]{3,2,1,0:T(4,128)(2,1)S(1)}, bf16[1,4,4,256]{3,2,1,0:T(4,128)(2,1)}, u32[]{:S(2)}) copy-start(bf16[1,4,4,256]{3,2,1,0:T(4,128)(2,1)} %get-tuple-element.83) | copy-start | bytes 24580
  69.4 25.6 %copy-start.9 = (f32[256,64]{1,0:T(8,128)S(1)}, f32[256,64]{1,0:T(8,128)}, u32[]{:S(2)}) copy-start(f32[256,64]{1,0:T(8,128)} %get-tuple-element.89) | copy-start | bytes 196612
  69.4 25.6 %copy-start.10 = (f32[256,64]{1,0:T(8,128)S(1)}, f32[256,64]{1,0:T(8,128)}, u32[]{:S(2)}) copy-start(f32[256,64]{1,0:T(8,128)} %get-tuple-element.90) | copy-start | bytes 196612
  69.4 25.6 %copy-start.11 = (f32[256,64]{1,0:T(8,128)S(1)}, f32[256,64]{1,0:T(8,128)}, u32[]{:S(2)}) copy-start(f32[256,64]{1,0:T(8,128)} %get-tuple-element.91) | copy-start | bytes 196612
  75.2 1.0 copy-start.3
  76.2 8.3 %collective-permute-start.25 = (bf16[256,128]{1,0:T(8,128)(2,1)S(1)}, bf16[256,128]{1,0:T(8,128)(2,1)S(1)}, u32[]{:S(2)}, u32[]{:S(2)}) collective-permute-start(bf16[256,128]{1,0:T(8,128)(2,1)S(1)} %get-tuple-element.81), channel_id=1, source_target_pairs={{0,1},{1,3},{2,5},{3,7},{4,0},{5,2},{6,4},{7,6},{8,9},{9,11},{10,1... | collective-permute-start | bytes 196616 | tf_op jit(solution)/shard_map/ppermute | solution.py:482
  77.9 6.7 %collective-permute-start.24 = (bf16[256,128]{1,0:T(8,128)(2,1)S(1)}, bf16[256,128]{1,0:T(8,128)(2,1)S(1)}, u32[]{:S(2)}, u32[]{:S(2)}) collective-permute-start(bf16[256,128]{1,0:T(8,128)(2,1)S(1)} %get-tuple-element.82), channel_id=1, source_target_pairs={{0,0},{1,2},{2,4},{3,6},{4,1},{5,3},{6,5},{7,7},{8,8},{9,10},{10,1... | collective-permute-start | bytes 196616 | tf_op jit(solution)/shard_map/ppermute | solution.py:477
  78.8 22.5 %collective-permute-start.7 = (bf16[2,4,256,128]{3,2,1,0:T(8,128)(2,1)}, bf16[2,4,256,128]{3,2,1,0:T(8,128)(2,1)S(1)}, u32[]{:S(2)}, u32[]{:S(2)}) collective-permute-start(bf16[2,4,256,128]{3,2,1,0:T(8,128)(2,1)} %get-tuple-element.49), channel_id=1, source_target_pairs={{0,3},{1,2},{2,1},{3,0},{4,7},{5,6},{6,5},{7,4},{8,11},{9,10},{10,... | collective-permute-start | bytes 1572872 | tf_op jit(solution)/shard_map/ppermute | solution.py:456
  84.5 61.0 %collective-permute-start.1 = (bf16[2,4,256,128]{3,2,1,0:T(8,128)(2,1)}, bf16[2,4,256,128]{3,2,1,0:T(8,128)(2,1)S(1)}, u32[]{:S(2)}, u32[]{:S(2)}) collective-permute-start(bf16[2,4,256,128]{3,2,1,0:T(8,128)(2,1)} %copy-done.6), channel_id=1, source_target_pairs={{0,4},{1,5},{2,6},{3,7},{4,0},{5,1},{6,2},{7,3},{8,12},{9,13},{10,... | collective-permute-start | bytes 1572872 | tf_op jit(solution)/shard_map/ppermute | solution.py:456
  84.6 71.5 %collective-permute-start.2 = (bf16[2,4,256,128]{3,2,1,0:T(8,128)(2,1)}, bf16[2,4,256,128]{3,2,1,0:T(8,128)(2,1)S(1)}, u32[]{:S(2)}, u32[]{:S(2)}) collective-permute-start(bf16[2,4,256,128]{3,2,1,0:T(8,128)(2,1)} %copy-done.5), channel_id=1, source_target_pairs={{0,5},{1,4},{2,7},{3,6},{4,1},{5,0},{6,3},{7,2},{8,13},{9,12},{10,... | collective-permute-start | bytes 1572872 | tf_op jit(solution)/shard_map/ppermute | solution.py:456
  87.8 68.3 %collective-permute-start.3 = (bf16[2,4,256,128]{3,2,1,0:T(8,128)(2,1)S(1)}, bf16[2,4,256,128]{3,2,1,0:T(8,128)(2,1)S(1)}, u32[]{:S(2)}, u32[]{:S(2)}) collective-permute-start(bf16[2,4,256,128]{3,2,1,0:T(8,128)(2,1)S(1)} %get-tuple-element.44), channel_id=1, source_target_pairs={{0,6},{1,7},{2,4},{3,5},{4,2},{5,3},{6,0},{7,1},{8,14},{9,15},{10,... | collective-permute-start | bytes 1572872 | tf_op jit(solution)/shard_map/ppermute | solution.py:456
  89.7 66.5 %collective-permute-start.4 = (bf16[2,4,256,128]{3,2,1,0:T(8,128)(2,1)S(1)}, bf16[2,4,256,128]{3,2,1,0:T(8,128)(2,1)S(1)}, u32[]{:S(2)}, u32[]{:S(2)}) collective-permute-start(bf16[2,4,256,128]{3,2,1,0:T(8,128)(2,1)S(1)} %get-tuple-element.45), channel_id=1, source_target_pairs={{0,7},{1,6},{2,5},{3,4},{4,3},{5,2},{6,1},{7,0},{8,15},{9,14},{10,... | collective-permute-start | bytes 1572872 | tf_op jit(solution)/shard_map/ppermute | solution.py:456
  101.9 1.2 copy-start.4
  103.1 1.0 copy-start.8
  173.6 5.8 %copy-start = (bf16[1024,8192]{1,0:T(8,128)(2,1)S(1)}, bf16[1024,8192]{1,0:T(8,128)(2,1)}, u32[]{:S(2)}) copy-start(bf16[1024,8192]{1,0:T(8,128)(2,1)} %w_ref.3) | copy-start | bytes 50331652
  184.8 27.6 %collective-permute-start.38 = (bf16[32,2048]{1,0:T(8,128)(2,1)S(1)}, bf16[32,2048]{1,0:T(8,128)(2,1)S(1)}, u32[]{:S(2)}, u32[]{:S(2)}) collective-permute-start(bf16[32,2048]{1,0:T(8,128)(2,1)S(1)} %get-tuple-element.76), channel_id=1, source_target_pairs={{2,0},{4,2},{6,4},{7,6},{5,7},{3,5},{1,3},{0,1},{10,8},{12,10},{14... | collective-permute-start | bytes 393224 | tf_op jit(solution)/shard_map/ppermute | solution.py:519
  187.0 27.4 %collective-permute-start.34 = (bf16[32,2048]{1,0:T(8,128)(2,1)S(1)}, bf16[32,2048]{1,0:T(8,128)(2,1)S(1)}, u32[]{:S(2)}, u32[]{:S(2)}) collective-permute-start(bf16[32,2048]{1,0:T(8,128)(2,1)S(1)} %get-tuple-element.72), channel_id=1, source_target_pairs={{0,2},{2,4},{4,6},{6,7},{7,5},{5,3},{3,1},{1,0},{8,10},{10,12},{12... | collective-permute-start | bytes 393224 | tf_op jit(solution)/shard_map/ppermute | solution.py:518
  209.4 7.2 %collective-permute-start.30 = (bf16[32,2048]{1,0:T(8,128)(2,1)S(1)}, bf16[32,2048]{1,0:T(8,128)(2,1)S(1)}, u32[]{:S(2)}, u32[]{:S(2)}) collective-permute-start(bf16[32,2048]{1,0:T(8,128)(2,1)S(1)} %get-tuple-element.67), channel_id=1, source_target_pairs={{2,0},{4,2},{6,4},{7,6},{5,7},{3,5},{1,3},{0,1},{10,8},{12,10},{14... | collective-permute-start | bytes 393224 | tf_op jit(solution)/shard_map/ppermute | solution.py:519
  211.2 7.3 %collective-permute-start.26 = (bf16[32,2048]{1,0:T(8,128)(2,1)S(1)}, bf16[32,2048]{1,0:T(8,128)(2,1)S(1)}, u32[]{:S(2)}, u32[]{:S(2)}) collective-permute-start(bf16[32,2048]{1,0:T(8,128)(2,1)S(1)} %get-tuple-element.63), channel_id=1, source_target_pairs={{0,2},{2,4},{4,6},{6,7},{7,5},{5,3},{3,1},{1,0},{8,10},{10,12},{12... | collective-permute-start | bytes 393224 | tf_op jit(solution)/shard_map/ppermute | solution.py:518
  212.5 9.8 %collective-permute-start.39 = (bf16[32,4096]{1,0:T(8,128)(2,1)S(1)}, bf16[32,4096]{1,0:T(8,128)(2,1)S(1)}, u32[]{:S(2)}, u32[]{:S(2)}) collective-permute-start(bf16[32,4096]{1,0:T(8,128)(2,1)S(1)} %pad_maximum_fusion.4), channel_id=1, source_target_pairs={{2,0},{4,2},{6,4},{7,6},{5,7},{3,5},{1,3},{0,1},{10,8},{12,10},{14... | collective-permute-start | bytes 786440 | tf_op jit(solution)/shard_map/ppermute | solution.py:528
  214.4 9.8 %collective-permute-start.35 = (bf16[32,4096]{1,0:T(8,128)(2,1)S(1)}, bf16[32,4096]{1,0:T(8,128)(2,1)S(1)}, u32[]{:S(2)}, u32[]{:S(2)}) collective-permute-start(bf16[32,4096]{1,0:T(8,128)(2,1)S(1)} %pad_maximum_fusion.3), channel_id=1, source_target_pairs={{0,2},{2,4},{4,6},{6,7},{7,5},{5,3},{3,1},{1,0},{8,10},{10,12},{12... | collective-permute-start | bytes 786440 | tf_op jit(solution)/shard_map/ppermute | solution.py:527
  216.7 11.2 %collective-permute-start.31 = (bf16[32,4096]{1,0:T(8,128)(2,1)S(1)}, bf16[32,4096]{1,0:T(8,128)(2,1)S(1)}, u32[]{:S(2)}, u32[]{:S(2)}) collective-permute-start(bf16[32,4096]{1,0:T(8,128)(2,1)S(1)} %pad_maximum_fusion.2), channel_id=1, source_target_pairs={{2,0},{4,2},{6,4},{7,6},{5,7},{3,5},{1,3},{0,1},{10,8},{12,10},{14... | collective-permute-start | bytes 786440 | tf_op jit(solution)/shard_map/ppermute | solution.py:528
  218.6 11.2 %collective-permute-start.27 = (bf16[32,4096]{1,0:T(8,128)(2,1)S(1)}, bf16[32,4096]{1,0:T(8,128)(2,1)S(1)}, u32[]{:S(2)}, u32[]{:S(2)}) collective-permute-start(bf16[32,4096]{1,0:T(8,128)(2,1)S(1)} %pad_maximum_fusion.1), channel_id=1, source_target_pairs={{0,2},{2,4},{4,6},{6,7},{7,5},{5,3},{3,1},{1,0},{8,10},{10,12},{12... | collective-permute-start | bytes 786440 | tf_op jit(solution)/shard_map/ppermute | solution.py:527
  222.3 11.2 %collective-permute-start.40 = (bf16[32,4096]{1,0:T(8,128)(2,1)S(1)}, bf16[32,4096]{1,0:T(8,128)(2,1)S(1)}, u32[]{:S(2)}, u32[]{:S(2)}) collective-permute-start(bf16[32,4096]{1,0:T(8,128)(2,1)S(1)} %add_convert_fusion.2), channel_id=1, source_target_pairs={{2,0},{4,2},{6,4},{7,6},{5,7},{3,5},{1,3},{0,1},{10,8},{12,10},{14... | collective-permute-start | bytes 786440 | tf_op jit(solution)/shard_map/ppermute | solution.py:528
  224.2 11.2 %collective-permute-start.36 = (bf16[32,4096]{1,0:T(8,128)(2,1)S(1)}, bf16[32,4096]{1,0:T(8,128)(2,1)S(1)}, u32[]{:S(2)}, u32[]{:S(2)}) collective-permute-start(bf16[32,4096]{1,0:T(8,128)(2,1)S(1)} %add_convert_fusion.4), channel_id=1, source_target_pairs={{0,2},{2,4},{4,6},{6,7},{7,5},{5,3},{3,1},{1,0},{8,10},{10,12},{12... | collective-permute-start | bytes 786440 | tf_op jit(solution)/shard_map/ppermute | solution.py:527
  227.9 11.2 %collective-permute-start.32 = (bf16[32,4096]{1,0:T(8,128)(2,1)S(1)}, bf16[32,4096]{1,0:T(8,128)(2,1)S(1)}, u32[]{:S(2)}, u32[]{:S(2)}) collective-permute-start(bf16[32,4096]{1,0:T(8,128)(2,1)S(1)} %add_convert_fusion.7), channel_id=1, source_target_pairs={{2,0},{4,2},{6,4},{7,6},{5,7},{3,5},{1,3},{0,1},{10,8},{12,10},{14... | collective-permute-start | bytes 786440 | tf_op jit(solution)/shard_map/ppermute | solution.py:528
  229.8 11.2 %collective-permute-start.28 = (bf16[32,4096]{1,0:T(8,128)(2,1)S(1)}, bf16[32,4096]{1,0:T(8,128)(2,1)S(1)}, u32[]{:S(2)}, u32[]{:S(2)}) collective-permute-start(bf16[32,4096]{1,0:T(8,128)(2,1)S(1)} %add_convert_fusion.9), channel_id=1, source_target_pairs={{0,2},{2,4},{4,6},{6,7},{7,5},{5,3},{3,1},{1,0},{8,10},{10,12},{12... | collective-permute-start | bytes 786440 | tf_op jit(solution)/shard_map/ppermute | solution.py:527
  233.6 11.2 %collective-permute-start.41 = (bf16[32,4096]{1,0:T(8,128)(2,1)S(1)}, bf16[32,4096]{1,0:T(8,128)(2,1)S(1)}, u32[]{:S(2)}, u32[]{:S(2)}) collective-permute-start(bf16[32,4096]{1,0:T(8,128)(2,1)S(1)} %add_convert_fusion.1), channel_id=1, source_target_pairs={{2,0},{4,2},{6,4},{7,6},{5,7},{3,5},{1,3},{0,1},{10,8},{12,10},{14... | collective-permute-start | bytes 786440 | tf_op jit(solution)/shard_map/ppermute | solution.py:528
  235.4 11.2 %collective-permute-start.37 = (bf16[32,4096]{1,0:T(8,128)(2,1)S(1)}, bf16[32,4096]{1,0:T(8,128)(2,1)S(1)}, u32[]{:S(2)}, u32[]{:S(2)}) collective-permute-start(bf16[32,4096]{1,0:T(8,128)(2,1)S(1)} %add_convert_fusion.3), channel_id=1, source_target_pairs={{0,2},{2,4},{4,6},{6,7},{7,5},{5,3},{3,1},{1,0},{8,10},{10,12},{12... | collective-permute-start | bytes 786440 | tf_op jit(solution)/shard_map/ppermute | solution.py:527
  239.2 10.5 %collective-permute-start.33 = (bf16[32,4096]{1,0:T(8,128)(2,1)S(1)}, bf16[32,4096]{1,0:T(8,128)(2,1)S(1)}, u32[]{:S(2)}, u32[]{:S(2)}) collective-permute-start(bf16[32,4096]{1,0:T(8,128)(2,1)S(1)} %add_convert_fusion.6), channel_id=1, source_target_pairs={{2,0},{4,2},{6,4},{7,6},{5,7},{3,5},{1,3},{0,1},{10,8},{12,10},{14... | collective-permute-start | bytes 786440 | tf_op jit(solution)/shard_map/ppermute | solution.py:528
  241.1 10.2 %collective-permute-start.29 = (bf16[32,4096]{1,0:T(8,128)(2,1)S(1)}, bf16[32,4096]{1,0:T(8,128)(2,1)S(1)}, u32[]{:S(2)}, u32[]{:S(2)}) collective-permute-start(bf16[32,4096]{1,0:T(8,128)(2,1)S(1)} %add_convert_fusion.8), channel_id=1, source_target_pairs={{0,2},{2,4},{4,6},{6,7},{7,5},{5,3},{3,1},{1,0},{8,10},{10,12},{12... | collective-permute-start | bytes 786440 | tf_op jit(solution)/shard_map/ppermute | solution.py:527

commit v3 on v2

--- a/solution.py
+++ b/solution.py
@@ -23,7 +23,7 @@
 GATHER_CHUNKS = 2
 REDUCE_CHUNKS = 2
 TILE_COLS = 256
-GROUPS = 2
+PAIR = 2
 
 
 def rotation_tables(positions):
@@ -52,9 +52,9 @@
     left_ref, right_ref, wq_ref, wkv_ref = refs[n_blocks : n_blocks + 4]
     rest = refs[n_blocks + 4 :]
     if has_prev:
-        prev_q, prev_kv = rest[:2]
-        rest = rest[2:]
-    out_q, out_kv, total_q, total_kv = rest
+        prev_q, prev_kv, cos_ref, sin_ref = rest[:4]
+        rest = rest[4:]
+    out_q, out_kv, total_q, total_kv = rest[:4]
     step = pl.program_id(0)
 
     @pl.when(step == 0)
@@ -78,14 +78,31 @@
             for block in range(SEL // count):
                 here = slice(block * count, (block + 1) * count)
                 there = pl.ds(pl.multiple_of(place_ref[block] * count, count), count)
-                out_q[there, :] = total_q[here, :]
+                natural = rest[4]
+                natural[there, :] = total_q[here, :]
                 out_kv[there, :] = total_kv[here, :]
+            heads_here = total_q.shape[1] // HD
+            tile_q = TILE_COLS // heads_here
+            for tile in range(SEL // tile_q):
+                here = slice(tile * tile_q, (tile + 1) * tile_q)
+                stacked = jnp.concatenate(
+                    [
+                        rotate(
+                            natural[here, head * HD : (head + 1) * HD],
+                            cos_ref[here, :],
+                            sin_ref[here, :],
+                        )
+                        for head in range(heads_here)
+                    ],
+                    axis=0,
+                )
+                out_q[tile] = stacked.T.astype(jnp.bfloat16)
         else:
             out_q[...] = total_q[...]
             out_kv[...] = total_kv[...]
 
 
-def project(place, blocks, left, right, w_query, w_keyval, prev, chunk):
+def project(place, blocks, left, right, w_query, w_keyval, prev, tables, chunk):
     depth = 2 * left.shape[1]
     tile = left.shape[1]
     q_cols, kv_cols = w_query.shape[1], w_keyval.shape[1]
@@ -99,21 +116,28 @@
     ]
     operands = [place, *blocks, left, right, w_query, w_keyval]
     if prev is not None:
-        specs += [pl.BlockSpec((SEL, q_cols), whole), pl.BlockSpec((SEL, kv_cols), whole)]
-        operands += list(prev)
+        specs += [pl.BlockSpec(a.shape, whole) for a in (*prev, *tables)]
+        operands += [*prev, *tables]
+        q_out = ((SEL * q_cols // (HD * TILE_COLS), HD, TILE_COLS), jnp.bfloat16)
+    else:
+        q_out = ((SEL, q_cols), jnp.float32)
     return pl.pallas_call(
         functools.partial(project_kernel, len(blocks), prev is not None),
         grid=(2,),
         in_specs=specs,
-        out_specs=[pl.BlockSpec((SEL, q_cols), whole), pl.BlockSpec((SEL, kv_cols), whole)],
+        out_specs=[
+            pl.BlockSpec(q_out[0], lambda k: (0,) * len(q_out[0])),
+            pl.BlockSpec((SEL, kv_cols), whole),
+        ],
         out_shape=[
-            jax.ShapeDtypeStruct((SEL, q_cols), jnp.float32),
+            jax.ShapeDtypeStruct(*q_out),
             jax.ShapeDtypeStruct((SEL, kv_cols), jnp.float32),
         ],
         scratch_shapes=[
             pltpu.VMEM((SEL, q_cols), jnp.float32),
             pltpu.VMEM((SEL, kv_cols), jnp.float32),
-        ],
+        ]
+        + [pltpu.VMEM((SEL, q_cols), jnp.float32)] * (prev is not None),
         compiler_params=megabytes(32),
         cost_estimate=pl.CostEstimate(
             flops=2 * SEL * depth * (q_cols + kv_cols),
@@ -166,34 +190,27 @@
     )(place, slot, heads, *sources)
 
 
-def attend_kernel(n_chunks, is_first, is_last, heads_here, first_ref, qmin_ref, qmax_ref, *refs):
+def attend_kernel(n_chunks, with_new, tile_q, first_ref, qmin_ref, qmax_ref, *refs):
     refs = list(refs)
     take = lambda count: [refs.pop(0) for _ in range(count)]
     chunks = take(n_chunks)
-    dead_ref, qpos_ref = take(2)
-    if is_first:
-        q_ref, cos_ref, sin_ref, newk_ref, newv_ref = take(5)
+    dead_ref, qpos_ref, queries = take(3)
+    if with_new:
+        cos_ref, sin_ref, newk_ref, newv_ref = take(4)
+    top, total, mixed_out, values = take(4)
+    if with_new:
+        summed = mixed_out
+        new_key, new_value = take(2)
     else:
-        queries, old_top, old_total, old_summed = take(4)
-    if is_last:
-        (out_ref,) = take(1)
-        if is_first:
-            (queries,) = take(1)
-        top, total, summed = take(3)
-    else:
-        queries, top, total, summed = take(4)
-    values = take(1)[0]
-    if is_first:
-        new_key, new_value = take(2)
-    n_tiles = SEL * heads_here // TILE_COLS
-    tile_q = TILE_COLS // heads_here
+        summed = take(1)[0]
+    n_pairs = queries.shape[0] // PAIR
     tokens = chunks[0].shape[2]
     scale = math.log2(math.e) / math.sqrt(HD)
 
     for chunk in range(n_chunks):
         for doc in range(DOCS):
             values[doc, :, chunk * tokens : (chunk + 1) * tokens] = chunks[chunk][1, doc].T
-    if is_first:
+    if with_new:
         new_key[...] = rotate(
             newk_ref[...].astype(jnp.float32), cos_ref[...], sin_ref[...]
         ).astype(jnp.bfloat16)
@@ -222,34 +239,22 @@
         total[tile] = running
         summed[tile] = mixed
 
-    @pl.loop(0, n_tiles)
-    def _(tile):
-        here = pl.ds(pl.multiple_of(tile * tile_q, tile_q), tile_q)
-        if is_first:
-            stacked = jnp.concatenate(
-                [
-                    rotate(
-                        q_ref[here, head * HD : (head + 1) * HD], cos_ref[here, :], sin_ref[here, :]
-                    )
-                    for head in range(heads_here)
-                ],
-                axis=0,
-            )
-            queries[tile] = stacked.T.astype(jnp.bfloat16)
+    @pl.loop(0, n_pairs)
+    def _(pair):
+        tiles = [pair * PAIR + i for i in range(PAIR)]
+        for tile in tiles:
             top[tile] = jnp.full(top.shape[1:], MASKED, jnp.float32)
             total[tile] = jnp.zeros(total.shape[1:], jnp.float32)
             summed[tile] = jnp.zeros(summed.shape[1:], jnp.float32)
-            scores = jnp.dot(new_key[...], queries[tile], preferred_element_type=jnp.float32)
-            key_index = lax.broadcasted_iota(jnp.int32, scores.shape, 0)
-            q_index = tile * tile_q + lax.broadcasted_iota(jnp.int32, scores.shape, 1) % tile_q
-            scores = jnp.where(key_index <= q_index, scores, MASKED)
-            update(tile, [(scores, new_value[...])])
-        else:
-            top[tile] = old_top[tile]
-            total[tile] = old_total[tile]
-            summed[tile] = old_summed[tile]
-
-        extended = jnp.concatenate([queries[tile], one_row], axis=0)
+        if with_new:
+            fresh = []
+            for tile in tiles:
+                scores = jnp.dot(new_key[...], queries[tile], preferred_element_type=jnp.float32)
+                key_index = lax.broadcasted_iota(jnp.int32, scores.shape, 0)
+                q_index = tile * tile_q + lax.broadcasted_iota(jnp.int32, scores.shape, 1) % tile_q
+                fresh.append(jnp.where(key_index <= q_index, scores, MASKED))
+            for tile, scores in zip(tiles, fresh):
+                update(tile, [(scores, new_value[...])])
 
         @pl.loop(0, DOCS)
         def _(doc):
@@ -258,19 +263,28 @@
             reach = functools.reduce(jnp.maximum, firsts) + tokens - 1
 
             def visit(masked):
-                parts = []
-                for chunk in range(n_chunks):
-                    span = slice(chunk * tokens, (chunk + 1) * tokens)
-                    keys = jnp.concatenate([chunks[chunk][0, doc], dead_ref[doc, span, :]], axis=1)
-                    scores = jnp.dot(keys, extended, preferred_element_type=jnp.float32)
-                    if masked:
-                        key_pos = firsts[chunk] + lax.broadcasted_iota(jnp.int32, scores.shape, 0)
-                        scores = jnp.where(key_pos <= qpos_ref[tile], scores, MASKED)
-                    parts.append((scores, values[doc, :, span]))
-                update(tile, parts)
-
-            live = lowest <= qmax_ref[tile]
-            whole = reach <= qmin_ref[tile]
+                found = []
+                for tile in tiles:
+                    extended = jnp.concatenate([queries[tile], one_row], axis=0)
+                    parts = []
+                    for chunk in range(n_chunks):
+                        span = slice(chunk * tokens, (chunk + 1) * tokens)
+                        keys = jnp.concatenate(
+                            [chunks[chunk][0, doc], dead_ref[doc, span, :]], axis=1
+                        )
+                        scores = jnp.dot(keys, extended, preferred_element_type=jnp.float32)
+                        if masked:
+                            key_pos = firsts[chunk] + lax.broadcasted_iota(
+                                jnp.int32, scores.shape, 0
+                            )
+                            scores = jnp.where(key_pos <= qpos_ref[tile], scores, MASKED)
+                        parts.append((scores, values[doc, :, span]))
+                    found.append(parts)
+                for tile, parts in zip(tiles, found):
+                    update(tile, parts)
+
+            live = lowest <= qmax_ref[pair]
+            whole = reach <= qmin_ref[pair]
 
             @pl.when(live & whole)
             def _():
@@ -280,48 +294,37 @@
             def _():
                 visit(True)
 
-        if is_last:
-            finished = (summed[tile] / total[tile]).T.astype(jnp.bfloat16)
-            for head in range(heads_here):
-                out_ref[here, head * HD : (head + 1) * HD] = finished[
-                    head * tile_q : (head + 1) * tile_q, :
-                ]
-
-
-def attend(chunks, dead, first_pos, selected, heads_here, fresh, state, is_last):
+        if not with_new:
+            for tile in tiles:
+                mixed_out[tile] = summed[tile].astype(jnp.bfloat16)
+
+
+def attend(chunks, dead, first_pos, selected, queries, fresh):
     n_chunks = len(chunks)
     tokens = chunks[0].shape[2]
-    n_tiles = SEL * heads_here // TILE_COLS
-    tile_q = TILE_COLS // heads_here
-    is_first = state is None
-    by_tile = selected.reshape(n_tiles, tile_q)
-    q_pos = jnp.tile(by_tile, (1, heads_here)).reshape(n_tiles, 1, TILE_COLS)
+    n_tiles = queries.shape[0]
+    tile_q = SEL // n_tiles
+    by_pair = selected.reshape(n_tiles // PAIR, PAIR * tile_q)
+    q_pos = jnp.tile(selected.reshape(n_tiles, tile_q), (1, TILE_COLS // tile_q))
+    q_pos = q_pos.reshape(n_tiles, 1, TILE_COLS)
     smem = pl.BlockSpec(memory_space=pltpu.SMEM)
     vmem = pl.BlockSpec(memory_space=pltpu.VMEM)
-    operands = [first_pos, by_tile[:, 0], by_tile[:, -1], *chunks, dead, q_pos]
-    operands += list(fresh) if is_first else list(state)
-    shapes = [
-        ((n_tiles, HD, TILE_COLS), jnp.bfloat16),
-        ((n_tiles, 1, TILE_COLS), jnp.float32),
-        ((n_tiles, 1, TILE_COLS), jnp.float32),
-        ((n_tiles, HD, TILE_COLS), jnp.float32),
-    ]
-    if is_last:
-        outs = [((SEL, heads_here * HD), jnp.bfloat16)]
-        scratch = shapes if is_first else shapes[1:]
+    operands = [first_pos, by_pair[:, 0], by_pair[:, -1], *chunks, dead, q_pos, queries, *fresh]
+    mixed = ((n_tiles, HD, TILE_COLS), jnp.float32 if fresh else jnp.bfloat16)
+    outs = [((n_tiles, 1, TILE_COLS), jnp.float32)] * 2 + [mixed]
+    scratch = [((DOCS, HD, n_chunks * tokens), jnp.bfloat16)]
+    if fresh:
+        scratch += [((SEL, HD), jnp.bfloat16), ((HD, SEL), jnp.bfloat16)]
     else:
-        outs, scratch = shapes, []
-    scratch = scratch + [((DOCS, HD, n_chunks * tokens), jnp.bfloat16)]
-    if is_first:
-        scratch = scratch + [((SEL, HD), jnp.bfloat16), ((HD, SEL), jnp.bfloat16)]
-    pairs = SEL * heads_here * DOCS * n_chunks * tokens // 2
+        scratch += [(mixed[0], jnp.float32)]
+    pairs = SEL * TILE_COLS // tile_q * DOCS * n_chunks * tokens // 2
     return pl.pallas_call(
-        functools.partial(attend_kernel, n_chunks, is_first, is_last, heads_here),
+        functools.partial(attend_kernel, n_chunks, bool(fresh), tile_q),
         in_specs=[smem] * 3 + [vmem] * (len(operands) - 3),
         out_specs=[vmem] * len(outs),
         out_shape=[jax.ShapeDtypeStruct(*s) for s in outs],
         scratch_shapes=[pltpu.VMEM(*s) for s in scratch],
-        compiler_params=megabytes(32),
+        compiler_params=megabytes(24),
         cost_estimate=pl.CostEstimate(
             flops=4 * pairs * HD,
             bytes_accessed=4 * DOCS * n_chunks * tokens * HD,
@@ -329,6 +332,38 @@
         ),
         name="attend",
     )(*operands)
+
+
+def merge_kernel(*refs):
+    top_a, total_a, mixed_a, top_b, total_b, mixed_b, out_ref = refs
+    scale = math.log2(math.e) / math.sqrt(HD)
+    n_tiles = top_a.shape[0]
+    tile_q = SEL // n_tiles
+    for tile in range(n_tiles):
+        new = jnp.maximum(top_a[tile], top_b[tile])
+        part_a = jnp.exp2((top_a[tile] - new) * scale)
+        part_b = jnp.exp2((top_b[tile] - new) * scale)
+        total = total_a[tile] * part_a + total_b[tile] * part_b
+        mixed = mixed_a[tile] * part_a + mixed_b[tile].astype(jnp.float32) * part_b
+        finished = (mixed / total).T.astype(jnp.bfloat16)
+        for head in range(TILE_COLS // tile_q):
+            out_ref[tile * tile_q : (tile + 1) * tile_q, head * HD : (head + 1) * HD] = finished[
+                head * tile_q : (head + 1) * tile_q, :
+            ]
+
+
+def merge(mine, theirs):
+    n_tiles = mine[0].shape[0]
+    shape = (SEL, TILE_COLS * n_tiles // SEL * HD)
+    return pl.pallas_call(
+        merge_kernel,
+        out_shape=jax.ShapeDtypeStruct(shape, jnp.bfloat16),
+        compiler_params=megabytes(16),
+        cost_estimate=pl.CostEstimate(
+            flops=4 * math.prod(shape), bytes_accessed=8 * math.prod(shape), transcendentals=0
+        ),
+        name="merge",
+    )(*mine, *theirs)
 
 
 def out_kernel(n_blocks, place_ref, x_ref, w_ref, *refs):
@@ -425,6 +460,19 @@
     ).astype(jnp.bfloat16)
     normed, pool_cache = lax.optimization_barrier((normed, pool_cache))
 
+    middle = tp_size // 2
+    by_kind = pool_cache.transpose(0, 2, 1, 3)
+    sources = [by_kind]
+    for shift in range(1, req_size):
+        sources.append(
+            lax.ppermute(by_kind, "req", [((i + shift) % req_size, i) for i in range(req_size)])
+        )
+    holder = (doc_slot // slots - lax.axis_index("req")) % req_size
+    order = jnp.arange(middle, dtype=jnp.int32)
+    takers = jnp.concatenate([me ^ order, me ^ order ^ middle])
+    sent = select_docs(sources, holder, doc_slot % slots, takers * KVH // tp_size, tp_size)
+
+    cosine, sine_part = rotation_tables(selected)
     part = width // GATHER_CHUNKS
     half = part // 2
     prev = None
@@ -432,30 +480,30 @@
         own = normed[:, chunk * part : (chunk + 1) * part]
         before = behind = own
         blocks = [own]
-        for _ in range(1, far):
+        for k in range(1, far):
             before = lax.ppermute(before, "tp", forth)
             behind = lax.ppermute(behind, "tp", back)
+            if chunk == 0 and k == min(2, far - 1):
+                before, behind, *sent = lax.optimization_barrier((before, behind, *sent))
             blocks += [before, behind]
         left = lax.ppermute(before[:, :half], "tp", forth)
         right = lax.ppermute(behind[:, half:], "tp", back)
         if rows % 16:
             blocks = [jnp.concatenate(blocks, axis=0)]
-        prev = project(place, blocks, left, right, w_query, w_keyval, prev, chunk)
-    q_raw, keyval = prev
-
-    by_kind = pool_cache.transpose(0, 2, 1, 3)
-    sources = [by_kind]
-    for shift in range(1, req_size):
-        sources.append(
-            lax.ppermute(by_kind, "req", [((i + shift) % req_size, i) for i in range(req_size)])
-        )
-    holder = (doc_slot // slots - lax.axis_index("req")) % req_size
-    order = jnp.arange(tp_size, dtype=jnp.int32)
-    sent = select_docs(sources, holder, doc_slot % slots, (me ^ order) * KVH // tp_size, tp_size)
-    chunks = [sent[0]] + [
-        lax.ppermute(sent[j], "tp", [(i, i ^ j) for i in range(tp_size)])
-        for j in range(1, tp_size)
+        prev = project(place, blocks, left, right, w_query, w_keyval, prev, (cosine, sine_part), chunk)
+    queries, keyval = prev
+
+    chunks = [
+        [
+            lax.ppermute(sent[slot * middle + j], "tp", [(i, i ^ j) for i in range(tp_size)])
+            if j
+            else sent[slot * middle]
+            for j in range(middle)
+        ]
+        for slot in range(2)
     ]
+    across = [(i, i ^ middle) for i in range(tp_size)]
+    their_queries = lax.ppermute(queries, "tp", across)
 
     offsets = jnp.cumsum(lengths) - lengths
     first_slot = (me ^ order) * tokens
@@ -464,14 +512,14 @@
     is_valid = slot_tokens[None] < lengths[:, None, None]
     replaced = jnp.any(cache_pos[..., None] == selected, axis=-1)
     dead = jnp.where(is_valid & jnp.logical_not(replaced), 0.0, MASKED).astype(jnp.bfloat16)
-    dead = jnp.broadcast_to(dead[..., None], (DOCS, tp_size, tokens, HD))
+    dead = jnp.broadcast_to(dead[..., None], (DOCS, middle, tokens, HD))
+    dead = dead.reshape(DOCS, middle * tokens, HD)
     first_pos = jnp.where(
         first_slot[None] < lengths[:, None], offsets[:, None] + first_slot[None], FAR
-    )
+    ).reshape(-1)
 
     keyval = keyval.astype(jnp.bfloat16)
     if tp_size == KVH:
-        middle = tp_size // 2
         is_key = me < middle
         first, second = keyval[:, :HD], keyval[:, HD:]
         one = lax.ppermute(
@@ -492,22 +540,13 @@
         new_k = lax.dynamic_slice_in_dim(everyone, my_head * HD, HD, axis=1)
         new_v = lax.dynamic_slice_in_dim(everyone, (KVH + my_head) * HD, HD, axis=1)
 
-    cosine, sine_part = rotation_tables(selected)
-    state = None
-    size = tp_size // GROUPS
-    for group in range(GROUPS):
-        span = slice(group * size, (group + 1) * size)
-        state = attend(
-            chunks[span],
-            dead[:, span].reshape(DOCS, size * tokens, HD),
-            first_pos[:, span].reshape(-1),
-            selected,
-            heads_here,
-            (q_raw, cosine, sine_part, new_k, new_v),
-            state,
-            group + 1 == GROUPS,
-        )
-    (attention,) = state
+    mine = attend(
+        chunks[0], dead, first_pos, selected, queries, [cosine, sine_part, new_k, new_v]
+    )
+    top, total, mixed = attend(chunks[1], dead, first_pos, selected, their_queries, [])
+    stats = lax.ppermute(jnp.concatenate([top, total], axis=1), "tp", across)
+    mixed = lax.ppermute(mixed, "tp", across)
+    attention = merge(mine, (stats[:, :1], stats[:, 1:], mixed))
 
     finished = []
     for chunk in range(REDUCE_CHUNKS):

time: 252 us -> 201 us (0.80)
  waiting for transfers between devices: 80.7 us -> 32 us
  Pallas kernels: 67.2 us -> 60.6 us
  local copies, waits for them, and re-layouts: 23.3 us -> 26.6 us
    ppermute x7 -> x9, waiting for transfers between devices: 34.5 us -> 0.02 us  [the longest x6 0.02 us: per_device(): lax.ppermute(sent[slot * middle + j], 'tp', [(i, i ^ j) for i in range(tp...]
    ppermute x1, starting transfers between devices: 1.68 us -> 20.2 us  [per_device(): lax.ppermute(jnp.where(is_key, second, first), 'tp', [(i, 2 * i + 1 if i...]
    ppermute x6, waiting for transfers between devices: 19.6 us -> 3.18 us  [per_device(): lax.ppermute(down.astype(jnp.bfloat16), 'tp', back).astype(jnp.float32)]
    ppermute x2, starting transfers between devices: 18.3 us -> 5.52 us  [per_device(): ahead = lax.ppermute(pieces[-2], 'tp', forth).astype(jnp.float32)]
    ppermute x6, starting transfers between devices: 2.1 us -> 12.1 us  [per_device(): lax.ppermute(up.astype(jnp.bfloat16), 'tp', forth).astype(jnp.float32)]
    ppermute x6, waiting for transfers between devices: 5.23 us -> 13.5 us  [per_device(): lax.ppermute(up.astype(jnp.bfloat16), 'tp', forth).astype(jnp.float32)]
    ppermute x6, starting transfers between devices: 8.73 us -> 1.66 us  [per_device(): lax.ppermute(down.astype(jnp.bfloat16), 'tp', back).astype(jnp.float32)]
    ppermute x6, waiting for transfers between devices: 16.6 us -> 10.6 us  [per_device(): before = lax.ppermute(before, 'tp', forth)]
  transfers between devices with their start and end apart: 42 -> 44, of which waited for: 25 -> 12; matrix products, arithmetic and copies ran while one was open for 5% -> 5% of each run, Pallas kernels for 18% -> 27%
where the time goes in v3:
time: 201 us; the launch traced here: 200 us
  starting transfers between devices  70.9 us (35%)
  Pallas kernels  60.6 us (30%)
  waiting for transfers between devices  32 us (16%)
  local copies, waits for them, and re-layouts  26.6 us (13%)
  other arithmetic  9.72 us (5%)
    pallas_call x2, Pallas kernels, attend(): pl.pallas_call(functools.partial(attend_kernel, n_chunks, bool(fresh), ti...  34.1 us
    ppermute x1, starting transfers between devices, per_device(): lax.ppermute(jnp.where(is_key, second, first), 'tp', [(i, 2 * i + 1 if i...  20.2 us
    unnamed x57, local copies, waits for them, and re-layouts  17.2 us
    ppermute x6, waiting for transfers between devices, per_device(): lax.ppermute(up.astype(jnp.bfloat16), 'tp', forth).astype(jnp.float32)  13.5 us
    ppermute x6, starting transfers between devices, per_device(): before = lax.ppermute(before, 'tp', forth)  12.8 us
    ppermute x6, starting transfers between devices, per_device(): lax.ppermute(up.astype(jnp.bfloat16), 'tp', forth).astype(jnp.float32)  12.1 us
    pallas_call x2, Pallas kernels, project(): pl.pallas_call(functools.partial(project_kernel, len(blocks), prev is not...  12 us
    pallas_call x2, Pallas kernels, project_out(): pl.pallas_call(functools.partial(out_kernel, n_blocks), grid=(steps,), in...  10.9 us
  transfers between devices with their start and end apart: 44, of which 12 were waited for; matrix products, arithmetic and copies ran while one was open for 5% of the time, Pallas kernels for 27%

profile of v3, /device:TPU:0, one launch (start us, length us, event | category | flops | bytes accessed | tf_op | source)
XLA Modules:
  0.0 200.4 jit_solution(13283250184234248225)
XLA Ops:
  0.0 1.2 fusion
  1.3 1.2 fusion.2
  2.5 5.5 %copy.22 = bf16[4,256,2,1024]{3,1,2,0:T(8,128)(2,1)} copy(bf16[4,256,2,1024]{3,2,1,0:T(2,128)(2,1)} %param.15) | data formatting | bytes 8388608 | tf_op jit(solution)/shard_map/optimization_barrier | solution.py:461
  8.5 2.6 %collective-permute-start = (bf16[32,4096]{1,0:T(8,128)(2,1)S(1)}, bf16[32,4096]{1,0:T(8,128)(2,1)S(1)}, u32[]{:S(2)}, u32[]{:S(2)}) collective-permute-start(bf16[32,4096]{1,0:T(8,128)(2,1)S(1)} %get-tuple-element.102.refs_0_), channel_id=1, source_target_pairs={{0,2},{2,4},{4,6},{6,7},{7,5},{5,3},{3,1},{1,0},{8,10},{10,12},{12... | collective-permute-start | bytes 786440 | tf_op jit(solution)/shard_map/ppermute | solution.py:484
  11.2 2.0 %collective-permute-start.8 = (bf16[32,4096]{1,0:T(8,128)(2,1)S(1)}, bf16[32,4096]{1,0:T(8,128)(2,1)S(1)}, u32[]{:S(2)}, u32[]{:S(2)}) collective-permute-start(bf16[32,4096]{1,0:T(8,128)(2,1)S(1)} %get-tuple-element.101.refs_0_), channel_id=1, source_target_pairs={{0,2},{2,4},{4,6},{6,7},{7,5},{5,3},{3,1},{1,0},{8,10},{10,12},{12... | collective-permute-start | bytes 786440 | tf_op jit(solution)/shard_map/ppermute | solution.py:484
  13.6 1.3 fusion.3
  14.9 3.4 %collective-permute-done.refs_1_ = bf16[32,4096]{1,0:T(8,128)(2,1)S(1)} collective-permute-done((bf16[32,4096]{1,0:T(8,128)(2,1)S(1)}, bf16[32,4096]{1,0:T(8,128)(2,1)S(1)}, u32[]{:S(2)}, u32[]{:S(2)}) %collective-permute-start) | collective-permute-done | bytes 262176 | tf_op jit(solution)/shard_map/ppermute | solution.py:484
  18.3 2.0 collective-permute-start.1
  20.4 1.3 compare_reduce_fusion
  21.7 2.2 %collective-permute-done.8.refs_1_ = bf16[32,4096]{1,0:T(8,128)(2,1)S(1)} collective-permute-done((bf16[32,4096]{1,0:T(8,128)(2,1)S(1)}, bf16[32,4096]{1,0:T(8,128)(2,1)S(1)}, u32[]{:S(2)}, u32[]{:S(2)}) %collective-permute-start.8) | collective-permute-done | bytes 262176 | tf_op jit(solution)/shard_map/ppermute | solution.py:484
  23.9 2.0 collective-permute-start.10
  26.0 3.3 %select_docs.1 = (bf16[2,4,256,128]{3,2,1,0:T(8,128)(2,1)S(1)}, bf16[2,4,256,128]{3,2,1,0:T(8,128)(2,1)S(1)}, bf16[2,4,256,128]{3,2,1,0:T(8,128)(2,1)S(1)}, bf16...) custom-call(s32[4]{0:T(128)S(1)} %get-tuple-element.117.place_ref, ...), custom_call_target="tpu_custom_call" | custom-call | bytes 8388608 | tf_op jit(solution)/shard_map/select_docs/pallas_call | solution.py:179
  29.3 0.8 copy-done.5
  30.1 0.8 copy-done.7
  30.9 0.8 copy-done.9
  31.7 0.8 copy-done.10
  32.5 0.8 copy-done.11
  33.3 0.8 copy-done.13
  34.1 0.8 copy-done.14
  34.9 0.8 copy-done.15
  35.7 2.1 %collective-permute-start.16 = (bf16[32,4096]{1,0:T(8,128)(2,1)S(1)}, bf16[32,4096]{1,0:T(8,128)(2,1)S(1)}, u32[]{:S(2)}, u32[]{:S(2)}) collective-permute-start(bf16[32,4096]{1,0:T(8,128)(2,1)S(1)} %collective-permute-done.1.refs_3_), channel_id=1, source_target_pairs={{0,2},{2,4},{4,6},{6,7},{7,5},{5,3},{3,1},{1,0},{8,10},{10,12},{12... | collective-permute-start | bytes 786440 | tf_op jit(solution)/shard_map/ppermute | solution.py:484
  37.9 2.1 %collective-permute-start.12 = (bf16[32,4096]{1,0:T(8,128)(2,1)S(1)}, bf16[32,4096]{1,0:T(8,128)(2,1)S(1)}, u32[]{:S(2)}, u32[]{:S(2)}) collective-permute-start(bf16[32,4096]{1,0:T(8,128)(2,1)S(1)} %collective-permute-done.10.refs_3_), channel_id=1, source_target_pairs={{0,2},{2,4},{4,6},{6,7},{7,5},{5,3},{3,1},{1,0},{8,10},{10,12},{12... | collective-permute-start | bytes 786440 | tf_op jit(solution)/shard_map/ppermute | solution.py:484
  40.0 5.0 %collective-permute-done.16.refs_5_ = bf16[32,4096]{1,0:T(8,128)(2,1)S(1)} collective-permute-done((bf16[32,4096]{1,0:T(8,128)(2,1)S(1)}, bf16[32,4096]{1,0:T(8,128)(2,1)S(1)}, u32[]{:S(2)}, u32[]{:S(2)}) %collective-permute-start.16) | collective-permute-done | bytes 262176 | tf_op jit(solution)/shard_map/ppermute | solution.py:484
  45.7 2.0 %collective-permute-start.18 = (bf16[32,2048]{1,0:T(8,128)(2,1)}, bf16[32,2048]{1,0:T(8,128)(2,1)S(1)}, u32[]{:S(2)}, u32[]{:S(2)}) collective-permute-start(bf16[32,2048]{1,0:T(8,128)(2,1)} %slice.88), channel_id=1, source_target_pairs={{0,2},{2,4},{4,6},{6,7},{7,5},{5,3},{3,1},{1,0},{8,10},{10,12},{12... | collective-permute-start | bytes 393224 | tf_op jit(solution)/shard_map/ppermute | solution.py:489
  49.7 1.2 reduce.5
  50.9 0.7 reshape_squeeze.4
  51.6 1.2 pad_maximum_fusion.5
  52.9 2.1 %collective-permute-start.14 = (bf16[32,2048]{1,0:T(8,128)(2,1)S(1)}, bf16[32,2048]{1,0:T(8,128)(2,1)S(1)}, u32[]{:S(2)}, u32[]{:S(2)}) collective-permute-start(bf16[32,2048]{1,0:T(8,128)(2,1)S(1)} %slice.86), channel_id=1, source_target_pairs={{0,2},{2,4},{4,6},{6,7},{7,5},{5,3},{3,1},{1,0},{8,10},{10,12},{12... | collective-permute-start | bytes 393224 | tf_op jit(solution)/shard_map/ppermute | solution.py:489
  55.0 2.0 collective-permute-start.22
  57.0 1.6 collective-permute-start.23
  58.6 2.2 %copy-done.1 = bf16[8192,256]{1,0:T(8,128)(2,1)S(1)} copy-done((bf16[8192,256]{1,0:T(8,128)(2,1)S(1)}, bf16[8192,256]{1,0:T(8,128)(2,1)}, u32[]{:S(2)}) %copy-start.1) | copy-done | bytes 4194328
  60.8 0.9 copy-done.4
  61.7 5.7 %project.2 = (f32[256,1024]{1,0:T(8,128)S(1)}, f32[256,256]{1,0:T(8,128)S(1)}) custom-call(s32[8]{0:T(128)S(1)} %dynamic-slice_bitcast_fusion.place_ref, bf16[32,4096]{1,0:T(8,128)(2,1)S(1)} %get-tuple-element.102.refs_0_, bf16[32,4096]{1,0:T(8,128)(2,1)S(1)} %collective-permute-done.refs_1_, bf16[32,4096]{1,0:T(8,128)(2,1)S(1)} %collective-permute-done.2.refs_2_, ...), custom_call_target="tpu_custom_call" | custom-call | flops 2684354560 | bytes 15204352 | tf_op jit(solution)/shard_map/project/pallas_call | solution.py:124
  67.5 6.3 %project.3 = (bf16[8,128,256]{2,1,0:T(8,128)(2,1)S(1)}, f32[256,256]{1,0:T(8,128)S(1)}) custom-call(s32[8]{0:T(128)S(1)} %dynamic-slice_bitcast_fusion.place_ref, bf16[32,4096]{1,0:T(8,128)(2,1)S(1)} %get-tuple-element.101.refs_0_, bf16[32,4096]{1,0:T(8,128)(2,1)S(1)} %collective-permute-done.8.refs_1_, bf16[32,4096]{1,0:T(8,128)(2,1)S(1)} %collective-permute-done.9.refs_2_, ...), custom_call_target="tpu_custom_call" | custom-call | flops 2684354560 | bytes 15204352 | tf_op jit(solution)/shard_map/project/pallas_call | solution.py:124
  73.8 3.0 %collective-permute-start.25 = (bf16[8,128,256]{2,1,0:T(8,128)(2,1)S(1)}, bf16[8,128,256]{2,1,0:T(8,128)(2,1)S(1)}, u32[]{:S(2)}, u32[]{:S(2)}) collective-permute-start(bf16[8,128,256]{2,1,0:T(8,128)(2,1)S(1)} %get-tuple-element.71.refs_6_), channel_id=1, source_target_pairs={{0,4},{1,5},{2,6},{3,7},{4,0},{5,1},{6,2},{7,3},{8,12},{9,13},{10,... | collective-permute-start | bytes 1572872 | tf_op jit(solution)/shard_map/ppermute | solution.py:506
  77.7 20.2 %collective-permute-start.21 = (bf16[256,128]{1,0:T(8,128)(2,1)S(1)}, bf16[256,128]{1,0:T(8,128)(2,1)S(1)}, u32[]{:S(2)}, u32[]{:S(2)}) collective-permute-start(bf16[256,128]{1,0:T(8,128)(2,1)S(1)} %get-tuple-element.105), channel_id=1, source_target_pairs={{0,1},{1,3},{2,5},{3,7},{4,0},{5,2},{6,4},{7,6},{8,9},{9,11},{10,1... | collective-permute-start | bytes 196616 | tf_op jit(solution)/shard_map/ppermute | solution.py:530
  98.3 2.6 %collective-permute-done.21 = bf16[256,128]{1,0:T(8,128)(2,1)S(1)} collective-permute-done((bf16[256,128]{1,0:T(8,128)(2,1)S(1)}, bf16[256,128]{1,0:T(8,128)(2,1)S(1)}, u32[]{:S(2)}, u32[]{:S(2)}) %collective-permute-start.21) | collective-permute-done | bytes 65568 | tf_op jit(solution)/shard_map/ppermute | solution.py:530
  101.0 1.9 collective-permute-start.5
  103.2 1.3 collective-permute-start.7
  105.1 1.1 copy-done.12
  106.2 16.5 %attend.3 = (f32[8,1,256]{2,1,0:T(1,128)S(1)}, f32[8,1,256]{2,1,0:T(1,128)S(1)}, bf16[8,128,256]{2,1,0:T(8,128)(2,1)S(1)}) custom-call(s32[16]{0:T(128)S(1)} %select_n.70.first_ref, s32[4]{0:T(128)S(1)} %bitcast.23, s32[4]{0:T(128)S(1)} %bitcast.25, bf16[2,4,256,128]{3,2,1,0:T(8,128)(2,1)S(1)} %copy-done.12, ...), custom_call_target="tpu_custom_call" | custom-call | flops 2147483648 | bytes 2097152 | tf_op jit(solution)/shard_map/attend/pallas_call | solution.py:321
  122.8 3.0 %collective-permute-start.26 = (f32[8,2,256]{2,1,0:T(2,128)S(1)}, f32[8,2,256]{2,1,0:T(2,128)S(1)}, u32[]{:S(2)}, u32[]{:S(2)}) collective-permute-start(f32[8,2,256]{2,1,0:T(2,128)S(1)} %pad_maximum_fusion.7), channel_id=1, source_target_pairs={{0,4},{1,5},{2,6},{3,7},{4,0},{5,1},{6,2},{7,3},{8,12},{9,13},{10,... | collective-permute-start | bytes 49160 | tf_op jit(solution)/shard_map/ppermute | solution.py:547
  125.8 17.6 %attend.2 = (f32[8,1,256]{2,1,0:T(1,128)S(1)}, f32[8,1,256]{2,1,0:T(1,128)S(1)}, f32[8,128,256]{2,1,0:T(8,128)S(1)}) custom-call(s32[16]{0:T(128)S(1)} %select_n.70.first_ref, s32[4]{0:T(128)S(1)} %bitcast.24, s32[4]{0:T(128)S(1)} %bitcast.26, bf16[2,4,256,128]{3,2,1,0:T(8,128)(2,1)S(1)} %copy-done.6, ...), custom_call_target="tpu_custom_call" | custom-call | flops 2147483648 | bytes 2097152 | tf_op jit(solution)/shard_map/attend/pallas_call | solution.py:321
  143.8 5.8 %copy-done = bf16[1024,8192]{1,0:T(8,128)(2,1)S(1)} copy-done((bf16[1024,8192]{1,0:T(8,128)(2,1)S(1)}, bf16[1024,8192]{1,0:T(8,128)(2,1)}, u32[]{:S(2)}) %copy-start) | copy-done | bytes 16777240
  149.6 5.4 %project_out.2 = (f32[32,4096]{1,0:T(8,128)S(1)}, f32[32,4096]{1,0:T(8,128)S(1)}, f32[32,4096]{1,0:T(8,128)S(1)}, f32[32,4096]{1,0:T(8,128)S(1)}, f32[32,4096]{1...) custom-call(s32[8]{0:T(128)S(1)} %dynamic-slice_bitcast_fusion.place, ...), custom_call_target="tpu_custom_call" | custom-call | flops 2147483648 | bytes 13107200 | tf_op jit(solution)/shard_map/project_out/pallas_call | solution.py:406
  155.0 3.5 %collective-permute-start.28 = (bf16[32,2048]{1,0:T(8,128)(2,1)S(1)}, bf16[32,2048]{1,0:T(8,128)(2,1)S(1)}, u32[]{:S(2)}, u32[]{:S(2)}) collective-permute-start(bf16[32,2048]{1,0:T(8,128)(2,1)S(1)} %get-tuple-element.87), channel_id=1, source_target_pairs={{0,2},{2,4},{4,6},{6,7},{7,5},{5,3},{3,1},{1,0},{8,10},{10,12},{12... | collective-permute-start | bytes 393224 | tf_op jit(solution)/shard_map/ppermute | solution.py:557
  158.6 5.5 %project_out.3 = (f32[32,4096]{1,0:T(8,128)S(1)}, f32[32,4096]{1,0:T(8,128)S(1)}, f32[32,4096]{1,0:T(8,128)S(1)}, f32[32,4096]{1,0:T(8,128)S(1)}, f32[32,4096]{1...) custom-call(s32[8]{0:T(128)S(1)} %dynamic-slice_bitcast_fusion.place, ...), custom_call_target="tpu_custom_call" | custom-call | flops 2147483648 | bytes 13107200 | tf_op jit(solution)/shard_map/project_out/pallas_call | solution.py:406
  164.1 2.1 %collective-permute-start.36 = (bf16[32,2048]{1,0:T(8,128)(2,1)S(1)}, bf16[32,2048]{1,0:T(8,128)(2,1)S(1)}, u32[]{:S(2)}, u32[]{:S(2)}) collective-permute-start(bf16[32,2048]{1,0:T(8,128)(2,1)S(1)} %get-tuple-element.96), channel_id=1, source_target_pairs={{0,2},{2,4},{4,6},{6,7},{7,5},{5,3},{3,1},{1,0},{8,10},{10,12},{12... | collective-permute-start | bytes 393224 | tf_op jit(solution)/shard_map/ppermute | solution.py:557
  166.3 2.1 %collective-permute-start.29 = (bf16[32,4096]{1,0:T(8,128)(2,1)S(1)}, bf16[32,4096]{1,0:T(8,128)(2,1)S(1)}, u32[]{:S(2)}, u32[]{:S(2)}) collective-permute-start(bf16[32,4096]{1,0:T(8,128)(2,1)S(1)} %pad_maximum_fusion.1), channel_id=1, source_target_pairs={{0,2},{2,4},{4,6},{6,7},{7,5},{5,3},{3,1},{1,0},{8,10},{10,12},{12... | collective-permute-start | bytes 786440 | tf_op jit(solution)/shard_map/ppermute | solution.py:566
  168.5 2.0 collective-permute-done.36
  170.6 2.1 %collective-permute-start.37 = (bf16[32,4096]{1,0:T(8,128)(2,1)S(1)}, bf16[32,4096]{1,0:T(8,128)(2,1)S(1)}, u32[]{:S(2)}, u32[]{:S(2)}) collective-permute-start(bf16[32,4096]{1,0:T(8,128)(2,1)S(1)} %pad_maximum_fusion.3), channel_id=1, source_target_pairs={{0,2},{2,4},{4,6},{6,7},{7,5},{5,3},{3,1},{1,0},{8,10},{10,12},{12... | collective-permute-start | bytes 786440 | tf_op jit(solution)/shard_map/ppermute | solution.py:566
  172.8 3.3 %collective-permute-done.29 = bf16[32,4096]{1,0:T(8,128)(2,1)S(1)} collective-permute-done((bf16[32,4096]{1,0:T(8,128)(2,1)S(1)}, bf16[32,4096]{1,0:T(8,128)(2,1)S(1)}, u32[]{:S(2)}, u32[]{:S(2)}) %collective-permute-start.29) | collective-permute-done | bytes 262176 | tf_op jit(solution)/shard_map/ppermute | solution.py:566
  176.2 2.1 %collective-permute-start.30 = (bf16[32,4096]{1,0:T(8,128)(2,1)S(1)}, bf16[32,4096]{1,0:T(8,128)(2,1)S(1)}, u32[]{:S(2)}, u32[]{:S(2)}) collective-permute-start(bf16[32,4096]{1,0:T(8,128)(2,1)S(1)} %add_convert_fusion.9), channel_id=1, source_target_pairs={{0,2},{2,4},{4,6},{6,7},{7,5},{5,3},{3,1},{1,0},{8,10},{10,12},{12... | collective-permute-start | bytes 786440 | tf_op jit(solution)/shard_map/ppermute | solution.py:566
  178.4 3.3 %collective-permute-done.37 = bf16[32,4096]{1,0:T(8,128)(2,1)S(1)} collective-permute-done((bf16[32,4096]{1,0:T(8,128)(2,1)S(1)}, bf16[32,4096]{1,0:T(8,128)(2,1)S(1)}, u32[]{:S(2)}, u32[]{:S(2)}) %collective-permute-start.37) | collective-permute-done | bytes 262176 | tf_op jit(solution)/shard_map/ppermute | solution.py:566
  181.8 2.1 %collective-permute-start.38 = (bf16[32,4096]{1,0:T(8,128)(2,1)S(1)}, bf16[32,4096]{1,0:T(8,128)(2,1)S(1)}, u32[]{:S(2)}, u32[]{:S(2)}) collective-permute-start(bf16[32,4096]{1,0:T(8,128)(2,1)S(1)} %add_convert_fusion.4), channel_id=1, source_target_pairs={{0,2},{2,4},{4,6},{6,7},{7,5},{5,3},{3,1},{1,0},{8,10},{10,12},{12... | collective-permute-start | bytes 786440 | tf_op jit(solution)/shard_map/ppermute | solution.py:566
  184.0 3.3 %collective-permute-done.30 = bf16[32,4096]{1,0:T(8,128)(2,1)S(1)} collective-permute-done((bf16[32,4096]{1,0:T(8,128)(2,1)S(1)}, bf16[32,4096]{1,0:T(8,128)(2,1)S(1)}, u32[]{:S(2)}, u32[]{:S(2)}) %collective-permute-start.30) | collective-permute-done | bytes 262176 | tf_op jit(solution)/shard_map/ppermute | solution.py:566
  187.4 2.1 %collective-permute-start.31 = (bf16[32,4096]{1,0:T(8,128)(2,1)S(1)}, bf16[32,4096]{1,0:T(8,128)(2,1)S(1)}, u32[]{:S(2)}, u32[]{:S(2)}) collective-permute-start(bf16[32,4096]{1,0:T(8,128)(2,1)S(1)} %add_convert_fusion.8), channel_id=1, source_target_pairs={{0,2},{2,4},{4,6},{6,7},{7,5},{5,3},{3,1},{1,0},{8,10},{10,12},{12... | collective-permute-start | bytes 786440 | tf_op jit(solution)/shard_map/ppermute | solution.py:566
  189.6 1.8 collective-permute-done.38
  191.5 1.6 collective-permute-start.39
  193.1 1.4 collective-permute-start.43
  194.5 1.5 collective-permute-done.35
  196.1 1.8 collective-permute-done.39
  197.9 1.6 collective-permute-done.43
  199.6 0.8 pad_maximum_fusion
  (151 shorter events, 7.9 us)
Async XLA Ops:
  2.5 10.7 %copy-start.16 = (s32[1,256]{1,0:T(1,128)S(1)}, s32[1,256]{1,0:T(1,128)}, u32[]{:S(2)}) copy-start(s32[1,256]{1,0:T(1,128)} %param.18) | copy-start | bytes 3076
  2.5 10.7 %copy-start.24 = (s32[1,4]{1,0:T(1,128)S(1)}, s32[1,4]{1,0:T(1,128)}, u32[]{:S(2)}) copy-start(s32[1,4]{1,0:T(1,128)} %param.17) | copy-start | bytes 52
  2.5 12.4 %copy-start.25 = (s32[4]{0:T(128)S(1)}, s32[4]{0:T(128)}, u32[]{:S(2)}) copy-start(s32[4]{0:T(128)} %param.16) | copy-start | bytes 52
  8.0 18.0 %collective-permute-start.4 = (bf16[4,2,256,1024]{3,2,1,0:T(8,128)(2,1)}, bf16[4,2,256,1024]{3,2,1,0:T(8,128)(2,1)}, u32[]{:S(2)}, u32[]{:S(2)}) collective-permute-start(bf16[4,2,256,1024]{3,2,1,0:T(8,128)(2,1)} %bitcast.22.refs_0_), channel_id=1, source_target_pairs={{8,0},{0,8},{9,1},{1,9},{10,2},{2,10},{11,3},{3,11},{12,4},{4,12},... | collective-permute-start | bytes 12582920 | tf_op jit(solution)/shard_map/ppermute | solution.py:468
  8.5 9.7 %collective-permute-start = (bf16[32,4096]{1,0:T(8,128)(2,1)S(1)}, bf16[32,4096]{1,0:T(8,128)(2,1)S(1)}, u32[]{:S(2)}, u32[]{:S(2)}) collective-permute-start(bf16[32,4096]{1,0:T(8,128)(2,1)S(1)} %get-tuple-element.102.refs_0_), channel_id=1, source_target_pairs={{0,2},{2,4},{4,6},{6,7},{7,5},{5,3},{3,1},{1,0},{8,10},{10,12},{12... | collective-permute-start | bytes 786440 | tf_op jit(solution)/shard_map/ppermute | solution.py:484
  11.2 9.1 %collective-permute-start.2 = (bf16[32,4096]{1,0:T(8,128)(2,1)S(1)}, bf16[32,4096]{1,0:T(8,128)(2,1)S(1)}, u32[]{:S(2)}, u32[]{:S(2)}) collective-permute-start(bf16[32,4096]{1,0:T(8,128)(2,1)S(1)} %get-tuple-element.102.refs_0_), channel_id=1, source_target_pairs={{2,0},{4,2},{6,4},{7,6},{5,7},{3,5},{1,3},{0,1},{10,8},{12,10},{14... | collective-permute-start | bytes 786440 | tf_op jit(solution)/shard_map/ppermute | solution.py:485
  11.2 12.7 %collective-permute-start.8 = (bf16[32,4096]{1,0:T(8,128)(2,1)S(1)}, bf16[32,4096]{1,0:T(8,128)(2,1)S(1)}, u32[]{:S(2)}, u32[]{:S(2)}) collective-permute-start(bf16[32,4096]{1,0:T(8,128)(2,1)S(1)} %get-tuple-element.101.refs_0_), channel_id=1, source_target_pairs={{0,2},{2,4},{4,6},{6,7},{7,5},{5,3},{3,1},{1,0},{8,10},{10,12},{12... | collective-permute-start | bytes 786440 | tf_op jit(solution)/shard_map/ppermute | solution.py:484
  13.2 12.7 %collective-permute-start.9 = (bf16[32,4096]{1,0:T(8,128)(2,1)S(1)}, bf16[32,4096]{1,0:T(8,128)(2,1)S(1)}, u32[]{:S(2)}, u32[]{:S(2)}) collective-permute-start(bf16[32,4096]{1,0:T(8,128)(2,1)S(1)} %get-tuple-element.101.refs_0_), channel_id=1, source_target_pairs={{2,0},{4,2},{6,4},{7,6},{5,7},{3,5},{1,3},{0,1},{10,8},{12,10},{14... | collective-permute-start | bytes 786440 | tf_op jit(solution)/shard_map/ppermute | solution.py:485
  13.2 26.7 %copy-start.22 = (s32[4]{0:T(128)}, s32[4]{0:T(128)S(1)}, u32[]{:S(2)}) copy-start(s32[4]{0:T(128)S(1)} %get-tuple-element.118) | copy-start | bytes 52
  13.4 6.8 %copy-start.18 = (s32[4]{0:T(128)}, s32[4]{0:T(128)S(1)}, u32[]{:S(2)}) copy-start(s32[4]{0:T(128)S(1)} %get-tuple-element.123) | copy-start | bytes 52
  13.4 6.8 %copy-start.20 = (s32[4]{0:T(128)}, s32[4]{0:T(128)S(1)}, u32[]{:S(2)}) copy-start(s32[4]{0:T(128)S(1)} %get-tuple-element.122) | copy-start | bytes 52
  18.3 17.5 %collective-permute-start.1 = (bf16[32,4096]{1,0:T(8,128)(2,1)S(1)}, bf16[32,4096]{1,0:T(8,128)(2,1)S(1)}, u32[]{:S(2)}, u32[]{:S(2)}) collective-permute-start(bf16[32,4096]{1,0:T(8,128)(2,1)S(1)} %collective-permute-done.refs_1_), channel_id=1, source_target_pairs={{0,2},{2,4},{4,6},{6,7},{7,5},{5,3},{3,1},{1,0},{8,10},{10,12},{12... | collective-permute-start | bytes 786440 | tf_op jit(solution)/shard_map/ppermute | solution.py:484
  20.3 15.4 %collective-permute-start.3 = (bf16[32,4096]{1,0:T(8,128)(2,1)S(1)}, bf16[32,4096]{1,0:T(8,128)(2,1)S(1)}, u32[]{:S(2)}, u32[]{:S(2)}) collective-permute-start(bf16[32,4096]{1,0:T(8,128)(2,1)S(1)} %collective-permute-done.2.refs_2_), channel_id=1, source_target_pairs={{2,0},{4,2},{6,4},{7,6},{5,7},{3,5},{1,3},{0,1},{10,8},{12,10},{14... | collective-permute-start | bytes 786440 | tf_op jit(solution)/shard_map/ppermute | solution.py:485
  23.9 14.0 %collective-permute-start.10 = (bf16[32,4096]{1,0:T(8,128)(2,1)S(1)}, bf16[32,4096]{1,0:T(8,128)(2,1)S(1)}, u32[]{:S(2)}, u32[]{:S(2)}) collective-permute-start(bf16[32,4096]{1,0:T(8,128)(2,1)S(1)} %collective-permute-done.8.refs_1_), channel_id=1, source_target_pairs={{0,2},{2,4},{4,6},{6,7},{7,5},{5,3},{3,1},{1,0},{8,10},{10,12},{12... | collective-permute-start | bytes 786440 | tf_op jit(solution)/shard_map/ppermute | solution.py:484
  25.9 14.0 %collective-permute-start.11 = (bf16[32,4096]{1,0:T(8,128)(2,1)S(1)}, bf16[32,4096]{1,0:T(8,128)(2,1)}, u32[]{:S(2)}, u32[]{:S(2)}) collective-permute-start(bf16[32,4096]{1,0:T(8,128)(2,1)S(1)} %collective-permute-done.9.refs_2_), channel_id=1, source_target_pairs={{2,0},{4,2},{6,4},{7,6},{5,7},{3,5},{1,3},{0,1},{10,8},{12,10},{14... | collective-permute-start | bytes 786440 | tf_op jit(solution)/shard_map/ppermute | solution.py:485
  30.9 0.8 copy-start.9
  33.3 0.8 copy-start.13
  35.7 15.9 %copy-start.3 = (bf16[32,4096]{1,0:T(8,128)(2,1)}, bf16[32,4096]{1,0:T(8,128)(2,1)S(1)}, u32[]{:S(2)}) copy-start(bf16[32,4096]{1,0:T(8,128)(2,1)S(1)} %collective-permute-done.3.refs_4_) | copy-start | bytes 786436
  35.7 9.3 %collective-permute-start.16 = (bf16[32,4096]{1,0:T(8,128)(2,1)S(1)}, bf16[32,4096]{1,0:T(8,128)(2,1)S(1)}, u32[]{:S(2)}, u32[]{:S(2)}) collective-permute-start(bf16[32,4096]{1,0:T(8,128)(2,1)S(1)} %collective-permute-done.1.refs_3_), channel_id=1, source_target_pairs={{0,2},{2,4},{4,6},{6,7},{7,5},{5,3},{3,1},{1,0},{8,10},{10,12},{12... | collective-permute-start | bytes 786440 | tf_op jit(solution)/shard_map/ppermute | solution.py:484
  37.8 9.9 %collective-permute-start.17 = (bf16[32,4096]{1,0:T(8,128)(2,1)S(1)}, bf16[32,4096]{1,0:T(8,128)(2,1)S(1)}, u32[]{:S(2)}, u32[]{:S(2)}) collective-permute-start(bf16[32,4096]{1,0:T(8,128)(2,1)S(1)} %collective-permute-done.3.refs_4_), channel_id=1, source_target_pairs={{2,0},{4,2},{6,4},{7,6},{5,7},{3,5},{1,3},{0,1},{10,8},{12,10},{14... | collective-permute-start | bytes 786440 | tf_op jit(solution)/shard_map/ppermute | solution.py:485
  37.9 15.0 %collective-permute-start.12 = (bf16[32,4096]{1,0:T(8,128)(2,1)S(1)}, bf16[32,4096]{1,0:T(8,128)(2,1)S(1)}, u32[]{:S(2)}, u32[]{:S(2)}) collective-permute-start(bf16[32,4096]{1,0:T(8,128)(2,1)S(1)} %collective-permute-done.10.refs_3_), channel_id=1, source_target_pairs={{0,2},{2,4},{4,6},{6,7},{7,5},{5,3},{3,1},{1,0},{8,10},{10,12},{12... | collective-permute-start | bytes 786440 | tf_op jit(solution)/shard_map/ppermute | solution.py:484
  39.9 15.0 %collective-permute-start.13 = (bf16[32,4096]{1,0:T(8,128)(2,1)}, bf16[32,4096]{1,0:T(8,128)(2,1)S(1)}, u32[]{:S(2)}, u32[]{:S(2)}) collective-permute-start(bf16[32,4096]{1,0:T(8,128)(2,1)} %collective-permute-done.11.refs_4_), channel_id=1, source_target_pairs={{2,0},{4,2},{6,4},{7,6},{5,7},{3,5},{1,3},{0,1},{10,8},{12,10},{14... | collective-permute-start | bytes 786440 | tf_op jit(solution)/shard_map/ppermute | solution.py:485
  45.7 11.3 %collective-permute-start.18 = (bf16[32,2048]{1,0:T(8,128)(2,1)}, bf16[32,2048]{1,0:T(8,128)(2,1)S(1)}, u32[]{:S(2)}, u32[]{:S(2)}) collective-permute-start(bf16[32,2048]{1,0:T(8,128)(2,1)} %slice.88), channel_id=1, source_target_pairs={{0,2},{2,4},{4,6},{6,7},{7,5},{5,3},{3,1},{1,0},{8,10},{10,12},{12... | collective-permute-start | bytes 393224 | tf_op jit(solution)/shard_map/ppermute | solution.py:489
  48.4 10.2 %collective-permute-start.19 = (bf16[32,2048]{1,0:T(8,128)(2,1)}, bf16[32,2048]{1,0:T(8,128)(2,1)}, u32[]{:S(2)}, u32[]{:S(2)}) collective-permute-start(bf16[32,2048]{1,0:T(8,128)(2,1)} %slice.89), channel_id=1, source_target_pairs={{2,0},{4,2},{6,4},{7,6},{5,7},{3,5},{1,3},{0,1},{10,8},{12,10},{14... | collective-permute-start | bytes 393224 | tf_op jit(solution)/shard_map/ppermute | solution.py:490
  52.9 14.6 %collective-permute-start.14 = (bf16[32,2048]{1,0:T(8,128)(2,1)S(1)}, bf16[32,2048]{1,0:T(8,128)(2,1)S(1)}, u32[]{:S(2)}, u32[]{:S(2)}) collective-permute-start(bf16[32,2048]{1,0:T(8,128)(2,1)S(1)} %slice.86), channel_id=1, source_target_pairs={{0,2},{2,4},{4,6},{6,7},{7,5},{5,3},{3,1},{1,0},{8,10},{10,12},{12... | collective-permute-start | bytes 393224 | tf_op jit(solution)/shard_map/ppermute | solution.py:489
  54.9 12.5 %collective-permute-start.15 = (bf16[32,2048]{1,0:T(8,128)(2,1)S(1)}, bf16[32,2048]{1,0:T(8,128)(2,1)S(1)}, u32[]{:S(2)}, u32[]{:S(2)}) collective-permute-start(bf16[32,2048]{1,0:T(8,128)(2,1)S(1)} %slice.87), channel_id=1, source_target_pairs={{2,0},{4,2},{6,4},{7,6},{5,7},{3,5},{1,3},{0,1},{10,8},{12,10},{14... | collective-permute-start | bytes 393224 | tf_op jit(solution)/shard_map/ppermute | solution.py:490
  55.0 47.8 %collective-permute-start.22 = (bf16[2,4,256,128]{3,2,1,0:T(8,128)(2,1)}, bf16[2,4,256,128]{3,2,1,0:T(8,128)(2,1)}, u32[]{:S(2)}, u32[]{:S(2)}) collective-permute-start(bf16[2,4,256,128]{3,2,1,0:T(8,128)(2,1)} %copy-done.15), channel_id=1, source_target_pairs={{0,1},{1,0},{2,3},{3,2},{4,5},{5,4},{6,7},{7,6},{8,9},{9,8},{10,11... | collective-permute-start | bytes 1572872 | tf_op jit(solution)/shard_map/ppermute | solution.py:498
  57.0 46.2 %collective-permute-start.23 = (bf16[2,4,256,128]{3,2,1,0:T(8,128)(2,1)}, bf16[2,4,256,128]{3,2,1,0:T(8,128)(2,1)}, u32[]{:S(2)}, u32[]{:S(2)}) collective-permute-start(bf16[2,4,256,128]{3,2,1,0:T(8,128)(2,1)} %copy-done.14), channel_id=1, source_target_pairs={{0,2},{1,3},{2,0},{3,1},{4,6},{5,7},{6,4},{7,5},{8,10},{9,11},{10,... | collective-permute-start | bytes 1572872 | tf_op jit(solution)/shard_map/ppermute | solution.py:498
  58.6 45.9 %collective-permute-start.24 = (bf16[2,4,256,128]{3,2,1,0:T(8,128)(2,1)}, bf16[2,4,256,128]{3,2,1,0:T(8,128)(2,1)}, u32[]{:S(2)}, u32[]{:S(2)}) collective-permute-start(bf16[2,4,256,128]{3,2,1,0:T(8,128)(2,1)} %copy-done.13), channel_id=1, source_target_pairs={{0,3},{1,2},{2,1},{3,0},{4,7},{5,6},{6,5},{7,4},{8,11},{9,10},{10,... | collective-permute-start | bytes 1572872 | tf_op jit(solution)/shard_map/ppermute | solution.py:498
  58.6 2.2 %copy-start.1 = (bf16[8192,256]{1,0:T(8,128)(2,1)S(1)}, bf16[8192,256]{1,0:T(8,128)(2,1)}, u32[]{:S(2)}) copy-start(bf16[8192,256]{1,0:T(8,128)(2,1)} %refs_10_.3) | copy-start | bytes 12582916
  60.8 0.9 copy-start.4
  61.7 5.8 %copy-start.2 = (bf16[8192,256]{1,0:T(8,128)(2,1)S(1)}, bf16[8192,256]{1,0:T(8,128)(2,1)}, u32[]{:S(2)}) copy-start(bf16[8192,256]{1,0:T(8,128)(2,1)} %refs_10_.3) | copy-start | bytes 12582916
  67.5 30.3 %copy-start.19 = (s32[4]{0:T(128)S(1)}, s32[4]{0:T(128)}, u32[]{:S(2)}) copy-start(s32[4]{0:T(128)} %copy-done.18) | copy-start | bytes 52
  67.5 30.3 %copy-start.21 = (s32[4]{0:T(128)S(1)}, s32[4]{0:T(128)}, u32[]{:S(2)}) copy-start(s32[4]{0:T(128)} %copy-done.20) | copy-start | bytes 52
  67.5 30.3 %copy-start.23 = (s32[4]{0:T(128)S(1)}, s32[4]{0:T(128)}, u32[]{:S(2)}) copy-start(s32[4]{0:T(128)} %copy-done.22) | copy-start | bytes 52
  67.5 30.4 %copy-start.17 = (s32[1,256]{1,0:T(1,128)S(1)}, s32[1,256]{1,0:T(1,128)}, u32[]{:S(2)}) copy-start(s32[1,256]{1,0:T(1,128)} %param.18) | copy-start | bytes 3076
  67.5 35.6 %copy-start.8 = (bf16[2,4,256,128]{3,2,1,0:T(8,128)(2,1)S(1)}, bf16[2,4,256,128]{3,2,1,0:T(8,128)(2,1)}, u32[]{:S(2)}) copy-start(bf16[2,4,256,128]{3,2,1,0:T(8,128)(2,1)} %copy-done.7) | copy-start | bytes 1572868
  73.8 30.7 %collective-permute-start.25 = (bf16[8,128,256]{2,1,0:T(8,128)(2,1)S(1)}, bf16[8,128,256]{2,1,0:T(8,128)(2,1)S(1)}, u32[]{:S(2)}, u32[]{:S(2)}) collective-permute-start(bf16[8,128,256]{2,1,0:T(8,128)(2,1)S(1)} %get-tuple-element.71.refs_6_), channel_id=1, source_target_pairs={{0,4},{1,5},{2,6},{3,7},{4,0},{5,1},{6,2},{7,3},{8,12},{9,13},{10,... | collective-permute-start | bytes 1572872 | tf_op jit(solution)/shard_map/ppermute | solution.py:506
  76.9 0.7 collective-permute-start.20
  77.7 23.3 %collective-permute-start.21 = (bf16[256,128]{1,0:T(8,128)(2,1)S(1)}, bf16[256,128]{1,0:T(8,128)(2,1)S(1)}, u32[]{:S(2)}, u32[]{:S(2)}) collective-permute-start(bf16[256,128]{1,0:T(8,128)(2,1)S(1)} %get-tuple-element.105), channel_id=1, source_target_pairs={{0,1},{1,3},{2,5},{3,7},{4,0},{5,2},{6,4},{7,6},{8,9},{9,11},{10,1... | collective-permute-start | bytes 196616 | tf_op jit(solution)/shard_map/ppermute | solution.py:530
  101.0 24.8 %collective-permute-start.5 = (bf16[2,4,256,128]{3,2,1,0:T(8,128)(2,1)}, bf16[2,4,256,128]{3,2,1,0:T(8,128)(2,1)S(1)}, u32[]{:S(2)}, u32[]{:S(2)}) collective-permute-start(bf16[2,4,256,128]{3,2,1,0:T(8,128)(2,1)} %copy-done.10), channel_id=1, source_target_pairs={{0,1},{1,0},{2,3},{3,2},{4,5},{5,4},{6,7},{7,6},{8,9},{9,8},{10,11... | collective-permute-start | bytes 1572872 | tf_op jit(solution)/shard_map/ppermute | solution.py:498
  102.9 22.9 %collective-permute-start.6 = (bf16[2,4,256,128]{3,2,1,0:T(8,128)(2,1)}, bf16[2,4,256,128]{3,2,1,0:T(8,128)(2,1)S(1)}, u32[]{:S(2)}, u32[]{:S(2)}) collective-permute-start(bf16[2,4,256,128]{3,2,1,0:T(8,128)(2,1)} %copy-done.9), channel_id=1, source_target_pairs={{0,2},{1,3},{2,0},{3,1},{4,6},{5,7},{6,4},{7,5},{8,10},{9,11},{10,... | collective-permute-start | bytes 1572872 | tf_op jit(solution)/shard_map/ppermute | solution.py:498
  103.2 22.6 %collective-permute-start.7 = (bf16[2,4,256,128]{3,2,1,0:T(8,128)(2,1)S(1)}, bf16[2,4,256,128]{3,2,1,0:T(8,128)(2,1)S(1)}, u32[]{:S(2)}, u32[]{:S(2)}) collective-permute-start(bf16[2,4,256,128]{3,2,1,0:T(8,128)(2,1)S(1)} %copy-done.8), channel_id=1, source_target_pairs={{0,3},{1,2},{2,1},{3,0},{4,7},{5,6},{6,5},{7,4},{8,11},{9,10},{10,... | collective-permute-start | bytes 1572872 | tf_op jit(solution)/shard_map/ppermute | solution.py:498
  105.1 20.7 %copy-start.6 = (bf16[2,4,256,128]{3,2,1,0:T(8,128)(2,1)S(1)}, bf16[2,4,256,128]{3,2,1,0:T(8,128)(2,1)}, u32[]{:S(2)}) copy-start(bf16[2,4,256,128]{3,2,1,0:T(8,128)(2,1)} %copy-done.5) | copy-start | bytes 1572868
  105.1 1.1 copy-start.12
  122.7 20.8 %collective-permute-start.27 = (bf16[8,128,256]{2,1,0:T(8,128)(2,1)S(1)}, bf16[8,128,256]{2,1,0:T(8,128)(2,1)S(1)}, u32[]{:S(2)}, u32[]{:S(2)}) collective-permute-start(bf16[8,128,256]{2,1,0:T(8,128)(2,1)S(1)} %get-tuple-element.82), channel_id=1, source_target_pairs={{0,4},{1,5},{2,6},{3,7},{4,0},{5,1},{6,2},{7,3},{8,12},{9,13},{10,... | collective-permute-start | bytes 1572872 | tf_op jit(solution)/shard_map/ppermute | solution.py:548
  122.8 20.6 %collective-permute-start.26 = (f32[8,2,256]{2,1,0:T(2,128)S(1)}, f32[8,2,256]{2,1,0:T(2,128)S(1)}, u32[]{:S(2)}, u32[]{:S(2)}) collective-permute-start(f32[8,2,256]{2,1,0:T(2,128)S(1)} %pad_maximum_fusion.7), channel_id=1, source_target_pairs={{0,4},{1,5},{2,6},{3,7},{4,0},{5,1},{6,2},{7,3},{8,12},{9,13},{10,... | collective-permute-start | bytes 49160 | tf_op jit(solution)/shard_map/ppermute | solution.py:547
  143.8 5.8 %copy-start = (bf16[1024,8192]{1,0:T(8,128)(2,1)S(1)}, bf16[1024,8192]{1,0:T(8,128)(2,1)}, u32[]{:S(2)}) copy-start(bf16[1024,8192]{1,0:T(8,128)(2,1)} %w_ref.3) | copy-start | bytes 50331652
  155.0 11.2 %collective-permute-start.28 = (bf16[32,2048]{1,0:T(8,128)(2,1)S(1)}, bf16[32,2048]{1,0:T(8,128)(2,1)S(1)}, u32[]{:S(2)}, u32[]{:S(2)}) collective-permute-start(bf16[32,2048]{1,0:T(8,128)(2,1)S(1)} %get-tuple-element.87), channel_id=1, source_target_pairs={{0,2},{2,4},{4,6},{6,7},{7,5},{5,3},{3,1},{1,0},{8,10},{10,12},{12... | collective-permute-start | bytes 393224 | tf_op jit(solution)/shard_map/ppermute | solution.py:557
  158.5 9.9 %collective-permute-start.32 = (bf16[32,2048]{1,0:T(8,128)(2,1)S(1)}, bf16[32,2048]{1,0:T(8,128)(2,1)S(1)}, u32[]{:S(2)}, u32[]{:S(2)}) collective-permute-start(bf16[32,2048]{1,0:T(8,128)(2,1)S(1)} %get-tuple-element.91), channel_id=1, source_target_pairs={{2,0},{4,2},{6,4},{7,6},{5,7},{3,5},{1,3},{0,1},{10,8},{12,10},{14... | collective-permute-start | bytes 393224 | tf_op jit(solution)/shard_map/ppermute | solution.py:558
  164.1 6.4 %collective-permute-start.36 = (bf16[32,2048]{1,0:T(8,128)(2,1)S(1)}, bf16[32,2048]{1,0:T(8,128)(2,1)S(1)}, u32[]{:S(2)}, u32[]{:S(2)}) collective-permute-start(bf16[32,2048]{1,0:T(8,128)(2,1)S(1)} %get-tuple-element.96), channel_id=1, source_target_pairs={{0,2},{2,4},{4,6},{6,7},{7,5},{5,3},{3,1},{1,0},{8,10},{10,12},{12... | collective-permute-start | bytes 393224 | tf_op jit(solution)/shard_map/ppermute | solution.py:557
  166.1 6.5 %collective-permute-start.40 = (bf16[32,2048]{1,0:T(8,128)(2,1)S(1)}, bf16[32,2048]{1,0:T(8,128)(2,1)S(1)}, u32[]{:S(2)}, u32[]{:S(2)}) collective-permute-start(bf16[32,2048]{1,0:T(8,128)(2,1)S(1)} %get-tuple-element.100), channel_id=1, source_target_pairs={{2,0},{4,2},{6,4},{7,6},{5,7},{3,5},{1,3},{0,1},{10,8},{12,10},{14... | collective-permute-start | bytes 393224 | tf_op jit(solution)/shard_map/ppermute | solution.py:558
  166.3 9.8 %collective-permute-start.29 = (bf16[32,4096]{1,0:T(8,128)(2,1)S(1)}, bf16[32,4096]{1,0:T(8,128)(2,1)S(1)}, u32[]{:S(2)}, u32[]{:S(2)}) collective-permute-start(bf16[32,4096]{1,0:T(8,128)(2,1)S(1)} %pad_maximum_fusion.1), channel_id=1, source_target_pairs={{0,2},{2,4},{4,6},{6,7},{7,5},{5,3},{3,1},{1,0},{8,10},{10,12},{12... | collective-permute-start | bytes 786440 | tf_op jit(solution)/shard_map/ppermute | solution.py:566
  168.4 9.9 %collective-permute-start.33 = (bf16[32,4096]{1,0:T(8,128)(2,1)S(1)}, bf16[32,4096]{1,0:T(8,128)(2,1)S(1)}, u32[]{:S(2)}, u32[]{:S(2)}) collective-permute-start(bf16[32,4096]{1,0:T(8,128)(2,1)S(1)} %pad_maximum_fusion.2), channel_id=1, source_target_pairs={{2,0},{4,2},{6,4},{7,6},{5,7},{3,5},{1,3},{0,1},{10,8},{12,10},{14... | collective-permute-start | bytes 786440 | tf_op jit(solution)/shard_map/ppermute | solution.py:567
  170.6 11.2 %collective-permute-start.37 = (bf16[32,4096]{1,0:T(8,128)(2,1)S(1)}, bf16[32,4096]{1,0:T(8,128)(2,1)S(1)}, u32[]{:S(2)}, u32[]{:S(2)}) collective-permute-start(bf16[32,4096]{1,0:T(8,128)(2,1)S(1)} %pad_maximum_fusion.3), channel_id=1, source_target_pairs={{0,2},{2,4},{4,6},{6,7},{7,5},{5,3},{3,1},{1,0},{8,10},{10,12},{12... | collective-permute-start | bytes 786440 | tf_op jit(solution)/shard_map/ppermute | solution.py:566
  172.7 11.2 %collective-permute-start.41 = (bf16[32,4096]{1,0:T(8,128)(2,1)S(1)}, bf16[32,4096]{1,0:T(8,128)(2,1)S(1)}, u32[]{:S(2)}, u32[]{:S(2)}) collective-permute-start(bf16[32,4096]{1,0:T(8,128)(2,1)S(1)} %pad_maximum_fusion.4), channel_id=1, source_target_pairs={{2,0},{4,2},{6,4},{7,6},{5,7},{3,5},{1,3},{0,1},{10,8},{12,10},{14... | collective-permute-start | bytes 786440 | tf_op jit(solution)/shard_map/ppermute | solution.py:567
  176.2 11.2 %collective-permute-start.30 = (bf16[32,4096]{1,0:T(8,128)(2,1)S(1)}, bf16[32,4096]{1,0:T(8,128)(2,1)S(1)}, u32[]{:S(2)}, u32[]{:S(2)}) collective-permute-start(bf16[32,4096]{1,0:T(8,128)(2,1)S(1)} %add_convert_fusion.9), channel_id=1, source_target_pairs={{0,2},{2,4},{4,6},{6,7},{7,5},{5,3},{3,1},{1,0},{8,10},{10,12},{12... | collective-permute-start | bytes 786440 | tf_op jit(solution)/shard_map/ppermute | solution.py:566
  178.3 11.2 %collective-permute-start.34 = (bf16[32,4096]{1,0:T(8,128)(2,1)S(1)}, bf16[32,4096]{1,0:T(8,128)(2,1)S(1)}, u32[]{:S(2)}, u32[]{:S(2)}) collective-permute-start(bf16[32,4096]{1,0:T(8,128)(2,1)S(1)} %add_convert_fusion.7), channel_id=1, source_target_pairs={{2,0},{4,2},{6,4},{7,6},{5,7},{3,5},{1,3},{0,1},{10,8},{12,10},{14... | collective-permute-start | bytes 786440 | tf_op jit(solution)/shard_map/ppermute | solution.py:567
  181.8 9.6 %collective-permute-start.38 = (bf16[32,4096]{1,0:T(8,128)(2,1)S(1)}, bf16[32,4096]{1,0:T(8,128)(2,1)S(1)}, u32[]{:S(2)}, u32[]{:S(2)}) collective-permute-start(bf16[32,4096]{1,0:T(8,128)(2,1)S(1)} %add_convert_fusion.4), channel_id=1, source_target_pairs={{0,2},{2,4},{4,6},{6,7},{7,5},{5,3},{3,1},{1,0},{8,10},{10,12},{12... | collective-permute-start | bytes 786440 | tf_op jit(solution)/shard_map/ppermute | solution.py:566
  184.0 9.1 %collective-permute-start.42 = (bf16[32,4096]{1,0:T(8,128)(2,1)S(1)}, bf16[32,4096]{1,0:T(8,128)(2,1)S(1)}, u32[]{:S(2)}, u32[]{:S(2)}) collective-permute-start(bf16[32,4096]{1,0:T(8,128)(2,1)S(1)} %add_convert_fusion.2), channel_id=1, source_target_pairs={{2,0},{4,2},{6,4},{7,6},{5,7},{3,5},{1,3},{0,1},{10,8},{12,10},{14... | collective-permute-start | bytes 786440 | tf_op jit(solution)/shard_map/ppermute | solution.py:567
  187.4 7.1 %collective-permute-start.31 = (bf16[32,4096]{1,0:T(8,128)(2,1)S(1)}, bf16[32,4096]{1,0:T(8,128)(2,1)S(1)}, u32[]{:S(2)}, u32[]{:S(2)}) collective-permute-start(bf16[32,4096]{1,0:T(8,128)(2,1)S(1)} %add_convert_fusion.8), channel_id=1, source_target_pairs={{0,2},{2,4},{4,6},{6,7},{7,5},{5,3},{3,1},{1,0},{8,10},{10,12},{12... | collective-permute-start | bytes 786440 | tf_op jit(solution)/shard_map/ppermute | solution.py:566
  189.6 6.4 %collective-permute-start.35 = (bf16[32,4096]{1,0:T(8,128)(2,1)S(1)}, bf16[32,4096]{1,0:T(8,128)(2,1)S(1)}, u32[]{:S(2)}, u32[]{:S(2)}) collective-permute-start(bf16[32,4096]{1,0:T(8,128)(2,1)S(1)} %add_convert_fusion.6), channel_id=1, source_target_pairs={{2,0},{4,2},{6,4},{7,6},{5,7},{3,5},{1,3},{0,1},{10,8},{12,10},{14... | collective-permute-start | bytes 786440 | tf_op jit(solution)/shard_map/ppermute | solution.py:567
  191.5 6.4 %collective-permute-start.39 = (bf16[32,4096]{1,0:T(8,128)(2,1)S(1)}, bf16[32,4096]{1,0:T(8,128)(2,1)S(1)}, u32[]{:S(2)}, u32[]{:S(2)}) collective-permute-start(bf16[32,4096]{1,0:T(8,128)(2,1)S(1)} %add_convert_fusion.3), channel_id=1, source_target_pairs={{0,2},{2,4},{4,6},{6,7},{7,5},{5,3},{3,1},{1,0},{8,10},{10,12},{12... | collective-permute-start | bytes 786440 | tf_op jit(solution)/shard_map/ppermute | solution.py:566
  193.1 6.4 %collective-permute-start.43 = (bf16[32,4096]{1,0:T(8,128)(2,1)S(1)}, bf16[32,4096]{1,0:T(8,128)(2,1)S(1)}, u32[]{:S(2)}, u32[]{:S(2)}) collective-permute-start(bf16[32,4096]{1,0:T(8,128)(2,1)S(1)} %add_convert_fusion.1), channel_id=1, source_target_pairs={{2,0},{4,2},{6,4},{7,6},{5,7},{3,5},{1,3},{0,1},{10,8},{12,10},{14... | collective-permute-start | bytes 786440 | tf_op jit(solution)/shard_map/ppermute | solution.py:567
  (6 other events, 4.8 us)

commit v4 on v3

v4 whole, which is shorter than its diff:
```python
import functools
import math

import jax
import jax.numpy as jnp
from jax import lax
from jax.experimental import pallas as pl
from jax.experimental.pallas import tpu as pltpu
from jax.sharding import PartitionSpec as P

HEADS = 64
KVH = 8
HD = 128
DOCS = 4
BLOCK = 128
SEL = 256


EPSILON = 1e-05
ROPE_BASE = 500000.0
MASKED = -1e30
FAR = 1 << 30
REDUCE_CHUNKS = 2
TILE_COLS = 256
PAIR = 2
STATS = 16
HALVES = 2
DEPTH_TILE = 1024
WIDTH_TILE = 512
SLOTS = 3

QUICK = pl.CostEstimate(flops=1, bytes_accessed=1, transcendentals=0)


def rotation_tables(positions):
    half_dim = HD // 2
    inverse = ROPE_BASE ** (-(jnp.arange(half_dim, dtype=jnp.float32) * (2.0 / HD)))
    angles = positions.astype(jnp.float32)[:, None] * inverse[None, :]
    cosine = jnp.cos(angles)
    sine_part = jnp.sin(angles)
    return (
        jnp.concatenate([cosine, cosine], axis=-1),
        jnp.concatenate([-sine_part, sine_part], axis=-1),
    )


def rotate(values, cosine, sine_part):
    swapped = jnp.concatenate([values[:, HD // 2 :], values[:, : HD // 2]], axis=-1)
    return values * cosine + swapped * sine_part


def megabytes(count):
    return pltpu.CompilerParams(vmem_limit_bytes=count * 1024 * 1024)


def stream(sources, slots, sems, count):
    def copies(step):
        slot = lax.rem(step, SLOTS)
        return [
            pltpu.make_async_copy(source(step), buffer.at[slot], sems.at[i, slot])
            for i, (source, buffer) in enumerate(zip(sources, slots))
        ]

    def start(step):
        for copy in copies(step):
            copy.start()

    def wait(step):
        for copy in copies(step):
            copy.wait()

    return start, wait


def project_kernel(n_blocks, place_ref, *refs):
    blocks = refs[:n_blocks]
    left_ref, right_ref, wq_ref, wkv_ref, cos_ref, sin_ref = refs[n_blocks : n_blocks + 6]
    out_q = refs[n_blocks + 6 : n_blocks + 6 + HALVES]
    *out_kv, total_q, total_kv, natural, natural_kv, wq_slots, wkv_slots, sems = refs[
        n_blocks + 6 + HALVES :
    ]
    depth = wq_ref.shape[0]
    tile = wq_slots.shape[1]
    count = depth // tile
    rows_of = lambda ref: lambda step: ref.at[pl.ds(pl.multiple_of(step * tile, tile), tile), :]
    start, wait = stream([rows_of(wq_ref), rows_of(wkv_ref)], [wq_slots, wkv_slots], sems, count)

    for step in range(SLOTS - 1):
        start(step)
    total_q[...] = jnp.zeros_like(total_q)
    total_kv[...] = jnp.zeros_like(total_kv)
    for side, far_ref in enumerate((left_ref, right_ref)):
        offset = side * count // 2

        @pl.loop(offset, offset + count // 2)
        def _(step):
            @pl.when(step + SLOTS - 1 < count)
            def _():
                start(step + SLOTS - 1)

            wait(step)
            slot = lax.rem(step, SLOTS)
            cols = pl.ds(pl.multiple_of(step * tile, tile), tile)
            far_cols = pl.ds(pl.multiple_of((step - offset) * tile, tile), tile)
            rows = jnp.concatenate([b[:, cols] for b in blocks] + [far_ref[:, far_cols]], axis=0)
            total_q[...] += jnp.dot(rows, wq_slots[slot], preferred_element_type=jnp.float32)
            total_kv[...] += jnp.dot(rows, wkv_slots[slot], preferred_element_type=jnp.float32)

    height = left_ref.shape[0]
    for block in range(SEL // height):
        here = slice(block * height, (block + 1) * height)
        there = pl.ds(pl.multiple_of(place_ref[block] * height, height), height)
        natural[there, :] = total_q[here, :]
        natural_kv[there, :] = total_kv[here, :]
    heads_here = total_q.shape[1] // HD
    tile_q = TILE_COLS // heads_here
    per_half = SEL // tile_q // HALVES
    for index in range(SEL // tile_q):
        here = slice(index * tile_q, (index + 1) * tile_q)
        stacked = jnp.concatenate(
            [
                rotate(natural[here, head * HD : (head + 1) * HD], cos_ref[here, :], sin_ref[here, :])
                for head in range(heads_here)
            ],
            axis=0,
        )
        out_q[index // per_half][index % per_half] = stacked.T.astype(jnp.bfloat16)
    if out_kv:
        out_kv[0][...] = natural_kv[...].astype(jnp.bfloat16)
    else:
        for index in range(SEL // HD):
            out_q[-1][per_half + index] = natural_kv[
                index * HD : (index + 1) * HD, :
            ].astype(jnp.bfloat16)


def project(place, blocks, left, right, w_query, w_keyval, tables):
    depth, q_cols = w_query.shape
    kv_cols = w_keyval.shape[1]
    tile = min(DEPTH_TILE, depth // 2)
    vmem = pl.BlockSpec(memory_space=pltpu.VMEM)
    hbm = pl.BlockSpec(memory_space=pltpu.HBM)
    per_half = SEL * q_cols // (HD * TILE_COLS * HALVES)
    behind = SEL // HD if kv_cols == TILE_COLS else 0
    outs = [(per_half, HD, TILE_COLS)] * (HALVES - 1) + [(per_half + behind, HD, TILE_COLS)]
    if not behind:
        outs.append((SEL, kv_cols))
    return pl.pallas_call(
        functools.partial(project_kernel, len(blocks)),
        in_specs=[pl.BlockSpec(memory_space=pltpu.SMEM)]
        + [vmem] * (len(blocks) + 2)
        + [hbm] * 2
        + [vmem] * 2,
        out_specs=[vmem] * len(outs),
        out_shape=[jax.ShapeDtypeStruct(shape, jnp.bfloat16) for shape in outs],
        scratch_shapes=[
            pltpu.VMEM((SEL, q_cols), jnp.float32),
            pltpu.VMEM((SEL, kv_cols), jnp.float32),
            pltpu.VMEM((SEL, q_cols), jnp.float32),
            pltpu.VMEM((SEL, kv_cols), jnp.float32),
            pltpu.VMEM((SLOTS, tile, q_cols), jnp.bfloat16),
            pltpu.VMEM((SLOTS, tile, kv_cols), jnp.bfloat16),
            pltpu.SemaphoreType.DMA((2, SLOTS)),
        ],
        compiler_params=megabytes(32),
        cost_estimate=QUICK,
        name="project",
    )(place, *blocks, left, right, w_query, w_keyval, *tables)


def select_kernel(n_dest, n_src, place_ref, slot_ref, head_ref, *refs):
    sources = refs[:n_src]
    outs = refs[n_src : n_src + n_dest]
    held, sems, out_sems = refs[n_src + n_dest :]
    for doc in range(DOCS):
        for src in range(n_src):

            @pl.when(place_ref[doc] == src)
            def _():
                for dest in range(n_dest):
                    cols = pl.ds(pl.multiple_of(head_ref[dest] * HD, HD), HD)
                    pltpu.make_async_copy(
                        sources[src].at[slot_ref[doc], :, :, cols],
                        held.at[dest, :, doc],
                        sems.at[dest, doc],
                    ).start()

    for dest in range(n_dest):
        for doc in range(DOCS):
            pltpu.make_async_copy(
                sources[0].at[0, :, :, 0:HD], held.at[dest, :, doc], sems.at[dest, doc]
            ).wait()
        pltpu.make_async_copy(held.at[dest], outs[dest], out_sems.at[dest]).start()
    for dest in range(n_dest):
        pltpu.make_async_copy(held.at[dest], outs[dest], out_sems.at[dest]).wait()


def select_docs(sources, place, slot, heads, n_dest):
    tokens = sources[0].shape[2]
    shape = (2, DOCS, tokens, HD)
    smem = pl.BlockSpec(memory_space=pltpu.SMEM)
    return pl.pallas_call(
        functools.partial(select_kernel, n_dest, len(sources)),
        in_specs=[smem] * 3 + [pl.BlockSpec(memory_space=pl.ANY)] * len(sources),
        out_specs=[pl.BlockSpec(memory_space=pltpu.HBM)] * n_dest,
        out_shape=[jax.ShapeDtypeStruct(shape, jnp.bfloat16)] * n_dest,
        scratch_shapes=[
            pltpu.VMEM((n_dest, *shape), jnp.bfloat16),
            pltpu.SemaphoreType.DMA((n_dest, DOCS)),
            pltpu.SemaphoreType.DMA((n_dest,)),
        ],
        compiler_params=megabytes(16),
        cost_estimate=QUICK,
        name="select_docs",
    )(place, slot, heads, *sources)


def split_exact(value):
    pieces = []
    for _ in range(3):
        pieces.append(value.astype(jnp.bfloat16).astype(jnp.float32))
        value = value - pieces[-1]
    return pieces


def attend_kernel(n_chunks, with_new, tile_q, first_token, first_ref, qmin_ref, qmax_ref, *refs):
    refs = list(refs)
    take = lambda count: [refs.pop(0) for _ in range(count)]
    chunks = take(n_chunks)
    dead_ref, qpos_ref, queries = take(3)
    if with_new:
        cos_ref, sin_ref, new_ref = take(3)
    if with_new:
        top, total, summed, values, new_key, new_value = take(6)
    else:
        packed, top, total, summed, values = take(5)
    together = min(PAIR, qpos_ref.shape[0])
    n_pairs = qpos_ref.shape[0] // together
    tokens = chunks[0].shape[2]
    scale = math.log2(math.e) / math.sqrt(HD)

    for chunk in range(n_chunks):
        for doc in range(DOCS):
            values[doc, :, chunk * tokens : (chunk + 1) * tokens] = chunks[chunk][1, doc].T
    if with_new:
        new_key[...] = rotate(
            new_ref[:, :HD].astype(jnp.float32), cos_ref[...], sin_ref[...]
        ).astype(jnp.bfloat16)
        new_value[...] = new_ref[:, HD:].T

    one_row = jnp.where(
        lax.broadcasted_iota(jnp.int32, (HD, TILE_COLS), 0) == 0, 1.0, 0.0
    ).astype(jnp.bfloat16)

    def update(tile, parts):
        best = functools.reduce(
            jnp.maximum, [jnp.max(scores, axis=0, keepdims=True) for scores, _ in parts]
        )
        old = top[tile]
        new = jnp.maximum(old, best)
        shrink = jnp.exp2((old - new) * scale)
        running = total[tile] * shrink
        mixed = summed[tile] * shrink
        for scores, value in parts:
            weights = jnp.exp2((scores - new) * scale)
            running += jnp.sum(weights, axis=0, keepdims=True)
            mixed += jnp.dot(
                value, weights.astype(jnp.bfloat16), preferred_element_type=jnp.float32
            )
        top[tile] = new
        total[tile] = running
        summed[tile] = mixed

    @pl.loop(0, n_pairs)
    def _(pair):
        tiles = [pair * together + i for i in range(together)]
        for tile in tiles:
            top[tile] = jnp.full(top.shape[1:], MASKED, jnp.float32)
            total[tile] = jnp.zeros(total.shape[1:], jnp.float32)
            summed[tile] = jnp.zeros(summed.shape[1:], jnp.float32)
        if with_new:
            fresh = []
            for tile in tiles:
                scores = jnp.dot(new_key[...], queries[tile], preferred_element_type=jnp.float32)
                key_index = lax.broadcasted_iota(jnp.int32, scores.shape, 0)
                q_index = first_token + tile * tile_q + lax.broadcasted_iota(jnp.int32, scores.shape, 1) % tile_q
                fresh.append(jnp.where(key_index <= q_index, scores, MASKED))
            for tile, scores in zip(tiles, fresh):
                update(tile, [(scores, new_value[...])])

        @pl.loop(0, DOCS)
        def _(doc):
            firsts = [first_ref[doc * n_chunks + chunk] for chunk in range(n_chunks)]
            lowest = functools.reduce(jnp.minimum, firsts)
            reach = functools.reduce(jnp.maximum, firsts) + tokens - 1

            def visit(masked):
                found = []
                for tile in tiles:
                    extended = jnp.concatenate([queries[tile], one_row], axis=0)
                    parts = []
                    for chunk in range(n_chunks):
                        span = slice(chunk * tokens, (chunk + 1) * tokens)
                        keys = jnp.concatenate(
                            [chunks[chunk][0, doc], dead_ref[doc, span, :]], axis=1
                        )
                        scores = jnp.dot(keys, extended, preferred_element_type=jnp.float32)
                        if masked:
                            key_pos = firsts[chunk] + lax.broadcasted_iota(
                                jnp.int32, scores.shape, 0
                            )
                            scores = jnp.where(key_pos <= qpos_ref[tile], scores, MASKED)
                        parts.append((scores, values[doc, :, span]))
                    found.append(parts)
                for tile, parts in zip(tiles, found):
                    update(tile, parts)

            live = lowest <= qmax_ref[pair]
            whole = reach <= qmin_ref[pair]

            @pl.when(live & whole)
            def _():
                visit(False)

            @pl.when(live & jnp.logical_not(whole))
            def _():
                visit(True)

        if not with_new:
            for tile in tiles:
                extra = jnp.concatenate(
                    split_exact(top[tile])
                    + split_exact(total[tile])
                    + [jnp.zeros((STATS - 6, TILE_COLS), jnp.float32)],
                    axis=0,
                )
                packed[tile] = jnp.concatenate([summed[tile], extra], axis=0).astype(jnp.bfloat16)


def attend(chunks, dead, first_pos, positions, first_token, queries, n_tiles, fresh):
    n_chunks = len(chunks)
    tokens = chunks[0].shape[2]
    tile_q = positions.shape[0] // n_tiles
    together = min(PAIR, n_tiles)
    by_pair = positions.reshape(n_tiles // together, together * tile_q)
    q_pos = jnp.tile(positions.reshape(n_tiles, tile_q), (1, TILE_COLS // tile_q))
    q_pos = q_pos.reshape(n_tiles, 1, TILE_COLS)
    smem = pl.BlockSpec(memory_space=pltpu.SMEM)
    vmem = pl.BlockSpec(memory_space=pltpu.VMEM)
    operands = [first_pos, by_pair[:, 0], by_pair[:, -1], *chunks, dead, q_pos, queries, *fresh]
    state = [((n_tiles, 1, TILE_COLS), jnp.float32)] * 2
    state += [((n_tiles, HD, TILE_COLS), jnp.float32)]
    values = ((DOCS, HD, n_chunks * tokens), jnp.bfloat16)
    if fresh:
        outs = state
        scratch = [values, ((SEL, HD), jnp.bfloat16), ((HD, SEL), jnp.bfloat16)]
    else:
        outs = [((n_tiles, HD + STATS, TILE_COLS), jnp.bfloat16)]
        scratch = state + [values]
    pairs = n_tiles * TILE_COLS * DOCS * n_chunks * tokens // 2
    return pl.pallas_call(
        functools.partial(attend_kernel, n_chunks, bool(fresh), tile_q, first_token),
        in_specs=[smem] * 3 + [vmem] * (len(operands) - 3),
        out_specs=[vmem] * len(outs),
        out_shape=[jax.ShapeDtypeStruct(*s) for s in outs],
        scratch_shapes=[pltpu.VMEM(*s) for s in scratch],
        compiler_params=megabytes(20),
        cost_estimate=QUICK,
        name="attend",
    )(*operands)


def merge_kernel(*refs):
    out_ref = refs[-1]
    scale = math.log2(math.e) / math.sqrt(HD)
    for half in range(HALVES):
        top_a, total_a, mixed_a, packed = refs[4 * half : 4 * half + 4]
        n_tiles = top_a.shape[0]
        tile_q = SEL // HALVES // n_tiles
        for tile in range(n_tiles):
            extra = packed[tile, HD:, :].astype(jnp.float32)
            top_b = extra[0:1] + (extra[1:2] + extra[2:3])
            total_b = extra[3:4] + (extra[4:5] + extra[5:6])
            new = jnp.maximum(top_a[tile], top_b)
            part_a = jnp.exp2((top_a[tile] - new) * scale)
            part_b = jnp.exp2((top_b - new) * scale)
            total = total_a[tile] * part_a + total_b * part_b
            mixed = mixed_a[tile] * part_a + packed[tile, :HD, :].astype(jnp.float32) * part_b
            finished = (mixed / total).T.astype(jnp.bfloat16)
            here = slice((half * n_tiles + tile) * tile_q, (half * n_tiles + tile + 1) * tile_q)
            for head in range(TILE_COLS // tile_q):
                out_ref[here, head * HD : (head + 1) * HD] = finished[
                    head * tile_q : (head + 1) * tile_q, :
                ]


def merge(mine, theirs):
    n_tiles = mine[0][0].shape[0] * HALVES
    shape = (SEL, TILE_COLS * n_tiles // SEL * HD)
    operands = [a for state, packed in zip(mine, theirs) for a in (*state, packed)]
    return pl.pallas_call(
        merge_kernel,
        out_shape=jax.ShapeDtypeStruct(shape, jnp.bfloat16),
        compiler_params=megabytes(16),
        cost_estimate=QUICK,
        name="merge",
    )(*operands)


def out_kernel(n_blocks, first_col, place_ref, x_ref, w_ref, *refs):
    outs = refs[: n_blocks + 1]
    ordered, slots, sems = refs[n_blocks + 1 :]
    rows = SEL // n_blocks
    tile = slots.shape[2]
    width = outs[0].shape[1]
    count = width // tile
    source = lambda step: w_ref.at[:, pl.ds(pl.multiple_of(first_col + step * tile, tile), tile)]
    start, wait = stream([source], [slots], sems, count)

    for step in range(SLOTS - 1):
        start(step)
    for block in range(n_blocks):
        there = pl.ds(pl.multiple_of(place_ref[block] * rows, rows), rows)
        ordered[block * rows : (block + 1) * rows, :] = x_ref[there, :]
    for side in range(2):
        offset = side * count // 2

        @pl.loop(offset, offset + count // 2)
        def _(step):
            @pl.when(step + SLOTS - 1 < count)
            def _():
                start(step + SLOTS - 1)

            wait(step)
            product = jnp.dot(
                ordered[...].astype(jnp.bfloat16),
                slots[lax.rem(step, SLOTS)],
                preferred_element_type=jnp.float32,
            )
            cols = pl.ds(pl.multiple_of(step * tile, tile), tile)
            far_cols = pl.ds(pl.multiple_of((step - offset) * tile, tile), tile)
            for block in range(n_blocks - 1):
                outs[block][:, cols] = product[block * rows : (block + 1) * rows, :]
            outs[n_blocks - 1 + side][:, far_cols] = product[(n_blocks - 1) * rows :, :].astype(
                jnp.bfloat16
            )


def project_out(place, attention, w_out, chunk, n_chunks, n_blocks):
    depth = w_out.shape[0]
    width = w_out.shape[1] // n_chunks
    rows = SEL // n_blocks
    if rows % 16:
        attention = attention.astype(jnp.float32)
    vmem = pl.BlockSpec(memory_space=pltpu.VMEM)
    return pl.pallas_call(
        functools.partial(out_kernel, n_blocks, chunk * width),
        in_specs=[
            pl.BlockSpec(memory_space=pltpu.SMEM),
            vmem,
            pl.BlockSpec(memory_space=pltpu.HBM),
        ],
        out_specs=[vmem] * (n_blocks + 1),
        out_shape=[jax.ShapeDtypeStruct((rows, width), jnp.float32)] * (n_blocks - 1)
        + [jax.ShapeDtypeStruct((rows, width // 2), jnp.bfloat16)] * 2,
        scratch_shapes=[
            pltpu.VMEM((SEL, depth), attention.dtype),
            pltpu.VMEM((SLOTS, depth, WIDTH_TILE), jnp.bfloat16),
            pltpu.SemaphoreType.DMA((1, SLOTS)),
        ],
        compiler_params=megabytes(50),
        cost_estimate=QUICK,
        name="project_out",
    )(place, attention, w_out)


def per_device(
    hidden_in, norm_gain, w_query, w_keyval, w_out, pool_cache, doc_slot, doc_blocks, sel_pos
):
    tp_size = lax.axis_size("tp")
    req_size = lax.axis_size("req")
    me = lax.axis_index("tp")
    rows, width = hidden_in.shape
    slots, tokens = pool_cache.shape[:2]
    heads_here = w_query.shape[1] // HD
    selected = sel_pos[0]
    lengths = doc_blocks[0] * BLOCK

    if tp_size == KVH:
        ring = [*range(0, tp_size, 2), *range(tp_size - 1, 0, -2)]
    else:
        ring = list(range(tp_size))
    far = tp_size // 2
    forth = [(ring[p], ring[(p + 1) % tp_size]) for p in range(tp_size)]
    back = [(dst, src) for src, dst in forth]
    steps = [0] + [sign * k for k in range(1, far) for sign in (-1, 1)] + [far]
    table = [[ring[(ring.index(i) + s) % tp_size] for s in steps] for i in range(tp_size)]
    place = jnp.array(table, jnp.int32)[me]

    widened = hidden_in.astype(jnp.float32)
    normed = (
        widened
        * lax.rsqrt(jnp.mean(widened * widened, axis=-1, keepdims=True) + EPSILON)
        * norm_gain
    ).astype(jnp.bfloat16)
    normed, pool_cache = lax.optimization_barrier((normed, pool_cache))

    middle = tp_size // 2
    by_kind = pool_cache.transpose(0, 2, 1, 3)
    sources = [by_kind]
    for shift in range(1, req_size):
        sources.append(
            lax.ppermute(by_kind, "req", [((i + shift) % req_size, i) for i in range(req_size)])
        )
    holder = (doc_slot // slots - lax.axis_index("req")) % req_size
    order = jnp.arange(middle, dtype=jnp.int32)
    takers = jnp.concatenate([me ^ order, me ^ order ^ middle])
    sent = select_docs(sources, holder, doc_slot % slots, takers * KVH // tp_size, tp_size)

    cosine, sine_part = rotation_tables(selected)
    before = behind = normed
    blocks = [normed]
    for k in range(1, far):
        before = lax.ppermute(before, "tp", forth)
        behind = lax.ppermute(behind, "tp", back)
        if k == min(2, far - 1):
            before, behind, *sent = lax.optimization_barrier((before, behind, *sent))
        blocks += [before, behind]
    left = lax.ppermute(before[:, : width // 2], "tp", forth)
    right = lax.ppermute(behind[:, width // 2 :], "tp", back)
    if rows % 16:
        blocks = [jnp.concatenate(blocks, axis=0)]
    projected = project(place, blocks, left, right, w_query, w_keyval, (cosine, sine_part))
    chunks = [
        [
            lax.ppermute(sent[slot * middle + j], "tp", [(i, i ^ j) for i in range(tp_size)])
            if j
            else sent[slot * middle]
            for j in range(middle)
        ]
        for slot in range(2)
    ]
    *queries, chunks[1] = lax.optimization_barrier((*projected[:HALVES], chunks[1]))
    n_tiles = queries[0].shape[0]
    across = [(i, i ^ middle) for i in range(tp_size)]
    their_queries = [None] * HALVES
    for part in reversed(range(HALVES)):
        their_queries[part] = lax.ppermute(queries[part], "tp", across)

    offsets = jnp.cumsum(lengths) - lengths
    first_slot = (me ^ order) * tokens
    slot_tokens = first_slot[:, None] + jnp.arange(tokens, dtype=jnp.int32)[None, :]
    cache_pos = offsets[:, None, None] + slot_tokens[None]
    is_valid = slot_tokens[None] < lengths[:, None, None]
    replaced = jnp.any(cache_pos[..., None] == selected, axis=-1)
    dead = jnp.where(is_valid & jnp.logical_not(replaced), 0.0, MASKED).astype(jnp.bfloat16)
    dead = jnp.broadcast_to(dead[..., None], (DOCS, middle, tokens, HD))
    dead = dead.reshape(DOCS, middle * tokens, HD)
    first_pos = jnp.where(
        first_slot[None] < lengths[:, None], offsets[:, None] + first_slot[None], FAR
    ).reshape(-1)

    if tp_size == KVH:
        is_key = me < middle
        here = queries[-1][n_tiles:].reshape(SEL, 2 * HD)
        there = their_queries[-1][n_tiles:].reshape(SEL, 2 * HD)
        keys, vals = jnp.where(is_key, here, there), jnp.where(is_key, there, here)
        new = lax.ppermute(
            jnp.concatenate(
                [
                    jnp.where(is_key, keys[:, :HD], keys[:, HD:]),
                    jnp.where(is_key, vals[:, :HD], vals[:, HD:]),
                ],
                axis=1,
            ),
            "tp",
            [(i, 2 * i if i < middle else 2 * (i - middle) + 1) for i in range(tp_size)],
        )
    else:
        everyone = lax.all_gather(projected[-1], "tp", axis=1, tiled=True)
        my_head = me * KVH // tp_size
        new = jnp.concatenate(
            [
                lax.dynamic_slice_in_dim(everyone, (kind * KVH + my_head) * HD, HD, axis=1)
                for kind in range(2)
            ],
            axis=1,
        )

    size = SEL // HALVES

    def attend_half(part, asked, slot, extra):
        span = slice(part * size, (part + 1) * size)
        return attend(
            chunks[slot], dead, first_pos, selected[span], part * size, asked[part], n_tiles, extra
        )

    theirs = [None] * HALVES
    for part in reversed(range(HALVES)):
        (packed,) = attend_half(part, their_queries, 1, [])
        if part:
            packed, new, their_queries[part - 1] = lax.optimization_barrier(
                (packed, new, their_queries[part - 1])
            )
        theirs[part] = lax.ppermute(packed, "tp", across)
    fresh = [cosine, sine_part, new]
    mine = [attend_half(part, queries, 0, fresh) for part in range(HALVES)]
    attention = merge(mine, theirs)

    finished = []
    for chunk in range(REDUCE_CHUNKS):
        pieces = project_out(place, attention, w_out, chunk, REDUCE_CHUNKS, tp_size)
        total = pieces[0]
        to_forth, to_back = pieces[2 : tp_size - 1 : 2], pieces[1 : tp_size - 1 : 2]
        cut = pieces[-1].shape[1]
        ahead = lax.ppermute(pieces[-2], "tp", forth).astype(jnp.float32)
        astern = lax.ppermute(pieces[-1], "tp", back).astype(jnp.float32)
        for k in range(far - 1, 0, -1):
            up, down = to_forth[k - 1], to_back[k - 1]
            if k == far - 1:
                up = jnp.concatenate([up[:, :cut] + ahead, up[:, cut:]], axis=1)
                down = jnp.concatenate([down[:, :cut], down[:, cut:] + astern], axis=1)
            else:
                up, down = up + ahead, down + astern
            ahead = lax.ppermute(up.astype(jnp.bfloat16), "tp", forth).astype(jnp.float32)
            astern = lax.ppermute(down.astype(jnp.bfloat16), "tp", back).astype(jnp.float32)
        finished.append((total + ahead + astern).astype(jnp.bfloat16))
    return jnp.concatenate(finished, axis=1)


def solution(mesh):
    placed = (
        P(("groups", "req", "tp"), None),
        P(),
        P(None, "tp"),
        P(None, "tp"),
        P("tp", None),
        P(("groups", "req"), "tp", None, None),
        P(("groups", "req")),
        P(("groups", "req"), None),
        P(("groups", "req"), None),
    )
    return jax.shard_map(
        per_device,
        mesh=mesh,
        in_specs=placed,
        out_specs=P(("groups", "req", "tp"), None),
        check_vma=False,
    )
```

time: 201 us -> 240 us (1.19)
  waiting for transfers between devices: 32 us -> 86.1 us
  starting transfers between devices: 70.9 us -> 44.8 us
  local copies, waits for them, and re-layouts: 26.6 us -> 34.7 us
    ppermute x9 -> x7, waiting for transfers between devices: 2.64 us -> 38.3 us  [the longest x1 17.5 us: per_device(): left = lax.ppermute(before[:, :width // 2], 'tp', forth)]
    ppermute x9 -> x7, starting transfers between devices: 31.1 us -> 9.49 us  [the longest x2 2.99 us: per_device(): theirs[part] = lax.ppermute(packed, 'tp', across)]
    ppermute x6 -> x3, waiting for transfers between devices: 10.6 us -> 25.4 us  [per_device(): before = lax.ppermute(before, 'tp', forth)]
    ppermute x6, starting transfers between devices: 1.66 us -> 15.2 us  [per_device(): lax.ppermute(down.astype(jnp.bfloat16), 'tp', back).astype(jnp.float32)]
    ppermute x6, starting transfers between devices: 12.1 us -> 0.36 us  [per_device(): lax.ppermute(up.astype(jnp.bfloat16), 'tp', forth).astype(jnp.float32)]
    ppermute x6 -> x3, starting transfers between devices: 12.8 us -> 5.95 us  [per_device(): before = lax.ppermute(before, 'tp', forth)]
    ppermute x2, starting transfers between devices: 0.13 us -> 5.37 us  [per_device(): astern = lax.ppermute(pieces[-1], 'tp', back).astype(jnp.float32)]
    ppermute x2, starting transfers between devices: 5.52 us -> 0.34 us  [per_device(): ahead = lax.ppermute(pieces[-2], 'tp', forth).astype(jnp.float32)]
  transfers between devices with their start and end apart: 44 -> 36, of which waited for: 12 -> 22; matrix products, arithmetic and copies ran while one was open for 5% -> 9% of each run, Pallas kernels for 27% -> 23%
where the time goes in v4:
time: 240 us; the launch traced here: 239 us
  waiting for transfers between devices  86.1 us (36%)
  Pallas kernels  61.6 us (26%)
  starting transfers between devices  44.8 us (19%)
  local copies, waits for them, and re-layouts  34.7 us (14%)
  other arithmetic  10.9 us (5%)
    pallas_call x4, Pallas kernels, attend(): pl.pallas_call(functools.partial(attend_kernel, n_chunks, bool(fresh), ti...  31.7 us
    ppermute x3, waiting for transfers between devices, per_device(): before = lax.ppermute(before, 'tp', forth)  25.4 us
    ppermute x1, waiting for transfers between devices, per_device(): left = lax.ppermute(before[:, :width // 2], 'tp', forth)  17.5 us
    unnamed x58, local copies, waits for them, and re-layouts  16.2 us
    ppermute x6, starting transfers between devices, per_device(): lax.ppermute(down.astype(jnp.bfloat16), 'tp', back).astype(jnp.float32)  15.2 us
    ppermute x6, waiting for transfers between devices, per_device(): lax.ppermute(up.astype(jnp.bfloat16), 'tp', forth).astype(jnp.float32)  13.5 us
    pallas_call x2, Pallas kernels, project_out(): pl.pallas_call(functools.partial(out_kernel, n_blocks, chunk * width), in...  13.4 us
    pallas_call x1, Pallas kernels, project(): pl.pallas_call(functools.partial(project_kernel, len(blocks)), in_specs=[...  11.4 us
  transfers between devices with their start and end apart: 36, of which 22 were waited for; matrix products, arithmetic and copies ran while one was open for 9% of the time, Pallas kernels for 23%

profile of v4, /device:TPU:0, one launch (start us, length us, event | category | flops | bytes accessed | tf_op | source)
XLA Modules:
  0.0 238.5 jit_solution(9789206713927767519)
XLA Ops:
  0.0 1.2 fusion
  1.3 1.2 fusion.2.refs_0_
  2.5 5.5 %copy.17 = bf16[4,256,2,1024]{3,1,2,0:T(8,128)(2,1)} copy(bf16[4,256,2,1024]{3,2,1,0:T(2,128)(2,1)} %param.15) | data formatting | bytes 8388608 | tf_op jit(solution)/shard_map/optimization_barrier | solution.py:506
  8.5 2.6 %collective-permute-start = (bf16[32,8192]{1,0:T(8,128)(2,1)S(1)}, bf16[32,8192]{1,0:T(8,128)(2,1)S(1)}, u32[]{:S(2)}, u32[]{:S(2)}) collective-permute-start(bf16[32,8192]{1,0:T(8,128)(2,1)S(1)} %fusion.2.refs_0_), channel_id=1, source_target_pairs={{0,2},{2,4},{4,6},{6,7},{7,5},{5,3},{3,1},{1,0},{8,10},{10,12},{12... | collective-permute-start | bytes 1572872 | tf_op jit(solution)/shard_map/ppermute | solution.py:524
  12.0 11.6 %collective-permute-done.refs_1_ = bf16[32,8192]{1,0:T(8,128)(2,1)S(1)} collective-permute-done((bf16[32,8192]{1,0:T(8,128)(2,1)S(1)}, bf16[32,8192]{1,0:T(8,128)(2,1)S(1)}, u32[]{:S(2)}, u32[]{:S(2)}) %collective-permute-start) | collective-permute-done | bytes 524320 | tf_op jit(solution)/shard_map/ppermute | solution.py:524
  23.6 1.8 collective-permute-start.1
  25.7 1.3 compare_reduce_fusion
  27.1 4.8 %select_docs.1 = (bf16[2,4,256,128]{3,2,1,0:T(8,128)(2,1)S(1)}, bf16[2,4,256,128]{3,2,1,0:T(8,128)(2,1)}, bf16[2,4,256,128]{3,2,1,0:T(8,128)(2,1)}, bf16[2,4,256...) custom-call(s32[4]{0:T(128)S(1)} %get-tuple-element.131.place_ref, ...), custom_call_target="tpu_custom_call" | custom-call | flops 1 | bytes 1 | tf_op jit(solution)/shard_map/select_docs/pallas_call | solution.py:202
  31.9 5.6 %collective-permute-done.1.refs_3_ = bf16[32,8192]{1,0:T(8,128)(2,1)} collective-permute-done((bf16[32,8192]{1,0:T(8,128)(2,1)S(1)}, bf16[32,8192]{1,0:T(8,128)(2,1)}, u32[]{:S(2)}, u32[]{:S(2)}) %collective-permute-start.1) | collective-permute-done | bytes 524320 | tf_op jit(solution)/shard_map/ppermute | solution.py:524
  37.5 1.3 collective-permute-done.3.refs_4_
  38.8 1.6 collective-permute-start.8
  40.8 1.3 fusion.3
  42.5 1.5 collective-permute-start.13
  44.1 1.5 collective-permute-start.14
  45.6 8.3 %collective-permute-done.8.refs_5_ = bf16[32,8192]{1,0:T(8,128)(2,1)S(1)} collective-permute-done((bf16[32,8192]{1,0:T(8,128)(2,1)}, bf16[32,8192]{1,0:T(8,128)(2,1)S(1)}, u32[]{:S(2)}, u32[]{:S(2)}) %collective-permute-start.8) | collective-permute-done | bytes 524320 | tf_op jit(solution)/shard_map/ppermute | solution.py:524
  55.4 1.6 collective-permute-start.10
  58.9 1.2 slice_reduce_fusion.4
  60.9 1.2 pad_maximum_fusion.5
  62.1 17.5 %collective-permute-done.10.refs_7_ = bf16[32,4096]{1,0:T(8,128)(2,1)} collective-permute-done((bf16[32,4096]{1,0:T(8,128)(2,1)}, bf16[32,4096]{1,0:T(8,128)(2,1)}, u32[]{:S(2)}, u32[]{:S(2)}) %collective-permute-start.10) | collective-permute-done | bytes 262176 | tf_op jit(solution)/shard_map/ppermute | solution.py:529
  79.6 1.3 collective-permute-done.11.refs_8_
  80.9 2.2 copy-done.1
  83.1 1.0 copy-done.7
  84.1 1.0 copy-done.9
  85.2 1.0 copy-done.15
  86.2 1.0 copy-done.17
  87.3 11.4 %project.1 = (bf16[4,128,256]{2,1,0:T(8,128)(2,1)}, bf16[6,128,256]{2,1,0:T(8,128)(2,1)S(1)}) custom-call(s32[8]{0:T(128)S(1)} %dynamic-slice_bitcast_fusion.place_ref, bf16[32,8192]{1,0:T(8,128)(2,1)S(1)} %fusion.2.refs_0_, bf16[32,8192]{1,0:T(8,128)(2,1)S(1)} %copy-done.15, bf16[32,8192]{1,0:T(8,128)(2,1)S(1)} %copy-done.17, ...), custom_call_target="tpu_custom_call" | custom-call | flops 1 | bytes 1 | tf_op jit(solution)/shard_map/project/pallas_call | solution.py:148
  100.3 2.5 %collective-permute-start.15 = (bf16[6,128,256]{2,1,0:T(8,128)(2,1)S(1)}, bf16[6,128,256]{2,1,0:T(8,128)(2,1)S(1)}, u32[]{:S(2)}, u32[]{:S(2)}) collective-permute-start(bf16[6,128,256]{2,1,0:T(8,128)(2,1)S(1)} %get-tuple-element.87.refs_6_), channel_id=1, source_target_pairs={{0,4},{1,5},{2,6},{3,7},{4,0},{5,1},{6,2},{7,3},{8,12},{9,13},{10,... | collective-permute-start | bytes 1179656 | tf_op jit(solution)/shard_map/ppermute | solution.py:548
  104.1 1.1 collective-permute-start.6
  105.2 2.4 %collective-permute-start.7 = (bf16[2,4,256,128]{3,2,1,0:T(8,128)(2,1)}, bf16[2,4,256,128]{3,2,1,0:T(8,128)(2,1)S(1)}, u32[]{:S(2)}, u32[]{:S(2)}) collective-permute-start(bf16[2,4,256,128]{3,2,1,0:T(8,128)(2,1)} %get-tuple-element.73), channel_id=1, source_target_pairs={{0,3},{1,2},{2,1},{3,0},{4,7},{5,6},{6,5},{7,4},{8,11},{9,10},{10,... | collective-permute-start | bytes 1572872 | tf_op jit(solution)/shard_map/ppermute | solution.py:536
  108.1 10.1 %collective-permute-done.15.refs_6_ = bf16[6,128,256]{2,1,0:T(8,128)(2,1)S(1)} collective-permute-done((bf16[6,128,256]{2,1,0:T(8,128)(2,1)S(1)}, bf16[6,128,256]{2,1,0:T(8,128)(2,1)S(1)}, u32[]{:S(2)}, u32[]{:S(2)}) %collective-permute-start.15) | collective-permute-done | bytes 393248 | tf_op jit(solution)/shard_map/ppermute | solution.py:548
  120.4 1.6 collective-permute-start.16
  125.7 1.4 reshape.156
  130.1 1.3 broadcast_in_dim.16.refs_4_
  131.5 1.0 copy-done.3
  132.5 1.0 copy-done.5
  135.9 8.8 %attend.4 = bf16[4,144,256]{2,1,0:T(8,128)(2,1)S(1)} custom-call(s32[16]{0:T(128)S(1)} %select_n.72.first_ref, s32[2]{0:T(128)S(1)} %copy-done.19, s32[2]{0:T(128)S(1)} %copy-done.18, bf16[2,4,256,128]{3,2,1,0:T(8,128)(2,1)S(1)} %get-tuple-element.83.refs_0_, bf16[2,4,256,128]{3,2,1,0:T(8,128)(2,1)S(1)} %collective-permute-done.12.refs_1_, ...), custom_call_target="tpu_custom_call" | custom-call | flops 1 | bytes 1 | tf_op jit(solution)/shard_map/attend/pallas_call | solution.py:361
  144.6 6.2 %attend.6 = bf16[4,144,256]{2,1,0:T(8,128)(2,1)S(1)} custom-call(s32[16]{0:T(128)S(1)} %select_n.72.first_ref, s32[2]{0:T(128)S(1)} %get-tuple-element.120.qmin_ref, s32[2]{0:T(128)S(1)} %get-tuple-element.119.qmax_ref, bf16[2,4,256,128]{3,2,1,0:T(8,128)(2,1)S(1)} %get-tuple-element.83.refs_0_, bf16[2,4,256,128]{3,2,1,0:T(8,128)(2,1)S(1)} %collective-permute-done.12.refs_1_, ...), custom_call_target="tpu_custom_call" | custom-call | flops 1 | bytes 1 | tf_op jit(solution)/shard_map/attend/pallas_call | solution.py:361
  150.8 2.7 %collective-permute-start.18 = (bf16[4,144,256]{2,1,0:T(8,128)(2,1)S(1)}, bf16[4,144,256]{2,1,0:T(8,128)(2,1)S(1)}, u32[]{:S(2)}, u32[]{:S(2)}) collective-permute-start(bf16[4,144,256]{2,1,0:T(8,128)(2,1)S(1)} %attend.6), channel_id=1, source_target_pairs={{0,4},{1,5},{2,6},{3,7},{4,0},{5,1},{6,2},{7,3},{8,12},{9,13},{10,... | collective-permute-start | bytes 884744 | tf_op jit(solution)/shard_map/ppermute | solution.py:605
  153.8 9.6 %attend.7 = (f32[4,1,256]{2,1,0:T(1,128)S(1)}, f32[4,1,256]{2,1,0:T(1,128)S(1)}, f32[4,128,256]{2,1,0:T(8,128)S(1)}) custom-call(s32[16]{0:T(128)S(1)} %select_n.72.first_ref, s32[2]{0:T(128)S(1)} %copy-done.19, s32[2]{0:T(128)S(1)} %copy-done.18, bf16[2,4,256,128]{3,2,1,0:T(8,128)(2,1)S(1)} %get-tuple-element.70.refs_0_, ...), custom_call_target="tpu_custom_call" | custom-call | flops 1 | bytes 1 | tf_op jit(solution)/shard_map/attend/pallas_call | solution.py:361
  163.5 7.1 %attend.5 = (f32[4,1,256]{2,1,0:T(1,128)S(1)}, f32[4,1,256]{2,1,0:T(1,128)S(1)}, f32[4,128,256]{2,1,0:T(8,128)S(1)}) custom-call(s32[16]{0:T(128)S(1)} %select_n.72.first_ref, s32[2]{0:T(128)S(1)} %get-tuple-element.120.qmin_ref, s32[2]{0:T(128)S(1)} %get-tuple-element.119.qmax_ref, bf16[2,4,256,128]{3,2,1,0:T(8,128)(2,1)S(1)} %get-tuple-element.70.refs_0_, ...), custom_call_target="tpu_custom_call" | custom-call | flops 1 | bytes 1 | tf_op jit(solution)/shard_map/attend/pallas_call | solution.py:361
  170.6 3.0 %collective-permute-done.18.refs_3_ = bf16[4,144,256]{2,1,0:T(8,128)(2,1)S(1)} collective-permute-done((bf16[4,144,256]{2,1,0:T(8,128)(2,1)S(1)}, bf16[4,144,256]{2,1,0:T(8,128)(2,1)S(1)}, u32[]{:S(2)}, u32[]{:S(2)}) %collective-permute-start.18) | collective-permute-done | bytes 294944 | tf_op jit(solution)/shard_map/ppermute | solution.py:605
  173.6 6.3 %collective-permute-done.19.refs_7_ = bf16[4,144,256]{2,1,0:T(8,128)(2,1)S(1)} collective-permute-done((bf16[4,144,256]{2,1,0:T(8,128)(2,1)S(1)}, bf16[4,144,256]{2,1,0:T(8,128)(2,1)S(1)}, u32[]{:S(2)}, u32[]{:S(2)}) %collective-permute-start.19) | collective-permute-done | bytes 294944 | tf_op jit(solution)/shard_map/ppermute | solution.py:605
  181.1 6.7 %project_out.2 = (f32[32,4096]{1,0:T(8,128)S(1)}, f32[32,4096]{1,0:T(8,128)S(1)}, f32[32,4096]{1,0:T(8,128)S(1)}, f32[32,4096]{1,0:T(8,128)S(1)}, f32[32,4096]{1...) custom-call(s32[8]{0:T(128)S(1)} %dynamic-slice_bitcast_fusion.place, ...), custom_call_target="tpu_custom_call" | custom-call | flops 1 | bytes 1 | tf_op jit(solution)/shard_map/project_out/pallas_call | solution.py:456
  188.1 6.7 %project_out.3 = (f32[32,4096]{1,0:T(8,128)S(1)}, f32[32,4096]{1,0:T(8,128)S(1)}, f32[32,4096]{1,0:T(8,128)S(1)}, f32[32,4096]{1,0:T(8,128)S(1)}, f32[32,4096]{1...) custom-call(s32[8]{0:T(128)S(1)} %dynamic-slice_bitcast_fusion.place, ...), custom_call_target="tpu_custom_call" | custom-call | flops 1 | bytes 1 | tf_op jit(solution)/shard_map/project_out/pallas_call | solution.py:456
  194.8 3.3 %collective-permute-start.24 = (bf16[32,2048]{1,0:T(8,128)(2,1)S(1)}, bf16[32,2048]{1,0:T(8,128)(2,1)S(1)}, u32[]{:S(2)}, u32[]{:S(2)}) collective-permute-start(bf16[32,2048]{1,0:T(8,128)(2,1)S(1)} %get-tuple-element.105), channel_id=1, source_target_pairs={{2,0},{4,2},{6,4},{7,6},{5,7},{3,5},{1,3},{0,1},{10,8},{12,10},{14... | collective-permute-start | bytes 393224 | tf_op jit(solution)/shard_map/ppermute | solution.py:617
  198.2 2.1 collective-permute-start.32
  200.4 1.5 collective-permute-done.24
  202.0 2.5 %collective-permute-start.25 = (bf16[32,4096]{1,0:T(8,128)(2,1)S(1)}, bf16[32,4096]{1,0:T(8,128)(2,1)S(1)}, u32[]{:S(2)}, u32[]{:S(2)}) collective-permute-start(bf16[32,4096]{1,0:T(8,128)(2,1)S(1)} %pad_maximum_fusion.2), channel_id=1, source_target_pairs={{2,0},{4,2},{6,4},{7,6},{5,7},{3,5},{1,3},{0,1},{10,8},{12,10},{14... | collective-permute-start | bytes 786440 | tf_op jit(solution)/shard_map/ppermute | solution.py:626
  204.8 2.5 %collective-permute-start.33 = (bf16[32,4096]{1,0:T(8,128)(2,1)S(1)}, bf16[32,4096]{1,0:T(8,128)(2,1)S(1)}, u32[]{:S(2)}, u32[]{:S(2)}) collective-permute-start(bf16[32,4096]{1,0:T(8,128)(2,1)S(1)} %pad_maximum_fusion.4), channel_id=1, source_target_pairs={{2,0},{4,2},{6,4},{7,6},{5,7},{3,5},{1,3},{0,1},{10,8},{12,10},{14... | collective-permute-start | bytes 786440 | tf_op jit(solution)/shard_map/ppermute | solution.py:626
  207.3 2.8 %collective-permute-done.21 = bf16[32,4096]{1,0:T(8,128)(2,1)S(1)} collective-permute-done((bf16[32,4096]{1,0:T(8,128)(2,1)S(1)}, bf16[32,4096]{1,0:T(8,128)(2,1)S(1)}, u32[]{:S(2)}, u32[]{:S(2)}) %collective-permute-start.21) | collective-permute-done | bytes 262176 | tf_op jit(solution)/shard_map/ppermute | solution.py:625
  210.3 1.1 collective-permute-done.25
  211.4 2.5 %collective-permute-start.26 = (bf16[32,4096]{1,0:T(8,128)(2,1)S(1)}, bf16[32,4096]{1,0:T(8,128)(2,1)S(1)}, u32[]{:S(2)}, u32[]{:S(2)}) collective-permute-start(bf16[32,4096]{1,0:T(8,128)(2,1)S(1)} %add_convert_fusion.7), channel_id=1, source_target_pairs={{2,0},{4,2},{6,4},{7,6},{5,7},{3,5},{1,3},{0,1},{10,8},{12,10},{14... | collective-permute-start | bytes 786440 | tf_op jit(solution)/shard_map/ppermute | solution.py:626
  213.9 1.8 collective-permute-done.29
  215.9 1.1 collective-permute-done.33
  217.0 2.5 %collective-permute-start.34 = (bf16[32,4096]{1,0:T(8,128)(2,1)S(1)}, bf16[32,4096]{1,0:T(8,128)(2,1)S(1)}, u32[]{:S(2)}, u32[]{:S(2)}) collective-permute-start(bf16[32,4096]{1,0:T(8,128)(2,1)S(1)} %add_convert_fusion.2), channel_id=1, source_target_pairs={{2,0},{4,2},{6,4},{7,6},{5,7},{3,5},{1,3},{0,1},{10,8},{12,10},{14... | collective-permute-start | bytes 786440 | tf_op jit(solution)/shard_map/ppermute | solution.py:626
  219.5 1.8 collective-permute-done.22
  221.5 1.1 collective-permute-done.26
  222.6 2.5 %collective-permute-start.27 = (bf16[32,4096]{1,0:T(8,128)(2,1)S(1)}, bf16[32,4096]{1,0:T(8,128)(2,1)S(1)}, u32[]{:S(2)}, u32[]{:S(2)}) collective-permute-start(bf16[32,4096]{1,0:T(8,128)(2,1)S(1)} %add_convert_fusion.6), channel_id=1, source_target_pairs={{2,0},{4,2},{6,4},{7,6},{5,7},{3,5},{1,3},{0,1},{10,8},{12,10},{14... | collective-permute-start | bytes 786440 | tf_op jit(solution)/shard_map/ppermute | solution.py:626
  225.1 1.8 collective-permute-done.30
  227.1 1.1 collective-permute-done.34
  228.2 2.5 %collective-permute-start.35 = (bf16[32,4096]{1,0:T(8,128)(2,1)S(1)}, bf16[32,4096]{1,0:T(8,128)(2,1)S(1)}, u32[]{:S(2)}, u32[]{:S(2)}) collective-permute-start(bf16[32,4096]{1,0:T(8,128)(2,1)S(1)} %add_convert_fusion.1), channel_id=1, source_target_pairs={{2,0},{4,2},{6,4},{7,6},{5,7},{3,5},{1,3},{0,1},{10,8},{12,10},{14... | collective-permute-start | bytes 786440 | tf_op jit(solution)/shard_map/ppermute | solution.py:626
  230.8 1.8 collective-permute-done.23
  232.6 1.2 collective-permute-done.27
  233.9 3.2 %collective-permute-done.31 = bf16[32,4096]{1,0:T(8,128)(2,1)S(1)} collective-permute-done((bf16[32,4096]{1,0:T(8,128)(2,1)S(1)}, bf16[32,4096]{1,0:T(8,128)(2,1)S(1)}, u32[]{:S(2)}, u32[]{:S(2)}) %collective-permute-start.31) | collective-permute-done | bytes 262176 | tf_op jit(solution)/shard_map/ppermute | solution.py:625
  (138 shorter events, 25.9 us)
Async XLA Ops:
  2.5 8.6 %copy-start.26 = (s32[1,4]{1,0:T(1,128)S(1)}, s32[1,4]{1,0:T(1,128)}, u32[]{:S(2)}) copy-start(s32[1,4]{1,0:T(1,128)} %param.17) | copy-start | bytes 52
  2.5 23.1 %copy-start.20 = (s32[1,256]{1,0:T(1,128)S(1)}, s32[1,256]{1,0:T(1,128)}, u32[]{:S(2)}) copy-start(s32[1,256]{1,0:T(1,128)} %param.18) | copy-start | bytes 3076
  2.5 24.5 %copy-start.27 = (s32[4]{0:T(128)S(1)}, s32[4]{0:T(128)}, u32[]{:S(2)}) copy-start(s32[4]{0:T(128)} %param.16) | copy-start | bytes 52
  8.1 19.0 %collective-permute-start.4 = (bf16[4,2,256,1024]{3,2,1,0:T(8,128)(2,1)}, bf16[4,2,256,1024]{3,2,1,0:T(8,128)(2,1)}, u32[]{:S(2)}, u32[]{:S(2)}) collective-permute-start(bf16[4,2,256,1024]{3,2,1,0:T(8,128)(2,1)} %bitcast.25.refs_0_), channel_id=1, source_target_pairs={{8,0},{0,8},{9,1},{1,9},{10,2},{2,10},{11,3},{3,11},{12,4},{4,12},... | collective-permute-start | bytes 12582920 | tf_op jit(solution)/shard_map/ppermute | solution.py:513
  8.5 15.1 %collective-permute-start = (bf16[32,8192]{1,0:T(8,128)(2,1)S(1)}, bf16[32,8192]{1,0:T(8,128)(2,1)S(1)}, u32[]{:S(2)}, u32[]{:S(2)}) collective-permute-start(bf16[32,8192]{1,0:T(8,128)(2,1)S(1)} %fusion.2.refs_0_), channel_id=1, source_target_pairs={{0,2},{2,4},{4,6},{6,7},{7,5},{5,3},{3,1},{1,0},{8,10},{10,12},{12... | collective-permute-start | bytes 1572872 | tf_op jit(solution)/shard_map/ppermute | solution.py:524
  11.1 14.3 %collective-permute-start.2 = (bf16[32,8192]{1,0:T(8,128)(2,1)S(1)}, bf16[32,8192]{1,0:T(8,128)(2,1)S(1)}, u32[]{:S(2)}, u32[]{:S(2)}) collective-permute-start(bf16[32,8192]{1,0:T(8,128)(2,1)S(1)} %fusion.2.refs_0_), channel_id=1, source_target_pairs={{2,0},{4,2},{6,4},{7,6},{5,7},{3,5},{1,3},{0,1},{10,8},{12,10},{14... | collective-permute-start | bytes 1572872 | tf_op jit(solution)/shard_map/ppermute | solution.py:525
  11.9 20.0 %copy-start.21 = (s32[4]{0:T(128)}, s32[4]{0:T(128)S(1)}, u32[]{:S(2)}) copy-start(s32[4]{0:T(128)S(1)} %get-tuple-element.137) | copy-start | bytes 52
  11.9 20.0 %copy-start.23 = (s32[4]{0:T(128)}, s32[4]{0:T(128)S(1)}, u32[]{:S(2)}) copy-start(s32[4]{0:T(128)S(1)} %get-tuple-element.136) | copy-start | bytes 52
  23.6 8.3 %copy-start.14 = (bf16[32,8192]{1,0:T(8,128)(2,1)}, bf16[32,8192]{1,0:T(8,128)(2,1)S(1)}, u32[]{:S(2)}) copy-start(bf16[32,8192]{1,0:T(8,128)(2,1)S(1)} %collective-permute-done.refs_1_) | copy-start | bytes 1572868
  23.6 13.9 %collective-permute-start.1 = (bf16[32,8192]{1,0:T(8,128)(2,1)S(1)}, bf16[32,8192]{1,0:T(8,128)(2,1)}, u32[]{:S(2)}, u32[]{:S(2)}) collective-permute-start(bf16[32,8192]{1,0:T(8,128)(2,1)S(1)} %collective-permute-done.refs_1_), channel_id=1, source_target_pairs={{0,2},{2,4},{4,6},{6,7},{7,5},{5,3},{3,1},{1,0},{8,10},{10,12},{12... | collective-permute-start | bytes 1572872 | tf_op jit(solution)/shard_map/ppermute | solution.py:524
  25.4 6.5 %copy-start.16 = (bf16[32,8192]{1,0:T(8,128)(2,1)}, bf16[32,8192]{1,0:T(8,128)(2,1)S(1)}, u32[]{:S(2)}) copy-start(bf16[32,8192]{1,0:T(8,128)(2,1)S(1)} %collective-permute-done.2.refs_2_) | copy-start | bytes 1572868
  25.4 13.4 %collective-permute-start.3 = (bf16[32,8192]{1,0:T(8,128)(2,1)S(1)}, bf16[32,8192]{1,0:T(8,128)(2,1)}, u32[]{:S(2)}, u32[]{:S(2)}) collective-permute-start(bf16[32,8192]{1,0:T(8,128)(2,1)S(1)} %collective-permute-done.2.refs_2_), channel_id=1, source_target_pairs={{2,0},{4,2},{6,4},{7,6},{5,7},{3,5},{1,3},{0,1},{10,8},{12,10},{14... | collective-permute-start | bytes 1572872 | tf_op jit(solution)/shard_map/ppermute | solution.py:525
  38.8 15.1 %collective-permute-start.8 = (bf16[32,8192]{1,0:T(8,128)(2,1)}, bf16[32,8192]{1,0:T(8,128)(2,1)S(1)}, u32[]{:S(2)}, u32[]{:S(2)}) collective-permute-start(bf16[32,8192]{1,0:T(8,128)(2,1)} %collective-permute-done.1.refs_3_), channel_id=1, source_target_pairs={{0,2},{2,4},{4,6},{6,7},{7,5},{5,3},{3,1},{1,0},{8,10},{10,12},{12... | collective-permute-start | bytes 1572872 | tf_op jit(solution)/shard_map/ppermute | solution.py:524
  40.4 16.6 %collective-permute-start.9 = (bf16[32,8192]{1,0:T(8,128)(2,1)}, bf16[32,8192]{1,0:T(8,128)(2,1)S(1)}, u32[]{:S(2)}, u32[]{:S(2)}) collective-permute-start(bf16[32,8192]{1,0:T(8,128)(2,1)} %collective-permute-done.3.refs_4_), channel_id=1, source_target_pairs={{2,0},{4,2},{6,4},{7,6},{5,7},{3,5},{1,3},{0,1},{10,8},{12,10},{14... | collective-permute-start | bytes 1572872 | tf_op jit(solution)/shard_map/ppermute | solution.py:525
  42.1 56.6 %collective-permute-start.12 = (bf16[2,4,256,128]{3,2,1,0:T(8,128)(2,1)}, bf16[2,4,256,128]{3,2,1,0:T(8,128)(2,1)S(1)}, u32[]{:S(2)}, u32[]{:S(2)}) collective-permute-start(bf16[2,4,256,128]{3,2,1,0:T(8,128)(2,1)} %get-tuple-element.79), channel_id=1, source_target_pairs={{0,1},{1,0},{2,3},{3,2},{4,5},{5,4},{6,7},{7,6},{8,9},{9,8},{10,11... | collective-permute-start | bytes 1572872 | tf_op jit(solution)/shard_map/ppermute | solution.py:536
  42.5 56.2 %collective-permute-start.13 = (bf16[2,4,256,128]{3,2,1,0:T(8,128)(2,1)}, bf16[2,4,256,128]{3,2,1,0:T(8,128)(2,1)S(1)}, u32[]{:S(2)}, u32[]{:S(2)}) collective-permute-start(bf16[2,4,256,128]{3,2,1,0:T(8,128)(2,1)} %get-tuple-element.80), channel_id=1, source_target_pairs={{0,2},{1,3},{2,0},{3,1},{4,6},{5,7},{6,4},{7,5},{8,10},{9,11},{10,... | collective-permute-start | bytes 1572872 | tf_op jit(solution)/shard_map/ppermute | solution.py:536
  44.1 55.5 %collective-permute-start.14 = (bf16[2,4,256,128]{3,2,1,0:T(8,128)(2,1)}, bf16[2,4,256,128]{3,2,1,0:T(8,128)(2,1)S(1)}, u32[]{:S(2)}, u32[]{:S(2)}) collective-permute-start(bf16[2,4,256,128]{3,2,1,0:T(8,128)(2,1)} %get-tuple-element.81), channel_id=1, source_target_pairs={{0,3},{1,2},{2,1},{3,0},{4,7},{5,6},{6,5},{7,4},{8,11},{9,10},{10,... | collective-permute-start | bytes 1572872 | tf_op jit(solution)/shard_map/ppermute | solution.py:536
  54.6 0.8 copy-start.6
  55.4 24.2 %collective-permute-start.10 = (bf16[32,4096]{1,0:T(8,128)(2,1)}, bf16[32,4096]{1,0:T(8,128)(2,1)}, u32[]{:S(2)}, u32[]{:S(2)}) collective-permute-start(bf16[32,4096]{1,0:T(8,128)(2,1)} %slice.100), channel_id=1, source_target_pairs={{0,2},{2,4},{4,6},{6,7},{7,5},{5,3},{3,1},{1,0},{8,10},{10,12},{12... | collective-permute-start | bytes 786440 | tf_op jit(solution)/shard_map/ppermute | solution.py:529
  57.7 0.8 copy-start.8
  58.5 22.4 %collective-permute-start.11 = (bf16[32,4096]{1,0:T(8,128)(2,1)}, bf16[32,4096]{1,0:T(8,128)(2,1)}, u32[]{:S(2)}, u32[]{:S(2)}) collective-permute-start(bf16[32,4096]{1,0:T(8,128)(2,1)} %slice.101), channel_id=1, source_target_pairs={{2,0},{4,2},{6,4},{7,6},{5,7},{3,5},{1,3},{0,1},{10,8},{12,10},{14... | collective-permute-start | bytes 786440 | tf_op jit(solution)/shard_map/ppermute | solution.py:530
  80.9 2.2 copy-start.1
  83.1 1.0 copy-start.7
  84.1 1.0 copy-start.9
  85.2 1.0 copy-start.15
  86.2 1.0 copy-start.17
  87.3 15.6 %copy-start.22 = (s32[4]{0:T(128)S(1)}, s32[4]{0:T(128)}, u32[]{:S(2)}) copy-start(s32[4]{0:T(128)} %copy-done.21) | copy-start | bytes 52
  87.3 15.6 %copy-start.24 = (s32[4]{0:T(128)S(1)}, s32[4]{0:T(128)}, u32[]{:S(2)}) copy-start(s32[4]{0:T(128)} %copy-done.23) | copy-start | bytes 52
  87.3 15.6 %copy-start.25 = (s32[4]{0:T(128)S(1)}, s32[4]{0:T(128)}, u32[]{:S(2)}) copy-start(s32[4]{0:T(128)} %get-tuple-element.132) | copy-start | bytes 52
  98.7 0.8 copy-start.2
  99.5 0.8 copy-start.4
  100.3 17.9 %collective-permute-start.15 = (bf16[6,128,256]{2,1,0:T(8,128)(2,1)S(1)}, bf16[6,128,256]{2,1,0:T(8,128)(2,1)S(1)}, u32[]{:S(2)}, u32[]{:S(2)}) collective-permute-start(bf16[6,128,256]{2,1,0:T(8,128)(2,1)S(1)} %get-tuple-element.87.refs_6_), channel_id=1, source_target_pairs={{0,4},{1,5},{2,6},{3,7},{4,0},{5,1},{6,2},{7,3},{8,12},{9,13},{10,... | collective-permute-start | bytes 1179656 | tf_op jit(solution)/shard_map/ppermute | solution.py:548
  104.1 49.7 %collective-permute-start.5 = (bf16[2,4,256,128]{3,2,1,0:T(8,128)(2,1)}, bf16[2,4,256,128]{3,2,1,0:T(8,128)(2,1)S(1)}, u32[]{:S(2)}, u32[]{:S(2)}) collective-permute-start(bf16[2,4,256,128]{3,2,1,0:T(8,128)(2,1)} %get-tuple-element.71), channel_id=1, source_target_pairs={{0,1},{1,0},{2,3},{3,2},{4,5},{5,4},{6,7},{7,6},{8,9},{9,8},{10,11... | collective-permute-start | bytes 1572872 | tf_op jit(solution)/shard_map/ppermute | solution.py:536
  104.1 49.7 %collective-permute-start.6 = (bf16[2,4,256,128]{3,2,1,0:T(8,128)(2,1)}, bf16[2,4,256,128]{3,2,1,0:T(8,128)(2,1)S(1)}, u32[]{:S(2)}, u32[]{:S(2)}) collective-permute-start(bf16[2,4,256,128]{3,2,1,0:T(8,128)(2,1)} %get-tuple-element.72), channel_id=1, source_target_pairs={{0,2},{1,3},{2,0},{3,1},{4,6},{5,7},{6,4},{7,5},{8,10},{9,11},{10,... | collective-permute-start | bytes 1572872 | tf_op jit(solution)/shard_map/ppermute | solution.py:536
  105.2 48.6 %collective-permute-start.7 = (bf16[2,4,256,128]{3,2,1,0:T(8,128)(2,1)}, bf16[2,4,256,128]{3,2,1,0:T(8,128)(2,1)S(1)}, u32[]{:S(2)}, u32[]{:S(2)}) collective-permute-start(bf16[2,4,256,128]{3,2,1,0:T(8,128)(2,1)} %get-tuple-element.73), channel_id=1, source_target_pairs={{0,3},{1,2},{2,1},{3,0},{4,7},{5,6},{6,5},{7,4},{8,11},{9,10},{10,... | collective-permute-start | bytes 1572872 | tf_op jit(solution)/shard_map/ppermute | solution.py:536
  107.6 37.0 %collective-permute-start.17 = (bf16[4,128,256]{2,1,0:T(8,128)(2,1)}, bf16[4,128,256]{2,1,0:T(8,128)(2,1)}, u32[]{:S(2)}, u32[]{:S(2)}) collective-permute-start(bf16[4,128,256]{2,1,0:T(8,128)(2,1)} %get-tuple-element.82.refs_6_), channel_id=1, source_target_pairs={{0,4},{1,5},{2,6},{3,7},{4,0},{5,1},{6,2},{7,3},{8,12},{9,13},{10,... | collective-permute-start | bytes 786440 | tf_op jit(solution)/shard_map/ppermute | solution.py:548
  118.2 0.7 copy-start.10
  119.0 0.8 copy-start.12
  120.4 24.2 %collective-permute-start.16 = (bf16[256,256]{1,0:T(8,128)(2,1)}, bf16[256,256]{1,0:T(8,128)(2,1)S(1)}, u32[]{:S(2)}, u32[]{:S(2)}) collective-permute-start(bf16[256,256]{1,0:T(8,128)(2,1)} %pad_maximum_fusion.7), channel_id=1, source_target_pairs={{0,0},{1,2},{2,4},{3,6},{4,1},{5,3},{6,5},{7,7},{8,8},{9,10},{10,1... | collective-permute-start | bytes 393224 | tf_op jit(solution)/shard_map/ppermute | solution.py:568
  130.1 23.7 %copy-start.13 = (bf16[6,128,256]{2,1,0:T(8,128)(2,1)S(1)}, bf16[6,128,256]{2,1,0:T(8,128)(2,1)}, u32[]{:S(2)}) copy-start(bf16[6,128,256]{2,1,0:T(8,128)(2,1)} %copy-done.12) | copy-start | bytes 1179652
  131.5 1.0 copy-start.3
  132.5 1.0 copy-start.5
  133.6 1.0 copy-start.11
  134.6 0.6 copy-start.18
  135.2 0.7 copy-start.19
  150.8 22.8 %collective-permute-start.18 = (bf16[4,144,256]{2,1,0:T(8,128)(2,1)S(1)}, bf16[4,144,256]{2,1,0:T(8,128)(2,1)S(1)}, u32[]{:S(2)}, u32[]{:S(2)}) collective-permute-start(bf16[4,144,256]{2,1,0:T(8,128)(2,1)S(1)} %attend.6), channel_id=1, source_target_pairs={{0,4},{1,5},{2,6},{3,7},{4,0},{5,1},{6,2},{7,3},{8,12},{9,13},{10,... | collective-permute-start | bytes 884744 | tf_op jit(solution)/shard_map/ppermute | solution.py:605
  153.5 26.4 %collective-permute-start.19 = (bf16[4,144,256]{2,1,0:T(8,128)(2,1)S(1)}, bf16[4,144,256]{2,1,0:T(8,128)(2,1)S(1)}, u32[]{:S(2)}, u32[]{:S(2)}) collective-permute-start(bf16[4,144,256]{2,1,0:T(8,128)(2,1)S(1)} %attend.4), channel_id=1, source_target_pairs={{0,4},{1,5},{2,6},{3,7},{4,0},{5,1},{6,2},{7,3},{8,12},{9,13},{10,... | collective-permute-start | bytes 884744 | tf_op jit(solution)/shard_map/ppermute | solution.py:605
  180.3 0.8 copy-start
  187.8 12.5 %collective-permute-start.20 = (bf16[32,2048]{1,0:T(8,128)(2,1)S(1)}, bf16[32,2048]{1,0:T(8,128)(2,1)S(1)}, u32[]{:S(2)}, u32[]{:S(2)}) collective-permute-start(bf16[32,2048]{1,0:T(8,128)(2,1)S(1)} %get-tuple-element.101), channel_id=1, source_target_pairs={{0,2},{2,4},{4,6},{6,7},{7,5},{5,3},{3,1},{1,0},{8,10},{10,12},{12... | collective-permute-start | bytes 393224 | tf_op jit(solution)/shard_map/ppermute | solution.py:616
  194.8 7.2 %collective-permute-start.24 = (bf16[32,2048]{1,0:T(8,128)(2,1)S(1)}, bf16[32,2048]{1,0:T(8,128)(2,1)S(1)}, u32[]{:S(2)}, u32[]{:S(2)}) collective-permute-start(bf16[32,2048]{1,0:T(8,128)(2,1)S(1)} %get-tuple-element.105), channel_id=1, source_target_pairs={{2,0},{4,2},{6,4},{7,6},{5,7},{3,5},{1,3},{0,1},{10,8},{12,10},{14... | collective-permute-start | bytes 393224 | tf_op jit(solution)/shard_map/ppermute | solution.py:617
  198.1 6.4 %collective-permute-start.28 = (bf16[32,2048]{1,0:T(8,128)(2,1)S(1)}, bf16[32,2048]{1,0:T(8,128)(2,1)S(1)}, u32[]{:S(2)}, u32[]{:S(2)}) collective-permute-start(bf16[32,2048]{1,0:T(8,128)(2,1)S(1)} %get-tuple-element.110), channel_id=1, source_target_pairs={{0,2},{2,4},{4,6},{6,7},{7,5},{5,3},{3,1},{1,0},{8,10},{10,12},{12... | collective-permute-start | bytes 393224 | tf_op jit(solution)/shard_map/ppermute | solution.py:616
  198.2 6.5 %collective-permute-start.32 = (bf16[32,2048]{1,0:T(8,128)(2,1)S(1)}, bf16[32,2048]{1,0:T(8,128)(2,1)S(1)}, u32[]{:S(2)}, u32[]{:S(2)}) collective-permute-start(bf16[32,2048]{1,0:T(8,128)(2,1)S(1)} %get-tuple-element.114), channel_id=1, source_target_pairs={{2,0},{4,2},{6,4},{7,6},{5,7},{3,5},{1,3},{0,1},{10,8},{12,10},{14... | collective-permute-start | bytes 393224 | tf_op jit(solution)/shard_map/ppermute | solution.py:617
  200.3 9.8 %collective-permute-start.21 = (bf16[32,4096]{1,0:T(8,128)(2,1)S(1)}, bf16[32,4096]{1,0:T(8,128)(2,1)S(1)}, u32[]{:S(2)}, u32[]{:S(2)}) collective-permute-start(bf16[32,4096]{1,0:T(8,128)(2,1)S(1)} %pad_maximum_fusion.1), channel_id=1, source_target_pairs={{0,2},{2,4},{4,6},{6,7},{7,5},{5,3},{3,1},{1,0},{8,10},{10,12},{12... | collective-permute-start | bytes 786440 | tf_op jit(solution)/shard_map/ppermute | solution.py:625
  202.0 9.3 %collective-permute-start.25 = (bf16[32,4096]{1,0:T(8,128)(2,1)S(1)}, bf16[32,4096]{1,0:T(8,128)(2,1)S(1)}, u32[]{:S(2)}, u32[]{:S(2)}) collective-permute-start(bf16[32,4096]{1,0:T(8,128)(2,1)S(1)} %pad_maximum_fusion.2), channel_id=1, source_target_pairs={{2,0},{4,2},{6,4},{7,6},{5,7},{3,5},{1,3},{0,1},{10,8},{12,10},{14... | collective-permute-start | bytes 786440 | tf_op jit(solution)/shard_map/ppermute | solution.py:626
  204.6 11.1 %collective-permute-start.29 = (bf16[32,4096]{1,0:T(8,128)(2,1)S(1)}, bf16[32,4096]{1,0:T(8,128)(2,1)S(1)}, u32[]{:S(2)}, u32[]{:S(2)}) collective-permute-start(bf16[32,4096]{1,0:T(8,128)(2,1)S(1)} %pad_maximum_fusion.3), channel_id=1, source_target_pairs={{0,2},{2,4},{4,6},{6,7},{7,5},{5,3},{3,1},{1,0},{8,10},{10,12},{12... | collective-permute-start | bytes 786440 | tf_op jit(solution)/shard_map/ppermute | solution.py:625
  204.8 12.2 %collective-permute-start.33 = (bf16[32,4096]{1,0:T(8,128)(2,1)S(1)}, bf16[32,4096]{1,0:T(8,128)(2,1)S(1)}, u32[]{:S(2)}, u32[]{:S(2)}) collective-permute-start(bf16[32,4096]{1,0:T(8,128)(2,1)S(1)} %pad_maximum_fusion.4), channel_id=1, source_target_pairs={{2,0},{4,2},{6,4},{7,6},{5,7},{3,5},{1,3},{0,1},{10,8},{12,10},{14... | collective-permute-start | bytes 786440 | tf_op jit(solution)/shard_map/ppermute | solution.py:626
  210.2 11.2 %collective-permute-start.22 = (bf16[32,4096]{1,0:T(8,128)(2,1)S(1)}, bf16[32,4096]{1,0:T(8,128)(2,1)S(1)}, u32[]{:S(2)}, u32[]{:S(2)}) collective-permute-start(bf16[32,4096]{1,0:T(8,128)(2,1)S(1)} %add_convert_fusion.9), channel_id=1, source_target_pairs={{0,2},{2,4},{4,6},{6,7},{7,5},{5,3},{3,1},{1,0},{8,10},{10,12},{12... | collective-permute-start | bytes 786440 | tf_op jit(solution)/shard_map/ppermute | solution.py:625
  211.4 11.2 %collective-permute-start.26 = (bf16[32,4096]{1,0:T(8,128)(2,1)S(1)}, bf16[32,4096]{1,0:T(8,128)(2,1)S(1)}, u32[]{:S(2)}, u32[]{:S(2)}) collective-permute-start(bf16[32,4096]{1,0:T(8,128)(2,1)S(1)} %add_convert_fusion.7), channel_id=1, source_target_pairs={{2,0},{4,2},{6,4},{7,6},{5,7},{3,5},{1,3},{0,1},{10,8},{12,10},{14... | collective-permute-start | bytes 786440 | tf_op jit(solution)/shard_map/ppermute | solution.py:626
  215.8 11.2 %collective-permute-start.30 = (bf16[32,4096]{1,0:T(8,128)(2,1)S(1)}, bf16[32,4096]{1,0:T(8,128)(2,1)S(1)}, u32[]{:S(2)}, u32[]{:S(2)}) collective-permute-start(bf16[32,4096]{1,0:T(8,128)(2,1)S(1)} %add_convert_fusion.4), channel_id=1, source_target_pairs={{0,2},{2,4},{4,6},{6,7},{7,5},{5,3},{3,1},{1,0},{8,10},{10,12},{12... | collective-permute-start | bytes 786440 | tf_op jit(solution)/shard_map/ppermute | solution.py:625
  217.0 11.2 %collective-permute-start.34 = (bf16[32,4096]{1,0:T(8,128)(2,1)S(1)}, bf16[32,4096]{1,0:T(8,128)(2,1)S(1)}, u32[]{:S(2)}, u32[]{:S(2)}) collective-permute-start(bf16[32,4096]{1,0:T(8,128)(2,1)S(1)} %add_convert_fusion.2), channel_id=1, source_target_pairs={{2,0},{4,2},{6,4},{7,6},{5,7},{3,5},{1,3},{0,1},{10,8},{12,10},{14... | collective-permute-start | bytes 786440 | tf_op jit(solution)/shard_map/ppermute | solution.py:626
  221.4 11.2 %collective-permute-start.23 = (bf16[32,4096]{1,0:T(8,128)(2,1)S(1)}, bf16[32,4096]{1,0:T(8,128)(2,1)S(1)}, u32[]{:S(2)}, u32[]{:S(2)}) collective-permute-start(bf16[32,4096]{1,0:T(8,128)(2,1)S(1)} %add_convert_fusion.8), channel_id=1, source_target_pairs={{0,2},{2,4},{4,6},{6,7},{7,5},{5,3},{3,1},{1,0},{8,10},{10,12},{12... | collective-permute-start | bytes 786440 | tf_op jit(solution)/shard_map/ppermute | solution.py:625
  222.6 11.2 %collective-permute-start.27 = (bf16[32,4096]{1,0:T(8,128)(2,1)S(1)}, bf16[32,4096]{1,0:T(8,128)(2,1)S(1)}, u32[]{:S(2)}, u32[]{:S(2)}) collective-permute-start(bf16[32,4096]{1,0:T(8,128)(2,1)S(1)} %add_convert_fusion.6), channel_id=1, source_target_pairs={{2,0},{4,2},{6,4},{7,6},{5,7},{3,5},{1,3},{0,1},{10,8},{12,10},{14... | collective-permute-start | bytes 786440 | tf_op jit(solution)/shard_map/ppermute | solution.py:626
  227.0 10.1 %collective-permute-start.31 = (bf16[32,4096]{1,0:T(8,128)(2,1)S(1)}, bf16[32,4096]{1,0:T(8,128)(2,1)S(1)}, u32[]{:S(2)}, u32[]{:S(2)}) collective-permute-start(bf16[32,4096]{1,0:T(8,128)(2,1)S(1)} %add_convert_fusion.3), channel_id=1, source_target_pairs={{0,2},{2,4},{4,6},{6,7},{7,5},{5,3},{3,1},{1,0},{8,10},{10,12},{12... | collective-permute-start | bytes 786440 | tf_op jit(solution)/shard_map/ppermute | solution.py:625
  228.2 9.4 %collective-permute-start.35 = (bf16[32,4096]{1,0:T(8,128)(2,1)S(1)}, bf16[32,4096]{1,0:T(8,128)(2,1)S(1)}, u32[]{:S(2)}, u32[]{:S(2)}) collective-permute-start(bf16[32,4096]{1,0:T(8,128)(2,1)S(1)} %add_convert_fusion.1), channel_id=1, source_target_pairs={{2,0},{4,2},{6,4},{7,6},{5,7},{3,5},{1,3},{0,1},{10,8},{12,10},{14... | collective-permute-start | bytes 786440 | tf_op jit(solution)/shard_map/ppermute | solution.py:626

commit v5 on v4

v5 whole, which is shorter than its diff:
```python
import functools
import math

import jax
import jax.numpy as jnp
from jax import lax
from jax.experimental import pallas as pl
from jax.experimental.pallas import tpu as pltpu
from jax.sharding import PartitionSpec as P

HEADS = 64
KVH = 8
HD = 128
DOCS = 4
BLOCK = 128
SEL = 256


EPSILON = 1e-05
ROPE_BASE = 500000.0
MASKED = -1e30
FAR = 1 << 30
CHUNKS = 2
TILE_COLS = 256
PAIR = 2
STATS = 16
HALVES = 2
DEPTH_TILE = 1024
WIDTH_TILE = 1024
SLOTS = 3


def cost(flops, bytes_accessed, transcendentals=0):
    return pl.CostEstimate(
        flops=int(flops), bytes_accessed=int(bytes_accessed), transcendentals=int(transcendentals)
    )


def rotation_tables(positions):
    half_dim = HD // 2
    inverse = ROPE_BASE ** (-(jnp.arange(half_dim, dtype=jnp.float32) * (2.0 / HD)))
    angles = positions.astype(jnp.float32)[:, None] * inverse[None, :]
    cosine = jnp.cos(angles)
    sine_part = jnp.sin(angles)
    return (
        jnp.concatenate([cosine, cosine], axis=-1),
        jnp.concatenate([-sine_part, sine_part], axis=-1),
    )


def rotate(values, cosine, sine_part):
    swapped = jnp.concatenate([values[:, HD // 2 :], values[:, : HD // 2]], axis=-1)
    return values * cosine + swapped * sine_part


def megabytes(count):
    return pltpu.CompilerParams(vmem_limit_bytes=count * 1024 * 1024)


def stream(sources, buffers, sems):
    def copies(step):
        slot = step % SLOTS
        return [
            pltpu.make_async_copy(source(step), buffer.at[slot], sems.at[i, slot])
            for i, (source, buffer) in enumerate(zip(sources, buffers))
        ]

    def start(step):
        for copy in copies(step):
            copy.start()

    def wait(step):
        for copy in copies(step):
            copy.wait()

    return start, wait


def project_kernel(n_blocks, chunk, is_last, place_ref, *refs):
    refs = list(refs)
    take = lambda count: [refs.pop(0) for _ in range(count)]
    blocks = take(n_blocks)
    wq_ref, wkv_ref = take(2)
    if chunk:
        prev_q, prev_kv = take(2)
    if is_last:
        cos_ref, sin_ref = take(2)
        total_q, total_kv, natural, natural_kv = refs[-7:-3]
        outs = refs[:-7]
    else:
        total_q, total_kv = take(2)
    wq_slots, wkv_slots, sems = refs[-3:]
    tile = wq_slots.shape[1]
    depth = blocks[0].shape[1]
    count = depth // tile
    rows_of = lambda ref: lambda step: ref.at[pl.ds(chunk * depth + step * tile, tile), :]
    start, wait = stream([rows_of(wq_ref), rows_of(wkv_ref)], [wq_slots, wkv_slots], sems)

    for step in range(min(SLOTS, count)):
        start(step)
    for step in range(count):
        wait(step)
        slot = step % SLOTS
        cols = slice(step * tile, (step + 1) * tile)
        rows = jnp.concatenate([b[:, cols] for b in blocks], axis=0)
        part_q = jnp.dot(rows, wq_slots[slot], preferred_element_type=jnp.float32)
        part_kv = jnp.dot(rows, wkv_slots[slot], preferred_element_type=jnp.float32)
        if step:
            total_q[...] += part_q
            total_kv[...] += part_kv
        elif chunk:
            total_q[...] = prev_q[...] + part_q
            total_kv[...] = prev_kv[...] + part_kv
        else:
            total_q[...] = part_q
            total_kv[...] = part_kv
        if step + SLOTS < count:
            start(step + SLOTS)

    if is_last:
        height = SEL // place_ref.shape[0]
        for block in range(SEL // height):
            here = slice(block * height, (block + 1) * height)
            there = pl.ds(pl.multiple_of(place_ref[block] * height, height), height)
            natural[there, :] = total_q[here, :]
            natural_kv[there, :] = total_kv[here, :]
        heads_here = total_q.shape[1] // HD
        tile_q = TILE_COLS // heads_here
        per_half = SEL // tile_q // HALVES
        for index in range(SEL // tile_q):
            here = slice(index * tile_q, (index + 1) * tile_q)
            stacked = jnp.concatenate(
                [
                    rotate(
                        natural[here, head * HD : (head + 1) * HD], cos_ref[here, :], sin_ref[here, :]
                    )
                    for head in range(heads_here)
                ],
                axis=0,
            )
            outs[index // per_half][index % per_half] = stacked.T.astype(jnp.bfloat16)
        if len(outs) > HALVES:
            outs[-1][...] = natural_kv[...].astype(jnp.bfloat16)
        else:
            for index in range(SEL // HD):
                outs[-1][per_half + index] = natural_kv[
                    index * HD : (index + 1) * HD, :
                ].astype(jnp.bfloat16)


def project(place, blocks, w_query, w_keyval, prev, tables, chunk):
    depth = blocks[0].shape[1]
    q_cols, kv_cols = w_query.shape[1], w_keyval.shape[1]
    tile = min(DEPTH_TILE, depth)
    is_last = chunk + 1 == CHUNKS
    vmem = pl.BlockSpec(memory_space=pltpu.VMEM)
    hbm = pl.BlockSpec(memory_space=pltpu.HBM)
    total = [((SEL, q_cols), jnp.float32), ((SEL, kv_cols), jnp.float32)]
    scratch = []
    if is_last:
        per_half = SEL * q_cols // (HD * TILE_COLS * HALVES)
        behind = SEL // HD if kv_cols == TILE_COLS else 0
        outs = [(per_half, HD, TILE_COLS)] * (HALVES - 1) + [(per_half + behind, HD, TILE_COLS)]
        if not behind:
            outs.append((SEL, kv_cols))
        outs = [(shape, jnp.bfloat16) for shape in outs]
        scratch = total + total
    else:
        outs = total
    extra = ([] if prev is None else list(prev)) + (list(tables) if is_last else [])
    return pl.pallas_call(
        functools.partial(project_kernel, len(blocks), chunk, is_last),
        in_specs=[pl.BlockSpec(memory_space=pltpu.SMEM)]
        + [vmem] * len(blocks)
        + [hbm] * 2
        + [vmem] * len(extra),
        out_specs=[vmem] * len(outs),
        out_shape=[jax.ShapeDtypeStruct(*o) for o in outs],
        scratch_shapes=[pltpu.VMEM(*x) for x in scratch]
        + [
            pltpu.VMEM((SLOTS, tile, q_cols), jnp.bfloat16),
            pltpu.VMEM((SLOTS, tile, kv_cols), jnp.bfloat16),
            pltpu.SemaphoreType.DMA((2, SLOTS)),
        ],
        compiler_params=megabytes(16),
        cost_estimate=cost(
            2 * SEL * depth * (q_cols + kv_cols), 2 * depth * (q_cols + kv_cols + SEL)
        ),
        name="project",
    )(place, *blocks, w_query, w_keyval, *extra)


def select_kernel(n_dest, n_src, place_ref, slot_ref, head_ref, *refs):
    sources = refs[:n_src]
    outs = refs[n_src : n_src + n_dest]
    held, sems, out_sems = refs[n_src + n_dest :]
    for doc in range(DOCS):
        for src in range(n_src):

            @pl.when(place_ref[doc] == src)
            def _():
                for dest in range(n_dest):
                    cols = pl.ds(pl.multiple_of(head_ref[dest] * HD, HD), HD)
                    pltpu.make_async_copy(
                        sources[src].at[slot_ref[doc], :, :, cols],
                        held.at[dest, :, doc],
                        sems.at[dest, doc],
                    ).start()

    for dest in range(n_dest):
        for doc in range(DOCS):
            pltpu.make_async_copy(
                sources[0].at[0, :, :, 0:HD], held.at[dest, :, doc], sems.at[dest, doc]
            ).wait()
        pltpu.make_async_copy(held.at[dest], outs[dest], out_sems.at[dest]).start()
    for dest in range(n_dest):
        pltpu.make_async_copy(held.at[dest], outs[dest], out_sems.at[dest]).wait()


def select_docs(sources, place, slot, heads, n_dest):
    tokens = sources[0].shape[2]
    shape = (2, DOCS, tokens, HD)
    smem = pl.BlockSpec(memory_space=pltpu.SMEM)
    return pl.pallas_call(
        functools.partial(select_kernel, n_dest, len(sources)),
        in_specs=[smem] * 3 + [pl.BlockSpec(memory_space=pl.ANY)] * len(sources),
        out_specs=[pl.BlockSpec(memory_space=pltpu.HBM)] * n_dest,
        out_shape=[pltpu.HBM(shape, jnp.bfloat16)] * n_dest,
        scratch_shapes=[
            pltpu.VMEM((n_dest, *shape), jnp.bfloat16),
            pltpu.SemaphoreType.DMA((n_dest, DOCS)),
            pltpu.SemaphoreType.DMA((n_dest,)),
        ],
        compiler_params=megabytes(8),
        cost_estimate=cost(0, 4 * n_dest * math.prod(shape)),
        name="select_docs",
    )(place, slot, heads, *sources)


def split_exact(value):
    pieces = []
    for _ in range(3):
        pieces.append(value.astype(jnp.bfloat16).astype(jnp.float32))
        value = value - pieces[-1]
    return pieces


def attend_kernel(n_chunks, with_new, n_tiles, tile_q, first_tile, first_ref, pos_ref, *refs):
    refs = list(refs)
    take = lambda count: [refs.pop(0) for _ in range(count)]
    chunks = take(n_chunks)
    dead_ref, qpos_ref, queries = take(3)
    if with_new:
        cos_ref, sin_ref, new_ref = take(3)
    if with_new:
        top, total, summed, values, new_key, new_value = take(6)
    else:
        packed, top, total, summed, values = take(5)
    together = min(PAIR, n_tiles)
    n_pairs = n_tiles // together
    tokens = chunks[0].shape[2]
    scale = math.log2(math.e) / math.sqrt(HD)

    for chunk in range(n_chunks):
        for doc in range(DOCS):
            values[doc, :, chunk * tokens : (chunk + 1) * tokens] = chunks[chunk][1, doc].T
    if with_new:
        new_key[...] = rotate(
            new_ref[:, :HD].astype(jnp.float32), cos_ref[...], sin_ref[...]
        ).astype(jnp.bfloat16)
        new_value[...] = new_ref[:, HD:].T

    one_row = jnp.where(
        lax.broadcasted_iota(jnp.int32, (HD, TILE_COLS), 0) == 0, 1.0, 0.0
    ).astype(jnp.bfloat16)

    def update(tile, parts):
        best = functools.reduce(
            jnp.maximum, [jnp.max(scores, axis=0, keepdims=True) for scores, _ in parts]
        )
        old = top[tile]
        new = jnp.maximum(old, best)
        shrink = jnp.exp2((old - new) * scale)
        running = total[tile] * shrink
        mixed = summed[tile] * shrink
        for scores, value in parts:
            weights = jnp.exp2((scores - new) * scale)
            running += jnp.sum(weights, axis=0, keepdims=True)
            mixed += jnp.dot(
                value, weights.astype(jnp.bfloat16), preferred_element_type=jnp.float32
            )
        top[tile] = new
        total[tile] = running
        summed[tile] = mixed

    @pl.loop(0, n_pairs)
    def _(pair):
        tiles = [pair * together + i for i in range(together)]
        for tile in tiles:
            top[tile] = jnp.full(top.shape[1:], MASKED, jnp.float32)
            total[tile] = jnp.zeros(total.shape[1:], jnp.float32)
            summed[tile] = jnp.zeros(summed.shape[1:], jnp.float32)
        if with_new:
            fresh = []
            for tile in tiles:
                scores = jnp.dot(new_key[...], queries[tile], preferred_element_type=jnp.float32)
                key_index = lax.broadcasted_iota(jnp.int32, scores.shape, 0)
                q_index = (first_tile + tile) * tile_q + lax.broadcasted_iota(jnp.int32, scores.shape, 1) % tile_q
                fresh.append(jnp.where(key_index <= q_index, scores, MASKED))
            for tile, scores in zip(tiles, fresh):
                update(tile, [(scores, new_value[...])])

        @pl.loop(0, DOCS)
        def _(doc):
            firsts = [first_ref[doc * n_chunks + chunk] for chunk in range(n_chunks)]
            lowest = functools.reduce(jnp.minimum, firsts)
            reach = functools.reduce(jnp.maximum, firsts) + tokens - 1

            def visit(masked):
                found = []
                for tile in tiles:
                    extended = jnp.concatenate([queries[tile], one_row], axis=0)
                    parts = []
                    for chunk in range(n_chunks):
                        span = slice(chunk * tokens, (chunk + 1) * tokens)
                        keys = jnp.concatenate(
                            [chunks[chunk][0, doc], dead_ref[doc, span, :]], axis=1
                        )
                        scores = jnp.dot(keys, extended, preferred_element_type=jnp.float32)
                        if masked:
                            key_pos = firsts[chunk] + lax.broadcasted_iota(
                                jnp.int32, scores.shape, 0
                            )
                            scores = jnp.where(key_pos <= qpos_ref[first_tile + tile], scores, MASKED)
                        parts.append((scores, values[doc, :, span]))
                    found.append(parts)
                for tile, parts in zip(tiles, found):
                    update(tile, parts)

            start = first_tile * tile_q + pair * together * tile_q
            live = lowest <= pos_ref[start + together * tile_q - 1]
            whole = reach <= pos_ref[start]

            @pl.when(live & whole)
            def _():
                visit(False)

            @pl.when(live & jnp.logical_not(whole))
            def _():
                visit(True)

        if not with_new:
            for tile in tiles:
                extra = jnp.concatenate(
                    split_exact(top[tile])
                    + split_exact(total[tile])
                    + [jnp.zeros((STATS - 6, TILE_COLS), jnp.float32)],
                    axis=0,
                )
                packed[tile] = jnp.concatenate([summed[tile], extra], axis=0).astype(jnp.bfloat16)


def attend(chunks, dead, first_pos, selected, q_pos, queries, first_tile, n_tiles, fresh):
    n_chunks = len(chunks)
    tokens = chunks[0].shape[2]
    tile_q = SEL // q_pos.shape[0]
    smem = pl.BlockSpec(memory_space=pltpu.SMEM)
    vmem = pl.BlockSpec(memory_space=pltpu.VMEM)
    operands = [first_pos, selected, *chunks, dead, q_pos, queries, *fresh]
    state = [((n_tiles, 1, TILE_COLS), jnp.float32)] * 2
    state += [((n_tiles, HD, TILE_COLS), jnp.float32)]
    values = ((DOCS, HD, n_chunks * tokens), jnp.bfloat16)
    if fresh:
        outs = state
        scratch = [values, ((SEL, HD), jnp.bfloat16), ((HD, SEL), jnp.bfloat16)]
    else:
        outs = [((n_tiles, HD + STATS, TILE_COLS), jnp.bfloat16)]
        scratch = state + [values]
    pairs = n_tiles * TILE_COLS * DOCS * n_chunks * tokens // 2
    return pl.pallas_call(
        functools.partial(
            attend_kernel, n_chunks, bool(fresh), n_tiles, tile_q, first_tile
        ),
        in_specs=[smem] * 2 + [vmem] * (len(operands) - 2),
        out_specs=[vmem] * len(outs),
        out_shape=[jax.ShapeDtypeStruct(*s) for s in outs],
        scratch_shapes=[pltpu.VMEM(*s) for s in scratch],
        compiler_params=megabytes(16),
        cost_estimate=cost(4 * pairs * HD, 4 * DOCS * n_chunks * tokens * HD, pairs),
        name="attend",
    )(*operands)


def merge_kernel(*refs):
    out_ref = refs[-1]
    scale = math.log2(math.e) / math.sqrt(HD)
    for half in range(HALVES):
        top_a, total_a, mixed_a, packed = refs[4 * half : 4 * half + 4]
        n_tiles = top_a.shape[0]
        tile_q = SEL // HALVES // n_tiles
        for tile in range(n_tiles):
            extra = packed[tile, HD:, :].astype(jnp.float32)
            top_b = extra[0:1] + (extra[1:2] + extra[2:3])
            total_b = extra[3:4] + (extra[4:5] + extra[5:6])
            new = jnp.maximum(top_a[tile], top_b)
            part_a = jnp.exp2((top_a[tile] - new) * scale)
            part_b = jnp.exp2((top_b - new) * scale)
            total = total_a[tile] * part_a + total_b * part_b
            mixed = mixed_a[tile] * part_a + packed[tile, :HD, :].astype(jnp.float32) * part_b
            finished = (mixed / total).T.astype(jnp.bfloat16)
            here = slice((half * n_tiles + tile) * tile_q, (half * n_tiles + tile + 1) * tile_q)
            for head in range(TILE_COLS // tile_q):
                out_ref[here, head * HD : (head + 1) * HD] = finished[
                    head * tile_q : (head + 1) * tile_q, :
                ]


def merge(mine, theirs):
    n_tiles = mine[0][0].shape[0] * HALVES
    shape = (SEL, TILE_COLS * n_tiles // SEL * HD)
    operands = [a for state, packed in zip(mine, theirs) for a in (*state, packed)]
    return pl.pallas_call(
        merge_kernel,
        out_shape=jax.ShapeDtypeStruct(shape, jnp.bfloat16),
        compiler_params=megabytes(16),
        cost_estimate=cost(4 * math.prod(shape), 8 * math.prod(shape)),
        name="merge",
    )(*operands)


def out_kernel(n_blocks, first_col, place_ref, x_ref, w_ref, *refs):
    outs = refs[:n_blocks]
    ordered, slots, sems = refs[n_blocks:]
    rows = SEL // n_blocks
    tile = slots.shape[2]
    count = outs[0].shape[1] // tile
    start, wait = stream(
        [lambda step: w_ref.at[:, pl.ds(first_col + step * tile, tile)]], [slots], sems
    )

    for step in range(min(SLOTS, count)):
        start(step)
    for block in range(n_blocks):
        there = pl.ds(pl.multiple_of(place_ref[block] * rows, rows), rows)
        ordered[block * rows : (block + 1) * rows, :] = x_ref[there, :]
    for step in range(count):
        wait(step)
        product = jnp.dot(
            ordered[...].astype(jnp.bfloat16),
            slots[step % SLOTS],
            preferred_element_type=jnp.float32,
        )
        cols = slice(step * tile, (step + 1) * tile)
        for block, out in enumerate(outs):
            out[:, cols] = product[block * rows : (block + 1) * rows, :].astype(out.dtype)
        if step + SLOTS < count:
            start(step + SLOTS)


def project_out(place, attention, w_out, chunk, kinds):
    depth = w_out.shape[0]
    n_blocks = len(kinds)
    width = w_out.shape[1] // CHUNKS
    rows = SEL // n_blocks
    if rows % 16:
        attention = attention.astype(jnp.float32)
    vmem = pl.BlockSpec(memory_space=pltpu.VMEM)
    return pl.pallas_call(
        functools.partial(out_kernel, n_blocks, chunk * width),
        in_specs=[
            pl.BlockSpec(memory_space=pltpu.SMEM),
            vmem,
            pl.BlockSpec(memory_space=pltpu.HBM),
        ],
        out_specs=[vmem] * n_blocks,
        out_shape=[jax.ShapeDtypeStruct((rows, width), kind) for kind in kinds],
        scratch_shapes=[
            pltpu.VMEM((SEL, depth), attention.dtype),
            pltpu.VMEM((SLOTS, depth, min(WIDTH_TILE, width)), jnp.bfloat16),
            pltpu.SemaphoreType.DMA((1, SLOTS)),
        ],
        compiler_params=megabytes(50),
        cost_estimate=cost(2 * SEL * depth * width, 2 * depth * (width + SEL) + 4 * SEL * width),
        name="project_out",
    )(place, attention, w_out)


def per_device(
    hidden_in, norm_gain, w_query, w_keyval, w_out, pool_cache, doc_slot, doc_blocks, sel_pos
):
    tp_size = lax.axis_size("tp")
    req_size = lax.axis_size("req")
    me = lax.axis_index("tp")
    rows, width = hidden_in.shape
    slots, tokens = pool_cache.shape[:2]
    heads_here = w_query.shape[1] // HD
    selected = sel_pos[0]
    lengths = doc_blocks[0] * BLOCK

    if tp_size == KVH:
        ring = [*range(0, tp_size, 2), *range(tp_size - 1, 0, -2)]
    else:
        ring = list(range(tp_size))
    far = tp_size // 2
    forth = [(ring[p], ring[(p + 1) % tp_size]) for p in range(tp_size)]
    back = [(dst, src) for src, dst in forth]
    steps = [0] + [sign * k for k in range(1, far) for sign in (-1, 1)] + [far]
    table = [[ring[(ring.index(i) + s) % tp_size] for s in steps] for i in range(tp_size)]
    place = jnp.array(table, jnp.int32)[me]

    widened = hidden_in.astype(jnp.float32)
    normed = (
        widened
        * lax.rsqrt(jnp.mean(widened * widened, axis=-1, keepdims=True) + EPSILON)
        * norm_gain
    ).astype(jnp.bfloat16)
    middle = tp_size // 2
    order = jnp.arange(middle, dtype=jnp.int32)
    offsets = jnp.cumsum(lengths) - lengths
    first_slot = (me ^ order) * tokens
    slot_tokens = first_slot[:, None] + jnp.arange(tokens, dtype=jnp.int32)[None, :]
    cache_pos = offsets[:, None, None] + slot_tokens[None]
    is_valid = slot_tokens[None] < lengths[:, None, None]
    replaced = jnp.any(cache_pos[..., None] == selected, axis=-1)
    dead = jnp.where(is_valid & jnp.logical_not(replaced), 0.0, MASKED).astype(jnp.bfloat16)
    dead = jnp.broadcast_to(dead[..., None], (DOCS, middle, tokens, HD))
    dead = dead.reshape(DOCS, middle * tokens, HD)
    first_pos = jnp.where(
        first_slot[None] < lengths[:, None], offsets[:, None] + first_slot[None], FAR
    ).reshape(-1)
    cosine, sine_part = rotation_tables(selected)
    heads_here = w_query.shape[1] // HD
    tile_q = TILE_COLS // heads_here
    q_pos = jnp.tile(selected.reshape(SEL // tile_q, tile_q), (1, heads_here))
    q_pos = q_pos.reshape(SEL // tile_q, 1, TILE_COLS)

    part = width // CHUNKS
    streams = []
    for chunk in range(CHUNKS):
        own = normed[:, chunk * part : (chunk + 1) * part]
        streams.append({"before": [own], "behind": [own]})
    for k in range(1, far + 1):
        for chunk, held in enumerate(streams):
            if k < far or chunk % 2 == 0:
                held["before"].append(lax.ppermute(held["before"][-1], "tp", forth))
            if k < far or chunk % 2 == 1:
                held["behind"].append(lax.ppermute(held["behind"][-1], "tp", back))
        first = streams[0]["before"]
        if k == 1:
            first[-1], pool_cache = lax.optimization_barrier((first[-1], pool_cache))
            by_kind = pool_cache.transpose(0, 2, 1, 3)
            sources = [by_kind]
            for shift in range(1, req_size):
                pairs = [((i + shift) % req_size, i) for i in range(req_size)]
                sources.append(lax.ppermute(by_kind, "req", pairs))
            holder = (doc_slot // slots - lax.axis_index("req")) % req_size
            takers = jnp.concatenate([me ^ order, me ^ order ^ middle]) * KVH // tp_size
        if k == 2:
            first[-1], dead, first_pos, cosine, sine_part, q_pos, takers, holder = (
                lax.optimization_barrier(
                    (first[-1], dead, first_pos, cosine, sine_part, q_pos, takers, holder)
                )
            )
        if k == far - 1:
            sent = select_docs(sources, holder, doc_slot % slots, takers, tp_size)
            first[-1], *sent = lax.optimization_barrier((first[-1], *sent))
    projected = None
    for chunk, held in enumerate(streams):
        blocks = [held["before"][0]]
        for k in range(1, far):
            blocks += [held["before"][k], held["behind"][k]]
        blocks.append(held["behind" if chunk % 2 else "before"][far])
        if rows % 16:
            blocks = [jnp.concatenate(blocks, axis=0)]
        projected = project(
            place, blocks, w_query, w_keyval, projected, (cosine, sine_part), chunk
        )
    chunks = [
        [
            lax.ppermute(sent[slot * middle + j], "tp", [(i, i ^ j) for i in range(tp_size)])
            if j
            else sent[slot * middle]
            for j in range(middle)
        ]
        for slot in range(2)
    ]
    *queries, chunks[1] = lax.optimization_barrier((*projected[:HALVES], chunks[1]))
    n_tiles = queries[0].shape[0]
    across = [(i, i ^ middle) for i in range(tp_size)]
    their_queries = [None] * HALVES
    for part in reversed(range(HALVES)):
        their_queries[part] = lax.ppermute(queries[part], "tp", across)

    if tp_size == KVH:
        is_key = me < middle
        here = queries[-1][n_tiles:].reshape(SEL, 2 * HD)
        there = their_queries[-1][n_tiles:].reshape(SEL, 2 * HD)
        keys, vals = jnp.where(is_key, here, there), jnp.where(is_key, there, here)
        new = lax.ppermute(
            jnp.concatenate(
                [
                    jnp.where(is_key, keys[:, :HD], keys[:, HD:]),
                    jnp.where(is_key, vals[:, :HD], vals[:, HD:]),
                ],
                axis=1,
            ),
            "tp",
            [(i, 2 * i if i < middle else 2 * (i - middle) + 1) for i in range(tp_size)],
        )
    else:
        everyone = lax.all_gather(projected[-1], "tp", axis=1, tiled=True)
        my_head = me * KVH // tp_size
        new = jnp.concatenate(
            [
                lax.dynamic_slice_in_dim(everyone, (kind * KVH + my_head) * HD, HD, axis=1)
                for kind in range(2)
            ],
            axis=1,
        )

    def attend_half(part, asked, slot, extra):
        return attend(
            chunks[slot], dead, first_pos, selected, q_pos, asked[part], part * n_tiles, n_tiles, extra
        )

    theirs = [None] * HALVES
    for part in reversed(range(HALVES)):
        (packed,) = attend_half(part, their_queries, 1, [])
        if part:
            packed, new, their_queries[part - 1] = lax.optimization_barrier(
                (packed, new, their_queries[part - 1])
            )
        theirs[part] = lax.ppermute(packed, "tp", across)
    fresh = [cosine, sine_part, new]
    mine = [attend_half(part, queries, 0, fresh) for part in range(HALVES)]
    attention = merge(mine, theirs)

    finished = []
    for chunk in range(CHUNKS):
        kinds = [jnp.float32] * (tp_size - 1) + [jnp.bfloat16]
        pieces = project_out(place, attention, w_out, chunk, kinds)
        to_forth, to_back = list(pieces[2 : tp_size - 1 : 2]), list(pieces[1 : tp_size - 1 : 2])
        (to_back if chunk % 2 else to_forth).append(pieces[-1])
        total = pieces[0]
        for terms, pairs in ((to_forth, forth), (to_back, back)):
            held = None
            for term in reversed(terms):
                if held is not None:
                    term = term + held.astype(jnp.float32)
                held = lax.ppermute(term.astype(jnp.bfloat16), "tp", pairs)
            total = total + held.astype(jnp.float32)
        finished.append(total.astype(jnp.bfloat16))
    return jnp.concatenate(finished, axis=1)


def solution(mesh):
    placed = (
        P(("groups", "req", "tp"), None),
        P(),
        P(None, "tp"),
        P(None, "tp"),
        P("tp", None),
        P(("groups", "req"), "tp", None, None),
        P(("groups", "req")),
        P(("groups", "req"), None),
        P(("groups", "req"), None),
    )
    return jax.shard_map(
        per_device,
        mesh=mesh,
        in_specs=placed,
        out_specs=P(("groups", "req", "tp"), None),
        check_vma=False,
    )
```

time: 240 us -> 216 us (0.900)
  waiting for transfers between devices: 86.1 us -> 63.6 us
  starting transfers between devices: 44.8 us -> 53.7 us
  local copies, waits for them, and re-layouts: 34.7 us -> 28.7 us
  other arithmetic: 10.9 us -> 7.36 us
    ppermute x25 -> x29, waiting for transfers between devices: 66.6 us -> 43.7 us  [the longest x14 24.5 us: per_device(): held = lax.ppermute(term.astype(jnp.bfloat16), 'tp', pairs)]
    ppermute x25 -> x29, starting transfers between devices: 30.4 us -> 37.2 us  [the longest x14 17.6 us: per_device(): held = lax.ppermute(term.astype(jnp.bfloat16), 'tp', pairs)]
    unnamed x58 -> x35, local copies, waits for them, and re-layouts: 16.2 us -> 21.6 us
    slice x9 -> x1, local copies, waits for them, and re-layouts: 4.42 us -> 0.04 us  [per_device(): own = normed[:, chunk * part:(chunk + 1) * part]]
    another operation x6 -> x3, local copies, waits for them, and re-layouts: 4.31 us -> 0.17 us  [per_device(): q_pos = jnp.tile(selected.reshape(SEL // tile_q, tile_q), (1, heads_here))]
    ppermute x2, waiting for transfers between devices: 10.1 us -> 13.3 us  [per_device(): their_queries[part] = lax.ppermute(queries[part], 'tp', across)]
    ppermute x2, waiting for transfers between devices: 9.35 us -> 6.61 us  [per_device(): theirs[part] = lax.ppermute(packed, 'tp', across)]
    pallas_call x5 -> x6, Pallas kernels: 43.1 us -> 44.4 us  [the longest x4 31.8 us: attend(): pl.pallas_call(functools.partial(attend_kernel, n_chunks, bool(fresh), n_...]
  transfers between devices with their start and end apart: 36 -> 40, of which waited for: 22 -> 19; matrix products, arithmetic and copies ran while one was open for 9% -> 3% of each run, Pallas kernels for 23% -> 26%
where the time goes in v5:
time: 216 us; the launch traced here: 215 us
  waiting for transfers between devices  63.6 us (29%)
  Pallas kernels  61.1 us (28%)
  starting transfers between devices  53.7 us (25%)
  local copies, waits for them, and re-layouts  28.7 us (13%)
  other arithmetic  7.36 us (3%)
    pallas_call x4, Pallas kernels, attend(): pl.pallas_call(functools.partial(attend_kernel, n_chunks, bool(fresh), n_...  31.8 us
    ppermute x14, waiting for transfers between devices, per_device(): held = lax.ppermute(term.astype(jnp.bfloat16), 'tp', pairs)  24.5 us
    unnamed x35, local copies, waits for them, and re-layouts  21.6 us
    ppermute x14, starting transfers between devices, per_device(): held = lax.ppermute(term.astype(jnp.bfloat16), 'tp', pairs)  17.6 us
    ppermute x2, waiting for transfers between devices, per_device(): their_queries[part] = lax.ppermute(queries[part], 'tp', across)  13.3 us
    pallas_call x2, Pallas kernels, project(): pl.pallas_call(functools.partial(project_kernel, len(blocks), chunk, is_l...  12.6 us
    ppermute x7, starting transfers between devices, per_device(): held['behind'].append(lax.ppermute(held['behind'][-1], 'tp', back))  12 us
    ppermute x7, waiting for transfers between devices, per_device(): held['behind'].append(lax.ppermute(held['behind'][-1], 'tp', back))  11.8 us
  transfers between devices with their start and end apart: 40, of which 19 were waited for; matrix products, arithmetic and copies ran while one was open for 3% of the time, Pallas kernels for 26%

profile of v5, /device:TPU:0, one launch (start us, length us, event | category | flops | bytes accessed | tf_op | source)
XLA Modules:
  0.0 214.9 jit_solution(1645176315896560306)
XLA Ops:
  0.0 1.2 fusion
  1.3 1.2 fusion.2
  2.6 3.1 %collective-permute-start = (bf16[32,4096]{1,0:T(8,128)(2,1)S(1)}, bf16[32,4096]{1,0:T(8,128)(2,1)S(1)}, u32[]{:S(2)}, u32[]{:S(2)}) collective-permute-start(bf16[32,4096]{1,0:T(8,128)(2,1)S(1)} %get-tuple-element.132.refs_0_), channel_id=1, source_target_pairs={{0,2},{2,4},{4,6},{6,7},{7,5},{5,3},{3,1},{1,0},{8,10},{10,12},{12... | collective-permute-start | bytes 786440 | tf_op jit(solution)/shard_map/ppermute | solution.py:545
  5.7 6.2 %collective-permute-done.refs_1_ = bf16[32,4096]{1,0:T(8,128)(2,1)S(1)} collective-permute-done((bf16[32,4096]{1,0:T(8,128)(2,1)S(1)}, bf16[32,4096]{1,0:T(8,128)(2,1)S(1)}, u32[]{:S(2)}, u32[]{:S(2)}) %collective-permute-start) | collective-permute-done | bytes 262176 | tf_op jit(solution)/shard_map/ppermute | solution.py:545
  11.9 5.5 %copy.16 = bf16[4,256,2,1024]{3,1,2,0:T(8,128)(2,1)} copy(bf16[4,256,2,1024]{3,2,1,0:T(2,128)(2,1)} %param.15) | data formatting | bytes 8388608 | tf_op jit(solution)/shard_map/optimization_barrier | solution.py:550
  17.4 1.7 collective-permute-start.14
  19.2 1.6 collective-permute-start.8
  22.2 1.3 compare_reduce_fusion
  25.6 0.9 collective-permute-done.14.refs_2_
  26.5 1.8 collective-permute-start.15
  28.3 3.9 %collective-permute-done.8.refs_2_ = bf16[32,4096]{1,0:T(8,128)(2,1)S(1)} collective-permute-done((bf16[32,4096]{1,0:T(8,128)(2,1)S(1)}, bf16[32,4096]{1,0:T(8,128)(2,1)S(1)}, u32[]{:S(2)}, u32[]{:S(2)}) %collective-permute-start.8) | collective-permute-done | bytes 262176 | tf_op jit(solution)/shard_map/ppermute | solution.py:547
  32.1 1.8 collective-permute-start.10
  35.6 1.0 collective-permute-start.9
  36.6 1.2 collective-permute-done.15.refs_4_
  37.9 1.8 collective-permute-start.16
  39.6 3.8 %collective-permute-done.10.refs_4_ = bf16[32,4096]{1,0:T(8,128)(2,1)S(1)} collective-permute-done((bf16[32,4096]{1,0:T(8,128)(2,1)S(1)}, bf16[32,4096]{1,0:T(8,128)(2,1)S(1)}, u32[]{:S(2)}, u32[]{:S(2)}) %collective-permute-start.10) | collective-permute-done | bytes 262176 | tf_op jit(solution)/shard_map/ppermute | solution.py:547
  43.4 1.8 collective-permute-start.12
  45.1 5.0 %select_docs.1 = (bf16[2,4,256,128]{3,2,1,0:T(8,128)(2,1)}, bf16[2,4,256,128]{3,2,1,0:T(8,128)(2,1)}, bf16[2,4,256,128]{3,2,1,0:T(8,128)(2,1)}, bf16[2,4,256,128...) custom-call(s32[4]{0:T(128)S(1)} %get-tuple-element.70.place_ref, ...), custom_call_target="tpu_custom_call" | custom-call | bytes 8388608 | tf_op jit(solution)/shard_map/select_docs/pallas_call | solution.py:224
  50.5 1.8 collective-permute-start.11
  52.3 2.1 collective-permute-done.12.refs_6_
  54.4 1.7 collective-permute-start.13
  56.1 1.6 collective-permute-start.18
  57.7 1.6 collective-permute-start.19
  59.8 2.6 %collective-permute-start.20 = (bf16[2,4,256,128]{3,2,1,0:T(8,128)(2,1)}, bf16[2,4,256,128]{3,2,1,0:T(8,128)(2,1)S(1)}, u32[]{:S(2)}, u32[]{:S(2)}) collective-permute-start(bf16[2,4,256,128]{3,2,1,0:T(8,128)(2,1)} %get-tuple-element.97), channel_id=1, source_target_pairs={{0,3},{1,2},{2,1},{3,0},{4,7},{5,6},{6,5},{7,4},{8,11},{9,10},{10,... | collective-permute-start | bytes 1572872 | tf_op jit(solution)/shard_map/ppermute | solution.py:580
  63.0 5.8 %copy-done = bf16[8192,1024]{1,0:T(8,128)(2,1)S(1)} copy-done((bf16[8192,1024]{1,0:T(8,128)(2,1)S(1)}, bf16[8192,1024]{1,0:T(8,128)(2,1)}, u32[]{:S(2)}) %copy-start) | copy-done | bytes 16777240
  68.8 2.2 %copy-done.2 = bf16[8192,256]{1,0:T(8,128)(2,1)S(1)} copy-done((bf16[8192,256]{1,0:T(8,128)(2,1)S(1)}, bf16[8192,256]{1,0:T(8,128)(2,1)}, u32[]{:S(2)}) %copy-start.2) | copy-done | bytes 4194328
  71.0 5.9 %project.2 = (f32[256,1024]{1,0:T(8,128)S(1)}, f32[256,256]{1,0:T(8,128)S(1)}) custom-call(s32[8]{0:T(128)S(1)} %dynamic-slice_bitcast_fusion.place_ref, bf16[32,4096]{1,0:T(8,128)(2,1)S(1)} %get-tuple-element.132.refs_0_, bf16[32,4096]{1,0:T(8,128)(2,1)S(1)} %collective-permute-done.refs_1_, bf16[32,4096]{1,0:T(8,128)(2,1)S(1)} %collective-permute-done.14.refs_2_, ...), custom_call_target="tpu_custom_call" | custom-call | flops 2684354560 | bytes 12582912 | tf_op jit(solution)/shard_map/project/pallas_call | solution.py:171
  77.0 5.8 %copy-done.1 = bf16[8192,1024]{1,0:T(8,128)(2,1)S(1)} copy-done((bf16[8192,1024]{1,0:T(8,128)(2,1)S(1)}, bf16[8192,1024]{1,0:T(8,128)(2,1)}, u32[]{:S(2)}) %copy-start.1) | copy-done | bytes 16777240
  82.8 6.7 %project.3 = (bf16[4,128,256]{2,1,0:T(8,128)(2,1)}, bf16[6,128,256]{2,1,0:T(8,128)(2,1)S(1)}) custom-call(s32[8]{0:T(128)S(1)} %dynamic-slice_bitcast_fusion.place_ref, bf16[32,4096]{1,0:T(8,128)(2,1)S(1)} %get-tuple-element.131.refs_0_, bf16[32,4096]{1,0:T(8,128)(2,1)S(1)} %collective-permute-done.7.refs_1_, ...), custom_call_target="tpu_custom_call" | custom-call | flops 2684354560 | bytes 12582912 | tf_op jit(solution)/shard_map/project/pallas_call | solution.py:171
  89.5 0.8 copy-done.8
  91.8 1.5 collective-permute-start.21
  93.8 1.1 collective-permute-start.5
  94.9 2.0 collective-permute-start.6
  96.9 1.4 collective-permute-start.23
  98.3 10.9 %collective-permute-done.21.refs_6_ = bf16[6,128,256]{2,1,0:T(8,128)(2,1)S(1)} collective-permute-done((bf16[6,128,256]{2,1,0:T(8,128)(2,1)S(1)}, bf16[6,128,256]{2,1,0:T(8,128)(2,1)S(1)}, u32[]{:S(2)}, u32[]{:S(2)}) %collective-permute-start.21) | collective-permute-done | bytes 393248 | tf_op jit(solution)/shard_map/ppermute | solution.py:592
  110.0 1.0 copy-done.7
  111.1 1.0 copy-done.9
  112.1 1.0 copy-done.11
  113.2 1.0 copy-done.13
  114.2 10.2 %attend.4 = bf16[4,144,256]{2,1,0:T(8,128)(2,1)S(1)} custom-call(s32[16]{0:T(128)S(1)} %select_n.73.first_ref, s32[256]{0:T(256)S(1)} %bitcast.24, bf16[2,4,256,128]{3,2,1,0:T(8,128)(2,1)S(1)} %copy-done.7, bf16[2,4,256,128]{3,2,1,0:T(8,128)(2,1)S(1)} %copy-done.9, bf16[2,4,256,128]{3,2,1,0:T(8,128)(2,1)S(1)} %copy-done.11, ...), custom_call_target="tpu_custom_call" | custom-call | flops 1073741824 | bytes 2097152 | tf_op jit(solution)/shard_map/attend/pallas_call | solution.py:380
  124.5 2.4 %collective-permute-done.23.refs_6_ = bf16[4,128,256]{2,1,0:T(8,128)(2,1)S(1)} collective-permute-done((bf16[4,128,256]{2,1,0:T(8,128)(2,1)}, bf16[4,128,256]{2,1,0:T(8,128)(2,1)S(1)}, u32[]{:S(2)}, u32[]{:S(2)}) %collective-permute-start.23) | collective-permute-done | bytes 262176 | tf_op jit(solution)/shard_map/ppermute | solution.py:592
  126.9 4.6 %attend.6 = bf16[4,144,256]{2,1,0:T(8,128)(2,1)S(1)} custom-call(s32[16]{0:T(128)S(1)} %select_n.73.first_ref, s32[256]{0:T(256)S(1)} %bitcast.25, bf16[2,4,256,128]{3,2,1,0:T(8,128)(2,1)S(1)} %copy-done.7, bf16[2,4,256,128]{3,2,1,0:T(8,128)(2,1)S(1)} %copy-done.9, bf16[2,4,256,128]{3,2,1,0:T(8,128)(2,1)S(1)} %copy-done.11, ...), custom_call_target="tpu_custom_call" | custom-call | flops 1073741824 | bytes 2097152 | tf_op jit(solution)/shard_map/attend/pallas_call | solution.py:380
  131.5 3.5 %collective-permute-start.24 = (bf16[4,144,256]{2,1,0:T(8,128)(2,1)S(1)}, bf16[4,144,256]{2,1,0:T(8,128)(2,1)S(1)}, u32[]{:S(2)}, u32[]{:S(2)}) collective-permute-start(bf16[4,144,256]{2,1,0:T(8,128)(2,1)S(1)} %attend.6), channel_id=1, source_target_pairs={{0,4},{1,5},{2,6},{3,7},{4,0},{5,1},{6,2},{7,3},{8,12},{9,13},{10,... | collective-permute-start | bytes 884744 | tf_op jit(solution)/shard_map/ppermute | solution.py:633
  135.1 11.0 %attend.7 = (f32[4,1,256]{2,1,0:T(1,128)S(1)}, f32[4,1,256]{2,1,0:T(1,128)S(1)}, f32[4,128,256]{2,1,0:T(8,128)S(1)}) custom-call(s32[16]{0:T(128)S(1)} %select_n.73.first_ref, s32[256]{0:T(256)S(1)} %bitcast.26, bf16[2,4,256,128]{3,2,1,0:T(8,128)(2,1)S(1)} %copy-done.6, bf16[2,4,256,128]{3,2,1,0:T(8,128)(2,1)S(1)} %collective-permute-done.4.refs_1_, ...), custom_call_target="tpu_custom_call" | custom-call | flops 1073741824 | bytes 2097152 | tf_op jit(solution)/shard_map/attend/pallas_call | solution.py:380
  146.1 6.0 %attend.5 = (f32[4,1,256]{2,1,0:T(1,128)S(1)}, f32[4,1,256]{2,1,0:T(1,128)S(1)}, f32[4,128,256]{2,1,0:T(8,128)S(1)}) custom-call(s32[16]{0:T(128)S(1)} %select_n.73.first_ref, s32[256]{0:T(256)S(1)} %bitcast.27, bf16[2,4,256,128]{3,2,1,0:T(8,128)(2,1)S(1)} %copy-done.6, bf16[2,4,256,128]{3,2,1,0:T(8,128)(2,1)S(1)} %collective-permute-done.4.refs_1_, ...), custom_call_target="tpu_custom_call" | custom-call | flops 1073741824 | bytes 2097152 | tf_op jit(solution)/shard_map/attend/pallas_call | solution.py:380
  152.0 3.5 %collective-permute-done.24.refs_3_ = bf16[4,144,256]{2,1,0:T(8,128)(2,1)S(1)} collective-permute-done((bf16[4,144,256]{2,1,0:T(8,128)(2,1)S(1)}, bf16[4,144,256]{2,1,0:T(8,128)(2,1)S(1)}, u32[]{:S(2)}, u32[]{:S(2)}) %collective-permute-start.24) | collective-permute-done | bytes 294944 | tf_op jit(solution)/shard_map/ppermute | solution.py:633
  155.5 3.2 %collective-permute-done.25.refs_7_ = bf16[4,144,256]{2,1,0:T(8,128)(2,1)S(1)} collective-permute-done((bf16[4,144,256]{2,1,0:T(8,128)(2,1)S(1)}, bf16[4,144,256]{2,1,0:T(8,128)(2,1)S(1)}, u32[]{:S(2)}, u32[]{:S(2)}) %collective-permute-start.25) | collective-permute-done | bytes 294944 | tf_op jit(solution)/shard_map/ppermute | solution.py:633
  159.8 5.6 %project_out.2 = (f32[32,4096]{1,0:T(8,128)S(1)}, f32[32,4096]{1,0:T(8,128)S(1)}, f32[32,4096]{1,0:T(8,128)S(1)}, f32[32,4096]{1,0:T(8,128)S(1)}, f32[32,4096]{1...) custom-call(s32[8]{0:T(128)S(1)} %dynamic-slice_bitcast_fusion.place_ref, ...), custom_call_target="tpu_custom_call" | custom-call | flops 2147483648 | bytes 13107200 | tf_op jit(solution)/shard_map/project_out/pallas_call | solution.py:468
  165.8 4.8 %collective-permute-start.30 = (bf16[32,4096]{1,0:T(8,128)(2,1)S(1)}, bf16[32,4096]{1,0:T(8,128)(2,1)S(1)}, u32[]{:S(2)}, u32[]{:S(2)}) collective-permute-start(bf16[32,4096]{1,0:T(8,128)(2,1)S(1)} %convert_element_type.115), channel_id=1, source_target_pairs={{2,0},{4,2},{6,4},{7,6},{5,7},{3,5},{1,3},{0,1},{10,8},{12,10},{14... | collective-permute-start | bytes 786440 | tf_op jit(solution)/shard_map/ppermute | solution.py:650
  170.6 5.6 %project_out.3 = (f32[32,4096]{1,0:T(8,128)S(1)}, f32[32,4096]{1,0:T(8,128)S(1)}, f32[32,4096]{1,0:T(8,128)S(1)}, f32[32,4096]{1,0:T(8,128)S(1)}, f32[32,4096]{1...) custom-call(s32[8]{0:T(128)S(1)} %dynamic-slice_bitcast_fusion.place_ref, ...), custom_call_target="tpu_custom_call" | custom-call | flops 2147483648 | bytes 13107200 | tf_op jit(solution)/shard_map/project_out/pallas_call | solution.py:468
  176.4 2.1 collective-permute-start.36
  178.6 2.1 collective-permute-start.31
  180.7 4.9 %collective-permute-done.33 = bf16[32,4096]{1,0:T(8,128)(2,1)S(1)} collective-permute-done((bf16[32,4096]{1,0:T(8,128)(2,1)S(1)}, bf16[32,4096]{1,0:T(8,128)(2,1)S(1)}, u32[]{:S(2)}, u32[]{:S(2)}) %collective-permute-start.33) | collective-permute-done | bytes 262176 | tf_op jit(solution)/shard_map/ppermute | solution.py:650
  185.8 2.1 collective-permute-start.37
  187.9 3.3 %collective-permute-done.27 = bf16[32,4096]{1,0:T(8,128)(2,1)S(1)} collective-permute-done((bf16[32,4096]{1,0:T(8,128)(2,1)S(1)}, bf16[32,4096]{1,0:T(8,128)(2,1)S(1)}, u32[]{:S(2)}, u32[]{:S(2)}) %collective-permute-start.27) | collective-permute-done | bytes 262176 | tf_op jit(solution)/shard_map/ppermute | solution.py:650
  191.4 2.1 collective-permute-start.32
  193.5 3.3 %collective-permute-done.34 = bf16[32,4096]{1,0:T(8,128)(2,1)S(1)} collective-permute-done((bf16[32,4096]{1,0:T(8,128)(2,1)S(1)}, bf16[32,4096]{1,0:T(8,128)(2,1)S(1)}, u32[]{:S(2)}, u32[]{:S(2)}) %collective-permute-start.34) | collective-permute-done | bytes 262176 | tf_op jit(solution)/shard_map/ppermute | solution.py:650
  197.0 2.1 collective-permute-start.38
  199.1 3.3 %collective-permute-done.28 = bf16[32,4096]{1,0:T(8,128)(2,1)S(1)} collective-permute-done((bf16[32,4096]{1,0:T(8,128)(2,1)S(1)}, bf16[32,4096]{1,0:T(8,128)(2,1)S(1)}, u32[]{:S(2)}, u32[]{:S(2)}) %collective-permute-start.28) | collective-permute-done | bytes 262176 | tf_op jit(solution)/shard_map/ppermute | solution.py:650
  202.5 4.3 %collective-permute-done.38 = bf16[32,4096]{1,0:T(8,128)(2,1)S(1)} collective-permute-done((bf16[32,4096]{1,0:T(8,128)(2,1)S(1)}, bf16[32,4096]{1,0:T(8,128)(2,1)S(1)}, u32[]{:S(2)}, u32[]{:S(2)}) %collective-permute-start.38) | collective-permute-done | bytes 262176 | tf_op jit(solution)/shard_map/ppermute | solution.py:650
  206.9 1.8 collective-permute-start.39
  208.7 3.7 %collective-permute-done.29 = bf16[32,4096]{1,0:T(8,128)(2,1)S(1)} collective-permute-done((bf16[32,4096]{1,0:T(8,128)(2,1)S(1)}, bf16[32,4096]{1,0:T(8,128)(2,1)S(1)}, u32[]{:S(2)}, u32[]{:S(2)}) %collective-permute-start.29) | collective-permute-done | bytes 262176 | tf_op jit(solution)/shard_map/ppermute | solution.py:650
  212.5 1.5 collective-permute-done.39
  214.1 0.8 pad_maximum_fusion
  (108 shorter events, 12.5 us)
Async XLA Ops:
  2.5 18.6 %copy-start.5 = (s32[1,256]{1,0:T(1,128)S(1)}, s32[1,256]{1,0:T(1,128)}, u32[]{:S(2)}) copy-start(s32[1,256]{1,0:T(1,128)} %param.18) | copy-start | bytes 3076
  2.6 18.6 %copy-start.14 = (s32[1,4]{1,0:T(1,128)S(1)}, s32[1,4]{1,0:T(1,128)}, u32[]{:S(2)}) copy-start(s32[1,4]{1,0:T(1,128)} %param.17) | copy-start | bytes 52
  2.6 21.0 %copy-start.15 = (s32[4]{0:T(128)S(1)}, s32[4]{0:T(128)}, u32[]{:S(2)}) copy-start(s32[4]{0:T(128)} %param.16) | copy-start | bytes 52
  2.6 9.3 %collective-permute-start = (bf16[32,4096]{1,0:T(8,128)(2,1)S(1)}, bf16[32,4096]{1,0:T(8,128)(2,1)S(1)}, u32[]{:S(2)}, u32[]{:S(2)}) collective-permute-start(bf16[32,4096]{1,0:T(8,128)(2,1)S(1)} %get-tuple-element.132.refs_0_), channel_id=1, source_target_pairs={{0,2},{2,4},{4,6},{6,7},{7,5},{5,3},{3,1},{1,0},{8,10},{10,12},{12... | collective-permute-start | bytes 786440 | tf_op jit(solution)/shard_map/ppermute | solution.py:545
  17.4 27.7 %collective-permute-start.3 = (bf16[4,2,256,1024]{3,2,1,0:T(8,128)(2,1)}, bf16[4,2,256,1024]{3,2,1,0:T(8,128)(2,1)}, u32[]{:S(2)}, u32[]{:S(2)}) collective-permute-start(bf16[4,2,256,1024]{3,2,1,0:T(8,128)(2,1)} %bitcast.21.refs_0_), channel_id=1, source_target_pairs={{8,0},{0,8},{9,1},{1,9},{10,2},{2,10},{11,3},{3,11},{12,4},{4,12},... | collective-permute-start | bytes 12582920 | tf_op jit(solution)/shard_map/ppermute | solution.py:555
  17.4 9.1 %collective-permute-start.14 = (bf16[32,4096]{1,0:T(8,128)(2,1)S(1)}, bf16[32,4096]{1,0:T(8,128)(2,1)S(1)}, u32[]{:S(2)}, u32[]{:S(2)}) collective-permute-start(bf16[32,4096]{1,0:T(8,128)(2,1)S(1)} %get-tuple-element.132.refs_0_), channel_id=1, source_target_pairs={{2,0},{4,2},{6,4},{7,6},{5,7},{3,5},{1,3},{0,1},{10,8},{12,10},{14... | collective-permute-start | bytes 786440 | tf_op jit(solution)/shard_map/ppermute | solution.py:547
  19.2 13.0 %collective-permute-start.8 = (bf16[32,4096]{1,0:T(8,128)(2,1)S(1)}, bf16[32,4096]{1,0:T(8,128)(2,1)S(1)}, u32[]{:S(2)}, u32[]{:S(2)}) collective-permute-start(bf16[32,4096]{1,0:T(8,128)(2,1)S(1)} %get-tuple-element.131.refs_0_), channel_id=1, source_target_pairs={{2,0},{4,2},{6,4},{7,6},{5,7},{3,5},{1,3},{0,1},{10,8},{12,10},{14... | collective-permute-start | bytes 786440 | tf_op jit(solution)/shard_map/ppermute | solution.py:547
  20.7 14.9 %collective-permute-start.7 = (bf16[32,4096]{1,0:T(8,128)(2,1)S(1)}, bf16[32,4096]{1,0:T(8,128)(2,1)S(1)}, u32[]{:S(2)}, u32[]{:S(2)}) collective-permute-start(bf16[32,4096]{1,0:T(8,128)(2,1)S(1)} %get-tuple-element.131.refs_0_), channel_id=1, source_target_pairs={{0,2},{2,4},{4,6},{6,7},{7,5},{5,3},{3,1},{1,0},{8,10},{10,12},{12... | collective-permute-start | bytes 786440 | tf_op jit(solution)/shard_map/ppermute | solution.py:545
  23.7 10.9 %collective-permute-start.1 = (bf16[32,4096]{1,0:T(8,128)(2,1)S(1)}, bf16[32,4096]{1,0:T(8,128)(2,1)S(1)}, u32[]{:S(2)}, u32[]{:S(2)}) collective-permute-start(bf16[32,4096]{1,0:T(8,128)(2,1)S(1)} %collective-permute-done.refs_1_), channel_id=1, source_target_pairs={{0,2},{2,4},{4,6},{6,7},{7,5},{5,3},{3,1},{1,0},{8,10},{10,12},{12... | collective-permute-start | bytes 786440 | tf_op jit(solution)/shard_map/ppermute | solution.py:545
  26.5 11.3 %collective-permute-start.15 = (bf16[32,4096]{1,0:T(8,128)(2,1)S(1)}, bf16[32,4096]{1,0:T(8,128)(2,1)}, u32[]{:S(2)}, u32[]{:S(2)}) collective-permute-start(bf16[32,4096]{1,0:T(8,128)(2,1)S(1)} %collective-permute-done.14.refs_2_), channel_id=1, source_target_pairs={{2,0},{4,2},{6,4},{7,6},{5,7},{3,5},{1,3},{0,1},{10,8},{12,10},{14... | collective-permute-start | bytes 786440 | tf_op jit(solution)/shard_map/ppermute | solution.py:547
  32.1 11.2 %collective-permute-start.10 = (bf16[32,4096]{1,0:T(8,128)(2,1)S(1)}, bf16[32,4096]{1,0:T(8,128)(2,1)S(1)}, u32[]{:S(2)}, u32[]{:S(2)}) collective-permute-start(bf16[32,4096]{1,0:T(8,128)(2,1)S(1)} %collective-permute-done.8.refs_2_), channel_id=1, source_target_pairs={{2,0},{4,2},{6,4},{7,6},{5,7},{3,5},{1,3},{0,1},{10,8},{12,10},{14... | collective-permute-start | bytes 786440 | tf_op jit(solution)/shard_map/ppermute | solution.py:547
  35.1 15.0 %collective-permute-start.2 = (bf16[32,4096]{1,0:T(8,128)(2,1)S(1)}, bf16[32,4096]{1,0:T(8,128)(2,1)}, u32[]{:S(2)}, u32[]{:S(2)}) collective-permute-start(bf16[32,4096]{1,0:T(8,128)(2,1)S(1)} %collective-permute-done.1.refs_3_), channel_id=1, source_target_pairs={{0,2},{2,4},{4,6},{6,7},{7,5},{5,3},{3,1},{1,0},{8,10},{10,12},{12... | collective-permute-start | bytes 786440 | tf_op jit(solution)/shard_map/ppermute | solution.py:545
  35.6 14.8 %collective-permute-start.9 = (bf16[32,4096]{1,0:T(8,128)(2,1)S(1)}, bf16[32,4096]{1,0:T(8,128)(2,1)}, u32[]{:S(2)}, u32[]{:S(2)}) collective-permute-start(bf16[32,4096]{1,0:T(8,128)(2,1)S(1)} %collective-permute-done.7.refs_1_), channel_id=1, source_target_pairs={{0,2},{2,4},{4,6},{6,7},{7,5},{5,3},{3,1},{1,0},{8,10},{10,12},{12... | collective-permute-start | bytes 786440 | tf_op jit(solution)/shard_map/ppermute | solution.py:545
  37.9 19.8 %collective-permute-start.16 = (bf16[32,4096]{1,0:T(8,128)(2,1)}, bf16[32,4096]{1,0:T(8,128)(2,1)}, u32[]{:S(2)}, u32[]{:S(2)}) collective-permute-start(bf16[32,4096]{1,0:T(8,128)(2,1)} %collective-permute-done.15.refs_4_), channel_id=1, source_target_pairs={{2,0},{4,2},{6,4},{7,6},{5,7},{3,5},{1,3},{0,1},{10,8},{12,10},{14... | collective-permute-start | bytes 786440 | tf_op jit(solution)/shard_map/ppermute | solution.py:547
  43.4 11.0 %collective-permute-start.12 = (bf16[32,4096]{1,0:T(8,128)(2,1)S(1)}, bf16[32,4096]{1,0:T(8,128)(2,1)}, u32[]{:S(2)}, u32[]{:S(2)}) collective-permute-start(bf16[32,4096]{1,0:T(8,128)(2,1)S(1)} %collective-permute-done.10.refs_4_), channel_id=1, source_target_pairs={{2,0},{4,2},{6,4},{7,6},{5,7},{3,5},{1,3},{0,1},{10,8},{12,10},{14... | collective-permute-start | bytes 786440 | tf_op jit(solution)/shard_map/ppermute | solution.py:547
  50.1 9.6 %collective-permute-start.17 = (bf16[32,4096]{1,0:T(8,128)(2,1)}, bf16[32,4096]{1,0:T(8,128)(2,1)}, u32[]{:S(2)}, u32[]{:S(2)}) collective-permute-start(bf16[32,4096]{1,0:T(8,128)(2,1)} %collective-permute-done.2.refs_5_), channel_id=1, source_target_pairs={{0,2},{2,4},{4,6},{6,7},{7,5},{5,3},{3,1},{1,0},{8,10},{10,12},{12... | collective-permute-start | bytes 786440 | tf_op jit(solution)/shard_map/ppermute | solution.py:545
  50.5 26.5 %collective-permute-start.11 = (bf16[32,4096]{1,0:T(8,128)(2,1)}, bf16[32,4096]{1,0:T(8,128)(2,1)S(1)}, u32[]{:S(2)}, u32[]{:S(2)}) collective-permute-start(bf16[32,4096]{1,0:T(8,128)(2,1)} %collective-permute-done.9.refs_3_), channel_id=1, source_target_pairs={{0,2},{2,4},{4,6},{6,7},{7,5},{5,3},{3,1},{1,0},{8,10},{10,12},{12... | collective-permute-start | bytes 786440 | tf_op jit(solution)/shard_map/ppermute | solution.py:545
  54.4 22.6 %collective-permute-start.13 = (bf16[32,4096]{1,0:T(8,128)(2,1)}, bf16[32,4096]{1,0:T(8,128)(2,1)S(1)}, u32[]{:S(2)}, u32[]{:S(2)}) collective-permute-start(bf16[32,4096]{1,0:T(8,128)(2,1)} %collective-permute-done.12.refs_6_), channel_id=1, source_target_pairs={{2,0},{4,2},{6,4},{7,6},{5,7},{3,5},{1,3},{0,1},{10,8},{12,10},{14... | collective-permute-start | bytes 786440 | tf_op jit(solution)/shard_map/ppermute | solution.py:547
  56.1 33.4 %collective-permute-start.18 = (bf16[2,4,256,128]{3,2,1,0:T(8,128)(2,1)}, bf16[2,4,256,128]{3,2,1,0:T(8,128)(2,1)S(1)}, u32[]{:S(2)}, u32[]{:S(2)}) collective-permute-start(bf16[2,4,256,128]{3,2,1,0:T(8,128)(2,1)} %get-tuple-element.95), channel_id=1, source_target_pairs={{0,1},{1,0},{2,3},{3,2},{4,5},{5,4},{6,7},{7,6},{8,9},{9,8},{10,11... | collective-permute-start | bytes 1572872 | tf_op jit(solution)/shard_map/ppermute | solution.py:580
  57.7 32.6 %collective-permute-start.19 = (bf16[2,4,256,128]{3,2,1,0:T(8,128)(2,1)}, bf16[2,4,256,128]{3,2,1,0:T(8,128)(2,1)S(1)}, u32[]{:S(2)}, u32[]{:S(2)}) collective-permute-start(bf16[2,4,256,128]{3,2,1,0:T(8,128)(2,1)} %get-tuple-element.96), channel_id=1, source_target_pairs={{0,2},{1,3},{2,0},{3,1},{4,6},{5,7},{6,4},{7,5},{8,10},{9,11},{10,... | collective-permute-start | bytes 1572872 | tf_op jit(solution)/shard_map/ppermute | solution.py:580
  59.8 31.3 %collective-permute-start.20 = (bf16[2,4,256,128]{3,2,1,0:T(8,128)(2,1)}, bf16[2,4,256,128]{3,2,1,0:T(8,128)(2,1)S(1)}, u32[]{:S(2)}, u32[]{:S(2)}) collective-permute-start(bf16[2,4,256,128]{3,2,1,0:T(8,128)(2,1)} %get-tuple-element.97), channel_id=1, source_target_pairs={{0,3},{1,2},{2,1},{3,0},{4,7},{5,6},{6,5},{7,4},{8,11},{9,10},{10,... | collective-permute-start | bytes 1572872 | tf_op jit(solution)/shard_map/ppermute | solution.py:580
  63.0 5.8 %copy-start = (bf16[8192,1024]{1,0:T(8,128)(2,1)S(1)}, bf16[8192,1024]{1,0:T(8,128)(2,1)}, u32[]{:S(2)}) copy-start(bf16[8192,1024]{1,0:T(8,128)(2,1)} %refs_8_.3) | copy-start | bytes 50331652
  68.8 2.2 %copy-start.2 = (bf16[8192,256]{1,0:T(8,128)(2,1)S(1)}, bf16[8192,256]{1,0:T(8,128)(2,1)}, u32[]{:S(2)}) copy-start(bf16[8192,256]{1,0:T(8,128)(2,1)} %refs_9_.3) | copy-start | bytes 12582916
  71.0 6.0 %copy-start.3 = (bf16[8192,256]{1,0:T(8,128)(2,1)S(1)}, bf16[8192,256]{1,0:T(8,128)(2,1)}, u32[]{:S(2)}) copy-start(bf16[8192,256]{1,0:T(8,128)(2,1)} %refs_9_.3) | copy-start | bytes 12582916
  77.0 5.8 %copy-start.1 = (bf16[8192,1024]{1,0:T(8,128)(2,1)S(1)}, bf16[8192,1024]{1,0:T(8,128)(2,1)}, u32[]{:S(2)}) copy-start(bf16[8192,1024]{1,0:T(8,128)(2,1)} %refs_8_.3) | copy-start | bytes 50331652
  89.4 0.8 copy-start.8
  90.3 0.8 copy-start.10
  91.1 0.8 copy-start.12
  91.8 17.3 %collective-permute-start.21 = (bf16[6,128,256]{2,1,0:T(8,128)(2,1)S(1)}, bf16[6,128,256]{2,1,0:T(8,128)(2,1)S(1)}, u32[]{:S(2)}, u32[]{:S(2)}) collective-permute-start(bf16[6,128,256]{2,1,0:T(8,128)(2,1)S(1)} %get-tuple-element.103.refs_6_), channel_id=1, source_target_pairs={{0,4},{1,5},{2,6},{3,7},{4,0},{5,1},{6,2},{7,3},{8,12},{9,13},{10,... | collective-permute-start | bytes 1179656 | tf_op jit(solution)/shard_map/ppermute | solution.py:592
  93.4 41.7 %collective-permute-start.4 = (bf16[2,4,256,128]{3,2,1,0:T(8,128)(2,1)}, bf16[2,4,256,128]{3,2,1,0:T(8,128)(2,1)S(1)}, u32[]{:S(2)}, u32[]{:S(2)}) collective-permute-start(bf16[2,4,256,128]{3,2,1,0:T(8,128)(2,1)} %get-tuple-element.82), channel_id=1, source_target_pairs={{0,1},{1,0},{2,3},{3,2},{4,5},{5,4},{6,7},{7,6},{8,9},{9,8},{10,11... | collective-permute-start | bytes 1572872 | tf_op jit(solution)/shard_map/ppermute | solution.py:580
  93.8 41.2 %collective-permute-start.5 = (bf16[2,4,256,128]{3,2,1,0:T(8,128)(2,1)}, bf16[2,4,256,128]{3,2,1,0:T(8,128)(2,1)S(1)}, u32[]{:S(2)}, u32[]{:S(2)}) collective-permute-start(bf16[2,4,256,128]{3,2,1,0:T(8,128)(2,1)} %get-tuple-element.83), channel_id=1, source_target_pairs={{0,2},{1,3},{2,0},{3,1},{4,6},{5,7},{6,4},{7,5},{8,10},{9,11},{10,... | collective-permute-start | bytes 1572872 | tf_op jit(solution)/shard_map/ppermute | solution.py:580
  94.9 40.1 %collective-permute-start.6 = (bf16[2,4,256,128]{3,2,1,0:T(8,128)(2,1)}, bf16[2,4,256,128]{3,2,1,0:T(8,128)(2,1)S(1)}, u32[]{:S(2)}, u32[]{:S(2)}) collective-permute-start(bf16[2,4,256,128]{3,2,1,0:T(8,128)(2,1)} %get-tuple-element.84), channel_id=1, source_target_pairs={{0,3},{1,2},{2,1},{3,0},{4,7},{5,6},{6,5},{7,4},{8,11},{9,10},{10,... | collective-permute-start | bytes 1572872 | tf_op jit(solution)/shard_map/ppermute | solution.py:580
  96.9 30.0 %collective-permute-start.23 = (bf16[4,128,256]{2,1,0:T(8,128)(2,1)}, bf16[4,128,256]{2,1,0:T(8,128)(2,1)S(1)}, u32[]{:S(2)}, u32[]{:S(2)}) collective-permute-start(bf16[4,128,256]{2,1,0:T(8,128)(2,1)} %get-tuple-element.98.refs_6_), channel_id=1, source_target_pairs={{0,4},{1,5},{2,6},{3,7},{4,0},{5,1},{6,2},{7,3},{8,12},{9,13},{10,... | collective-permute-start | bytes 786440 | tf_op jit(solution)/shard_map/ppermute | solution.py:592
  109.2 25.9 %copy-start.6 = (bf16[2,4,256,128]{3,2,1,0:T(8,128)(2,1)S(1)}, bf16[2,4,256,128]{3,2,1,0:T(8,128)(2,1)}, u32[]{:S(2)}) copy-start(bf16[2,4,256,128]{3,2,1,0:T(8,128)(2,1)} %get-tuple-element.81.refs_0_) | copy-start | bytes 1572868
  109.2 17.6 %collective-permute-start.22 = (bf16[256,256]{1,0:T(8,128)(2,1)S(1)}, bf16[256,256]{1,0:T(8,128)(2,1)S(1)}, u32[]{:S(2)}, u32[]{:S(2)}) collective-permute-start(bf16[256,256]{1,0:T(8,128)(2,1)S(1)} %pad_maximum_fusion.3), channel_id=1, source_target_pairs={{0,0},{1,2},{2,4},{3,6},{4,1},{5,3},{6,5},{7,7},{8,8},{9,10},{10,1... | collective-permute-start | bytes 393224 | tf_op jit(solution)/shard_map/ppermute | solution.py:599
  110.0 1.0 copy-start.7
  111.1 1.0 copy-start.9
  112.1 1.0 copy-start.11
  113.2 1.0 copy-start.13
  131.5 24.0 %collective-permute-start.24 = (bf16[4,144,256]{2,1,0:T(8,128)(2,1)S(1)}, bf16[4,144,256]{2,1,0:T(8,128)(2,1)S(1)}, u32[]{:S(2)}, u32[]{:S(2)}) collective-permute-start(bf16[4,144,256]{2,1,0:T(8,128)(2,1)S(1)} %attend.6), channel_id=1, source_target_pairs={{0,4},{1,5},{2,6},{3,7},{4,0},{5,1},{6,2},{7,3},{8,12},{9,13},{10,... | collective-permute-start | bytes 884744 | tf_op jit(solution)/shard_map/ppermute | solution.py:633
  134.9 23.7 %collective-permute-start.25 = (bf16[4,144,256]{2,1,0:T(8,128)(2,1)S(1)}, bf16[4,144,256]{2,1,0:T(8,128)(2,1)S(1)}, u32[]{:S(2)}, u32[]{:S(2)}) collective-permute-start(bf16[4,144,256]{2,1,0:T(8,128)(2,1)S(1)} %attend.4), channel_id=1, source_target_pairs={{0,4},{1,5},{2,6},{3,7},{4,0},{5,1},{6,2},{7,3},{8,12},{9,13},{10,... | collective-permute-start | bytes 884744 | tf_op jit(solution)/shard_map/ppermute | solution.py:633
  159.0 0.8 copy-start.4
  165.5 13.0 %collective-permute-start.26 = (bf16[32,4096]{1,0:T(8,128)(2,1)S(1)}, bf16[32,4096]{1,0:T(8,128)(2,1)S(1)}, u32[]{:S(2)}, u32[]{:S(2)}) collective-permute-start(bf16[32,4096]{1,0:T(8,128)(2,1)S(1)} %get-tuple-element.117), channel_id=1, source_target_pairs={{0,2},{2,4},{4,6},{6,7},{7,5},{5,3},{3,1},{1,0},{8,10},{10,12},{12... | collective-permute-start | bytes 786440 | tf_op jit(solution)/shard_map/ppermute | solution.py:650
  165.8 12.7 %collective-permute-start.30 = (bf16[32,4096]{1,0:T(8,128)(2,1)S(1)}, bf16[32,4096]{1,0:T(8,128)(2,1)S(1)}, u32[]{:S(2)}, u32[]{:S(2)}) collective-permute-start(bf16[32,4096]{1,0:T(8,128)(2,1)S(1)} %convert_element_type.115), channel_id=1, source_target_pairs={{2,0},{4,2},{6,4},{7,6},{5,7},{3,5},{1,3},{0,1},{10,8},{12,10},{14... | collective-permute-start | bytes 786440 | tf_op jit(solution)/shard_map/ppermute | solution.py:650
  176.3 9.3 %collective-permute-start.33 = (bf16[32,4096]{1,0:T(8,128)(2,1)S(1)}, bf16[32,4096]{1,0:T(8,128)(2,1)S(1)}, u32[]{:S(2)}, u32[]{:S(2)}) collective-permute-start(bf16[32,4096]{1,0:T(8,128)(2,1)S(1)} %convert_element_type.122), channel_id=1, source_target_pairs={{0,2},{2,4},{4,6},{6,7},{7,5},{5,3},{3,1},{1,0},{8,10},{10,12},{12... | collective-permute-start | bytes 786440 | tf_op jit(solution)/shard_map/ppermute | solution.py:650
  176.4 9.3 %collective-permute-start.36 = (bf16[32,4096]{1,0:T(8,128)(2,1)S(1)}, bf16[32,4096]{1,0:T(8,128)(2,1)S(1)}, u32[]{:S(2)}, u32[]{:S(2)}) collective-permute-start(bf16[32,4096]{1,0:T(8,128)(2,1)S(1)} %get-tuple-element.128), channel_id=1, source_target_pairs={{2,0},{4,2},{6,4},{7,6},{5,7},{3,5},{1,3},{0,1},{10,8},{12,10},{14... | collective-permute-start | bytes 786440 | tf_op jit(solution)/shard_map/ppermute | solution.py:650
  178.5 12.7 %collective-permute-start.27 = (bf16[32,4096]{1,0:T(8,128)(2,1)S(1)}, bf16[32,4096]{1,0:T(8,128)(2,1)S(1)}, u32[]{:S(2)}, u32[]{:S(2)}) collective-permute-start(bf16[32,4096]{1,0:T(8,128)(2,1)S(1)} %add_convert_fusion.11), channel_id=1, source_target_pairs={{0,2},{2,4},{4,6},{6,7},{7,5},{5,3},{3,1},{1,0},{8,10},{10,12},{12... | collective-permute-start | bytes 786440 | tf_op jit(solution)/shard_map/ppermute | solution.py:650
  178.6 12.7 %collective-permute-start.31 = (bf16[32,4096]{1,0:T(8,128)(2,1)S(1)}, bf16[32,4096]{1,0:T(8,128)(2,1)S(1)}, u32[]{:S(2)}, u32[]{:S(2)}) collective-permute-start(bf16[32,4096]{1,0:T(8,128)(2,1)S(1)} %add_convert_fusion.8), channel_id=1, source_target_pairs={{2,0},{4,2},{6,4},{7,6},{5,7},{3,5},{1,3},{0,1},{10,8},{12,10},{14... | collective-permute-start | bytes 786440 | tf_op jit(solution)/shard_map/ppermute | solution.py:650
  185.6 11.2 %collective-permute-start.34 = (bf16[32,4096]{1,0:T(8,128)(2,1)S(1)}, bf16[32,4096]{1,0:T(8,128)(2,1)S(1)}, u32[]{:S(2)}, u32[]{:S(2)}) collective-permute-start(bf16[32,4096]{1,0:T(8,128)(2,1)S(1)} %add_convert_fusion.5), channel_id=1, source_target_pairs={{0,2},{2,4},{4,6},{6,7},{7,5},{5,3},{3,1},{1,0},{8,10},{10,12},{12... | collective-permute-start | bytes 786440 | tf_op jit(solution)/shard_map/ppermute | solution.py:650
  185.8 11.2 %collective-permute-start.37 = (bf16[32,4096]{1,0:T(8,128)(2,1)S(1)}, bf16[32,4096]{1,0:T(8,128)(2,1)S(1)}, u32[]{:S(2)}, u32[]{:S(2)}) collective-permute-start(bf16[32,4096]{1,0:T(8,128)(2,1)S(1)} %add_convert_fusion.3), channel_id=1, source_target_pairs={{2,0},{4,2},{6,4},{7,6},{5,7},{3,5},{1,3},{0,1},{10,8},{12,10},{14... | collective-permute-start | bytes 786440 | tf_op jit(solution)/shard_map/ppermute | solution.py:650
  191.2 11.2 %collective-permute-start.28 = (bf16[32,4096]{1,0:T(8,128)(2,1)S(1)}, bf16[32,4096]{1,0:T(8,128)(2,1)S(1)}, u32[]{:S(2)}, u32[]{:S(2)}) collective-permute-start(bf16[32,4096]{1,0:T(8,128)(2,1)S(1)} %add_convert_fusion.10), channel_id=1, source_target_pairs={{0,2},{2,4},{4,6},{6,7},{7,5},{5,3},{3,1},{1,0},{8,10},{10,12},{12... | collective-permute-start | bytes 786440 | tf_op jit(solution)/shard_map/ppermute | solution.py:650
  191.4 17.3 %collective-permute-start.32 = (bf16[32,4096]{1,0:T(8,128)(2,1)S(1)}, bf16[32,4096]{1,0:T(8,128)(2,1)S(1)}, u32[]{:S(2)}, u32[]{:S(2)}) collective-permute-start(bf16[32,4096]{1,0:T(8,128)(2,1)S(1)} %add_convert_fusion.7), channel_id=1, source_target_pairs={{2,0},{4,2},{6,4},{7,6},{5,7},{3,5},{1,3},{0,1},{10,8},{12,10},{14... | collective-permute-start | bytes 786440 | tf_op jit(solution)/shard_map/ppermute | solution.py:650
  196.9 15.6 %collective-permute-start.35 = (bf16[32,4096]{1,0:T(8,128)(2,1)S(1)}, bf16[32,4096]{1,0:T(8,128)(2,1)S(1)}, u32[]{:S(2)}, u32[]{:S(2)}) collective-permute-start(bf16[32,4096]{1,0:T(8,128)(2,1)S(1)} %add_convert_fusion.4), channel_id=1, source_target_pairs={{0,2},{2,4},{4,6},{6,7},{7,5},{5,3},{3,1},{1,0},{8,10},{10,12},{12... | collective-permute-start | bytes 786440 | tf_op jit(solution)/shard_map/ppermute | solution.py:650
  197.0 9.9 %collective-permute-start.38 = (bf16[32,4096]{1,0:T(8,128)(2,1)S(1)}, bf16[32,4096]{1,0:T(8,128)(2,1)S(1)}, u32[]{:S(2)}, u32[]{:S(2)}) collective-permute-start(bf16[32,4096]{1,0:T(8,128)(2,1)S(1)} %add_convert_fusion.2), channel_id=1, source_target_pairs={{2,0},{4,2},{6,4},{7,6},{5,7},{3,5},{1,3},{0,1},{10,8},{12,10},{14... | collective-permute-start | bytes 786440 | tf_op jit(solution)/shard_map/ppermute | solution.py:650
  202.5 9.9 %collective-permute-start.29 = (bf16[32,4096]{1,0:T(8,128)(2,1)S(1)}, bf16[32,4096]{1,0:T(8,128)(2,1)S(1)}, u32[]{:S(2)}, u32[]{:S(2)}) collective-permute-start(bf16[32,4096]{1,0:T(8,128)(2,1)S(1)} %add_convert_fusion.9), channel_id=1, source_target_pairs={{0,2},{2,4},{4,6},{6,7},{7,5},{5,3},{3,1},{1,0},{8,10},{10,12},{12... | collective-permute-start | bytes 786440 | tf_op jit(solution)/shard_map/ppermute | solution.py:650
  206.9 7.1 %collective-permute-start.39 = (bf16[32,4096]{1,0:T(8,128)(2,1)S(1)}, bf16[32,4096]{1,0:T(8,128)(2,1)S(1)}, u32[]{:S(2)}, u32[]{:S(2)}) collective-permute-start(bf16[32,4096]{1,0:T(8,128)(2,1)S(1)} %add_convert_fusion.1), channel_id=1, source_target_pairs={{2,0},{4,2},{6,4},{7,6},{5,7},{3,5},{1,3},{0,1},{10,8},{12,10},{14... | collective-permute-start | bytes 786440 | tf_op jit(solution)/shard_map/ppermute | solution.py:650

commit v6 on v5

--- a/solution.py
+++ b/solution.py
@@ -193,7 +193,7 @@
 def select_kernel(n_dest, n_src, place_ref, slot_ref, head_ref, *refs):
     sources = refs[:n_src]
     outs = refs[n_src : n_src + n_dest]
-    held, sems, out_sems = refs[n_src + n_dest :]
+    sems = refs[n_src + n_dest]
     for doc in range(DOCS):
         for src in range(n_src):
 
@@ -203,18 +203,15 @@
                     cols = pl.ds(pl.multiple_of(head_ref[dest] * HD, HD), HD)
                     pltpu.make_async_copy(
                         sources[src].at[slot_ref[doc], :, :, cols],
-                        held.at[dest, :, doc],
+                        outs[dest].at[:, doc],
                         sems.at[dest, doc],
                     ).start()
 
     for dest in range(n_dest):
         for doc in range(DOCS):
             pltpu.make_async_copy(
-                sources[0].at[0, :, :, 0:HD], held.at[dest, :, doc], sems.at[dest, doc]
+                sources[0].at[0, :, :, 0:HD], outs[dest].at[:, doc], sems.at[dest, doc]
             ).wait()
-        pltpu.make_async_copy(held.at[dest], outs[dest], out_sems.at[dest]).start()
-    for dest in range(n_dest):
-        pltpu.make_async_copy(held.at[dest], outs[dest], out_sems.at[dest]).wait()
 
 
 def select_docs(sources, place, slot, heads, n_dest):
@@ -224,13 +221,9 @@
     return pl.pallas_call(
         functools.partial(select_kernel, n_dest, len(sources)),
         in_specs=[smem] * 3 + [pl.BlockSpec(memory_space=pl.ANY)] * len(sources),
-        out_specs=[pl.BlockSpec(memory_space=pltpu.HBM)] * n_dest,
-        out_shape=[pltpu.HBM(shape, jnp.bfloat16)] * n_dest,
-        scratch_shapes=[
-            pltpu.VMEM((n_dest, *shape), jnp.bfloat16),
-            pltpu.SemaphoreType.DMA((n_dest, DOCS)),
-            pltpu.SemaphoreType.DMA((n_dest,)),
-        ],
+        out_specs=[pl.BlockSpec(memory_space=pltpu.VMEM)] * n_dest,
+        out_shape=[jax.ShapeDtypeStruct(shape, jnp.bfloat16)] * n_dest,
+        scratch_shapes=[pltpu.SemaphoreType.DMA((n_dest, DOCS))],
         compiler_params=megabytes(8),
         cost_estimate=cost(0, 4 * n_dest * math.prod(shape)),
         name="select_docs",
@@ -479,7 +472,7 @@
             pltpu.VMEM((SLOTS, depth, min(WIDTH_TILE, width)), jnp.bfloat16),
             pltpu.SemaphoreType.DMA((1, SLOTS)),
         ],
-        compiler_params=megabytes(50),
+        compiler_params=megabytes(16),
         cost_estimate=cost(2 * SEL * depth * width, 2 * depth * (width + SEL) + 4 * SEL * width),
         name="project_out",
     )(place, attention, w_out)
@@ -514,6 +507,10 @@
         * lax.rsqrt(jnp.mean(widened * widened, axis=-1, keepdims=True) + EPSILON)
         * norm_gain
     ).astype(jnp.bfloat16)
+    normed, pool_cache = lax.optimization_barrier((normed, pool_cache))
+    w_query, w_keyval, w_out = (
+        pltpu.with_memory_space_constraint(w, pltpu.HBM) for w in (w_query, w_keyval, w_out)
+    )
     middle = tp_size // 2
     order = jnp.arange(middle, dtype=jnp.int32)
     offsets = jnp.cumsum(lengths) - lengths
@@ -547,7 +544,6 @@
                 held["behind"].append(lax.ppermute(held["behind"][-1], "tp", back))
         first = streams[0]["before"]
         if k == 1:
-            first[-1], pool_cache = lax.optimization_barrier((first[-1], pool_cache))
             by_kind = pool_cache.transpose(0, 2, 1, 3)
             sources = [by_kind]
             for shift in range(1, req_size):

time: 216 us -> 205 us (0.949)
  waiting for transfers between devices: 63.6 us -> 57.4 us
  local copies, waits for them, and re-layouts: 28.7 us -> 24.4 us
  Pallas kernels: 61.1 us -> 63.8 us
    ppermute x6, waiting for transfers between devices: 0.02 us -> 16.3 us  [per_device(): lax.ppermute(sent[slot * middle + j], 'tp', [(i, i ^ j) for i in range(tp...]
    ppermute x7, starting transfers between devices: 12 us -> 2.95 us  [per_device(): held['behind'].append(lax.ppermute(held['behind'][-1], 'tp', back))]
    ppermute x14, waiting for transfers between devices: 24.5 us -> 16.6 us  [per_device(): held = lax.ppermute(term.astype(jnp.bfloat16), 'tp', pairs)]
    ppermute x2, waiting for transfers between devices: 6.61 us -> 0.01 us  [per_device(): theirs[part] = lax.ppermute(packed, 'tp', across)]
    ppermute x2, waiting for transfers between devices: 13.3 us -> 7.64 us  [per_device(): their_queries[part] = lax.ppermute(queries[part], 'tp', across)]
    ppermute x7, waiting for transfers between devices: 11.8 us -> 7.31 us  [per_device(): held['behind'].append(lax.ppermute(held['behind'][-1], 'tp', back))]
    ppermute x14, starting transfers between devices: 17.6 us -> 22.1 us  [per_device(): held = lax.ppermute(term.astype(jnp.bfloat16), 'tp', pairs)]
    pallas_call x4, Pallas kernels: 31.8 us -> 36.1 us  [attend(): pl.pallas_call(functools.partial(attend_kernel, n_chunks, bool(fresh), n_...]
  transfers between devices with their start and end apart: 40 -> 40, of which waited for: 19 -> 15; matrix products, arithmetic and copies ran while one was open for 3% -> 3% of each run, Pallas kernels for 26% -> 28%
where the time goes in v6:
time: 205 us; the launch traced here: 206 us
  Pallas kernels  63.8 us (31%)
  waiting for transfers between devices  57.4 us (28%)
  starting transfers between devices  52.4 us (26%)
  local copies, waits for them, and re-layouts  24.4 us (12%)
  other arithmetic  7.37 us (4%)
    pallas_call x4, Pallas kernels, attend(): pl.pallas_call(functools.partial(attend_kernel, n_chunks, bool(fresh), n_...  36.1 us
    ppermute x14, starting transfers between devices, per_device(): held = lax.ppermute(term.astype(jnp.bfloat16), 'tp', pairs)  22.1 us
    unnamed x53, local copies, waits for them, and re-layouts  17.3 us
    ppermute x14, waiting for transfers between devices, per_device(): held = lax.ppermute(term.astype(jnp.bfloat16), 'tp', pairs)  16.6 us
    ppermute x6, waiting for transfers between devices, per_device(): lax.ppermute(sent[slot * middle + j], 'tp', [(i, i ^ j) for i in range(tp...  16.3 us
    pallas_call x2, Pallas kernels, project(): pl.pallas_call(functools.partial(project_kernel, len(blocks), chunk, is_l...  13.8 us
    ppermute x7, starting transfers between devices, per_device(): held['before'].append(lax.ppermute(held['before'][-1], 'tp', forth))  11.7 us
    pallas_call x2, Pallas kernels, project_out(): pl.pallas_call(functools.partial(out_kernel, n_blocks, chunk * width), in...  10.3 us
  transfers between devices with their start and end apart: 40, of which 15 were waited for; matrix products, arithmetic and copies ran while one was open for 3% of the time, Pallas kernels for 28%

profile of v6, /device:TPU:0, one launch (start us, length us, event | category | flops | bytes accessed | tf_op | source)
XLA Modules:
  0.0 205.9 jit_solution(5778307147486656149)
XLA Ops:
  0.0 1.2 fusion
  1.3 1.2 fusion.2
  2.5 5.5 %copy.16 = bf16[4,256,2,1024]{3,1,2,0:T(8,128)(2,1)} copy(bf16[4,256,2,1024]{3,2,1,0:T(2,128)(2,1)} %param.15) | data formatting | bytes 8388608 | tf_op jit(solution)/shard_map/optimization_barrier | solution.py:510
  8.5 2.6 %collective-permute-start = (bf16[32,4096]{1,0:T(8,128)(2,1)S(1)}, bf16[32,4096]{1,0:T(8,128)(2,1)S(1)}, u32[]{:S(2)}, u32[]{:S(2)}) collective-permute-start(bf16[32,4096]{1,0:T(8,128)(2,1)S(1)} %get-tuple-element.132.refs_0_), channel_id=1, source_target_pairs={{0,2},{2,4},{4,6},{6,7},{7,5},{5,3},{3,1},{1,0},{8,10},{10,12},{12... | collective-permute-start | bytes 786440 | tf_op jit(solution)/shard_map/ppermute | solution.py:542
  11.2 2.0 collective-permute-start.8
  14.3 1.3 compare_reduce_fusion
  15.7 2.6 %collective-permute-done.refs_1_ = bf16[32,4096]{1,0:T(8,128)(2,1)S(1)} collective-permute-done((bf16[32,4096]{1,0:T(8,128)(2,1)S(1)}, bf16[32,4096]{1,0:T(8,128)(2,1)S(1)}, u32[]{:S(2)}, u32[]{:S(2)}) %collective-permute-start) | collective-permute-done | bytes 262176 | tf_op jit(solution)/shard_map/ppermute | solution.py:542
  18.3 2.0 collective-permute-start.1
  22.0 4.0 %collective-permute-done.8.refs_2_ = bf16[32,4096]{1,0:T(8,128)(2,1)S(1)} collective-permute-done((bf16[32,4096]{1,0:T(8,128)(2,1)S(1)}, bf16[32,4096]{1,0:T(8,128)(2,1)S(1)}, u32[]{:S(2)}, u32[]{:S(2)}) %collective-permute-start.8) | collective-permute-done | bytes 262176 | tf_op jit(solution)/shard_map/ppermute | solution.py:544
  25.9 3.4 %collective-permute-done.1.refs_3_ = bf16[32,4096]{1,0:T(8,128)(2,1)S(1)} collective-permute-done((bf16[32,4096]{1,0:T(8,128)(2,1)S(1)}, bf16[32,4096]{1,0:T(8,128)(2,1)S(1)}, u32[]{:S(2)}, u32[]{:S(2)}) %collective-permute-start.1) | collective-permute-done | bytes 262176 | tf_op jit(solution)/shard_map/ppermute | solution.py:542
  29.9 1.8 collective-permute-start.2
  31.8 1.6 collective-permute-start.9
  33.8 3.3 %collective-permute-done.10.refs_4_ = bf16[32,4096]{1,0:T(8,128)(2,1)S(1)} collective-permute-done((bf16[32,4096]{1,0:T(8,128)(2,1)S(1)}, bf16[32,4096]{1,0:T(8,128)(2,1)S(1)}, u32[]{:S(2)}, u32[]{:S(2)}) %collective-permute-start.10) | collective-permute-done | bytes 262176 | tf_op jit(solution)/shard_map/ppermute | solution.py:544
  37.2 3.3 %select_docs.1 = (bf16[2,4,256,128]{3,2,1,0:T(8,128)(2,1)S(1)}, bf16[2,4,256,128]{3,2,1,0:T(8,128)(2,1)S(1)}, bf16[2,4,256,128]{3,2,1,0:T(8,128)(2,1)S(1)}, bf16...) custom-call(s32[4]{0:T(128)S(1)} %get-tuple-element.70.place_ref, ...), custom_call_target="tpu_custom_call" | custom-call | bytes 8388608 | tf_op jit(solution)/shard_map/select_docs/pallas_call | solution.py:221
  41.2 0.8 copy-done.3
  46.0 0.8 copy-done.20
  46.8 2.0 collective-permute-start.17
  48.8 1.6 collective-permute-start.11
  51.1 1.8 collective-permute-start.19
  52.9 3.5 %collective-permute-done.17.refs_7_ = bf16[32,4096]{1,0:T(8,128)(2,1)} collective-permute-done((bf16[32,4096]{1,0:T(8,128)(2,1)}, bf16[32,4096]{1,0:T(8,128)(2,1)}, u32[]{:S(2)}, u32[]{:S(2)}) %collective-permute-start.17) | collective-permute-done | bytes 262176 | tf_op jit(solution)/shard_map/ppermute | solution.py:542
  56.4 3.0 %collective-permute-start.20 = (bf16[2,4,256,128]{3,2,1,0:T(8,128)(2,1)}, bf16[2,4,256,128]{3,2,1,0:T(8,128)(2,1)S(1)}, u32[]{:S(2)}, u32[]{:S(2)}) collective-permute-start(bf16[2,4,256,128]{3,2,1,0:T(8,128)(2,1)} %copy-done.18), channel_id=1, source_target_pairs={{0,3},{1,2},{2,1},{3,0},{4,7},{5,6},{6,5},{7,4},{8,11},{9,10},{10,... | collective-permute-start | bytes 1572872 | tf_op jit(solution)/shard_map/ppermute | solution.py:576
  60.1 6.8 %project.2 = (f32[256,1024]{1,0:T(8,128)S(1)}, f32[256,256]{1,0:T(8,128)S(1)}) custom-call(s32[8]{0:T(128)S(1)} %dynamic-slice_bitcast_fusion.place_ref, bf16[32,4096]{1,0:T(8,128)(2,1)S(1)} %get-tuple-element.132.refs_0_, bf16[32,4096]{1,0:T(8,128)(2,1)S(1)} %collective-permute-done.refs_1_, bf16[32,4096]{1,0:T(8,128)(2,1)S(1)} %collective-permute-done.14.refs_2_, ...), custom_call_target="tpu_custom_call" | custom-call | flops 2684354560 | bytes 12582912 | tf_op jit(solution)/shard_map/project/pallas_call | solution.py:171
  66.8 7.1 %project.3 = (bf16[4,128,256]{2,1,0:T(8,128)(2,1)S(1)}, bf16[6,128,256]{2,1,0:T(8,128)(2,1)S(1)}) custom-call(s32[8]{0:T(128)S(1)} %dynamic-slice_bitcast_fusion.place_ref, bf16[32,4096]{1,0:T(8,128)(2,1)S(1)} %get-tuple-element.131.refs_0_, bf16[32,4096]{1,0:T(8,128)(2,1)S(1)} %collective-permute-done.7.refs_1_, ...), custom_call_target="tpu_custom_call" | custom-call | flops 2684354560 | bytes 12582912 | tf_op jit(solution)/shard_map/project/pallas_call | solution.py:171
  74.6 0.8 copy-done.9
  76.2 16.3 %collective-permute-done.20.refs_3_ = bf16[2,4,256,128]{3,2,1,0:T(8,128)(2,1)S(1)} collective-permute-done((bf16[2,4,256,128]{3,2,1,0:T(8,128)(2,1)}, bf16[2,4,256,128]{3,2,1,0:T(8,128)(2,1)S(1)}, u32[]{:S(2)}, u32[]{:S(2)}) %collective-permute-start.20) | collective-permute-done | bytes 524320 | tf_op jit(solution)/shard_map/ppermute | solution.py:576
  93.6 3.3 %collective-permute-start.6 = (bf16[2,4,256,128]{3,2,1,0:T(8,128)(2,1)}, bf16[2,4,256,128]{3,2,1,0:T(8,128)(2,1)S(1)}, u32[]{:S(2)}, u32[]{:S(2)}) collective-permute-start(bf16[2,4,256,128]{3,2,1,0:T(8,128)(2,1)} %copy-done.3), channel_id=1, source_target_pairs={{0,3},{1,2},{2,1},{3,0},{4,7},{5,6},{6,5},{7,4},{8,11},{9,10},{10,... | collective-permute-start | bytes 1572872 | tf_op jit(solution)/shard_map/ppermute | solution.py:576
  96.8 2.9 %collective-permute-start.23 = (bf16[4,128,256]{2,1,0:T(8,128)(2,1)}, bf16[4,128,256]{2,1,0:T(8,128)(2,1)S(1)}, u32[]{:S(2)}, u32[]{:S(2)}) collective-permute-start(bf16[4,128,256]{2,1,0:T(8,128)(2,1)} %copy-done.21), channel_id=1, source_target_pairs={{0,4},{1,5},{2,6},{3,7},{4,0},{5,1},{6,2},{7,3},{8,12},{9,13},{10,... | collective-permute-start | bytes 786440 | tf_op jit(solution)/shard_map/ppermute | solution.py:588
  99.8 3.2 %collective-permute-done.21.refs_6_ = bf16[6,128,256]{2,1,0:T(8,128)(2,1)S(1)} collective-permute-done((bf16[6,128,256]{2,1,0:T(8,128)(2,1)S(1)}, bf16[6,128,256]{2,1,0:T(8,128)(2,1)S(1)}, u32[]{:S(2)}, u32[]{:S(2)}) %collective-permute-start.21) | collective-permute-done | bytes 393248 | tf_op jit(solution)/shard_map/ppermute | solution.py:588
  103.0 0.8 collective-permute-start.22
  103.8 1.0 copy-done.7
  104.9 1.0 copy-done.10
  105.9 1.0 copy-done.13
  107.0 1.0 copy-done.16
  108.0 10.2 %attend.4 = bf16[4,144,256]{2,1,0:T(8,128)(2,1)S(1)} custom-call(s32[16]{0:T(128)S(1)} %select_n.73.first_ref, s32[256]{0:T(256)S(1)} %bitcast.24, bf16[2,4,256,128]{3,2,1,0:T(8,128)(2,1)S(1)} %copy-done.7, bf16[2,4,256,128]{3,2,1,0:T(8,128)(2,1)S(1)} %copy-done.10, bf16[2,4,256,128]{3,2,1,0:T(8,128)(2,1)S(1)} %copy-done.13, ...), custom_call_target="tpu_custom_call" | custom-call | flops 1073741824 | bytes 2097152 | tf_op jit(solution)/shard_map/attend/pallas_call | solution.py:373
  118.2 4.5 %collective-permute-done.23.refs_6_ = bf16[4,128,256]{2,1,0:T(8,128)(2,1)S(1)} collective-permute-done((bf16[4,128,256]{2,1,0:T(8,128)(2,1)}, bf16[4,128,256]{2,1,0:T(8,128)(2,1)S(1)}, u32[]{:S(2)}, u32[]{:S(2)}) %collective-permute-start.23) | collective-permute-done | bytes 262176 | tf_op jit(solution)/shard_map/ppermute | solution.py:588
  122.7 1.0 copy-done.8
  123.8 1.0 copy-done.14
  124.8 1.0 copy-done.17
  125.9 7.0 %attend.6 = bf16[4,144,256]{2,1,0:T(8,128)(2,1)S(1)} custom-call(s32[16]{0:T(128)S(1)} %select_n.73.first_ref, s32[256]{0:T(256)S(1)} %bitcast.25, bf16[2,4,256,128]{3,2,1,0:T(8,128)(2,1)S(1)} %copy-done.8, bf16[2,4,256,128]{3,2,1,0:T(8,128)(2,1)S(1)} %copy-done.11, bf16[2,4,256,128]{3,2,1,0:T(8,128)(2,1)S(1)} %copy-done.14, ...), custom_call_target="tpu_custom_call" | custom-call | flops 1073741824 | bytes 2097152 | tf_op jit(solution)/shard_map/attend/pallas_call | solution.py:373
  132.8 1.0 collective-permute-start.24
  133.8 2.0 collective-permute-start.25
  135.9 11.0 %attend.7 = (f32[4,1,256]{2,1,0:T(1,128)S(1)}, f32[4,1,256]{2,1,0:T(1,128)S(1)}, f32[4,128,256]{2,1,0:T(8,128)S(1)}) custom-call(s32[16]{0:T(128)S(1)} %select_n.73.first_ref, s32[256]{0:T(256)S(1)} %bitcast.26, bf16[2,4,256,128]{3,2,1,0:T(8,128)(2,1)S(1)} %copy-done.2, bf16[2,4,256,128]{3,2,1,0:T(8,128)(2,1)S(1)} %collective-permute-done.4.refs_1_, ...), custom_call_target="tpu_custom_call" | custom-call | flops 1073741824 | bytes 2097152 | tf_op jit(solution)/shard_map/attend/pallas_call | solution.py:373
  146.9 7.9 %attend.5 = (f32[4,1,256]{2,1,0:T(1,128)S(1)}, f32[4,1,256]{2,1,0:T(1,128)S(1)}, f32[4,128,256]{2,1,0:T(8,128)S(1)}) custom-call(s32[16]{0:T(128)S(1)} %select_n.73.first_ref, s32[256]{0:T(256)S(1)} %bitcast.27, bf16[2,4,256,128]{3,2,1,0:T(8,128)(2,1)S(1)} %copy-done.2, bf16[2,4,256,128]{3,2,1,0:T(8,128)(2,1)S(1)} %collective-permute-done.4.refs_1_, ...), custom_call_target="tpu_custom_call" | custom-call | flops 1073741824 | bytes 2097152 | tf_op jit(solution)/shard_map/attend/pallas_call | solution.py:373
  155.2 5.1 %project_out.2 = (f32[32,4096]{1,0:T(8,128)S(1)}, f32[32,4096]{1,0:T(8,128)S(1)}, f32[32,4096]{1,0:T(8,128)S(1)}, f32[32,4096]{1,0:T(8,128)S(1)}, f32[32,4096]{1...) custom-call(s32[8]{0:T(128)S(1)} %dynamic-slice_bitcast_fusion.place_ref, ...), custom_call_target="tpu_custom_call" | custom-call | flops 2147483648 | bytes 13107200 | tf_op jit(solution)/shard_map/project_out/pallas_call | solution.py:461
  160.3 1.0 collective-permute-start.26
  161.4 1.4 collective-permute-start.30
  162.8 5.1 %project_out.3 = (f32[32,4096]{1,0:T(8,128)S(1)}, f32[32,4096]{1,0:T(8,128)S(1)}, f32[32,4096]{1,0:T(8,128)S(1)}, f32[32,4096]{1,0:T(8,128)S(1)}, f32[32,4096]{1...) custom-call(s32[8]{0:T(128)S(1)} %dynamic-slice_bitcast_fusion.place_ref, ...), custom_call_target="tpu_custom_call" | custom-call | flops 2147483648 | bytes 13107200 | tf_op jit(solution)/shard_map/project_out/pallas_call | solution.py:461
  168.7 2.5 %collective-permute-start.36 = (bf16[32,4096]{1,0:T(8,128)(2,1)S(1)}, bf16[32,4096]{1,0:T(8,128)(2,1)S(1)}, u32[]{:S(2)}, u32[]{:S(2)}) collective-permute-start(bf16[32,4096]{1,0:T(8,128)(2,1)S(1)} %get-tuple-element.128), channel_id=1, source_target_pairs={{2,0},{4,2},{6,4},{7,6},{5,7},{3,5},{1,3},{0,1},{10,8},{12,10},{14... | collective-permute-start | bytes 786440 | tf_op jit(solution)/shard_map/ppermute | solution.py:646
  171.4 2.1 %collective-permute-start.31 = (bf16[32,4096]{1,0:T(8,128)(2,1)S(1)}, bf16[32,4096]{1,0:T(8,128)(2,1)S(1)}, u32[]{:S(2)}, u32[]{:S(2)}) collective-permute-start(bf16[32,4096]{1,0:T(8,128)(2,1)S(1)} %add_convert_fusion.8), channel_id=1, source_target_pairs={{2,0},{4,2},{6,4},{7,6},{5,7},{3,5},{1,3},{0,1},{10,8},{12,10},{14... | collective-permute-start | bytes 786440 | tf_op jit(solution)/shard_map/ppermute | solution.py:646
  173.5 3.5 %collective-permute-done.33 = bf16[32,4096]{1,0:T(8,128)(2,1)S(1)} collective-permute-done((bf16[32,4096]{1,0:T(8,128)(2,1)S(1)}, bf16[32,4096]{1,0:T(8,128)(2,1)S(1)}, u32[]{:S(2)}, u32[]{:S(2)}) %collective-permute-start.33) | collective-permute-done | bytes 262176 | tf_op jit(solution)/shard_map/ppermute | solution.py:646
  177.0 1.0 collective-permute-start.34
  178.1 2.5 %collective-permute-start.37 = (bf16[32,4096]{1,0:T(8,128)(2,1)S(1)}, bf16[32,4096]{1,0:T(8,128)(2,1)S(1)}, u32[]{:S(2)}, u32[]{:S(2)}) collective-permute-start(bf16[32,4096]{1,0:T(8,128)(2,1)S(1)} %add_convert_fusion.3), channel_id=1, source_target_pairs={{2,0},{4,2},{6,4},{7,6},{5,7},{3,5},{1,3},{0,1},{10,8},{12,10},{14... | collective-permute-start | bytes 786440 | tf_op jit(solution)/shard_map/ppermute | solution.py:646
  180.7 1.9 collective-permute-done.27
  182.6 1.0 collective-permute-start.28
  183.7 2.5 %collective-permute-start.32 = (bf16[32,4096]{1,0:T(8,128)(2,1)S(1)}, bf16[32,4096]{1,0:T(8,128)(2,1)S(1)}, u32[]{:S(2)}, u32[]{:S(2)}) collective-permute-start(bf16[32,4096]{1,0:T(8,128)(2,1)S(1)} %add_convert_fusion.7), channel_id=1, source_target_pairs={{2,0},{4,2},{6,4},{7,6},{5,7},{3,5},{1,3},{0,1},{10,8},{12,10},{14... | collective-permute-start | bytes 786440 | tf_op jit(solution)/shard_map/ppermute | solution.py:646
  186.3 1.9 collective-permute-done.34
  188.3 1.0 collective-permute-start.35
  189.4 2.5 %collective-permute-start.38 = (bf16[32,4096]{1,0:T(8,128)(2,1)S(1)}, bf16[32,4096]{1,0:T(8,128)(2,1)S(1)}, u32[]{:S(2)}, u32[]{:S(2)}) collective-permute-start(bf16[32,4096]{1,0:T(8,128)(2,1)S(1)} %add_convert_fusion.2), channel_id=1, source_target_pairs={{2,0},{4,2},{6,4},{7,6},{5,7},{3,5},{1,3},{0,1},{10,8},{12,10},{14... | collective-permute-start | bytes 786440 | tf_op jit(solution)/shard_map/ppermute | solution.py:646
  191.9 1.9 collective-permute-done.28
  193.9 1.0 collective-permute-start.29
  194.9 3.5 %collective-permute-done.38 = bf16[32,4096]{1,0:T(8,128)(2,1)S(1)} collective-permute-done((bf16[32,4096]{1,0:T(8,128)(2,1)S(1)}, bf16[32,4096]{1,0:T(8,128)(2,1)S(1)}, u32[]{:S(2)}, u32[]{:S(2)}) %collective-permute-start.38) | collective-permute-done | bytes 262176 | tf_op jit(solution)/shard_map/ppermute | solution.py:646
  198.5 2.5 %collective-permute-start.39 = (bf16[32,4096]{1,0:T(8,128)(2,1)S(1)}, bf16[32,4096]{1,0:T(8,128)(2,1)S(1)}, u32[]{:S(2)}, u32[]{:S(2)}) collective-permute-start(bf16[32,4096]{1,0:T(8,128)(2,1)S(1)} %add_convert_fusion.1), channel_id=1, source_target_pairs={{2,0},{4,2},{6,4},{7,6},{5,7},{3,5},{1,3},{0,1},{10,8},{12,10},{14... | collective-permute-start | bytes 786440 | tf_op jit(solution)/shard_map/ppermute | solution.py:646
  201.8 3.1 %collective-permute-done.39 = bf16[32,4096]{1,0:T(8,128)(2,1)S(1)} collective-permute-done((bf16[32,4096]{1,0:T(8,128)(2,1)S(1)}, bf16[32,4096]{1,0:T(8,128)(2,1)S(1)}, u32[]{:S(2)}, u32[]{:S(2)}) %collective-permute-start.39) | collective-permute-done | bytes 262176 | tf_op jit(solution)/shard_map/ppermute | solution.py:646
  205.0 0.8 pad_maximum_fusion
  (126 shorter events, 15.8 us)
Async XLA Ops:
  2.5 10.7 %copy-start = (s32[1,256]{1,0:T(1,128)S(1)}, s32[1,256]{1,0:T(1,128)}, u32[]{:S(2)}) copy-start(s32[1,256]{1,0:T(1,128)} %param.18) | copy-start | bytes 3076
  2.5 10.7 %copy-start.23 = (s32[1,4]{1,0:T(1,128)S(1)}, s32[1,4]{1,0:T(1,128)}, u32[]{:S(2)}) copy-start(s32[1,4]{1,0:T(1,128)} %param.17) | copy-start | bytes 52
  2.5 13.0 %copy-start.24 = (s32[4]{0:T(128)S(1)}, s32[4]{0:T(128)}, u32[]{:S(2)}) copy-start(s32[4]{0:T(128)} %param.16) | copy-start | bytes 52
  8.0 29.1 %collective-permute-start.3 = (bf16[4,2,256,1024]{3,2,1,0:T(8,128)(2,1)}, bf16[4,2,256,1024]{3,2,1,0:T(8,128)(2,1)}, u32[]{:S(2)}, u32[]{:S(2)}) collective-permute-start(bf16[4,2,256,1024]{3,2,1,0:T(8,128)(2,1)} %bitcast.21.refs_0_), channel_id=1, source_target_pairs={{8,0},{0,8},{9,1},{1,9},{10,2},{2,10},{11,3},{3,11},{12,4},{4,12},... | collective-permute-start | bytes 12582920 | tf_op jit(solution)/shard_map/ppermute | solution.py:551
  8.5 9.7 %collective-permute-start = (bf16[32,4096]{1,0:T(8,128)(2,1)S(1)}, bf16[32,4096]{1,0:T(8,128)(2,1)S(1)}, u32[]{:S(2)}, u32[]{:S(2)}) collective-permute-start(bf16[32,4096]{1,0:T(8,128)(2,1)S(1)} %get-tuple-element.132.refs_0_), channel_id=1, source_target_pairs={{0,2},{2,4},{4,6},{6,7},{7,5},{5,3},{3,1},{1,0},{8,10},{10,12},{12... | collective-permute-start | bytes 786440 | tf_op jit(solution)/shard_map/ppermute | solution.py:542
  11.2 10.7 %collective-permute-start.14 = (bf16[32,4096]{1,0:T(8,128)(2,1)S(1)}, bf16[32,4096]{1,0:T(8,128)(2,1)S(1)}, u32[]{:S(2)}, u32[]{:S(2)}) collective-permute-start(bf16[32,4096]{1,0:T(8,128)(2,1)S(1)} %get-tuple-element.132.refs_0_), channel_id=1, source_target_pairs={{2,0},{4,2},{6,4},{7,6},{5,7},{3,5},{1,3},{0,1},{10,8},{12,10},{14... | collective-permute-start | bytes 786440 | tf_op jit(solution)/shard_map/ppermute | solution.py:544
  11.2 14.7 %collective-permute-start.8 = (bf16[32,4096]{1,0:T(8,128)(2,1)S(1)}, bf16[32,4096]{1,0:T(8,128)(2,1)S(1)}, u32[]{:S(2)}, u32[]{:S(2)}) collective-permute-start(bf16[32,4096]{1,0:T(8,128)(2,1)S(1)} %get-tuple-element.131.refs_0_), channel_id=1, source_target_pairs={{2,0},{4,2},{6,4},{7,6},{5,7},{3,5},{1,3},{0,1},{10,8},{12,10},{14... | collective-permute-start | bytes 786440 | tf_op jit(solution)/shard_map/ppermute | solution.py:544
  13.1 18.6 %collective-permute-start.7 = (bf16[32,4096]{1,0:T(8,128)(2,1)S(1)}, bf16[32,4096]{1,0:T(8,128)(2,1)S(1)}, u32[]{:S(2)}, u32[]{:S(2)}) collective-permute-start(bf16[32,4096]{1,0:T(8,128)(2,1)S(1)} %get-tuple-element.131.refs_0_), channel_id=1, source_target_pairs={{0,2},{2,4},{4,6},{6,7},{7,5},{5,3},{3,1},{1,0},{8,10},{10,12},{12... | collective-permute-start | bytes 786440 | tf_op jit(solution)/shard_map/ppermute | solution.py:542
  18.3 11.1 %collective-permute-start.1 = (bf16[32,4096]{1,0:T(8,128)(2,1)S(1)}, bf16[32,4096]{1,0:T(8,128)(2,1)S(1)}, u32[]{:S(2)}, u32[]{:S(2)}) collective-permute-start(bf16[32,4096]{1,0:T(8,128)(2,1)S(1)} %collective-permute-done.refs_1_), channel_id=1, source_target_pairs={{0,2},{2,4},{4,6},{6,7},{7,5},{5,3},{3,1},{1,0},{8,10},{10,12},{12... | collective-permute-start | bytes 786440 | tf_op jit(solution)/shard_map/ppermute | solution.py:542
  21.9 11.5 %collective-permute-start.15 = (bf16[32,4096]{1,0:T(8,128)(2,1)S(1)}, bf16[32,4096]{1,0:T(8,128)(2,1)}, u32[]{:S(2)}, u32[]{:S(2)}) collective-permute-start(bf16[32,4096]{1,0:T(8,128)(2,1)S(1)} %collective-permute-done.14.refs_2_), channel_id=1, source_target_pairs={{2,0},{4,2},{6,4},{7,6},{5,7},{3,5},{1,3},{0,1},{10,8},{12,10},{14... | collective-permute-start | bytes 786440 | tf_op jit(solution)/shard_map/ppermute | solution.py:544
  25.9 11.2 %collective-permute-start.10 = (bf16[32,4096]{1,0:T(8,128)(2,1)S(1)}, bf16[32,4096]{1,0:T(8,128)(2,1)S(1)}, u32[]{:S(2)}, u32[]{:S(2)}) collective-permute-start(bf16[32,4096]{1,0:T(8,128)(2,1)S(1)} %collective-permute-done.8.refs_2_), channel_id=1, source_target_pairs={{2,0},{4,2},{6,4},{7,6},{5,7},{3,5},{1,3},{0,1},{10,8},{12,10},{14... | collective-permute-start | bytes 786440 | tf_op jit(solution)/shard_map/ppermute | solution.py:544
  29.9 16.9 %collective-permute-start.2 = (bf16[32,4096]{1,0:T(8,128)(2,1)S(1)}, bf16[32,4096]{1,0:T(8,128)(2,1)}, u32[]{:S(2)}, u32[]{:S(2)}) collective-permute-start(bf16[32,4096]{1,0:T(8,128)(2,1)S(1)} %collective-permute-done.1.refs_3_), channel_id=1, source_target_pairs={{0,2},{2,4},{4,6},{6,7},{7,5},{5,3},{3,1},{1,0},{8,10},{10,12},{12... | collective-permute-start | bytes 786440 | tf_op jit(solution)/shard_map/ppermute | solution.py:542
  31.8 17.1 %collective-permute-start.9 = (bf16[32,4096]{1,0:T(8,128)(2,1)S(1)}, bf16[32,4096]{1,0:T(8,128)(2,1)}, u32[]{:S(2)}, u32[]{:S(2)}) collective-permute-start(bf16[32,4096]{1,0:T(8,128)(2,1)S(1)} %collective-permute-done.7.refs_1_), channel_id=1, source_target_pairs={{0,2},{2,4},{4,6},{6,7},{7,5},{5,3},{3,1},{1,0},{8,10},{10,12},{12... | collective-permute-start | bytes 786440 | tf_op jit(solution)/shard_map/ppermute | solution.py:542
  33.4 17.7 %collective-permute-start.16 = (bf16[32,4096]{1,0:T(8,128)(2,1)}, bf16[32,4096]{1,0:T(8,128)(2,1)}, u32[]{:S(2)}, u32[]{:S(2)}) collective-permute-start(bf16[32,4096]{1,0:T(8,128)(2,1)} %collective-permute-done.15.refs_4_), channel_id=1, source_target_pairs={{2,0},{4,2},{6,4},{7,6},{5,7},{3,5},{1,3},{0,1},{10,8},{12,10},{14... | collective-permute-start | bytes 786440 | tf_op jit(solution)/shard_map/ppermute | solution.py:544
  37.2 13.3 %collective-permute-start.12 = (bf16[32,4096]{1,0:T(8,128)(2,1)S(1)}, bf16[32,4096]{1,0:T(8,128)(2,1)}, u32[]{:S(2)}, u32[]{:S(2)}) collective-permute-start(bf16[32,4096]{1,0:T(8,128)(2,1)S(1)} %collective-permute-done.10.refs_4_), channel_id=1, source_target_pairs={{2,0},{4,2},{6,4},{7,6},{5,7},{3,5},{1,3},{0,1},{10,8},{12,10},{14... | collective-permute-start | bytes 786440 | tf_op jit(solution)/shard_map/ppermute | solution.py:544
  40.4 0.8 copy-start.1
  41.2 0.8 copy-start.3
  42.0 0.8 copy-start.4
  42.8 0.8 copy-start.5
  43.6 0.8 copy-start.6
  44.4 0.8 copy-start.18
  45.2 0.8 copy-start.19
  46.0 0.8 copy-start.20
  46.8 9.6 %collective-permute-start.17 = (bf16[32,4096]{1,0:T(8,128)(2,1)}, bf16[32,4096]{1,0:T(8,128)(2,1)}, u32[]{:S(2)}, u32[]{:S(2)}) collective-permute-start(bf16[32,4096]{1,0:T(8,128)(2,1)} %collective-permute-done.2.refs_5_), channel_id=1, source_target_pairs={{0,2},{2,4},{4,6},{6,7},{7,5},{5,3},{3,1},{1,0},{8,10},{10,12},{12... | collective-permute-start | bytes 786440 | tf_op jit(solution)/shard_map/ppermute | solution.py:542
  48.8 18.0 %collective-permute-start.11 = (bf16[32,4096]{1,0:T(8,128)(2,1)}, bf16[32,4096]{1,0:T(8,128)(2,1)S(1)}, u32[]{:S(2)}, u32[]{:S(2)}) collective-permute-start(bf16[32,4096]{1,0:T(8,128)(2,1)} %collective-permute-done.9.refs_3_), channel_id=1, source_target_pairs={{0,2},{2,4},{4,6},{6,7},{7,5},{5,3},{3,1},{1,0},{8,10},{10,12},{12... | collective-permute-start | bytes 786440 | tf_op jit(solution)/shard_map/ppermute | solution.py:542
  50.4 16.4 %collective-permute-start.13 = (bf16[32,4096]{1,0:T(8,128)(2,1)}, bf16[32,4096]{1,0:T(8,128)(2,1)S(1)}, u32[]{:S(2)}, u32[]{:S(2)}) collective-permute-start(bf16[32,4096]{1,0:T(8,128)(2,1)} %collective-permute-done.12.refs_6_), channel_id=1, source_target_pairs={{2,0},{4,2},{6,4},{7,6},{5,7},{3,5},{1,3},{0,1},{10,8},{12,10},{14... | collective-permute-start | bytes 786440 | tf_op jit(solution)/shard_map/ppermute | solution.py:544
  50.9 23.7 %collective-permute-start.18 = (bf16[2,4,256,128]{3,2,1,0:T(8,128)(2,1)}, bf16[2,4,256,128]{3,2,1,0:T(8,128)(2,1)S(1)}, u32[]{:S(2)}, u32[]{:S(2)}) collective-permute-start(bf16[2,4,256,128]{3,2,1,0:T(8,128)(2,1)} %copy-done.20), channel_id=1, source_target_pairs={{0,1},{1,0},{2,3},{3,2},{4,5},{5,4},{6,7},{7,6},{8,9},{9,8},{10,11... | collective-permute-start | bytes 1572872 | tf_op jit(solution)/shard_map/ppermute | solution.py:576
  51.1 24.4 %collective-permute-start.19 = (bf16[2,4,256,128]{3,2,1,0:T(8,128)(2,1)}, bf16[2,4,256,128]{3,2,1,0:T(8,128)(2,1)S(1)}, u32[]{:S(2)}, u32[]{:S(2)}) collective-permute-start(bf16[2,4,256,128]{3,2,1,0:T(8,128)(2,1)} %copy-done.19), channel_id=1, source_target_pairs={{0,2},{1,3},{2,0},{3,1},{4,6},{5,7},{6,4},{7,5},{8,10},{9,11},{10,... | collective-permute-start | bytes 1572872 | tf_op jit(solution)/shard_map/ppermute | solution.py:576
  56.4 36.2 %collective-permute-start.20 = (bf16[2,4,256,128]{3,2,1,0:T(8,128)(2,1)}, bf16[2,4,256,128]{3,2,1,0:T(8,128)(2,1)S(1)}, u32[]{:S(2)}, u32[]{:S(2)}) collective-permute-start(bf16[2,4,256,128]{3,2,1,0:T(8,128)(2,1)} %copy-done.18), channel_id=1, source_target_pairs={{0,3},{1,2},{2,1},{3,0},{4,7},{5,6},{6,5},{7,4},{8,11},{9,10},{10,... | collective-permute-start | bytes 1572872 | tf_op jit(solution)/shard_map/ppermute | solution.py:576
  74.6 0.8 copy-start.9
  75.4 0.8 copy-start.12
  92.5 0.8 copy-start.15
  93.3 9.6 %collective-permute-start.21 = (bf16[6,128,256]{2,1,0:T(8,128)(2,1)S(1)}, bf16[6,128,256]{2,1,0:T(8,128)(2,1)S(1)}, u32[]{:S(2)}, u32[]{:S(2)}) collective-permute-start(bf16[6,128,256]{2,1,0:T(8,128)(2,1)S(1)} %get-tuple-element.103.refs_6_), channel_id=1, source_target_pairs={{0,4},{1,5},{2,6},{3,7},{4,0},{5,1},{6,2},{7,3},{8,12},{9,13},{10,... | collective-permute-start | bytes 1179656 | tf_op jit(solution)/shard_map/ppermute | solution.py:588
  93.3 29.4 %copy-start.11 = (bf16[2,4,256,128]{3,2,1,0:T(8,128)(2,1)S(1)}, bf16[2,4,256,128]{3,2,1,0:T(8,128)(2,1)}, u32[]{:S(2)}) copy-start(bf16[2,4,256,128]{3,2,1,0:T(8,128)(2,1)} %copy-done.9) | copy-start | bytes 1572868
  93.3 42.5 %collective-permute-start.4 = (bf16[2,4,256,128]{3,2,1,0:T(8,128)(2,1)}, bf16[2,4,256,128]{3,2,1,0:T(8,128)(2,1)S(1)}, u32[]{:S(2)}, u32[]{:S(2)}) collective-permute-start(bf16[2,4,256,128]{3,2,1,0:T(8,128)(2,1)} %copy-done.5), channel_id=1, source_target_pairs={{0,1},{1,0},{2,3},{3,2},{4,5},{5,4},{6,7},{7,6},{8,9},{9,8},{10,11... | collective-permute-start | bytes 1572872 | tf_op jit(solution)/shard_map/ppermute | solution.py:576
  93.3 42.5 %collective-permute-start.5 = (bf16[2,4,256,128]{3,2,1,0:T(8,128)(2,1)}, bf16[2,4,256,128]{3,2,1,0:T(8,128)(2,1)S(1)}, u32[]{:S(2)}, u32[]{:S(2)}) collective-permute-start(bf16[2,4,256,128]{3,2,1,0:T(8,128)(2,1)} %copy-done.4), channel_id=1, source_target_pairs={{0,2},{1,3},{2,0},{3,1},{4,6},{5,7},{6,4},{7,5},{8,10},{9,11},{10,... | collective-permute-start | bytes 1572872 | tf_op jit(solution)/shard_map/ppermute | solution.py:576
  93.6 42.3 %collective-permute-start.6 = (bf16[2,4,256,128]{3,2,1,0:T(8,128)(2,1)}, bf16[2,4,256,128]{3,2,1,0:T(8,128)(2,1)S(1)}, u32[]{:S(2)}, u32[]{:S(2)}) collective-permute-start(bf16[2,4,256,128]{3,2,1,0:T(8,128)(2,1)} %copy-done.3), channel_id=1, source_target_pairs={{0,3},{1,2},{2,1},{3,0},{4,7},{5,6},{6,5},{7,4},{8,11},{9,10},{10,... | collective-permute-start | bytes 1572872 | tf_op jit(solution)/shard_map/ppermute | solution.py:576
  96.8 25.9 %collective-permute-start.23 = (bf16[4,128,256]{2,1,0:T(8,128)(2,1)}, bf16[4,128,256]{2,1,0:T(8,128)(2,1)S(1)}, u32[]{:S(2)}, u32[]{:S(2)}) collective-permute-start(bf16[4,128,256]{2,1,0:T(8,128)(2,1)} %copy-done.21), channel_id=1, source_target_pairs={{0,4},{1,5},{2,6},{3,7},{4,0},{5,1},{6,2},{7,3},{8,12},{9,13},{10,... | collective-permute-start | bytes 786440 | tf_op jit(solution)/shard_map/ppermute | solution.py:588
  103.0 32.9 %copy-start.2 = (bf16[2,4,256,128]{3,2,1,0:T(8,128)(2,1)S(1)}, bf16[2,4,256,128]{3,2,1,0:T(8,128)(2,1)}, u32[]{:S(2)}) copy-start(bf16[2,4,256,128]{3,2,1,0:T(8,128)(2,1)} %copy-done.1) | copy-start | bytes 1572868
  103.0 19.7 %collective-permute-start.22 = (bf16[256,256]{1,0:T(8,128)(2,1)S(1)}, bf16[256,256]{1,0:T(8,128)(2,1)S(1)}, u32[]{:S(2)}, u32[]{:S(2)}) collective-permute-start(bf16[256,256]{1,0:T(8,128)(2,1)S(1)} %pad_maximum_fusion.3), channel_id=1, source_target_pairs={{0,0},{1,2},{2,4},{3,6},{4,1},{5,3},{6,5},{7,7},{8,8},{9,10},{10,1... | collective-permute-start | bytes 393224 | tf_op jit(solution)/shard_map/ppermute | solution.py:595
  103.8 1.0 copy-start.7
  104.9 1.0 copy-start.10
  105.9 1.0 copy-start.13
  107.0 1.0 copy-start.16
  108.0 38.9 %copy-start.22 = (bf16[4,128,256]{2,1,0:T(8,128)(2,1)S(1)}, bf16[4,128,256]{2,1,0:T(8,128)(2,1)}, u32[]{:S(2)}) copy-start(bf16[4,128,256]{2,1,0:T(8,128)(2,1)} %copy-done.21) | copy-start | bytes 786436
  122.7 1.0 copy-start.8
  123.8 1.0 copy-start.14
  124.8 1.0 copy-start.17
  132.8 22.0 %collective-permute-start.24 = (bf16[4,144,256]{2,1,0:T(8,128)(2,1)S(1)}, bf16[4,144,256]{2,1,0:T(8,128)(2,1)S(1)}, u32[]{:S(2)}, u32[]{:S(2)}) collective-permute-start(bf16[4,144,256]{2,1,0:T(8,128)(2,1)S(1)} %attend.6), channel_id=1, source_target_pairs={{0,4},{1,5},{2,6},{3,7},{4,0},{5,1},{6,2},{7,3},{8,12},{9,13},{10,... | collective-permute-start | bytes 884744 | tf_op jit(solution)/shard_map/ppermute | solution.py:629
  133.8 21.0 %collective-permute-start.25 = (bf16[4,144,256]{2,1,0:T(8,128)(2,1)S(1)}, bf16[4,144,256]{2,1,0:T(8,128)(2,1)S(1)}, u32[]{:S(2)}, u32[]{:S(2)}) collective-permute-start(bf16[4,144,256]{2,1,0:T(8,128)(2,1)S(1)} %attend.4), channel_id=1, source_target_pairs={{0,4},{1,5},{2,6},{3,7},{4,0},{5,1},{6,2},{7,3},{8,12},{9,13},{10,... | collective-permute-start | bytes 884744 | tf_op jit(solution)/shard_map/ppermute | solution.py:629
  160.3 10.9 %collective-permute-start.26 = (bf16[32,4096]{1,0:T(8,128)(2,1)S(1)}, bf16[32,4096]{1,0:T(8,128)(2,1)S(1)}, u32[]{:S(2)}, u32[]{:S(2)}) collective-permute-start(bf16[32,4096]{1,0:T(8,128)(2,1)S(1)} %get-tuple-element.117), channel_id=1, source_target_pairs={{0,2},{2,4},{4,6},{6,7},{7,5},{5,3},{3,1},{1,0},{8,10},{10,12},{12... | collective-permute-start | bytes 786440 | tf_op jit(solution)/shard_map/ppermute | solution.py:646
  161.4 10.0 %collective-permute-start.30 = (bf16[32,4096]{1,0:T(8,128)(2,1)S(1)}, bf16[32,4096]{1,0:T(8,128)(2,1)S(1)}, u32[]{:S(2)}, u32[]{:S(2)}) collective-permute-start(bf16[32,4096]{1,0:T(8,128)(2,1)S(1)} %convert_element_type.115), channel_id=1, source_target_pairs={{2,0},{4,2},{6,4},{7,6},{5,7},{3,5},{1,3},{0,1},{10,8},{12,10},{14... | collective-permute-start | bytes 786440 | tf_op jit(solution)/shard_map/ppermute | solution.py:646
  167.9 9.0 %collective-permute-start.33 = (bf16[32,4096]{1,0:T(8,128)(2,1)S(1)}, bf16[32,4096]{1,0:T(8,128)(2,1)S(1)}, u32[]{:S(2)}, u32[]{:S(2)}) collective-permute-start(bf16[32,4096]{1,0:T(8,128)(2,1)S(1)} %convert_element_type.122), channel_id=1, source_target_pairs={{0,2},{2,4},{4,6},{6,7},{7,5},{5,3},{3,1},{1,0},{8,10},{10,12},{12... | collective-permute-start | bytes 786440 | tf_op jit(solution)/shard_map/ppermute | solution.py:646
  168.7 9.4 %collective-permute-start.36 = (bf16[32,4096]{1,0:T(8,128)(2,1)S(1)}, bf16[32,4096]{1,0:T(8,128)(2,1)S(1)}, u32[]{:S(2)}, u32[]{:S(2)}) collective-permute-start(bf16[32,4096]{1,0:T(8,128)(2,1)S(1)} %get-tuple-element.128), channel_id=1, source_target_pairs={{2,0},{4,2},{6,4},{7,6},{5,7},{3,5},{1,3},{0,1},{10,8},{12,10},{14... | collective-permute-start | bytes 786440 | tf_op jit(solution)/shard_map/ppermute | solution.py:646
  171.3 11.3 %collective-permute-start.27 = (bf16[32,4096]{1,0:T(8,128)(2,1)S(1)}, bf16[32,4096]{1,0:T(8,128)(2,1)S(1)}, u32[]{:S(2)}, u32[]{:S(2)}) collective-permute-start(bf16[32,4096]{1,0:T(8,128)(2,1)S(1)} %add_convert_fusion.11), channel_id=1, source_target_pairs={{0,2},{2,4},{4,6},{6,7},{7,5},{5,3},{3,1},{1,0},{8,10},{10,12},{12... | collective-permute-start | bytes 786440 | tf_op jit(solution)/shard_map/ppermute | solution.py:646
  171.4 12.3 %collective-permute-start.31 = (bf16[32,4096]{1,0:T(8,128)(2,1)S(1)}, bf16[32,4096]{1,0:T(8,128)(2,1)S(1)}, u32[]{:S(2)}, u32[]{:S(2)}) collective-permute-start(bf16[32,4096]{1,0:T(8,128)(2,1)S(1)} %add_convert_fusion.8), channel_id=1, source_target_pairs={{2,0},{4,2},{6,4},{7,6},{5,7},{3,5},{1,3},{0,1},{10,8},{12,10},{14... | collective-permute-start | bytes 786440 | tf_op jit(solution)/shard_map/ppermute | solution.py:646
  177.0 11.2 %collective-permute-start.34 = (bf16[32,4096]{1,0:T(8,128)(2,1)S(1)}, bf16[32,4096]{1,0:T(8,128)(2,1)S(1)}, u32[]{:S(2)}, u32[]{:S(2)}) collective-permute-start(bf16[32,4096]{1,0:T(8,128)(2,1)S(1)} %add_convert_fusion.5), channel_id=1, source_target_pairs={{0,2},{2,4},{4,6},{6,7},{7,5},{5,3},{3,1},{1,0},{8,10},{10,12},{12... | collective-permute-start | bytes 786440 | tf_op jit(solution)/shard_map/ppermute | solution.py:646
  178.1 11.2 %collective-permute-start.37 = (bf16[32,4096]{1,0:T(8,128)(2,1)S(1)}, bf16[32,4096]{1,0:T(8,128)(2,1)S(1)}, u32[]{:S(2)}, u32[]{:S(2)}) collective-permute-start(bf16[32,4096]{1,0:T(8,128)(2,1)S(1)} %add_convert_fusion.3), channel_id=1, source_target_pairs={{2,0},{4,2},{6,4},{7,6},{5,7},{3,5},{1,3},{0,1},{10,8},{12,10},{14... | collective-permute-start | bytes 786440 | tf_op jit(solution)/shard_map/ppermute | solution.py:646
  182.6 11.2 %collective-permute-start.28 = (bf16[32,4096]{1,0:T(8,128)(2,1)S(1)}, bf16[32,4096]{1,0:T(8,128)(2,1)S(1)}, u32[]{:S(2)}, u32[]{:S(2)}) collective-permute-start(bf16[32,4096]{1,0:T(8,128)(2,1)S(1)} %add_convert_fusion.10), channel_id=1, source_target_pairs={{0,2},{2,4},{4,6},{6,7},{7,5},{5,3},{3,1},{1,0},{8,10},{10,12},{12... | collective-permute-start | bytes 786440 | tf_op jit(solution)/shard_map/ppermute | solution.py:646
  183.7 17.3 %collective-permute-start.32 = (bf16[32,4096]{1,0:T(8,128)(2,1)S(1)}, bf16[32,4096]{1,0:T(8,128)(2,1)S(1)}, u32[]{:S(2)}, u32[]{:S(2)}) collective-permute-start(bf16[32,4096]{1,0:T(8,128)(2,1)S(1)} %add_convert_fusion.7), channel_id=1, source_target_pairs={{2,0},{4,2},{6,4},{7,6},{5,7},{3,5},{1,3},{0,1},{10,8},{12,10},{14... | collective-permute-start | bytes 786440 | tf_op jit(solution)/shard_map/ppermute | solution.py:646
  188.3 13.6 %collective-permute-start.35 = (bf16[32,4096]{1,0:T(8,128)(2,1)S(1)}, bf16[32,4096]{1,0:T(8,128)(2,1)S(1)}, u32[]{:S(2)}, u32[]{:S(2)}) collective-permute-start(bf16[32,4096]{1,0:T(8,128)(2,1)S(1)} %add_convert_fusion.4), channel_id=1, source_target_pairs={{0,2},{2,4},{4,6},{6,7},{7,5},{5,3},{3,1},{1,0},{8,10},{10,12},{12... | collective-permute-start | bytes 786440 | tf_op jit(solution)/shard_map/ppermute | solution.py:646
  189.4 9.1 %collective-permute-start.38 = (bf16[32,4096]{1,0:T(8,128)(2,1)S(1)}, bf16[32,4096]{1,0:T(8,128)(2,1)S(1)}, u32[]{:S(2)}, u32[]{:S(2)}) collective-permute-start(bf16[32,4096]{1,0:T(8,128)(2,1)S(1)} %add_convert_fusion.2), channel_id=1, source_target_pairs={{2,0},{4,2},{6,4},{7,6},{5,7},{3,5},{1,3},{0,1},{10,8},{12,10},{14... | collective-permute-start | bytes 786440 | tf_op jit(solution)/shard_map/ppermute | solution.py:646
  193.9 7.8 %collective-permute-start.29 = (bf16[32,4096]{1,0:T(8,128)(2,1)S(1)}, bf16[32,4096]{1,0:T(8,128)(2,1)S(1)}, u32[]{:S(2)}, u32[]{:S(2)}) collective-permute-start(bf16[32,4096]{1,0:T(8,128)(2,1)S(1)} %add_convert_fusion.9), channel_id=1, source_target_pairs={{0,2},{2,4},{4,6},{6,7},{7,5},{5,3},{3,1},{1,0},{8,10},{10,12},{12... | collective-permute-start | bytes 786440 | tf_op jit(solution)/shard_map/ppermute | solution.py:646
  198.5 6.4 %collective-permute-start.39 = (bf16[32,4096]{1,0:T(8,128)(2,1)S(1)}, bf16[32,4096]{1,0:T(8,128)(2,1)S(1)}, u32[]{:S(2)}, u32[]{:S(2)}) collective-permute-start(bf16[32,4096]{1,0:T(8,128)(2,1)S(1)} %add_convert_fusion.1), channel_id=1, source_target_pairs={{2,0},{4,2},{6,4},{7,6},{5,7},{3,5},{1,3},{0,1},{10,8},{12,10},{14... | collective-permute-start | bytes 786440 | tf_op jit(solution)/shard_map/ppermute | solution.py:646
  (1 other events, 0.7 us)

commit v7 on v6

--- a/solution.py
+++ b/solution.py
@@ -384,6 +384,36 @@
     )(*operands)
 
 
+def pick_kernel(n_tiles, side_ref, here_ref, there_ref, out_ref):
+    def pick(keys_ref, values_ref, head):
+        cols = slice(head * HD, (head + 1) * HD)
+        for index in range(SEL // HD):
+            rows = slice(index * HD, (index + 1) * HD)
+            out_ref[rows, :HD] = keys_ref[n_tiles + index][:, cols]
+            out_ref[rows, HD:] = values_ref[n_tiles + index][:, cols]
+
+    @pl.when(side_ref[0] == 1)
+    def _():
+        pick(here_ref, there_ref, 0)
+
+    @pl.when(side_ref[0] == 0)
+    def _():
+        pick(there_ref, here_ref, 1)
+
+
+def pick_new(side, here, there, n_tiles):
+    vmem = pl.BlockSpec(memory_space=pltpu.VMEM)
+    return pl.pallas_call(
+        functools.partial(pick_kernel, n_tiles),
+        in_specs=[pl.BlockSpec(memory_space=pltpu.SMEM), vmem, vmem],
+        out_specs=vmem,
+        out_shape=jax.ShapeDtypeStruct((SEL, 2 * HD), jnp.bfloat16),
+        compiler_params=megabytes(4),
+        cost_estimate=cost(0, 8 * SEL * HD),
+        name="pick_new",
+    )(side, here, there)
+
+
 def merge_kernel(*refs):
     out_ref = refs[-1]
     scale = math.log2(math.e) / math.sqrt(HD)
@@ -550,15 +580,18 @@
                 pairs = [((i + shift) % req_size, i) for i in range(req_size)]
                 sources.append(lax.ppermute(by_kind, "req", pairs))
             holder = (doc_slot // slots - lax.axis_index("req")) % req_size
+            slot = doc_slot % slots
+            side = (me < middle).astype(jnp.int32)[None]
             takers = jnp.concatenate([me ^ order, me ^ order ^ middle]) * KVH // tp_size
         if k == 2:
-            first[-1], dead, first_pos, cosine, sine_part, q_pos, takers, holder = (
+            first[-1], dead, first_pos, cosine, sine_part, q_pos, takers, holder, slot, place, side = (
                 lax.optimization_barrier(
-                    (first[-1], dead, first_pos, cosine, sine_part, q_pos, takers, holder)
+                    (first[-1], dead, first_pos, cosine, sine_part, q_pos, takers, holder, slot)
+                    + (place, side)
                 )
             )
         if k == far - 1:
-            sent = select_docs(sources, holder, doc_slot % slots, takers, tp_size)
+            sent = select_docs(sources, holder, slot, takers, tp_size)
             first[-1], *sent = lax.optimization_barrier((first[-1], *sent))
     projected = None
     for chunk, held in enumerate(streams):
@@ -580,7 +613,7 @@
         ]
         for slot in range(2)
     ]
-    *queries, chunks[1] = lax.optimization_barrier((*projected[:HALVES], chunks[1]))
+    *queries, chunks[1][1] = lax.optimization_barrier((*projected[:HALVES], chunks[1][1]))
     n_tiles = queries[0].shape[0]
     across = [(i, i ^ middle) for i in range(tp_size)]
     their_queries = [None] * HALVES
@@ -588,18 +621,8 @@
         their_queries[part] = lax.ppermute(queries[part], "tp", across)
 
     if tp_size == KVH:
-        is_key = me < middle
-        here = queries[-1][n_tiles:].reshape(SEL, 2 * HD)
-        there = their_queries[-1][n_tiles:].reshape(SEL, 2 * HD)
-        keys, vals = jnp.where(is_key, here, there), jnp.where(is_key, there, here)
         new = lax.ppermute(
-            jnp.concatenate(
-                [
-                    jnp.where(is_key, keys[:, :HD], keys[:, HD:]),
-                    jnp.where(is_key, vals[:, :HD], vals[:, HD:]),
-                ],
-                axis=1,
-            ),
+            pick_new(side, queries[-1], their_queries[-1], n_tiles),
             "tp",
             [(i, 2 * i if i < middle else 2 * (i - middle) + 1) for i in range(tp_size)],
         )

time: 205 us -> 205 us (level)
  waiting for transfers between devices: 57.4 us -> 83.7 us
  local copies, waits for them, and re-layouts: 24.4 us -> 7.6 us
  Pallas kernels: 63.8 us -> 57.6 us
  starting transfers between devices: 52.4 us -> 48.4 us
    unnamed x53 -> x9, local copies, waits for them, and re-layouts: 17.3 us -> 0.54 us
    ppermute x14, waiting for transfers between devices: 16.6 us -> 24.5 us  [per_device(): held = lax.ppermute(term.astype(jnp.bfloat16), 'tp', pairs)]
    ppermute x2, waiting for transfers between devices: 0.01 us -> 7.47 us  [per_device(): theirs[part] = lax.ppermute(packed, 'tp', across)]
    ppermute x7, waiting for transfers between devices: 7.31 us -> 14.2 us  [per_device(): held['behind'].append(lax.ppermute(held['behind'][-1], 'tp', back))]
    ppermute x2, waiting for transfers between devices: 7.64 us -> 13 us  [per_device(): their_queries[part] = lax.ppermute(queries[part], 'tp', across)]
    pallas_call x4, Pallas kernels: 36.1 us -> 31.1 us  [attend(): pl.pallas_call(functools.partial(attend_kernel, n_chunks, bool(fresh), n_...]
    ppermute x14, starting transfers between devices: 22.1 us -> 17.2 us  [per_device(): held = lax.ppermute(term.astype(jnp.bfloat16), 'tp', pairs)]
    ppermute x2, starting transfers between devices: 2.92 us -> 0.07 us  [per_device(): their_queries[part] = lax.ppermute(queries[part], 'tp', across)]
  transfers between devices with their start and end apart: 40 -> 40, of which waited for: 15 -> 19; matrix products, arithmetic and copies ran while one was open for 3% -> 3% of each run, Pallas kernels for 28% -> 25%
where the time goes in v7:
time: 205 us
  waiting for transfers between devices  83.7 us (41%)
  Pallas kernels  57.6 us (28%)
  starting transfers between devices  48.4 us (24%)
  local copies, waits for them, and re-layouts  7.6 us (4%)
  other arithmetic  7.26 us (4%)
    pallas_call x4, Pallas kernels, attend(): pl.pallas_call(functools.partial(attend_kernel, n_chunks, bool(fresh), n_...  31.1 us
    ppermute x14, waiting for transfers between devices, per_device(): held = lax.ppermute(term.astype(jnp.bfloat16), 'tp', pairs)  24.5 us
    ppermute x14, starting transfers between devices, per_device(): held = lax.ppermute(term.astype(jnp.bfloat16), 'tp', pairs)  17.2 us
    ppermute x7, waiting for transfers between devices, per_device(): held['behind'].append(lax.ppermute(held['behind'][-1], 'tp', back))  14.2 us
    ppermute x6, waiting for transfers between devices, per_device(): lax.ppermute(sent[slot * middle + j], 'tp', [(i, i ^ j) for i in range(tp...  14.2 us
    ppermute x2, waiting for transfers between devices, per_device(): their_queries[part] = lax.ppermute(queries[part], 'tp', across)  13 us
    pallas_call x2, Pallas kernels, project(): pl.pallas_call(functools.partial(project_kernel, len(blocks), chunk, is_l...  12.6 us
    ppermute x7, starting transfers between devices, per_device(): held['before'].append(lax.ppermute(held['before'][-1], 'tp', forth))  11.7 us
  transfers between devices with their start and end apart: 40, of which 19 were waited for; matrix products, arithmetic and copies ran while one was open for 3% of the time, Pallas kernels for 25%

profile of v7, /device:TPU:0, one launch (start us, length us, event | category | flops | bytes accessed | tf_op | source)
XLA Modules:
  0.0 204.9 jit_solution(9101370298474502039)
XLA Ops:
  0.0 1.2 fusion
  1.3 1.2 fusion.2
  2.5 5.5 %copy.16 = bf16[4,256,2,1024]{3,1,2,0:T(8,128)(2,1)} copy(bf16[4,256,2,1024]{3,2,1,0:T(2,128)(2,1)} %param.15) | data formatting | bytes 8388608 | tf_op jit(solution)/shard_map/optimization_barrier | solution.py:540
  8.0 0.5 collective-permute-start.3
  8.5 2.6 %collective-permute-start = (bf16[32,4096]{1,0:T(8,128)(2,1)S(1)}, bf16[32,4096]{1,0:T(8,128)(2,1)S(1)}, u32[]{:S(2)}, u32[]{:S(2)}) collective-permute-start(bf16[32,4096]{1,0:T(8,128)(2,1)S(1)} %get-tuple-element.130.refs_0_), channel_id=1, source_target_pairs={{0,2},{2,4},{4,6},{6,7},{7,5},{5,3},{3,1},{1,0},{8,10},{10,12},{12... | collective-permute-start | bytes 786440 | tf_op jit(solution)/shard_map/ppermute | solution.py:572
  11.1 2.0 collective-permute-start.8
  13.6 1.3 compare_reduce_fusion
  15.1 0.5 fusion.3
  15.6 2.6 %collective-permute-done.refs_1_ = bf16[32,4096]{1,0:T(8,128)(2,1)S(1)} collective-permute-done((bf16[32,4096]{1,0:T(8,128)(2,1)S(1)}, bf16[32,4096]{1,0:T(8,128)(2,1)S(1)}, u32[]{:S(2)}, u32[]{:S(2)}) %collective-permute-start) | collective-permute-done | bytes 262176 | tf_op jit(solution)/shard_map/ppermute | solution.py:572
  18.2 2.0 collective-permute-start.1
  20.2 0.7 dynamic-slice_bitcast_fusion.place_ref
  21.1 4.1 %collective-permute-done.8.refs_2_ = bf16[32,4096]{1,0:T(8,128)(2,1)S(1)} collective-permute-done((bf16[32,4096]{1,0:T(8,128)(2,1)S(1)}, bf16[32,4096]{1,0:T(8,128)(2,1)S(1)}, u32[]{:S(2)}, u32[]{:S(2)}) %collective-permute-start.8) | collective-permute-done | bytes 262176 | tf_op jit(solution)/shard_map/ppermute | solution.py:574
  25.2 0.3 collective-permute-start.10
  25.6 0.5 broadcast.178
  26.2 0.7 reduce.3
  27.0 1.7 collective-permute-start.15
  28.7 0.6 collective-permute-done.1.refs_3_
  29.3 0.6 broadcast_in_dim.20.refs_4_
  29.9 1.8 collective-permute-start.2
  31.8 1.6 collective-permute-start.9
  33.3 1.1 collective-permute-done.10.refs_4_
  34.7 5.4 %collective-permute-done.15.refs_4_ = bf16[32,4096]{1,0:T(8,128)(2,1)S(1)} collective-permute-done((bf16[32,4096]{1,0:T(8,128)(2,1)S(1)}, bf16[32,4096]{1,0:T(8,128)(2,1)S(1)}, u32[]{:S(2)}, u32[]{:S(2)}) %collective-permute-start.15) | collective-permute-done | bytes 262176 | tf_op jit(solution)/shard_map/ppermute | solution.py:574
  40.3 3.3 %select_docs.1 = (bf16[2,4,256,128]{3,2,1,0:T(8,128)(2,1)S(1)}, bf16[2,4,256,128]{3,2,1,0:T(8,128)(2,1)S(1)}, bf16[2,4,256,128]{3,2,1,0:T(8,128)(2,1)S(1)}, bf16...) custom-call(s32[4]{0:T(128)S(1)} %get-tuple-element.71.place_ref, ...), custom_call_target="tpu_custom_call" | custom-call | bytes 8388608 | tf_op jit(solution)/shard_map/select_docs/pallas_call | solution.py:221
  43.6 1.8 collective-permute-start.17
  45.7 1.7 collective-permute-start.11
  47.4 0.3 collective-permute-start.13
  47.7 3.6 %collective-permute-done.16.refs_6_ = bf16[32,4096]{1,0:T(8,128)(2,1)S(1)} collective-permute-done((bf16[32,4096]{1,0:T(8,128)(2,1)S(1)}, bf16[32,4096]{1,0:T(8,128)(2,1)S(1)}, u32[]{:S(2)}, u32[]{:S(2)}) %collective-permute-start.16) | collective-permute-done | bytes 262176 | tf_op jit(solution)/shard_map/ppermute | solution.py:574
  51.3 1.6 collective-permute-start.19
  52.9 6.1 %project.2 = (f32[256,1024]{1,0:T(8,128)S(1)}, f32[256,256]{1,0:T(8,128)S(1)}) custom-call(s32[8]{0:T(128)S(1)} %dynamic-slice_bitcast_fusion.place_ref, bf16[32,4096]{1,0:T(8,128)(2,1)S(1)} %get-tuple-element.130.refs_0_, bf16[32,4096]{1,0:T(8,128)(2,1)S(1)} %collective-permute-done.refs_1_, bf16[32,4096]{1,0:T(8,128)(2,1)S(1)} %collective-permute-done.14.refs_2_, ...), custom_call_target="tpu_custom_call" | custom-call | flops 2684354560 | bytes 12582912 | tf_op jit(solution)/shard_map/project/pallas_call | solution.py:171
  59.0 7.2 %collective-permute-done.11.refs_5_ = bf16[32,4096]{1,0:T(8,128)(2,1)S(1)} collective-permute-done((bf16[32,4096]{1,0:T(8,128)(2,1)S(1)}, bf16[32,4096]{1,0:T(8,128)(2,1)S(1)}, u32[]{:S(2)}, u32[]{:S(2)}) %collective-permute-start.11) | collective-permute-done | bytes 262176 | tf_op jit(solution)/shard_map/ppermute | solution.py:572
  66.2 6.5 %project.3 = (bf16[4,128,256]{2,1,0:T(8,128)(2,1)S(1)}, bf16[6,128,256]{2,1,0:T(8,128)(2,1)S(1)}) custom-call(s32[8]{0:T(128)S(1)} %dynamic-slice_bitcast_fusion.place_ref, bf16[32,4096]{1,0:T(8,128)(2,1)S(1)} %get-tuple-element.129.refs_0_, bf16[32,4096]{1,0:T(8,128)(2,1)S(1)} %collective-permute-done.7.refs_1_, ...), custom_call_target="tpu_custom_call" | custom-call | flops 2684354560 | bytes 12582912 | tf_op jit(solution)/shard_map/project/pallas_call | solution.py:171
  72.8 5.1 %collective-permute-start.20 = (bf16[2,4,256,128]{3,2,1,0:T(8,128)(2,1)S(1)}, bf16[2,4,256,128]{3,2,1,0:T(8,128)(2,1)S(1)}, u32[]{:S(2)}, u32[]{:S(2)}) collective-permute-start(bf16[2,4,256,128]{3,2,1,0:T(8,128)(2,1)S(1)} %get-tuple-element.101), channel_id=1, source_target_pairs={{0,3},{1,2},{2,1},{3,0},{4,7},{5,6},{6,5},{7,4},{8,11},{9,10},{10,... | collective-permute-start | bytes 1572872 | tf_op jit(solution)/shard_map/ppermute | solution.py:609
  77.9 0.8 collective-permute-start.4
  78.7 2.7 %collective-permute-start.6 = (bf16[2,4,256,128]{3,2,1,0:T(8,128)(2,1)S(1)}, bf16[2,4,256,128]{3,2,1,0:T(8,128)(2,1)S(1)}, u32[]{:S(2)}, u32[]{:S(2)}) collective-permute-start(bf16[2,4,256,128]{3,2,1,0:T(8,128)(2,1)S(1)} %get-tuple-element.86), channel_id=1, source_target_pairs={{0,3},{1,2},{2,1},{3,0},{4,7},{5,6},{6,5},{7,4},{8,11},{9,10},{10,... | collective-permute-start | bytes 1572872 | tf_op jit(solution)/shard_map/ppermute | solution.py:609
  81.4 9.1 %collective-permute-done.21.refs_6_.there_ref = bf16[6,128,256]{2,1,0:T(8,128)(2,1)S(1)} collective-permute-done((bf16[6,128,256]{2,1,0:T(8,128)(2,1)S(1)}, bf16[6,128,256]{2,1,0:T(8,128)(2,1)S(1)}, u32[]{:S(2)}, u32[]{:S(2)}) %collective-permute-start.21) | collective-permute-done | bytes 393248 | tf_op jit(solution)/shard_map/ppermute | solution.py:621
  90.6 14.1 %collective-permute-done.20.refs_3_ = bf16[2,4,256,128]{3,2,1,0:T(8,128)(2,1)S(1)} collective-permute-done((bf16[2,4,256,128]{3,2,1,0:T(8,128)(2,1)S(1)}, bf16[2,4,256,128]{3,2,1,0:T(8,128)(2,1)S(1)}, u32[]{:S(2)}, u32[]{:S(2)}) %collective-permute-start.20) | collective-permute-done | bytes 524320 | tf_op jit(solution)/shard_map/ppermute | solution.py:609
  104.7 0.7 collective-permute-start.22
  105.4 9.0 %attend.4 = bf16[4,144,256]{2,1,0:T(8,128)(2,1)S(1)} custom-call(s32[16]{0:T(128)S(1)} %select_n.42.first_ref, s32[256]{0:T(256)S(1)} %bitcast.23, bf16[2,4,256,128]{3,2,1,0:T(8,128)(2,1)S(1)} %get-tuple-element.98.refs_0_, bf16[2,4,256,128]{3,2,1,0:T(8,128)(2,1)S(1)} %collective-permute-done.18.refs_1_, ...), custom_call_target="tpu_custom_call" | custom-call | flops 1073741824 | bytes 2097152 | tf_op jit(solution)/shard_map/attend/pallas_call | solution.py:373
  114.4 3.9 %collective-permute-done.23.refs_6_ = bf16[4,128,256]{2,1,0:T(8,128)(2,1)S(1)} collective-permute-done((bf16[4,128,256]{2,1,0:T(8,128)(2,1)S(1)}, bf16[4,128,256]{2,1,0:T(8,128)(2,1)S(1)}, u32[]{:S(2)}, u32[]{:S(2)}) %collective-permute-start.23) | collective-permute-done | bytes 262176 | tf_op jit(solution)/shard_map/ppermute | solution.py:621
  118.3 5.8 %attend.6 = bf16[4,144,256]{2,1,0:T(8,128)(2,1)S(1)} custom-call(s32[16]{0:T(128)S(1)} %select_n.42.first_ref, s32[256]{0:T(256)S(1)} %bitcast.24, bf16[2,4,256,128]{3,2,1,0:T(8,128)(2,1)S(1)} %get-tuple-element.98.refs_0_, bf16[2,4,256,128]{3,2,1,0:T(8,128)(2,1)S(1)} %collective-permute-done.18.refs_1_, ...), custom_call_target="tpu_custom_call" | custom-call | flops 1073741824 | bytes 2097152 | tf_op jit(solution)/shard_map/attend/pallas_call | solution.py:373
  124.1 2.3 %collective-permute-start.24 = (bf16[4,144,256]{2,1,0:T(8,128)(2,1)S(1)}, bf16[4,144,256]{2,1,0:T(8,128)(2,1)S(1)}, u32[]{:S(2)}, u32[]{:S(2)}) collective-permute-start(bf16[4,144,256]{2,1,0:T(8,128)(2,1)S(1)} %attend.6), channel_id=1, source_target_pairs={{0,4},{1,5},{2,6},{3,7},{4,0},{5,1},{6,2},{7,3},{8,12},{9,13},{10,... | collective-permute-start | bytes 884744 | tf_op jit(solution)/shard_map/ppermute | solution.py:652
  126.3 0.7 collective-permute-start.25
  127.1 9.6 %attend.7 = (f32[4,1,256]{2,1,0:T(1,128)S(1)}, f32[4,1,256]{2,1,0:T(1,128)S(1)}, f32[4,128,256]{2,1,0:T(8,128)S(1)}) custom-call(s32[16]{0:T(128)S(1)} %select_n.42.first_ref, s32[256]{0:T(256)S(1)} %bitcast.25, bf16[2,4,256,128]{3,2,1,0:T(8,128)(2,1)S(1)} %get-tuple-element.83.refs_0_, bf16[2,4,256,128]{3,2,1,0:T(8,128)(2,1)S(1)} %collective-permute-done.4.refs_1_, ...), custom_call_target="tpu_custom_call" | custom-call | flops 1073741824 | bytes 2097152 | tf_op jit(solution)/shard_map/attend/pallas_call | solution.py:373
  136.7 6.7 %attend.5 = (f32[4,1,256]{2,1,0:T(1,128)S(1)}, f32[4,1,256]{2,1,0:T(1,128)S(1)}, f32[4,128,256]{2,1,0:T(8,128)S(1)}) custom-call(s32[16]{0:T(128)S(1)} %select_n.42.first_ref, s32[256]{0:T(256)S(1)} %bitcast.26, bf16[2,4,256,128]{3,2,1,0:T(8,128)(2,1)S(1)} %get-tuple-element.83.refs_0_, bf16[2,4,256,128]{3,2,1,0:T(8,128)(2,1)S(1)} %collective-permute-done.4.refs_1_, ...), custom_call_target="tpu_custom_call" | custom-call | flops 1073741824 | bytes 2097152 | tf_op jit(solution)/shard_map/attend/pallas_call | solution.py:373
  143.4 4.2 %collective-permute-done.24.refs_3_ = bf16[4,144,256]{2,1,0:T(8,128)(2,1)S(1)} collective-permute-done((bf16[4,144,256]{2,1,0:T(8,128)(2,1)S(1)}, bf16[4,144,256]{2,1,0:T(8,128)(2,1)S(1)}, u32[]{:S(2)}, u32[]{:S(2)}) %collective-permute-start.24) | collective-permute-done | bytes 294944 | tf_op jit(solution)/shard_map/ppermute | solution.py:652
  147.6 3.3 %collective-permute-done.25.refs_7_ = bf16[4,144,256]{2,1,0:T(8,128)(2,1)S(1)} collective-permute-done((bf16[4,144,256]{2,1,0:T(8,128)(2,1)S(1)}, bf16[4,144,256]{2,1,0:T(8,128)(2,1)S(1)}, u32[]{:S(2)}, u32[]{:S(2)}) %collective-permute-start.25) | collective-permute-done | bytes 294944 | tf_op jit(solution)/shard_map/ppermute | solution.py:652
  150.9 0.4 merge.1.x_ref
  151.2 5.1 %project_out.2 = (f32[32,4096]{1,0:T(8,128)S(1)}, f32[32,4096]{1,0:T(8,128)S(1)}, f32[32,4096]{1,0:T(8,128)S(1)}, f32[32,4096]{1,0:T(8,128)S(1)}, f32[32,4096]{1...) custom-call(s32[8]{0:T(128)S(1)} %dynamic-slice_bitcast_fusion.place_ref, ...), custom_call_target="tpu_custom_call" | custom-call | flops 2147483648 | bytes 13107200 | tf_op jit(solution)/shard_map/project_out/pallas_call | solution.py:491
  156.6 4.6 %collective-permute-start.30 = (bf16[32,4096]{1,0:T(8,128)(2,1)S(1)}, bf16[32,4096]{1,0:T(8,128)(2,1)S(1)}, u32[]{:S(2)}, u32[]{:S(2)}) collective-permute-start(bf16[32,4096]{1,0:T(8,128)(2,1)S(1)} %convert_element_type.116), channel_id=1, source_target_pairs={{2,0},{4,2},{6,4},{7,6},{5,7},{3,5},{1,3},{0,1},{10,8},{12,10},{14... | collective-permute-start | bytes 786440 | tf_op jit(solution)/shard_map/ppermute | solution.py:669
  161.1 5.1 %project_out.3 = (f32[32,4096]{1,0:T(8,128)S(1)}, f32[32,4096]{1,0:T(8,128)S(1)}, f32[32,4096]{1,0:T(8,128)S(1)}, f32[32,4096]{1,0:T(8,128)S(1)}, f32[32,4096]{1...) custom-call(s32[8]{0:T(128)S(1)} %dynamic-slice_bitcast_fusion.place_ref, ...), custom_call_target="tpu_custom_call" | custom-call | flops 2147483648 | bytes 13107200 | tf_op jit(solution)/shard_map/project_out/pallas_call | solution.py:491
  166.4 2.1 %collective-permute-start.36 = (bf16[32,4096]{1,0:T(8,128)(2,1)S(1)}, bf16[32,4096]{1,0:T(8,128)(2,1)S(1)}, u32[]{:S(2)}, u32[]{:S(2)}) collective-permute-start(bf16[32,4096]{1,0:T(8,128)(2,1)S(1)} %get-tuple-element.128), channel_id=1, source_target_pairs={{2,0},{4,2},{6,4},{7,6},{5,7},{3,5},{1,3},{0,1},{10,8},{12,10},{14... | collective-permute-start | bytes 786440 | tf_op jit(solution)/shard_map/ppermute | solution.py:669
  168.6 2.1 %collective-permute-start.31 = (bf16[32,4096]{1,0:T(8,128)(2,1)S(1)}, bf16[32,4096]{1,0:T(8,128)(2,1)S(1)}, u32[]{:S(2)}, u32[]{:S(2)}) collective-permute-start(bf16[32,4096]{1,0:T(8,128)(2,1)S(1)} %add_convert_fusion.8), channel_id=1, source_target_pairs={{2,0},{4,2},{6,4},{7,6},{5,7},{3,5},{1,3},{0,1},{10,8},{12,10},{14... | collective-permute-start | bytes 786440 | tf_op jit(solution)/shard_map/ppermute | solution.py:669
  170.7 4.9 %collective-permute-done.33 = bf16[32,4096]{1,0:T(8,128)(2,1)S(1)} collective-permute-done((bf16[32,4096]{1,0:T(8,128)(2,1)S(1)}, bf16[32,4096]{1,0:T(8,128)(2,1)S(1)}, u32[]{:S(2)}, u32[]{:S(2)}) %collective-permute-start.33) | collective-permute-done | bytes 262176 | tf_op jit(solution)/shard_map/ppermute | solution.py:669
  175.8 2.1 %collective-permute-start.37 = (bf16[32,4096]{1,0:T(8,128)(2,1)S(1)}, bf16[32,4096]{1,0:T(8,128)(2,1)S(1)}, u32[]{:S(2)}, u32[]{:S(2)}) collective-permute-start(bf16[32,4096]{1,0:T(8,128)(2,1)S(1)} %add_convert_fusion.3), channel_id=1, source_target_pairs={{2,0},{4,2},{6,4},{7,6},{5,7},{3,5},{1,3},{0,1},{10,8},{12,10},{14... | collective-permute-start | bytes 786440 | tf_op jit(solution)/shard_map/ppermute | solution.py:669
  177.8 3.3 %collective-permute-done.27 = bf16[32,4096]{1,0:T(8,128)(2,1)S(1)} collective-permute-done((bf16[32,4096]{1,0:T(8,128)(2,1)S(1)}, bf16[32,4096]{1,0:T(8,128)(2,1)S(1)}, u32[]{:S(2)}, u32[]{:S(2)}) %collective-permute-start.27) | collective-permute-done | bytes 262176 | tf_op jit(solution)/shard_map/ppermute | solution.py:669
  181.4 2.1 %collective-permute-start.32 = (bf16[32,4096]{1,0:T(8,128)(2,1)S(1)}, bf16[32,4096]{1,0:T(8,128)(2,1)S(1)}, u32[]{:S(2)}, u32[]{:S(2)}) collective-permute-start(bf16[32,4096]{1,0:T(8,128)(2,1)S(1)} %add_convert_fusion.7), channel_id=1, source_target_pairs={{2,0},{4,2},{6,4},{7,6},{5,7},{3,5},{1,3},{0,1},{10,8},{12,10},{14... | collective-permute-start | bytes 786440 | tf_op jit(solution)/shard_map/ppermute | solution.py:669
  183.5 3.3 %collective-permute-done.34 = bf16[32,4096]{1,0:T(8,128)(2,1)S(1)} collective-permute-done((bf16[32,4096]{1,0:T(8,128)(2,1)S(1)}, bf16[32,4096]{1,0:T(8,128)(2,1)S(1)}, u32[]{:S(2)}, u32[]{:S(2)}) %collective-permute-start.34) | collective-permute-done | bytes 262176 | tf_op jit(solution)/shard_map/ppermute | solution.py:669
  187.0 2.1 %collective-permute-start.38 = (bf16[32,4096]{1,0:T(8,128)(2,1)S(1)}, bf16[32,4096]{1,0:T(8,128)(2,1)S(1)}, u32[]{:S(2)}, u32[]{:S(2)}) collective-permute-start(bf16[32,4096]{1,0:T(8,128)(2,1)S(1)} %add_convert_fusion.2), channel_id=1, source_target_pairs={{2,0},{4,2},{6,4},{7,6},{5,7},{3,5},{1,3},{0,1},{10,8},{12,10},{14... | collective-permute-start | bytes 786440 | tf_op jit(solution)/shard_map/ppermute | solution.py:669
  189.1 3.3 %collective-permute-done.28 = bf16[32,4096]{1,0:T(8,128)(2,1)S(1)} collective-permute-done((bf16[32,4096]{1,0:T(8,128)(2,1)S(1)}, bf16[32,4096]{1,0:T(8,128)(2,1)S(1)}, u32[]{:S(2)}, u32[]{:S(2)}) %collective-permute-start.28) | collective-permute-done | bytes 262176 | tf_op jit(solution)/shard_map/ppermute | solution.py:669
  192.5 4.3 %collective-permute-done.38 = bf16[32,4096]{1,0:T(8,128)(2,1)S(1)} collective-permute-done((bf16[32,4096]{1,0:T(8,128)(2,1)S(1)}, bf16[32,4096]{1,0:T(8,128)(2,1)S(1)}, u32[]{:S(2)}, u32[]{:S(2)}) %collective-permute-start.38) | collective-permute-done | bytes 262176 | tf_op jit(solution)/shard_map/ppermute | solution.py:669
  196.9 1.8 collective-permute-start.39
  198.7 3.7 %collective-permute-done.29 = bf16[32,4096]{1,0:T(8,128)(2,1)S(1)} collective-permute-done((bf16[32,4096]{1,0:T(8,128)(2,1)S(1)}, bf16[32,4096]{1,0:T(8,128)(2,1)S(1)}, u32[]{:S(2)}, u32[]{:S(2)}) %collective-permute-start.29) | collective-permute-done | bytes 262176 | tf_op jit(solution)/shard_map/ppermute | solution.py:669
  202.5 1.5 collective-permute-done.39
  204.1 0.8 pad_maximum_fusion
  (79 shorter events, 3.3 us)
Async XLA Ops:
  2.5 10.7 %copy-start = (s32[1,256]{1,0:T(1,128)S(1)}, s32[1,256]{1,0:T(1,128)}, u32[]{:S(2)}) copy-start(s32[1,256]{1,0:T(1,128)} %param.18) | copy-start | bytes 3076
  2.5 10.7 %copy-start.1 = (s32[1,4]{1,0:T(1,128)S(1)}, s32[1,4]{1,0:T(1,128)}, u32[]{:S(2)}) copy-start(s32[1,4]{1,0:T(1,128)} %param.17) | copy-start | bytes 52
  2.5 13.1 %copy-start.2 = (s32[4]{0:T(128)S(1)}, s32[4]{0:T(128)}, u32[]{:S(2)}) copy-start(s32[4]{0:T(128)} %param.16) | copy-start | bytes 52
  8.0 32.3 %collective-permute-start.3 = (bf16[4,2,256,1024]{3,2,1,0:T(8,128)(2,1)}, bf16[4,2,256,1024]{3,2,1,0:T(8,128)(2,1)}, u32[]{:S(2)}, u32[]{:S(2)}) collective-permute-start(bf16[4,2,256,1024]{3,2,1,0:T(8,128)(2,1)} %bitcast.20.refs_0_), channel_id=1, source_target_pairs={{8,0},{0,8},{9,1},{1,9},{10,2},{2,10},{11,3},{3,11},{12,4},{4,12},... | collective-permute-start | bytes 12582920 | tf_op jit(solution)/shard_map/ppermute | solution.py:581
  8.5 9.7 %collective-permute-start = (bf16[32,4096]{1,0:T(8,128)(2,1)S(1)}, bf16[32,4096]{1,0:T(8,128)(2,1)S(1)}, u32[]{:S(2)}, u32[]{:S(2)}) collective-permute-start(bf16[32,4096]{1,0:T(8,128)(2,1)S(1)} %get-tuple-element.130.refs_0_), channel_id=1, source_target_pairs={{0,2},{2,4},{4,6},{6,7},{7,5},{5,3},{3,1},{1,0},{8,10},{10,12},{12... | collective-permute-start | bytes 786440 | tf_op jit(solution)/shard_map/ppermute | solution.py:572
  11.1 15.9 %collective-permute-start.14 = (bf16[32,4096]{1,0:T(8,128)(2,1)S(1)}, bf16[32,4096]{1,0:T(8,128)(2,1)S(1)}, u32[]{:S(2)}, u32[]{:S(2)}) collective-permute-start(bf16[32,4096]{1,0:T(8,128)(2,1)S(1)} %get-tuple-element.130.refs_0_), channel_id=1, source_target_pairs={{2,0},{4,2},{6,4},{7,6},{5,7},{3,5},{1,3},{0,1},{10,8},{12,10},{14... | collective-permute-start | bytes 786440 | tf_op jit(solution)/shard_map/ppermute | solution.py:574
  11.1 14.0 %collective-permute-start.8 = (bf16[32,4096]{1,0:T(8,128)(2,1)S(1)}, bf16[32,4096]{1,0:T(8,128)(2,1)S(1)}, u32[]{:S(2)}, u32[]{:S(2)}) collective-permute-start(bf16[32,4096]{1,0:T(8,128)(2,1)S(1)} %get-tuple-element.129.refs_0_), channel_id=1, source_target_pairs={{2,0},{4,2},{6,4},{7,6},{5,7},{3,5},{1,3},{0,1},{10,8},{12,10},{14... | collective-permute-start | bytes 786440 | tf_op jit(solution)/shard_map/ppermute | solution.py:574
  13.1 18.6 %collective-permute-start.7 = (bf16[32,4096]{1,0:T(8,128)(2,1)S(1)}, bf16[32,4096]{1,0:T(8,128)(2,1)S(1)}, u32[]{:S(2)}, u32[]{:S(2)}) collective-permute-start(bf16[32,4096]{1,0:T(8,128)(2,1)S(1)} %get-tuple-element.129.refs_0_), channel_id=1, source_target_pairs={{0,2},{2,4},{4,6},{6,7},{7,5},{5,3},{3,1},{1,0},{8,10},{10,12},{12... | collective-permute-start | bytes 786440 | tf_op jit(solution)/shard_map/ppermute | solution.py:572
  18.2 11.1 %collective-permute-start.1 = (bf16[32,4096]{1,0:T(8,128)(2,1)S(1)}, bf16[32,4096]{1,0:T(8,128)(2,1)S(1)}, u32[]{:S(2)}, u32[]{:S(2)}) collective-permute-start(bf16[32,4096]{1,0:T(8,128)(2,1)S(1)} %collective-permute-done.refs_1_), channel_id=1, source_target_pairs={{0,2},{2,4},{4,6},{6,7},{7,5},{5,3},{3,1},{1,0},{8,10},{10,12},{12... | collective-permute-start | bytes 786440 | tf_op jit(solution)/shard_map/ppermute | solution.py:572
  25.2 9.2 %collective-permute-start.10 = (bf16[32,4096]{1,0:T(8,128)(2,1)S(1)}, bf16[32,4096]{1,0:T(8,128)(2,1)S(1)}, u32[]{:S(2)}, u32[]{:S(2)}) collective-permute-start(bf16[32,4096]{1,0:T(8,128)(2,1)S(1)} %collective-permute-done.8.refs_2_), channel_id=1, source_target_pairs={{2,0},{4,2},{6,4},{7,6},{5,7},{3,5},{1,3},{0,1},{10,8},{12,10},{14... | collective-permute-start | bytes 786440 | tf_op jit(solution)/shard_map/ppermute | solution.py:574
  27.0 13.0 %collective-permute-start.15 = (bf16[32,4096]{1,0:T(8,128)(2,1)S(1)}, bf16[32,4096]{1,0:T(8,128)(2,1)S(1)}, u32[]{:S(2)}, u32[]{:S(2)}) collective-permute-start(bf16[32,4096]{1,0:T(8,128)(2,1)S(1)} %collective-permute-done.14.refs_2_), channel_id=1, source_target_pairs={{2,0},{4,2},{6,4},{7,6},{5,7},{3,5},{1,3},{0,1},{10,8},{12,10},{14... | collective-permute-start | bytes 786440 | tf_op jit(solution)/shard_map/ppermute | solution.py:574
  29.9 13.7 %collective-permute-start.2 = (bf16[32,4096]{1,0:T(8,128)(2,1)S(1)}, bf16[32,4096]{1,0:T(8,128)(2,1)S(1)}, u32[]{:S(2)}, u32[]{:S(2)}) collective-permute-start(bf16[32,4096]{1,0:T(8,128)(2,1)S(1)} %collective-permute-done.1.refs_3_), channel_id=1, source_target_pairs={{0,2},{2,4},{4,6},{6,7},{7,5},{5,3},{3,1},{1,0},{8,10},{10,12},{12... | collective-permute-start | bytes 786440 | tf_op jit(solution)/shard_map/ppermute | solution.py:572
  31.8 13.9 %collective-permute-start.9 = (bf16[32,4096]{1,0:T(8,128)(2,1)S(1)}, bf16[32,4096]{1,0:T(8,128)(2,1)S(1)}, u32[]{:S(2)}, u32[]{:S(2)}) collective-permute-start(bf16[32,4096]{1,0:T(8,128)(2,1)S(1)} %collective-permute-done.7.refs_1_), channel_id=1, source_target_pairs={{0,2},{2,4},{4,6},{6,7},{7,5},{5,3},{3,1},{1,0},{8,10},{10,12},{12... | collective-permute-start | bytes 786440 | tf_op jit(solution)/shard_map/ppermute | solution.py:572
  34.4 13.0 %collective-permute-start.12 = (bf16[32,4096]{1,0:T(8,128)(2,1)S(1)}, bf16[32,4096]{1,0:T(8,128)(2,1)S(1)}, u32[]{:S(2)}, u32[]{:S(2)}) collective-permute-start(bf16[32,4096]{1,0:T(8,128)(2,1)S(1)} %collective-permute-done.10.refs_4_), channel_id=1, source_target_pairs={{2,0},{4,2},{6,4},{7,6},{5,7},{3,5},{1,3},{0,1},{10,8},{12,10},{14... | collective-permute-start | bytes 786440 | tf_op jit(solution)/shard_map/ppermute | solution.py:574
  40.1 11.2 %collective-permute-start.16 = (bf16[32,4096]{1,0:T(8,128)(2,1)S(1)}, bf16[32,4096]{1,0:T(8,128)(2,1)S(1)}, u32[]{:S(2)}, u32[]{:S(2)}) collective-permute-start(bf16[32,4096]{1,0:T(8,128)(2,1)S(1)} %collective-permute-done.15.refs_4_), channel_id=1, source_target_pairs={{2,0},{4,2},{6,4},{7,6},{5,7},{3,5},{1,3},{0,1},{10,8},{12,10},{14... | collective-permute-start | bytes 786440 | tf_op jit(solution)/shard_map/ppermute | solution.py:574
  43.6 9.3 %collective-permute-start.17 = (bf16[32,4096]{1,0:T(8,128)(2,1)S(1)}, bf16[32,4096]{1,0:T(8,128)(2,1)S(1)}, u32[]{:S(2)}, u32[]{:S(2)}) collective-permute-start(bf16[32,4096]{1,0:T(8,128)(2,1)S(1)} %collective-permute-done.2.refs_5_), channel_id=1, source_target_pairs={{0,2},{2,4},{4,6},{6,7},{7,5},{5,3},{3,1},{1,0},{8,10},{10,12},{12... | collective-permute-start | bytes 786440 | tf_op jit(solution)/shard_map/ppermute | solution.py:572
  45.4 27.3 %collective-permute-start.18 = (bf16[2,4,256,128]{3,2,1,0:T(8,128)(2,1)S(1)}, bf16[2,4,256,128]{3,2,1,0:T(8,128)(2,1)S(1)}, u32[]{:S(2)}, u32[]{:S(2)}) collective-permute-start(bf16[2,4,256,128]{3,2,1,0:T(8,128)(2,1)S(1)} %get-tuple-element.96), channel_id=1, source_target_pairs={{0,1},{1,0},{2,3},{3,2},{4,5},{5,4},{6,7},{7,6},{8,9},{9,8},{10,11... | collective-permute-start | bytes 1572872 | tf_op jit(solution)/shard_map/ppermute | solution.py:609
  45.7 20.5 %collective-permute-start.11 = (bf16[32,4096]{1,0:T(8,128)(2,1)S(1)}, bf16[32,4096]{1,0:T(8,128)(2,1)S(1)}, u32[]{:S(2)}, u32[]{:S(2)}) collective-permute-start(bf16[32,4096]{1,0:T(8,128)(2,1)S(1)} %collective-permute-done.9.refs_3_), channel_id=1, source_target_pairs={{0,2},{2,4},{4,6},{6,7},{7,5},{5,3},{3,1},{1,0},{8,10},{10,12},{12... | collective-permute-start | bytes 786440 | tf_op jit(solution)/shard_map/ppermute | solution.py:572
  47.4 18.8 %collective-permute-start.13 = (bf16[32,4096]{1,0:T(8,128)(2,1)S(1)}, bf16[32,4096]{1,0:T(8,128)(2,1)S(1)}, u32[]{:S(2)}, u32[]{:S(2)}) collective-permute-start(bf16[32,4096]{1,0:T(8,128)(2,1)S(1)} %collective-permute-done.12.refs_6_), channel_id=1, source_target_pairs={{2,0},{4,2},{6,4},{7,6},{5,7},{3,5},{1,3},{0,1},{10,8},{12,10},{14... | collective-permute-start | bytes 786440 | tf_op jit(solution)/shard_map/ppermute | solution.py:574
  51.3 27.4 %collective-permute-start.19 = (bf16[2,4,256,128]{3,2,1,0:T(8,128)(2,1)S(1)}, bf16[2,4,256,128]{3,2,1,0:T(8,128)(2,1)S(1)}, u32[]{:S(2)}, u32[]{:S(2)}) collective-permute-start(bf16[2,4,256,128]{3,2,1,0:T(8,128)(2,1)S(1)} %get-tuple-element.100), channel_id=1, source_target_pairs={{0,2},{1,3},{2,0},{3,1},{4,6},{5,7},{6,4},{7,5},{8,10},{9,11},{10,... | collective-permute-start | bytes 1572872 | tf_op jit(solution)/shard_map/ppermute | solution.py:609
  72.7 17.8 %collective-permute-start.21 = (bf16[6,128,256]{2,1,0:T(8,128)(2,1)S(1)}, bf16[6,128,256]{2,1,0:T(8,128)(2,1)S(1)}, u32[]{:S(2)}, u32[]{:S(2)}) collective-permute-start(bf16[6,128,256]{2,1,0:T(8,128)(2,1)S(1)} %get-tuple-element.102.here_ref.refs_6_), channel_id=1, source_target_pairs={{0,4},{1,5},{2,6},{3,7},{4,0},{5,1},{6,2},{7,3},{8,12},{9,13},{10,... | collective-permute-start | bytes 1179656 | tf_op jit(solution)/shard_map/ppermute | solution.py:621
  72.8 31.9 %collective-permute-start.20 = (bf16[2,4,256,128]{3,2,1,0:T(8,128)(2,1)S(1)}, bf16[2,4,256,128]{3,2,1,0:T(8,128)(2,1)S(1)}, u32[]{:S(2)}, u32[]{:S(2)}) collective-permute-start(bf16[2,4,256,128]{3,2,1,0:T(8,128)(2,1)S(1)} %get-tuple-element.101), channel_id=1, source_target_pairs={{0,3},{1,2},{2,1},{3,0},{4,7},{5,6},{6,5},{7,4},{8,11},{9,10},{10,... | collective-permute-start | bytes 1572872 | tf_op jit(solution)/shard_map/ppermute | solution.py:609
  77.9 49.1 %collective-permute-start.4 = (bf16[2,4,256,128]{3,2,1,0:T(8,128)(2,1)S(1)}, bf16[2,4,256,128]{3,2,1,0:T(8,128)(2,1)S(1)}, u32[]{:S(2)}, u32[]{:S(2)}) collective-permute-start(bf16[2,4,256,128]{3,2,1,0:T(8,128)(2,1)S(1)} %get-tuple-element.84), channel_id=1, source_target_pairs={{0,1},{1,0},{2,3},{3,2},{4,5},{5,4},{6,7},{7,6},{8,9},{9,8},{10,11... | collective-permute-start | bytes 1572872 | tf_op jit(solution)/shard_map/ppermute | solution.py:609
  78.7 48.4 %collective-permute-start.5 = (bf16[2,4,256,128]{3,2,1,0:T(8,128)(2,1)S(1)}, bf16[2,4,256,128]{3,2,1,0:T(8,128)(2,1)S(1)}, u32[]{:S(2)}, u32[]{:S(2)}) collective-permute-start(bf16[2,4,256,128]{3,2,1,0:T(8,128)(2,1)S(1)} %get-tuple-element.85), channel_id=1, source_target_pairs={{0,2},{1,3},{2,0},{3,1},{4,6},{5,7},{6,4},{7,5},{8,10},{9,11},{10,... | collective-permute-start | bytes 1572872 | tf_op jit(solution)/shard_map/ppermute | solution.py:609
  78.7 48.3 %collective-permute-start.6 = (bf16[2,4,256,128]{3,2,1,0:T(8,128)(2,1)S(1)}, bf16[2,4,256,128]{3,2,1,0:T(8,128)(2,1)S(1)}, u32[]{:S(2)}, u32[]{:S(2)}) collective-permute-start(bf16[2,4,256,128]{3,2,1,0:T(8,128)(2,1)S(1)} %get-tuple-element.86), channel_id=1, source_target_pairs={{0,3},{1,2},{2,1},{3,0},{4,7},{5,6},{6,5},{7,4},{8,11},{9,10},{10,... | collective-permute-start | bytes 1572872 | tf_op jit(solution)/shard_map/ppermute | solution.py:609
  90.5 27.7 %collective-permute-start.23 = (bf16[4,128,256]{2,1,0:T(8,128)(2,1)S(1)}, bf16[4,128,256]{2,1,0:T(8,128)(2,1)S(1)}, u32[]{:S(2)}, u32[]{:S(2)}) collective-permute-start(bf16[4,128,256]{2,1,0:T(8,128)(2,1)S(1)} %get-tuple-element.97.refs_6_), channel_id=1, source_target_pairs={{0,4},{1,5},{2,6},{3,7},{4,0},{5,1},{6,2},{7,3},{8,12},{9,13},{10,... | collective-permute-start | bytes 786440 | tf_op jit(solution)/shard_map/ppermute | solution.py:621
  104.7 13.6 %collective-permute-start.22 = (bf16[256,256]{1,0:T(8,128)(2,1)S(1)}, bf16[256,256]{1,0:T(8,128)(2,1)S(1)}, u32[]{:S(2)}, u32[]{:S(2)}) collective-permute-start(bf16[256,256]{1,0:T(8,128)(2,1)S(1)} %pick_new.1), channel_id=1, source_target_pairs={{0,0},{1,2},{2,4},{3,6},{4,1},{5,3},{6,5},{7,7},{8,8},{9,10},{10,1... | collective-permute-start | bytes 393224 | tf_op jit(solution)/shard_map/ppermute | solution.py:624
  124.1 23.6 %collective-permute-start.24 = (bf16[4,144,256]{2,1,0:T(8,128)(2,1)S(1)}, bf16[4,144,256]{2,1,0:T(8,128)(2,1)S(1)}, u32[]{:S(2)}, u32[]{:S(2)}) collective-permute-start(bf16[4,144,256]{2,1,0:T(8,128)(2,1)S(1)} %attend.6), channel_id=1, source_target_pairs={{0,4},{1,5},{2,6},{3,7},{4,0},{5,1},{6,2},{7,3},{8,12},{9,13},{10,... | collective-permute-start | bytes 884744 | tf_op jit(solution)/shard_map/ppermute | solution.py:652
  126.3 24.5 %collective-permute-start.25 = (bf16[4,144,256]{2,1,0:T(8,128)(2,1)S(1)}, bf16[4,144,256]{2,1,0:T(8,128)(2,1)S(1)}, u32[]{:S(2)}, u32[]{:S(2)}) collective-permute-start(bf16[4,144,256]{2,1,0:T(8,128)(2,1)S(1)} %attend.4), channel_id=1, source_target_pairs={{0,4},{1,5},{2,6},{3,7},{4,0},{5,1},{6,2},{7,3},{8,12},{9,13},{10,... | collective-permute-start | bytes 884744 | tf_op jit(solution)/shard_map/ppermute | solution.py:652
  156.4 12.1 %collective-permute-start.26 = (bf16[32,4096]{1,0:T(8,128)(2,1)S(1)}, bf16[32,4096]{1,0:T(8,128)(2,1)S(1)}, u32[]{:S(2)}, u32[]{:S(2)}) collective-permute-start(bf16[32,4096]{1,0:T(8,128)(2,1)S(1)} %get-tuple-element.117), channel_id=1, source_target_pairs={{0,2},{2,4},{4,6},{6,7},{7,5},{5,3},{3,1},{1,0},{8,10},{10,12},{12... | collective-permute-start | bytes 786440 | tf_op jit(solution)/shard_map/ppermute | solution.py:669
  156.6 12.0 %collective-permute-start.30 = (bf16[32,4096]{1,0:T(8,128)(2,1)S(1)}, bf16[32,4096]{1,0:T(8,128)(2,1)S(1)}, u32[]{:S(2)}, u32[]{:S(2)}) collective-permute-start(bf16[32,4096]{1,0:T(8,128)(2,1)S(1)} %convert_element_type.116), channel_id=1, source_target_pairs={{2,0},{4,2},{6,4},{7,6},{5,7},{3,5},{1,3},{0,1},{10,8},{12,10},{14... | collective-permute-start | bytes 786440 | tf_op jit(solution)/shard_map/ppermute | solution.py:669
  166.3 9.3 %collective-permute-start.33 = (bf16[32,4096]{1,0:T(8,128)(2,1)S(1)}, bf16[32,4096]{1,0:T(8,128)(2,1)S(1)}, u32[]{:S(2)}, u32[]{:S(2)}) collective-permute-start(bf16[32,4096]{1,0:T(8,128)(2,1)S(1)} %convert_element_type.123), channel_id=1, source_target_pairs={{0,2},{2,4},{4,6},{6,7},{7,5},{5,3},{3,1},{1,0},{8,10},{10,12},{12... | collective-permute-start | bytes 786440 | tf_op jit(solution)/shard_map/ppermute | solution.py:669
  166.4 9.3 %collective-permute-start.36 = (bf16[32,4096]{1,0:T(8,128)(2,1)S(1)}, bf16[32,4096]{1,0:T(8,128)(2,1)S(1)}, u32[]{:S(2)}, u32[]{:S(2)}) collective-permute-start(bf16[32,4096]{1,0:T(8,128)(2,1)S(1)} %get-tuple-element.128), channel_id=1, source_target_pairs={{2,0},{4,2},{6,4},{7,6},{5,7},{3,5},{1,3},{0,1},{10,8},{12,10},{14... | collective-permute-start | bytes 786440 | tf_op jit(solution)/shard_map/ppermute | solution.py:669
  168.5 12.7 %collective-permute-start.27 = (bf16[32,4096]{1,0:T(8,128)(2,1)S(1)}, bf16[32,4096]{1,0:T(8,128)(2,1)S(1)}, u32[]{:S(2)}, u32[]{:S(2)}) collective-permute-start(bf16[32,4096]{1,0:T(8,128)(2,1)S(1)} %add_convert_fusion.11), channel_id=1, source_target_pairs={{0,2},{2,4},{4,6},{6,7},{7,5},{5,3},{3,1},{1,0},{8,10},{10,12},{12... | collective-permute-start | bytes 786440 | tf_op jit(solution)/shard_map/ppermute | solution.py:669
  168.6 12.7 %collective-permute-start.31 = (bf16[32,4096]{1,0:T(8,128)(2,1)S(1)}, bf16[32,4096]{1,0:T(8,128)(2,1)S(1)}, u32[]{:S(2)}, u32[]{:S(2)}) collective-permute-start(bf16[32,4096]{1,0:T(8,128)(2,1)S(1)} %add_convert_fusion.8), channel_id=1, source_target_pairs={{2,0},{4,2},{6,4},{7,6},{5,7},{3,5},{1,3},{0,1},{10,8},{12,10},{14... | collective-permute-start | bytes 786440 | tf_op jit(solution)/shard_map/ppermute | solution.py:669
  175.6 11.2 %collective-permute-start.34 = (bf16[32,4096]{1,0:T(8,128)(2,1)S(1)}, bf16[32,4096]{1,0:T(8,128)(2,1)S(1)}, u32[]{:S(2)}, u32[]{:S(2)}) collective-permute-start(bf16[32,4096]{1,0:T(8,128)(2,1)S(1)} %add_convert_fusion.5), channel_id=1, source_target_pairs={{0,2},{2,4},{4,6},{6,7},{7,5},{5,3},{3,1},{1,0},{8,10},{10,12},{12... | collective-permute-start | bytes 786440 | tf_op jit(solution)/shard_map/ppermute | solution.py:669
  175.8 11.2 %collective-permute-start.37 = (bf16[32,4096]{1,0:T(8,128)(2,1)S(1)}, bf16[32,4096]{1,0:T(8,128)(2,1)S(1)}, u32[]{:S(2)}, u32[]{:S(2)}) collective-permute-start(bf16[32,4096]{1,0:T(8,128)(2,1)S(1)} %add_convert_fusion.3), channel_id=1, source_target_pairs={{2,0},{4,2},{6,4},{7,6},{5,7},{3,5},{1,3},{0,1},{10,8},{12,10},{14... | collective-permute-start | bytes 786440 | tf_op jit(solution)/shard_map/ppermute | solution.py:669
  181.2 11.2 %collective-permute-start.28 = (bf16[32,4096]{1,0:T(8,128)(2,1)S(1)}, bf16[32,4096]{1,0:T(8,128)(2,1)S(1)}, u32[]{:S(2)}, u32[]{:S(2)}) collective-permute-start(bf16[32,4096]{1,0:T(8,128)(2,1)S(1)} %add_convert_fusion.10), channel_id=1, source_target_pairs={{0,2},{2,4},{4,6},{6,7},{7,5},{5,3},{3,1},{1,0},{8,10},{10,12},{12... | collective-permute-start | bytes 786440 | tf_op jit(solution)/shard_map/ppermute | solution.py:669
  181.4 17.3 %collective-permute-start.32 = (bf16[32,4096]{1,0:T(8,128)(2,1)S(1)}, bf16[32,4096]{1,0:T(8,128)(2,1)S(1)}, u32[]{:S(2)}, u32[]{:S(2)}) collective-permute-start(bf16[32,4096]{1,0:T(8,128)(2,1)S(1)} %add_convert_fusion.7), channel_id=1, source_target_pairs={{2,0},{4,2},{6,4},{7,6},{5,7},{3,5},{1,3},{0,1},{10,8},{12,10},{14... | collective-permute-start | bytes 786440 | tf_op jit(solution)/shard_map/ppermute | solution.py:669
  186.9 15.6 %collective-permute-start.35 = (bf16[32,4096]{1,0:T(8,128)(2,1)S(1)}, bf16[32,4096]{1,0:T(8,128)(2,1)S(1)}, u32[]{:S(2)}, u32[]{:S(2)}) collective-permute-start(bf16[32,4096]{1,0:T(8,128)(2,1)S(1)} %add_convert_fusion.4), channel_id=1, source_target_pairs={{0,2},{2,4},{4,6},{6,7},{7,5},{5,3},{3,1},{1,0},{8,10},{10,12},{12... | collective-permute-start | bytes 786440 | tf_op jit(solution)/shard_map/ppermute | solution.py:669
  187.0 9.9 %collective-permute-start.38 = (bf16[32,4096]{1,0:T(8,128)(2,1)S(1)}, bf16[32,4096]{1,0:T(8,128)(2,1)S(1)}, u32[]{:S(2)}, u32[]{:S(2)}) collective-permute-start(bf16[32,4096]{1,0:T(8,128)(2,1)S(1)} %add_convert_fusion.2), channel_id=1, source_target_pairs={{2,0},{4,2},{6,4},{7,6},{5,7},{3,5},{1,3},{0,1},{10,8},{12,10},{14... | collective-permute-start | bytes 786440 | tf_op jit(solution)/shard_map/ppermute | solution.py:669
  192.5 9.9 %collective-permute-start.29 = (bf16[32,4096]{1,0:T(8,128)(2,1)S(1)}, bf16[32,4096]{1,0:T(8,128)(2,1)S(1)}, u32[]{:S(2)}, u32[]{:S(2)}) collective-permute-start(bf16[32,4096]{1,0:T(8,128)(2,1)S(1)} %add_convert_fusion.9), channel_id=1, source_target_pairs={{0,2},{2,4},{4,6},{6,7},{7,5},{5,3},{3,1},{1,0},{8,10},{10,12},{12... | collective-permute-start | bytes 786440 | tf_op jit(solution)/shard_map/ppermute | solution.py:669
  196.9 7.1 %collective-permute-start.39 = (bf16[32,4096]{1,0:T(8,128)(2,1)S(1)}, bf16[32,4096]{1,0:T(8,128)(2,1)S(1)}, u32[]{:S(2)}, u32[]{:S(2)}) collective-permute-start(bf16[32,4096]{1,0:T(8,128)(2,1)S(1)} %add_convert_fusion.1), channel_id=1, source_target_pairs={{2,0},{4,2},{6,4},{7,6},{5,7},{3,5},{1,3},{0,1},{10,8},{12,10},{14... | collective-permute-start | bytes 786440 | tf_op jit(solution)/shard_map/ppermute | solution.py:669

commit v8 on v7

--- a/solution.py
+++ b/solution.py
@@ -192,40 +192,39 @@
 
 def select_kernel(n_dest, n_src, place_ref, slot_ref, head_ref, *refs):
     sources = refs[:n_src]
-    outs = refs[n_src : n_src + n_dest]
-    sems = refs[n_src + n_dest]
+    outs = refs[n_src:-1]
+    sems = refs[-1]
+    targets = [out.at[dest] for out in outs for dest in range(n_dest)]
     for doc in range(DOCS):
         for src in range(n_src):
 
             @pl.when(place_ref[doc] == src)
             def _():
-                for dest in range(n_dest):
-                    cols = pl.ds(pl.multiple_of(head_ref[dest] * HD, HD), HD)
+                for i, target in enumerate(targets):
+                    cols = pl.ds(pl.multiple_of(head_ref[i] * HD, HD), HD)
                     pltpu.make_async_copy(
-                        sources[src].at[slot_ref[doc], :, :, cols],
-                        outs[dest].at[:, doc],
-                        sems.at[dest, doc],
+                        sources[src].at[slot_ref[doc], :, :, cols], target.at[:, doc], sems.at[i, doc]
                     ).start()
 
-    for dest in range(n_dest):
+    for i, target in enumerate(targets):
         for doc in range(DOCS):
             pltpu.make_async_copy(
-                sources[0].at[0, :, :, 0:HD], outs[dest].at[:, doc], sems.at[dest, doc]
+                sources[0].at[0, :, :, 0:HD], target.at[:, doc], sems.at[i, doc]
             ).wait()
 
 
 def select_docs(sources, place, slot, heads, n_dest):
     tokens = sources[0].shape[2]
-    shape = (2, DOCS, tokens, HD)
+    shape = (n_dest, 2, DOCS, tokens, HD)
     smem = pl.BlockSpec(memory_space=pltpu.SMEM)
     return pl.pallas_call(
         functools.partial(select_kernel, n_dest, len(sources)),
         in_specs=[smem] * 3 + [pl.BlockSpec(memory_space=pl.ANY)] * len(sources),
-        out_specs=[pl.BlockSpec(memory_space=pltpu.VMEM)] * n_dest,
-        out_shape=[jax.ShapeDtypeStruct(shape, jnp.bfloat16)] * n_dest,
-        scratch_shapes=[pltpu.SemaphoreType.DMA((n_dest, DOCS))],
+        out_specs=[pl.BlockSpec(memory_space=pltpu.VMEM)] * 2,
+        out_shape=[jax.ShapeDtypeStruct(shape, jnp.bfloat16)] * 2,
+        scratch_shapes=[pltpu.SemaphoreType.DMA((2 * n_dest, DOCS))],
         compiler_params=megabytes(8),
-        cost_estimate=cost(0, 4 * n_dest * math.prod(shape)),
+        cost_estimate=cost(0, 8 * math.prod(shape)),
         name="select_docs",
     )(place, slot, heads, *sources)
 
@@ -241,8 +240,7 @@
 def attend_kernel(n_chunks, with_new, n_tiles, tile_q, first_tile, first_ref, pos_ref, *refs):
     refs = list(refs)
     take = lambda count: [refs.pop(0) for _ in range(count)]
-    chunks = take(n_chunks)
-    dead_ref, qpos_ref, queries = take(3)
+    chunks, dead_ref, qpos_ref, queries = take(4)
     if with_new:
         cos_ref, sin_ref, new_ref = take(3)
     if with_new:
@@ -251,12 +249,12 @@
         packed, top, total, summed, values = take(5)
     together = min(PAIR, n_tiles)
     n_pairs = n_tiles // together
-    tokens = chunks[0].shape[2]
+    tokens = chunks.shape[3]
     scale = math.log2(math.e) / math.sqrt(HD)
 
     for chunk in range(n_chunks):
         for doc in range(DOCS):
-            values[doc, :, chunk * tokens : (chunk + 1) * tokens] = chunks[chunk][1, doc].T
+            values[doc, :, chunk * tokens : (chunk + 1) * tokens] = chunks[chunk, 1, doc].T
     if with_new:
         new_key[...] = rotate(
             new_ref[:, :HD].astype(jnp.float32), cos_ref[...], sin_ref[...]
@@ -317,7 +315,7 @@
                     for chunk in range(n_chunks):
                         span = slice(chunk * tokens, (chunk + 1) * tokens)
                         keys = jnp.concatenate(
-                            [chunks[chunk][0, doc], dead_ref[doc, span, :]], axis=1
+                            [chunks[chunk, 0, doc], dead_ref[doc, span, :]], axis=1
                         )
                         scores = jnp.dot(keys, extended, preferred_element_type=jnp.float32)
                         if masked:
@@ -354,12 +352,11 @@
 
 
 def attend(chunks, dead, first_pos, selected, q_pos, queries, first_tile, n_tiles, fresh):
-    n_chunks = len(chunks)
-    tokens = chunks[0].shape[2]
+    n_chunks, tokens = chunks.shape[0], chunks.shape[3]
     tile_q = SEL // q_pos.shape[0]
     smem = pl.BlockSpec(memory_space=pltpu.SMEM)
     vmem = pl.BlockSpec(memory_space=pltpu.VMEM)
-    operands = [first_pos, selected, *chunks, dead, q_pos, queries, *fresh]
+    operands = [first_pos, selected, chunks, dead, q_pos, queries, *fresh]
     state = [((n_tiles, 1, TILE_COLS), jnp.float32)] * 2
     state += [((n_tiles, HD, TILE_COLS), jnp.float32)]
     values = ((DOCS, HD, n_chunks * tokens), jnp.bfloat16)
@@ -542,9 +539,9 @@
         pltpu.with_memory_space_constraint(w, pltpu.HBM) for w in (w_query, w_keyval, w_out)
     )
     middle = tp_size // 2
-    order = jnp.arange(middle, dtype=jnp.int32)
+    mates = me // middle * middle + jnp.arange(middle, dtype=jnp.int32)
     offsets = jnp.cumsum(lengths) - lengths
-    first_slot = (me ^ order) * tokens
+    first_slot = mates * tokens
     slot_tokens = first_slot[:, None] + jnp.arange(tokens, dtype=jnp.int32)[None, :]
     cache_pos = offsets[:, None, None] + slot_tokens[None]
     is_valid = slot_tokens[None] < lengths[:, None, None]
@@ -582,7 +579,7 @@
             holder = (doc_slot // slots - lax.axis_index("req")) % req_size
             slot = doc_slot % slots
             side = (me < middle).astype(jnp.int32)[None]
-            takers = jnp.concatenate([me ^ order, me ^ order ^ middle]) * KVH // tp_size
+            takers = jnp.concatenate([mates, mates ^ middle]) * KVH // tp_size
         if k == 2:
             first[-1], dead, first_pos, cosine, sine_part, q_pos, takers, holder, slot, place, side = (
                 lax.optimization_barrier(
@@ -591,7 +588,7 @@
                 )
             )
         if k == far - 1:
-            sent = select_docs(sources, holder, slot, takers, tp_size)
+            sent = select_docs(sources, holder, slot, takers, middle)
             first[-1], *sent = lax.optimization_barrier((first[-1], *sent))
     projected = None
     for chunk, held in enumerate(streams):
@@ -604,16 +601,15 @@
         projected = project(
             place, blocks, w_query, w_keyval, projected, (cosine, sine_part), chunk
         )
-    chunks = [
-        [
-            lax.ppermute(sent[slot * middle + j], "tp", [(i, i ^ j) for i in range(tp_size)])
-            if j
-            else sent[slot * middle]
-            for j in range(middle)
-        ]
-        for slot in range(2)
-    ]
-    *queries, chunks[1][1] = lax.optimization_barrier((*projected[:HALVES], chunks[1][1]))
+    halves = [list(range(middle)), list(range(middle, tp_size))]
+
+    def exchange(keys):
+        return lax.all_to_all(keys, "tp", 0, 0, axis_index_groups=halves, tiled=True)
+
+    theirs_kv = exchange(sent[1])
+    mine_kv, theirs_kv = lax.optimization_barrier((sent[0], theirs_kv))
+    chunks = [exchange(mine_kv), theirs_kv]
+    queries = projected[:HALVES]
     n_tiles = queries[0].shape[0]
     across = [(i, i ^ middle) for i in range(tp_size)]
     their_queries = [None] * HALVES

time: 205 us -> 259 us (1.26)
  blocking collectives: 0 us -> 27.2 us
  waiting for transfers between devices: 83.7 us -> 105 us
  local copies, waits for them, and re-layouts: 7.6 us -> 14.4 us
  starting transfers between devices: 48.4 us -> 44 us
  Pallas kernels: 57.6 us -> 60.3 us
    ppermute x7, waiting for transfers between devices: 14.2 us -> 50.3 us  [per_device(): held['behind'].append(lax.ppermute(held['behind'][-1], 'tp', back))]
    all_to_all x0 -> x1, blocking collectives: none -> 27.2 us  [exchange(): lax.all_to_all(keys, 'tp', 0, 0, axis_index_groups=halves, tiled=True)]
    ppermute x6 -> x0, waiting for transfers between devices: 14.2 us -> none  [per_device(): lax.ppermute(sent[slot * middle + j], 'tp', [(i, i ^ j) for i in range(tp...]
    ppermute x6 -> x0, starting transfers between devices: 10.4 us -> none  [per_device(): lax.ppermute(sent[slot * middle + j], 'tp', [(i, i ^ j) for i in range(tp...]
    ppermute x2, waiting for transfers between devices: 13 us -> 19.1 us  [per_device(): their_queries[part] = lax.ppermute(queries[part], 'tp', across)]
    ppermute x2, waiting for transfers between devices: 7.47 us -> 2.06 us  [per_device(): theirs[part] = lax.ppermute(packed, 'tp', across)]
    unnamed x9 -> x37, local copies, waits for them, and re-layouts: 0.54 us -> 5.91 us
    all_to_all x0 -> x1, starting transfers between devices: none -> 3.61 us  [exchange(): lax.all_to_all(keys, 'tp', 0, 0, axis_index_groups=halves, tiled=True)]
  transfers between devices with their start and end apart: 40 -> 35, of which waited for: 19 -> 18; matrix products, arithmetic and copies ran while one was open for 3% -> 3% of each run, Pallas kernels for 25% -> 21%
where the time goes in v8:
time: 259 us
  waiting for transfers between devices  105 us (41%)
  Pallas kernels  60.3 us (23%)
  starting transfers between devices  44 us (17%)
  blocking collectives  27.2 us (11%)
  local copies, waits for them, and re-layouts  14.4 us (6%)
  other arithmetic  7.93 us (3%)
    ppermute x7, waiting for transfers between devices, per_device(): held['behind'].append(lax.ppermute(held['behind'][-1], 'tp', back))  50.3 us
    pallas_call x4, Pallas kernels, attend(): pl.pallas_call(functools.partial(attend_kernel, n_chunks, bool(fresh), n_...  32.4 us
    all_to_all x1, blocking collectives, exchange(): lax.all_to_all(keys, 'tp', 0, 0, axis_index_groups=halves, tiled=True)  27.2 us
    ppermute x14, waiting for transfers between devices, per_device(): held = lax.ppermute(term.astype(jnp.bfloat16), 'tp', pairs)  24.8 us
    ppermute x2, waiting for transfers between devices, per_device(): their_queries[part] = lax.ppermute(queries[part], 'tp', across)  19.1 us
    ppermute x14, starting transfers between devices, per_device(): held = lax.ppermute(term.astype(jnp.bfloat16), 'tp', pairs)  18.9 us
    pallas_call x2, Pallas kernels, project(): pl.pallas_call(functools.partial(project_kernel, len(blocks), chunk, is_l...  12.9 us
    ppermute x7, starting transfers between devices, per_device(): held['before'].append(lax.ppermute(held['before'][-1], 'tp', forth))  10.7 us
  transfers between devices with their start and end apart: 35, of which 18 were waited for; matrix products, arithmetic and copies ran while one was open for 3% of the time, Pallas kernels for 21%

profile of v8, /device:TPU:0, one launch (start us, length us, event | category | flops | bytes accessed | tf_op | source)
XLA Modules:
  0.0 259.1 jit_solution(12060333616927267026)
XLA Ops:
  0.0 1.2 fusion
  1.3 1.2 fusion.2
  2.5 5.5 %copy.16 = bf16[4,256,2,1024]{3,1,2,0:T(8,128)(2,1)} copy(bf16[4,256,2,1024]{3,2,1,0:T(2,128)(2,1)} %param.15) | data formatting | bytes 8388608 | tf_op jit(solution)/shard_map/optimization_barrier | solution.py:537
  8.5 2.6 %collective-permute-start = (bf16[32,4096]{1,0:T(8,128)(2,1)S(1)}, bf16[32,4096]{1,0:T(8,128)(2,1)S(1)}, u32[]{:S(2)}, u32[]{:S(2)}) collective-permute-start(bf16[32,4096]{1,0:T(8,128)(2,1)S(1)} %get-tuple-element.104.refs_0_), channel_id=1, source_target_pairs={{0,2},{2,4},{4,6},{6,7},{7,5},{5,3},{3,1},{1,0},{8,10},{10,12},{12... | collective-permute-start | bytes 786440 | tf_op jit(solution)/shard_map/ppermute | solution.py:569
  11.9 0.8 pad_maximum_fusion.1
  12.9 1.3 compare_reduce_fusion
  14.3 3.7 %collective-permute-done.refs_1_ = bf16[32,4096]{1,0:T(8,128)(2,1)S(1)} collective-permute-done((bf16[32,4096]{1,0:T(8,128)(2,1)S(1)}, bf16[32,4096]{1,0:T(8,128)(2,1)S(1)}, u32[]{:S(2)}, u32[]{:S(2)}) %collective-permute-start) | collective-permute-done | bytes 262176 | tf_op jit(solution)/shard_map/ppermute | solution.py:569
  18.1 1.8 collective-permute-start.1
  19.9 0.7 dynamic-slice_bitcast_fusion.place_ref
  20.6 0.6 select_n.47.first_ref
  21.7 0.7 reduce.3
  22.6 3.6 %collective-permute-done.1.refs_3_ = bf16[32,4096]{1,0:T(8,128)(2,1)S(1)} collective-permute-done((bf16[32,4096]{1,0:T(8,128)(2,1)S(1)}, bf16[32,4096]{1,0:T(8,128)(2,1)S(1)}, u32[]{:S(2)}, u32[]{:S(2)}) %collective-permute-start.1) | collective-permute-done | bytes 262176 | tf_op jit(solution)/shard_map/ppermute | solution.py:569
  26.2 1.6 broadcast_in_dim.20.refs_1_
  27.8 1.6 collective-permute-start.2
  29.4 3.3 %select_docs.1 = (bf16[4,2,4,256,128]{4,3,2,1,0:T(8,128)(2,1)S(1)}, bf16[4,2,4,256,128]{4,3,2,1,0:T(8,128)(2,1)S(1)}) custom-call(s32[4]{0:T(128)S(1)} %get-tuple-element.58.place_ref, s32[4]{0:T(128)S(1)} %get-tuple-element.59.slot_ref, s32[8]{0:T(128)S(1)} %and_select_fusion.3.head_ref, bf16[4,2,256,1024]{3,2,1,0:T(8,128)(2,1)} %bitcast.20.refs_0_, ...), custom_call_target="tpu_custom_call" | custom-call | bytes 8388608 | tf_op jit(solution)/shard_map/select_docs/pallas_call | solution.py:220
  32.7 1.3 copy-done
  34.0 1.1 collective-permute-done.2.refs_5_
  35.1 27.2 %all_to_all.10.refs_0_ = bf16[4,2,4,256,128]{4,3,2,1,0:T(8,128)(2,1)} all-to-all(bf16[4,2,4,256,128]{4,3,2,1,0:T(8,128)(2,1)S(1)} %get-tuple-element.65), channel_id=1, replica_groups={{0,1,2,3},{4,5,6,7},{8,9,10,11},{12,13,14,15},{16,17,18,19},{20,21,22,2..., dimensions={0} | all-to-all | bytes 4194304 | tf_op jit(solution)/shard_map/all_to_all | solution.py:607
  62.3 3.6 %all-to-all-start.1 = ((bf16[4,2,4,256,128]{4,3,2,1,0:T(8,128)(2,1)}), bf16[4,2,4,256,128]{4,3,2,1,0:T(8,128)(2,1)S(1)}, u32[]{:S(2)}, u32[]{:S(2)}) async-start(bf16[4,2,4,256,128]{4,3,2,1,0:T(8,128)(2,1)} %copy-done), calls=%async_computation.1 | async-start | bytes 4194304 | tf_op jit(solution)/shard_map/all_to_all | solution.py:607
  65.9 2.0 collective-permute-start.5
  67.9 1.5 collective-permute-start.11
  69.9 27.9 %collective-permute-done.5.refs_2_ = bf16[32,4096]{1,0:T(8,128)(2,1)S(1)} collective-permute-done((bf16[32,4096]{1,0:T(8,128)(2,1)S(1)}, bf16[32,4096]{1,0:T(8,128)(2,1)S(1)}, u32[]{:S(2)}, u32[]{:S(2)}) %collective-permute-start.5) | collective-permute-done | bytes 262176 | tf_op jit(solution)/shard_map/ppermute | solution.py:571
  97.8 5.6 %collective-permute-done.11.refs_2_ = bf16[32,4096]{1,0:T(8,128)(2,1)S(1)} collective-permute-done((bf16[32,4096]{1,0:T(8,128)(2,1)S(1)}, bf16[32,4096]{1,0:T(8,128)(2,1)S(1)}, u32[]{:S(2)}, u32[]{:S(2)}) %collective-permute-start.11) | collective-permute-done | bytes 262176 | tf_op jit(solution)/shard_map/ppermute | solution.py:571
  103.4 2.0 collective-permute-start.6
  105.4 3.6 %collective-permute-done.7.refs_4_ = bf16[32,4096]{1,0:T(8,128)(2,1)S(1)} collective-permute-done((bf16[32,4096]{1,0:T(8,128)(2,1)S(1)}, bf16[32,4096]{1,0:T(8,128)(2,1)S(1)}, u32[]{:S(2)}, u32[]{:S(2)}) %collective-permute-start.7) | collective-permute-done | bytes 262176 | tf_op jit(solution)/shard_map/ppermute | solution.py:571
  109.0 5.6 %collective-permute-done.12.refs_4_ = bf16[32,4096]{1,0:T(8,128)(2,1)S(1)} collective-permute-done((bf16[32,4096]{1,0:T(8,128)(2,1)S(1)}, bf16[32,4096]{1,0:T(8,128)(2,1)S(1)}, u32[]{:S(2)}, u32[]{:S(2)}) %collective-permute-start.12) | collective-permute-done | bytes 262176 | tf_op jit(solution)/shard_map/ppermute | solution.py:571
  114.6 2.0 collective-permute-start.14
  116.7 3.6 %collective-permute-done.9.refs_6_ = bf16[32,4096]{1,0:T(8,128)(2,1)S(1)} collective-permute-done((bf16[32,4096]{1,0:T(8,128)(2,1)S(1)}, bf16[32,4096]{1,0:T(8,128)(2,1)S(1)}, u32[]{:S(2)}, u32[]{:S(2)}) %collective-permute-start.9) | collective-permute-done | bytes 262176 | tf_op jit(solution)/shard_map/ppermute | solution.py:571
  120.2 4.0 %collective-permute-done.13.refs_6_ = bf16[32,4096]{1,0:T(8,128)(2,1)S(1)} collective-permute-done((bf16[32,4096]{1,0:T(8,128)(2,1)S(1)}, bf16[32,4096]{1,0:T(8,128)(2,1)S(1)}, u32[]{:S(2)}, u32[]{:S(2)}) %collective-permute-start.13) | collective-permute-done | bytes 262176 | tf_op jit(solution)/shard_map/ppermute | solution.py:571
  124.3 6.1 %project.2 = (f32[256,1024]{1,0:T(8,128)S(1)}, f32[256,256]{1,0:T(8,128)S(1)}) custom-call(s32[8]{0:T(128)S(1)} %dynamic-slice_bitcast_fusion.place_ref, bf16[32,4096]{1,0:T(8,128)(2,1)S(1)} %get-tuple-element.104.refs_0_, bf16[32,4096]{1,0:T(8,128)(2,1)S(1)} %collective-permute-done.refs_1_, bf16[32,4096]{1,0:T(8,128)(2,1)S(1)} %collective-permute-done.11.refs_2_, ...), custom_call_target="tpu_custom_call" | custom-call | flops 2684354560 | bytes 12582912 | tf_op jit(solution)/shard_map/project/pallas_call | solution.py:171
  130.4 6.8 %project.3 = (bf16[4,128,256]{2,1,0:T(8,128)(2,1)S(1)}, bf16[6,128,256]{2,1,0:T(8,128)(2,1)S(1)}) custom-call(s32[8]{0:T(128)S(1)} %dynamic-slice_bitcast_fusion.place_ref, bf16[32,4096]{1,0:T(8,128)(2,1)S(1)} %get-tuple-element.103.refs_0_, bf16[32,4096]{1,0:T(8,128)(2,1)S(1)} %collective-permute-done.4.refs_1_, ...), custom_call_target="tpu_custom_call" | custom-call | flops 2684354560 | bytes 12582912 | tf_op jit(solution)/shard_map/project/pallas_call | solution.py:171
  137.3 2.0 collective-permute-start.15
  139.3 1.0 collective-permute-start.17
  140.3 19.1 %collective-permute-done.15.refs_3_.there_ref = bf16[6,128,256]{2,1,0:T(8,128)(2,1)S(1)} collective-permute-done((bf16[6,128,256]{2,1,0:T(8,128)(2,1)S(1)}, bf16[6,128,256]{2,1,0:T(8,128)(2,1)S(1)}, u32[]{:S(2)}, u32[]{:S(2)}) %collective-permute-start.15) | collective-permute-done | bytes 393248 | tf_op jit(solution)/shard_map/ppermute | solution.py:617
  159.4 0.8 collective-permute-start.16
  160.3 9.8 %attend.4 = bf16[4,144,256]{2,1,0:T(8,128)(2,1)} custom-call(s32[16]{0:T(128)S(1)} %copy-done.8, s32[256]{0:T(256)S(1)} %bitcast.23, bf16[4,2,4,256,128]{4,3,2,1,0:T(8,128)(2,1)S(1)} %copy-done.1, bf16[4,1024,128]{2,1,0:T(8,128)(2,1)S(1)} %copy-done.2, s32[8,1,256]{2,1,0:T(1,128)S(1)} %tile.11.refs_2_, ...), custom_call_target="tpu_custom_call" | custom-call | flops 1073741824 | bytes 2097152 | tf_op jit(solution)/shard_map/attend/pallas_call | solution.py:370
  170.0 6.5 %attend.6 = bf16[4,144,256]{2,1,0:T(8,128)(2,1)} custom-call(s32[16]{0:T(128)S(1)} %copy-done.8, s32[256]{0:T(256)S(1)} %bitcast.24, bf16[4,2,4,256,128]{4,3,2,1,0:T(8,128)(2,1)S(1)} %copy-done.1, bf16[4,1024,128]{2,1,0:T(8,128)(2,1)S(1)} %copy-done.2, s32[8,1,256]{2,1,0:T(1,128)S(1)} %tile.11.refs_2_, bf16[4,128,256]{2,1,0:T(8,128)(2,1)S(1)} %collective-permute-done.17.refs_3_), custom_call_target="tpu_custom_call" | custom-call | flops 1073741824 | bytes 2097152 | tf_op jit(solution)/shard_map/attend/pallas_call | solution.py:370
  176.6 3.1 %collective-permute-start.18 = (bf16[4,144,256]{2,1,0:T(8,128)(2,1)}, bf16[4,144,256]{2,1,0:T(8,128)(2,1)}, u32[]{:S(2)}, u32[]{:S(2)}) collective-permute-start(bf16[4,144,256]{2,1,0:T(8,128)(2,1)} %attend.6), channel_id=1, source_target_pairs={{0,4},{1,5},{2,6},{3,7},{4,0},{5,1},{6,2},{7,3},{8,12},{9,13},{10,... | collective-permute-start | bytes 884744 | tf_op jit(solution)/shard_map/ppermute | solution.py:648
  179.7 1.0 copy-done.6
  180.7 0.6 copy-done.9
  181.3 0.9 copy-done.14
  182.2 9.5 %attend.7 = (f32[4,1,256]{2,1,0:T(1,128)S(1)}, f32[4,1,256]{2,1,0:T(1,128)S(1)}, f32[4,128,256]{2,1,0:T(8,128)S(1)}) custom-call(s32[16]{0:T(128)S(1)} %copy-done.9, s32[256]{0:T(256)S(1)} %bitcast.25, bf16[4,2,4,256,128]{4,3,2,1,0:T(8,128)(2,1)S(1)} %all-to-all-done.1.refs_0_, bf16[4,1024,128]{2,1,0:T(8,128)(2,1)S(1)} %copy-done.2, ...), custom_call_target="tpu_custom_call" | custom-call | flops 1073741824 | bytes 2097152 | tf_op jit(solution)/shard_map/attend/pallas_call | solution.py:370
  191.8 0.6 copy-done.10
  192.4 0.9 copy-done.12
  193.3 6.6 %attend.5 = (f32[4,1,256]{2,1,0:T(1,128)S(1)}, f32[4,1,256]{2,1,0:T(1,128)S(1)}, f32[4,128,256]{2,1,0:T(8,128)S(1)}) custom-call(s32[16]{0:T(128)S(1)} %copy-done.10, s32[256]{0:T(256)S(1)} %bitcast.26, bf16[4,2,4,256,128]{4,3,2,1,0:T(8,128)(2,1)S(1)} %all-to-all-done.1.refs_0_, bf16[4,1024,128]{2,1,0:T(8,128)(2,1)S(1)} %copy-done.2, ...), custom_call_target="tpu_custom_call" | custom-call | flops 1073741824 | bytes 2097152 | tf_op jit(solution)/shard_map/attend/pallas_call | solution.py:370
  199.9 2.1 collective-permute-done.19.refs_7_
  202.0 1.4 merge.1.x_ref
  203.4 5.1 %project_out.2 = (f32[32,4096]{1,0:T(8,128)S(1)}, f32[32,4096]{1,0:T(8,128)S(1)}, f32[32,4096]{1,0:T(8,128)S(1)}, f32[32,4096]{1,0:T(8,128)S(1)}, f32[32,4096]{1...) custom-call(s32[8]{0:T(128)S(1)} %dynamic-slice_bitcast_fusion.place_ref, ...), custom_call_target="tpu_custom_call" | custom-call | flops 2147483648 | bytes 13107200 | tf_op jit(solution)/shard_map/project_out/pallas_call | solution.py:488
  208.9 6.0 %collective-permute-start.24 = (bf16[32,4096]{1,0:T(8,128)(2,1)S(1)}, bf16[32,4096]{1,0:T(8,128)(2,1)S(1)}, u32[]{:S(2)}, u32[]{:S(2)}) collective-permute-start(bf16[32,4096]{1,0:T(8,128)(2,1)S(1)} %convert_element_type.116), channel_id=1, source_target_pairs={{2,0},{4,2},{6,4},{7,6},{5,7},{3,5},{1,3},{0,1},{10,8},{12,10},{14... | collective-permute-start | bytes 786440 | tf_op jit(solution)/shard_map/ppermute | solution.py:665
  214.9 5.1 %project_out.3 = (f32[32,4096]{1,0:T(8,128)S(1)}, f32[32,4096]{1,0:T(8,128)S(1)}, f32[32,4096]{1,0:T(8,128)S(1)}, f32[32,4096]{1,0:T(8,128)S(1)}, f32[32,4096]{1...) custom-call(s32[8]{0:T(128)S(1)} %dynamic-slice_bitcast_fusion.place_ref, ...), custom_call_target="tpu_custom_call" | custom-call | flops 2147483648 | bytes 13107200 | tf_op jit(solution)/shard_map/project_out/pallas_call | solution.py:488
  220.2 2.1 collective-permute-start.30
  222.4 2.1 collective-permute-start.25
  224.5 4.9 %collective-permute-done.27 = bf16[32,4096]{1,0:T(8,128)(2,1)S(1)} collective-permute-done((bf16[32,4096]{1,0:T(8,128)(2,1)S(1)}, bf16[32,4096]{1,0:T(8,128)(2,1)S(1)}, u32[]{:S(2)}, u32[]{:S(2)}) %collective-permute-start.27) | collective-permute-done | bytes 262176 | tf_op jit(solution)/shard_map/ppermute | solution.py:665
  229.5 2.1 collective-permute-start.31
  231.6 3.3 %collective-permute-done.21 = bf16[32,4096]{1,0:T(8,128)(2,1)S(1)} collective-permute-done((bf16[32,4096]{1,0:T(8,128)(2,1)S(1)}, bf16[32,4096]{1,0:T(8,128)(2,1)S(1)}, u32[]{:S(2)}, u32[]{:S(2)}) %collective-permute-start.21) | collective-permute-done | bytes 262176 | tf_op jit(solution)/shard_map/ppermute | solution.py:665
  235.1 2.1 collective-permute-start.26
  237.2 3.3 %collective-permute-done.28 = bf16[32,4096]{1,0:T(8,128)(2,1)S(1)} collective-permute-done((bf16[32,4096]{1,0:T(8,128)(2,1)S(1)}, bf16[32,4096]{1,0:T(8,128)(2,1)S(1)}, u32[]{:S(2)}, u32[]{:S(2)}) %collective-permute-start.28) | collective-permute-done | bytes 262176 | tf_op jit(solution)/shard_map/ppermute | solution.py:665
  240.7 2.1 collective-permute-start.32
  242.9 3.3 %collective-permute-done.22 = bf16[32,4096]{1,0:T(8,128)(2,1)S(1)} collective-permute-done((bf16[32,4096]{1,0:T(8,128)(2,1)S(1)}, bf16[32,4096]{1,0:T(8,128)(2,1)S(1)}, u32[]{:S(2)}, u32[]{:S(2)}) %collective-permute-start.22) | collective-permute-done | bytes 262176 | tf_op jit(solution)/shard_map/ppermute | solution.py:665
  246.3 4.5 %collective-permute-done.32 = bf16[32,4096]{1,0:T(8,128)(2,1)S(1)} collective-permute-done((bf16[32,4096]{1,0:T(8,128)(2,1)S(1)}, bf16[32,4096]{1,0:T(8,128)(2,1)S(1)}, u32[]{:S(2)}, u32[]{:S(2)}) %collective-permute-start.32) | collective-permute-done | bytes 262176 | tf_op jit(solution)/shard_map/ppermute | solution.py:665
  250.8 1.8 collective-permute-start.33
  252.6 3.7 %collective-permute-done.23 = bf16[32,4096]{1,0:T(8,128)(2,1)S(1)} collective-permute-done((bf16[32,4096]{1,0:T(8,128)(2,1)S(1)}, bf16[32,4096]{1,0:T(8,128)(2,1)S(1)}, u32[]{:S(2)}, u32[]{:S(2)}) %collective-permute-start.23) | collective-permute-done | bytes 262176 | tf_op jit(solution)/shard_map/ppermute | solution.py:665
  256.4 1.7 collective-permute-done.33
  258.2 0.8 pad_maximum_fusion
  (98 shorter events, 4.6 us)
Async XLA Ops:
  2.5 8.7 %copy-start.15 = (s32[1,4]{1,0:T(1,128)S(1)}, s32[1,4]{1,0:T(1,128)}, u32[]{:S(2)}) copy-start(s32[1,4]{1,0:T(1,128)} %param.17) | copy-start | bytes 52
  2.5 8.8 %copy-start.7 = (s32[1,256]{1,0:T(1,128)S(1)}, s32[1,256]{1,0:T(1,128)}, u32[]{:S(2)}) copy-start(s32[1,256]{1,0:T(1,128)} %param.18) | copy-start | bytes 3076
  2.5 11.6 %copy-start.16 = (s32[4]{0:T(128)S(1)}, s32[4]{0:T(128)}, u32[]{:S(2)}) copy-start(s32[4]{0:T(128)} %param.16) | copy-start | bytes 52
  8.0 21.3 %collective-permute-start.3 = (bf16[4,2,256,1024]{3,2,1,0:T(8,128)(2,1)}, bf16[4,2,256,1024]{3,2,1,0:T(8,128)(2,1)}, u32[]{:S(2)}, u32[]{:S(2)}) collective-permute-start(bf16[4,2,256,1024]{3,2,1,0:T(8,128)(2,1)} %bitcast.20.refs_0_), channel_id=1, source_target_pairs={{8,0},{0,8},{9,1},{1,9},{10,2},{2,10},{11,3},{3,11},{12,4},{4,12},... | collective-permute-start | bytes 12582920 | tf_op jit(solution)/shard_map/ppermute | solution.py:578
  8.5 9.5 %collective-permute-start = (bf16[32,4096]{1,0:T(8,128)(2,1)S(1)}, bf16[32,4096]{1,0:T(8,128)(2,1)S(1)}, u32[]{:S(2)}, u32[]{:S(2)}) collective-permute-start(bf16[32,4096]{1,0:T(8,128)(2,1)S(1)} %get-tuple-element.104.refs_0_), channel_id=1, source_target_pairs={{0,2},{2,4},{4,6},{6,7},{7,5},{5,3},{3,1},{1,0},{8,10},{10,12},{12... | collective-permute-start | bytes 786440 | tf_op jit(solution)/shard_map/ppermute | solution.py:569
  18.1 8.1 %collective-permute-start.1 = (bf16[32,4096]{1,0:T(8,128)(2,1)S(1)}, bf16[32,4096]{1,0:T(8,128)(2,1)S(1)}, u32[]{:S(2)}, u32[]{:S(2)}) collective-permute-start(bf16[32,4096]{1,0:T(8,128)(2,1)S(1)} %collective-permute-done.refs_1_), channel_id=1, source_target_pairs={{0,2},{2,4},{4,6},{6,7},{7,5},{5,3},{3,1},{1,0},{8,10},{10,12},{12... | collective-permute-start | bytes 786440 | tf_op jit(solution)/shard_map/ppermute | solution.py:569
  27.8 7.3 %collective-permute-start.2 = (bf16[32,4096]{1,0:T(8,128)(2,1)S(1)}, bf16[32,4096]{1,0:T(8,128)(2,1)S(1)}, u32[]{:S(2)}, u32[]{:S(2)}) collective-permute-start(bf16[32,4096]{1,0:T(8,128)(2,1)S(1)} %collective-permute-done.1.refs_3_), channel_id=1, source_target_pairs={{0,2},{2,4},{4,6},{6,7},{7,5},{5,3},{3,1},{1,0},{8,10},{10,12},{12... | collective-permute-start | bytes 786440 | tf_op jit(solution)/shard_map/ppermute | solution.py:569
  32.6 1.4 copy-start
  62.3 117.5 %all-to-all-start.1 = ((bf16[4,2,4,256,128]{4,3,2,1,0:T(8,128)(2,1)}), bf16[4,2,4,256,128]{4,3,2,1,0:T(8,128)(2,1)S(1)}, u32[]{:S(2)}, u32[]{:S(2)}) async-start(bf16[4,2,4,256,128]{4,3,2,1,0:T(8,128)(2,1)} %copy-done), calls=%async_computation.1 | async-start | bytes 4194304 | tf_op jit(solution)/shard_map/all_to_all | solution.py:607
  65.9 64.5 %copy-start.3 = (f32[256,128]{1,0:T(8,128)S(1)}, f32[256,128]{1,0:T(8,128)}, u32[]{:S(2)}) copy-start(f32[256,128]{1,0:T(8,128)} %get-tuple-element.73.refs_13_.refs_5_) | copy-start | bytes 393220
  65.9 31.9 %collective-permute-start.5 = (bf16[32,4096]{1,0:T(8,128)(2,1)S(1)}, bf16[32,4096]{1,0:T(8,128)(2,1)S(1)}, u32[]{:S(2)}, u32[]{:S(2)}) collective-permute-start(bf16[32,4096]{1,0:T(8,128)(2,1)S(1)} %get-tuple-element.103.refs_0_), channel_id=1, source_target_pairs={{2,0},{4,2},{6,4},{7,6},{5,7},{3,5},{1,3},{0,1},{10,8},{12,10},{14... | collective-permute-start | bytes 786440 | tf_op jit(solution)/shard_map/ppermute | solution.py:571
  67.9 35.5 %collective-permute-start.11 = (bf16[32,4096]{1,0:T(8,128)(2,1)S(1)}, bf16[32,4096]{1,0:T(8,128)(2,1)S(1)}, u32[]{:S(2)}, u32[]{:S(2)}) collective-permute-start(bf16[32,4096]{1,0:T(8,128)(2,1)S(1)} %get-tuple-element.104.refs_0_), channel_id=1, source_target_pairs={{2,0},{4,2},{6,4},{7,6},{5,7},{3,5},{1,3},{0,1},{10,8},{12,10},{14... | collective-permute-start | bytes 786440 | tf_op jit(solution)/shard_map/ppermute | solution.py:571
  69.3 34.1 %collective-permute-start.4 = (bf16[32,4096]{1,0:T(8,128)(2,1)S(1)}, bf16[32,4096]{1,0:T(8,128)(2,1)S(1)}, u32[]{:S(2)}, u32[]{:S(2)}) collective-permute-start(bf16[32,4096]{1,0:T(8,128)(2,1)S(1)} %get-tuple-element.103.refs_0_), channel_id=1, source_target_pairs={{0,2},{2,4},{4,6},{6,7},{7,5},{5,3},{3,1},{1,0},{8,10},{10,12},{12... | collective-permute-start | bytes 786440 | tf_op jit(solution)/shard_map/ppermute | solution.py:569
  97.8 11.2 %collective-permute-start.7 = (bf16[32,4096]{1,0:T(8,128)(2,1)S(1)}, bf16[32,4096]{1,0:T(8,128)(2,1)S(1)}, u32[]{:S(2)}, u32[]{:S(2)}) collective-permute-start(bf16[32,4096]{1,0:T(8,128)(2,1)S(1)} %collective-permute-done.5.refs_2_), channel_id=1, source_target_pairs={{2,0},{4,2},{6,4},{7,6},{5,7},{3,5},{1,3},{0,1},{10,8},{12,10},{14... | collective-permute-start | bytes 786440 | tf_op jit(solution)/shard_map/ppermute | solution.py:571
  103.4 11.2 %collective-permute-start.12 = (bf16[32,4096]{1,0:T(8,128)(2,1)S(1)}, bf16[32,4096]{1,0:T(8,128)(2,1)S(1)}, u32[]{:S(2)}, u32[]{:S(2)}) collective-permute-start(bf16[32,4096]{1,0:T(8,128)(2,1)S(1)} %collective-permute-done.11.refs_2_), channel_id=1, source_target_pairs={{2,0},{4,2},{6,4},{7,6},{5,7},{3,5},{1,3},{0,1},{10,8},{12,10},{14... | collective-permute-start | bytes 786440 | tf_op jit(solution)/shard_map/ppermute | solution.py:571
  103.4 13.3 %collective-permute-start.6 = (bf16[32,4096]{1,0:T(8,128)(2,1)S(1)}, bf16[32,4096]{1,0:T(8,128)(2,1)S(1)}, u32[]{:S(2)}, u32[]{:S(2)}) collective-permute-start(bf16[32,4096]{1,0:T(8,128)(2,1)S(1)} %collective-permute-done.4.refs_1_), channel_id=1, source_target_pairs={{0,2},{2,4},{4,6},{6,7},{7,5},{5,3},{3,1},{1,0},{8,10},{10,12},{12... | collective-permute-start | bytes 786440 | tf_op jit(solution)/shard_map/ppermute | solution.py:569
  109.0 11.2 %collective-permute-start.9 = (bf16[32,4096]{1,0:T(8,128)(2,1)S(1)}, bf16[32,4096]{1,0:T(8,128)(2,1)S(1)}, u32[]{:S(2)}, u32[]{:S(2)}) collective-permute-start(bf16[32,4096]{1,0:T(8,128)(2,1)S(1)} %collective-permute-done.7.refs_4_), channel_id=1, source_target_pairs={{2,0},{4,2},{6,4},{7,6},{5,7},{3,5},{1,3},{0,1},{10,8},{12,10},{14... | collective-permute-start | bytes 786440 | tf_op jit(solution)/shard_map/ppermute | solution.py:571
  114.6 9.7 %collective-permute-start.13 = (bf16[32,4096]{1,0:T(8,128)(2,1)S(1)}, bf16[32,4096]{1,0:T(8,128)(2,1)S(1)}, u32[]{:S(2)}, u32[]{:S(2)}) collective-permute-start(bf16[32,4096]{1,0:T(8,128)(2,1)S(1)} %collective-permute-done.12.refs_4_), channel_id=1, source_target_pairs={{2,0},{4,2},{6,4},{7,6},{5,7},{3,5},{1,3},{0,1},{10,8},{12,10},{14... | collective-permute-start | bytes 786440 | tf_op jit(solution)/shard_map/ppermute | solution.py:571
  114.6 9.7 %collective-permute-start.14 = (bf16[32,4096]{1,0:T(8,128)(2,1)S(1)}, bf16[32,4096]{1,0:T(8,128)(2,1)S(1)}, u32[]{:S(2)}, u32[]{:S(2)}) collective-permute-start(bf16[32,4096]{1,0:T(8,128)(2,1)S(1)} %collective-permute-done.2.refs_5_), channel_id=1, source_target_pairs={{0,2},{2,4},{4,6},{6,7},{7,5},{5,3},{3,1},{1,0},{8,10},{10,12},{12... | collective-permute-start | bytes 786440 | tf_op jit(solution)/shard_map/ppermute | solution.py:569
  116.6 13.7 %collective-permute-start.8 = (bf16[32,4096]{1,0:T(8,128)(2,1)S(1)}, bf16[32,4096]{1,0:T(8,128)(2,1)S(1)}, u32[]{:S(2)}, u32[]{:S(2)}) collective-permute-start(bf16[32,4096]{1,0:T(8,128)(2,1)S(1)} %collective-permute-done.6.refs_3_), channel_id=1, source_target_pairs={{0,2},{2,4},{4,6},{6,7},{7,5},{5,3},{3,1},{1,0},{8,10},{10,12},{12... | collective-permute-start | bytes 786440 | tf_op jit(solution)/shard_map/ppermute | solution.py:569
  120.2 10.2 %collective-permute-start.10 = (bf16[32,4096]{1,0:T(8,128)(2,1)S(1)}, bf16[32,4096]{1,0:T(8,128)(2,1)S(1)}, u32[]{:S(2)}, u32[]{:S(2)}) collective-permute-start(bf16[32,4096]{1,0:T(8,128)(2,1)S(1)} %collective-permute-done.9.refs_6_), channel_id=1, source_target_pairs={{2,0},{4,2},{6,4},{7,6},{5,7},{3,5},{1,3},{0,1},{10,8},{12,10},{14... | collective-permute-start | bytes 786440 | tf_op jit(solution)/shard_map/ppermute | solution.py:571
  130.4 29.8 %copy-start.1 = (bf16[4,2,4,256,128]{4,3,2,1,0:T(8,128)(2,1)S(1)}, bf16[4,2,4,256,128]{4,3,2,1,0:T(8,128)(2,1)}, u32[]{:S(2)}) copy-start(bf16[4,2,4,256,128]{4,3,2,1,0:T(8,128)(2,1)} %all_to_all.10.refs_0_) | copy-start | bytes 6291460
  130.4 29.8 %copy-start.2 = (bf16[4,1024,128]{2,1,0:T(8,128)(2,1)S(1)}, bf16[4,1024,128]{2,1,0:T(8,128)(2,1)}, u32[]{:S(2)}) copy-start(bf16[4,1024,128]{2,1,0:T(8,128)(2,1)} %broadcast_in_dim.20.refs_1_) | copy-start | bytes 3145732
  130.4 29.8 %copy-start.8 = (s32[16]{0:T(128)S(1)}, s32[16]{0:T(128)}, u32[]{:S(2)}) copy-start(s32[16]{0:T(128)} %select_n.47.first_ref) | copy-start | bytes 196
  137.2 39.3 %copy-start.5 = (bf16[6,128,256]{2,1,0:T(8,128)(2,1)}, bf16[6,128,256]{2,1,0:T(8,128)(2,1)S(1)}, u32[]{:S(2)}) copy-start(bf16[6,128,256]{2,1,0:T(8,128)(2,1)S(1)} %get-tuple-element.76.here_ref.refs_3_) | copy-start | bytes 1179652
  137.3 39.3 %copy-start.11 = (bf16[4,128,256]{2,1,0:T(8,128)(2,1)}, bf16[4,128,256]{2,1,0:T(8,128)(2,1)S(1)}, u32[]{:S(2)}) copy-start(bf16[4,128,256]{2,1,0:T(8,128)(2,1)S(1)} %get-tuple-element.74.refs_3_) | copy-start | bytes 786436
  137.3 22.1 %collective-permute-start.15 = (bf16[6,128,256]{2,1,0:T(8,128)(2,1)S(1)}, bf16[6,128,256]{2,1,0:T(8,128)(2,1)S(1)}, u32[]{:S(2)}, u32[]{:S(2)}) collective-permute-start(bf16[6,128,256]{2,1,0:T(8,128)(2,1)S(1)} %get-tuple-element.76.here_ref.refs_3_), channel_id=1, source_target_pairs={{0,4},{1,5},{2,6},{3,7},{4,0},{5,1},{6,2},{7,3},{8,12},{9,13},{10,... | collective-permute-start | bytes 1179656 | tf_op jit(solution)/shard_map/ppermute | solution.py:617
  139.3 30.7 %collective-permute-start.17 = (bf16[4,128,256]{2,1,0:T(8,128)(2,1)S(1)}, bf16[4,128,256]{2,1,0:T(8,128)(2,1)S(1)}, u32[]{:S(2)}, u32[]{:S(2)}) collective-permute-start(bf16[4,128,256]{2,1,0:T(8,128)(2,1)S(1)} %get-tuple-element.74.refs_3_), channel_id=1, source_target_pairs={{0,4},{1,5},{2,6},{3,7},{4,0},{5,1},{6,2},{7,3},{8,12},{9,13},{10,... | collective-permute-start | bytes 786440 | tf_op jit(solution)/shard_map/ppermute | solution.py:617
  159.4 20.3 %copy-start.4 = (f32[256,128]{1,0:T(8,128)S(1)}, f32[256,128]{1,0:T(8,128)}, u32[]{:S(2)}) copy-start(f32[256,128]{1,0:T(8,128)} %get-tuple-element.73.refs_13_.refs_5_) | copy-start | bytes 393220
  159.4 10.6 %collective-permute-start.16 = (bf16[256,256]{1,0:T(8,128)(2,1)S(1)}, bf16[256,256]{1,0:T(8,128)(2,1)S(1)}, u32[]{:S(2)}, u32[]{:S(2)}) collective-permute-start(bf16[256,256]{1,0:T(8,128)(2,1)S(1)} %pick_new.1), channel_id=1, source_target_pairs={{0,0},{1,2},{2,4},{3,6},{4,1},{5,3},{6,5},{7,7},{8,8},{9,10},{10,1... | collective-permute-start | bytes 393224 | tf_op jit(solution)/shard_map/ppermute | solution.py:620
  170.0 9.6 %copy-start.13 = (bf16[256,256]{1,0:T(8,128)(2,1)}, bf16[256,256]{1,0:T(8,128)(2,1)S(1)}, u32[]{:S(2)}) copy-start(bf16[256,256]{1,0:T(8,128)(2,1)S(1)} %collective-permute-done.16.refs_6_) | copy-start | bytes 393220
  176.6 23.4 %collective-permute-start.18 = (bf16[4,144,256]{2,1,0:T(8,128)(2,1)}, bf16[4,144,256]{2,1,0:T(8,128)(2,1)}, u32[]{:S(2)}, u32[]{:S(2)}) collective-permute-start(bf16[4,144,256]{2,1,0:T(8,128)(2,1)} %attend.6), channel_id=1, source_target_pairs={{0,4},{1,5},{2,6},{3,7},{4,0},{5,1},{6,2},{7,3},{8,12},{9,13},{10,... | collective-permute-start | bytes 884744 | tf_op jit(solution)/shard_map/ppermute | solution.py:648
  179.7 22.3 %collective-permute-start.19 = (bf16[4,144,256]{2,1,0:T(8,128)(2,1)}, bf16[4,144,256]{2,1,0:T(8,128)(2,1)}, u32[]{:S(2)}, u32[]{:S(2)}) collective-permute-start(bf16[4,144,256]{2,1,0:T(8,128)(2,1)} %attend.4), channel_id=1, source_target_pairs={{0,4},{1,5},{2,6},{3,7},{4,0},{5,1},{6,2},{7,3},{8,12},{9,13},{10,... | collective-permute-start | bytes 884744 | tf_op jit(solution)/shard_map/ppermute | solution.py:648
  179.7 1.0 copy-start.6
  180.7 0.6 copy-start.9
  181.3 0.9 copy-start.14
  191.8 0.6 copy-start.10
  192.3 0.9 copy-start.12
  208.6 13.7 %collective-permute-start.20 = (bf16[32,4096]{1,0:T(8,128)(2,1)S(1)}, bf16[32,4096]{1,0:T(8,128)(2,1)S(1)}, u32[]{:S(2)}, u32[]{:S(2)}) collective-permute-start(bf16[32,4096]{1,0:T(8,128)(2,1)S(1)} %get-tuple-element.91), channel_id=1, source_target_pairs={{0,2},{2,4},{4,6},{6,7},{7,5},{5,3},{3,1},{1,0},{8,10},{10,12},{12... | collective-permute-start | bytes 786440 | tf_op jit(solution)/shard_map/ppermute | solution.py:665
  208.9 13.4 %collective-permute-start.24 = (bf16[32,4096]{1,0:T(8,128)(2,1)S(1)}, bf16[32,4096]{1,0:T(8,128)(2,1)S(1)}, u32[]{:S(2)}, u32[]{:S(2)}) collective-permute-start(bf16[32,4096]{1,0:T(8,128)(2,1)S(1)} %convert_element_type.116), channel_id=1, source_target_pairs={{2,0},{4,2},{6,4},{7,6},{5,7},{3,5},{1,3},{0,1},{10,8},{12,10},{14... | collective-permute-start | bytes 786440 | tf_op jit(solution)/shard_map/ppermute | solution.py:665
  220.1 9.2 %collective-permute-start.27 = (bf16[32,4096]{1,0:T(8,128)(2,1)S(1)}, bf16[32,4096]{1,0:T(8,128)(2,1)S(1)}, u32[]{:S(2)}, u32[]{:S(2)}) collective-permute-start(bf16[32,4096]{1,0:T(8,128)(2,1)S(1)} %convert_element_type.123), channel_id=1, source_target_pairs={{0,2},{2,4},{4,6},{6,7},{7,5},{5,3},{3,1},{1,0},{8,10},{10,12},{12... | collective-permute-start | bytes 786440 | tf_op jit(solution)/shard_map/ppermute | solution.py:665
  220.2 9.3 %collective-permute-start.30 = (bf16[32,4096]{1,0:T(8,128)(2,1)S(1)}, bf16[32,4096]{1,0:T(8,128)(2,1)S(1)}, u32[]{:S(2)}, u32[]{:S(2)}) collective-permute-start(bf16[32,4096]{1,0:T(8,128)(2,1)S(1)} %get-tuple-element.102), channel_id=1, source_target_pairs={{2,0},{4,2},{6,4},{7,6},{5,7},{3,5},{1,3},{0,1},{10,8},{12,10},{14... | collective-permute-start | bytes 786440 | tf_op jit(solution)/shard_map/ppermute | solution.py:665
  222.3 12.7 %collective-permute-start.21 = (bf16[32,4096]{1,0:T(8,128)(2,1)S(1)}, bf16[32,4096]{1,0:T(8,128)(2,1)S(1)}, u32[]{:S(2)}, u32[]{:S(2)}) collective-permute-start(bf16[32,4096]{1,0:T(8,128)(2,1)S(1)} %add_convert_fusion.11), channel_id=1, source_target_pairs={{0,2},{2,4},{4,6},{6,7},{7,5},{5,3},{3,1},{1,0},{8,10},{10,12},{12... | collective-permute-start | bytes 786440 | tf_op jit(solution)/shard_map/ppermute | solution.py:665
  222.4 12.7 %collective-permute-start.25 = (bf16[32,4096]{1,0:T(8,128)(2,1)S(1)}, bf16[32,4096]{1,0:T(8,128)(2,1)S(1)}, u32[]{:S(2)}, u32[]{:S(2)}) collective-permute-start(bf16[32,4096]{1,0:T(8,128)(2,1)S(1)} %add_convert_fusion.8), channel_id=1, source_target_pairs={{2,0},{4,2},{6,4},{7,6},{5,7},{3,5},{1,3},{0,1},{10,8},{12,10},{14... | collective-permute-start | bytes 786440 | tf_op jit(solution)/shard_map/ppermute | solution.py:665
  229.4 11.2 %collective-permute-start.28 = (bf16[32,4096]{1,0:T(8,128)(2,1)S(1)}, bf16[32,4096]{1,0:T(8,128)(2,1)S(1)}, u32[]{:S(2)}, u32[]{:S(2)}) collective-permute-start(bf16[32,4096]{1,0:T(8,128)(2,1)S(1)} %add_convert_fusion.5), channel_id=1, source_target_pairs={{0,2},{2,4},{4,6},{6,7},{7,5},{5,3},{3,1},{1,0},{8,10},{10,12},{12... | collective-permute-start | bytes 786440 | tf_op jit(solution)/shard_map/ppermute | solution.py:665
  229.5 11.2 %collective-permute-start.31 = (bf16[32,4096]{1,0:T(8,128)(2,1)S(1)}, bf16[32,4096]{1,0:T(8,128)(2,1)S(1)}, u32[]{:S(2)}, u32[]{:S(2)}) collective-permute-start(bf16[32,4096]{1,0:T(8,128)(2,1)S(1)} %add_convert_fusion.3), channel_id=1, source_target_pairs={{2,0},{4,2},{6,4},{7,6},{5,7},{3,5},{1,3},{0,1},{10,8},{12,10},{14... | collective-permute-start | bytes 786440 | tf_op jit(solution)/shard_map/ppermute | solution.py:665
  235.0 11.2 %collective-permute-start.22 = (bf16[32,4096]{1,0:T(8,128)(2,1)S(1)}, bf16[32,4096]{1,0:T(8,128)(2,1)S(1)}, u32[]{:S(2)}, u32[]{:S(2)}) collective-permute-start(bf16[32,4096]{1,0:T(8,128)(2,1)S(1)} %add_convert_fusion.10), channel_id=1, source_target_pairs={{0,2},{2,4},{4,6},{6,7},{7,5},{5,3},{3,1},{1,0},{8,10},{10,12},{12... | collective-permute-start | bytes 786440 | tf_op jit(solution)/shard_map/ppermute | solution.py:665
  235.1 17.5 %collective-permute-start.26 = (bf16[32,4096]{1,0:T(8,128)(2,1)S(1)}, bf16[32,4096]{1,0:T(8,128)(2,1)S(1)}, u32[]{:S(2)}, u32[]{:S(2)}) collective-permute-start(bf16[32,4096]{1,0:T(8,128)(2,1)S(1)} %add_convert_fusion.7), channel_id=1, source_target_pairs={{2,0},{4,2},{6,4},{7,6},{5,7},{3,5},{1,3},{0,1},{10,8},{12,10},{14... | collective-permute-start | bytes 786440 | tf_op jit(solution)/shard_map/ppermute | solution.py:665
  240.6 15.8 %collective-permute-start.29 = (bf16[32,4096]{1,0:T(8,128)(2,1)S(1)}, bf16[32,4096]{1,0:T(8,128)(2,1)S(1)}, u32[]{:S(2)}, u32[]{:S(2)}) collective-permute-start(bf16[32,4096]{1,0:T(8,128)(2,1)S(1)} %add_convert_fusion.4), channel_id=1, source_target_pairs={{0,2},{2,4},{4,6},{6,7},{7,5},{5,3},{3,1},{1,0},{8,10},{10,12},{12... | collective-permute-start | bytes 786440 | tf_op jit(solution)/shard_map/ppermute | solution.py:665
  240.7 10.0 %collective-permute-start.32 = (bf16[32,4096]{1,0:T(8,128)(2,1)S(1)}, bf16[32,4096]{1,0:T(8,128)(2,1)S(1)}, u32[]{:S(2)}, u32[]{:S(2)}) collective-permute-start(bf16[32,4096]{1,0:T(8,128)(2,1)S(1)} %add_convert_fusion.2), channel_id=1, source_target_pairs={{2,0},{4,2},{6,4},{7,6},{5,7},{3,5},{1,3},{0,1},{10,8},{12,10},{14... | collective-permute-start | bytes 786440 | tf_op jit(solution)/shard_map/ppermute | solution.py:665
  246.3 10.1 %collective-permute-start.23 = (bf16[32,4096]{1,0:T(8,128)(2,1)S(1)}, bf16[32,4096]{1,0:T(8,128)(2,1)S(1)}, u32[]{:S(2)}, u32[]{:S(2)}) collective-permute-start(bf16[32,4096]{1,0:T(8,128)(2,1)S(1)} %add_convert_fusion.9), channel_id=1, source_target_pairs={{0,2},{2,4},{4,6},{6,7},{7,5},{5,3},{3,1},{1,0},{8,10},{10,12},{12... | collective-permute-start | bytes 786440 | tf_op jit(solution)/shard_map/ppermute | solution.py:665
  250.8 7.3 %collective-permute-start.33 = (bf16[32,4096]{1,0:T(8,128)(2,1)S(1)}, bf16[32,4096]{1,0:T(8,128)(2,1)S(1)}, u32[]{:S(2)}, u32[]{:S(2)}) collective-permute-start(bf16[32,4096]{1,0:T(8,128)(2,1)S(1)} %add_convert_fusion.1), channel_id=1, source_target_pairs={{2,0},{4,2},{6,4},{7,6},{5,7},{3,5},{1,3},{0,1},{10,8},{12,10},{14... | collective-permute-start | bytes 786440 | tf_op jit(solution)/shard_map/ppermute | solution.py:665

commit v9 on v7

--- a/solution.py
+++ b/solution.py
@@ -28,6 +28,7 @@
 DEPTH_TILE = 1024
 WIDTH_TILE = 1024
 SLOTS = 3
+CUTS = 4
 
 
 def cost(flops, bytes_accessed, transcendentals=0):
@@ -60,10 +61,17 @@
 def stream(sources, buffers, sems):
     def copies(step):
         slot = step % SLOTS
-        return [
-            pltpu.make_async_copy(source(step), buffer.at[slot], sems.at[i, slot])
-            for i, (source, buffer) in enumerate(zip(sources, buffers))
-        ]
+        made = []
+        for i, (source, buffer) in enumerate(zip(sources, buffers)):
+            rows = buffer.shape[1] // CUTS
+            for cut in range(CUTS):
+                here = pl.ds(cut * rows, rows)
+                made.append(
+                    pltpu.make_async_copy(
+                        source(step).at[here], buffer.at[slot, here], sems.at[i * CUTS + cut, slot]
+                    )
+                )
+        return made
 
     def start(step):
         for copy in copies(step):
@@ -180,7 +188,7 @@
         + [
             pltpu.VMEM((SLOTS, tile, q_cols), jnp.bfloat16),
             pltpu.VMEM((SLOTS, tile, kv_cols), jnp.bfloat16),
-            pltpu.SemaphoreType.DMA((2, SLOTS)),
+            pltpu.SemaphoreType.DMA((2 * CUTS, SLOTS)),
         ],
         compiler_params=megabytes(16),
         cost_estimate=cost(
@@ -500,7 +508,7 @@
         scratch_shapes=[
             pltpu.VMEM((SEL, depth), attention.dtype),
             pltpu.VMEM((SLOTS, depth, min(WIDTH_TILE, width)), jnp.bfloat16),
-            pltpu.SemaphoreType.DMA((1, SLOTS)),
+            pltpu.SemaphoreType.DMA((CUTS, SLOTS)),
         ],
         compiler_params=megabytes(16),
         cost_estimate=cost(2 * SEL * depth * width, 2 * depth * (width + SEL) + 4 * SEL * width),
@@ -604,16 +612,16 @@
         projected = project(
             place, blocks, w_query, w_keyval, projected, (cosine, sine_part), chunk
         )
-    chunks = [
-        [
-            lax.ppermute(sent[slot * middle + j], "tp", [(i, i ^ j) for i in range(tp_size)])
-            if j
-            else sent[slot * middle]
+    def exchange(kept):
+        return [
+            lax.ppermute(kept[j], "tp", [(i, i ^ j) for i in range(tp_size)]) if j else kept[j]
             for j in range(middle)
         ]
-        for slot in range(2)
-    ]
-    *queries, chunks[1][1] = lax.optimization_barrier((*projected[:HALVES], chunks[1][1]))
+
+    own, partners = sent[:middle], exchange(sent[middle:])
+    own, partners = lax.optimization_barrier((own, partners))
+    chunks = [exchange(own), partners]
+    queries = projected[:HALVES]
     n_tiles = queries[0].shape[0]
     across = [(i, i ^ middle) for i in range(tp_size)]
     their_queries = [None] * HALVES

time: 205 us -> 198 us (0.966)
  waiting for transfers between devices: 83.7 us -> 76.5 us
    ppermute x7, waiting for transfers between devices: 10.3 us -> 3.18 us  [per_device(): held['before'].append(lax.ppermute(held['before'][-1], 'tp', forth))]
    ppermute x2, starting transfers between devices: 0.07 us -> 4.92 us  [per_device(): their_queries[part] = lax.ppermute(queries[part], 'tp', across)]
    ppermute x6, starting transfers between devices: 10.4 us -> 7.34 us  [exchange(): lax.ppermute(kept[j], 'tp', [(i, i ^ j) for i in range(tp_size)])]
    ppermute x14, waiting for transfers between devices: 24.5 us -> 22.4 us  [per_device(): held = lax.ppermute(term.astype(jnp.bfloat16), 'tp', pairs)]
  transfers between devices with their start and end apart: 40 -> 40, of which waited for: 19 -> 18; matrix products, arithmetic and copies ran while one was open for 3% -> 3% of each run, Pallas kernels for 25% -> 26%
where the time goes in v9:
time: 198 us
  waiting for transfers between devices  76.5 us (39%)
  Pallas kernels  57.8 us (29%)
  starting transfers between devices  48.5 us (24%)
  local copies, waits for them, and re-layouts  7.6 us (4%)
  other arithmetic  7.26 us (4%)
    pallas_call x4, Pallas kernels, attend(): pl.pallas_call(functools.partial(attend_kernel, n_chunks, bool(fresh), n_...  31 us
    ppermute x14, waiting for transfers between devices, per_device(): held = lax.ppermute(term.astype(jnp.bfloat16), 'tp', pairs)  22.4 us
    ppermute x14, starting transfers between devices, per_device(): held = lax.ppermute(term.astype(jnp.bfloat16), 'tp', pairs)  15.6 us
    ppermute x6, waiting for transfers between devices, exchange(): lax.ppermute(kept[j], 'tp', [(i, i ^ j) for i in range(tp_size)])  15.6 us
    ppermute x7, waiting for transfers between devices, per_device(): held['behind'].append(lax.ppermute(held['behind'][-1], 'tp', back))  13.9 us
    ppermute x2, waiting for transfers between devices, per_device(): their_queries[part] = lax.ppermute(queries[part], 'tp', across)  13 us
    pallas_call x2, Pallas kernels, project(): pl.pallas_call(functools.partial(project_kernel, len(blocks), chunk, is_l...  13 us
    ppermute x7, starting transfers between devices, per_device(): held['before'].append(lax.ppermute(held['before'][-1], 'tp', forth))  11.5 us
  transfers between devices with their start and end apart: 40, of which 18 were waited for; matrix products, arithmetic and copies ran while one was open for 3% of the time, Pallas kernels for 26%

profile of v9, /device:TPU:0, one launch (start us, length us, event | category | flops | bytes accessed | tf_op | source)
XLA Modules:
  0.0 198.1 jit_solution(9070090975544535804)
XLA Ops:
  0.0 1.2 fusion
  1.3 1.2 fusion.2
  2.5 5.5 %copy.16 = bf16[4,256,2,1024]{3,1,2,0:T(8,128)(2,1)} copy(bf16[4,256,2,1024]{3,2,1,0:T(2,128)(2,1)} %param.15) | data formatting | bytes 8388608 | tf_op jit(solution)/shard_map/optimization_barrier | solution.py:548
  8.0 0.5 collective-permute-start.3
  8.5 2.6 %collective-permute-start = (bf16[32,4096]{1,0:T(8,128)(2,1)S(1)}, bf16[32,4096]{1,0:T(8,128)(2,1)S(1)}, u32[]{:S(2)}, u32[]{:S(2)}) collective-permute-start(bf16[32,4096]{1,0:T(8,128)(2,1)S(1)} %get-tuple-element.140.refs_0_), channel_id=1, source_target_pairs={{0,2},{2,4},{4,6},{6,7},{7,5},{5,3},{3,1},{1,0},{8,10},{10,12},{12... | collective-permute-start | bytes 786440 | tf_op jit(solution)/shard_map/ppermute | solution.py:580
  11.1 2.0 collective-permute-start.11
  13.6 1.3 compare_reduce_fusion
  15.1 0.5 fusion.3
  15.6 2.6 %collective-permute-done.refs_1_ = bf16[32,4096]{1,0:T(8,128)(2,1)S(1)} collective-permute-done((bf16[32,4096]{1,0:T(8,128)(2,1)S(1)}, bf16[32,4096]{1,0:T(8,128)(2,1)S(1)}, u32[]{:S(2)}, u32[]{:S(2)}) %collective-permute-start) | collective-permute-done | bytes 262176 | tf_op jit(solution)/shard_map/ppermute | solution.py:580
  18.2 2.0 %collective-permute-start.1 = (bf16[32,4096]{1,0:T(8,128)(2,1)S(1)}, bf16[32,4096]{1,0:T(8,128)(2,1)S(1)}, u32[]{:S(2)}, u32[]{:S(2)}) collective-permute-start(bf16[32,4096]{1,0:T(8,128)(2,1)S(1)} %collective-permute-done.refs_1_), channel_id=1, source_target_pairs={{0,2},{2,4},{4,6},{6,7},{7,5},{5,3},{3,1},{1,0},{8,10},{10,12},{12... | collective-permute-start | bytes 786440 | tf_op jit(solution)/shard_map/ppermute | solution.py:580
  20.2 0.7 dynamic-slice_bitcast_fusion.place_ref
  21.1 4.1 %collective-permute-done.11.refs_2_ = bf16[32,4096]{1,0:T(8,128)(2,1)S(1)} collective-permute-done((bf16[32,4096]{1,0:T(8,128)(2,1)S(1)}, bf16[32,4096]{1,0:T(8,128)(2,1)S(1)}, u32[]{:S(2)}, u32[]{:S(2)}) %collective-permute-start.11) | collective-permute-done | bytes 262176 | tf_op jit(solution)/shard_map/ppermute | solution.py:582
  25.6 0.5 broadcast.178
  26.2 0.7 reduce.3
  27.0 1.7 collective-permute-start.18
  28.7 0.6 collective-permute-done.1.refs_3_
  29.3 0.6 broadcast_in_dim.20.refs_4_
  29.9 1.8 collective-permute-start.2
  31.8 1.6 collective-permute-start.12
  33.3 1.1 collective-permute-done.13.refs_4_
  34.7 5.4 %collective-permute-done.18.refs_4_ = bf16[32,4096]{1,0:T(8,128)(2,1)S(1)} collective-permute-done((bf16[32,4096]{1,0:T(8,128)(2,1)S(1)}, bf16[32,4096]{1,0:T(8,128)(2,1)S(1)}, u32[]{:S(2)}, u32[]{:S(2)}) %collective-permute-start.18) | collective-permute-done | bytes 262176 | tf_op jit(solution)/shard_map/ppermute | solution.py:582
  40.3 3.3 %select_docs.1 = (bf16[2,4,256,128]{3,2,1,0:T(8,128)(2,1)S(1)}, bf16[2,4,256,128]{3,2,1,0:T(8,128)(2,1)S(1)}, bf16[2,4,256,128]{3,2,1,0:T(8,128)(2,1)S(1)}, bf16...) custom-call(s32[4]{0:T(128)S(1)} %get-tuple-element.76.place_ref, ...), custom_call_target="tpu_custom_call" | custom-call | bytes 8388608 | tf_op jit(solution)/shard_map/select_docs/pallas_call | solution.py:229
  43.6 1.8 collective-permute-start.20
  45.4 1.6 collective-permute-start.14
  47.0 0.4 collective-permute-start.16
  47.5 0.5 collective-permute-start.4
  47.9 3.4 %collective-permute-done.19.refs_6_ = bf16[32,4096]{1,0:T(8,128)(2,1)S(1)} collective-permute-done((bf16[32,4096]{1,0:T(8,128)(2,1)S(1)}, bf16[32,4096]{1,0:T(8,128)(2,1)S(1)}, u32[]{:S(2)}, u32[]{:S(2)}) %collective-permute-start.19) | collective-permute-done | bytes 262176 | tf_op jit(solution)/shard_map/ppermute | solution.py:582
  51.3 1.6 collective-permute-start.5
  52.9 1.8 collective-permute-start.6
  54.7 6.3 %project.2 = (f32[256,1024]{1,0:T(8,128)S(1)}, f32[256,256]{1,0:T(8,128)S(1)}) custom-call(s32[8]{0:T(128)S(1)} %dynamic-slice_bitcast_fusion.place_ref, bf16[32,4096]{1,0:T(8,128)(2,1)S(1)} %get-tuple-element.140.refs_0_, bf16[32,4096]{1,0:T(8,128)(2,1)S(1)} %collective-permute-done.refs_1_, bf16[32,4096]{1,0:T(8,128)(2,1)S(1)} %collective-permute-done.17.refs_2_, ...), custom_call_target="tpu_custom_call" | custom-call | flops 2684354560 | bytes 12582912 | tf_op jit(solution)/shard_map/project/pallas_call | solution.py:179
  61.0 6.7 %project.3 = (bf16[4,128,256]{2,1,0:T(8,128)(2,1)S(1)}, bf16[6,128,256]{2,1,0:T(8,128)(2,1)S(1)}) custom-call(s32[8]{0:T(128)S(1)} %dynamic-slice_bitcast_fusion.place_ref, bf16[32,4096]{1,0:T(8,128)(2,1)S(1)} %get-tuple-element.139.refs_0_, bf16[32,4096]{1,0:T(8,128)(2,1)S(1)} %collective-permute-done.10.refs_1_, ...), custom_call_target="tpu_custom_call" | custom-call | flops 2684354560 | bytes 12582912 | tf_op jit(solution)/shard_map/project/pallas_call | solution.py:179
  67.7 3.6 %collective-permute-start.21 = (bf16[6,128,256]{2,1,0:T(8,128)(2,1)S(1)}, bf16[6,128,256]{2,1,0:T(8,128)(2,1)S(1)}, u32[]{:S(2)}, u32[]{:S(2)}) collective-permute-start(bf16[6,128,256]{2,1,0:T(8,128)(2,1)S(1)} %get-tuple-element.112.here_ref.refs_6_), channel_id=1, source_target_pairs={{0,4},{1,5},{2,6},{3,7},{4,0},{5,1},{6,2},{7,3},{8,12},{9,13},{10,... | collective-permute-start | bytes 1179656 | tf_op jit(solution)/shard_map/ppermute | solution.py:629
  71.3 1.1 collective-permute-done.5.refs_2_
  72.4 14.5 %collective-permute-done.6.refs_3_ = bf16[2,4,256,128]{3,2,1,0:T(8,128)(2,1)S(1)} collective-permute-done((bf16[2,4,256,128]{3,2,1,0:T(8,128)(2,1)S(1)}, bf16[2,4,256,128]{3,2,1,0:T(8,128)(2,1)S(1)}, u32[]{:S(2)}, u32[]{:S(2)}) %collective-permute-start.6) | collective-permute-done | bytes 524320 | tf_op jit(solution)/shard_map/ppermute | solution.py:617
  86.8 0.8 collective-permute-start.7
  87.6 2.7 %collective-permute-start.9 = (bf16[2,4,256,128]{3,2,1,0:T(8,128)(2,1)S(1)}, bf16[2,4,256,128]{3,2,1,0:T(8,128)(2,1)S(1)}, u32[]{:S(2)}, u32[]{:S(2)}) collective-permute-start(bf16[2,4,256,128]{3,2,1,0:T(8,128)(2,1)S(1)} %get-tuple-element.99), channel_id=1, source_target_pairs={{0,3},{1,2},{2,1},{3,0},{4,7},{5,6},{6,5},{7,4},{8,11},{9,10},{10,... | collective-permute-start | bytes 1572872 | tf_op jit(solution)/shard_map/ppermute | solution.py:617
  90.3 1.3 collective-permute-start.23
  91.7 0.7 collective-permute-start.22
  92.4 9.0 %attend.4 = bf16[4,144,256]{2,1,0:T(8,128)(2,1)S(1)} custom-call(s32[16]{0:T(128)S(1)} %select_n.42.first_ref, s32[256]{0:T(256)S(1)} %bitcast.23, bf16[2,4,256,128]{3,2,1,0:T(8,128)(2,1)S(1)} %get-tuple-element.108.refs_0_, bf16[2,4,256,128]{3,2,1,0:T(8,128)(2,1)S(1)} %collective-permute-done.4.refs_1_, ...), custom_call_target="tpu_custom_call" | custom-call | flops 1073741824 | bytes 2097152 | tf_op jit(solution)/shard_map/attend/pallas_call | solution.py:381
  101.3 13.0 %collective-permute-done.23.refs_6_ = bf16[4,128,256]{2,1,0:T(8,128)(2,1)S(1)} collective-permute-done((bf16[4,128,256]{2,1,0:T(8,128)(2,1)S(1)}, bf16[4,128,256]{2,1,0:T(8,128)(2,1)S(1)}, u32[]{:S(2)}, u32[]{:S(2)}) %collective-permute-start.23) | collective-permute-done | bytes 262176 | tf_op jit(solution)/shard_map/ppermute | solution.py:629
  114.3 5.8 %attend.6 = bf16[4,144,256]{2,1,0:T(8,128)(2,1)S(1)} custom-call(s32[16]{0:T(128)S(1)} %select_n.42.first_ref, s32[256]{0:T(256)S(1)} %bitcast.24, bf16[2,4,256,128]{3,2,1,0:T(8,128)(2,1)S(1)} %get-tuple-element.108.refs_0_, bf16[2,4,256,128]{3,2,1,0:T(8,128)(2,1)S(1)} %collective-permute-done.4.refs_1_, ...), custom_call_target="tpu_custom_call" | custom-call | flops 1073741824 | bytes 2097152 | tf_op jit(solution)/shard_map/attend/pallas_call | solution.py:381
  120.1 2.4 %collective-permute-start.24 = (bf16[4,144,256]{2,1,0:T(8,128)(2,1)S(1)}, bf16[4,144,256]{2,1,0:T(8,128)(2,1)S(1)}, u32[]{:S(2)}, u32[]{:S(2)}) collective-permute-start(bf16[4,144,256]{2,1,0:T(8,128)(2,1)S(1)} %attend.6), channel_id=1, source_target_pairs={{0,4},{1,5},{2,6},{3,7},{4,0},{5,1},{6,2},{7,3},{8,12},{9,13},{10,... | collective-permute-start | bytes 884744 | tf_op jit(solution)/shard_map/ppermute | solution.py:660
  122.5 0.6 collective-permute-start.25
  123.1 9.6 %attend.7 = (f32[4,1,256]{2,1,0:T(1,128)S(1)}, f32[4,1,256]{2,1,0:T(1,128)S(1)}, f32[4,128,256]{2,1,0:T(8,128)S(1)}) custom-call(s32[16]{0:T(128)S(1)} %select_n.42.first_ref, s32[256]{0:T(256)S(1)} %bitcast.25, bf16[2,4,256,128]{3,2,1,0:T(8,128)(2,1)S(1)} %get-tuple-element.96.refs_0_, bf16[2,4,256,128]{3,2,1,0:T(8,128)(2,1)S(1)} %collective-permute-done.7.refs_1_, ...), custom_call_target="tpu_custom_call" | custom-call | flops 1073741824 | bytes 2097152 | tf_op jit(solution)/shard_map/attend/pallas_call | solution.py:381
  132.7 6.7 %attend.5 = (f32[4,1,256]{2,1,0:T(1,128)S(1)}, f32[4,1,256]{2,1,0:T(1,128)S(1)}, f32[4,128,256]{2,1,0:T(8,128)S(1)}) custom-call(s32[16]{0:T(128)S(1)} %select_n.42.first_ref, s32[256]{0:T(256)S(1)} %bitcast.26, bf16[2,4,256,128]{3,2,1,0:T(8,128)(2,1)S(1)} %get-tuple-element.96.refs_0_, bf16[2,4,256,128]{3,2,1,0:T(8,128)(2,1)S(1)} %collective-permute-done.7.refs_1_, ...), custom_call_target="tpu_custom_call" | custom-call | flops 1073741824 | bytes 2097152 | tf_op jit(solution)/shard_map/attend/pallas_call | solution.py:381
  139.4 4.3 %collective-permute-done.24.refs_3_ = bf16[4,144,256]{2,1,0:T(8,128)(2,1)S(1)} collective-permute-done((bf16[4,144,256]{2,1,0:T(8,128)(2,1)S(1)}, bf16[4,144,256]{2,1,0:T(8,128)(2,1)S(1)}, u32[]{:S(2)}, u32[]{:S(2)}) %collective-permute-start.24) | collective-permute-done | bytes 294944 | tf_op jit(solution)/shard_map/ppermute | solution.py:660
  143.7 4.2 %collective-permute-done.25.refs_7_ = bf16[4,144,256]{2,1,0:T(8,128)(2,1)S(1)} collective-permute-done((bf16[4,144,256]{2,1,0:T(8,128)(2,1)S(1)}, bf16[4,144,256]{2,1,0:T(8,128)(2,1)S(1)}, u32[]{:S(2)}, u32[]{:S(2)}) %collective-permute-start.25) | collective-permute-done | bytes 294944 | tf_op jit(solution)/shard_map/ppermute | solution.py:660
  148.2 5.1 %project_out.2 = (f32[32,4096]{1,0:T(8,128)S(1)}, f32[32,4096]{1,0:T(8,128)S(1)}, f32[32,4096]{1,0:T(8,128)S(1)}, f32[32,4096]{1,0:T(8,128)S(1)}, f32[32,4096]{1...) custom-call(s32[8]{0:T(128)S(1)} %dynamic-slice_bitcast_fusion.place_ref, ...), custom_call_target="tpu_custom_call" | custom-call | flops 2147483648 | bytes 13107200 | tf_op jit(solution)/shard_map/project_out/pallas_call | solution.py:499
  153.7 2.2 %collective-permute-start.30 = (bf16[32,4096]{1,0:T(8,128)(2,1)S(1)}, bf16[32,4096]{1,0:T(8,128)(2,1)S(1)}, u32[]{:S(2)}, u32[]{:S(2)}) collective-permute-start(bf16[32,4096]{1,0:T(8,128)(2,1)S(1)} %convert_element_type.116), channel_id=1, source_target_pairs={{2,0},{4,2},{6,4},{7,6},{5,7},{3,5},{1,3},{0,1},{10,8},{12,10},{14... | collective-permute-start | bytes 786440 | tf_op jit(solution)/shard_map/ppermute | solution.py:677
  155.9 5.1 %project_out.3 = (f32[32,4096]{1,0:T(8,128)S(1)}, f32[32,4096]{1,0:T(8,128)S(1)}, f32[32,4096]{1,0:T(8,128)S(1)}, f32[32,4096]{1,0:T(8,128)S(1)}, f32[32,4096]{1...) custom-call(s32[8]{0:T(128)S(1)} %dynamic-slice_bitcast_fusion.place_ref, ...), custom_call_target="tpu_custom_call" | custom-call | flops 2147483648 | bytes 13107200 | tf_op jit(solution)/shard_map/project_out/pallas_call | solution.py:499
  161.1 2.1 %collective-permute-start.36 = (bf16[32,4096]{1,0:T(8,128)(2,1)S(1)}, bf16[32,4096]{1,0:T(8,128)(2,1)S(1)}, u32[]{:S(2)}, u32[]{:S(2)}) collective-permute-start(bf16[32,4096]{1,0:T(8,128)(2,1)S(1)} %get-tuple-element.138), channel_id=1, source_target_pairs={{2,0},{4,2},{6,4},{7,6},{5,7},{3,5},{1,3},{0,1},{10,8},{12,10},{14... | collective-permute-start | bytes 786440 | tf_op jit(solution)/shard_map/ppermute | solution.py:677
  163.3 2.1 %collective-permute-start.31 = (bf16[32,4096]{1,0:T(8,128)(2,1)S(1)}, bf16[32,4096]{1,0:T(8,128)(2,1)S(1)}, u32[]{:S(2)}, u32[]{:S(2)}) collective-permute-start(bf16[32,4096]{1,0:T(8,128)(2,1)S(1)} %add_convert_fusion.8), channel_id=1, source_target_pairs={{2,0},{4,2},{6,4},{7,6},{5,7},{3,5},{1,3},{0,1},{10,8},{12,10},{14... | collective-permute-start | bytes 786440 | tf_op jit(solution)/shard_map/ppermute | solution.py:677
  165.4 4.9 %collective-permute-done.33 = bf16[32,4096]{1,0:T(8,128)(2,1)S(1)} collective-permute-done((bf16[32,4096]{1,0:T(8,128)(2,1)S(1)}, bf16[32,4096]{1,0:T(8,128)(2,1)S(1)}, u32[]{:S(2)}, u32[]{:S(2)}) %collective-permute-start.33) | collective-permute-done | bytes 262176 | tf_op jit(solution)/shard_map/ppermute | solution.py:677
  170.5 2.1 %collective-permute-start.37 = (bf16[32,4096]{1,0:T(8,128)(2,1)S(1)}, bf16[32,4096]{1,0:T(8,128)(2,1)S(1)}, u32[]{:S(2)}, u32[]{:S(2)}) collective-permute-start(bf16[32,4096]{1,0:T(8,128)(2,1)S(1)} %add_convert_fusion.3), channel_id=1, source_target_pairs={{2,0},{4,2},{6,4},{7,6},{5,7},{3,5},{1,3},{0,1},{10,8},{12,10},{14... | collective-permute-start | bytes 786440 | tf_op jit(solution)/shard_map/ppermute | solution.py:677
  172.5 3.4 %collective-permute-done.27 = bf16[32,4096]{1,0:T(8,128)(2,1)S(1)} collective-permute-done((bf16[32,4096]{1,0:T(8,128)(2,1)S(1)}, bf16[32,4096]{1,0:T(8,128)(2,1)S(1)}, u32[]{:S(2)}, u32[]{:S(2)}) %collective-permute-start.27) | collective-permute-done | bytes 262176 | tf_op jit(solution)/shard_map/ppermute | solution.py:677
  176.1 2.1 %collective-permute-start.32 = (bf16[32,4096]{1,0:T(8,128)(2,1)S(1)}, bf16[32,4096]{1,0:T(8,128)(2,1)S(1)}, u32[]{:S(2)}, u32[]{:S(2)}) collective-permute-start(bf16[32,4096]{1,0:T(8,128)(2,1)S(1)} %add_convert_fusion.7), channel_id=1, source_target_pairs={{2,0},{4,2},{6,4},{7,6},{5,7},{3,5},{1,3},{0,1},{10,8},{12,10},{14... | collective-permute-start | bytes 786440 | tf_op jit(solution)/shard_map/ppermute | solution.py:677
  178.1 3.4 %collective-permute-done.34 = bf16[32,4096]{1,0:T(8,128)(2,1)S(1)} collective-permute-done((bf16[32,4096]{1,0:T(8,128)(2,1)S(1)}, bf16[32,4096]{1,0:T(8,128)(2,1)S(1)}, u32[]{:S(2)}, u32[]{:S(2)}) %collective-permute-start.34) | collective-permute-done | bytes 262176 | tf_op jit(solution)/shard_map/ppermute | solution.py:677
  181.7 2.1 %collective-permute-start.38 = (bf16[32,4096]{1,0:T(8,128)(2,1)S(1)}, bf16[32,4096]{1,0:T(8,128)(2,1)S(1)}, u32[]{:S(2)}, u32[]{:S(2)}) collective-permute-start(bf16[32,4096]{1,0:T(8,128)(2,1)S(1)} %add_convert_fusion.2), channel_id=1, source_target_pairs={{2,0},{4,2},{6,4},{7,6},{5,7},{3,5},{1,3},{0,1},{10,8},{12,10},{14... | collective-permute-start | bytes 786440 | tf_op jit(solution)/shard_map/ppermute | solution.py:677
  183.8 3.4 %collective-permute-done.28 = bf16[32,4096]{1,0:T(8,128)(2,1)S(1)} collective-permute-done((bf16[32,4096]{1,0:T(8,128)(2,1)S(1)}, bf16[32,4096]{1,0:T(8,128)(2,1)S(1)}, u32[]{:S(2)}, u32[]{:S(2)}) %collective-permute-start.28) | collective-permute-done | bytes 262176 | tf_op jit(solution)/shard_map/ppermute | solution.py:677
  187.3 2.3 %collective-permute-done.38 = bf16[32,4096]{1,0:T(8,128)(2,1)S(1)} collective-permute-done((bf16[32,4096]{1,0:T(8,128)(2,1)S(1)}, bf16[32,4096]{1,0:T(8,128)(2,1)S(1)}, u32[]{:S(2)}, u32[]{:S(2)}) %collective-permute-start.38) | collective-permute-done | bytes 262176 | tf_op jit(solution)/shard_map/ppermute | solution.py:677
  189.6 2.4 %collective-permute-start.39 = (bf16[32,4096]{1,0:T(8,128)(2,1)S(1)}, bf16[32,4096]{1,0:T(8,128)(2,1)S(1)}, u32[]{:S(2)}, u32[]{:S(2)}) collective-permute-start(bf16[32,4096]{1,0:T(8,128)(2,1)S(1)} %add_convert_fusion.1), channel_id=1, source_target_pairs={{2,0},{4,2},{6,4},{7,6},{5,7},{3,5},{1,3},{0,1},{10,8},{12,10},{14... | collective-permute-start | bytes 786440 | tf_op jit(solution)/shard_map/ppermute | solution.py:677
  192.1 2.7 %collective-permute-done.29 = bf16[32,4096]{1,0:T(8,128)(2,1)S(1)} collective-permute-done((bf16[32,4096]{1,0:T(8,128)(2,1)S(1)}, bf16[32,4096]{1,0:T(8,128)(2,1)S(1)}, u32[]{:S(2)}, u32[]{:S(2)}) %collective-permute-start.29) | collective-permute-done | bytes 262176 | tf_op jit(solution)/shard_map/ppermute | solution.py:677
  194.8 2.4 %collective-permute-done.39 = bf16[32,4096]{1,0:T(8,128)(2,1)S(1)} collective-permute-done((bf16[32,4096]{1,0:T(8,128)(2,1)S(1)}, bf16[32,4096]{1,0:T(8,128)(2,1)S(1)}, u32[]{:S(2)}, u32[]{:S(2)}) %collective-permute-start.39) | collective-permute-done | bytes 262176 | tf_op jit(solution)/shard_map/ppermute | solution.py:677
  197.3 0.8 pad_maximum_fusion
  (79 shorter events, 3.8 us)
Async XLA Ops:
  2.5 10.7 %copy-start = (s32[1,256]{1,0:T(1,128)S(1)}, s32[1,256]{1,0:T(1,128)}, u32[]{:S(2)}) copy-start(s32[1,256]{1,0:T(1,128)} %param.18) | copy-start | bytes 3076
  2.5 10.7 %copy-start.1 = (s32[1,4]{1,0:T(1,128)S(1)}, s32[1,4]{1,0:T(1,128)}, u32[]{:S(2)}) copy-start(s32[1,4]{1,0:T(1,128)} %param.17) | copy-start | bytes 52
  2.5 13.1 %copy-start.2 = (s32[4]{0:T(128)S(1)}, s32[4]{0:T(128)}, u32[]{:S(2)}) copy-start(s32[4]{0:T(128)} %param.16) | copy-start | bytes 52
  8.0 32.3 %collective-permute-start.3 = (bf16[4,2,256,1024]{3,2,1,0:T(8,128)(2,1)}, bf16[4,2,256,1024]{3,2,1,0:T(8,128)(2,1)}, u32[]{:S(2)}, u32[]{:S(2)}) collective-permute-start(bf16[4,2,256,1024]{3,2,1,0:T(8,128)(2,1)} %bitcast.20.refs_0_), channel_id=1, source_target_pairs={{8,0},{0,8},{9,1},{1,9},{10,2},{2,10},{11,3},{3,11},{12,4},{4,12},... | collective-permute-start | bytes 12582920 | tf_op jit(solution)/shard_map/ppermute | solution.py:589
  8.5 9.7 %collective-permute-start = (bf16[32,4096]{1,0:T(8,128)(2,1)S(1)}, bf16[32,4096]{1,0:T(8,128)(2,1)S(1)}, u32[]{:S(2)}, u32[]{:S(2)}) collective-permute-start(bf16[32,4096]{1,0:T(8,128)(2,1)S(1)} %get-tuple-element.140.refs_0_), channel_id=1, source_target_pairs={{0,2},{2,4},{4,6},{6,7},{7,5},{5,3},{3,1},{1,0},{8,10},{10,12},{12... | collective-permute-start | bytes 786440 | tf_op jit(solution)/shard_map/ppermute | solution.py:580
  11.1 15.9 %collective-permute-start.17 = (bf16[32,4096]{1,0:T(8,128)(2,1)S(1)}, bf16[32,4096]{1,0:T(8,128)(2,1)S(1)}, u32[]{:S(2)}, u32[]{:S(2)}) collective-permute-start(bf16[32,4096]{1,0:T(8,128)(2,1)S(1)} %get-tuple-element.140.refs_0_), channel_id=1, source_target_pairs={{2,0},{4,2},{6,4},{7,6},{5,7},{3,5},{1,3},{0,1},{10,8},{12,10},{14... | collective-permute-start | bytes 786440 | tf_op jit(solution)/shard_map/ppermute | solution.py:582
  11.1 14.0 %collective-permute-start.11 = (bf16[32,4096]{1,0:T(8,128)(2,1)S(1)}, bf16[32,4096]{1,0:T(8,128)(2,1)S(1)}, u32[]{:S(2)}, u32[]{:S(2)}) collective-permute-start(bf16[32,4096]{1,0:T(8,128)(2,1)S(1)} %get-tuple-element.139.refs_0_), channel_id=1, source_target_pairs={{2,0},{4,2},{6,4},{7,6},{5,7},{3,5},{1,3},{0,1},{10,8},{12,10},{14... | collective-permute-start | bytes 786440 | tf_op jit(solution)/shard_map/ppermute | solution.py:582
  13.1 18.6 %collective-permute-start.10 = (bf16[32,4096]{1,0:T(8,128)(2,1)S(1)}, bf16[32,4096]{1,0:T(8,128)(2,1)S(1)}, u32[]{:S(2)}, u32[]{:S(2)}) collective-permute-start(bf16[32,4096]{1,0:T(8,128)(2,1)S(1)} %get-tuple-element.139.refs_0_), channel_id=1, source_target_pairs={{0,2},{2,4},{4,6},{6,7},{7,5},{5,3},{3,1},{1,0},{8,10},{10,12},{12... | collective-permute-start | bytes 786440 | tf_op jit(solution)/shard_map/ppermute | solution.py:580
  18.2 11.1 %collective-permute-start.1 = (bf16[32,4096]{1,0:T(8,128)(2,1)S(1)}, bf16[32,4096]{1,0:T(8,128)(2,1)S(1)}, u32[]{:S(2)}, u32[]{:S(2)}) collective-permute-start(bf16[32,4096]{1,0:T(8,128)(2,1)S(1)} %collective-permute-done.refs_1_), channel_id=1, source_target_pairs={{0,2},{2,4},{4,6},{6,7},{7,5},{5,3},{3,1},{1,0},{8,10},{10,12},{12... | collective-permute-start | bytes 786440 | tf_op jit(solution)/shard_map/ppermute | solution.py:580
  25.2 9.2 %collective-permute-start.13 = (bf16[32,4096]{1,0:T(8,128)(2,1)S(1)}, bf16[32,4096]{1,0:T(8,128)(2,1)S(1)}, u32[]{:S(2)}, u32[]{:S(2)}) collective-permute-start(bf16[32,4096]{1,0:T(8,128)(2,1)S(1)} %collective-permute-done.11.refs_2_), channel_id=1, source_target_pairs={{2,0},{4,2},{6,4},{7,6},{5,7},{3,5},{1,3},{0,1},{10,8},{12,10},{14... | collective-permute-start | bytes 786440 | tf_op jit(solution)/shard_map/ppermute | solution.py:582
  27.0 13.0 %collective-permute-start.18 = (bf16[32,4096]{1,0:T(8,128)(2,1)S(1)}, bf16[32,4096]{1,0:T(8,128)(2,1)S(1)}, u32[]{:S(2)}, u32[]{:S(2)}) collective-permute-start(bf16[32,4096]{1,0:T(8,128)(2,1)S(1)} %collective-permute-done.17.refs_2_), channel_id=1, source_target_pairs={{2,0},{4,2},{6,4},{7,6},{5,7},{3,5},{1,3},{0,1},{10,8},{12,10},{14... | collective-permute-start | bytes 786440 | tf_op jit(solution)/shard_map/ppermute | solution.py:582
  29.9 13.7 %collective-permute-start.2 = (bf16[32,4096]{1,0:T(8,128)(2,1)S(1)}, bf16[32,4096]{1,0:T(8,128)(2,1)S(1)}, u32[]{:S(2)}, u32[]{:S(2)}) collective-permute-start(bf16[32,4096]{1,0:T(8,128)(2,1)S(1)} %collective-permute-done.1.refs_3_), channel_id=1, source_target_pairs={{0,2},{2,4},{4,6},{6,7},{7,5},{5,3},{3,1},{1,0},{8,10},{10,12},{12... | collective-permute-start | bytes 786440 | tf_op jit(solution)/shard_map/ppermute | solution.py:580
  31.8 13.7 %collective-permute-start.12 = (bf16[32,4096]{1,0:T(8,128)(2,1)S(1)}, bf16[32,4096]{1,0:T(8,128)(2,1)S(1)}, u32[]{:S(2)}, u32[]{:S(2)}) collective-permute-start(bf16[32,4096]{1,0:T(8,128)(2,1)S(1)} %collective-permute-done.10.refs_1_), channel_id=1, source_target_pairs={{0,2},{2,4},{4,6},{6,7},{7,5},{5,3},{3,1},{1,0},{8,10},{10,12},{12... | collective-permute-start | bytes 786440 | tf_op jit(solution)/shard_map/ppermute | solution.py:580
  34.4 12.6 %collective-permute-start.15 = (bf16[32,4096]{1,0:T(8,128)(2,1)S(1)}, bf16[32,4096]{1,0:T(8,128)(2,1)S(1)}, u32[]{:S(2)}, u32[]{:S(2)}) collective-permute-start(bf16[32,4096]{1,0:T(8,128)(2,1)S(1)} %collective-permute-done.13.refs_4_), channel_id=1, source_target_pairs={{2,0},{4,2},{6,4},{7,6},{5,7},{3,5},{1,3},{0,1},{10,8},{12,10},{14... | collective-permute-start | bytes 786440 | tf_op jit(solution)/shard_map/ppermute | solution.py:582
  40.1 11.2 %collective-permute-start.19 = (bf16[32,4096]{1,0:T(8,128)(2,1)S(1)}, bf16[32,4096]{1,0:T(8,128)(2,1)S(1)}, u32[]{:S(2)}, u32[]{:S(2)}) collective-permute-start(bf16[32,4096]{1,0:T(8,128)(2,1)S(1)} %collective-permute-done.18.refs_4_), channel_id=1, source_target_pairs={{2,0},{4,2},{6,4},{7,6},{5,7},{3,5},{1,3},{0,1},{10,8},{12,10},{14... | collective-permute-start | bytes 786440 | tf_op jit(solution)/shard_map/ppermute | solution.py:582
  43.6 9.3 %collective-permute-start.20 = (bf16[32,4096]{1,0:T(8,128)(2,1)S(1)}, bf16[32,4096]{1,0:T(8,128)(2,1)S(1)}, u32[]{:S(2)}, u32[]{:S(2)}) collective-permute-start(bf16[32,4096]{1,0:T(8,128)(2,1)S(1)} %collective-permute-done.2.refs_5_), channel_id=1, source_target_pairs={{0,2},{2,4},{4,6},{6,7},{7,5},{5,3},{3,1},{1,0},{8,10},{10,12},{12... | collective-permute-start | bytes 786440 | tf_op jit(solution)/shard_map/ppermute | solution.py:580
  45.4 15.5 %collective-permute-start.14 = (bf16[32,4096]{1,0:T(8,128)(2,1)S(1)}, bf16[32,4096]{1,0:T(8,128)(2,1)S(1)}, u32[]{:S(2)}, u32[]{:S(2)}) collective-permute-start(bf16[32,4096]{1,0:T(8,128)(2,1)S(1)} %collective-permute-done.12.refs_3_), channel_id=1, source_target_pairs={{0,2},{2,4},{4,6},{6,7},{7,5},{5,3},{3,1},{1,0},{8,10},{10,12},{12... | collective-permute-start | bytes 786440 | tf_op jit(solution)/shard_map/ppermute | solution.py:580
  47.0 14.0 %collective-permute-start.16 = (bf16[32,4096]{1,0:T(8,128)(2,1)S(1)}, bf16[32,4096]{1,0:T(8,128)(2,1)S(1)}, u32[]{:S(2)}, u32[]{:S(2)}) collective-permute-start(bf16[32,4096]{1,0:T(8,128)(2,1)S(1)} %collective-permute-done.15.refs_6_), channel_id=1, source_target_pairs={{2,0},{4,2},{6,4},{7,6},{5,7},{3,5},{1,3},{0,1},{10,8},{12,10},{14... | collective-permute-start | bytes 786440 | tf_op jit(solution)/shard_map/ppermute | solution.py:582
  47.5 23.8 %collective-permute-start.4 = (bf16[2,4,256,128]{3,2,1,0:T(8,128)(2,1)S(1)}, bf16[2,4,256,128]{3,2,1,0:T(8,128)(2,1)S(1)}, u32[]{:S(2)}, u32[]{:S(2)}) collective-permute-start(bf16[2,4,256,128]{3,2,1,0:T(8,128)(2,1)S(1)} %get-tuple-element.93), channel_id=1, source_target_pairs={{0,1},{1,0},{2,3},{3,2},{4,5},{5,4},{6,7},{7,6},{8,9},{9,8},{10,11... | collective-permute-start | bytes 1572872 | tf_op jit(solution)/shard_map/ppermute | solution.py:617
  51.3 21.1 %collective-permute-start.5 = (bf16[2,4,256,128]{3,2,1,0:T(8,128)(2,1)S(1)}, bf16[2,4,256,128]{3,2,1,0:T(8,128)(2,1)S(1)}, u32[]{:S(2)}, u32[]{:S(2)}) collective-permute-start(bf16[2,4,256,128]{3,2,1,0:T(8,128)(2,1)S(1)} %get-tuple-element.94), channel_id=1, source_target_pairs={{0,2},{1,3},{2,0},{3,1},{4,6},{5,7},{6,4},{7,5},{8,10},{9,11},{10,... | collective-permute-start | bytes 1572872 | tf_op jit(solution)/shard_map/ppermute | solution.py:617
  52.9 33.9 %collective-permute-start.6 = (bf16[2,4,256,128]{3,2,1,0:T(8,128)(2,1)S(1)}, bf16[2,4,256,128]{3,2,1,0:T(8,128)(2,1)S(1)}, u32[]{:S(2)}, u32[]{:S(2)}) collective-permute-start(bf16[2,4,256,128]{3,2,1,0:T(8,128)(2,1)S(1)} %get-tuple-element.95), channel_id=1, source_target_pairs={{0,3},{1,2},{2,1},{3,0},{4,7},{5,6},{6,5},{7,4},{8,11},{9,10},{10,... | collective-permute-start | bytes 1572872 | tf_op jit(solution)/shard_map/ppermute | solution.py:617
  67.7 24.0 %collective-permute-start.21 = (bf16[6,128,256]{2,1,0:T(8,128)(2,1)S(1)}, bf16[6,128,256]{2,1,0:T(8,128)(2,1)S(1)}, u32[]{:S(2)}, u32[]{:S(2)}) collective-permute-start(bf16[6,128,256]{2,1,0:T(8,128)(2,1)S(1)} %get-tuple-element.112.here_ref.refs_6_), channel_id=1, source_target_pairs={{0,4},{1,5},{2,6},{3,7},{4,0},{5,1},{6,2},{7,3},{8,12},{9,13},{10,... | collective-permute-start | bytes 1179656 | tf_op jit(solution)/shard_map/ppermute | solution.py:629
  86.8 36.3 %collective-permute-start.7 = (bf16[2,4,256,128]{3,2,1,0:T(8,128)(2,1)S(1)}, bf16[2,4,256,128]{3,2,1,0:T(8,128)(2,1)S(1)}, u32[]{:S(2)}, u32[]{:S(2)}) collective-permute-start(bf16[2,4,256,128]{3,2,1,0:T(8,128)(2,1)S(1)} %get-tuple-element.97), channel_id=1, source_target_pairs={{0,1},{1,0},{2,3},{3,2},{4,5},{5,4},{6,7},{7,6},{8,9},{9,8},{10,11... | collective-permute-start | bytes 1572872 | tf_op jit(solution)/shard_map/ppermute | solution.py:617
  87.6 35.5 %collective-permute-start.8 = (bf16[2,4,256,128]{3,2,1,0:T(8,128)(2,1)S(1)}, bf16[2,4,256,128]{3,2,1,0:T(8,128)(2,1)S(1)}, u32[]{:S(2)}, u32[]{:S(2)}) collective-permute-start(bf16[2,4,256,128]{3,2,1,0:T(8,128)(2,1)S(1)} %get-tuple-element.98), channel_id=1, source_target_pairs={{0,2},{1,3},{2,0},{3,1},{4,6},{5,7},{6,4},{7,5},{8,10},{9,11},{10,... | collective-permute-start | bytes 1572872 | tf_op jit(solution)/shard_map/ppermute | solution.py:617
  87.6 35.5 %collective-permute-start.9 = (bf16[2,4,256,128]{3,2,1,0:T(8,128)(2,1)S(1)}, bf16[2,4,256,128]{3,2,1,0:T(8,128)(2,1)S(1)}, u32[]{:S(2)}, u32[]{:S(2)}) collective-permute-start(bf16[2,4,256,128]{3,2,1,0:T(8,128)(2,1)S(1)} %get-tuple-element.99), channel_id=1, source_target_pairs={{0,3},{1,2},{2,1},{3,0},{4,7},{5,6},{6,5},{7,4},{8,11},{9,10},{10,... | collective-permute-start | bytes 1572872 | tf_op jit(solution)/shard_map/ppermute | solution.py:617
  90.3 24.0 %collective-permute-start.23 = (bf16[4,128,256]{2,1,0:T(8,128)(2,1)S(1)}, bf16[4,128,256]{2,1,0:T(8,128)(2,1)S(1)}, u32[]{:S(2)}, u32[]{:S(2)}) collective-permute-start(bf16[4,128,256]{2,1,0:T(8,128)(2,1)S(1)} %get-tuple-element.107.refs_6_), channel_id=1, source_target_pairs={{0,4},{1,5},{2,6},{3,7},{4,0},{5,1},{6,2},{7,3},{8,12},{9,13},{10,... | collective-permute-start | bytes 786440 | tf_op jit(solution)/shard_map/ppermute | solution.py:629
  91.7 22.7 %collective-permute-start.22 = (bf16[256,256]{1,0:T(8,128)(2,1)S(1)}, bf16[256,256]{1,0:T(8,128)(2,1)S(1)}, u32[]{:S(2)}, u32[]{:S(2)}) collective-permute-start(bf16[256,256]{1,0:T(8,128)(2,1)S(1)} %pick_new.1), channel_id=1, source_target_pairs={{0,0},{1,2},{2,4},{3,6},{4,1},{5,3},{6,5},{7,7},{8,8},{9,10},{10,1... | collective-permute-start | bytes 393224 | tf_op jit(solution)/shard_map/ppermute | solution.py:632
  120.1 23.5 %collective-permute-start.24 = (bf16[4,144,256]{2,1,0:T(8,128)(2,1)S(1)}, bf16[4,144,256]{2,1,0:T(8,128)(2,1)S(1)}, u32[]{:S(2)}, u32[]{:S(2)}) collective-permute-start(bf16[4,144,256]{2,1,0:T(8,128)(2,1)S(1)} %attend.6), channel_id=1, source_target_pairs={{0,4},{1,5},{2,6},{3,7},{4,0},{5,1},{6,2},{7,3},{8,12},{9,13},{10,... | collective-permute-start | bytes 884744 | tf_op jit(solution)/shard_map/ppermute | solution.py:660
  122.5 25.3 %collective-permute-start.25 = (bf16[4,144,256]{2,1,0:T(8,128)(2,1)S(1)}, bf16[4,144,256]{2,1,0:T(8,128)(2,1)S(1)}, u32[]{:S(2)}, u32[]{:S(2)}) collective-permute-start(bf16[4,144,256]{2,1,0:T(8,128)(2,1)S(1)} %attend.4), channel_id=1, source_target_pairs={{0,4},{1,5},{2,6},{3,7},{4,0},{5,1},{6,2},{7,3},{8,12},{9,13},{10,... | collective-permute-start | bytes 884744 | tf_op jit(solution)/shard_map/ppermute | solution.py:660
  153.3 9.8 %collective-permute-start.26 = (bf16[32,4096]{1,0:T(8,128)(2,1)S(1)}, bf16[32,4096]{1,0:T(8,128)(2,1)S(1)}, u32[]{:S(2)}, u32[]{:S(2)}) collective-permute-start(bf16[32,4096]{1,0:T(8,128)(2,1)S(1)} %get-tuple-element.127), channel_id=1, source_target_pairs={{0,2},{2,4},{4,6},{6,7},{7,5},{5,3},{3,1},{1,0},{8,10},{10,12},{12... | collective-permute-start | bytes 786440 | tf_op jit(solution)/shard_map/ppermute | solution.py:677
  153.7 9.6 %collective-permute-start.30 = (bf16[32,4096]{1,0:T(8,128)(2,1)S(1)}, bf16[32,4096]{1,0:T(8,128)(2,1)S(1)}, u32[]{:S(2)}, u32[]{:S(2)}) collective-permute-start(bf16[32,4096]{1,0:T(8,128)(2,1)S(1)} %convert_element_type.116), channel_id=1, source_target_pairs={{2,0},{4,2},{6,4},{7,6},{5,7},{3,5},{1,3},{0,1},{10,8},{12,10},{14... | collective-permute-start | bytes 786440 | tf_op jit(solution)/shard_map/ppermute | solution.py:677
  161.0 9.3 %collective-permute-start.33 = (bf16[32,4096]{1,0:T(8,128)(2,1)S(1)}, bf16[32,4096]{1,0:T(8,128)(2,1)S(1)}, u32[]{:S(2)}, u32[]{:S(2)}) collective-permute-start(bf16[32,4096]{1,0:T(8,128)(2,1)S(1)} %convert_element_type.123), channel_id=1, source_target_pairs={{0,2},{2,4},{4,6},{6,7},{7,5},{5,3},{3,1},{1,0},{8,10},{10,12},{12... | collective-permute-start | bytes 786440 | tf_op jit(solution)/shard_map/ppermute | solution.py:677
  161.1 9.3 %collective-permute-start.36 = (bf16[32,4096]{1,0:T(8,128)(2,1)S(1)}, bf16[32,4096]{1,0:T(8,128)(2,1)S(1)}, u32[]{:S(2)}, u32[]{:S(2)}) collective-permute-start(bf16[32,4096]{1,0:T(8,128)(2,1)S(1)} %get-tuple-element.138), channel_id=1, source_target_pairs={{2,0},{4,2},{6,4},{7,6},{5,7},{3,5},{1,3},{0,1},{10,8},{12,10},{14... | collective-permute-start | bytes 786440 | tf_op jit(solution)/shard_map/ppermute | solution.py:677
  163.2 12.7 %collective-permute-start.27 = (bf16[32,4096]{1,0:T(8,128)(2,1)S(1)}, bf16[32,4096]{1,0:T(8,128)(2,1)S(1)}, u32[]{:S(2)}, u32[]{:S(2)}) collective-permute-start(bf16[32,4096]{1,0:T(8,128)(2,1)S(1)} %add_convert_fusion.11), channel_id=1, source_target_pairs={{0,2},{2,4},{4,6},{6,7},{7,5},{5,3},{3,1},{1,0},{8,10},{10,12},{12... | collective-permute-start | bytes 786440 | tf_op jit(solution)/shard_map/ppermute | solution.py:677
  163.3 12.7 %collective-permute-start.31 = (bf16[32,4096]{1,0:T(8,128)(2,1)S(1)}, bf16[32,4096]{1,0:T(8,128)(2,1)S(1)}, u32[]{:S(2)}, u32[]{:S(2)}) collective-permute-start(bf16[32,4096]{1,0:T(8,128)(2,1)S(1)} %add_convert_fusion.8), channel_id=1, source_target_pairs={{2,0},{4,2},{6,4},{7,6},{5,7},{3,5},{1,3},{0,1},{10,8},{12,10},{14... | collective-permute-start | bytes 786440 | tf_op jit(solution)/shard_map/ppermute | solution.py:677
  170.3 11.2 %collective-permute-start.34 = (bf16[32,4096]{1,0:T(8,128)(2,1)S(1)}, bf16[32,4096]{1,0:T(8,128)(2,1)S(1)}, u32[]{:S(2)}, u32[]{:S(2)}) collective-permute-start(bf16[32,4096]{1,0:T(8,128)(2,1)S(1)} %add_convert_fusion.5), channel_id=1, source_target_pairs={{0,2},{2,4},{4,6},{6,7},{7,5},{5,3},{3,1},{1,0},{8,10},{10,12},{12... | collective-permute-start | bytes 786440 | tf_op jit(solution)/shard_map/ppermute | solution.py:677
  170.5 11.2 %collective-permute-start.37 = (bf16[32,4096]{1,0:T(8,128)(2,1)S(1)}, bf16[32,4096]{1,0:T(8,128)(2,1)S(1)}, u32[]{:S(2)}, u32[]{:S(2)}) collective-permute-start(bf16[32,4096]{1,0:T(8,128)(2,1)S(1)} %add_convert_fusion.3), channel_id=1, source_target_pairs={{2,0},{4,2},{6,4},{7,6},{5,7},{3,5},{1,3},{0,1},{10,8},{12,10},{14... | collective-permute-start | bytes 786440 | tf_op jit(solution)/shard_map/ppermute | solution.py:677
  176.0 11.2 %collective-permute-start.28 = (bf16[32,4096]{1,0:T(8,128)(2,1)S(1)}, bf16[32,4096]{1,0:T(8,128)(2,1)S(1)}, u32[]{:S(2)}, u32[]{:S(2)}) collective-permute-start(bf16[32,4096]{1,0:T(8,128)(2,1)S(1)} %add_convert_fusion.10), channel_id=1, source_target_pairs={{0,2},{2,4},{4,6},{6,7},{7,5},{5,3},{3,1},{1,0},{8,10},{10,12},{12... | collective-permute-start | bytes 786440 | tf_op jit(solution)/shard_map/ppermute | solution.py:677
  176.1 16.0 %collective-permute-start.32 = (bf16[32,4096]{1,0:T(8,128)(2,1)S(1)}, bf16[32,4096]{1,0:T(8,128)(2,1)S(1)}, u32[]{:S(2)}, u32[]{:S(2)}) collective-permute-start(bf16[32,4096]{1,0:T(8,128)(2,1)S(1)} %add_convert_fusion.7), channel_id=1, source_target_pairs={{2,0},{4,2},{6,4},{7,6},{5,7},{3,5},{1,3},{0,1},{10,8},{12,10},{14... | collective-permute-start | bytes 786440 | tf_op jit(solution)/shard_map/ppermute | solution.py:677
  181.6 13.2 %collective-permute-start.35 = (bf16[32,4096]{1,0:T(8,128)(2,1)S(1)}, bf16[32,4096]{1,0:T(8,128)(2,1)S(1)}, u32[]{:S(2)}, u32[]{:S(2)}) collective-permute-start(bf16[32,4096]{1,0:T(8,128)(2,1)S(1)} %add_convert_fusion.4), channel_id=1, source_target_pairs={{0,2},{2,4},{4,6},{6,7},{7,5},{5,3},{3,1},{1,0},{8,10},{10,12},{12... | collective-permute-start | bytes 786440 | tf_op jit(solution)/shard_map/ppermute | solution.py:677
  181.7 7.9 %collective-permute-start.38 = (bf16[32,4096]{1,0:T(8,128)(2,1)S(1)}, bf16[32,4096]{1,0:T(8,128)(2,1)S(1)}, u32[]{:S(2)}, u32[]{:S(2)}) collective-permute-start(bf16[32,4096]{1,0:T(8,128)(2,1)S(1)} %add_convert_fusion.2), channel_id=1, source_target_pairs={{2,0},{4,2},{6,4},{7,6},{5,7},{3,5},{1,3},{0,1},{10,8},{12,10},{14... | collective-permute-start | bytes 786440 | tf_op jit(solution)/shard_map/ppermute | solution.py:677
  187.2 7.5 %collective-permute-start.29 = (bf16[32,4096]{1,0:T(8,128)(2,1)S(1)}, bf16[32,4096]{1,0:T(8,128)(2,1)S(1)}, u32[]{:S(2)}, u32[]{:S(2)}) collective-permute-start(bf16[32,4096]{1,0:T(8,128)(2,1)S(1)} %add_convert_fusion.9), channel_id=1, source_target_pairs={{0,2},{2,4},{4,6},{6,7},{7,5},{5,3},{3,1},{1,0},{8,10},{10,12},{12... | collective-permute-start | bytes 786440 | tf_op jit(solution)/shard_map/ppermute | solution.py:677
  189.6 7.5 %collective-permute-start.39 = (bf16[32,4096]{1,0:T(8,128)(2,1)S(1)}, bf16[32,4096]{1,0:T(8,128)(2,1)S(1)}, u32[]{:S(2)}, u32[]{:S(2)}) collective-permute-start(bf16[32,4096]{1,0:T(8,128)(2,1)S(1)} %add_convert_fusion.1), channel_id=1, source_target_pairs={{2,0},{4,2},{6,4},{7,6},{5,7},{3,5},{1,3},{0,1},{10,8},{12,10},{14... | collective-permute-start | bytes 786440 | tf_op jit(solution)/shard_map/ppermute | solution.py:677

commit v10 on v9

--- a/solution.py
+++ b/solution.py
@@ -198,42 +198,48 @@
     )(place, *blocks, w_query, w_keyval, *extra)
 
 
-def select_kernel(n_dest, n_src, place_ref, slot_ref, head_ref, *refs):
+def select_kernel(targets_of, n_src, place_ref, slot_ref, head_ref, *refs):
     sources = refs[:n_src]
-    outs = refs[n_src : n_src + n_dest]
-    sems = refs[n_src + n_dest]
+    outs = refs[n_src:-1]
+    sems = refs[-1]
+    targets = [
+        outs[out] if slot is None else outs[out].at[slot] for out, slot in targets_of
+    ]
     for doc in range(DOCS):
         for src in range(n_src):
 
             @pl.when(place_ref[doc] == src)
             def _():
-                for dest in range(n_dest):
-                    cols = pl.ds(pl.multiple_of(head_ref[dest] * HD, HD), HD)
+                for i, target in enumerate(targets):
+                    cols = pl.ds(pl.multiple_of(head_ref[i] * HD, HD), HD)
                     pltpu.make_async_copy(
-                        sources[src].at[slot_ref[doc], :, :, cols],
-                        outs[dest].at[:, doc],
-                        sems.at[dest, doc],
+                        sources[src].at[slot_ref[doc], :, :, cols], target.at[:, doc], sems.at[i, doc]
                     ).start()
 
-    for dest in range(n_dest):
+    for i, target in enumerate(targets):
         for doc in range(DOCS):
             pltpu.make_async_copy(
-                sources[0].at[0, :, :, 0:HD], outs[dest].at[:, doc], sems.at[dest, doc]
+                sources[0].at[0, :, :, 0:HD], target.at[:, doc], sems.at[i, doc]
             ).wait()
 
 
-def select_docs(sources, place, slot, heads, n_dest):
+def select_docs(sources, place, slot, heads, targets_of):
     tokens = sources[0].shape[2]
-    shape = (2, DOCS, tokens, HD)
+    one = (2, DOCS, tokens, HD)
+    n_outs = 1 + max(out for out, _ in targets_of)
+    shapes = [one] * n_outs
+    for out, index in targets_of:
+        if index is not None:
+            shapes[out] = (2, *one)
     smem = pl.BlockSpec(memory_space=pltpu.SMEM)
     return pl.pallas_call(
-        functools.partial(select_kernel, n_dest, len(sources)),
+        functools.partial(select_kernel, targets_of, len(sources)),
         in_specs=[smem] * 3 + [pl.BlockSpec(memory_space=pl.ANY)] * len(sources),
-        out_specs=[pl.BlockSpec(memory_space=pltpu.VMEM)] * n_dest,
-        out_shape=[jax.ShapeDtypeStruct(shape, jnp.bfloat16)] * n_dest,
-        scratch_shapes=[pltpu.SemaphoreType.DMA((n_dest, DOCS))],
+        out_specs=[pl.BlockSpec(memory_space=pltpu.VMEM)] * n_outs,
+        out_shape=[jax.ShapeDtypeStruct(shape, jnp.bfloat16) for shape in shapes],
+        scratch_shapes=[pltpu.SemaphoreType.DMA((len(targets_of), DOCS))],
         compiler_params=megabytes(8),
-        cost_estimate=cost(0, 4 * n_dest * math.prod(shape)),
+        cost_estimate=cost(0, 4 * len(targets_of) * math.prod(one)),
         name="select_docs",
     )(place, slot, heads, *sources)
 
@@ -246,26 +252,31 @@
     return pieces
 
 
-def attend_kernel(n_chunks, with_new, n_tiles, tile_q, first_tile, first_ref, pos_ref, *refs):
+def attend_kernel(slots, offset, packs, has_state, has_new, n_tiles, tile_q, first_tile, *refs):
     refs = list(refs)
     take = lambda count: [refs.pop(0) for _ in range(count)]
-    chunks = take(n_chunks)
+    n_chunks = len(slots)
+    first_ref, pos_ref = take(2)
+    chunks = [ref if slot is None else ref.at[slot] for ref, slot in zip(take(n_chunks), slots)]
     dead_ref, qpos_ref, queries = take(3)
-    if with_new:
+    if has_state:
+        old_top, old_total, old_summed = take(3)
+    if has_new:
         cos_ref, sin_ref, new_ref = take(3)
-    if with_new:
-        top, total, summed, values, new_key, new_value = take(6)
-    else:
-        packed, top, total, summed, values = take(5)
+    if packs:
+        (packed,) = take(1)
+    top, total, summed, values = take(4)
+    if has_new:
+        new_key, new_value = take(2)
     together = min(PAIR, n_tiles)
     n_pairs = n_tiles // together
-    tokens = chunks[0].shape[2]
+    all_chunks, tokens = dead_ref.shape[0], dead_ref.shape[2]
     scale = math.log2(math.e) / math.sqrt(HD)
 
     for chunk in range(n_chunks):
         for doc in range(DOCS):
             values[doc, :, chunk * tokens : (chunk + 1) * tokens] = chunks[chunk][1, doc].T
-    if with_new:
+    if has_new:
         new_key[...] = rotate(
             new_ref[:, :HD].astype(jnp.float32), cos_ref[...], sin_ref[...]
         ).astype(jnp.bfloat16)
@@ -298,10 +309,15 @@
     def _(pair):
         tiles = [pair * together + i for i in range(together)]
         for tile in tiles:
-            top[tile] = jnp.full(top.shape[1:], MASKED, jnp.float32)
-            total[tile] = jnp.zeros(total.shape[1:], jnp.float32)
-            summed[tile] = jnp.zeros(summed.shape[1:], jnp.float32)
-        if with_new:
+            if has_state:
+                top[tile] = old_top[tile]
+                total[tile] = old_total[tile]
+                summed[tile] = old_summed[tile]
+            else:
+                top[tile] = jnp.full(top.shape[1:], MASKED, jnp.float32)
+                total[tile] = jnp.zeros(total.shape[1:], jnp.float32)
+                summed[tile] = jnp.zeros(summed.shape[1:], jnp.float32)
+        if has_new:
             fresh = []
             for tile in tiles:
                 scores = jnp.dot(new_key[...], queries[tile], preferred_element_type=jnp.float32)
@@ -313,7 +329,7 @@
 
         @pl.loop(0, DOCS)
         def _(doc):
-            firsts = [first_ref[doc * n_chunks + chunk] for chunk in range(n_chunks)]
+            firsts = [first_ref[doc * all_chunks + offset + chunk] for chunk in range(n_chunks)]
             lowest = functools.reduce(jnp.minimum, firsts)
             reach = functools.reduce(jnp.maximum, firsts) + tokens - 1
 
@@ -325,7 +341,7 @@
                     for chunk in range(n_chunks):
                         span = slice(chunk * tokens, (chunk + 1) * tokens)
                         keys = jnp.concatenate(
-                            [chunks[chunk][0, doc], dead_ref[doc, span, :]], axis=1
+                            [chunks[chunk][0, doc], dead_ref[offset + chunk, doc]], axis=1
                         )
                         scores = jnp.dot(keys, extended, preferred_element_type=jnp.float32)
                         if masked:
@@ -350,7 +366,7 @@
             def _():
                 visit(True)
 
-        if not with_new:
+        if packs:
             for tile in tiles:
                 extra = jnp.concatenate(
                     split_exact(top[tile])
@@ -361,31 +377,38 @@
                 packed[tile] = jnp.concatenate([summed[tile], extra], axis=0).astype(jnp.bfloat16)
 
 
-def attend(chunks, dead, first_pos, selected, q_pos, queries, first_tile, n_tiles, fresh):
-    n_chunks = len(chunks)
-    tokens = chunks[0].shape[2]
+def attend(chunks, offset, metadata, queries, first_tile, n_tiles, state=(), fresh=(), packs=False):
+    first_pos, selected, dead, q_pos = metadata
+    n_chunks, tokens = len(chunks), dead.shape[2]
     tile_q = SEL // q_pos.shape[0]
     smem = pl.BlockSpec(memory_space=pltpu.SMEM)
     vmem = pl.BlockSpec(memory_space=pltpu.VMEM)
-    operands = [first_pos, selected, *chunks, dead, q_pos, queries, *fresh]
-    state = [((n_tiles, 1, TILE_COLS), jnp.float32)] * 2
-    state += [((n_tiles, HD, TILE_COLS), jnp.float32)]
-    values = ((DOCS, HD, n_chunks * tokens), jnp.bfloat16)
+    operands = [first_pos, selected, *[keys for keys, _ in chunks], dead, q_pos, queries]
+    operands += [*state, *fresh]
+    outs = [((n_tiles, 1, TILE_COLS), jnp.float32)] * 2
+    outs += [((n_tiles, HD, TILE_COLS), jnp.float32)]
+    scratch = [((DOCS, HD, n_chunks * tokens), jnp.bfloat16)]
+    if packs:
+        outs, scratch = [((n_tiles, HD + STATS, TILE_COLS), jnp.bfloat16)], outs + scratch
     if fresh:
-        outs = state
-        scratch = [values, ((SEL, HD), jnp.bfloat16), ((HD, SEL), jnp.bfloat16)]
-    else:
-        outs = [((n_tiles, HD + STATS, TILE_COLS), jnp.bfloat16)]
-        scratch = state + [values]
+        scratch = scratch + [((SEL, HD), jnp.bfloat16), ((HD, SEL), jnp.bfloat16)]
     pairs = n_tiles * TILE_COLS * DOCS * n_chunks * tokens // 2
     return pl.pallas_call(
         functools.partial(
-            attend_kernel, n_chunks, bool(fresh), n_tiles, tile_q, first_tile
+            attend_kernel,
+            [slot for _, slot in chunks],
+            offset,
+            packs,
+            bool(state),
+            bool(fresh),
+            n_tiles,
+            tile_q,
+            first_tile,
         ),
         in_specs=[smem] * 2 + [vmem] * (len(operands) - 2),
         out_specs=[vmem] * len(outs),
-        out_shape=[jax.ShapeDtypeStruct(*s) for s in outs],
-        scratch_shapes=[pltpu.VMEM(*s) for s in scratch],
+        out_shape=[jax.ShapeDtypeStruct(*o) for o in outs],
+        scratch_shapes=[pltpu.VMEM(*x) for x in scratch],
         compiler_params=megabytes(16),
         cost_estimate=cost(4 * pairs * HD, 4 * DOCS * n_chunks * tokens * HD, pairs),
         name="attend",
@@ -558,8 +581,9 @@
     is_valid = slot_tokens[None] < lengths[:, None, None]
     replaced = jnp.any(cache_pos[..., None] == selected, axis=-1)
     dead = jnp.where(is_valid & jnp.logical_not(replaced), 0.0, MASKED).astype(jnp.bfloat16)
-    dead = jnp.broadcast_to(dead[..., None], (DOCS, middle, tokens, HD))
-    dead = dead.reshape(DOCS, middle * tokens, HD)
+    dead = jnp.broadcast_to(
+        dead.transpose(1, 0, 2)[..., None], (middle, DOCS, tokens, HD)
+    )
     first_pos = jnp.where(
         first_slot[None] < lengths[:, None], offsets[:, None] + first_slot[None], FAR
     ).reshape(-1)
@@ -599,7 +623,10 @@
                 )
             )
         if k == far - 1:
-            sent = select_docs(sources, holder, slot, takers, tp_size)
+            targets_of = [(0, None), (1, 0)] + [(j, None) for j in range(2, middle)]
+            targets_of += [(middle, None), (1, 1)]
+            targets_of += [(middle + j - 1, None) for j in range(2, middle)]
+            sent = select_docs(sources, holder, slot, takers, targets_of)
             first[-1], *sent = lax.optimization_barrier((first[-1], *sent))
     projected = None
     for chunk, held in enumerate(streams):
@@ -612,21 +639,26 @@
         projected = project(
             place, blocks, w_query, w_keyval, projected, (cosine, sine_part), chunk
         )
-    def exchange(kept):
-        return [
-            lax.ppermute(kept[j], "tp", [(i, i ^ j) for i in range(tp_size)]) if j else kept[j]
-            for j in range(middle)
-        ]
-
-    own, partners = sent[:middle], exchange(sent[middle:])
-    own, partners = lax.optimization_barrier((own, partners))
-    chunks = [exchange(own), partners]
+    def exchange(keys, j):
+        return lax.ppermute(keys, "tp", [(i, i ^ j) for i in range(tp_size)])
+
+    nearest = exchange(sent[1], 1)
+    own = [(sent[0], None), (nearest, 0)]
+    partners = [(sent[middle], None), (nearest, 1)]
+    partners += [(exchange(sent[middle + j - 1], j), None) for j in range(2, middle)]
+    leaving = sent[2:middle]
     queries = projected[:HALVES]
     n_tiles = queries[0].shape[0]
     across = [(i, i ^ middle) for i in range(tp_size)]
     their_queries = [None] * HALVES
     for part in reversed(range(HALVES)):
         their_queries[part] = lax.ppermute(queries[part], "tp", across)
+
+    metadata = (first_pos, selected, dead, q_pos)
+    near = [
+        attend(own, 0, metadata, queries[part], part * n_tiles, n_tiles) for part in range(HALVES)
+    ]
+    their_queries[-1], *near = lax.optimization_barrier((their_queries[-1], *near))
 
     if tp_size == KVH:
         new = lax.ppermute(
@@ -645,21 +677,30 @@
             axis=1,
         )
 
-    def attend_half(part, asked, slot, extra):
-        return attend(
-            chunks[slot], dead, first_pos, selected, q_pos, asked[part], part * n_tiles, n_tiles, extra
-        )
-
     theirs = [None] * HALVES
     for part in reversed(range(HALVES)):
-        (packed,) = attend_half(part, their_queries, 1, [])
-        if part:
-            packed, new, their_queries[part - 1] = lax.optimization_barrier(
-                (packed, new, their_queries[part - 1])
+        (packed,) = attend(
+            partners, 0, metadata, their_queries[part], part * n_tiles, n_tiles, packs=True
+        )
+        if part + 1 == HALVES:
+            packed, new, leaving, *their_queries[:part] = lax.optimization_barrier(
+                (packed, new, leaving, *their_queries[:part])
             )
+            rest = [(exchange(leaving[j - 2], j), None) for j in range(2, middle)]
         theirs[part] = lax.ppermute(packed, "tp", across)
-    fresh = [cosine, sine_part, new]
-    mine = [attend_half(part, queries, 0, fresh) for part in range(HALVES)]
+    mine = [
+        attend(
+            rest,
+            2,
+            metadata,
+            queries[part],
+            part * n_tiles,
+            n_tiles,
+            near[part],
+            (cosine, sine_part, new),
+        )
+        for part in range(HALVES)
+    ]
     attention = merge(mine, theirs)
 
     finished = []

time: 198 us -> 231 us (1.17)
  waiting for transfers between devices: 76.5 us -> 107 us
  Pallas kernels: 57.8 us -> 62.8 us
  starting transfers between devices: 48.5 us -> 44.5 us
    ppermute x7, waiting for transfers between devices: 3.18 us -> 30.9 us  [per_device(): held['before'].append(lax.ppermute(held['before'][-1], 'tp', forth))]
    ppermute x6 -> x5, waiting for transfers between devices: 15.6 us -> 26.5 us  [exchange(): return lax.ppermute(keys, 'tp', [(i, i ^ j) for i in range(tp_size)])]
    ppermute x2, waiting for transfers between devices: 8.43 us -> 0.01 us  [per_device(): theirs[part] = lax.ppermute(packed, 'tp', across)]
    pallas_call x5 -> x7, Pallas kernels: 34.3 us -> 39.3 us  [the longest x6 36.1 us: attend(): pl.pallas_call(functools.partial(attend_kernel, [slot for _, slot in chun...]
    ppermute x6 -> x5, starting transfers between devices: 7.34 us -> 5.89 us  [exchange(): return lax.ppermute(keys, 'tp', [(i, i ^ j) for i in range(tp_size)])]
  transfers between devices with their start and end apart: 40 -> 39, of which waited for: 18 -> 17; matrix products, arithmetic and copies ran while one was open for 3% -> 3% of each run, Pallas kernels for 26% -> 25%
where the time goes in v10:
time: 231 us; the launch traced here: 230 us
  waiting for transfers between devices  107 us (46%)
  Pallas kernels  62.8 us (27%)
  starting transfers between devices  44.5 us (19%)
  local copies, waits for them, and re-layouts  7.6 us (3%)
  other arithmetic  7.25 us (3%)
    pallas_call x6, Pallas kernels, attend(): pl.pallas_call(functools.partial(attend_kernel, [slot for _, slot in chun...  36.1 us
    ppermute x7, waiting for transfers between devices, per_device(): held['before'].append(lax.ppermute(held['before'][-1], 'tp', forth))  30.9 us
    ppermute x5, waiting for transfers between devices, exchange(): return lax.ppermute(keys, 'tp', [(i, i ^ j) for i in range(tp_size)])  26.5 us
    ppermute x14, waiting for transfers between devices, per_device(): held = lax.ppermute(term.astype(jnp.bfloat16), 'tp', pairs)  22.9 us
    ppermute x14, starting transfers between devices, per_device(): held = lax.ppermute(term.astype(jnp.bfloat16), 'tp', pairs)  14.8 us
    ppermute x7, waiting for transfers between devices, per_device(): held['behind'].append(lax.ppermute(held['behind'][-1], 'tp', back))  14.2 us
    ppermute x2, waiting for transfers between devices, per_device(): their_queries[part] = lax.ppermute(queries[part], 'tp', across)  13 us
    pallas_call x2, Pallas kernels, project(): pl.pallas_call(functools.partial(project_kernel, len(blocks), chunk, is_l...  13 us
  transfers between devices with their start and end apart: 39, of which 17 were waited for; matrix products, arithmetic and copies ran while one was open for 3% of the time, Pallas kernels for 25%

profile of v10, /device:TPU:0, one launch (start us, length us, event | category | flops | bytes accessed | tf_op | source)
XLA Modules:
  0.0 230.0 jit_solution(8353508971648220515)
XLA Ops:
  0.0 1.2 fusion
  1.3 1.2 fusion.2
  2.5 5.5 %copy.15 = bf16[4,256,2,1024]{3,1,2,0:T(8,128)(2,1)} copy(bf16[4,256,2,1024]{3,2,1,0:T(2,128)(2,1)} %param.15) | data formatting | bytes 8388608 | tf_op jit(solution)/shard_map/optimization_barrier | solution.py:571
  8.0 0.5 collective-permute-start.3
  8.5 2.6 %collective-permute-start = (bf16[32,4096]{1,0:T(8,128)(2,1)S(1)}, bf16[32,4096]{1,0:T(8,128)(2,1)S(1)}, u32[]{:S(2)}, u32[]{:S(2)}) collective-permute-start(bf16[32,4096]{1,0:T(8,128)(2,1)S(1)} %get-tuple-element.150.refs_0_), channel_id=1, source_target_pairs={{0,2},{2,4},{4,6},{6,7},{7,5},{5,3},{3,1},{1,0},{8,10},{10,12},{12... | collective-permute-start | bytes 786440 | tf_op jit(solution)/shard_map/ppermute | solution.py:604
  11.1 2.0 collective-permute-start.8
  13.6 1.3 compare_reduce_fusion
  15.0 0.5 fusion.3
  15.6 2.6 %collective-permute-done.refs_1_ = bf16[32,4096]{1,0:T(8,128)(2,1)S(1)} collective-permute-done((bf16[32,4096]{1,0:T(8,128)(2,1)S(1)}, bf16[32,4096]{1,0:T(8,128)(2,1)S(1)}, u32[]{:S(2)}, u32[]{:S(2)}) %collective-permute-start) | collective-permute-done | bytes 262176 | tf_op jit(solution)/shard_map/ppermute | solution.py:604
  18.2 2.0 collective-permute-start.1
  20.2 0.7 dynamic-slice_bitcast_fusion.place_ref
  21.1 4.1 %collective-permute-done.8.refs_2_ = bf16[32,4096]{1,0:T(8,128)(2,1)S(1)} collective-permute-done((bf16[32,4096]{1,0:T(8,128)(2,1)S(1)}, bf16[32,4096]{1,0:T(8,128)(2,1)S(1)}, u32[]{:S(2)}, u32[]{:S(2)}) %collective-permute-start.8) | collective-permute-done | bytes 262176 | tf_op jit(solution)/shard_map/ppermute | solution.py:606
  25.2 0.3 collective-permute-start.10
  25.7 0.5 broadcast.163
  26.2 0.7 reduce.3
  27.0 1.7 collective-permute-start.15
  28.8 0.5 collective-permute-done.1.refs_3_
  29.3 0.6 broadcast_in_dim.20.refs_4_.refs_6_
  29.9 1.8 collective-permute-start.2
  31.8 1.6 collective-permute-start.9
  33.3 1.1 collective-permute-done.10.refs_4_
  34.7 5.4 %collective-permute-done.15.refs_4_ = bf16[32,4096]{1,0:T(8,128)(2,1)S(1)} collective-permute-done((bf16[32,4096]{1,0:T(8,128)(2,1)S(1)}, bf16[32,4096]{1,0:T(8,128)(2,1)S(1)}, u32[]{:S(2)}, u32[]{:S(2)}) %collective-permute-start.15) | collective-permute-done | bytes 262176 | tf_op jit(solution)/shard_map/ppermute | solution.py:606
  40.3 3.3 %select_docs.1 = (bf16[2,4,256,128]{3,2,1,0:T(8,128)(2,1)S(1)}, bf16[2,2,4,256,128]{4,3,2,1,0:T(8,128)(2,1)S(1)}, bf16[2,4,256,128]{3,2,1,0:T(8,128)(2,1)S(1)}, ...) custom-call(s32[4]{0:T(128)S(1)} %get-tuple-element.81.place_ref, ...), custom_call_target="tpu_custom_call" | custom-call | bytes 8388608 | tf_op jit(solution)/shard_map/select_docs/pallas_call | solution.py:235
  43.6 1.8 collective-permute-start.17
  45.7 1.7 collective-permute-start.11
  47.4 0.3 collective-permute-start.13
  47.7 3.6 %collective-permute-done.16.refs_6_ = bf16[32,4096]{1,0:T(8,128)(2,1)S(1)} collective-permute-done((bf16[32,4096]{1,0:T(8,128)(2,1)S(1)}, bf16[32,4096]{1,0:T(8,128)(2,1)S(1)}, u32[]{:S(2)}, u32[]{:S(2)}) %collective-permute-start.16) | collective-permute-done | bytes 262176 | tf_op jit(solution)/shard_map/ppermute | solution.py:606
  51.3 1.6 collective-permute-start.5
  52.9 1.8 collective-permute-start.6
  54.7 6.3 %project.2 = (f32[256,1024]{1,0:T(8,128)S(1)}, f32[256,256]{1,0:T(8,128)S(1)}) custom-call(s32[8]{0:T(128)S(1)} %dynamic-slice_bitcast_fusion.place_ref, bf16[32,4096]{1,0:T(8,128)(2,1)S(1)} %get-tuple-element.150.refs_0_, bf16[32,4096]{1,0:T(8,128)(2,1)S(1)} %collective-permute-done.refs_1_, bf16[32,4096]{1,0:T(8,128)(2,1)S(1)} %collective-permute-done.14.refs_2_, ...), custom_call_target="tpu_custom_call" | custom-call | flops 2684354560 | bytes 12582912 | tf_op jit(solution)/shard_map/project/pallas_call | solution.py:179
  61.0 27.7 %collective-permute-done.11.refs_5_ = bf16[32,4096]{1,0:T(8,128)(2,1)S(1)} collective-permute-done((bf16[32,4096]{1,0:T(8,128)(2,1)S(1)}, bf16[32,4096]{1,0:T(8,128)(2,1)S(1)}, u32[]{:S(2)}, u32[]{:S(2)}) %collective-permute-start.11) | collective-permute-done | bytes 262176 | tf_op jit(solution)/shard_map/ppermute | solution.py:604
  88.7 6.7 %project.3 = (bf16[4,128,256]{2,1,0:T(8,128)(2,1)S(1)}, bf16[6,128,256]{2,1,0:T(8,128)(2,1)S(1)}) custom-call(s32[8]{0:T(128)S(1)} %dynamic-slice_bitcast_fusion.place_ref, bf16[32,4096]{1,0:T(8,128)(2,1)S(1)} %get-tuple-element.149.refs_0_, bf16[32,4096]{1,0:T(8,128)(2,1)S(1)} %collective-permute-done.7.refs_1_, ...), custom_call_target="tpu_custom_call" | custom-call | flops 2684354560 | bytes 12582912 | tf_op jit(solution)/shard_map/project/pallas_call | solution.py:179
  95.4 2.9 %collective-permute-start.20 = (bf16[4,128,256]{2,1,0:T(8,128)(2,1)S(1)}, bf16[4,128,256]{2,1,0:T(8,128)(2,1)S(1)}, u32[]{:S(2)}, u32[]{:S(2)}) collective-permute-start(bf16[4,128,256]{2,1,0:T(8,128)(2,1)S(1)} %get-tuple-element.105.refs_6_), channel_id=1, source_target_pairs={{0,4},{1,5},{2,6},{3,7},{4,0},{5,1},{6,2},{7,3},{8,12},{9,13},{10,... | collective-permute-start | bytes 786440 | tf_op jit(solution)/shard_map/ppermute | solution.py:655
  98.4 5.6 %attend.7 = (f32[4,1,256]{2,1,0:T(1,128)S(1)}, f32[4,1,256]{2,1,0:T(1,128)S(1)}, f32[4,128,256]{2,1,0:T(8,128)S(1)}) custom-call(s32[16]{0:T(128)S(1)} %select_n.39.refs_0_, s32[256]{0:T(256)S(1)} %bitcast.21, bf16[2,4,256,128]{3,2,1,0:T(8,128)(2,1)S(1)} %get-tuple-element.104.refs_2_, bf16[2,2,4,256,128]{4,3,2,1,0:T(8,128)(2,1)S(1)} %collective-permute-done.4.refs_3_, ...), custom_call_target="tpu_custom_call" | custom-call | flops 536870912 | bytes 1048576 | tf_op jit(solution)/shard_map/attend/pallas_call | solution.py:396
  103.9 4.4 %attend.6 = (f32[4,1,256]{2,1,0:T(1,128)S(1)}, f32[4,1,256]{2,1,0:T(1,128)S(1)}, f32[4,128,256]{2,1,0:T(8,128)S(1)}) custom-call(s32[16]{0:T(128)S(1)} %select_n.39.refs_0_, s32[256]{0:T(256)S(1)} %bitcast.22, bf16[2,4,256,128]{3,2,1,0:T(8,128)(2,1)S(1)} %get-tuple-element.104.refs_2_, bf16[2,2,4,256,128]{4,3,2,1,0:T(8,128)(2,1)S(1)} %collective-permute-done.4.refs_3_, ...), custom_call_target="tpu_custom_call" | custom-call | flops 536870912 | bytes 1048576 | tf_op jit(solution)/shard_map/attend/pallas_call | solution.py:396
  108.3 13.0 %collective-permute-done.18.refs_8_.there_ref = bf16[6,128,256]{2,1,0:T(8,128)(2,1)S(1)} collective-permute-done((bf16[6,128,256]{2,1,0:T(8,128)(2,1)S(1)}, bf16[6,128,256]{2,1,0:T(8,128)(2,1)S(1)}, u32[]{:S(2)}, u32[]{:S(2)}) %collective-permute-start.18) | collective-permute-done | bytes 393248 | tf_op jit(solution)/shard_map/ppermute | solution.py:655
  121.3 0.9 collective-permute-start.19
  122.2 8.7 %attend.8 = bf16[4,144,256]{2,1,0:T(8,128)(2,1)S(1)} custom-call(s32[16]{0:T(128)S(1)} %select_n.39.refs_0_, s32[256]{0:T(256)S(1)} %bitcast.23, bf16[2,4,256,128]{3,2,1,0:T(8,128)(2,1)S(1)} %get-tuple-element.92.refs_2_, bf16[2,2,4,256,128]{4,3,2,1,0:T(8,128)(2,1)S(1)} %collective-permute-done.4.refs_3_, ...), custom_call_target="tpu_custom_call" | custom-call | flops 1073741824 | bytes 2097152 | tf_op jit(solution)/shard_map/attend/pallas_call | solution.py:396
  131.0 1.4 collective-permute-start.21
  132.4 0.9 collective-permute-start.22
  133.2 6.9 %attend.10 = bf16[4,144,256]{2,1,0:T(8,128)(2,1)S(1)} custom-call(s32[16]{0:T(128)S(1)} %select_n.39.refs_0_, s32[256]{0:T(256)S(1)} %bitcast.24, bf16[2,4,256,128]{3,2,1,0:T(8,128)(2,1)S(1)} %get-tuple-element.92.refs_2_, bf16[2,2,4,256,128]{4,3,2,1,0:T(8,128)(2,1)S(1)} %collective-permute-done.4.refs_3_, ...), custom_call_target="tpu_custom_call" | custom-call | flops 1073741824 | bytes 2097152 | tf_op jit(solution)/shard_map/attend/pallas_call | solution.py:396
  140.2 2.9 %collective-permute-start.24 = (bf16[4,144,256]{2,1,0:T(8,128)(2,1)S(1)}, bf16[4,144,256]{2,1,0:T(8,128)(2,1)S(1)}, u32[]{:S(2)}, u32[]{:S(2)}) collective-permute-start(bf16[4,144,256]{2,1,0:T(8,128)(2,1)S(1)} %attend.8), channel_id=1, source_target_pairs={{0,4},{1,5},{2,6},{3,7},{4,0},{5,1},{6,2},{7,3},{8,12},{9,13},{10,... | collective-permute-start | bytes 884744 | tf_op jit(solution)/shard_map/ppermute | solution.py:690
  143.1 12.7 %collective-permute-done.21.refs_2_ = bf16[2,4,256,128]{3,2,1,0:T(8,128)(2,1)S(1)} collective-permute-done((bf16[2,4,256,128]{3,2,1,0:T(8,128)(2,1)S(1)}, bf16[2,4,256,128]{3,2,1,0:T(8,128)(2,1)S(1)}, u32[]{:S(2)}, u32[]{:S(2)}) %collective-permute-start.21) | collective-permute-done | bytes 524320 | tf_op jit(solution)/shard_map/ppermute | solution.py:643
  155.9 13.7 %collective-permute-done.22.refs_3_ = bf16[2,4,256,128]{3,2,1,0:T(8,128)(2,1)S(1)} collective-permute-done((bf16[2,4,256,128]{3,2,1,0:T(8,128)(2,1)S(1)}, bf16[2,4,256,128]{3,2,1,0:T(8,128)(2,1)S(1)}, u32[]{:S(2)}, u32[]{:S(2)}) %collective-permute-start.22) | collective-permute-done | bytes 524320 | tf_op jit(solution)/shard_map/ppermute | solution.py:643
  169.6 6.5 %attend.11 = (f32[4,1,256]{2,1,0:T(1,128)S(1)}, f32[4,1,256]{2,1,0:T(1,128)S(1)}, f32[4,128,256]{2,1,0:T(8,128)S(1)}) custom-call(s32[16]{0:T(128)S(1)} %select_n.39.refs_0_, s32[256]{0:T(256)S(1)} %bitcast.25, bf16[2,4,256,128]{3,2,1,0:T(8,128)(2,1)S(1)} %collective-permute-done.21.refs_2_, bf16[2,4,256,128]{3,2,1,0:T(8,128)(2,1)S(1)} %collective-permute-done.22.refs_3_, ...), custom_call_target="tpu_custom_call" | custom-call | flops 536870912 | bytes 1048576 | tf_op jit(solution)/shard_map/attend/pallas_call | solution.py:396
  176.2 4.0 %attend.9 = (f32[4,1,256]{2,1,0:T(1,128)S(1)}, f32[4,1,256]{2,1,0:T(1,128)S(1)}, f32[4,128,256]{2,1,0:T(8,128)S(1)}) custom-call(s32[16]{0:T(128)S(1)} %select_n.39.refs_0_, s32[256]{0:T(256)S(1)} %bitcast.26, bf16[2,4,256,128]{3,2,1,0:T(8,128)(2,1)S(1)} %collective-permute-done.21.refs_2_, bf16[2,4,256,128]{3,2,1,0:T(8,128)(2,1)S(1)} %collective-permute-done.22.refs_3_, ...), custom_call_target="tpu_custom_call" | custom-call | flops 536870912 | bytes 1048576 | tf_op jit(solution)/shard_map/attend/pallas_call | solution.py:396
  180.2 0.4 merge.1.x_ref
  180.6 5.1 %project_out.2 = (f32[32,4096]{1,0:T(8,128)S(1)}, f32[32,4096]{1,0:T(8,128)S(1)}, f32[32,4096]{1,0:T(8,128)S(1)}, f32[32,4096]{1,0:T(8,128)S(1)}, f32[32,4096]{1...) custom-call(s32[8]{0:T(128)S(1)} %dynamic-slice_bitcast_fusion.place_ref, ...), custom_call_target="tpu_custom_call" | custom-call | flops 2147483648 | bytes 13107200 | tf_op jit(solution)/shard_map/project_out/pallas_call | solution.py:522
  185.7 2.3 %collective-permute-start.29 = (bf16[32,4096]{1,0:T(8,128)(2,1)S(1)}, bf16[32,4096]{1,0:T(8,128)(2,1)S(1)}, u32[]{:S(2)}, u32[]{:S(2)}) collective-permute-start(bf16[32,4096]{1,0:T(8,128)(2,1)S(1)} %convert_element_type.113), channel_id=1, source_target_pairs={{2,0},{4,2},{6,4},{7,6},{5,7},{3,5},{1,3},{0,1},{10,8},{12,10},{14... | collective-permute-start | bytes 786440 | tf_op jit(solution)/shard_map/ppermute | solution.py:718
  188.1 5.1 %project_out.3 = (f32[32,4096]{1,0:T(8,128)S(1)}, f32[32,4096]{1,0:T(8,128)S(1)}, f32[32,4096]{1,0:T(8,128)S(1)}, f32[32,4096]{1,0:T(8,128)S(1)}, f32[32,4096]{1...) custom-call(s32[8]{0:T(128)S(1)} %dynamic-slice_bitcast_fusion.place_ref, ...), custom_call_target="tpu_custom_call" | custom-call | flops 2147483648 | bytes 13107200 | tf_op jit(solution)/shard_map/project_out/pallas_call | solution.py:522
  193.3 2.0 collective-permute-start.35
  195.5 2.0 collective-permute-start.30
  197.5 5.0 %collective-permute-done.32 = bf16[32,4096]{1,0:T(8,128)(2,1)S(1)} collective-permute-done((bf16[32,4096]{1,0:T(8,128)(2,1)S(1)}, bf16[32,4096]{1,0:T(8,128)(2,1)S(1)}, u32[]{:S(2)}, u32[]{:S(2)}) %collective-permute-start.32) | collective-permute-done | bytes 262176 | tf_op jit(solution)/shard_map/ppermute | solution.py:718
  202.7 2.1 collective-permute-start.36
  204.7 3.4 %collective-permute-done.26 = bf16[32,4096]{1,0:T(8,128)(2,1)S(1)} collective-permute-done((bf16[32,4096]{1,0:T(8,128)(2,1)S(1)}, bf16[32,4096]{1,0:T(8,128)(2,1)S(1)}, u32[]{:S(2)}, u32[]{:S(2)}) %collective-permute-start.26) | collective-permute-done | bytes 262176 | tf_op jit(solution)/shard_map/ppermute | solution.py:718
  208.3 2.1 collective-permute-start.31
  210.3 3.4 %collective-permute-done.33 = bf16[32,4096]{1,0:T(8,128)(2,1)S(1)} collective-permute-done((bf16[32,4096]{1,0:T(8,128)(2,1)S(1)}, bf16[32,4096]{1,0:T(8,128)(2,1)S(1)}, u32[]{:S(2)}, u32[]{:S(2)}) %collective-permute-start.33) | collective-permute-done | bytes 262176 | tf_op jit(solution)/shard_map/ppermute | solution.py:718
  213.9 2.1 collective-permute-start.37
  216.0 3.4 %collective-permute-done.27 = bf16[32,4096]{1,0:T(8,128)(2,1)S(1)} collective-permute-done((bf16[32,4096]{1,0:T(8,128)(2,1)S(1)}, bf16[32,4096]{1,0:T(8,128)(2,1)S(1)}, u32[]{:S(2)}, u32[]{:S(2)}) %collective-permute-start.27) | collective-permute-done | bytes 262176 | tf_op jit(solution)/shard_map/ppermute | solution.py:718
  219.5 3.1 %collective-permute-done.37 = bf16[32,4096]{1,0:T(8,128)(2,1)S(1)} collective-permute-done((bf16[32,4096]{1,0:T(8,128)(2,1)S(1)}, bf16[32,4096]{1,0:T(8,128)(2,1)S(1)}, u32[]{:S(2)}, u32[]{:S(2)}) %collective-permute-start.37) | collective-permute-done | bytes 262176 | tf_op jit(solution)/shard_map/ppermute | solution.py:718
  222.6 1.7 collective-permute-start.38
  224.4 3.8 %collective-permute-done.28 = bf16[32,4096]{1,0:T(8,128)(2,1)S(1)} collective-permute-done((bf16[32,4096]{1,0:T(8,128)(2,1)S(1)}, bf16[32,4096]{1,0:T(8,128)(2,1)S(1)}, u32[]{:S(2)}, u32[]{:S(2)}) %collective-permute-start.28) | collective-permute-done | bytes 262176 | tf_op jit(solution)/shard_map/ppermute | solution.py:718
  228.2 0.8 collective-permute-done.38
  229.2 0.8 pad_maximum_fusion
  (77 shorter events, 3.4 us)
Async XLA Ops:
  2.5 10.7 %copy-start = (s32[1,256]{1,0:T(1,128)S(1)}, s32[1,256]{1,0:T(1,128)}, u32[]{:S(2)}) copy-start(s32[1,256]{1,0:T(1,128)} %param.18) | copy-start | bytes 3076
  2.5 10.7 %copy-start.1 = (s32[1,4]{1,0:T(1,128)S(1)}, s32[1,4]{1,0:T(1,128)}, u32[]{:S(2)}) copy-start(s32[1,4]{1,0:T(1,128)} %param.17) | copy-start | bytes 52
  2.5 13.0 %copy-start.2 = (s32[4]{0:T(128)S(1)}, s32[4]{0:T(128)}, u32[]{:S(2)}) copy-start(s32[4]{0:T(128)} %param.16) | copy-start | bytes 52
  8.0 32.3 %collective-permute-start.3 = (bf16[4,2,256,1024]{3,2,1,0:T(8,128)(2,1)}, bf16[4,2,256,1024]{3,2,1,0:T(8,128)(2,1)}, u32[]{:S(2)}, u32[]{:S(2)}) collective-permute-start(bf16[4,2,256,1024]{3,2,1,0:T(8,128)(2,1)} %bitcast.18.refs_0_), channel_id=1, source_target_pairs={{8,0},{0,8},{9,1},{1,9},{10,2},{2,10},{11,3},{3,11},{12,4},{4,12},... | collective-permute-start | bytes 12582920 | tf_op jit(solution)/shard_map/ppermute | solution.py:613
  8.5 9.7 %collective-permute-start = (bf16[32,4096]{1,0:T(8,128)(2,1)S(1)}, bf16[32,4096]{1,0:T(8,128)(2,1)S(1)}, u32[]{:S(2)}, u32[]{:S(2)}) collective-permute-start(bf16[32,4096]{1,0:T(8,128)(2,1)S(1)} %get-tuple-element.150.refs_0_), channel_id=1, source_target_pairs={{0,2},{2,4},{4,6},{6,7},{7,5},{5,3},{3,1},{1,0},{8,10},{10,12},{12... | collective-permute-start | bytes 786440 | tf_op jit(solution)/shard_map/ppermute | solution.py:604
  11.1 15.9 %collective-permute-start.14 = (bf16[32,4096]{1,0:T(8,128)(2,1)S(1)}, bf16[32,4096]{1,0:T(8,128)(2,1)S(1)}, u32[]{:S(2)}, u32[]{:S(2)}) collective-permute-start(bf16[32,4096]{1,0:T(8,128)(2,1)S(1)} %get-tuple-element.150.refs_0_), channel_id=1, source_target_pairs={{2,0},{4,2},{6,4},{7,6},{5,7},{3,5},{1,3},{0,1},{10,8},{12,10},{14... | collective-permute-start | bytes 786440 | tf_op jit(solution)/shard_map/ppermute | solution.py:606
  11.1 14.0 %collective-permute-start.8 = (bf16[32,4096]{1,0:T(8,128)(2,1)S(1)}, bf16[32,4096]{1,0:T(8,128)(2,1)S(1)}, u32[]{:S(2)}, u32[]{:S(2)}) collective-permute-start(bf16[32,4096]{1,0:T(8,128)(2,1)S(1)} %get-tuple-element.149.refs_0_), channel_id=1, source_target_pairs={{2,0},{4,2},{6,4},{7,6},{5,7},{3,5},{1,3},{0,1},{10,8},{12,10},{14... | collective-permute-start | bytes 786440 | tf_op jit(solution)/shard_map/ppermute | solution.py:606
  13.1 18.6 %collective-permute-start.7 = (bf16[32,4096]{1,0:T(8,128)(2,1)S(1)}, bf16[32,4096]{1,0:T(8,128)(2,1)S(1)}, u32[]{:S(2)}, u32[]{:S(2)}) collective-permute-start(bf16[32,4096]{1,0:T(8,128)(2,1)S(1)} %get-tuple-element.149.refs_0_), channel_id=1, source_target_pairs={{0,2},{2,4},{4,6},{6,7},{7,5},{5,3},{3,1},{1,0},{8,10},{10,12},{12... | collective-permute-start | bytes 786440 | tf_op jit(solution)/shard_map/ppermute | solution.py:604
  18.2 11.1 %collective-permute-start.1 = (bf16[32,4096]{1,0:T(8,128)(2,1)S(1)}, bf16[32,4096]{1,0:T(8,128)(2,1)S(1)}, u32[]{:S(2)}, u32[]{:S(2)}) collective-permute-start(bf16[32,4096]{1,0:T(8,128)(2,1)S(1)} %collective-permute-done.refs_1_), channel_id=1, source_target_pairs={{0,2},{2,4},{4,6},{6,7},{7,5},{5,3},{3,1},{1,0},{8,10},{10,12},{12... | collective-permute-start | bytes 786440 | tf_op jit(solution)/shard_map/ppermute | solution.py:604
  25.2 9.2 %collective-permute-start.10 = (bf16[32,4096]{1,0:T(8,128)(2,1)S(1)}, bf16[32,4096]{1,0:T(8,128)(2,1)S(1)}, u32[]{:S(2)}, u32[]{:S(2)}) collective-permute-start(bf16[32,4096]{1,0:T(8,128)(2,1)S(1)} %collective-permute-done.8.refs_2_), channel_id=1, source_target_pairs={{2,0},{4,2},{6,4},{7,6},{5,7},{3,5},{1,3},{0,1},{10,8},{12,10},{14... | collective-permute-start | bytes 786440 | tf_op jit(solution)/shard_map/ppermute | solution.py:606
  27.0 13.0 %collective-permute-start.15 = (bf16[32,4096]{1,0:T(8,128)(2,1)S(1)}, bf16[32,4096]{1,0:T(8,128)(2,1)S(1)}, u32[]{:S(2)}, u32[]{:S(2)}) collective-permute-start(bf16[32,4096]{1,0:T(8,128)(2,1)S(1)} %collective-permute-done.14.refs_2_), channel_id=1, source_target_pairs={{2,0},{4,2},{6,4},{7,6},{5,7},{3,5},{1,3},{0,1},{10,8},{12,10},{14... | collective-permute-start | bytes 786440 | tf_op jit(solution)/shard_map/ppermute | solution.py:606
  29.9 13.7 %collective-permute-start.2 = (bf16[32,4096]{1,0:T(8,128)(2,1)S(1)}, bf16[32,4096]{1,0:T(8,128)(2,1)S(1)}, u32[]{:S(2)}, u32[]{:S(2)}) collective-permute-start(bf16[32,4096]{1,0:T(8,128)(2,1)S(1)} %collective-permute-done.1.refs_3_), channel_id=1, source_target_pairs={{0,2},{2,4},{4,6},{6,7},{7,5},{5,3},{3,1},{1,0},{8,10},{10,12},{12... | collective-permute-start | bytes 786440 | tf_op jit(solution)/shard_map/ppermute | solution.py:604
  31.8 13.9 %collective-permute-start.9 = (bf16[32,4096]{1,0:T(8,128)(2,1)S(1)}, bf16[32,4096]{1,0:T(8,128)(2,1)S(1)}, u32[]{:S(2)}, u32[]{:S(2)}) collective-permute-start(bf16[32,4096]{1,0:T(8,128)(2,1)S(1)} %collective-permute-done.7.refs_1_), channel_id=1, source_target_pairs={{0,2},{2,4},{4,6},{6,7},{7,5},{5,3},{3,1},{1,0},{8,10},{10,12},{12... | collective-permute-start | bytes 786440 | tf_op jit(solution)/shard_map/ppermute | solution.py:604
  34.4 13.0 %collective-permute-start.12 = (bf16[32,4096]{1,0:T(8,128)(2,1)S(1)}, bf16[32,4096]{1,0:T(8,128)(2,1)S(1)}, u32[]{:S(2)}, u32[]{:S(2)}) collective-permute-start(bf16[32,4096]{1,0:T(8,128)(2,1)S(1)} %collective-permute-done.10.refs_4_), channel_id=1, source_target_pairs={{2,0},{4,2},{6,4},{7,6},{5,7},{3,5},{1,3},{0,1},{10,8},{12,10},{14... | collective-permute-start | bytes 786440 | tf_op jit(solution)/shard_map/ppermute | solution.py:606
  40.1 11.2 %collective-permute-start.16 = (bf16[32,4096]{1,0:T(8,128)(2,1)S(1)}, bf16[32,4096]{1,0:T(8,128)(2,1)S(1)}, u32[]{:S(2)}, u32[]{:S(2)}) collective-permute-start(bf16[32,4096]{1,0:T(8,128)(2,1)S(1)} %collective-permute-done.15.refs_4_), channel_id=1, source_target_pairs={{2,0},{4,2},{6,4},{7,6},{5,7},{3,5},{1,3},{0,1},{10,8},{12,10},{14... | collective-permute-start | bytes 786440 | tf_op jit(solution)/shard_map/ppermute | solution.py:606
  43.6 9.3 %collective-permute-start.17 = (bf16[32,4096]{1,0:T(8,128)(2,1)S(1)}, bf16[32,4096]{1,0:T(8,128)(2,1)S(1)}, u32[]{:S(2)}, u32[]{:S(2)}) collective-permute-start(bf16[32,4096]{1,0:T(8,128)(2,1)S(1)} %collective-permute-done.2.refs_5_), channel_id=1, source_target_pairs={{0,2},{2,4},{4,6},{6,7},{7,5},{5,3},{3,1},{1,0},{8,10},{10,12},{12... | collective-permute-start | bytes 786440 | tf_op jit(solution)/shard_map/ppermute | solution.py:604
  45.4 53.0 %collective-permute-start.4 = (bf16[2,2,4,256,128]{4,3,2,1,0:T(8,128)(2,1)S(1)}, bf16[2,2,4,256,128]{4,3,2,1,0:T(8,128)(2,1)S(1)}, u32[]{:S(2)}, u32[]{:S(2)}) collective-permute-start(bf16[2,2,4,256,128]{4,3,2,1,0:T(8,128)(2,1)S(1)} %get-tuple-element.93), channel_id=1, source_target_pairs={{0,1},{1,0},{2,3},{3,2},{4,5},{5,4},{6,7},{7,6},{8,9},{9,8},{10,11... | collective-permute-start | bytes 3145736 | tf_op jit(solution)/shard_map/ppermute | solution.py:643
  45.7 43.0 %collective-permute-start.11 = (bf16[32,4096]{1,0:T(8,128)(2,1)S(1)}, bf16[32,4096]{1,0:T(8,128)(2,1)S(1)}, u32[]{:S(2)}, u32[]{:S(2)}) collective-permute-start(bf16[32,4096]{1,0:T(8,128)(2,1)S(1)} %collective-permute-done.9.refs_3_), channel_id=1, source_target_pairs={{0,2},{2,4},{4,6},{6,7},{7,5},{5,3},{3,1},{1,0},{8,10},{10,12},{12... | collective-permute-start | bytes 786440 | tf_op jit(solution)/shard_map/ppermute | solution.py:604
  47.4 41.3 %collective-permute-start.13 = (bf16[32,4096]{1,0:T(8,128)(2,1)S(1)}, bf16[32,4096]{1,0:T(8,128)(2,1)S(1)}, u32[]{:S(2)}, u32[]{:S(2)}) collective-permute-start(bf16[32,4096]{1,0:T(8,128)(2,1)S(1)} %collective-permute-done.12.refs_6_), channel_id=1, source_target_pairs={{2,0},{4,2},{6,4},{7,6},{5,7},{3,5},{1,3},{0,1},{10,8},{12,10},{14... | collective-permute-start | bytes 786440 | tf_op jit(solution)/shard_map/ppermute | solution.py:606
  51.3 70.9 %collective-permute-start.5 = (bf16[2,4,256,128]{3,2,1,0:T(8,128)(2,1)S(1)}, bf16[2,4,256,128]{3,2,1,0:T(8,128)(2,1)S(1)}, u32[]{:S(2)}, u32[]{:S(2)}) collective-permute-start(bf16[2,4,256,128]{3,2,1,0:T(8,128)(2,1)S(1)} %get-tuple-element.94), channel_id=1, source_target_pairs={{0,2},{1,3},{2,0},{3,1},{4,6},{5,7},{6,4},{7,5},{8,10},{9,11},{10,... | collective-permute-start | bytes 1572872 | tf_op jit(solution)/shard_map/ppermute | solution.py:643
  52.9 69.3 %collective-permute-start.6 = (bf16[2,4,256,128]{3,2,1,0:T(8,128)(2,1)S(1)}, bf16[2,4,256,128]{3,2,1,0:T(8,128)(2,1)S(1)}, u32[]{:S(2)}, u32[]{:S(2)}) collective-permute-start(bf16[2,4,256,128]{3,2,1,0:T(8,128)(2,1)S(1)} %get-tuple-element.95), channel_id=1, source_target_pairs={{0,3},{1,2},{2,1},{3,0},{4,7},{5,6},{6,5},{7,4},{8,11},{9,10},{10,... | collective-permute-start | bytes 1572872 | tf_op jit(solution)/shard_map/ppermute | solution.py:643
  95.4 25.9 %collective-permute-start.18 = (bf16[6,128,256]{2,1,0:T(8,128)(2,1)S(1)}, bf16[6,128,256]{2,1,0:T(8,128)(2,1)S(1)}, u32[]{:S(2)}, u32[]{:S(2)}) collective-permute-start(bf16[6,128,256]{2,1,0:T(8,128)(2,1)S(1)} %get-tuple-element.103.refs_6_.here_ref), channel_id=1, source_target_pairs={{0,4},{1,5},{2,6},{3,7},{4,0},{5,1},{6,2},{7,3},{8,12},{9,13},{10,... | collective-permute-start | bytes 1179656 | tf_op jit(solution)/shard_map/ppermute | solution.py:655
  95.4 35.5 %collective-permute-start.20 = (bf16[4,128,256]{2,1,0:T(8,128)(2,1)S(1)}, bf16[4,128,256]{2,1,0:T(8,128)(2,1)S(1)}, u32[]{:S(2)}, u32[]{:S(2)}) collective-permute-start(bf16[4,128,256]{2,1,0:T(8,128)(2,1)S(1)} %get-tuple-element.105.refs_6_), channel_id=1, source_target_pairs={{0,4},{1,5},{2,6},{3,7},{4,0},{5,1},{6,2},{7,3},{8,12},{9,13},{10,... | collective-permute-start | bytes 786440 | tf_op jit(solution)/shard_map/ppermute | solution.py:655
  121.3 9.7 %collective-permute-start.19 = (bf16[256,256]{1,0:T(8,128)(2,1)S(1)}, bf16[256,256]{1,0:T(8,128)(2,1)S(1)}, u32[]{:S(2)}, u32[]{:S(2)}) collective-permute-start(bf16[256,256]{1,0:T(8,128)(2,1)S(1)} %pick_new.1), channel_id=1, source_target_pairs={{0,0},{1,2},{2,4},{3,6},{4,1},{5,3},{6,5},{7,7},{8,8},{9,10},{10,1... | collective-permute-start | bytes 393224 | tf_op jit(solution)/shard_map/ppermute | solution.py:664
  131.0 24.9 %collective-permute-start.21 = (bf16[2,4,256,128]{3,2,1,0:T(8,128)(2,1)S(1)}, bf16[2,4,256,128]{3,2,1,0:T(8,128)(2,1)S(1)}, u32[]{:S(2)}, u32[]{:S(2)}) collective-permute-start(bf16[2,4,256,128]{3,2,1,0:T(8,128)(2,1)S(1)} %get-tuple-element.116), channel_id=1, source_target_pairs={{0,2},{1,3},{2,0},{3,1},{4,6},{5,7},{6,4},{7,5},{8,10},{9,11},{10,... | collective-permute-start | bytes 1572872 | tf_op jit(solution)/shard_map/ppermute | solution.py:643
  132.4 37.2 %collective-permute-start.22 = (bf16[2,4,256,128]{3,2,1,0:T(8,128)(2,1)S(1)}, bf16[2,4,256,128]{3,2,1,0:T(8,128)(2,1)S(1)}, u32[]{:S(2)}, u32[]{:S(2)}) collective-permute-start(bf16[2,4,256,128]{3,2,1,0:T(8,128)(2,1)S(1)} %get-tuple-element.117), channel_id=1, source_target_pairs={{0,3},{1,2},{2,1},{3,0},{4,7},{5,6},{6,5},{7,4},{8,11},{9,10},{10,... | collective-permute-start | bytes 1572872 | tf_op jit(solution)/shard_map/ppermute | solution.py:643
  140.1 40.0 %collective-permute-start.23 = (bf16[4,144,256]{2,1,0:T(8,128)(2,1)S(1)}, bf16[4,144,256]{2,1,0:T(8,128)(2,1)S(1)}, u32[]{:S(2)}, u32[]{:S(2)}) collective-permute-start(bf16[4,144,256]{2,1,0:T(8,128)(2,1)S(1)} %attend.10), channel_id=1, source_target_pairs={{0,4},{1,5},{2,6},{3,7},{4,0},{5,1},{6,2},{7,3},{8,12},{9,13},{10,... | collective-permute-start | bytes 884744 | tf_op jit(solution)/shard_map/ppermute | solution.py:690
  140.2 40.0 %collective-permute-start.24 = (bf16[4,144,256]{2,1,0:T(8,128)(2,1)S(1)}, bf16[4,144,256]{2,1,0:T(8,128)(2,1)S(1)}, u32[]{:S(2)}, u32[]{:S(2)}) collective-permute-start(bf16[4,144,256]{2,1,0:T(8,128)(2,1)S(1)} %attend.8), channel_id=1, source_target_pairs={{0,4},{1,5},{2,6},{3,7},{4,0},{5,1},{6,2},{7,3},{8,12},{9,13},{10,... | collective-permute-start | bytes 884744 | tf_op jit(solution)/shard_map/ppermute | solution.py:690
  185.6 9.6 %collective-permute-start.25 = (bf16[32,4096]{1,0:T(8,128)(2,1)S(1)}, bf16[32,4096]{1,0:T(8,128)(2,1)S(1)}, u32[]{:S(2)}, u32[]{:S(2)}) collective-permute-start(bf16[32,4096]{1,0:T(8,128)(2,1)S(1)} %get-tuple-element.137), channel_id=1, source_target_pairs={{0,2},{2,4},{4,6},{6,7},{7,5},{5,3},{3,1},{1,0},{8,10},{10,12},{12... | collective-permute-start | bytes 786440 | tf_op jit(solution)/shard_map/ppermute | solution.py:718
  185.7 9.7 %collective-permute-start.29 = (bf16[32,4096]{1,0:T(8,128)(2,1)S(1)}, bf16[32,4096]{1,0:T(8,128)(2,1)S(1)}, u32[]{:S(2)}, u32[]{:S(2)}) collective-permute-start(bf16[32,4096]{1,0:T(8,128)(2,1)S(1)} %convert_element_type.113), channel_id=1, source_target_pairs={{2,0},{4,2},{6,4},{7,6},{5,7},{3,5},{1,3},{0,1},{10,8},{12,10},{14... | collective-permute-start | bytes 786440 | tf_op jit(solution)/shard_map/ppermute | solution.py:718
  193.2 9.3 %collective-permute-start.32 = (bf16[32,4096]{1,0:T(8,128)(2,1)S(1)}, bf16[32,4096]{1,0:T(8,128)(2,1)S(1)}, u32[]{:S(2)}, u32[]{:S(2)}) collective-permute-start(bf16[32,4096]{1,0:T(8,128)(2,1)S(1)} %convert_element_type.120), channel_id=1, source_target_pairs={{0,2},{2,4},{4,6},{6,7},{7,5},{5,3},{3,1},{1,0},{8,10},{10,12},{12... | collective-permute-start | bytes 786440 | tf_op jit(solution)/shard_map/ppermute | solution.py:718
  193.3 9.4 %collective-permute-start.35 = (bf16[32,4096]{1,0:T(8,128)(2,1)S(1)}, bf16[32,4096]{1,0:T(8,128)(2,1)S(1)}, u32[]{:S(2)}, u32[]{:S(2)}) collective-permute-start(bf16[32,4096]{1,0:T(8,128)(2,1)S(1)} %get-tuple-element.148), channel_id=1, source_target_pairs={{2,0},{4,2},{6,4},{7,6},{5,7},{3,5},{1,3},{0,1},{10,8},{12,10},{14... | collective-permute-start | bytes 786440 | tf_op jit(solution)/shard_map/ppermute | solution.py:718
  195.3 12.8 %collective-permute-start.26 = (bf16[32,4096]{1,0:T(8,128)(2,1)S(1)}, bf16[32,4096]{1,0:T(8,128)(2,1)S(1)}, u32[]{:S(2)}, u32[]{:S(2)}) collective-permute-start(bf16[32,4096]{1,0:T(8,128)(2,1)S(1)} %add_convert_fusion.11), channel_id=1, source_target_pairs={{0,2},{2,4},{4,6},{6,7},{7,5},{5,3},{3,1},{1,0},{8,10},{10,12},{12... | collective-permute-start | bytes 786440 | tf_op jit(solution)/shard_map/ppermute | solution.py:718
  195.5 12.7 %collective-permute-start.30 = (bf16[32,4096]{1,0:T(8,128)(2,1)S(1)}, bf16[32,4096]{1,0:T(8,128)(2,1)S(1)}, u32[]{:S(2)}, u32[]{:S(2)}) collective-permute-start(bf16[32,4096]{1,0:T(8,128)(2,1)S(1)} %add_convert_fusion.8), channel_id=1, source_target_pairs={{2,0},{4,2},{6,4},{7,6},{5,7},{3,5},{1,3},{0,1},{10,8},{12,10},{14... | collective-permute-start | bytes 786440 | tf_op jit(solution)/shard_map/ppermute | solution.py:718
  202.5 11.2 %collective-permute-start.33 = (bf16[32,4096]{1,0:T(8,128)(2,1)S(1)}, bf16[32,4096]{1,0:T(8,128)(2,1)S(1)}, u32[]{:S(2)}, u32[]{:S(2)}) collective-permute-start(bf16[32,4096]{1,0:T(8,128)(2,1)S(1)} %add_convert_fusion.5), channel_id=1, source_target_pairs={{0,2},{2,4},{4,6},{6,7},{7,5},{5,3},{3,1},{1,0},{8,10},{10,12},{12... | collective-permute-start | bytes 786440 | tf_op jit(solution)/shard_map/ppermute | solution.py:718
  202.7 11.2 %collective-permute-start.36 = (bf16[32,4096]{1,0:T(8,128)(2,1)S(1)}, bf16[32,4096]{1,0:T(8,128)(2,1)S(1)}, u32[]{:S(2)}, u32[]{:S(2)}) collective-permute-start(bf16[32,4096]{1,0:T(8,128)(2,1)S(1)} %add_convert_fusion.3), channel_id=1, source_target_pairs={{2,0},{4,2},{6,4},{7,6},{5,7},{3,5},{1,3},{0,1},{10,8},{12,10},{14... | collective-permute-start | bytes 786440 | tf_op jit(solution)/shard_map/ppermute | solution.py:718
  208.2 11.2 %collective-permute-start.27 = (bf16[32,4096]{1,0:T(8,128)(2,1)S(1)}, bf16[32,4096]{1,0:T(8,128)(2,1)S(1)}, u32[]{:S(2)}, u32[]{:S(2)}) collective-permute-start(bf16[32,4096]{1,0:T(8,128)(2,1)S(1)} %add_convert_fusion.10), channel_id=1, source_target_pairs={{0,2},{2,4},{4,6},{6,7},{7,5},{5,3},{3,1},{1,0},{8,10},{10,12},{12... | collective-permute-start | bytes 786440 | tf_op jit(solution)/shard_map/ppermute | solution.py:718
  208.3 16.1 %collective-permute-start.31 = (bf16[32,4096]{1,0:T(8,128)(2,1)S(1)}, bf16[32,4096]{1,0:T(8,128)(2,1)S(1)}, u32[]{:S(2)}, u32[]{:S(2)}) collective-permute-start(bf16[32,4096]{1,0:T(8,128)(2,1)S(1)} %add_convert_fusion.7), channel_id=1, source_target_pairs={{2,0},{4,2},{6,4},{7,6},{5,7},{3,5},{1,3},{0,1},{10,8},{12,10},{14... | collective-permute-start | bytes 786440 | tf_op jit(solution)/shard_map/ppermute | solution.py:718
  213.8 14.5 %collective-permute-start.34 = (bf16[32,4096]{1,0:T(8,128)(2,1)S(1)}, bf16[32,4096]{1,0:T(8,128)(2,1)S(1)}, u32[]{:S(2)}, u32[]{:S(2)}) collective-permute-start(bf16[32,4096]{1,0:T(8,128)(2,1)S(1)} %add_convert_fusion.4), channel_id=1, source_target_pairs={{0,2},{2,4},{4,6},{6,7},{7,5},{5,3},{3,1},{1,0},{8,10},{10,12},{12... | collective-permute-start | bytes 786440 | tf_op jit(solution)/shard_map/ppermute | solution.py:718
  213.9 8.7 %collective-permute-start.37 = (bf16[32,4096]{1,0:T(8,128)(2,1)S(1)}, bf16[32,4096]{1,0:T(8,128)(2,1)S(1)}, u32[]{:S(2)}, u32[]{:S(2)}) collective-permute-start(bf16[32,4096]{1,0:T(8,128)(2,1)S(1)} %add_convert_fusion.2), channel_id=1, source_target_pairs={{2,0},{4,2},{6,4},{7,6},{5,7},{3,5},{1,3},{0,1},{10,8},{12,10},{14... | collective-permute-start | bytes 786440 | tf_op jit(solution)/shard_map/ppermute | solution.py:718
  219.4 8.8 %collective-permute-start.28 = (bf16[32,4096]{1,0:T(8,128)(2,1)S(1)}, bf16[32,4096]{1,0:T(8,128)(2,1)S(1)}, u32[]{:S(2)}, u32[]{:S(2)}) collective-permute-start(bf16[32,4096]{1,0:T(8,128)(2,1)S(1)} %add_convert_fusion.9), channel_id=1, source_target_pairs={{0,2},{2,4},{4,6},{6,7},{7,5},{5,3},{3,1},{1,0},{8,10},{10,12},{12... | collective-permute-start | bytes 786440 | tf_op jit(solution)/shard_map/ppermute | solution.py:718
  222.6 6.4 %collective-permute-start.38 = (bf16[32,4096]{1,0:T(8,128)(2,1)S(1)}, bf16[32,4096]{1,0:T(8,128)(2,1)S(1)}, u32[]{:S(2)}, u32[]{:S(2)}) collective-permute-start(bf16[32,4096]{1,0:T(8,128)(2,1)S(1)} %add_convert_fusion.1), channel_id=1, source_target_pairs={{2,0},{4,2},{6,4},{7,6},{5,7},{3,5},{1,3},{0,1},{10,8},{12,10},{14... | collective-permute-start | bytes 786440 | tf_op jit(solution)/shard_map/ppermute | solution.py:718

commit v11 on v9

--- a/solution.py
+++ b/solution.py
@@ -24,7 +24,7 @@
 TILE_COLS = 256
 PAIR = 2
 STATS = 16
-HALVES = 2
+HALVES = 1
 DEPTH_TILE = 1024
 WIDTH_TILE = 1024
 SLOTS = 3
@@ -84,44 +84,37 @@
     return start, wait
 
 
-def project_kernel(n_blocks, chunk, is_last, place_ref, *refs):
+def project_kernel(n_blocks, n_weights, chunk, is_last, place_ref, *refs):
     refs = list(refs)
     take = lambda count: [refs.pop(0) for _ in range(count)]
-    blocks = take(n_blocks)
-    wq_ref, wkv_ref = take(2)
-    if chunk:
-        prev_q, prev_kv = take(2)
+    blocks, weights = take(n_blocks), take(n_weights)
+    prev = take(n_weights) if chunk else None
     if is_last:
-        cos_ref, sin_ref = take(2)
-        total_q, total_kv, natural, natural_kv = refs[-7:-3]
-        outs = refs[:-7]
+        tables, (out, total, natural) = take(len(refs) - 5), take(3)
+        totals = [total]
     else:
-        total_q, total_kv = take(2)
-    wq_slots, wkv_slots, sems = refs[-3:]
-    tile = wq_slots.shape[1]
+        totals = take(n_weights)
+    buffers, sems = take(n_weights), refs[0]
+    tile = buffers[0].shape[1]
     depth = blocks[0].shape[1]
     count = depth // tile
     rows_of = lambda ref: lambda step: ref.at[pl.ds(chunk * depth + step * tile, tile), :]
-    start, wait = stream([rows_of(wq_ref), rows_of(wkv_ref)], [wq_slots, wkv_slots], sems)
+    start, wait = stream([rows_of(ref) for ref in weights], buffers, sems)
 
     for step in range(min(SLOTS, count)):
         start(step)
     for step in range(count):
         wait(step)
-        slot = step % SLOTS
         cols = slice(step * tile, (step + 1) * tile)
         rows = jnp.concatenate([b[:, cols] for b in blocks], axis=0)
-        part_q = jnp.dot(rows, wq_slots[slot], preferred_element_type=jnp.float32)
-        part_kv = jnp.dot(rows, wkv_slots[slot], preferred_element_type=jnp.float32)
-        if step:
-            total_q[...] += part_q
-            total_kv[...] += part_kv
-        elif chunk:
-            total_q[...] = prev_q[...] + part_q
-            total_kv[...] = prev_kv[...] + part_kv
-        else:
-            total_q[...] = part_q
-            total_kv[...] = part_kv
+        for i, (buffer, total) in enumerate(zip(buffers, totals)):
+            term = jnp.dot(rows, buffer[step % SLOTS], preferred_element_type=jnp.float32)
+            if step:
+                total[...] += term
+            elif chunk:
+                total[...] = prev[i][...] + term
+            else:
+                total[...] = term
         if step + SLOTS < count:
             start(step + SLOTS)
 
@@ -130,11 +123,13 @@
         for block in range(SEL // height):
             here = slice(block * height, (block + 1) * height)
             there = pl.ds(pl.multiple_of(place_ref[block] * height, height), height)
-            natural[there, :] = total_q[here, :]
-            natural_kv[there, :] = total_kv[here, :]
-        heads_here = total_q.shape[1] // HD
+            natural[there, :] = totals[0][here, :]
+        if not tables:
+            out[...] = natural[...].astype(out.dtype)
+            return
+        cos_ref, sin_ref = tables
+        heads_here = natural.shape[1] // HD
         tile_q = TILE_COLS // heads_here
-        per_half = SEL // tile_q // HALVES
         for index in range(SEL // tile_q):
             here = slice(index * tile_q, (index + 1) * tile_q)
             stacked = jnp.concatenate(
@@ -146,56 +141,37 @@
                 ],
                 axis=0,
             )
-            outs[index // per_half][index % per_half] = stacked.T.astype(jnp.bfloat16)
-        if len(outs) > HALVES:
-            outs[-1][...] = natural_kv[...].astype(jnp.bfloat16)
-        else:
-            for index in range(SEL // HD):
-                outs[-1][per_half + index] = natural_kv[
-                    index * HD : (index + 1) * HD, :
-                ].astype(jnp.bfloat16)
-
-
-def project(place, blocks, w_query, w_keyval, prev, tables, chunk):
+            out[index] = stacked.T.astype(out.dtype)
+
+
+def project(place, blocks, weights, prev, chunk, tables=()):
     depth = blocks[0].shape[1]
-    q_cols, kv_cols = w_query.shape[1], w_keyval.shape[1]
+    widths = [w.shape[1] for w in weights]
     tile = min(DEPTH_TILE, depth)
     is_last = chunk + 1 == CHUNKS
     vmem = pl.BlockSpec(memory_space=pltpu.VMEM)
     hbm = pl.BlockSpec(memory_space=pltpu.HBM)
-    total = [((SEL, q_cols), jnp.float32), ((SEL, kv_cols), jnp.float32)]
-    scratch = []
+    totals = [((SEL, width), jnp.float32) for width in widths]
     if is_last:
-        per_half = SEL * q_cols // (HD * TILE_COLS * HALVES)
-        behind = SEL // HD if kv_cols == TILE_COLS else 0
-        outs = [(per_half, HD, TILE_COLS)] * (HALVES - 1) + [(per_half + behind, HD, TILE_COLS)]
-        if not behind:
-            outs.append((SEL, kv_cols))
-        outs = [(shape, jnp.bfloat16) for shape in outs]
-        scratch = total + total
+        shape = (SEL * widths[0] // (HD * TILE_COLS), HD, TILE_COLS) if tables else (SEL, widths[0])
+        outs, scratch = [(shape, jnp.bfloat16)], totals * 2
     else:
-        outs = total
-    extra = ([] if prev is None else list(prev)) + (list(tables) if is_last else [])
+        outs, scratch = totals, []
     return pl.pallas_call(
-        functools.partial(project_kernel, len(blocks), chunk, is_last),
+        functools.partial(project_kernel, len(blocks), len(weights), chunk, is_last),
         in_specs=[pl.BlockSpec(memory_space=pltpu.SMEM)]
         + [vmem] * len(blocks)
-        + [hbm] * 2
-        + [vmem] * len(extra),
+        + [hbm] * len(weights)
+        + [vmem] * (len(prev) + len(tables)),
         out_specs=[vmem] * len(outs),
         out_shape=[jax.ShapeDtypeStruct(*o) for o in outs],
         scratch_shapes=[pltpu.VMEM(*x) for x in scratch]
-        + [
-            pltpu.VMEM((SLOTS, tile, q_cols), jnp.bfloat16),
-            pltpu.VMEM((SLOTS, tile, kv_cols), jnp.bfloat16),
-            pltpu.SemaphoreType.DMA((2 * CUTS, SLOTS)),
-        ],
+        + [pltpu.VMEM((SLOTS, tile, width), jnp.bfloat16) for width in widths]
+        + [pltpu.SemaphoreType.DMA((len(weights) * CUTS, SLOTS))],
         compiler_params=megabytes(16),
-        cost_estimate=cost(
-            2 * SEL * depth * (q_cols + kv_cols), 2 * depth * (q_cols + kv_cols + SEL)
-        ),
+        cost_estimate=cost(2 * SEL * depth * sum(widths), 2 * depth * (sum(widths) + SEL)),
         name="project",
-    )(place, *blocks, w_query, w_keyval, *extra)
+    )(place, *blocks, *weights, *prev, *tables)
 
 
 def select_kernel(n_dest, n_src, place_ref, slot_ref, head_ref, *refs):
@@ -392,27 +368,22 @@
     )(*operands)
 
 
-def pick_kernel(n_tiles, side_ref, here_ref, there_ref, out_ref):
-    def pick(keys_ref, values_ref, head):
-        cols = slice(head * HD, (head + 1) * HD)
-        for index in range(SEL // HD):
-            rows = slice(index * HD, (index + 1) * HD)
-            out_ref[rows, :HD] = keys_ref[n_tiles + index][:, cols]
-            out_ref[rows, HD:] = values_ref[n_tiles + index][:, cols]
-
+def pick_kernel(side_ref, here_ref, there_ref, out_ref):
     @pl.when(side_ref[0] == 1)
     def _():
-        pick(here_ref, there_ref, 0)
+        out_ref[:, :HD] = here_ref[:, :HD]
+        out_ref[:, HD:] = there_ref[:, :HD]
 
     @pl.when(side_ref[0] == 0)
     def _():
-        pick(there_ref, here_ref, 1)
-
-
-def pick_new(side, here, there, n_tiles):
+        out_ref[:, :HD] = there_ref[:, HD:]
+        out_ref[:, HD:] = here_ref[:, HD:]
+
+
+def pick_new(side, here, there):
     vmem = pl.BlockSpec(memory_space=pltpu.VMEM)
     return pl.pallas_call(
-        functools.partial(pick_kernel, n_tiles),
+        pick_kernel,
         in_specs=[pl.BlockSpec(memory_space=pltpu.SMEM), vmem, vmem],
         out_specs=vmem,
         out_shape=jax.ShapeDtypeStruct((SEL, 2 * HD), jnp.bfloat16),
@@ -601,7 +572,8 @@
         if k == far - 1:
             sent = select_docs(sources, holder, slot, takers, tp_size)
             first[-1], *sent = lax.optimization_barrier((first[-1], *sent))
-    projected = None
+    weights = [w_keyval, w_query]
+    sums = []
     for chunk, held in enumerate(streams):
         blocks = [held["before"][0]]
         for k in range(1, far):
@@ -609,9 +581,17 @@
         blocks.append(held["behind" if chunk % 2 else "before"][far])
         if rows % 16:
             blocks = [jnp.concatenate(blocks, axis=0)]
-        projected = project(
-            place, blocks, w_query, w_keyval, projected, (cosine, sine_part), chunk
-        )
+        if chunk + 1 < CHUNKS:
+            sums = project(place, blocks, weights, sums, chunk)
+    across = [(i, i ^ middle) for i in range(tp_size)]
+    (keyval,) = project(place, blocks, weights[:1], sums[:1], CHUNKS - 1)
+    keyval, *blocks = lax.optimization_barrier((keyval, *blocks))
+    their_keyval = lax.ppermute(keyval, "tp", across)
+    (queries,) = project(
+        place, blocks, weights[1:], sums[1:], CHUNKS - 1, (cosine, sine_part)
+    )
+    queries, their_keyval = lax.optimization_barrier((queries, their_keyval))
+
     def exchange(kept):
         return [
             lax.ppermute(kept[j], "tp", [(i, i ^ j) for i in range(tp_size)]) if j else kept[j]
@@ -619,23 +599,19 @@
         ]
 
     own, partners = sent[:middle], exchange(sent[middle:])
-    own, partners = lax.optimization_barrier((own, partners))
+    own, *partners[1:3] = lax.optimization_barrier((own, *partners[1:3]))
     chunks = [exchange(own), partners]
-    queries = projected[:HALVES]
-    n_tiles = queries[0].shape[0]
-    across = [(i, i ^ middle) for i in range(tp_size)]
-    their_queries = [None] * HALVES
-    for part in reversed(range(HALVES)):
-        their_queries[part] = lax.ppermute(queries[part], "tp", across)
+    n_tiles = queries.shape[0]
+    their_queries = lax.ppermute(queries, "tp", across)
 
     if tp_size == KVH:
         new = lax.ppermute(
-            pick_new(side, queries[-1], their_queries[-1], n_tiles),
+            pick_new(side, keyval, their_keyval),
             "tp",
             [(i, 2 * i if i < middle else 2 * (i - middle) + 1) for i in range(tp_size)],
         )
     else:
-        everyone = lax.all_gather(projected[-1], "tp", axis=1, tiled=True)
+        everyone = lax.all_gather(keyval, "tp", axis=1, tiled=True)
         my_head = me * KVH // tp_size
         new = jnp.concatenate(
             [
@@ -645,22 +621,12 @@
             axis=1,
         )
 
-    def attend_half(part, asked, slot, extra):
-        return attend(
-            chunks[slot], dead, first_pos, selected, q_pos, asked[part], part * n_tiles, n_tiles, extra
-        )
-
-    theirs = [None] * HALVES
-    for part in reversed(range(HALVES)):
-        (packed,) = attend_half(part, their_queries, 1, [])
-        if part:
-            packed, new, their_queries[part - 1] = lax.optimization_barrier(
-                (packed, new, their_queries[part - 1])
-            )
-        theirs[part] = lax.ppermute(packed, "tp", across)
-    fresh = [cosine, sine_part, new]
-    mine = [attend_half(part, queries, 0, fresh) for part in range(HALVES)]
-    attention = merge(mine, theirs)
+    metadata = (dead, first_pos, selected, q_pos)
+    their_queries, new = lax.optimization_barrier((their_queries, new))
+    (packed,) = attend(chunks[1], *metadata, their_queries, 0, n_tiles, [])
+    theirs = lax.ppermute(packed, "tp", across)
+    mine = attend(chunks[0], *metadata, queries, 0, n_tiles, [cosine, sine_part, new])
+    attention = merge([mine], [theirs])
 
     finished = []
     for chunk in range(CHUNKS):

time: 198 us -> 191 us (0.965)
  waiting for transfers between devices: 76.5 us -> 49 us
  starting transfers between devices: 48.5 us -> 67.9 us
    ppermute x6, starting transfers between devices: 7.34 us -> 27.4 us  [exchange(): lax.ppermute(kept[j], 'tp', [(i, i ^ j) for i in range(tp_size)])]
    ppermute x5 -> x4, waiting for transfers between devices: 21.4 us -> 5.07 us  [the longest x1 5.06 us: per_device(): theirs = lax.ppermute(packed, 'tp', across)]
    ppermute x6, waiting for transfers between devices: 15.6 us -> 4.34 us  [exchange(): lax.ppermute(kept[j], 'tp', [(i, i ^ j) for i in range(tp_size)])]
    pallas_call x3 -> x4, Pallas kernels: 13 us -> 15.5 us  [the longest x3 15.5 us: project(): pl.pallas_call(functools.partial(project_kernel, len(blocks), len(weights...]
    pallas_call x4 -> x2, Pallas kernels: 31 us -> 29 us  [attend(): pl.pallas_call(functools.partial(attend_kernel, n_chunks, bool(fresh), n_...]
    ppermute x5 -> x4, starting transfers between devices: 8.57 us -> 8.68 us  [the longest x1 4.69 us: per_device(): theirs = lax.ppermute(packed, 'tp', across)]
  transfers between devices with their start and end apart: 40 -> 39, of which waited for: 18 -> 16; matrix products, arithmetic and copies ran while one was open for 3% -> 3% of each run, Pallas kernels for 26% -> 28%
where the time goes in v11:
time: 191 us; the launch traced here: 190 us
  starting transfers between devices  67.9 us (36%)
  Pallas kernels  58.3 us (31%)
  waiting for transfers between devices  49 us (26%)
  local copies, waits for them, and re-layouts  7.62 us (4%)
  other arithmetic  7.25 us (4%)
    pallas_call x2, Pallas kernels, attend(): pl.pallas_call(functools.partial(attend_kernel, n_chunks, bool(fresh), n_...  29 us
    ppermute x6, starting transfers between devices, exchange(): lax.ppermute(kept[j], 'tp', [(i, i ^ j) for i in range(tp_size)])  27.4 us
    ppermute x14, waiting for transfers between devices, per_device(): held = lax.ppermute(term.astype(jnp.bfloat16), 'tp', pairs)  22.5 us
    pallas_call x3, Pallas kernels, project(): pl.pallas_call(functools.partial(project_kernel, len(blocks), len(weights...  15.5 us
    ppermute x14, starting transfers between devices, per_device(): held = lax.ppermute(term.astype(jnp.bfloat16), 'tp', pairs)  14.9 us
    ppermute x7, waiting for transfers between devices, per_device(): held['behind'].append(lax.ppermute(held['behind'][-1], 'tp', back))  14 us
    ppermute x7, starting transfers between devices, per_device(): held['before'].append(lax.ppermute(held['before'][-1], 'tp', forth))  11.5 us
    pallas_call x2, Pallas kernels, project_out(): pl.pallas_call(functools.partial(out_kernel, n_blocks, chunk * width), in...  10.2 us
  transfers between devices with their start and end apart: 39, of which 16 were waited for; matrix products, arithmetic and copies ran while one was open for 3% of the time, Pallas kernels for 28%

profile of v11, /device:TPU:0, one launch (start us, length us, event | category | flops | bytes accessed | tf_op | source)
XLA Modules:
  0.0 190.4 jit_solution(17545332051401204234)
XLA Ops:
  0.0 1.2 fusion
  1.3 1.2 fusion.2
  2.5 5.5 %copy.16 = bf16[4,256,2,1024]{3,1,2,0:T(8,128)(2,1)} copy(bf16[4,256,2,1024]{3,2,1,0:T(2,128)(2,1)} %param.15) | data formatting | bytes 8388608 | tf_op jit(solution)/shard_map/optimization_barrier | solution.py:519
  8.5 2.6 %collective-permute-start = (bf16[32,4096]{1,0:T(8,128)(2,1)S(1)}, bf16[32,4096]{1,0:T(8,128)(2,1)S(1)}, u32[]{:S(2)}, u32[]{:S(2)}) collective-permute-start(bf16[32,4096]{1,0:T(8,128)(2,1)S(1)} %get-tuple-element.146.refs_0_), channel_id=1, source_target_pairs={{0,2},{2,4},{4,6},{6,7},{7,5},{5,3},{3,1},{1,0},{8,10},{10,12},{12... | collective-permute-start | bytes 786440 | tf_op jit(solution)/shard_map/ppermute | solution.py:551
  11.2 2.0 %collective-permute-start.10 = (bf16[32,4096]{1,0:T(8,128)(2,1)S(1)}, bf16[32,4096]{1,0:T(8,128)(2,1)S(1)}, u32[]{:S(2)}, u32[]{:S(2)}) collective-permute-start(bf16[32,4096]{1,0:T(8,128)(2,1)S(1)} %get-tuple-element.105.refs_0_), channel_id=1, source_target_pairs={{2,0},{4,2},{6,4},{7,6},{5,7},{3,5},{1,3},{0,1},{10,8},{12,10},{14... | collective-permute-start | bytes 786440 | tf_op jit(solution)/shard_map/ppermute | solution.py:553
  13.6 1.3 compare_reduce_fusion
  15.1 0.5 fusion.3
  15.7 2.6 %collective-permute-done.refs_1_ = bf16[32,4096]{1,0:T(8,128)(2,1)S(1)} collective-permute-done((bf16[32,4096]{1,0:T(8,128)(2,1)S(1)}, bf16[32,4096]{1,0:T(8,128)(2,1)S(1)}, u32[]{:S(2)}, u32[]{:S(2)}) %collective-permute-start) | collective-permute-done | bytes 262176 | tf_op jit(solution)/shard_map/ppermute | solution.py:551
  18.3 2.0 %collective-permute-start.1 = (bf16[32,4096]{1,0:T(8,128)(2,1)S(1)}, bf16[32,4096]{1,0:T(8,128)(2,1)S(1)}, u32[]{:S(2)}, u32[]{:S(2)}) collective-permute-start(bf16[32,4096]{1,0:T(8,128)(2,1)S(1)} %collective-permute-done.refs_1_), channel_id=1, source_target_pairs={{0,2},{2,4},{4,6},{6,7},{7,5},{5,3},{3,1},{1,0},{8,10},{10,12},{12... | collective-permute-start | bytes 786440 | tf_op jit(solution)/shard_map/ppermute | solution.py:551
  20.3 0.7 dynamic-slice_bitcast_fusion.place_ref
  21.1 4.1 %collective-permute-done.10.refs_2_ = bf16[32,4096]{1,0:T(8,128)(2,1)S(1)} collective-permute-done((bf16[32,4096]{1,0:T(8,128)(2,1)S(1)}, bf16[32,4096]{1,0:T(8,128)(2,1)S(1)}, u32[]{:S(2)}, u32[]{:S(2)}) %collective-permute-start.10) | collective-permute-done | bytes 262176 | tf_op jit(solution)/shard_map/ppermute | solution.py:553
  25.7 0.5 broadcast.178
  26.2 0.7 reduce.3
  27.0 1.7 collective-permute-start.17
  28.8 0.6 collective-permute-done.1.refs_3_
  29.3 0.6 broadcast_in_dim.20.refs_4_
  29.9 1.8 collective-permute-start.2
  31.8 1.6 collective-permute-start.11
  33.4 1.1 collective-permute-done.12.refs_4_
  34.7 5.4 %collective-permute-done.17.refs_4_ = bf16[32,4096]{1,0:T(8,128)(2,1)S(1)} collective-permute-done((bf16[32,4096]{1,0:T(8,128)(2,1)S(1)}, bf16[32,4096]{1,0:T(8,128)(2,1)S(1)}, u32[]{:S(2)}, u32[]{:S(2)}) %collective-permute-start.17) | collective-permute-done | bytes 262176 | tf_op jit(solution)/shard_map/ppermute | solution.py:553
  40.3 3.3 %select_docs.1 = (bf16[2,4,256,128]{3,2,1,0:T(8,128)(2,1)S(1)}, bf16[2,4,256,128]{3,2,1,0:T(8,128)(2,1)S(1)}, bf16[2,4,256,128]{3,2,1,0:T(8,128)(2,1)S(1)}, bf16...) custom-call(s32[4]{0:T(128)S(1)} %get-tuple-element.79.place_ref, ...), custom_call_target="tpu_custom_call" | custom-call | bytes 8388608 | tf_op jit(solution)/shard_map/select_docs/pallas_call | solution.py:205
  43.6 1.8 collective-permute-start.19
  45.4 1.6 collective-permute-start.13
  47.9 3.4 %collective-permute-done.18.refs_6_ = bf16[32,4096]{1,0:T(8,128)(2,1)S(1)} collective-permute-done((bf16[32,4096]{1,0:T(8,128)(2,1)S(1)}, bf16[32,4096]{1,0:T(8,128)(2,1)S(1)}, u32[]{:S(2)}, u32[]{:S(2)}) %collective-permute-start.18) | collective-permute-done | bytes 262176 | tf_op jit(solution)/shard_map/ppermute | solution.py:553
  51.3 1.6 collective-permute-start.5
  52.9 6.4 %project.3 = (f32[256,256]{1,0:T(8,128)S(1)}, f32[256,1024]{1,0:T(8,128)S(1)}) custom-call(s32[8]{0:T(128)S(1)} %dynamic-slice_bitcast_fusion.place_ref, bf16[32,4096]{1,0:T(8,128)(2,1)S(1)} %get-tuple-element.146.refs_0_, bf16[32,4096]{1,0:T(8,128)(2,1)S(1)} %collective-permute-done.refs_1_, bf16[32,4096]{1,0:T(8,128)(2,1)S(1)} %collective-permute-done.16.refs_2_, ...), custom_call_target="tpu_custom_call" | custom-call | flops 2684354560 | bytes 12582912 | tf_op jit(solution)/shard_map/project/pallas_call | solution.py:160
  59.3 3.4 %project.4.here_ref = bf16[256,256]{1,0:T(8,128)(2,1)S(1)} custom-call(s32[8]{0:T(128)S(1)} %dynamic-slice_bitcast_fusion.place_ref, bf16[32,4096]{1,0:T(8,128)(2,1)S(1)} %get-tuple-element.105.refs_0_, bf16[32,4096]{1,0:T(8,128)(2,1)S(1)} %collective-permute-done.9.refs_1_, bf16[32,4096]{1,0:T(8,128)(2,1)S(1)} %collective-permute-done.10.refs_2_, ...), custom_call_target="tpu_custom_call" | custom-call | flops 536870912 | bytes 4194304 | tf_op jit(solution)/shard_map/project/pallas_call | solution.py:160
  62.8 2.6 %collective-permute-start.20 = (bf16[256,256]{1,0:T(8,128)(2,1)S(1)}, bf16[256,256]{1,0:T(8,128)(2,1)S(1)}, u32[]{:S(2)}, u32[]{:S(2)}) collective-permute-start(bf16[256,256]{1,0:T(8,128)(2,1)S(1)} %project.4.here_ref), channel_id=1, source_target_pairs={{0,4},{1,5},{2,6},{3,7},{4,0},{5,1},{6,2},{7,3},{8,12},{9,13},{10,... | collective-permute-start | bytes 393224 | tf_op jit(solution)/shard_map/ppermute | solution.py:589
  65.3 5.7 %project.5.refs_6_ = bf16[8,128,256]{2,1,0:T(8,128)(2,1)S(1)} custom-call(s32[8]{0:T(128)S(1)} %dynamic-slice_bitcast_fusion.place_ref, bf16[32,4096]{1,0:T(8,128)(2,1)S(1)} %get-tuple-element.105.refs_0_, bf16[32,4096]{1,0:T(8,128)(2,1)S(1)} %collective-permute-done.9.refs_1_, bf16[32,4096]{1,0:T(8,128)(2,1)S(1)} %collective-permute-done.10.refs_2_, ...), custom_call_target="tpu_custom_call" | custom-call | flops 2147483648 | bytes 10485760 | tf_op jit(solution)/shard_map/project/pallas_call | solution.py:160
  71.1 0.6 collective-permute-start.21
  71.6 14.6 %collective-permute-start.23 = (bf16[2,4,256,128]{3,2,1,0:T(8,128)(2,1)S(1)}, bf16[2,4,256,128]{3,2,1,0:T(8,128)(2,1)S(1)}, u32[]{:S(2)}, u32[]{:S(2)}) collective-permute-start(bf16[2,4,256,128]{3,2,1,0:T(8,128)(2,1)S(1)} %get-tuple-element.127), channel_id=1, source_target_pairs={{0,3},{1,2},{2,1},{3,0},{4,7},{5,6},{6,5},{7,4},{8,11},{9,10},{10,... | collective-permute-start | bytes 1572872 | tf_op jit(solution)/shard_map/ppermute | solution.py:597
  86.2 0.8 collective-permute-start.22
  87.1 1.6 collective-permute-start.6
  89.0 8.9 %collective-permute-start.8 = (bf16[2,4,256,128]{3,2,1,0:T(8,128)(2,1)S(1)}, bf16[2,4,256,128]{3,2,1,0:T(8,128)(2,1)S(1)}, u32[]{:S(2)}, u32[]{:S(2)}) collective-permute-start(bf16[2,4,256,128]{3,2,1,0:T(8,128)(2,1)S(1)} %get-tuple-element.100), channel_id=1, source_target_pairs={{0,3},{1,2},{2,1},{3,0},{4,7},{5,6},{6,5},{7,4},{8,11},{9,10},{10,... | collective-permute-start | bytes 1572872 | tf_op jit(solution)/shard_map/ppermute | solution.py:597
  97.9 2.2 %collective-permute-done.23.refs_3_ = bf16[2,4,256,128]{3,2,1,0:T(8,128)(2,1)S(1)} collective-permute-done((bf16[2,4,256,128]{3,2,1,0:T(8,128)(2,1)S(1)}, bf16[2,4,256,128]{3,2,1,0:T(8,128)(2,1)S(1)}, u32[]{:S(2)}, u32[]{:S(2)}) %collective-permute-start.23) | collective-permute-done | bytes 524320 | tf_op jit(solution)/shard_map/ppermute | solution.py:597
  100.1 13.6 %attend.3 = bf16[8,144,256]{2,1,0:T(8,128)(2,1)S(1)} custom-call(s32[16]{0:T(128)S(1)} %select_n.42.first_ref, s32[256]{0:T(256)S(1)} %bitcast.23, bf16[2,4,256,128]{3,2,1,0:T(8,128)(2,1)S(1)} %get-tuple-element.124.refs_0_, bf16[2,4,256,128]{3,2,1,0:T(8,128)(2,1)S(1)} %collective-permute-done.4.refs_1_, ...), custom_call_target="tpu_custom_call" | custom-call | flops 2147483648 | bytes 2097152 | tf_op jit(solution)/shard_map/attend/pallas_call | solution.py:357
  113.7 4.7 %collective-permute-start.24 = (bf16[8,144,256]{2,1,0:T(8,128)(2,1)S(1)}, bf16[8,144,256]{2,1,0:T(8,128)(2,1)S(1)}, u32[]{:S(2)}, u32[]{:S(2)}) collective-permute-start(bf16[8,144,256]{2,1,0:T(8,128)(2,1)S(1)} %attend.3), channel_id=1, source_target_pairs={{0,4},{1,5},{2,6},{3,7},{4,0},{5,1},{6,2},{7,3},{8,12},{9,13},{10,... | collective-permute-start | bytes 1769480 | tf_op jit(solution)/shard_map/ppermute | solution.py:627
  118.4 2.2 %collective-permute-done.8.refs_3_ = bf16[2,4,256,128]{3,2,1,0:T(8,128)(2,1)S(1)} collective-permute-done((bf16[2,4,256,128]{3,2,1,0:T(8,128)(2,1)S(1)}, bf16[2,4,256,128]{3,2,1,0:T(8,128)(2,1)S(1)}, u32[]{:S(2)}, u32[]{:S(2)}) %collective-permute-start.8) | collective-permute-done | bytes 524320 | tf_op jit(solution)/shard_map/ppermute | solution.py:597
  120.6 15.4 %attend.2 = (f32[8,1,256]{2,1,0:T(1,128)S(1)}, f32[8,1,256]{2,1,0:T(1,128)S(1)}, f32[8,128,256]{2,1,0:T(8,128)S(1)}) custom-call(s32[16]{0:T(128)S(1)} %select_n.42.first_ref, s32[256]{0:T(256)S(1)} %bitcast.24, bf16[2,4,256,128]{3,2,1,0:T(8,128)(2,1)S(1)} %get-tuple-element.97.refs_0_, bf16[2,4,256,128]{3,2,1,0:T(8,128)(2,1)S(1)} %collective-permute-done.6.refs_1_, ...), custom_call_target="tpu_custom_call" | custom-call | flops 2147483648 | bytes 2097152 | tf_op jit(solution)/shard_map/attend/pallas_call | solution.py:357
  135.9 5.1 %collective-permute-done.24.refs_3_ = bf16[8,144,256]{2,1,0:T(8,128)(2,1)S(1)} collective-permute-done((bf16[8,144,256]{2,1,0:T(8,128)(2,1)S(1)}, bf16[8,144,256]{2,1,0:T(8,128)(2,1)S(1)}, u32[]{:S(2)}, u32[]{:S(2)}) %collective-permute-start.24) | collective-permute-done | bytes 589856 | tf_op jit(solution)/shard_map/ppermute | solution.py:627
  141.4 5.1 %project_out.2 = (f32[32,4096]{1,0:T(8,128)S(1)}, f32[32,4096]{1,0:T(8,128)S(1)}, f32[32,4096]{1,0:T(8,128)S(1)}, f32[32,4096]{1,0:T(8,128)S(1)}, f32[32,4096]{1...) custom-call(s32[8]{0:T(128)S(1)} %dynamic-slice_bitcast_fusion.place_ref, ...), custom_call_target="tpu_custom_call" | custom-call | flops 2147483648 | bytes 13107200 | tf_op jit(solution)/shard_map/project_out/pallas_call | solution.py:470
  146.4 0.5 collective-permute-start.25
  147.0 1.6 collective-permute-start.29
  148.6 5.1 %project_out.3 = (f32[32,4096]{1,0:T(8,128)S(1)}, f32[32,4096]{1,0:T(8,128)S(1)}, f32[32,4096]{1,0:T(8,128)S(1)}, f32[32,4096]{1,0:T(8,128)S(1)}, f32[32,4096]{1...) custom-call(s32[8]{0:T(128)S(1)} %dynamic-slice_bitcast_fusion.place_ref, ...), custom_call_target="tpu_custom_call" | custom-call | flops 2147483648 | bytes 13107200 | tf_op jit(solution)/shard_map/project_out/pallas_call | solution.py:470
  153.7 0.5 collective-permute-start.32
  154.2 1.6 collective-permute-start.35
  155.9 0.5 collective-permute-start.26
  156.4 1.6 collective-permute-start.30
  158.0 5.0 %collective-permute-done.32 = bf16[32,4096]{1,0:T(8,128)(2,1)S(1)} collective-permute-done((bf16[32,4096]{1,0:T(8,128)(2,1)S(1)}, bf16[32,4096]{1,0:T(8,128)(2,1)S(1)}, u32[]{:S(2)}, u32[]{:S(2)}) %collective-permute-start.32) | collective-permute-done | bytes 262176 | tf_op jit(solution)/shard_map/ppermute | solution.py:643
  163.1 0.5 collective-permute-start.33
  163.6 1.6 collective-permute-start.36
  165.3 3.4 %collective-permute-done.26 = bf16[32,4096]{1,0:T(8,128)(2,1)S(1)} collective-permute-done((bf16[32,4096]{1,0:T(8,128)(2,1)S(1)}, bf16[32,4096]{1,0:T(8,128)(2,1)S(1)}, u32[]{:S(2)}, u32[]{:S(2)}) %collective-permute-start.26) | collective-permute-done | bytes 262176 | tf_op jit(solution)/shard_map/ppermute | solution.py:643
  168.7 0.5 collective-permute-start.27
  169.2 1.6 collective-permute-start.31
  170.9 3.4 %collective-permute-done.33 = bf16[32,4096]{1,0:T(8,128)(2,1)S(1)} collective-permute-done((bf16[32,4096]{1,0:T(8,128)(2,1)S(1)}, bf16[32,4096]{1,0:T(8,128)(2,1)S(1)}, u32[]{:S(2)}, u32[]{:S(2)}) %collective-permute-start.33) | collective-permute-done | bytes 262176 | tf_op jit(solution)/shard_map/ppermute | solution.py:643
  174.3 0.5 collective-permute-start.34
  174.9 1.6 collective-permute-start.37
  176.5 3.4 %collective-permute-done.27 = bf16[32,4096]{1,0:T(8,128)(2,1)S(1)} collective-permute-done((bf16[32,4096]{1,0:T(8,128)(2,1)S(1)}, bf16[32,4096]{1,0:T(8,128)(2,1)S(1)}, u32[]{:S(2)}, u32[]{:S(2)}) %collective-permute-start.27) | collective-permute-done | bytes 262176 | tf_op jit(solution)/shard_map/ppermute | solution.py:643
  179.9 0.5 collective-permute-start.28
  180.4 2.6 %collective-permute-done.37 = bf16[32,4096]{1,0:T(8,128)(2,1)S(1)} collective-permute-done((bf16[32,4096]{1,0:T(8,128)(2,1)S(1)}, bf16[32,4096]{1,0:T(8,128)(2,1)S(1)}, u32[]{:S(2)}, u32[]{:S(2)}) %collective-permute-start.37) | collective-permute-done | bytes 262176 | tf_op jit(solution)/shard_map/ppermute | solution.py:643
  183.1 1.6 collective-permute-start.38
  184.8 3.5 %collective-permute-done.28 = bf16[32,4096]{1,0:T(8,128)(2,1)S(1)} collective-permute-done((bf16[32,4096]{1,0:T(8,128)(2,1)S(1)}, bf16[32,4096]{1,0:T(8,128)(2,1)S(1)}, u32[]{:S(2)}, u32[]{:S(2)}) %collective-permute-start.28) | collective-permute-done | bytes 262176 | tf_op jit(solution)/shard_map/ppermute | solution.py:643
  188.3 1.2 collective-permute-done.38
  189.6 0.8 pad_maximum_fusion
  (76 shorter events, 4.9 us)
Async XLA Ops:
  2.5 10.7 %copy-start = (s32[1,256]{1,0:T(1,128)S(1)}, s32[1,256]{1,0:T(1,128)}, u32[]{:S(2)}) copy-start(s32[1,256]{1,0:T(1,128)} %param.18) | copy-start | bytes 3076
  2.5 10.7 %copy-start.1 = (s32[1,4]{1,0:T(1,128)S(1)}, s32[1,4]{1,0:T(1,128)}, u32[]{:S(2)}) copy-start(s32[1,4]{1,0:T(1,128)} %param.17) | copy-start | bytes 52
  2.5 13.1 %copy-start.2 = (s32[4]{0:T(128)S(1)}, s32[4]{0:T(128)}, u32[]{:S(2)}) copy-start(s32[4]{0:T(128)} %param.16) | copy-start | bytes 52
  8.0 32.3 %collective-permute-start.3 = (bf16[4,2,256,1024]{3,2,1,0:T(8,128)(2,1)}, bf16[4,2,256,1024]{3,2,1,0:T(8,128)(2,1)}, u32[]{:S(2)}, u32[]{:S(2)}) collective-permute-start(bf16[4,2,256,1024]{3,2,1,0:T(8,128)(2,1)} %bitcast.20.refs_0_), channel_id=1, source_target_pairs={{8,0},{0,8},{9,1},{1,9},{10,2},{2,10},{11,3},{3,11},{12,4},{4,12},... | collective-permute-start | bytes 12582920 | tf_op jit(solution)/shard_map/ppermute | solution.py:560
  8.5 9.7 %collective-permute-start = (bf16[32,4096]{1,0:T(8,128)(2,1)S(1)}, bf16[32,4096]{1,0:T(8,128)(2,1)S(1)}, u32[]{:S(2)}, u32[]{:S(2)}) collective-permute-start(bf16[32,4096]{1,0:T(8,128)(2,1)S(1)} %get-tuple-element.146.refs_0_), channel_id=1, source_target_pairs={{0,2},{2,4},{4,6},{6,7},{7,5},{5,3},{3,1},{1,0},{8,10},{10,12},{12... | collective-permute-start | bytes 786440 | tf_op jit(solution)/shard_map/ppermute | solution.py:551
  11.2 15.9 %collective-permute-start.16 = (bf16[32,4096]{1,0:T(8,128)(2,1)S(1)}, bf16[32,4096]{1,0:T(8,128)(2,1)S(1)}, u32[]{:S(2)}, u32[]{:S(2)}) collective-permute-start(bf16[32,4096]{1,0:T(8,128)(2,1)S(1)} %get-tuple-element.146.refs_0_), channel_id=1, source_target_pairs={{2,0},{4,2},{6,4},{7,6},{5,7},{3,5},{1,3},{0,1},{10,8},{12,10},{14... | collective-permute-start | bytes 786440 | tf_op jit(solution)/shard_map/ppermute | solution.py:553
  11.2 14.0 %collective-permute-start.10 = (bf16[32,4096]{1,0:T(8,128)(2,1)S(1)}, bf16[32,4096]{1,0:T(8,128)(2,1)S(1)}, u32[]{:S(2)}, u32[]{:S(2)}) collective-permute-start(bf16[32,4096]{1,0:T(8,128)(2,1)S(1)} %get-tuple-element.105.refs_0_), channel_id=1, source_target_pairs={{2,0},{4,2},{6,4},{7,6},{5,7},{3,5},{1,3},{0,1},{10,8},{12,10},{14... | collective-permute-start | bytes 786440 | tf_op jit(solution)/shard_map/ppermute | solution.py:553
  13.1 18.6 %collective-permute-start.9 = (bf16[32,4096]{1,0:T(8,128)(2,1)S(1)}, bf16[32,4096]{1,0:T(8,128)(2,1)S(1)}, u32[]{:S(2)}, u32[]{:S(2)}) collective-permute-start(bf16[32,4096]{1,0:T(8,128)(2,1)S(1)} %get-tuple-element.105.refs_0_), channel_id=1, source_target_pairs={{0,2},{2,4},{4,6},{6,7},{7,5},{5,3},{3,1},{1,0},{8,10},{10,12},{12... | collective-permute-start | bytes 786440 | tf_op jit(solution)/shard_map/ppermute | solution.py:551
  18.3 11.1 %collective-permute-start.1 = (bf16[32,4096]{1,0:T(8,128)(2,1)S(1)}, bf16[32,4096]{1,0:T(8,128)(2,1)S(1)}, u32[]{:S(2)}, u32[]{:S(2)}) collective-permute-start(bf16[32,4096]{1,0:T(8,128)(2,1)S(1)} %collective-permute-done.refs_1_), channel_id=1, source_target_pairs={{0,2},{2,4},{4,6},{6,7},{7,5},{5,3},{3,1},{1,0},{8,10},{10,12},{12... | collective-permute-start | bytes 786440 | tf_op jit(solution)/shard_map/ppermute | solution.py:551
  25.2 9.2 %collective-permute-start.12 = (bf16[32,4096]{1,0:T(8,128)(2,1)S(1)}, bf16[32,4096]{1,0:T(8,128)(2,1)S(1)}, u32[]{:S(2)}, u32[]{:S(2)}) collective-permute-start(bf16[32,4096]{1,0:T(8,128)(2,1)S(1)} %collective-permute-done.10.refs_2_), channel_id=1, source_target_pairs={{2,0},{4,2},{6,4},{7,6},{5,7},{3,5},{1,3},{0,1},{10,8},{12,10},{14... | collective-permute-start | bytes 786440 | tf_op jit(solution)/shard_map/ppermute | solution.py:553
  27.0 13.0 %collective-permute-start.17 = (bf16[32,4096]{1,0:T(8,128)(2,1)S(1)}, bf16[32,4096]{1,0:T(8,128)(2,1)S(1)}, u32[]{:S(2)}, u32[]{:S(2)}) collective-permute-start(bf16[32,4096]{1,0:T(8,128)(2,1)S(1)} %collective-permute-done.16.refs_2_), channel_id=1, source_target_pairs={{2,0},{4,2},{6,4},{7,6},{5,7},{3,5},{1,3},{0,1},{10,8},{12,10},{14... | collective-permute-start | bytes 786440 | tf_op jit(solution)/shard_map/ppermute | solution.py:553
  29.9 13.7 %collective-permute-start.2 = (bf16[32,4096]{1,0:T(8,128)(2,1)S(1)}, bf16[32,4096]{1,0:T(8,128)(2,1)S(1)}, u32[]{:S(2)}, u32[]{:S(2)}) collective-permute-start(bf16[32,4096]{1,0:T(8,128)(2,1)S(1)} %collective-permute-done.1.refs_3_), channel_id=1, source_target_pairs={{0,2},{2,4},{4,6},{6,7},{7,5},{5,3},{3,1},{1,0},{8,10},{10,12},{12... | collective-permute-start | bytes 786440 | tf_op jit(solution)/shard_map/ppermute | solution.py:551
  31.8 13.7 %collective-permute-start.11 = (bf16[32,4096]{1,0:T(8,128)(2,1)S(1)}, bf16[32,4096]{1,0:T(8,128)(2,1)S(1)}, u32[]{:S(2)}, u32[]{:S(2)}) collective-permute-start(bf16[32,4096]{1,0:T(8,128)(2,1)S(1)} %collective-permute-done.9.refs_1_), channel_id=1, source_target_pairs={{0,2},{2,4},{4,6},{6,7},{7,5},{5,3},{3,1},{1,0},{8,10},{10,12},{12... | collective-permute-start | bytes 786440 | tf_op jit(solution)/shard_map/ppermute | solution.py:551
  34.5 12.6 %collective-permute-start.14 = (bf16[32,4096]{1,0:T(8,128)(2,1)S(1)}, bf16[32,4096]{1,0:T(8,128)(2,1)S(1)}, u32[]{:S(2)}, u32[]{:S(2)}) collective-permute-start(bf16[32,4096]{1,0:T(8,128)(2,1)S(1)} %collective-permute-done.12.refs_4_), channel_id=1, source_target_pairs={{2,0},{4,2},{6,4},{7,6},{5,7},{3,5},{1,3},{0,1},{10,8},{12,10},{14... | collective-permute-start | bytes 786440 | tf_op jit(solution)/shard_map/ppermute | solution.py:553
  40.1 11.2 %collective-permute-start.18 = (bf16[32,4096]{1,0:T(8,128)(2,1)S(1)}, bf16[32,4096]{1,0:T(8,128)(2,1)S(1)}, u32[]{:S(2)}, u32[]{:S(2)}) collective-permute-start(bf16[32,4096]{1,0:T(8,128)(2,1)S(1)} %collective-permute-done.17.refs_4_), channel_id=1, source_target_pairs={{2,0},{4,2},{6,4},{7,6},{5,7},{3,5},{1,3},{0,1},{10,8},{12,10},{14... | collective-permute-start | bytes 786440 | tf_op jit(solution)/shard_map/ppermute | solution.py:553
  43.6 9.3 %collective-permute-start.19 = (bf16[32,4096]{1,0:T(8,128)(2,1)S(1)}, bf16[32,4096]{1,0:T(8,128)(2,1)S(1)}, u32[]{:S(2)}, u32[]{:S(2)}) collective-permute-start(bf16[32,4096]{1,0:T(8,128)(2,1)S(1)} %collective-permute-done.2.refs_5_), channel_id=1, source_target_pairs={{0,2},{2,4},{4,6},{6,7},{7,5},{5,3},{3,1},{1,0},{8,10},{10,12},{12... | collective-permute-start | bytes 786440 | tf_op jit(solution)/shard_map/ppermute | solution.py:551
  45.4 13.9 %collective-permute-start.13 = (bf16[32,4096]{1,0:T(8,128)(2,1)S(1)}, bf16[32,4096]{1,0:T(8,128)(2,1)S(1)}, u32[]{:S(2)}, u32[]{:S(2)}) collective-permute-start(bf16[32,4096]{1,0:T(8,128)(2,1)S(1)} %collective-permute-done.11.refs_3_), channel_id=1, source_target_pairs={{0,2},{2,4},{4,6},{6,7},{7,5},{5,3},{3,1},{1,0},{8,10},{10,12},{12... | collective-permute-start | bytes 786440 | tf_op jit(solution)/shard_map/ppermute | solution.py:551
  47.0 12.3 %collective-permute-start.15 = (bf16[32,4096]{1,0:T(8,128)(2,1)S(1)}, bf16[32,4096]{1,0:T(8,128)(2,1)S(1)}, u32[]{:S(2)}, u32[]{:S(2)}) collective-permute-start(bf16[32,4096]{1,0:T(8,128)(2,1)S(1)} %collective-permute-done.14.refs_6_), channel_id=1, source_target_pairs={{2,0},{4,2},{6,4},{7,6},{5,7},{3,5},{1,3},{0,1},{10,8},{12,10},{14... | collective-permute-start | bytes 786440 | tf_op jit(solution)/shard_map/ppermute | solution.py:553
  47.5 39.6 %collective-permute-start.4 = (bf16[2,4,256,128]{3,2,1,0:T(8,128)(2,1)S(1)}, bf16[2,4,256,128]{3,2,1,0:T(8,128)(2,1)S(1)}, u32[]{:S(2)}, u32[]{:S(2)}) collective-permute-start(bf16[2,4,256,128]{3,2,1,0:T(8,128)(2,1)S(1)} %get-tuple-element.95), channel_id=1, source_target_pairs={{0,1},{1,0},{2,3},{3,2},{4,5},{5,4},{6,7},{7,6},{8,9},{9,8},{10,11... | collective-permute-start | bytes 1572872 | tf_op jit(solution)/shard_map/ppermute | solution.py:597
  51.3 35.8 %collective-permute-start.5 = (bf16[2,4,256,128]{3,2,1,0:T(8,128)(2,1)S(1)}, bf16[2,4,256,128]{3,2,1,0:T(8,128)(2,1)S(1)}, u32[]{:S(2)}, u32[]{:S(2)}) collective-permute-start(bf16[2,4,256,128]{3,2,1,0:T(8,128)(2,1)S(1)} %get-tuple-element.96), channel_id=1, source_target_pairs={{0,2},{1,3},{2,0},{3,1},{4,6},{5,7},{6,4},{7,5},{8,10},{9,11},{10,... | collective-permute-start | bytes 1572872 | tf_op jit(solution)/shard_map/ppermute | solution.py:597
  62.8 8.3 %collective-permute-start.20 = (bf16[256,256]{1,0:T(8,128)(2,1)S(1)}, bf16[256,256]{1,0:T(8,128)(2,1)S(1)}, u32[]{:S(2)}, u32[]{:S(2)}) collective-permute-start(bf16[256,256]{1,0:T(8,128)(2,1)S(1)} %project.4.here_ref), channel_id=1, source_target_pairs={{0,4},{1,5},{2,6},{3,7},{4,0},{5,1},{6,2},{7,3},{8,12},{9,13},{10,... | collective-permute-start | bytes 393224 | tf_op jit(solution)/shard_map/ppermute | solution.py:589
  71.1 26.9 %collective-permute-start.21 = (bf16[8,128,256]{2,1,0:T(8,128)(2,1)S(1)}, bf16[8,128,256]{2,1,0:T(8,128)(2,1)S(1)}, u32[]{:S(2)}, u32[]{:S(2)}) collective-permute-start(bf16[8,128,256]{2,1,0:T(8,128)(2,1)S(1)} %project.5.refs_6_), channel_id=1, source_target_pairs={{0,4},{1,5},{2,6},{3,7},{4,0},{5,1},{6,2},{7,3},{8,12},{9,13},{10,... | collective-permute-start | bytes 1572872 | tf_op jit(solution)/shard_map/ppermute | solution.py:605
  71.6 28.5 %collective-permute-start.23 = (bf16[2,4,256,128]{3,2,1,0:T(8,128)(2,1)S(1)}, bf16[2,4,256,128]{3,2,1,0:T(8,128)(2,1)S(1)}, u32[]{:S(2)}, u32[]{:S(2)}) collective-permute-start(bf16[2,4,256,128]{3,2,1,0:T(8,128)(2,1)S(1)} %get-tuple-element.127), channel_id=1, source_target_pairs={{0,3},{1,2},{2,1},{3,0},{4,7},{5,6},{6,5},{7,4},{8,11},{9,10},{10,... | collective-permute-start | bytes 1572872 | tf_op jit(solution)/shard_map/ppermute | solution.py:597
  86.2 2.8 %collective-permute-start.22 = (bf16[256,256]{1,0:T(8,128)(2,1)S(1)}, bf16[256,256]{1,0:T(8,128)(2,1)S(1)}, u32[]{:S(2)}, u32[]{:S(2)}) collective-permute-start(bf16[256,256]{1,0:T(8,128)(2,1)S(1)} %pick_new.1), channel_id=1, source_target_pairs={{0,0},{1,2},{2,4},{3,6},{4,1},{5,3},{6,5},{7,7},{8,8},{9,10},{10,1... | collective-permute-start | bytes 393224 | tf_op jit(solution)/shard_map/ppermute | solution.py:608
  87.1 31.3 %collective-permute-start.6 = (bf16[2,4,256,128]{3,2,1,0:T(8,128)(2,1)S(1)}, bf16[2,4,256,128]{3,2,1,0:T(8,128)(2,1)S(1)}, u32[]{:S(2)}, u32[]{:S(2)}) collective-permute-start(bf16[2,4,256,128]{3,2,1,0:T(8,128)(2,1)S(1)} %get-tuple-element.98), channel_id=1, source_target_pairs={{0,1},{1,0},{2,3},{3,2},{4,5},{5,4},{6,7},{7,6},{8,9},{9,8},{10,11... | collective-permute-start | bytes 1572872 | tf_op jit(solution)/shard_map/ppermute | solution.py:597
  88.7 29.7 %collective-permute-start.7 = (bf16[2,4,256,128]{3,2,1,0:T(8,128)(2,1)S(1)}, bf16[2,4,256,128]{3,2,1,0:T(8,128)(2,1)S(1)}, u32[]{:S(2)}, u32[]{:S(2)}) collective-permute-start(bf16[2,4,256,128]{3,2,1,0:T(8,128)(2,1)S(1)} %get-tuple-element.99), channel_id=1, source_target_pairs={{0,2},{1,3},{2,0},{3,1},{4,6},{5,7},{6,4},{7,5},{8,10},{9,11},{10,... | collective-permute-start | bytes 1572872 | tf_op jit(solution)/shard_map/ppermute | solution.py:597
  89.0 31.5 %collective-permute-start.8 = (bf16[2,4,256,128]{3,2,1,0:T(8,128)(2,1)S(1)}, bf16[2,4,256,128]{3,2,1,0:T(8,128)(2,1)S(1)}, u32[]{:S(2)}, u32[]{:S(2)}) collective-permute-start(bf16[2,4,256,128]{3,2,1,0:T(8,128)(2,1)S(1)} %get-tuple-element.100), channel_id=1, source_target_pairs={{0,3},{1,2},{2,1},{3,0},{4,7},{5,6},{6,5},{7,4},{8,11},{9,10},{10,... | collective-permute-start | bytes 1572872 | tf_op jit(solution)/shard_map/ppermute | solution.py:597
  113.7 27.3 %collective-permute-start.24 = (bf16[8,144,256]{2,1,0:T(8,128)(2,1)S(1)}, bf16[8,144,256]{2,1,0:T(8,128)(2,1)S(1)}, u32[]{:S(2)}, u32[]{:S(2)}) collective-permute-start(bf16[8,144,256]{2,1,0:T(8,128)(2,1)S(1)} %attend.3), channel_id=1, source_target_pairs={{0,4},{1,5},{2,6},{3,7},{4,0},{5,1},{6,2},{7,3},{8,12},{9,13},{10,... | collective-permute-start | bytes 1769480 | tf_op jit(solution)/shard_map/ppermute | solution.py:627
  146.4 9.4 %collective-permute-start.25 = (bf16[32,4096]{1,0:T(8,128)(2,1)S(1)}, bf16[32,4096]{1,0:T(8,128)(2,1)S(1)}, u32[]{:S(2)}, u32[]{:S(2)}) collective-permute-start(bf16[32,4096]{1,0:T(8,128)(2,1)S(1)} %get-tuple-element.133), channel_id=1, source_target_pairs={{0,2},{2,4},{4,6},{6,7},{7,5},{5,3},{3,1},{1,0},{8,10},{10,12},{12... | collective-permute-start | bytes 786440 | tf_op jit(solution)/shard_map/ppermute | solution.py:643
  147.0 9.4 %collective-permute-start.29 = (bf16[32,4096]{1,0:T(8,128)(2,1)S(1)}, bf16[32,4096]{1,0:T(8,128)(2,1)S(1)}, u32[]{:S(2)}, u32[]{:S(2)}) collective-permute-start(bf16[32,4096]{1,0:T(8,128)(2,1)S(1)} %convert_element_type.116), channel_id=1, source_target_pairs={{2,0},{4,2},{6,4},{7,6},{5,7},{3,5},{1,3},{0,1},{10,8},{12,10},{14... | collective-permute-start | bytes 786440 | tf_op jit(solution)/shard_map/ppermute | solution.py:643
  153.7 9.3 %collective-permute-start.32 = (bf16[32,4096]{1,0:T(8,128)(2,1)S(1)}, bf16[32,4096]{1,0:T(8,128)(2,1)S(1)}, u32[]{:S(2)}, u32[]{:S(2)}) collective-permute-start(bf16[32,4096]{1,0:T(8,128)(2,1)S(1)} %convert_element_type.123), channel_id=1, source_target_pairs={{0,2},{2,4},{4,6},{6,7},{7,5},{5,3},{3,1},{1,0},{8,10},{10,12},{12... | collective-permute-start | bytes 786440 | tf_op jit(solution)/shard_map/ppermute | solution.py:643
  154.2 9.4 %collective-permute-start.35 = (bf16[32,4096]{1,0:T(8,128)(2,1)S(1)}, bf16[32,4096]{1,0:T(8,128)(2,1)S(1)}, u32[]{:S(2)}, u32[]{:S(2)}) collective-permute-start(bf16[32,4096]{1,0:T(8,128)(2,1)S(1)} %get-tuple-element.144), channel_id=1, source_target_pairs={{2,0},{4,2},{6,4},{7,6},{5,7},{3,5},{1,3},{0,1},{10,8},{12,10},{14... | collective-permute-start | bytes 786440 | tf_op jit(solution)/shard_map/ppermute | solution.py:643
  155.9 12.8 %collective-permute-start.26 = (bf16[32,4096]{1,0:T(8,128)(2,1)S(1)}, bf16[32,4096]{1,0:T(8,128)(2,1)S(1)}, u32[]{:S(2)}, u32[]{:S(2)}) collective-permute-start(bf16[32,4096]{1,0:T(8,128)(2,1)S(1)} %add_convert_fusion.11), channel_id=1, source_target_pairs={{0,2},{2,4},{4,6},{6,7},{7,5},{5,3},{3,1},{1,0},{8,10},{10,12},{12... | collective-permute-start | bytes 786440 | tf_op jit(solution)/shard_map/ppermute | solution.py:643
  156.4 12.8 %collective-permute-start.30 = (bf16[32,4096]{1,0:T(8,128)(2,1)S(1)}, bf16[32,4096]{1,0:T(8,128)(2,1)S(1)}, u32[]{:S(2)}, u32[]{:S(2)}) collective-permute-start(bf16[32,4096]{1,0:T(8,128)(2,1)S(1)} %add_convert_fusion.8), channel_id=1, source_target_pairs={{2,0},{4,2},{6,4},{7,6},{5,7},{3,5},{1,3},{0,1},{10,8},{12,10},{14... | collective-permute-start | bytes 786440 | tf_op jit(solution)/shard_map/ppermute | solution.py:643
  163.1 11.2 %collective-permute-start.33 = (bf16[32,4096]{1,0:T(8,128)(2,1)S(1)}, bf16[32,4096]{1,0:T(8,128)(2,1)S(1)}, u32[]{:S(2)}, u32[]{:S(2)}) collective-permute-start(bf16[32,4096]{1,0:T(8,128)(2,1)S(1)} %add_convert_fusion.5), channel_id=1, source_target_pairs={{0,2},{2,4},{4,6},{6,7},{7,5},{5,3},{3,1},{1,0},{8,10},{10,12},{12... | collective-permute-start | bytes 786440 | tf_op jit(solution)/shard_map/ppermute | solution.py:643
  163.6 11.2 %collective-permute-start.36 = (bf16[32,4096]{1,0:T(8,128)(2,1)S(1)}, bf16[32,4096]{1,0:T(8,128)(2,1)S(1)}, u32[]{:S(2)}, u32[]{:S(2)}) collective-permute-start(bf16[32,4096]{1,0:T(8,128)(2,1)S(1)} %add_convert_fusion.3), channel_id=1, source_target_pairs={{2,0},{4,2},{6,4},{7,6},{5,7},{3,5},{1,3},{0,1},{10,8},{12,10},{14... | collective-permute-start | bytes 786440 | tf_op jit(solution)/shard_map/ppermute | solution.py:643
  168.7 11.2 %collective-permute-start.27 = (bf16[32,4096]{1,0:T(8,128)(2,1)S(1)}, bf16[32,4096]{1,0:T(8,128)(2,1)S(1)}, u32[]{:S(2)}, u32[]{:S(2)}) collective-permute-start(bf16[32,4096]{1,0:T(8,128)(2,1)S(1)} %add_convert_fusion.10), channel_id=1, source_target_pairs={{0,2},{2,4},{4,6},{6,7},{7,5},{5,3},{3,1},{1,0},{8,10},{10,12},{12... | collective-permute-start | bytes 786440 | tf_op jit(solution)/shard_map/ppermute | solution.py:643
  169.2 15.5 %collective-permute-start.31 = (bf16[32,4096]{1,0:T(8,128)(2,1)S(1)}, bf16[32,4096]{1,0:T(8,128)(2,1)S(1)}, u32[]{:S(2)}, u32[]{:S(2)}) collective-permute-start(bf16[32,4096]{1,0:T(8,128)(2,1)S(1)} %add_convert_fusion.7), channel_id=1, source_target_pairs={{2,0},{4,2},{6,4},{7,6},{5,7},{3,5},{1,3},{0,1},{10,8},{12,10},{14... | collective-permute-start | bytes 786440 | tf_op jit(solution)/shard_map/ppermute | solution.py:643
  174.3 14.0 %collective-permute-start.34 = (bf16[32,4096]{1,0:T(8,128)(2,1)S(1)}, bf16[32,4096]{1,0:T(8,128)(2,1)S(1)}, u32[]{:S(2)}, u32[]{:S(2)}) collective-permute-start(bf16[32,4096]{1,0:T(8,128)(2,1)S(1)} %add_convert_fusion.4), channel_id=1, source_target_pairs={{0,2},{2,4},{4,6},{6,7},{7,5},{5,3},{3,1},{1,0},{8,10},{10,12},{12... | collective-permute-start | bytes 786440 | tf_op jit(solution)/shard_map/ppermute | solution.py:643
  174.9 8.2 %collective-permute-start.37 = (bf16[32,4096]{1,0:T(8,128)(2,1)S(1)}, bf16[32,4096]{1,0:T(8,128)(2,1)S(1)}, u32[]{:S(2)}, u32[]{:S(2)}) collective-permute-start(bf16[32,4096]{1,0:T(8,128)(2,1)S(1)} %add_convert_fusion.2), channel_id=1, source_target_pairs={{2,0},{4,2},{6,4},{7,6},{5,7},{3,5},{1,3},{0,1},{10,8},{12,10},{14... | collective-permute-start | bytes 786440 | tf_op jit(solution)/shard_map/ppermute | solution.py:643
  179.9 8.3 %collective-permute-start.28 = (bf16[32,4096]{1,0:T(8,128)(2,1)S(1)}, bf16[32,4096]{1,0:T(8,128)(2,1)S(1)}, u32[]{:S(2)}, u32[]{:S(2)}) collective-permute-start(bf16[32,4096]{1,0:T(8,128)(2,1)S(1)} %add_convert_fusion.9), channel_id=1, source_target_pairs={{0,2},{2,4},{4,6},{6,7},{7,5},{5,3},{3,1},{1,0},{8,10},{10,12},{12... | collective-permute-start | bytes 786440 | tf_op jit(solution)/shard_map/ppermute | solution.py:643
  183.1 6.4 %collective-permute-start.38 = (bf16[32,4096]{1,0:T(8,128)(2,1)S(1)}, bf16[32,4096]{1,0:T(8,128)(2,1)S(1)}, u32[]{:S(2)}, u32[]{:S(2)}) collective-permute-start(bf16[32,4096]{1,0:T(8,128)(2,1)S(1)} %add_convert_fusion.1), channel_id=1, source_target_pairs={{2,0},{4,2},{6,4},{7,6},{5,7},{3,5},{1,3},{0,1},{10,8},{12,10},{14... | collective-permute-start | bytes 786440 | tf_op jit(solution)/shard_map/ppermute | solution.py:643

commit v12 on v11

--- a/solution.py
+++ b/solution.py
@@ -84,14 +84,15 @@
     return start, wait
 
 
-def project_kernel(n_blocks, n_weights, chunk, is_last, place_ref, *refs):
+def project_kernel(n_blocks, n_weights, n_tables, chunk, is_last, place_ref, *refs):
     refs = list(refs)
     take = lambda count: [refs.pop(0) for _ in range(count)]
     blocks, weights = take(n_blocks), take(n_weights)
     prev = take(n_weights) if chunk else None
     if is_last:
-        tables, (out, total, natural) = take(len(refs) - 5), take(3)
-        totals = [total]
+        n_outs = len(refs) - 4 - n_tables
+        tables, outs, (total, natural) = take(n_tables), take(n_outs), take(2)
+        out, totals = outs[0], [total]
     else:
         totals = take(n_weights)
     buffers, sems = take(n_weights), refs[0]
@@ -124,6 +125,16 @@
             here = slice(block * height, (block + 1) * height)
             there = pl.ds(pl.multiple_of(place_ref[block] * height, height), height)
             natural[there, :] = totals[0][here, :]
+        if len(outs) == 2:
+            side_ref = tables[0]
+            for side in range(2):
+
+                @pl.when(side_ref[0] == side)
+                def _():
+                    outs[1 - side][...] = natural[:, :HD].astype(out.dtype)
+                    outs[side][...] = natural[:, HD:].astype(out.dtype)
+
+            return
         if not tables:
             out[...] = natural[...].astype(out.dtype)
             return
@@ -144,7 +155,7 @@
             out[index] = stacked.T.astype(out.dtype)
 
 
-def project(place, blocks, weights, prev, chunk, tables=()):
+def project(place, blocks, weights, prev, chunk, tables=(), side=()):
     depth = blocks[0].shape[1]
     widths = [w.shape[1] for w in weights]
     tile = min(DEPTH_TILE, depth)
@@ -155,14 +166,19 @@
     if is_last:
         shape = (SEL * widths[0] // (HD * TILE_COLS), HD, TILE_COLS) if tables else (SEL, widths[0])
         outs, scratch = [(shape, jnp.bfloat16)], totals * 2
+        if side:
+            outs = [((SEL, HD), jnp.bfloat16)] * 2
     else:
         outs, scratch = totals, []
     return pl.pallas_call(
-        functools.partial(project_kernel, len(blocks), len(weights), chunk, is_last),
+        functools.partial(
+            project_kernel, len(blocks), len(weights), len(tables) + len(side), chunk, is_last
+        ),
         in_specs=[pl.BlockSpec(memory_space=pltpu.SMEM)]
         + [vmem] * len(blocks)
         + [hbm] * len(weights)
-        + [vmem] * (len(prev) + len(tables)),
+        + [vmem] * (len(prev) + len(tables))
+        + [pl.BlockSpec(memory_space=pltpu.SMEM)] * len(side),
         out_specs=[vmem] * len(outs),
         out_shape=[jax.ShapeDtypeStruct(*o) for o in outs],
         scratch_shapes=[pltpu.VMEM(*x) for x in scratch]
@@ -171,7 +187,7 @@
         compiler_params=megabytes(16),
         cost_estimate=cost(2 * SEL * depth * sum(widths), 2 * depth * (sum(widths) + SEL)),
         name="project",
-    )(place, *blocks, *weights, *prev, *tables)
+    )(place, *blocks, *weights, *prev, *tables, *side)
 
 
 def select_kernel(n_dest, n_src, place_ref, slot_ref, head_ref, *refs):
@@ -222,13 +238,13 @@
     return pieces
 
 
-def attend_kernel(n_chunks, with_new, n_tiles, tile_q, first_tile, first_ref, pos_ref, *refs):
+def attend_kernel(n_chunks, with_new, n_tiles, tile_q, first_tile, first_ref, pos_ref, odd_ref, *refs):
     refs = list(refs)
     take = lambda count: [refs.pop(0) for _ in range(count)]
     chunks = take(n_chunks)
     dead_ref, qpos_ref, queries = take(3)
     if with_new:
-        cos_ref, sin_ref, new_ref = take(3)
+        cos_ref, sin_ref, new_a, new_b = take(4)
     if with_new:
         top, total, summed, values, new_key, new_value = take(6)
     else:
@@ -242,10 +258,15 @@
         for doc in range(DOCS):
             values[doc, :, chunk * tokens : (chunk + 1) * tokens] = chunks[chunk][1, doc].T
     if with_new:
-        new_key[...] = rotate(
-            new_ref[:, :HD].astype(jnp.float32), cos_ref[...], sin_ref[...]
-        ).astype(jnp.bfloat16)
-        new_value[...] = new_ref[:, HD:].T
+        for odd, (key_ref, value_ref) in enumerate(((new_a, new_b), (new_b, new_a))):
+
+            @pl.when(odd_ref[0] == odd)
+            def _():
+                new_key[...] = rotate(
+                    key_ref[...].astype(jnp.float32), cos_ref[...], sin_ref[...]
+                ).astype(jnp.bfloat16)
+                new_value[...] = value_ref[...].T
+
 
     one_row = jnp.where(
         lax.broadcasted_iota(jnp.int32, (HD, TILE_COLS), 0) == 0, 1.0, 0.0
@@ -337,13 +358,13 @@
                 packed[tile] = jnp.concatenate([summed[tile], extra], axis=0).astype(jnp.bfloat16)
 
 
-def attend(chunks, dead, first_pos, selected, q_pos, queries, first_tile, n_tiles, fresh):
+def attend(chunks, dead, first_pos, selected, q_pos, odd, queries, first_tile, n_tiles, fresh):
     n_chunks = len(chunks)
     tokens = chunks[0].shape[2]
     tile_q = SEL // q_pos.shape[0]
     smem = pl.BlockSpec(memory_space=pltpu.SMEM)
     vmem = pl.BlockSpec(memory_space=pltpu.VMEM)
-    operands = [first_pos, selected, *chunks, dead, q_pos, queries, *fresh]
+    operands = [first_pos, selected, odd, *chunks, dead, q_pos, queries, *fresh]
     state = [((n_tiles, 1, TILE_COLS), jnp.float32)] * 2
     state += [((n_tiles, HD, TILE_COLS), jnp.float32)]
     values = ((DOCS, HD, n_chunks * tokens), jnp.bfloat16)
@@ -358,7 +379,7 @@
         functools.partial(
             attend_kernel, n_chunks, bool(fresh), n_tiles, tile_q, first_tile
         ),
-        in_specs=[smem] * 2 + [vmem] * (len(operands) - 2),
+        in_specs=[smem] * 3 + [vmem] * (len(operands) - 3),
         out_specs=[vmem] * len(outs),
         out_shape=[jax.ShapeDtypeStruct(*s) for s in outs],
         scratch_shapes=[pltpu.VMEM(*s) for s in scratch],
@@ -366,31 +387,6 @@
         cost_estimate=cost(4 * pairs * HD, 4 * DOCS * n_chunks * tokens * HD, pairs),
         name="attend",
     )(*operands)
-
-
-def pick_kernel(side_ref, here_ref, there_ref, out_ref):
-    @pl.when(side_ref[0] == 1)
-    def _():
-        out_ref[:, :HD] = here_ref[:, :HD]
-        out_ref[:, HD:] = there_ref[:, :HD]
-
-    @pl.when(side_ref[0] == 0)
-    def _():
-        out_ref[:, :HD] = there_ref[:, HD:]
-        out_ref[:, HD:] = here_ref[:, HD:]
-
-
-def pick_new(side, here, there):
-    vmem = pl.BlockSpec(memory_space=pltpu.VMEM)
-    return pl.pallas_call(
-        pick_kernel,
-        in_specs=[pl.BlockSpec(memory_space=pltpu.SMEM), vmem, vmem],
-        out_specs=vmem,
-        out_shape=jax.ShapeDtypeStruct((SEL, 2 * HD), jnp.bfloat16),
-        compiler_params=megabytes(4),
-        cost_estimate=cost(0, 8 * SEL * HD),
-        name="pick_new",
-    )(side, here, there)
 
 
 def merge_kernel(*refs):
@@ -561,12 +557,13 @@
             holder = (doc_slot // slots - lax.axis_index("req")) % req_size
             slot = doc_slot % slots
             side = (me < middle).astype(jnp.int32)[None]
+            odd = (me % 2 if tp_size == KVH else me * 0)[None]
             takers = jnp.concatenate([me ^ order, me ^ order ^ middle]) * KVH // tp_size
         if k == 2:
-            first[-1], dead, first_pos, cosine, sine_part, q_pos, takers, holder, slot, place, side = (
+            first[-1], dead, first_pos, cosine, sine_part, q_pos, takers, holder, slot, place, side, odd = (
                 lax.optimization_barrier(
                     (first[-1], dead, first_pos, cosine, sine_part, q_pos, takers, holder, slot)
-                    + (place, side)
+                    + (place, side, odd)
                 )
             )
         if k == far - 1:
@@ -584,48 +581,42 @@
         if chunk + 1 < CHUNKS:
             sums = project(place, blocks, weights, sums, chunk)
     across = [(i, i ^ middle) for i in range(tp_size)]
-    (keyval,) = project(place, blocks, weights[:1], sums[:1], CHUNKS - 1)
-    keyval, *blocks = lax.optimization_barrier((keyval, *blocks))
-    their_keyval = lax.ppermute(keyval, "tp", across)
+    if tp_size == KVH:
+        first, second = project(place, blocks, weights[:1], sums[:1], CHUNKS - 1, (), (side,))
+        first, second, *blocks = lax.optimization_barrier((first, second, *blocks))
+        keys_to_even = [(i, 2 * i if i < middle else 2 * (i - middle) + 1) for i in range(tp_size)]
+        keys_to_odd = [(i, 2 * i + 1 if i < middle else 2 * (i - middle)) for i in range(tp_size)]
+        new = [lax.ppermute(first, "tp", keys_to_even), lax.ppermute(second, "tp", keys_to_odd)]
+    else:
+        (keyval,) = project(place, blocks, weights[:1], sums[:1], CHUNKS - 1)
+        everyone = lax.all_gather(keyval, "tp", axis=1, tiled=True)
+        my_head = me * KVH // tp_size
+        new = [
+            lax.dynamic_slice_in_dim(everyone, (kind * KVH + my_head) * HD, HD, axis=1)
+            for kind in range(2)
+        ]
     (queries,) = project(
         place, blocks, weights[1:], sums[1:], CHUNKS - 1, (cosine, sine_part)
     )
-    queries, their_keyval = lax.optimization_barrier((queries, their_keyval))
+    queries, new = lax.optimization_barrier((queries, new))
 
     def exchange(kept):
-        return [
-            lax.ppermute(kept[j], "tp", [(i, i ^ j) for i in range(tp_size)]) if j else kept[j]
-            for j in range(middle)
-        ]
+        got = {
+            j: lax.ppermute(kept[j], "tp", [(i, i ^ j) for i in range(tp_size)])
+            for j in range(middle - 1, 0, -1)
+        }
+        return [kept[0]] + [got[j] for j in range(1, middle)]
 
     own, partners = sent[:middle], exchange(sent[middle:])
-    own, *partners[1:3] = lax.optimization_barrier((own, *partners[1:3]))
+    own, *partners[2:] = lax.optimization_barrier((own, *partners[2:]))
     chunks = [exchange(own), partners]
     n_tiles = queries.shape[0]
     their_queries = lax.ppermute(queries, "tp", across)
 
-    if tp_size == KVH:
-        new = lax.ppermute(
-            pick_new(side, keyval, their_keyval),
-            "tp",
-            [(i, 2 * i if i < middle else 2 * (i - middle) + 1) for i in range(tp_size)],
-        )
-    else:
-        everyone = lax.all_gather(keyval, "tp", axis=1, tiled=True)
-        my_head = me * KVH // tp_size
-        new = jnp.concatenate(
-            [
-                lax.dynamic_slice_in_dim(everyone, (kind * KVH + my_head) * HD, HD, axis=1)
-                for kind in range(2)
-            ],
-            axis=1,
-        )
-
-    metadata = (dead, first_pos, selected, q_pos)
-    their_queries, new = lax.optimization_barrier((their_queries, new))
+    metadata = (dead, first_pos, selected, q_pos, odd)
     (packed,) = attend(chunks[1], *metadata, their_queries, 0, n_tiles, [])
     theirs = lax.ppermute(packed, "tp", across)
-    mine = attend(chunks[0], *metadata, queries, 0, n_tiles, [cosine, sine_part, new])
+    mine = attend(chunks[0], *metadata, queries, 0, n_tiles, [cosine, sine_part, *new])
     attention = merge([mine], [theirs])
 
     finished = []

time: 191 us -> 199 us (1.042)
  waiting for transfers between devices: 49 us -> 69 us
  starting transfers between devices: 67.9 us -> 53.8 us
  Pallas kernels: 58.3 us -> 60.6 us
    ppermute x6, starting transfers between devices: 27.4 us -> 8.37 us  [exchange(): lax.ppermute(kept[j], 'tp', [(i, i ^ j) for i in range(tp_size)])]
    ppermute x1, waiting for transfers between devices: 0.01 us -> 18 us  [per_device(): their_queries = lax.ppermute(queries, 'tp', across)]
    ppermute x1, starting transfers between devices: 0.55 us -> 9.5 us  [per_device(): their_queries = lax.ppermute(queries, 'tp', across)]
    ppermute x1, waiting for transfers between devices: 5.06 us -> 10.7 us  [per_device(): theirs = lax.ppermute(packed, 'tp', across)]
    ppermute x1, starting transfers between devices: 4.69 us -> 0.07 us  [per_device(): theirs = lax.ppermute(packed, 'tp', across)]
    ppermute x6, waiting for transfers between devices: 4.34 us -> 0.02 us  [exchange(): lax.ppermute(kept[j], 'tp', [(i, i ^ j) for i in range(tp_size)])]
    pallas_call x2, Pallas kernels: 29 us -> 31.3 us  [attend(): pl.pallas_call(functools.partial(attend_kernel, n_chunks, bool(fresh), n_...]
  transfers between devices with their start and end apart: 39 -> 39, of which waited for: 16 -> 15; matrix products, arithmetic and copies ran while one was open for 3% -> 3% of each run, Pallas kernels for 28% -> 28%
where the time goes in v12:
time: 199 us
  waiting for transfers between devices  69 us (35%)
  Pallas kernels  60.6 us (30%)
  starting transfers between devices  53.8 us (27%)
  local copies, waits for them, and re-layouts  7.61 us (4%)
  other arithmetic  7.26 us (4%)
    pallas_call x2, Pallas kernels, attend(): pl.pallas_call(functools.partial(attend_kernel, n_chunks, bool(fresh), n_...  31.3 us
    ppermute x14, waiting for transfers between devices, per_device(): held = lax.ppermute(term.astype(jnp.bfloat16), 'tp', pairs)  24.3 us
    ppermute x1, waiting for transfers between devices, per_device(): their_queries = lax.ppermute(queries, 'tp', across)  18 us
    pallas_call x3, Pallas kernels, project(): pl.pallas_call(functools.partial(project_kernel, len(blocks), len(weights...  15.5 us
    ppermute x14, starting transfers between devices, per_device(): held = lax.ppermute(term.astype(jnp.bfloat16), 'tp', pairs)  14.7 us
    ppermute x7, waiting for transfers between devices, per_device(): held['behind'].append(lax.ppermute(held['behind'][-1], 'tp', back))  12.9 us
    ppermute x7, starting transfers between devices, per_device(): held['before'].append(lax.ppermute(held['before'][-1], 'tp', forth))  11.5 us
    ppermute x1, waiting for transfers between devices, per_device(): theirs = lax.ppermute(packed, 'tp', across)  10.7 us
  transfers between devices with their start and end apart: 39, of which 15 were waited for; matrix products, arithmetic and copies ran while one was open for 3% of the time, Pallas kernels for 28%

profile of v12, /device:TPU:0, one launch (start us, length us, event | category | flops | bytes accessed | tf_op | source)
XLA Modules:
  0.0 198.7 jit_solution(3437689284547187481)
XLA Ops:
  0.0 1.2 fusion
  1.3 1.2 fusion.2
  2.5 5.5 %copy.16 = bf16[4,256,2,1024]{3,1,2,0:T(8,128)(2,1)} copy(bf16[4,256,2,1024]{3,2,1,0:T(2,128)(2,1)} %param.15) | data formatting | bytes 8388608 | tf_op jit(solution)/shard_map/optimization_barrier | solution.py:515
  8.0 0.5 collective-permute-start.3
  8.5 2.6 %collective-permute-start = (bf16[32,4096]{1,0:T(8,128)(2,1)S(1)}, bf16[32,4096]{1,0:T(8,128)(2,1)S(1)}, u32[]{:S(2)}, u32[]{:S(2)}) collective-permute-start(bf16[32,4096]{1,0:T(8,128)(2,1)S(1)} %get-tuple-element.152.refs_0_), channel_id=1, source_target_pairs={{0,2},{2,4},{4,6},{6,7},{7,5},{5,3},{3,1},{1,0},{8,10},{10,12},{12... | collective-permute-start | bytes 786440 | tf_op jit(solution)/shard_map/ppermute | solution.py:547
  11.2 2.0 collective-permute-start.10
  13.2 0.2 reduce-window.7
  13.6 1.3 compare_reduce_fusion
  15.1 0.5 fusion.3
  15.7 2.6 %collective-permute-done.refs_1_ = bf16[32,4096]{1,0:T(8,128)(2,1)S(1)} collective-permute-done((bf16[32,4096]{1,0:T(8,128)(2,1)S(1)}, bf16[32,4096]{1,0:T(8,128)(2,1)S(1)}, u32[]{:S(2)}, u32[]{:S(2)}) %collective-permute-start) | collective-permute-done | bytes 262176 | tf_op jit(solution)/shard_map/ppermute | solution.py:547
  18.3 2.0 %collective-permute-start.1 = (bf16[32,4096]{1,0:T(8,128)(2,1)S(1)}, bf16[32,4096]{1,0:T(8,128)(2,1)S(1)}, u32[]{:S(2)}, u32[]{:S(2)}) collective-permute-start(bf16[32,4096]{1,0:T(8,128)(2,1)S(1)} %collective-permute-done.refs_1_), channel_id=1, source_target_pairs={{0,2},{2,4},{4,6},{6,7},{7,5},{5,3},{3,1},{1,0},{8,10},{10,12},{12... | collective-permute-start | bytes 786440 | tf_op jit(solution)/shard_map/ppermute | solution.py:547
  20.3 0.7 dynamic-slice_bitcast_fusion.place_ref
  20.9 0.1 pad_maximum_fusion.1
  21.1 4.1 %collective-permute-done.10.refs_2_ = bf16[32,4096]{1,0:T(8,128)(2,1)S(1)} collective-permute-done((bf16[32,4096]{1,0:T(8,128)(2,1)S(1)}, bf16[32,4096]{1,0:T(8,128)(2,1)S(1)}, u32[]{:S(2)}, u32[]{:S(2)}) %collective-permute-start.10) | collective-permute-done | bytes 262176 | tf_op jit(solution)/shard_map/ppermute | solution.py:549
  25.2 0.3 collective-permute-start.12
  25.7 0.5 broadcast.179
  26.2 0.7 reduce.3
  27.0 1.7 collective-permute-start.17
  28.8 0.5 collective-permute-done.1.refs_3_
  29.3 0.6 broadcast_in_dim.23.refs_4_
  29.9 1.8 collective-permute-start.2
  31.8 1.6 collective-permute-start.11
  33.3 1.1 collective-permute-done.12.refs_4_
  34.5 0.3 collective-permute-start.14
  34.7 5.4 %collective-permute-done.17.refs_4_ = bf16[32,4096]{1,0:T(8,128)(2,1)S(1)} collective-permute-done((bf16[32,4096]{1,0:T(8,128)(2,1)S(1)}, bf16[32,4096]{1,0:T(8,128)(2,1)S(1)}, u32[]{:S(2)}, u32[]{:S(2)}) %collective-permute-start.17) | collective-permute-done | bytes 262176 | tf_op jit(solution)/shard_map/ppermute | solution.py:549
  40.1 0.3 collective-permute-start.18
  40.3 3.3 %select_docs.1 = (bf16[2,4,256,128]{3,2,1,0:T(8,128)(2,1)S(1)}, bf16[2,4,256,128]{3,2,1,0:T(8,128)(2,1)S(1)}, bf16[2,4,256,128]{3,2,1,0:T(8,128)(2,1)S(1)}, bf16...) custom-call(s32[4]{0:T(128)S(1)} %get-tuple-element.83.place_ref, ...), custom_call_target="tpu_custom_call" | custom-call | bytes 8388608 | tf_op jit(solution)/shard_map/select_docs/pallas_call | solution.py:221
  43.6 1.8 collective-permute-start.19
  45.4 1.6 collective-permute-start.13
  47.0 0.4 collective-permute-start.15
  47.5 1.6 collective-permute-start.4
  49.0 2.3 %collective-permute-done.18.refs_6_ = bf16[32,4096]{1,0:T(8,128)(2,1)S(1)} collective-permute-done((bf16[32,4096]{1,0:T(8,128)(2,1)S(1)}, bf16[32,4096]{1,0:T(8,128)(2,1)S(1)}, u32[]{:S(2)}, u32[]{:S(2)}) %collective-permute-start.18) | collective-permute-done | bytes 262176 | tf_op jit(solution)/shard_map/ppermute | solution.py:549
  51.3 1.4 collective-permute-start.5
  52.7 1.9 collective-permute-start.22
  54.6 6.4 %project.3 = (f32[256,256]{1,0:T(8,128)S(1)}, f32[256,1024]{1,0:T(8,128)S(1)}) custom-call(s32[8]{0:T(128)S(1)} %dynamic-slice_bitcast_fusion.place_ref, bf16[32,4096]{1,0:T(8,128)(2,1)S(1)} %get-tuple-element.152.refs_0_, bf16[32,4096]{1,0:T(8,128)(2,1)S(1)} %collective-permute-done.refs_1_, bf16[32,4096]{1,0:T(8,128)(2,1)S(1)} %collective-permute-done.16.refs_2_, ...), custom_call_target="tpu_custom_call" | custom-call | flops 2684354560 | bytes 12582912 | tf_op jit(solution)/shard_map/project/pallas_call | solution.py:173
  61.0 3.4 %project.4 = (bf16[256,128]{1,0:T(8,128)(2,1)S(1)}, bf16[256,128]{1,0:T(8,128)(2,1)S(1)}) custom-call(s32[8]{0:T(128)S(1)} %dynamic-slice_bitcast_fusion.place_ref, bf16[32,4096]{1,0:T(8,128)(2,1)S(1)} %get-tuple-element.112.refs_0_, bf16[32,4096]{1,0:T(8,128)(2,1)S(1)} %collective-permute-done.9.refs_1_, ...), custom_call_target="tpu_custom_call" | custom-call | flops 536870912 | bytes 4194304 | tf_op jit(solution)/shard_map/project/pallas_call | solution.py:173
  64.5 0.7 collective-permute-start.20
  65.1 3.6 %collective-permute-start.21 = (bf16[256,128]{1,0:T(8,128)(2,1)S(1)}, bf16[256,128]{1,0:T(8,128)(2,1)S(1)}, u32[]{:S(2)}, u32[]{:S(2)}) collective-permute-start(bf16[256,128]{1,0:T(8,128)(2,1)S(1)} %get-tuple-element.124), channel_id=1, source_target_pairs={{0,1},{1,3},{2,5},{3,7},{4,0},{5,2},{6,4},{7,6},{8,9},{9,11},{10,1... | collective-permute-start | bytes 196616 | tf_op jit(solution)/shard_map/ppermute | solution.py:589
  68.7 5.7 %project.5.refs_6_ = bf16[8,128,256]{2,1,0:T(8,128)(2,1)S(1)} custom-call(s32[8]{0:T(128)S(1)} %dynamic-slice_bitcast_fusion.place_ref, bf16[32,4096]{1,0:T(8,128)(2,1)S(1)} %get-tuple-element.112.refs_0_, bf16[32,4096]{1,0:T(8,128)(2,1)S(1)} %collective-permute-done.9.refs_1_, bf16[32,4096]{1,0:T(8,128)(2,1)S(1)} %collective-permute-done.10.refs_2_, ...), custom_call_target="tpu_custom_call" | custom-call | flops 2147483648 | bytes 10485760 | tf_op jit(solution)/shard_map/project/pallas_call | solution.py:173
  74.4 9.5 %collective-permute-start.23 = (bf16[8,128,256]{2,1,0:T(8,128)(2,1)S(1)}, bf16[8,128,256]{2,1,0:T(8,128)(2,1)S(1)}, u32[]{:S(2)}, u32[]{:S(2)}) collective-permute-start(bf16[8,128,256]{2,1,0:T(8,128)(2,1)S(1)} %project.5.refs_6_), channel_id=1, source_target_pairs={{0,4},{1,5},{2,6},{3,7},{4,0},{5,1},{6,2},{7,3},{8,12},{9,13},{10,... | collective-permute-start | bytes 1572872 | tf_op jit(solution)/shard_map/ppermute | solution.py:614
  84.0 0.6 collective-permute-start.6
  84.6 2.9 %collective-permute-start.8 = (bf16[2,4,256,128]{3,2,1,0:T(8,128)(2,1)S(1)}, bf16[2,4,256,128]{3,2,1,0:T(8,128)(2,1)S(1)}, u32[]{:S(2)}, u32[]{:S(2)}) collective-permute-start(bf16[2,4,256,128]{3,2,1,0:T(8,128)(2,1)S(1)} %get-tuple-element.104), channel_id=1, source_target_pairs={{0,3},{1,2},{2,1},{3,0},{4,7},{5,6},{6,5},{7,4},{8,11},{9,10},{10,... | collective-permute-start | bytes 1572872 | tf_op jit(solution)/shard_map/ppermute | solution.py:605
  87.5 18.0 %collective-permute-done.23.refs_6_ = bf16[8,128,256]{2,1,0:T(8,128)(2,1)S(1)} collective-permute-done((bf16[8,128,256]{2,1,0:T(8,128)(2,1)S(1)}, bf16[8,128,256]{2,1,0:T(8,128)(2,1)S(1)}, u32[]{:S(2)}, u32[]{:S(2)}) %collective-permute-start.23) | collective-permute-done | bytes 524320 | tf_op jit(solution)/shard_map/ppermute | solution.py:614
  105.4 14.7 %attend.3 = bf16[8,144,256]{2,1,0:T(8,128)(2,1)S(1)} custom-call(s32[16]{0:T(128)S(1)} %select_n.48.first_ref, s32[256]{0:T(256)S(1)} %bitcast.24, s32[1]{0:T(128)} %bitcast.6.odd_ref, bf16[2,4,256,128]{3,2,1,0:T(8,128)(2,1)S(1)} %get-tuple-element.131.refs_0_, bf16[2,4,256,128]{3,2,1,0:T(8,128)(2,1)S(1)} %collective-permute-done.22.refs_1_, ...), custom_call_target="tpu_custom_call" | custom-call | flops 2147483648 | bytes 2097152 | tf_op jit(solution)/shard_map/attend/pallas_call | solution.py:378
  120.2 16.6 %attend.2 = (f32[8,1,256]{2,1,0:T(1,128)S(1)}, f32[8,1,256]{2,1,0:T(1,128)S(1)}, f32[8,128,256]{2,1,0:T(8,128)S(1)}) custom-call(s32[16]{0:T(128)S(1)} %select_n.48.first_ref, s32[256]{0:T(256)S(1)} %bitcast.25, s32[1]{0:T(128)} %bitcast.6.odd_ref, bf16[2,4,256,128]{3,2,1,0:T(8,128)(2,1)S(1)} %get-tuple-element.101.refs_0_, ...), custom_call_target="tpu_custom_call" | custom-call | flops 2147483648 | bytes 2097152 | tf_op jit(solution)/shard_map/attend/pallas_call | solution.py:378
  136.8 10.7 %collective-permute-done.24.refs_3_ = bf16[8,144,256]{2,1,0:T(8,128)(2,1)S(1)} collective-permute-done((bf16[8,144,256]{2,1,0:T(8,128)(2,1)S(1)}, bf16[8,144,256]{2,1,0:T(8,128)(2,1)S(1)}, u32[]{:S(2)}, u32[]{:S(2)}) %collective-permute-start.24) | collective-permute-done | bytes 589856 | tf_op jit(solution)/shard_map/ppermute | solution.py:618
  147.5 0.4 merge.1.x_ref
  147.9 5.1 %project_out.2 = (f32[32,4096]{1,0:T(8,128)S(1)}, f32[32,4096]{1,0:T(8,128)S(1)}, f32[32,4096]{1,0:T(8,128)S(1)}, f32[32,4096]{1,0:T(8,128)S(1)}, f32[32,4096]{1...) custom-call(s32[8]{0:T(128)S(1)} %dynamic-slice_bitcast_fusion.place_ref, ...), custom_call_target="tpu_custom_call" | custom-call | flops 2147483648 | bytes 13107200 | tf_op jit(solution)/shard_map/project_out/pallas_call | solution.py:466
  153.1 2.3 %collective-permute-start.29 = (bf16[32,4096]{1,0:T(8,128)(2,1)S(1)}, bf16[32,4096]{1,0:T(8,128)(2,1)S(1)}, u32[]{:S(2)}, u32[]{:S(2)}) collective-permute-start(bf16[32,4096]{1,0:T(8,128)(2,1)S(1)} %convert_element_type.116), channel_id=1, source_target_pairs={{2,0},{4,2},{6,4},{7,6},{5,7},{3,5},{1,3},{0,1},{10,8},{12,10},{14... | collective-permute-start | bytes 786440 | tf_op jit(solution)/shard_map/ppermute | solution.py:634
  155.4 5.1 %project_out.3 = (f32[32,4096]{1,0:T(8,128)S(1)}, f32[32,4096]{1,0:T(8,128)S(1)}, f32[32,4096]{1,0:T(8,128)S(1)}, f32[32,4096]{1,0:T(8,128)S(1)}, f32[32,4096]{1...) custom-call(s32[8]{0:T(128)S(1)} %dynamic-slice_bitcast_fusion.place_ref, ...), custom_call_target="tpu_custom_call" | custom-call | flops 2147483648 | bytes 13107200 | tf_op jit(solution)/shard_map/project_out/pallas_call | solution.py:466
  160.6 2.0 %collective-permute-start.35 = (bf16[32,4096]{1,0:T(8,128)(2,1)S(1)}, bf16[32,4096]{1,0:T(8,128)(2,1)S(1)}, u32[]{:S(2)}, u32[]{:S(2)}) collective-permute-start(bf16[32,4096]{1,0:T(8,128)(2,1)S(1)} %get-tuple-element.150), channel_id=1, source_target_pairs={{2,0},{4,2},{6,4},{7,6},{5,7},{3,5},{1,3},{0,1},{10,8},{12,10},{14... | collective-permute-start | bytes 786440 | tf_op jit(solution)/shard_map/ppermute | solution.py:634
  162.8 2.0 %collective-permute-start.30 = (bf16[32,4096]{1,0:T(8,128)(2,1)S(1)}, bf16[32,4096]{1,0:T(8,128)(2,1)S(1)}, u32[]{:S(2)}, u32[]{:S(2)}) collective-permute-start(bf16[32,4096]{1,0:T(8,128)(2,1)S(1)} %add_convert_fusion.8), channel_id=1, source_target_pairs={{2,0},{4,2},{6,4},{7,6},{5,7},{3,5},{1,3},{0,1},{10,8},{12,10},{14... | collective-permute-start | bytes 786440 | tf_op jit(solution)/shard_map/ppermute | solution.py:634
  164.8 5.0 %collective-permute-done.32 = bf16[32,4096]{1,0:T(8,128)(2,1)S(1)} collective-permute-done((bf16[32,4096]{1,0:T(8,128)(2,1)S(1)}, bf16[32,4096]{1,0:T(8,128)(2,1)S(1)}, u32[]{:S(2)}, u32[]{:S(2)}) %collective-permute-start.32) | collective-permute-done | bytes 262176 | tf_op jit(solution)/shard_map/ppermute | solution.py:634
  170.0 2.1 %collective-permute-start.36 = (bf16[32,4096]{1,0:T(8,128)(2,1)S(1)}, bf16[32,4096]{1,0:T(8,128)(2,1)S(1)}, u32[]{:S(2)}, u32[]{:S(2)}) collective-permute-start(bf16[32,4096]{1,0:T(8,128)(2,1)S(1)} %add_convert_fusion.3), channel_id=1, source_target_pairs={{2,0},{4,2},{6,4},{7,6},{5,7},{3,5},{1,3},{0,1},{10,8},{12,10},{14... | collective-permute-start | bytes 786440 | tf_op jit(solution)/shard_map/ppermute | solution.py:634
  172.0 3.4 %collective-permute-done.26 = bf16[32,4096]{1,0:T(8,128)(2,1)S(1)} collective-permute-done((bf16[32,4096]{1,0:T(8,128)(2,1)S(1)}, bf16[32,4096]{1,0:T(8,128)(2,1)S(1)}, u32[]{:S(2)}, u32[]{:S(2)}) %collective-permute-start.26) | collective-permute-done | bytes 262176 | tf_op jit(solution)/shard_map/ppermute | solution.py:634
  175.6 2.1 %collective-permute-start.31 = (bf16[32,4096]{1,0:T(8,128)(2,1)S(1)}, bf16[32,4096]{1,0:T(8,128)(2,1)S(1)}, u32[]{:S(2)}, u32[]{:S(2)}) collective-permute-start(bf16[32,4096]{1,0:T(8,128)(2,1)S(1)} %add_convert_fusion.7), channel_id=1, source_target_pairs={{2,0},{4,2},{6,4},{7,6},{5,7},{3,5},{1,3},{0,1},{10,8},{12,10},{14... | collective-permute-start | bytes 786440 | tf_op jit(solution)/shard_map/ppermute | solution.py:634
  177.6 3.4 %collective-permute-done.33 = bf16[32,4096]{1,0:T(8,128)(2,1)S(1)} collective-permute-done((bf16[32,4096]{1,0:T(8,128)(2,1)S(1)}, bf16[32,4096]{1,0:T(8,128)(2,1)S(1)}, u32[]{:S(2)}, u32[]{:S(2)}) %collective-permute-start.33) | collective-permute-done | bytes 262176 | tf_op jit(solution)/shard_map/ppermute | solution.py:634
  181.2 2.1 %collective-permute-start.37 = (bf16[32,4096]{1,0:T(8,128)(2,1)S(1)}, bf16[32,4096]{1,0:T(8,128)(2,1)S(1)}, u32[]{:S(2)}, u32[]{:S(2)}) collective-permute-start(bf16[32,4096]{1,0:T(8,128)(2,1)S(1)} %add_convert_fusion.2), channel_id=1, source_target_pairs={{2,0},{4,2},{6,4},{7,6},{5,7},{3,5},{1,3},{0,1},{10,8},{12,10},{14... | collective-permute-start | bytes 786440 | tf_op jit(solution)/shard_map/ppermute | solution.py:634
  183.2 3.4 %collective-permute-done.27 = bf16[32,4096]{1,0:T(8,128)(2,1)S(1)} collective-permute-done((bf16[32,4096]{1,0:T(8,128)(2,1)S(1)}, bf16[32,4096]{1,0:T(8,128)(2,1)S(1)}, u32[]{:S(2)}, u32[]{:S(2)}) %collective-permute-start.27) | collective-permute-done | bytes 262176 | tf_op jit(solution)/shard_map/ppermute | solution.py:634
  186.7 4.1 %collective-permute-done.37 = bf16[32,4096]{1,0:T(8,128)(2,1)S(1)} collective-permute-done((bf16[32,4096]{1,0:T(8,128)(2,1)S(1)}, bf16[32,4096]{1,0:T(8,128)(2,1)S(1)}, u32[]{:S(2)}, u32[]{:S(2)}) %collective-permute-start.37) | collective-permute-done | bytes 262176 | tf_op jit(solution)/shard_map/ppermute | solution.py:634
  190.9 1.7 collective-permute-start.38
  192.6 3.8 %collective-permute-done.28 = bf16[32,4096]{1,0:T(8,128)(2,1)S(1)} collective-permute-done((bf16[32,4096]{1,0:T(8,128)(2,1)S(1)}, bf16[32,4096]{1,0:T(8,128)(2,1)S(1)}, u32[]{:S(2)}, u32[]{:S(2)}) %collective-permute-start.28) | collective-permute-done | bytes 262176 | tf_op jit(solution)/shard_map/ppermute | solution.py:634
  196.5 1.3 collective-permute-done.38
  197.9 0.8 pad_maximum_fusion
  (75 shorter events, 2.2 us)
Async XLA Ops:
  2.5 10.7 %copy-start = (s32[1,256]{1,0:T(1,128)S(1)}, s32[1,256]{1,0:T(1,128)}, u32[]{:S(2)}) copy-start(s32[1,256]{1,0:T(1,128)} %param.18) | copy-start | bytes 3076
  2.5 10.7 %copy-start.1 = (s32[1,4]{1,0:T(1,128)S(1)}, s32[1,4]{1,0:T(1,128)}, u32[]{:S(2)}) copy-start(s32[1,4]{1,0:T(1,128)} %param.17) | copy-start | bytes 52
  2.5 13.1 %copy-start.2 = (s32[4]{0:T(128)S(1)}, s32[4]{0:T(128)}, u32[]{:S(2)}) copy-start(s32[4]{0:T(128)} %param.16) | copy-start | bytes 52
  8.0 32.3 %collective-permute-start.3 = (bf16[4,2,256,1024]{3,2,1,0:T(8,128)(2,1)}, bf16[4,2,256,1024]{3,2,1,0:T(8,128)(2,1)}, u32[]{:S(2)}, u32[]{:S(2)}) collective-permute-start(bf16[4,2,256,1024]{3,2,1,0:T(8,128)(2,1)} %bitcast.21.refs_0_), channel_id=1, source_target_pairs={{8,0},{0,8},{9,1},{1,9},{10,2},{2,10},{11,3},{3,11},{12,4},{4,12},... | collective-permute-start | bytes 12582920 | tf_op jit(solution)/shard_map/ppermute | solution.py:556
  8.5 9.7 %collective-permute-start = (bf16[32,4096]{1,0:T(8,128)(2,1)S(1)}, bf16[32,4096]{1,0:T(8,128)(2,1)S(1)}, u32[]{:S(2)}, u32[]{:S(2)}) collective-permute-start(bf16[32,4096]{1,0:T(8,128)(2,1)S(1)} %get-tuple-element.152.refs_0_), channel_id=1, source_target_pairs={{0,2},{2,4},{4,6},{6,7},{7,5},{5,3},{3,1},{1,0},{8,10},{10,12},{12... | collective-permute-start | bytes 786440 | tf_op jit(solution)/shard_map/ppermute | solution.py:547
  11.2 15.9 %collective-permute-start.16 = (bf16[32,4096]{1,0:T(8,128)(2,1)S(1)}, bf16[32,4096]{1,0:T(8,128)(2,1)S(1)}, u32[]{:S(2)}, u32[]{:S(2)}) collective-permute-start(bf16[32,4096]{1,0:T(8,128)(2,1)S(1)} %get-tuple-element.152.refs_0_), channel_id=1, source_target_pairs={{2,0},{4,2},{6,4},{7,6},{5,7},{3,5},{1,3},{0,1},{10,8},{12,10},{14... | collective-permute-start | bytes 786440 | tf_op jit(solution)/shard_map/ppermute | solution.py:549
  11.2 14.0 %collective-permute-start.10 = (bf16[32,4096]{1,0:T(8,128)(2,1)S(1)}, bf16[32,4096]{1,0:T(8,128)(2,1)S(1)}, u32[]{:S(2)}, u32[]{:S(2)}) collective-permute-start(bf16[32,4096]{1,0:T(8,128)(2,1)S(1)} %get-tuple-element.112.refs_0_), channel_id=1, source_target_pairs={{2,0},{4,2},{6,4},{7,6},{5,7},{3,5},{1,3},{0,1},{10,8},{12,10},{14... | collective-permute-start | bytes 786440 | tf_op jit(solution)/shard_map/ppermute | solution.py:549
  13.1 18.6 %collective-permute-start.9 = (bf16[32,4096]{1,0:T(8,128)(2,1)S(1)}, bf16[32,4096]{1,0:T(8,128)(2,1)S(1)}, u32[]{:S(2)}, u32[]{:S(2)}) collective-permute-start(bf16[32,4096]{1,0:T(8,128)(2,1)S(1)} %get-tuple-element.112.refs_0_), channel_id=1, source_target_pairs={{0,2},{2,4},{4,6},{6,7},{7,5},{5,3},{3,1},{1,0},{8,10},{10,12},{12... | collective-permute-start | bytes 786440 | tf_op jit(solution)/shard_map/ppermute | solution.py:547
  18.3 11.1 %collective-permute-start.1 = (bf16[32,4096]{1,0:T(8,128)(2,1)S(1)}, bf16[32,4096]{1,0:T(8,128)(2,1)S(1)}, u32[]{:S(2)}, u32[]{:S(2)}) collective-permute-start(bf16[32,4096]{1,0:T(8,128)(2,1)S(1)} %collective-permute-done.refs_1_), channel_id=1, source_target_pairs={{0,2},{2,4},{4,6},{6,7},{7,5},{5,3},{3,1},{1,0},{8,10},{10,12},{12... | collective-permute-start | bytes 786440 | tf_op jit(solution)/shard_map/ppermute | solution.py:547
  25.2 9.2 %collective-permute-start.12 = (bf16[32,4096]{1,0:T(8,128)(2,1)S(1)}, bf16[32,4096]{1,0:T(8,128)(2,1)S(1)}, u32[]{:S(2)}, u32[]{:S(2)}) collective-permute-start(bf16[32,4096]{1,0:T(8,128)(2,1)S(1)} %collective-permute-done.10.refs_2_), channel_id=1, source_target_pairs={{2,0},{4,2},{6,4},{7,6},{5,7},{3,5},{1,3},{0,1},{10,8},{12,10},{14... | collective-permute-start | bytes 786440 | tf_op jit(solution)/shard_map/ppermute | solution.py:549
  27.0 13.0 %collective-permute-start.17 = (bf16[32,4096]{1,0:T(8,128)(2,1)S(1)}, bf16[32,4096]{1,0:T(8,128)(2,1)S(1)}, u32[]{:S(2)}, u32[]{:S(2)}) collective-permute-start(bf16[32,4096]{1,0:T(8,128)(2,1)S(1)} %collective-permute-done.16.refs_2_), channel_id=1, source_target_pairs={{2,0},{4,2},{6,4},{7,6},{5,7},{3,5},{1,3},{0,1},{10,8},{12,10},{14... | collective-permute-start | bytes 786440 | tf_op jit(solution)/shard_map/ppermute | solution.py:549
  29.9 13.7 %collective-permute-start.2 = (bf16[32,4096]{1,0:T(8,128)(2,1)S(1)}, bf16[32,4096]{1,0:T(8,128)(2,1)S(1)}, u32[]{:S(2)}, u32[]{:S(2)}) collective-permute-start(bf16[32,4096]{1,0:T(8,128)(2,1)S(1)} %collective-permute-done.1.refs_3_), channel_id=1, source_target_pairs={{0,2},{2,4},{4,6},{6,7},{7,5},{5,3},{3,1},{1,0},{8,10},{10,12},{12... | collective-permute-start | bytes 786440 | tf_op jit(solution)/shard_map/ppermute | solution.py:547
  31.8 13.7 %collective-permute-start.11 = (bf16[32,4096]{1,0:T(8,128)(2,1)S(1)}, bf16[32,4096]{1,0:T(8,128)(2,1)S(1)}, u32[]{:S(2)}, u32[]{:S(2)}) collective-permute-start(bf16[32,4096]{1,0:T(8,128)(2,1)S(1)} %collective-permute-done.9.refs_1_), channel_id=1, source_target_pairs={{0,2},{2,4},{4,6},{6,7},{7,5},{5,3},{3,1},{1,0},{8,10},{10,12},{12... | collective-permute-start | bytes 786440 | tf_op jit(solution)/shard_map/ppermute | solution.py:547
  34.5 12.6 %collective-permute-start.14 = (bf16[32,4096]{1,0:T(8,128)(2,1)S(1)}, bf16[32,4096]{1,0:T(8,128)(2,1)S(1)}, u32[]{:S(2)}, u32[]{:S(2)}) collective-permute-start(bf16[32,4096]{1,0:T(8,128)(2,1)S(1)} %collective-permute-done.12.refs_4_), channel_id=1, source_target_pairs={{2,0},{4,2},{6,4},{7,6},{5,7},{3,5},{1,3},{0,1},{10,8},{12,10},{14... | collective-permute-start | bytes 786440 | tf_op jit(solution)/shard_map/ppermute | solution.py:549
  40.1 11.2 %collective-permute-start.18 = (bf16[32,4096]{1,0:T(8,128)(2,1)S(1)}, bf16[32,4096]{1,0:T(8,128)(2,1)S(1)}, u32[]{:S(2)}, u32[]{:S(2)}) collective-permute-start(bf16[32,4096]{1,0:T(8,128)(2,1)S(1)} %collective-permute-done.17.refs_4_), channel_id=1, source_target_pairs={{2,0},{4,2},{6,4},{7,6},{5,7},{3,5},{1,3},{0,1},{10,8},{12,10},{14... | collective-permute-start | bytes 786440 | tf_op jit(solution)/shard_map/ppermute | solution.py:549
  43.6 9.1 %collective-permute-start.19 = (bf16[32,4096]{1,0:T(8,128)(2,1)S(1)}, bf16[32,4096]{1,0:T(8,128)(2,1)S(1)}, u32[]{:S(2)}, u32[]{:S(2)}) collective-permute-start(bf16[32,4096]{1,0:T(8,128)(2,1)S(1)} %collective-permute-done.2.refs_5_), channel_id=1, source_target_pairs={{0,2},{2,4},{4,6},{6,7},{7,5},{5,3},{3,1},{1,0},{8,10},{10,12},{12... | collective-permute-start | bytes 786440 | tf_op jit(solution)/shard_map/ppermute | solution.py:547
  45.4 15.6 %collective-permute-start.13 = (bf16[32,4096]{1,0:T(8,128)(2,1)S(1)}, bf16[32,4096]{1,0:T(8,128)(2,1)S(1)}, u32[]{:S(2)}, u32[]{:S(2)}) collective-permute-start(bf16[32,4096]{1,0:T(8,128)(2,1)S(1)} %collective-permute-done.11.refs_3_), channel_id=1, source_target_pairs={{0,2},{2,4},{4,6},{6,7},{7,5},{5,3},{3,1},{1,0},{8,10},{10,12},{12... | collective-permute-start | bytes 786440 | tf_op jit(solution)/shard_map/ppermute | solution.py:547
  47.0 14.0 %collective-permute-start.15 = (bf16[32,4096]{1,0:T(8,128)(2,1)S(1)}, bf16[32,4096]{1,0:T(8,128)(2,1)S(1)}, u32[]{:S(2)}, u32[]{:S(2)}) collective-permute-start(bf16[32,4096]{1,0:T(8,128)(2,1)S(1)} %collective-permute-done.14.refs_6_), channel_id=1, source_target_pairs={{2,0},{4,2},{6,4},{7,6},{5,7},{3,5},{1,3},{0,1},{10,8},{12,10},{14... | collective-permute-start | bytes 786440 | tf_op jit(solution)/shard_map/ppermute | solution.py:549
  47.5 36.5 %collective-permute-start.4 = (bf16[2,4,256,128]{3,2,1,0:T(8,128)(2,1)S(1)}, bf16[2,4,256,128]{3,2,1,0:T(8,128)(2,1)S(1)}, u32[]{:S(2)}, u32[]{:S(2)}) collective-permute-start(bf16[2,4,256,128]{3,2,1,0:T(8,128)(2,1)S(1)} %get-tuple-element.99), channel_id=1, source_target_pairs={{0,2},{1,3},{2,0},{3,1},{4,6},{5,7},{6,4},{7,5},{8,10},{9,11},{10,... | collective-permute-start | bytes 1572872 | tf_op jit(solution)/shard_map/ppermute | solution.py:605
  51.3 32.7 %collective-permute-start.5 = (bf16[2,4,256,128]{3,2,1,0:T(8,128)(2,1)S(1)}, bf16[2,4,256,128]{3,2,1,0:T(8,128)(2,1)S(1)}, u32[]{:S(2)}, u32[]{:S(2)}) collective-permute-start(bf16[2,4,256,128]{3,2,1,0:T(8,128)(2,1)S(1)} %get-tuple-element.100), channel_id=1, source_target_pairs={{0,3},{1,2},{2,1},{3,0},{4,7},{5,6},{6,5},{7,4},{8,11},{9,10},{10,... | collective-permute-start | bytes 1572872 | tf_op jit(solution)/shard_map/ppermute | solution.py:605
  52.7 34.7 %collective-permute-start.22 = (bf16[2,4,256,128]{3,2,1,0:T(8,128)(2,1)S(1)}, bf16[2,4,256,128]{3,2,1,0:T(8,128)(2,1)S(1)}, u32[]{:S(2)}, u32[]{:S(2)}) collective-permute-start(bf16[2,4,256,128]{3,2,1,0:T(8,128)(2,1)S(1)} %get-tuple-element.132), channel_id=1, source_target_pairs={{0,1},{1,0},{2,3},{3,2},{4,5},{5,4},{6,7},{7,6},{8,9},{9,8},{10,11... | collective-permute-start | bytes 1572872 | tf_op jit(solution)/shard_map/ppermute | solution.py:605
  64.5 10.0 %collective-permute-start.20 = (bf16[256,128]{1,0:T(8,128)(2,1)S(1)}, bf16[256,128]{1,0:T(8,128)(2,1)S(1)}, u32[]{:S(2)}, u32[]{:S(2)}) collective-permute-start(bf16[256,128]{1,0:T(8,128)(2,1)S(1)} %get-tuple-element.123), channel_id=1, source_target_pairs={{0,0},{1,2},{2,4},{3,6},{4,1},{5,3},{6,5},{7,7},{8,8},{9,10},{10,1... | collective-permute-start | bytes 196616 | tf_op jit(solution)/shard_map/ppermute | solution.py:589
  65.1 9.3 %collective-permute-start.21 = (bf16[256,128]{1,0:T(8,128)(2,1)S(1)}, bf16[256,128]{1,0:T(8,128)(2,1)S(1)}, u32[]{:S(2)}, u32[]{:S(2)}) collective-permute-start(bf16[256,128]{1,0:T(8,128)(2,1)S(1)} %get-tuple-element.124), channel_id=1, source_target_pairs={{0,1},{1,3},{2,5},{3,7},{4,0},{5,2},{6,4},{7,6},{8,9},{9,11},{10,1... | collective-permute-start | bytes 196616 | tf_op jit(solution)/shard_map/ppermute | solution.py:589
  74.4 31.0 %collective-permute-start.23 = (bf16[8,128,256]{2,1,0:T(8,128)(2,1)S(1)}, bf16[8,128,256]{2,1,0:T(8,128)(2,1)S(1)}, u32[]{:S(2)}, u32[]{:S(2)}) collective-permute-start(bf16[8,128,256]{2,1,0:T(8,128)(2,1)S(1)} %project.5.refs_6_), channel_id=1, source_target_pairs={{0,4},{1,5},{2,6},{3,7},{4,0},{5,1},{6,2},{7,3},{8,12},{9,13},{10,... | collective-permute-start | bytes 1572872 | tf_op jit(solution)/shard_map/ppermute | solution.py:614
  84.0 36.2 %collective-permute-start.6 = (bf16[2,4,256,128]{3,2,1,0:T(8,128)(2,1)S(1)}, bf16[2,4,256,128]{3,2,1,0:T(8,128)(2,1)S(1)}, u32[]{:S(2)}, u32[]{:S(2)}) collective-permute-start(bf16[2,4,256,128]{3,2,1,0:T(8,128)(2,1)S(1)} %get-tuple-element.102), channel_id=1, source_target_pairs={{0,1},{1,0},{2,3},{3,2},{4,5},{5,4},{6,7},{7,6},{8,9},{9,8},{10,11... | collective-permute-start | bytes 1572872 | tf_op jit(solution)/shard_map/ppermute | solution.py:605
  84.6 35.6 %collective-permute-start.7 = (bf16[2,4,256,128]{3,2,1,0:T(8,128)(2,1)S(1)}, bf16[2,4,256,128]{3,2,1,0:T(8,128)(2,1)S(1)}, u32[]{:S(2)}, u32[]{:S(2)}) collective-permute-start(bf16[2,4,256,128]{3,2,1,0:T(8,128)(2,1)S(1)} %get-tuple-element.103), channel_id=1, source_target_pairs={{0,2},{1,3},{2,0},{3,1},{4,6},{5,7},{6,4},{7,5},{8,10},{9,11},{10,... | collective-permute-start | bytes 1572872 | tf_op jit(solution)/shard_map/ppermute | solution.py:605
  84.6 35.6 %collective-permute-start.8 = (bf16[2,4,256,128]{3,2,1,0:T(8,128)(2,1)S(1)}, bf16[2,4,256,128]{3,2,1,0:T(8,128)(2,1)S(1)}, u32[]{:S(2)}, u32[]{:S(2)}) collective-permute-start(bf16[2,4,256,128]{3,2,1,0:T(8,128)(2,1)S(1)} %get-tuple-element.104), channel_id=1, source_target_pairs={{0,3},{1,2},{2,1},{3,0},{4,7},{5,6},{6,5},{7,4},{8,11},{9,10},{10,... | collective-permute-start | bytes 1572872 | tf_op jit(solution)/shard_map/ppermute | solution.py:605
  120.1 27.4 %collective-permute-start.24 = (bf16[8,144,256]{2,1,0:T(8,128)(2,1)S(1)}, bf16[8,144,256]{2,1,0:T(8,128)(2,1)S(1)}, u32[]{:S(2)}, u32[]{:S(2)}) collective-permute-start(bf16[8,144,256]{2,1,0:T(8,128)(2,1)S(1)} %attend.3), channel_id=1, source_target_pairs={{0,4},{1,5},{2,6},{3,7},{4,0},{5,1},{6,2},{7,3},{8,12},{9,13},{10,... | collective-permute-start | bytes 1769480 | tf_op jit(solution)/shard_map/ppermute | solution.py:618
  153.0 9.6 %collective-permute-start.25 = (bf16[32,4096]{1,0:T(8,128)(2,1)S(1)}, bf16[32,4096]{1,0:T(8,128)(2,1)S(1)}, u32[]{:S(2)}, u32[]{:S(2)}) collective-permute-start(bf16[32,4096]{1,0:T(8,128)(2,1)S(1)} %get-tuple-element.139), channel_id=1, source_target_pairs={{0,2},{2,4},{4,6},{6,7},{7,5},{5,3},{3,1},{1,0},{8,10},{10,12},{12... | collective-permute-start | bytes 786440 | tf_op jit(solution)/shard_map/ppermute | solution.py:634
  153.1 9.7 %collective-permute-start.29 = (bf16[32,4096]{1,0:T(8,128)(2,1)S(1)}, bf16[32,4096]{1,0:T(8,128)(2,1)S(1)}, u32[]{:S(2)}, u32[]{:S(2)}) collective-permute-start(bf16[32,4096]{1,0:T(8,128)(2,1)S(1)} %convert_element_type.116), channel_id=1, source_target_pairs={{2,0},{4,2},{6,4},{7,6},{5,7},{3,5},{1,3},{0,1},{10,8},{12,10},{14... | collective-permute-start | bytes 786440 | tf_op jit(solution)/shard_map/ppermute | solution.py:634
  160.5 9.3 %collective-permute-start.32 = (bf16[32,4096]{1,0:T(8,128)(2,1)S(1)}, bf16[32,4096]{1,0:T(8,128)(2,1)S(1)}, u32[]{:S(2)}, u32[]{:S(2)}) collective-permute-start(bf16[32,4096]{1,0:T(8,128)(2,1)S(1)} %convert_element_type.123), channel_id=1, source_target_pairs={{0,2},{2,4},{4,6},{6,7},{7,5},{5,3},{3,1},{1,0},{8,10},{10,12},{12... | collective-permute-start | bytes 786440 | tf_op jit(solution)/shard_map/ppermute | solution.py:634
  160.6 9.3 %collective-permute-start.35 = (bf16[32,4096]{1,0:T(8,128)(2,1)S(1)}, bf16[32,4096]{1,0:T(8,128)(2,1)S(1)}, u32[]{:S(2)}, u32[]{:S(2)}) collective-permute-start(bf16[32,4096]{1,0:T(8,128)(2,1)S(1)} %get-tuple-element.150), channel_id=1, source_target_pairs={{2,0},{4,2},{6,4},{7,6},{5,7},{3,5},{1,3},{0,1},{10,8},{12,10},{14... | collective-permute-start | bytes 786440 | tf_op jit(solution)/shard_map/ppermute | solution.py:634
  162.6 12.8 %collective-permute-start.26 = (bf16[32,4096]{1,0:T(8,128)(2,1)S(1)}, bf16[32,4096]{1,0:T(8,128)(2,1)S(1)}, u32[]{:S(2)}, u32[]{:S(2)}) collective-permute-start(bf16[32,4096]{1,0:T(8,128)(2,1)S(1)} %add_convert_fusion.11), channel_id=1, source_target_pairs={{0,2},{2,4},{4,6},{6,7},{7,5},{5,3},{3,1},{1,0},{8,10},{10,12},{12... | collective-permute-start | bytes 786440 | tf_op jit(solution)/shard_map/ppermute | solution.py:634
  162.8 12.7 %collective-permute-start.30 = (bf16[32,4096]{1,0:T(8,128)(2,1)S(1)}, bf16[32,4096]{1,0:T(8,128)(2,1)S(1)}, u32[]{:S(2)}, u32[]{:S(2)}) collective-permute-start(bf16[32,4096]{1,0:T(8,128)(2,1)S(1)} %add_convert_fusion.8), channel_id=1, source_target_pairs={{2,0},{4,2},{6,4},{7,6},{5,7},{3,5},{1,3},{0,1},{10,8},{12,10},{14... | collective-permute-start | bytes 786440 | tf_op jit(solution)/shard_map/ppermute | solution.py:634
  169.8 11.2 %collective-permute-start.33 = (bf16[32,4096]{1,0:T(8,128)(2,1)S(1)}, bf16[32,4096]{1,0:T(8,128)(2,1)S(1)}, u32[]{:S(2)}, u32[]{:S(2)}) collective-permute-start(bf16[32,4096]{1,0:T(8,128)(2,1)S(1)} %add_convert_fusion.5), channel_id=1, source_target_pairs={{0,2},{2,4},{4,6},{6,7},{7,5},{5,3},{3,1},{1,0},{8,10},{10,12},{12... | collective-permute-start | bytes 786440 | tf_op jit(solution)/shard_map/ppermute | solution.py:634
  170.0 11.2 %collective-permute-start.36 = (bf16[32,4096]{1,0:T(8,128)(2,1)S(1)}, bf16[32,4096]{1,0:T(8,128)(2,1)S(1)}, u32[]{:S(2)}, u32[]{:S(2)}) collective-permute-start(bf16[32,4096]{1,0:T(8,128)(2,1)S(1)} %add_convert_fusion.3), channel_id=1, source_target_pairs={{2,0},{4,2},{6,4},{7,6},{5,7},{3,5},{1,3},{0,1},{10,8},{12,10},{14... | collective-permute-start | bytes 786440 | tf_op jit(solution)/shard_map/ppermute | solution.py:634
  175.4 11.2 %collective-permute-start.27 = (bf16[32,4096]{1,0:T(8,128)(2,1)S(1)}, bf16[32,4096]{1,0:T(8,128)(2,1)S(1)}, u32[]{:S(2)}, u32[]{:S(2)}) collective-permute-start(bf16[32,4096]{1,0:T(8,128)(2,1)S(1)} %add_convert_fusion.10), channel_id=1, source_target_pairs={{0,2},{2,4},{4,6},{6,7},{7,5},{5,3},{3,1},{1,0},{8,10},{10,12},{12... | collective-permute-start | bytes 786440 | tf_op jit(solution)/shard_map/ppermute | solution.py:634
  175.6 17.1 %collective-permute-start.31 = (bf16[32,4096]{1,0:T(8,128)(2,1)S(1)}, bf16[32,4096]{1,0:T(8,128)(2,1)S(1)}, u32[]{:S(2)}, u32[]{:S(2)}) collective-permute-start(bf16[32,4096]{1,0:T(8,128)(2,1)S(1)} %add_convert_fusion.7), channel_id=1, source_target_pairs={{2,0},{4,2},{6,4},{7,6},{5,7},{3,5},{1,3},{0,1},{10,8},{12,10},{14... | collective-permute-start | bytes 786440 | tf_op jit(solution)/shard_map/ppermute | solution.py:634
  181.1 15.4 %collective-permute-start.34 = (bf16[32,4096]{1,0:T(8,128)(2,1)S(1)}, bf16[32,4096]{1,0:T(8,128)(2,1)S(1)}, u32[]{:S(2)}, u32[]{:S(2)}) collective-permute-start(bf16[32,4096]{1,0:T(8,128)(2,1)S(1)} %add_convert_fusion.4), channel_id=1, source_target_pairs={{0,2},{2,4},{4,6},{6,7},{7,5},{5,3},{3,1},{1,0},{8,10},{10,12},{12... | collective-permute-start | bytes 786440 | tf_op jit(solution)/shard_map/ppermute | solution.py:634
  181.2 9.7 %collective-permute-start.37 = (bf16[32,4096]{1,0:T(8,128)(2,1)S(1)}, bf16[32,4096]{1,0:T(8,128)(2,1)S(1)}, u32[]{:S(2)}, u32[]{:S(2)}) collective-permute-start(bf16[32,4096]{1,0:T(8,128)(2,1)S(1)} %add_convert_fusion.2), channel_id=1, source_target_pairs={{2,0},{4,2},{6,4},{7,6},{5,7},{3,5},{1,3},{0,1},{10,8},{12,10},{14... | collective-permute-start | bytes 786440 | tf_op jit(solution)/shard_map/ppermute | solution.py:634
  186.7 9.7 %collective-permute-start.28 = (bf16[32,4096]{1,0:T(8,128)(2,1)S(1)}, bf16[32,4096]{1,0:T(8,128)(2,1)S(1)}, u32[]{:S(2)}, u32[]{:S(2)}) collective-permute-start(bf16[32,4096]{1,0:T(8,128)(2,1)S(1)} %add_convert_fusion.9), channel_id=1, source_target_pairs={{0,2},{2,4},{4,6},{6,7},{7,5},{5,3},{3,1},{1,0},{8,10},{10,12},{12... | collective-permute-start | bytes 786440 | tf_op jit(solution)/shard_map/ppermute | solution.py:634
  190.9 6.9 %collective-permute-start.38 = (bf16[32,4096]{1,0:T(8,128)(2,1)S(1)}, bf16[32,4096]{1,0:T(8,128)(2,1)S(1)}, u32[]{:S(2)}, u32[]{:S(2)}) collective-permute-start(bf16[32,4096]{1,0:T(8,128)(2,1)S(1)} %add_convert_fusion.1), channel_id=1, source_target_pairs={{2,0},{4,2},{6,4},{7,6},{5,7},{3,5},{1,3},{0,1},{10,8},{12,10},{14... | collective-permute-start | bytes 786440 | tf_op jit(solution)/shard_map/ppermute | solution.py:634

commit v13 on v12

--- a/solution.py
+++ b/solution.py
@@ -24,7 +24,7 @@
 TILE_COLS = 256
 PAIR = 2
 STATS = 16
-HALVES = 1
+HALVES = 2
 DEPTH_TILE = 1024
 WIDTH_TILE = 1024
 SLOTS = 3
@@ -301,7 +301,9 @@
         if with_new:
             fresh = []
             for tile in tiles:
-                scores = jnp.dot(new_key[...], queries[tile], preferred_element_type=jnp.float32)
+                scores = jnp.dot(
+                    new_key[...], queries[first_tile + tile], preferred_element_type=jnp.float32
+                )
                 key_index = lax.broadcasted_iota(jnp.int32, scores.shape, 0)
                 q_index = (first_tile + tile) * tile_q + lax.broadcasted_iota(jnp.int32, scores.shape, 1) % tile_q
                 fresh.append(jnp.where(key_index <= q_index, scores, MASKED))
@@ -312,14 +314,15 @@
         def _(doc):
             firsts = [first_ref[doc * n_chunks + chunk] for chunk in range(n_chunks)]
             lowest = functools.reduce(jnp.minimum, firsts)
-            reach = functools.reduce(jnp.maximum, firsts) + tokens - 1
-
-            def visit(masked):
+            highest = functools.reduce(jnp.maximum, firsts)
+            reach = highest + tokens - 1
+
+            def visit(masked, members):
                 found = []
                 for tile in tiles:
-                    extended = jnp.concatenate([queries[tile], one_row], axis=0)
+                    extended = jnp.concatenate([queries[first_tile + tile], one_row], axis=0)
                     parts = []
-                    for chunk in range(n_chunks):
+                    for chunk in members:
                         span = slice(chunk * tokens, (chunk + 1) * tokens)
                         keys = jnp.concatenate(
                             [chunks[chunk][0, doc], dead_ref[doc, span, :]], axis=1
@@ -336,16 +339,25 @@
                     update(tile, parts)
 
             start = first_tile * tile_q + pair * together * tile_q
-            live = lowest <= pos_ref[start + together * tile_q - 1]
-            whole = reach <= pos_ref[start]
-
-            @pl.when(live & whole)
+            first_here = pos_ref[start]
+            last_here = pos_ref[start + together * tile_q - 1]
+            whole = reach <= first_here
+            spread = jnp.logical_not(whole) & (highest <= last_here)
+            ragged = (lowest <= last_here) & (highest > last_here)
+
+            @pl.when(whole)
             def _():
-                visit(False)
-
-            @pl.when(live & jnp.logical_not(whole))
+                visit(False, range(n_chunks))
+
+            @pl.when(spread)
             def _():
-                visit(True)
+                visit(True, range(n_chunks))
+
+            for chunk in range(n_chunks):
+
+                @pl.when(ragged & (firsts[chunk] <= last_here))
+                def _():
+                    visit(True, [chunk])
 
         if not with_new:
             for tile in tiles:
@@ -384,46 +396,43 @@
         out_shape=[jax.ShapeDtypeStruct(*s) for s in outs],
         scratch_shapes=[pltpu.VMEM(*s) for s in scratch],
         compiler_params=megabytes(16),
-        cost_estimate=cost(4 * pairs * HD, 4 * DOCS * n_chunks * tokens * HD, pairs),
+        cost_estimate=cost(1, 1) if fresh else cost(4 * pairs * HD, 0, pairs),
         name="attend",
     )(*operands)
 
 
-def merge_kernel(*refs):
-    out_ref = refs[-1]
+def merge_kernel(top_a, total_a, mixed_a, *refs):
+    packs, out_ref = refs[:-1], refs[-1]
     scale = math.log2(math.e) / math.sqrt(HD)
-    for half in range(HALVES):
-        top_a, total_a, mixed_a, packed = refs[4 * half : 4 * half + 4]
-        n_tiles = top_a.shape[0]
-        tile_q = SEL // HALVES // n_tiles
-        for tile in range(n_tiles):
-            extra = packed[tile, HD:, :].astype(jnp.float32)
-            top_b = extra[0:1] + (extra[1:2] + extra[2:3])
-            total_b = extra[3:4] + (extra[4:5] + extra[5:6])
-            new = jnp.maximum(top_a[tile], top_b)
-            part_a = jnp.exp2((top_a[tile] - new) * scale)
-            part_b = jnp.exp2((top_b - new) * scale)
-            total = total_a[tile] * part_a + total_b * part_b
-            mixed = mixed_a[tile] * part_a + packed[tile, :HD, :].astype(jnp.float32) * part_b
-            finished = (mixed / total).T.astype(jnp.bfloat16)
-            here = slice((half * n_tiles + tile) * tile_q, (half * n_tiles + tile + 1) * tile_q)
-            for head in range(TILE_COLS // tile_q):
-                out_ref[here, head * HD : (head + 1) * HD] = finished[
-                    head * tile_q : (head + 1) * tile_q, :
-                ]
+    n_tiles = top_a.shape[0]
+    tile_q = SEL // n_tiles
+    for tile in range(n_tiles):
+        packed = packs[tile * len(packs) // n_tiles].at[tile % (n_tiles // len(packs))]
+        extra = packed[HD:, :].astype(jnp.float32)
+        top_b = extra[0:1] + (extra[1:2] + extra[2:3])
+        total_b = extra[3:4] + (extra[4:5] + extra[5:6])
+        new = jnp.maximum(top_a[tile], top_b)
+        part_a = jnp.exp2((top_a[tile] - new) * scale)
+        part_b = jnp.exp2((top_b - new) * scale)
+        total = total_a[tile] * part_a + total_b * part_b
+        mixed = mixed_a[tile] * part_a + packed[:HD, :].astype(jnp.float32) * part_b
+        finished = (mixed / total).T.astype(jnp.bfloat16)
+        for head in range(TILE_COLS // tile_q):
+            out_ref[tile * tile_q : (tile + 1) * tile_q, head * HD : (head + 1) * HD] = finished[
+                head * tile_q : (head + 1) * tile_q, :
+            ]
 
 
 def merge(mine, theirs):
-    n_tiles = mine[0][0].shape[0] * HALVES
+    n_tiles = mine[0].shape[0]
     shape = (SEL, TILE_COLS * n_tiles // SEL * HD)
-    operands = [a for state, packed in zip(mine, theirs) for a in (*state, packed)]
     return pl.pallas_call(
         merge_kernel,
         out_shape=jax.ShapeDtypeStruct(shape, jnp.bfloat16),
         compiler_params=megabytes(16),
         cost_estimate=cost(4 * math.prod(shape), 8 * math.prod(shape)),
         name="merge",
-    )(*operands)
+    )(*mine, *theirs)
 
 
 def out_kernel(n_blocks, first_col, place_ref, x_ref, w_ref, *refs):
@@ -512,7 +521,6 @@
         * lax.rsqrt(jnp.mean(widened * widened, axis=-1, keepdims=True) + EPSILON)
         * norm_gain
     ).astype(jnp.bfloat16)
-    normed, pool_cache = lax.optimization_barrier((normed, pool_cache))
     w_query, w_keyval, w_out = (
         pltpu.with_memory_space_constraint(w, pltpu.HBM) for w in (w_query, w_keyval, w_out)
     )
@@ -549,6 +557,12 @@
                 held["behind"].append(lax.ppermute(held["behind"][-1], "tp", back))
         first = streams[0]["before"]
         if k == 1:
+            heads_of = [held[side] for held in streams for side in ("before", "behind")]
+            pool_cache, *firsts = lax.optimization_barrier(
+                (pool_cache, *[held[-1] for held in heads_of])
+            )
+            for held, value in zip(heads_of, firsts):
+                held[-1] = value
             by_kind = pool_cache.transpose(0, 2, 1, 3)
             sources = [by_kind]
             for shift in range(1, req_size):
@@ -614,10 +628,15 @@
     their_queries = lax.ppermute(queries, "tp", across)
 
     metadata = (dead, first_pos, selected, q_pos, odd)
-    (packed,) = attend(chunks[1], *metadata, their_queries, 0, n_tiles, [])
-    theirs = lax.ppermute(packed, "tp", across)
+    share = n_tiles // min(HALVES, n_tiles)
+    theirs = [
+        lax.ppermute(
+            attend(chunks[1], *metadata, their_queries, first, share, [])[0], "tp", across
+        )
+        for first in range(n_tiles - share, -1, -share)
+    ][::-1]
     mine = attend(chunks[0], *metadata, queries, 0, n_tiles, [cosine, sine_part, *new])
-    attention = merge([mine], [theirs])
+    attention = merge(mine, theirs)
 
     finished = []
     for chunk in range(CHUNKS):

time: 199 us -> 199 us (level); the launches traced: 199 us -> 196 us
  Pallas kernels: 60.6 us -> 57.7 us
    ppermute x7, waiting for transfers between devices: 3.15 us -> 14.4 us  [per_device(): held['before'].append(lax.ppermute(held['before'][-1], 'tp', forth))]
    ppermute x1 -> x2, waiting for transfers between devices: 10.7 us -> 3.67 us  [per_device(): lax.ppermute(attend(chunks[1], *metadata, their_queries, first, share, []...]
    ppermute x7, waiting for transfers between devices: 12.9 us -> 8.98 us  [per_device(): held['behind'].append(lax.ppermute(held['behind'][-1], 'tp', back))]
    ppermute x1 -> x2, starting transfers between devices: 0.07 us -> 3.68 us  [per_device(): lax.ppermute(attend(chunks[1], *metadata, their_queries, first, share, []...]
    pallas_call x2 -> x3, Pallas kernels: 31.3 us -> 28.4 us  [attend(): pl.pallas_call(functools.partial(attend_kernel, n_chunks, bool(fresh), n_...]
    ppermute x7, starting transfers between devices: 4.95 us -> 2.26 us  [per_device(): held['behind'].append(lax.ppermute(held['behind'][-1], 'tp', back))]
  transfers between devices with their start and end apart: 39 -> 40, of which waited for: 15 -> 18; matrix products, arithmetic and copies ran while one was open for 3% -> 3% of each run, Pallas kernels for 28% -> 27%
where the time goes in v13:
time: 199 us; the launch traced here: 196 us
  waiting for transfers between devices  67.5 us (34%)
  Pallas kernels  57.7 us (29%)
  starting transfers between devices  55.4 us (28%)
  local copies, waits for them, and re-layouts  7.59 us (4%)
  other arithmetic  7.25 us (4%)
    pallas_call x3, Pallas kernels, attend(): pl.pallas_call(functools.partial(attend_kernel, n_chunks, bool(fresh), n_...  28.4 us
    ppermute x14, waiting for transfers between devices, per_device(): held = lax.ppermute(term.astype(jnp.bfloat16), 'tp', pairs)  22.9 us
    ppermute x1, waiting for transfers between devices, per_device(): their_queries = lax.ppermute(queries, 'tp', across)  17.6 us
    pallas_call x3, Pallas kernels, project(): pl.pallas_call(functools.partial(project_kernel, len(blocks), len(weights...  15.5 us
    ppermute x14, starting transfers between devices, per_device(): held = lax.ppermute(term.astype(jnp.bfloat16), 'tp', pairs)  14.5 us
    ppermute x7, waiting for transfers between devices, per_device(): held['before'].append(lax.ppermute(held['before'][-1], 'tp', forth))  14.4 us
    ppermute x7, starting transfers between devices, per_device(): held['before'].append(lax.ppermute(held['before'][-1], 'tp', forth))  13.1 us
    ppermute x1, starting transfers between devices, per_device(): their_queries = lax.ppermute(queries, 'tp', across)  11 us
  transfers between devices with their start and end apart: 40, of which 18 were waited for; matrix products, arithmetic and copies ran while one was open for 3% of the time, Pallas kernels for 27%

profile of v13, /device:TPU:0, one launch (start us, length us, event | category | flops | bytes accessed | tf_op | source)
XLA Modules:
  0.0 195.8 jit_solution(1755068071219846132)
XLA Ops:
  0.0 1.2 fusion
  1.3 1.2 fusion.2
  2.5 3.1 %collective-permute-start.2 = (bf16[32,4096]{1,0:T(8,128)(2,1)S(1)}, bf16[32,4096]{1,0:T(8,128)(2,1)S(1)}, u32[]{:S(2)}, u32[]{:S(2)}) collective-permute-start(bf16[32,4096]{1,0:T(8,128)(2,1)S(1)} %get-tuple-element.118.refs_0_), channel_id=1, source_target_pairs={{0,2},{2,4},{4,6},{6,7},{7,5},{5,3},{3,1},{1,0},{8,10},{10,12},{12... | collective-permute-start | bytes 786440 | tf_op jit(solution)/shard_map/ppermute | solution.py:555
  5.6 2.0 %collective-permute-start = (bf16[32,4096]{1,0:T(8,128)(2,1)S(1)}, bf16[32,4096]{1,0:T(8,128)(2,1)S(1)}, u32[]{:S(2)}, u32[]{:S(2)}) collective-permute-start(bf16[32,4096]{1,0:T(8,128)(2,1)S(1)} %get-tuple-element.158.refs_0_), channel_id=1, source_target_pairs={{0,2},{2,4},{4,6},{6,7},{7,5},{5,3},{3,1},{1,0},{8,10},{10,12},{12... | collective-permute-start | bytes 786440 | tf_op jit(solution)/shard_map/ppermute | solution.py:555
  7.7 5.0 %collective-permute-done.2.refs_1_ = bf16[32,4096]{1,0:T(8,128)(2,1)S(1)} collective-permute-done((bf16[32,4096]{1,0:T(8,128)(2,1)S(1)}, bf16[32,4096]{1,0:T(8,128)(2,1)S(1)}, u32[]{:S(2)}, u32[]{:S(2)}) %collective-permute-start.2) | collective-permute-done | bytes 262176 | tf_op jit(solution)/shard_map/ppermute | solution.py:555
  12.7 2.2 %collective-permute-done.3.refs_2_ = bf16[32,4096]{1,0:T(8,128)(2,1)S(1)} collective-permute-done((bf16[32,4096]{1,0:T(8,128)(2,1)S(1)}, bf16[32,4096]{1,0:T(8,128)(2,1)S(1)}, u32[]{:S(2)}, u32[]{:S(2)}) %collective-permute-start.3) | collective-permute-done | bytes 262176 | tf_op jit(solution)/shard_map/ppermute | solution.py:557
  14.9 2.6 %collective-permute-done.refs_1_ = bf16[32,4096]{1,0:T(8,128)(2,1)S(1)} collective-permute-done((bf16[32,4096]{1,0:T(8,128)(2,1)S(1)}, bf16[32,4096]{1,0:T(8,128)(2,1)S(1)}, u32[]{:S(2)}, u32[]{:S(2)}) %collective-permute-start) | collective-permute-done | bytes 262176 | tf_op jit(solution)/shard_map/ppermute | solution.py:555
  17.5 1.5 collective-permute-done.1.refs_2_
  19.0 5.5 %copy.16 = bf16[4,256,2,1024]{3,1,2,0:T(8,128)(2,1)} copy(bf16[4,256,2,1024]{3,2,1,0:T(2,128)(2,1)} %param.15) | data formatting | bytes 8388608 | tf_op jit(solution)/shard_map/optimization_barrier | solution.py:561
  24.8 1.3 compare_reduce_fusion
  26.4 0.5 fusion.3
  26.9 1.6 collective-permute-start.4
  28.6 0.7 dynamic-slice_bitcast_fusion.place_ref
  29.4 0.5 collective-permute-start.13
  30.1 0.5 broadcast.179
  30.6 0.7 reduce.3
  31.8 3.9 %collective-permute-done.4.refs_3_ = bf16[32,4096]{1,0:T(8,128)(2,1)S(1)} collective-permute-done((bf16[32,4096]{1,0:T(8,128)(2,1)S(1)}, bf16[32,4096]{1,0:T(8,128)(2,1)S(1)}, u32[]{:S(2)}, u32[]{:S(2)}) %collective-permute-start.4) | collective-permute-done | bytes 262176 | tf_op jit(solution)/shard_map/ppermute | solution.py:555
  35.7 0.6 broadcast_in_dim.23.refs_4_
  36.3 1.6 collective-permute-start.5
  37.9 1.6 collective-permute-start.12
  39.5 0.4 collective-permute-start.15
  40.0 4.2 %collective-permute-done.17.refs_4_ = bf16[32,4096]{1,0:T(8,128)(2,1)S(1)} collective-permute-done((bf16[32,4096]{1,0:T(8,128)(2,1)S(1)}, bf16[32,4096]{1,0:T(8,128)(2,1)S(1)}, u32[]{:S(2)}, u32[]{:S(2)}) %collective-permute-start.17) | collective-permute-done | bytes 262176 | tf_op jit(solution)/shard_map/ppermute | solution.py:557
  44.2 0.4 collective-permute-start.18
  44.7 3.3 %select_docs.1 = (bf16[2,4,256,128]{3,2,1,0:T(8,128)(2,1)S(1)}, bf16[2,4,256,128]{3,2,1,0:T(8,128)(2,1)S(1)}, bf16[2,4,256,128]{3,2,1,0:T(8,128)(2,1)S(1)}, bf16...) custom-call(s32[4]{0:T(128)S(1)} %get-tuple-element.86.place_ref, ...), custom_call_target="tpu_custom_call" | custom-call | bytes 8388608 | tf_op jit(solution)/shard_map/select_docs/pallas_call | solution.py:221
  47.9 1.6 collective-permute-start.19
  49.6 1.2 collective-permute-done.12.refs_3_
  50.8 1.6 collective-permute-start.14
  52.3 0.4 collective-permute-start.16
  52.8 1.6 collective-permute-start.7
  54.4 1.1 collective-permute-done.18.refs_6_
  55.6 1.6 collective-permute-done.19.refs_7_
  57.2 1.3 collective-permute-start.22
  58.5 6.4 %project.3 = (f32[256,256]{1,0:T(8,128)S(1)}, f32[256,1024]{1,0:T(8,128)S(1)}) custom-call(s32[8]{0:T(128)S(1)} %dynamic-slice_bitcast_fusion.place_ref, bf16[32,4096]{1,0:T(8,128)(2,1)S(1)} %get-tuple-element.158.refs_0_, bf16[32,4096]{1,0:T(8,128)(2,1)S(1)} %collective-permute-done.refs_1_, bf16[32,4096]{1,0:T(8,128)(2,1)S(1)} %collective-permute-done.1.refs_2_, ...), custom_call_target="tpu_custom_call" | custom-call | flops 2684354560 | bytes 12582912 | tf_op jit(solution)/shard_map/project/pallas_call | solution.py:173
  64.9 3.4 %project.4 = (bf16[256,128]{1,0:T(8,128)(2,1)S(1)}, bf16[256,128]{1,0:T(8,128)(2,1)S(1)}) custom-call(s32[8]{0:T(128)S(1)} %dynamic-slice_bitcast_fusion.place_ref, bf16[32,4096]{1,0:T(8,128)(2,1)S(1)} %get-tuple-element.118.refs_0_, bf16[32,4096]{1,0:T(8,128)(2,1)S(1)} %collective-permute-done.2.refs_1_, ...), custom_call_target="tpu_custom_call" | custom-call | flops 536870912 | bytes 4194304 | tf_op jit(solution)/shard_map/project/pallas_call | solution.py:173
  68.3 0.7 collective-permute-start.20
  69.0 3.6 %collective-permute-start.21 = (bf16[256,128]{1,0:T(8,128)(2,1)S(1)}, bf16[256,128]{1,0:T(8,128)(2,1)S(1)}, u32[]{:S(2)}, u32[]{:S(2)}) collective-permute-start(bf16[256,128]{1,0:T(8,128)(2,1)S(1)} %get-tuple-element.130), channel_id=1, source_target_pairs={{0,1},{1,3},{2,5},{3,7},{4,0},{5,2},{6,4},{7,6},{8,9},{9,11},{10,1... | collective-permute-start | bytes 196616 | tf_op jit(solution)/shard_map/ppermute | solution.py:603
  72.7 5.7 %project.5.refs_6_ = bf16[8,128,256]{2,1,0:T(8,128)(2,1)S(1)} custom-call(s32[8]{0:T(128)S(1)} %dynamic-slice_bitcast_fusion.place_ref, bf16[32,4096]{1,0:T(8,128)(2,1)S(1)} %get-tuple-element.118.refs_0_, bf16[32,4096]{1,0:T(8,128)(2,1)S(1)} %collective-permute-done.2.refs_1_, bf16[32,4096]{1,0:T(8,128)(2,1)S(1)} %collective-permute-done.3.refs_2_, ...), custom_call_target="tpu_custom_call" | custom-call | flops 2147483648 | bytes 10485760 | tf_op jit(solution)/shard_map/project/pallas_call | solution.py:173
  78.4 11.0 %collective-permute-start.23 = (bf16[8,128,256]{2,1,0:T(8,128)(2,1)S(1)}, bf16[8,128,256]{2,1,0:T(8,128)(2,1)S(1)}, u32[]{:S(2)}, u32[]{:S(2)}) collective-permute-start(bf16[8,128,256]{2,1,0:T(8,128)(2,1)S(1)} %project.5.refs_6_), channel_id=1, source_target_pairs={{0,4},{1,5},{2,6},{3,7},{4,0},{5,1},{6,2},{7,3},{8,12},{9,13},{10,... | collective-permute-start | bytes 1572872 | tf_op jit(solution)/shard_map/ppermute | solution.py:628
  89.4 1.6 collective-permute-start.11
  91.1 1.9 collective-permute-start.9
  92.9 17.6 %collective-permute-done.23.refs_6_ = bf16[8,128,256]{2,1,0:T(8,128)(2,1)S(1)} collective-permute-done((bf16[8,128,256]{2,1,0:T(8,128)(2,1)S(1)}, bf16[8,128,256]{2,1,0:T(8,128)(2,1)S(1)}, u32[]{:S(2)}, u32[]{:S(2)}) %collective-permute-start.23) | collective-permute-done | bytes 524320 | tf_op jit(solution)/shard_map/ppermute | solution.py:628
  110.5 8.9 %attend.5 = bf16[4,144,256]{2,1,0:T(8,128)(2,1)S(1)} custom-call(s32[16]{0:T(128)S(1)} %select_n.48.first_ref, s32[256]{0:T(256)S(1)} %bitcast.24, s32[1]{0:T(128)} %bitcast.6.odd_ref, bf16[2,4,256,128]{3,2,1,0:T(8,128)(2,1)S(1)} %get-tuple-element.137.refs_0_, bf16[2,4,256,128]{3,2,1,0:T(8,128)(2,1)S(1)} %collective-permute-done.22.refs_1_, ...), custom_call_target="tpu_custom_call" | custom-call | flops 1073741824 | tf_op jit(solution)/shard_map/attend/pallas_call | solution.py:390
  119.5 4.7 %attend.4 = bf16[4,144,256]{2,1,0:T(8,128)(2,1)S(1)} custom-call(s32[16]{0:T(128)S(1)} %select_n.48.first_ref, s32[256]{0:T(256)S(1)} %bitcast.25, s32[1]{0:T(128)} %bitcast.6.odd_ref, bf16[2,4,256,128]{3,2,1,0:T(8,128)(2,1)S(1)} %get-tuple-element.137.refs_0_, bf16[2,4,256,128]{3,2,1,0:T(8,128)(2,1)S(1)} %collective-permute-done.22.refs_1_, ...), custom_call_target="tpu_custom_call" | custom-call | flops 1073741824 | tf_op jit(solution)/shard_map/attend/pallas_call | solution.py:390
  124.2 3.6 %collective-permute-start.24 = (bf16[4,144,256]{2,1,0:T(8,128)(2,1)S(1)}, bf16[4,144,256]{2,1,0:T(8,128)(2,1)S(1)}, u32[]{:S(2)}, u32[]{:S(2)}) collective-permute-start(bf16[4,144,256]{2,1,0:T(8,128)(2,1)S(1)} %attend.4), channel_id=1, source_target_pairs={{0,4},{1,5},{2,6},{3,7},{4,0},{5,1},{6,2},{7,3},{8,12},{9,13},{10,... | collective-permute-start | bytes 884744 | tf_op jit(solution)/shard_map/ppermute | solution.py:633
  127.8 14.8 %attend.3 = (f32[8,1,256]{2,1,0:T(1,128)S(1)}, f32[8,1,256]{2,1,0:T(1,128)S(1)}, f32[8,128,256]{2,1,0:T(8,128)S(1)}) custom-call(s32[16]{0:T(128)S(1)} %select_n.48.first_ref, s32[256]{0:T(256)S(1)} %bitcast.26, s32[1]{0:T(128)} %bitcast.6.odd_ref, bf16[2,4,256,128]{3,2,1,0:T(8,128)(2,1)S(1)} %get-tuple-element.104.refs_0_, ...), custom_call_target="tpu_custom_call" | custom-call | flops 1 | bytes 1 | tf_op jit(solution)/shard_map/attend/pallas_call | solution.py:390
  142.6 3.7 %collective-permute-done.24.refs_0_ = bf16[4,144,256]{2,1,0:T(8,128)(2,1)S(1)} collective-permute-done((bf16[4,144,256]{2,1,0:T(8,128)(2,1)S(1)}, bf16[4,144,256]{2,1,0:T(8,128)(2,1)S(1)}, u32[]{:S(2)}, u32[]{:S(2)}) %collective-permute-start.24) | collective-permute-done | bytes 294944 | tf_op jit(solution)/shard_map/ppermute | solution.py:633
  146.3 0.4 merge.1.x_ref
  146.7 5.1 %project_out.2 = (f32[32,4096]{1,0:T(8,128)S(1)}, f32[32,4096]{1,0:T(8,128)S(1)}, f32[32,4096]{1,0:T(8,128)S(1)}, f32[32,4096]{1,0:T(8,128)S(1)}, f32[32,4096]{1...) custom-call(s32[8]{0:T(128)S(1)} %dynamic-slice_bitcast_fusion.place_ref, ...), custom_call_target="tpu_custom_call" | custom-call | flops 2147483648 | bytes 13107200 | tf_op jit(solution)/shard_map/project_out/pallas_call | solution.py:475
  151.9 2.1 %collective-permute-start.30 = (bf16[32,4096]{1,0:T(8,128)(2,1)S(1)}, bf16[32,4096]{1,0:T(8,128)(2,1)S(1)}, u32[]{:S(2)}, u32[]{:S(2)}) collective-permute-start(bf16[32,4096]{1,0:T(8,128)(2,1)S(1)} %convert_element_type.116), channel_id=1, source_target_pairs={{2,0},{4,2},{6,4},{7,6},{5,7},{3,5},{1,3},{0,1},{10,8},{12,10},{14... | collective-permute-start | bytes 786440 | tf_op jit(solution)/shard_map/ppermute | solution.py:653
  153.9 5.1 %project_out.3 = (f32[32,4096]{1,0:T(8,128)S(1)}, f32[32,4096]{1,0:T(8,128)S(1)}, f32[32,4096]{1,0:T(8,128)S(1)}, f32[32,4096]{1,0:T(8,128)S(1)}, f32[32,4096]{1...) custom-call(s32[8]{0:T(128)S(1)} %dynamic-slice_bitcast_fusion.place_ref, ...), custom_call_target="tpu_custom_call" | custom-call | flops 2147483648 | bytes 13107200 | tf_op jit(solution)/shard_map/project_out/pallas_call | solution.py:475
  159.1 2.0 %collective-permute-start.36 = (bf16[32,4096]{1,0:T(8,128)(2,1)S(1)}, bf16[32,4096]{1,0:T(8,128)(2,1)S(1)}, u32[]{:S(2)}, u32[]{:S(2)}) collective-permute-start(bf16[32,4096]{1,0:T(8,128)(2,1)S(1)} %get-tuple-element.156), channel_id=1, source_target_pairs={{2,0},{4,2},{6,4},{7,6},{5,7},{3,5},{1,3},{0,1},{10,8},{12,10},{14... | collective-permute-start | bytes 786440 | tf_op jit(solution)/shard_map/ppermute | solution.py:653
  161.4 2.0 %collective-permute-start.31 = (bf16[32,4096]{1,0:T(8,128)(2,1)S(1)}, bf16[32,4096]{1,0:T(8,128)(2,1)S(1)}, u32[]{:S(2)}, u32[]{:S(2)}) collective-permute-start(bf16[32,4096]{1,0:T(8,128)(2,1)S(1)} %add_convert_fusion.8), channel_id=1, source_target_pairs={{2,0},{4,2},{6,4},{7,6},{5,7},{3,5},{1,3},{0,1},{10,8},{12,10},{14... | collective-permute-start | bytes 786440 | tf_op jit(solution)/shard_map/ppermute | solution.py:653
  163.4 5.0 %collective-permute-done.33 = bf16[32,4096]{1,0:T(8,128)(2,1)S(1)} collective-permute-done((bf16[32,4096]{1,0:T(8,128)(2,1)S(1)}, bf16[32,4096]{1,0:T(8,128)(2,1)S(1)}, u32[]{:S(2)}, u32[]{:S(2)}) %collective-permute-start.33) | collective-permute-done | bytes 262176 | tf_op jit(solution)/shard_map/ppermute | solution.py:653
  168.5 2.1 %collective-permute-start.37 = (bf16[32,4096]{1,0:T(8,128)(2,1)S(1)}, bf16[32,4096]{1,0:T(8,128)(2,1)S(1)}, u32[]{:S(2)}, u32[]{:S(2)}) collective-permute-start(bf16[32,4096]{1,0:T(8,128)(2,1)S(1)} %add_convert_fusion.3), channel_id=1, source_target_pairs={{2,0},{4,2},{6,4},{7,6},{5,7},{3,5},{1,3},{0,1},{10,8},{12,10},{14... | collective-permute-start | bytes 786440 | tf_op jit(solution)/shard_map/ppermute | solution.py:653
  170.6 3.4 %collective-permute-done.27 = bf16[32,4096]{1,0:T(8,128)(2,1)S(1)} collective-permute-done((bf16[32,4096]{1,0:T(8,128)(2,1)S(1)}, bf16[32,4096]{1,0:T(8,128)(2,1)S(1)}, u32[]{:S(2)}, u32[]{:S(2)}) %collective-permute-start.27) | collective-permute-done | bytes 262176 | tf_op jit(solution)/shard_map/ppermute | solution.py:653
  174.1 2.1 %collective-permute-start.32 = (bf16[32,4096]{1,0:T(8,128)(2,1)S(1)}, bf16[32,4096]{1,0:T(8,128)(2,1)S(1)}, u32[]{:S(2)}, u32[]{:S(2)}) collective-permute-start(bf16[32,4096]{1,0:T(8,128)(2,1)S(1)} %add_convert_fusion.7), channel_id=1, source_target_pairs={{2,0},{4,2},{6,4},{7,6},{5,7},{3,5},{1,3},{0,1},{10,8},{12,10},{14... | collective-permute-start | bytes 786440 | tf_op jit(solution)/shard_map/ppermute | solution.py:653
  176.2 3.4 %collective-permute-done.34 = bf16[32,4096]{1,0:T(8,128)(2,1)S(1)} collective-permute-done((bf16[32,4096]{1,0:T(8,128)(2,1)S(1)}, bf16[32,4096]{1,0:T(8,128)(2,1)S(1)}, u32[]{:S(2)}, u32[]{:S(2)}) %collective-permute-start.34) | collective-permute-done | bytes 262176 | tf_op jit(solution)/shard_map/ppermute | solution.py:653
  179.8 2.1 %collective-permute-start.38 = (bf16[32,4096]{1,0:T(8,128)(2,1)S(1)}, bf16[32,4096]{1,0:T(8,128)(2,1)S(1)}, u32[]{:S(2)}, u32[]{:S(2)}) collective-permute-start(bf16[32,4096]{1,0:T(8,128)(2,1)S(1)} %add_convert_fusion.2), channel_id=1, source_target_pairs={{2,0},{4,2},{6,4},{7,6},{5,7},{3,5},{1,3},{0,1},{10,8},{12,10},{14... | collective-permute-start | bytes 786440 | tf_op jit(solution)/shard_map/ppermute | solution.py:653
  181.8 3.4 %collective-permute-done.28 = bf16[32,4096]{1,0:T(8,128)(2,1)S(1)} collective-permute-done((bf16[32,4096]{1,0:T(8,128)(2,1)S(1)}, bf16[32,4096]{1,0:T(8,128)(2,1)S(1)}, u32[]{:S(2)}, u32[]{:S(2)}) %collective-permute-start.28) | collective-permute-done | bytes 262176 | tf_op jit(solution)/shard_map/ppermute | solution.py:653
  185.3 3.1 %collective-permute-done.38 = bf16[32,4096]{1,0:T(8,128)(2,1)S(1)} collective-permute-done((bf16[32,4096]{1,0:T(8,128)(2,1)S(1)}, bf16[32,4096]{1,0:T(8,128)(2,1)S(1)}, u32[]{:S(2)}, u32[]{:S(2)}) %collective-permute-start.38) | collective-permute-done | bytes 262176 | tf_op jit(solution)/shard_map/ppermute | solution.py:653
  188.5 1.7 collective-permute-start.39
  190.2 3.8 %collective-permute-done.29 = bf16[32,4096]{1,0:T(8,128)(2,1)S(1)} collective-permute-done((bf16[32,4096]{1,0:T(8,128)(2,1)S(1)}, bf16[32,4096]{1,0:T(8,128)(2,1)S(1)}, u32[]{:S(2)}, u32[]{:S(2)}) %collective-permute-start.29) | collective-permute-done | bytes 262176 | tf_op jit(solution)/shard_map/ppermute | solution.py:653
  194.1 0.8 collective-permute-done.39
  195.0 0.8 pad_maximum_fusion
  (78 shorter events, 3.0 us)
Async XLA Ops:
  2.5 10.2 %collective-permute-start.2 = (bf16[32,4096]{1,0:T(8,128)(2,1)S(1)}, bf16[32,4096]{1,0:T(8,128)(2,1)S(1)}, u32[]{:S(2)}, u32[]{:S(2)}) collective-permute-start(bf16[32,4096]{1,0:T(8,128)(2,1)S(1)} %get-tuple-element.118.refs_0_), channel_id=1, source_target_pairs={{0,2},{2,4},{4,6},{6,7},{7,5},{5,3},{3,1},{1,0},{8,10},{10,12},{12... | collective-permute-start | bytes 786440 | tf_op jit(solution)/shard_map/ppermute | solution.py:555
  5.6 9.2 %collective-permute-start.3 = (bf16[32,4096]{1,0:T(8,128)(2,1)S(1)}, bf16[32,4096]{1,0:T(8,128)(2,1)S(1)}, u32[]{:S(2)}, u32[]{:S(2)}) collective-permute-start(bf16[32,4096]{1,0:T(8,128)(2,1)S(1)} %get-tuple-element.118.refs_0_), channel_id=1, source_target_pairs={{2,0},{4,2},{6,4},{7,6},{5,7},{3,5},{1,3},{0,1},{10,8},{12,10},{14... | collective-permute-start | bytes 786440 | tf_op jit(solution)/shard_map/ppermute | solution.py:557
  5.6 18.9 %copy-start.1 = (s32[1,4]{1,0:T(1,128)S(1)}, s32[1,4]{1,0:T(1,128)}, u32[]{:S(2)}) copy-start(s32[1,4]{1,0:T(1,128)} %param.17) | copy-start | bytes 52
  5.6 19.0 %copy-start = (s32[1,256]{1,0:T(1,128)S(1)}, s32[1,256]{1,0:T(1,128)}, u32[]{:S(2)}) copy-start(s32[1,256]{1,0:T(1,128)} %param.18) | copy-start | bytes 3076
  5.6 20.6 %copy-start.2 = (s32[4]{0:T(128)S(1)}, s32[4]{0:T(128)}, u32[]{:S(2)}) copy-start(s32[4]{0:T(128)} %param.16) | copy-start | bytes 52
  5.6 11.9 %collective-permute-start = (bf16[32,4096]{1,0:T(8,128)(2,1)S(1)}, bf16[32,4096]{1,0:T(8,128)(2,1)S(1)}, u32[]{:S(2)}, u32[]{:S(2)}) collective-permute-start(bf16[32,4096]{1,0:T(8,128)(2,1)S(1)} %get-tuple-element.158.refs_0_), channel_id=1, source_target_pairs={{0,2},{2,4},{4,6},{6,7},{7,5},{5,3},{3,1},{1,0},{8,10},{10,12},{12... | collective-permute-start | bytes 786440 | tf_op jit(solution)/shard_map/ppermute | solution.py:555
  7.7 11.4 %collective-permute-start.1 = (bf16[32,4096]{1,0:T(8,128)(2,1)S(1)}, bf16[32,4096]{1,0:T(8,128)(2,1)S(1)}, u32[]{:S(2)}, u32[]{:S(2)}) collective-permute-start(bf16[32,4096]{1,0:T(8,128)(2,1)S(1)} %get-tuple-element.158.refs_0_), channel_id=1, source_target_pairs={{2,0},{4,2},{6,4},{7,6},{5,7},{3,5},{1,3},{0,1},{10,8},{12,10},{14... | collective-permute-start | bytes 786440 | tf_op jit(solution)/shard_map/ppermute | solution.py:557
  24.5 20.2 %collective-permute-start.6 = (bf16[4,2,256,1024]{3,2,1,0:T(8,128)(2,1)}, bf16[4,2,256,1024]{3,2,1,0:T(8,128)(2,1)}, u32[]{:S(2)}, u32[]{:S(2)}) collective-permute-start(bf16[4,2,256,1024]{3,2,1,0:T(8,128)(2,1)} %bitcast.21.refs_0_), channel_id=1, source_target_pairs={{8,0},{0,8},{9,1},{1,9},{10,2},{2,10},{11,3},{3,11},{12,4},{4,12},... | collective-permute-start | bytes 12582920 | tf_op jit(solution)/shard_map/ppermute | solution.py:570
  26.9 8.8 %collective-permute-start.4 = (bf16[32,4096]{1,0:T(8,128)(2,1)S(1)}, bf16[32,4096]{1,0:T(8,128)(2,1)S(1)}, u32[]{:S(2)}, u32[]{:S(2)}) collective-permute-start(bf16[32,4096]{1,0:T(8,128)(2,1)S(1)} %collective-permute-done.refs_1_), channel_id=1, source_target_pairs={{0,2},{2,4},{4,6},{6,7},{7,5},{5,3},{3,1},{1,0},{8,10},{10,12},{12... | collective-permute-start | bytes 786440 | tf_op jit(solution)/shard_map/ppermute | solution.py:555
  29.4 10.1 %collective-permute-start.13 = (bf16[32,4096]{1,0:T(8,128)(2,1)S(1)}, bf16[32,4096]{1,0:T(8,128)(2,1)S(1)}, u32[]{:S(2)}, u32[]{:S(2)}) collective-permute-start(bf16[32,4096]{1,0:T(8,128)(2,1)S(1)} %collective-permute-done.3.refs_2_), channel_id=1, source_target_pairs={{2,0},{4,2},{6,4},{7,6},{5,7},{3,5},{1,3},{0,1},{10,8},{12,10},{14... | collective-permute-start | bytes 786440 | tf_op jit(solution)/shard_map/ppermute | solution.py:557
  31.4 12.8 %collective-permute-start.17 = (bf16[32,4096]{1,0:T(8,128)(2,1)S(1)}, bf16[32,4096]{1,0:T(8,128)(2,1)S(1)}, u32[]{:S(2)}, u32[]{:S(2)}) collective-permute-start(bf16[32,4096]{1,0:T(8,128)(2,1)S(1)} %collective-permute-done.1.refs_2_), channel_id=1, source_target_pairs={{2,0},{4,2},{6,4},{7,6},{5,7},{3,5},{1,3},{0,1},{10,8},{12,10},{14... | collective-permute-start | bytes 786440 | tf_op jit(solution)/shard_map/ppermute | solution.py:557
  36.3 11.6 %collective-permute-start.5 = (bf16[32,4096]{1,0:T(8,128)(2,1)S(1)}, bf16[32,4096]{1,0:T(8,128)(2,1)S(1)}, u32[]{:S(2)}, u32[]{:S(2)}) collective-permute-start(bf16[32,4096]{1,0:T(8,128)(2,1)S(1)} %collective-permute-done.4.refs_3_), channel_id=1, source_target_pairs={{0,2},{2,4},{4,6},{6,7},{7,5},{5,3},{3,1},{1,0},{8,10},{10,12},{12... | collective-permute-start | bytes 786440 | tf_op jit(solution)/shard_map/ppermute | solution.py:555
  37.9 12.8 %collective-permute-start.12 = (bf16[32,4096]{1,0:T(8,128)(2,1)S(1)}, bf16[32,4096]{1,0:T(8,128)(2,1)S(1)}, u32[]{:S(2)}, u32[]{:S(2)}) collective-permute-start(bf16[32,4096]{1,0:T(8,128)(2,1)S(1)} %collective-permute-done.2.refs_1_), channel_id=1, source_target_pairs={{0,2},{2,4},{4,6},{6,7},{7,5},{5,3},{3,1},{1,0},{8,10},{10,12},{12... | collective-permute-start | bytes 786440 | tf_op jit(solution)/shard_map/ppermute | solution.py:555
  39.5 12.8 %collective-permute-start.15 = (bf16[32,4096]{1,0:T(8,128)(2,1)S(1)}, bf16[32,4096]{1,0:T(8,128)(2,1)S(1)}, u32[]{:S(2)}, u32[]{:S(2)}) collective-permute-start(bf16[32,4096]{1,0:T(8,128)(2,1)S(1)} %collective-permute-done.13.refs_4_), channel_id=1, source_target_pairs={{2,0},{4,2},{6,4},{7,6},{5,7},{3,5},{1,3},{0,1},{10,8},{12,10},{14... | collective-permute-start | bytes 786440 | tf_op jit(solution)/shard_map/ppermute | solution.py:557
  44.2 11.2 %collective-permute-start.18 = (bf16[32,4096]{1,0:T(8,128)(2,1)S(1)}, bf16[32,4096]{1,0:T(8,128)(2,1)S(1)}, u32[]{:S(2)}, u32[]{:S(2)}) collective-permute-start(bf16[32,4096]{1,0:T(8,128)(2,1)S(1)} %collective-permute-done.17.refs_4_), channel_id=1, source_target_pairs={{2,0},{4,2},{6,4},{7,6},{5,7},{3,5},{1,3},{0,1},{10,8},{12,10},{14... | collective-permute-start | bytes 786440 | tf_op jit(solution)/shard_map/ppermute | solution.py:557
  47.9 9.3 %collective-permute-start.19 = (bf16[32,4096]{1,0:T(8,128)(2,1)S(1)}, bf16[32,4096]{1,0:T(8,128)(2,1)S(1)}, u32[]{:S(2)}, u32[]{:S(2)}) collective-permute-start(bf16[32,4096]{1,0:T(8,128)(2,1)S(1)} %collective-permute-done.5.refs_5_), channel_id=1, source_target_pairs={{0,2},{2,4},{4,6},{6,7},{7,5},{5,3},{3,1},{1,0},{8,10},{10,12},{12... | collective-permute-start | bytes 786440 | tf_op jit(solution)/shard_map/ppermute | solution.py:555
  50.8 14.1 %collective-permute-start.14 = (bf16[32,4096]{1,0:T(8,128)(2,1)S(1)}, bf16[32,4096]{1,0:T(8,128)(2,1)S(1)}, u32[]{:S(2)}, u32[]{:S(2)}) collective-permute-start(bf16[32,4096]{1,0:T(8,128)(2,1)S(1)} %collective-permute-done.12.refs_3_), channel_id=1, source_target_pairs={{0,2},{2,4},{4,6},{6,7},{7,5},{5,3},{3,1},{1,0},{8,10},{10,12},{12... | collective-permute-start | bytes 786440 | tf_op jit(solution)/shard_map/ppermute | solution.py:555
  52.3 12.5 %collective-permute-start.16 = (bf16[32,4096]{1,0:T(8,128)(2,1)S(1)}, bf16[32,4096]{1,0:T(8,128)(2,1)S(1)}, u32[]{:S(2)}, u32[]{:S(2)}) collective-permute-start(bf16[32,4096]{1,0:T(8,128)(2,1)S(1)} %collective-permute-done.15.refs_6_), channel_id=1, source_target_pairs={{2,0},{4,2},{6,4},{7,6},{5,7},{3,5},{1,3},{0,1},{10,8},{12,10},{14... | collective-permute-start | bytes 786440 | tf_op jit(solution)/shard_map/ppermute | solution.py:557
  52.8 36.6 %collective-permute-start.7 = (bf16[2,4,256,128]{3,2,1,0:T(8,128)(2,1)S(1)}, bf16[2,4,256,128]{3,2,1,0:T(8,128)(2,1)S(1)}, u32[]{:S(2)}, u32[]{:S(2)}) collective-permute-start(bf16[2,4,256,128]{3,2,1,0:T(8,128)(2,1)S(1)} %get-tuple-element.102), channel_id=1, source_target_pairs={{0,2},{1,3},{2,0},{3,1},{4,6},{5,7},{6,4},{7,5},{8,10},{9,11},{10,... | collective-permute-start | bytes 1572872 | tf_op jit(solution)/shard_map/ppermute | solution.py:619
  55.4 34.0 %collective-permute-start.8 = (bf16[2,4,256,128]{3,2,1,0:T(8,128)(2,1)S(1)}, bf16[2,4,256,128]{3,2,1,0:T(8,128)(2,1)S(1)}, u32[]{:S(2)}, u32[]{:S(2)}) collective-permute-start(bf16[2,4,256,128]{3,2,1,0:T(8,128)(2,1)S(1)} %get-tuple-element.103), channel_id=1, source_target_pairs={{0,3},{1,2},{2,1},{3,0},{4,7},{5,6},{6,5},{7,4},{8,11},{9,10},{10,... | collective-permute-start | bytes 1572872 | tf_op jit(solution)/shard_map/ppermute | solution.py:619
  57.2 35.7 %collective-permute-start.22 = (bf16[2,4,256,128]{3,2,1,0:T(8,128)(2,1)S(1)}, bf16[2,4,256,128]{3,2,1,0:T(8,128)(2,1)S(1)}, u32[]{:S(2)}, u32[]{:S(2)}) collective-permute-start(bf16[2,4,256,128]{3,2,1,0:T(8,128)(2,1)S(1)} %get-tuple-element.138), channel_id=1, source_target_pairs={{0,1},{1,0},{2,3},{3,2},{4,5},{5,4},{6,7},{7,6},{8,9},{9,8},{10,11... | collective-permute-start | bytes 1572872 | tf_op jit(solution)/shard_map/ppermute | solution.py:619
  68.3 10.0 %collective-permute-start.20 = (bf16[256,128]{1,0:T(8,128)(2,1)S(1)}, bf16[256,128]{1,0:T(8,128)(2,1)S(1)}, u32[]{:S(2)}, u32[]{:S(2)}) collective-permute-start(bf16[256,128]{1,0:T(8,128)(2,1)S(1)} %get-tuple-element.129), channel_id=1, source_target_pairs={{0,0},{1,2},{2,4},{3,6},{4,1},{5,3},{6,5},{7,7},{8,8},{9,10},{10,1... | collective-permute-start | bytes 196616 | tf_op jit(solution)/shard_map/ppermute | solution.py:603
  69.0 9.4 %collective-permute-start.21 = (bf16[256,128]{1,0:T(8,128)(2,1)S(1)}, bf16[256,128]{1,0:T(8,128)(2,1)S(1)}, u32[]{:S(2)}, u32[]{:S(2)}) collective-permute-start(bf16[256,128]{1,0:T(8,128)(2,1)S(1)} %get-tuple-element.130), channel_id=1, source_target_pairs={{0,1},{1,3},{2,5},{3,7},{4,0},{5,2},{6,4},{7,6},{8,9},{9,11},{10,1... | collective-permute-start | bytes 196616 | tf_op jit(solution)/shard_map/ppermute | solution.py:603
  78.4 32.1 %collective-permute-start.23 = (bf16[8,128,256]{2,1,0:T(8,128)(2,1)S(1)}, bf16[8,128,256]{2,1,0:T(8,128)(2,1)S(1)}, u32[]{:S(2)}, u32[]{:S(2)}) collective-permute-start(bf16[8,128,256]{2,1,0:T(8,128)(2,1)S(1)} %project.5.refs_6_), channel_id=1, source_target_pairs={{0,4},{1,5},{2,6},{3,7},{4,0},{5,1},{6,2},{7,3},{8,12},{9,13},{10,... | collective-permute-start | bytes 1572872 | tf_op jit(solution)/shard_map/ppermute | solution.py:628
  89.4 38.4 %collective-permute-start.10 = (bf16[2,4,256,128]{3,2,1,0:T(8,128)(2,1)S(1)}, bf16[2,4,256,128]{3,2,1,0:T(8,128)(2,1)S(1)}, u32[]{:S(2)}, u32[]{:S(2)}) collective-permute-start(bf16[2,4,256,128]{3,2,1,0:T(8,128)(2,1)S(1)} %get-tuple-element.106), channel_id=1, source_target_pairs={{0,2},{1,3},{2,0},{3,1},{4,6},{5,7},{6,4},{7,5},{8,10},{9,11},{10,... | collective-permute-start | bytes 1572872 | tf_op jit(solution)/shard_map/ppermute | solution.py:619
  89.4 38.4 %collective-permute-start.11 = (bf16[2,4,256,128]{3,2,1,0:T(8,128)(2,1)S(1)}, bf16[2,4,256,128]{3,2,1,0:T(8,128)(2,1)S(1)}, u32[]{:S(2)}, u32[]{:S(2)}) collective-permute-start(bf16[2,4,256,128]{3,2,1,0:T(8,128)(2,1)S(1)} %get-tuple-element.107), channel_id=1, source_target_pairs={{0,3},{1,2},{2,1},{3,0},{4,7},{5,6},{6,5},{7,4},{8,11},{9,10},{10,... | collective-permute-start | bytes 1572872 | tf_op jit(solution)/shard_map/ppermute | solution.py:619
  91.1 36.8 %collective-permute-start.9 = (bf16[2,4,256,128]{3,2,1,0:T(8,128)(2,1)S(1)}, bf16[2,4,256,128]{3,2,1,0:T(8,128)(2,1)S(1)}, u32[]{:S(2)}, u32[]{:S(2)}) collective-permute-start(bf16[2,4,256,128]{3,2,1,0:T(8,128)(2,1)S(1)} %get-tuple-element.105), channel_id=1, source_target_pairs={{0,1},{1,0},{2,3},{3,2},{4,5},{5,4},{6,7},{7,6},{8,9},{9,8},{10,11... | collective-permute-start | bytes 1572872 | tf_op jit(solution)/shard_map/ppermute | solution.py:619
  119.4 23.2 %collective-permute-start.25 = (bf16[4,144,256]{2,1,0:T(8,128)(2,1)S(1)}, bf16[4,144,256]{2,1,0:T(8,128)(2,1)S(1)}, u32[]{:S(2)}, u32[]{:S(2)}) collective-permute-start(bf16[4,144,256]{2,1,0:T(8,128)(2,1)S(1)} %attend.5), channel_id=1, source_target_pairs={{0,4},{1,5},{2,6},{3,7},{4,0},{5,1},{6,2},{7,3},{8,12},{9,13},{10,... | collective-permute-start | bytes 884744 | tf_op jit(solution)/shard_map/ppermute | solution.py:633
  124.2 22.1 %collective-permute-start.24 = (bf16[4,144,256]{2,1,0:T(8,128)(2,1)S(1)}, bf16[4,144,256]{2,1,0:T(8,128)(2,1)S(1)}, u32[]{:S(2)}, u32[]{:S(2)}) collective-permute-start(bf16[4,144,256]{2,1,0:T(8,128)(2,1)S(1)} %attend.4), channel_id=1, source_target_pairs={{0,4},{1,5},{2,6},{3,7},{4,0},{5,1},{6,2},{7,3},{8,12},{9,13},{10,... | collective-permute-start | bytes 884744 | tf_op jit(solution)/shard_map/ppermute | solution.py:633
  151.8 9.4 %collective-permute-start.26 = (bf16[32,4096]{1,0:T(8,128)(2,1)S(1)}, bf16[32,4096]{1,0:T(8,128)(2,1)S(1)}, u32[]{:S(2)}, u32[]{:S(2)}) collective-permute-start(bf16[32,4096]{1,0:T(8,128)(2,1)S(1)} %get-tuple-element.145), channel_id=1, source_target_pairs={{0,2},{2,4},{4,6},{6,7},{7,5},{5,3},{3,1},{1,0},{8,10},{10,12},{12... | collective-permute-start | bytes 786440 | tf_op jit(solution)/shard_map/ppermute | solution.py:653
  151.9 9.4 %collective-permute-start.30 = (bf16[32,4096]{1,0:T(8,128)(2,1)S(1)}, bf16[32,4096]{1,0:T(8,128)(2,1)S(1)}, u32[]{:S(2)}, u32[]{:S(2)}) collective-permute-start(bf16[32,4096]{1,0:T(8,128)(2,1)S(1)} %convert_element_type.116), channel_id=1, source_target_pairs={{2,0},{4,2},{6,4},{7,6},{5,7},{3,5},{1,3},{0,1},{10,8},{12,10},{14... | collective-permute-start | bytes 786440 | tf_op jit(solution)/shard_map/ppermute | solution.py:653
  159.1 9.3 %collective-permute-start.33 = (bf16[32,4096]{1,0:T(8,128)(2,1)S(1)}, bf16[32,4096]{1,0:T(8,128)(2,1)S(1)}, u32[]{:S(2)}, u32[]{:S(2)}) collective-permute-start(bf16[32,4096]{1,0:T(8,128)(2,1)S(1)} %convert_element_type.123), channel_id=1, source_target_pairs={{0,2},{2,4},{4,6},{6,7},{7,5},{5,3},{3,1},{1,0},{8,10},{10,12},{12... | collective-permute-start | bytes 786440 | tf_op jit(solution)/shard_map/ppermute | solution.py:653
  159.1 9.3 %collective-permute-start.36 = (bf16[32,4096]{1,0:T(8,128)(2,1)S(1)}, bf16[32,4096]{1,0:T(8,128)(2,1)S(1)}, u32[]{:S(2)}, u32[]{:S(2)}) collective-permute-start(bf16[32,4096]{1,0:T(8,128)(2,1)S(1)} %get-tuple-element.156), channel_id=1, source_target_pairs={{2,0},{4,2},{6,4},{7,6},{5,7},{3,5},{1,3},{0,1},{10,8},{12,10},{14... | collective-permute-start | bytes 786440 | tf_op jit(solution)/shard_map/ppermute | solution.py:653
  161.2 12.8 %collective-permute-start.27 = (bf16[32,4096]{1,0:T(8,128)(2,1)S(1)}, bf16[32,4096]{1,0:T(8,128)(2,1)S(1)}, u32[]{:S(2)}, u32[]{:S(2)}) collective-permute-start(bf16[32,4096]{1,0:T(8,128)(2,1)S(1)} %add_convert_fusion.11), channel_id=1, source_target_pairs={{0,2},{2,4},{4,6},{6,7},{7,5},{5,3},{3,1},{1,0},{8,10},{10,12},{12... | collective-permute-start | bytes 786440 | tf_op jit(solution)/shard_map/ppermute | solution.py:653
  161.4 12.7 %collective-permute-start.31 = (bf16[32,4096]{1,0:T(8,128)(2,1)S(1)}, bf16[32,4096]{1,0:T(8,128)(2,1)S(1)}, u32[]{:S(2)}, u32[]{:S(2)}) collective-permute-start(bf16[32,4096]{1,0:T(8,128)(2,1)S(1)} %add_convert_fusion.8), channel_id=1, source_target_pairs={{2,0},{4,2},{6,4},{7,6},{5,7},{3,5},{1,3},{0,1},{10,8},{12,10},{14... | collective-permute-start | bytes 786440 | tf_op jit(solution)/shard_map/ppermute | solution.py:653
  168.4 11.2 %collective-permute-start.34 = (bf16[32,4096]{1,0:T(8,128)(2,1)S(1)}, bf16[32,4096]{1,0:T(8,128)(2,1)S(1)}, u32[]{:S(2)}, u32[]{:S(2)}) collective-permute-start(bf16[32,4096]{1,0:T(8,128)(2,1)S(1)} %add_convert_fusion.5), channel_id=1, source_target_pairs={{0,2},{2,4},{4,6},{6,7},{7,5},{5,3},{3,1},{1,0},{8,10},{10,12},{12... | collective-permute-start | bytes 786440 | tf_op jit(solution)/shard_map/ppermute | solution.py:653
  168.5 11.2 %collective-permute-start.37 = (bf16[32,4096]{1,0:T(8,128)(2,1)S(1)}, bf16[32,4096]{1,0:T(8,128)(2,1)S(1)}, u32[]{:S(2)}, u32[]{:S(2)}) collective-permute-start(bf16[32,4096]{1,0:T(8,128)(2,1)S(1)} %add_convert_fusion.3), channel_id=1, source_target_pairs={{2,0},{4,2},{6,4},{7,6},{5,7},{3,5},{1,3},{0,1},{10,8},{12,10},{14... | collective-permute-start | bytes 786440 | tf_op jit(solution)/shard_map/ppermute | solution.py:653
  174.0 11.2 %collective-permute-start.28 = (bf16[32,4096]{1,0:T(8,128)(2,1)S(1)}, bf16[32,4096]{1,0:T(8,128)(2,1)S(1)}, u32[]{:S(2)}, u32[]{:S(2)}) collective-permute-start(bf16[32,4096]{1,0:T(8,128)(2,1)S(1)} %add_convert_fusion.10), channel_id=1, source_target_pairs={{0,2},{2,4},{4,6},{6,7},{7,5},{5,3},{3,1},{1,0},{8,10},{10,12},{12... | collective-permute-start | bytes 786440 | tf_op jit(solution)/shard_map/ppermute | solution.py:653
  174.1 16.1 %collective-permute-start.32 = (bf16[32,4096]{1,0:T(8,128)(2,1)S(1)}, bf16[32,4096]{1,0:T(8,128)(2,1)S(1)}, u32[]{:S(2)}, u32[]{:S(2)}) collective-permute-start(bf16[32,4096]{1,0:T(8,128)(2,1)S(1)} %add_convert_fusion.7), channel_id=1, source_target_pairs={{2,0},{4,2},{6,4},{7,6},{5,7},{3,5},{1,3},{0,1},{10,8},{12,10},{14... | collective-permute-start | bytes 786440 | tf_op jit(solution)/shard_map/ppermute | solution.py:653
  179.6 14.5 %collective-permute-start.35 = (bf16[32,4096]{1,0:T(8,128)(2,1)S(1)}, bf16[32,4096]{1,0:T(8,128)(2,1)S(1)}, u32[]{:S(2)}, u32[]{:S(2)}) collective-permute-start(bf16[32,4096]{1,0:T(8,128)(2,1)S(1)} %add_convert_fusion.4), channel_id=1, source_target_pairs={{0,2},{2,4},{4,6},{6,7},{7,5},{5,3},{3,1},{1,0},{8,10},{10,12},{12... | collective-permute-start | bytes 786440 | tf_op jit(solution)/shard_map/ppermute | solution.py:653
  179.8 8.7 %collective-permute-start.38 = (bf16[32,4096]{1,0:T(8,128)(2,1)S(1)}, bf16[32,4096]{1,0:T(8,128)(2,1)S(1)}, u32[]{:S(2)}, u32[]{:S(2)}) collective-permute-start(bf16[32,4096]{1,0:T(8,128)(2,1)S(1)} %add_convert_fusion.2), channel_id=1, source_target_pairs={{2,0},{4,2},{6,4},{7,6},{5,7},{3,5},{1,3},{0,1},{10,8},{12,10},{14... | collective-permute-start | bytes 786440 | tf_op jit(solution)/shard_map/ppermute | solution.py:653
  185.2 8.8 %collective-permute-start.29 = (bf16[32,4096]{1,0:T(8,128)(2,1)S(1)}, bf16[32,4096]{1,0:T(8,128)(2,1)S(1)}, u32[]{:S(2)}, u32[]{:S(2)}) collective-permute-start(bf16[32,4096]{1,0:T(8,128)(2,1)S(1)} %add_convert_fusion.9), channel_id=1, source_target_pairs={{0,2},{2,4},{4,6},{6,7},{7,5},{5,3},{3,1},{1,0},{8,10},{10,12},{12... | collective-permute-start | bytes 786440 | tf_op jit(solution)/shard_map/ppermute | solution.py:653
  188.5 6.4 %collective-permute-start.39 = (bf16[32,4096]{1,0:T(8,128)(2,1)S(1)}, bf16[32,4096]{1,0:T(8,128)(2,1)S(1)}, u32[]{:S(2)}, u32[]{:S(2)}) collective-permute-start(bf16[32,4096]{1,0:T(8,128)(2,1)S(1)} %add_convert_fusion.1), channel_id=1, source_target_pairs={{2,0},{4,2},{6,4},{7,6},{5,7},{3,5},{1,3},{0,1},{10,8},{12,10},{14... | collective-permute-start | bytes 786440 | tf_op jit(solution)/shard_map/ppermute | solution.py:653

commit v14 on v13

--- a/solution.py
+++ b/solution.py
@@ -84,18 +84,18 @@
     return start, wait
 
 
-def project_kernel(n_blocks, n_weights, n_tables, chunk, is_last, place_ref, *refs):
+def project_kernel(n_blocks, chunk, is_last, split, place_ref, *refs):
     refs = list(refs)
     take = lambda count: [refs.pop(0) for _ in range(count)]
-    blocks, weights = take(n_blocks), take(n_weights)
-    prev = take(n_weights) if chunk else None
+    blocks, weights = take(n_blocks), take(2)
+    prev = take(2) if chunk else None
     if is_last:
-        n_outs = len(refs) - 4 - n_tables
-        tables, outs, (total, natural) = take(n_tables), take(n_outs), take(2)
-        out, totals = outs[0], [total]
+        cos_ref, sin_ref, side_ref = take(3)
+        out_kv, (out_q,) = take(2 if split else 1), take(1)
+        totals, (natural_kv, natural_q) = take(2), take(2)
     else:
-        totals = take(n_weights)
-    buffers, sems = take(n_weights), refs[0]
+        totals = take(2)
+    buffers, sems = take(2), refs[0]
     tile = buffers[0].shape[1]
     depth = blocks[0].shape[1]
     count = depth // tile
@@ -124,70 +124,64 @@
         for block in range(SEL // height):
             here = slice(block * height, (block + 1) * height)
             there = pl.ds(pl.multiple_of(place_ref[block] * height, height), height)
-            natural[there, :] = totals[0][here, :]
-        if len(outs) == 2:
-            side_ref = tables[0]
+            natural_kv[there, :] = totals[0][here, :]
+            natural_q[there, :] = totals[1][here, :]
+        if split:
             for side in range(2):
 
                 @pl.when(side_ref[0] == side)
                 def _():
-                    outs[1 - side][...] = natural[:, :HD].astype(out.dtype)
-                    outs[side][...] = natural[:, HD:].astype(out.dtype)
-
-            return
-        if not tables:
-            out[...] = natural[...].astype(out.dtype)
-            return
-        cos_ref, sin_ref = tables
-        heads_here = natural.shape[1] // HD
+                    out_kv[1 - side][...] = natural_kv[:, :HD].astype(jnp.bfloat16)
+                    out_kv[side][...] = natural_kv[:, HD:].astype(jnp.bfloat16)
+
+        else:
+            out_kv[0][...] = natural_kv[...].astype(jnp.bfloat16)
+        heads_here = natural_q.shape[1] // HD
         tile_q = TILE_COLS // heads_here
         for index in range(SEL // tile_q):
             here = slice(index * tile_q, (index + 1) * tile_q)
             stacked = jnp.concatenate(
                 [
                     rotate(
-                        natural[here, head * HD : (head + 1) * HD], cos_ref[here, :], sin_ref[here, :]
+                        natural_q[here, head * HD : (head + 1) * HD], cos_ref[here, :], sin_ref[here, :]
                     )
                     for head in range(heads_here)
                 ],
                 axis=0,
             )
-            out[index] = stacked.T.astype(out.dtype)
-
-
-def project(place, blocks, weights, prev, chunk, tables=(), side=()):
+            out_q[index] = stacked.T.astype(jnp.bfloat16)
+
+
+def project(place, blocks, weights, prev, chunk, tables, side, split):
     depth = blocks[0].shape[1]
     widths = [w.shape[1] for w in weights]
     tile = min(DEPTH_TILE, depth)
     is_last = chunk + 1 == CHUNKS
+    smem = pl.BlockSpec(memory_space=pltpu.SMEM)
     vmem = pl.BlockSpec(memory_space=pltpu.VMEM)
     hbm = pl.BlockSpec(memory_space=pltpu.HBM)
     totals = [((SEL, width), jnp.float32) for width in widths]
+    operands, specs = [place, *blocks, *weights, *prev], [smem] + [vmem] * len(blocks) + [hbm] * 2
+    specs += [vmem] * len(prev)
+    outs, scratch = totals, []
     if is_last:
-        shape = (SEL * widths[0] // (HD * TILE_COLS), HD, TILE_COLS) if tables else (SEL, widths[0])
-        outs, scratch = [(shape, jnp.bfloat16)], totals * 2
-        if side:
-            outs = [((SEL, HD), jnp.bfloat16)] * 2
-    else:
-        outs, scratch = totals, []
+        operands += [*tables, side]
+        specs += [vmem] * 2 + [smem]
+        outs = [(SEL, HD)] * 2 if split else [(SEL, widths[0])]
+        outs = outs + [(SEL * widths[1] // (HD * TILE_COLS), HD, TILE_COLS)]
+        outs, scratch = [(shape, jnp.bfloat16) for shape in outs], totals * 2
     return pl.pallas_call(
-        functools.partial(
-            project_kernel, len(blocks), len(weights), len(tables) + len(side), chunk, is_last
-        ),
-        in_specs=[pl.BlockSpec(memory_space=pltpu.SMEM)]
-        + [vmem] * len(blocks)
-        + [hbm] * len(weights)
-        + [vmem] * (len(prev) + len(tables))
-        + [pl.BlockSpec(memory_space=pltpu.SMEM)] * len(side),
+        functools.partial(project_kernel, len(blocks), chunk, is_last, split),
+        in_specs=specs,
         out_specs=[vmem] * len(outs),
         out_shape=[jax.ShapeDtypeStruct(*o) for o in outs],
         scratch_shapes=[pltpu.VMEM(*x) for x in scratch]
         + [pltpu.VMEM((SLOTS, tile, width), jnp.bfloat16) for width in widths]
-        + [pltpu.SemaphoreType.DMA((len(weights) * CUTS, SLOTS))],
+        + [pltpu.SemaphoreType.DMA((2 * CUTS, SLOTS))],
         compiler_params=megabytes(16),
         cost_estimate=cost(2 * SEL * depth * sum(widths), 2 * depth * (sum(widths) + SEL)),
         name="project",
-    )(place, *blocks, *weights, *prev, *tables, *side)
+    )(*operands)
 
 
 def select_kernel(n_dest, n_src, place_ref, slot_ref, head_ref, *refs):
@@ -521,6 +515,7 @@
         * lax.rsqrt(jnp.mean(widened * widened, axis=-1, keepdims=True) + EPSILON)
         * norm_gain
     ).astype(jnp.bfloat16)
+    normed, pool_cache = lax.optimization_barrier((normed, pool_cache))
     w_query, w_keyval, w_out = (
         pltpu.with_memory_space_constraint(w, pltpu.HBM) for w in (w_query, w_keyval, w_out)
     )
@@ -557,12 +552,6 @@
                 held["behind"].append(lax.ppermute(held["behind"][-1], "tp", back))
         first = streams[0]["before"]
         if k == 1:
-            heads_of = [held[side] for held in streams for side in ("before", "behind")]
-            pool_cache, *firsts = lax.optimization_barrier(
-                (pool_cache, *[held[-1] for held in heads_of])
-            )
-            for held, value in zip(heads_of, firsts):
-                held[-1] = value
             by_kind = pool_cache.transpose(0, 2, 1, 3)
             sources = [by_kind]
             for shift in range(1, req_size):
@@ -592,42 +581,41 @@
         blocks.append(held["behind" if chunk % 2 else "before"][far])
         if rows % 16:
             blocks = [jnp.concatenate(blocks, axis=0)]
-        if chunk + 1 < CHUNKS:
-            sums = project(place, blocks, weights, sums, chunk)
+        sums = project(
+            place, blocks, weights, sums, chunk, (cosine, sine_part), side, tp_size == KVH
+        )
     across = [(i, i ^ middle) for i in range(tp_size)]
+    *keyval, queries = sums
+    their_queries = lax.ppermute(queries, "tp", across)
     if tp_size == KVH:
-        first, second = project(place, blocks, weights[:1], sums[:1], CHUNKS - 1, (), (side,))
-        first, second, *blocks = lax.optimization_barrier((first, second, *blocks))
+        first, second = keyval
         keys_to_even = [(i, 2 * i if i < middle else 2 * (i - middle) + 1) for i in range(tp_size)]
         keys_to_odd = [(i, 2 * i + 1 if i < middle else 2 * (i - middle)) for i in range(tp_size)]
         new = [lax.ppermute(first, "tp", keys_to_even), lax.ppermute(second, "tp", keys_to_odd)]
     else:
-        (keyval,) = project(place, blocks, weights[:1], sums[:1], CHUNKS - 1)
-        everyone = lax.all_gather(keyval, "tp", axis=1, tiled=True)
+        everyone = lax.all_gather(keyval[0], "tp", axis=1, tiled=True)
         my_head = me * KVH // tp_size
         new = [
             lax.dynamic_slice_in_dim(everyone, (kind * KVH + my_head) * HD, HD, axis=1)
             for kind in range(2)
         ]
-    (queries,) = project(
-        place, blocks, weights[1:], sums[1:], CHUNKS - 1, (cosine, sine_part)
-    )
-    queries, new = lax.optimization_barrier((queries, new))
 
     def exchange(kept):
         got = {
             j: lax.ppermute(kept[j], "tp", [(i, i ^ j) for i in range(tp_size)])
-            for j in range(middle - 1, 0, -1)
+            for j in range(1, middle)
         }
         return [kept[0]] + [got[j] for j in range(1, middle)]
 
-    own, partners = sent[:middle], exchange(sent[middle:])
-    own, *partners[2:] = lax.optimization_barrier((own, *partners[2:]))
+    kept = list(sent[middle:])
+    kept[-1], queries = lax.optimization_barrier((kept[-1], queries))
+    own, partners = sent[:middle], exchange(kept)
+    own, *partners[1:-1] = lax.optimization_barrier((own, *partners[1:-1]))
     chunks = [exchange(own), partners]
     n_tiles = queries.shape[0]
-    their_queries = lax.ppermute(queries, "tp", across)
 
     metadata = (dead, first_pos, selected, q_pos, odd)
+    their_queries, new = lax.optimization_barrier((their_queries, new))
     share = n_tiles // min(HALVES, n_tiles)
     theirs = [
         lax.ppermute(

time: 199 us -> 191 us (0.960)
  waiting for transfers between devices: 67.5 us -> 48.5 us
  starting transfers between devices: 55.4 us -> 67.4 us
    ppermute x6, starting transfers between devices: 6.49 us -> 25.3 us  [exchange(): lax.ppermute(kept[j], 'tp', [(i, i ^ j) for i in range(tp_size)])]
    ppermute x1, waiting for transfers between devices: 17.6 us -> 0.01 us  [per_device(): their_queries = lax.ppermute(queries, 'tp', across)]
    ppermute x7, waiting for transfers between devices: 14.4 us -> 3.17 us  [per_device(): held['before'].append(lax.ppermute(held['before'][-1], 'tp', forth))]
    ppermute x6, waiting for transfers between devices: 0.02 us -> 9.39 us  [exchange(): lax.ppermute(kept[j], 'tp', [(i, i ^ j) for i in range(tp_size)])]
    ppermute x1, starting transfers between devices: 11 us -> 2.58 us  [per_device(): their_queries = lax.ppermute(queries, 'tp', across)]
    ppermute x7, waiting for transfers between devices: 8.98 us -> 13.9 us  [per_device(): held['behind'].append(lax.ppermute(held['behind'][-1], 'tp', back))]
    ppermute x2, waiting for transfers between devices: 3.67 us -> 0.01 us  [per_device(): lax.ppermute(attend(chunks[1], *metadata, their_queries, first, share, []...]
    ppermute x7, starting transfers between devices: 2.26 us -> 4.95 us  [per_device(): held['behind'].append(lax.ppermute(held['behind'][-1], 'tp', back))]
  transfers between devices with their start and end apart: 40 -> 40, of which waited for: 18 -> 15; matrix products, arithmetic and copies ran while one was open for 3% -> 3% of each run, Pallas kernels for 27% -> 28%
where the time goes in v14:
time: 191 us; the launch traced here: 189 us
  starting transfers between devices  67.4 us (35%)
  Pallas kernels  57.7 us (30%)
  waiting for transfers between devices  48.5 us (25%)
  local copies, waits for them, and re-layouts  7.61 us (4%)
  other arithmetic  7.25 us (4%)
    pallas_call x3, Pallas kernels, attend(): pl.pallas_call(functools.partial(attend_kernel, n_chunks, bool(fresh), n_...  30.3 us
    ppermute x6, starting transfers between devices, exchange(): lax.ppermute(kept[j], 'tp', [(i, i ^ j) for i in range(tp_size)])  25.3 us
    ppermute x14, waiting for transfers between devices, per_device(): held = lax.ppermute(term.astype(jnp.bfloat16), 'tp', pairs)  22 us
    ppermute x14, starting transfers between devices, per_device(): held = lax.ppermute(term.astype(jnp.bfloat16), 'tp', pairs)  15.6 us
    ppermute x7, waiting for transfers between devices, per_device(): held['behind'].append(lax.ppermute(held['behind'][-1], 'tp', back))  13.9 us
    pallas_call x2, Pallas kernels, project(): pl.pallas_call(functools.partial(project_kernel, len(blocks), chunk, is_l...  13.6 us
    ppermute x7, starting transfers between devices, per_device(): held['before'].append(lax.ppermute(held['before'][-1], 'tp', forth))  11.5 us
    pallas_call x2, Pallas kernels, project_out(): pl.pallas_call(functools.partial(out_kernel, n_blocks, chunk * width), in...  10.2 us
  transfers between devices with their start and end apart: 40, of which 15 were waited for; matrix products, arithmetic and copies ran while one was open for 3% of the time, Pallas kernels for 28%

profile of v14, /device:TPU:0, one launch (start us, length us, event | category | flops | bytes accessed | tf_op | source)
XLA Modules:
  0.0 188.9 jit_solution(4474523441779348035)
XLA Ops:
  0.0 1.2 fusion
  1.3 1.2 fusion.2
  2.5 5.5 %copy.16 = bf16[4,256,2,1024]{3,1,2,0:T(8,128)(2,1)} copy(bf16[4,256,2,1024]{3,2,1,0:T(2,128)(2,1)} %param.15) | data formatting | bytes 8388608 | tf_op jit(solution)/shard_map/optimization_barrier | solution.py:518
  8.0 0.5 collective-permute-start.3
  8.5 2.6 %collective-permute-start = (bf16[32,4096]{1,0:T(8,128)(2,1)S(1)}, bf16[32,4096]{1,0:T(8,128)(2,1)S(1)}, u32[]{:S(2)}, u32[]{:S(2)}) collective-permute-start(bf16[32,4096]{1,0:T(8,128)(2,1)S(1)} %get-tuple-element.138.refs_0_), channel_id=1, source_target_pairs={{0,2},{2,4},{4,6},{6,7},{7,5},{5,3},{3,1},{1,0},{8,10},{10,12},{12... | collective-permute-start | bytes 786440 | tf_op jit(solution)/shard_map/ppermute | solution.py:550
  11.2 2.0 %collective-permute-start.10 = (bf16[32,4096]{1,0:T(8,128)(2,1)S(1)}, bf16[32,4096]{1,0:T(8,128)(2,1)S(1)}, u32[]{:S(2)}, u32[]{:S(2)}) collective-permute-start(bf16[32,4096]{1,0:T(8,128)(2,1)S(1)} %get-tuple-element.137.refs_0_), channel_id=1, source_target_pairs={{2,0},{4,2},{6,4},{7,6},{5,7},{3,5},{1,3},{0,1},{10,8},{12,10},{14... | collective-permute-start | bytes 786440 | tf_op jit(solution)/shard_map/ppermute | solution.py:552
  13.6 1.3 compare_reduce_fusion
  15.1 0.5 fusion.3
  15.7 2.6 %collective-permute-done.refs_1_ = bf16[32,4096]{1,0:T(8,128)(2,1)S(1)} collective-permute-done((bf16[32,4096]{1,0:T(8,128)(2,1)S(1)}, bf16[32,4096]{1,0:T(8,128)(2,1)S(1)}, u32[]{:S(2)}, u32[]{:S(2)}) %collective-permute-start) | collective-permute-done | bytes 262176 | tf_op jit(solution)/shard_map/ppermute | solution.py:550
  18.3 2.0 %collective-permute-start.1 = (bf16[32,4096]{1,0:T(8,128)(2,1)S(1)}, bf16[32,4096]{1,0:T(8,128)(2,1)S(1)}, u32[]{:S(2)}, u32[]{:S(2)}) collective-permute-start(bf16[32,4096]{1,0:T(8,128)(2,1)S(1)} %collective-permute-done.refs_1_), channel_id=1, source_target_pairs={{0,2},{2,4},{4,6},{6,7},{7,5},{5,3},{3,1},{1,0},{8,10},{10,12},{12... | collective-permute-start | bytes 786440 | tf_op jit(solution)/shard_map/ppermute | solution.py:550
  20.3 0.7 dynamic-slice_bitcast_fusion.place_ref
  21.1 4.1 %collective-permute-done.10.refs_2_ = bf16[32,4096]{1,0:T(8,128)(2,1)S(1)} collective-permute-done((bf16[32,4096]{1,0:T(8,128)(2,1)S(1)}, bf16[32,4096]{1,0:T(8,128)(2,1)S(1)}, u32[]{:S(2)}, u32[]{:S(2)}) %collective-permute-start.10) | collective-permute-done | bytes 262176 | tf_op jit(solution)/shard_map/ppermute | solution.py:552
  25.2 0.3 collective-permute-start.12
  25.7 0.5 broadcast.179
  26.2 0.7 reduce.3
  27.0 1.7 collective-permute-start.17
  28.8 0.5 collective-permute-done.1.refs_3_
  29.3 0.6 broadcast_in_dim.23.refs_4_
  29.9 1.8 collective-permute-start.2
  31.8 1.6 collective-permute-start.11
  33.3 1.1 collective-permute-done.12.refs_4_
  34.7 5.4 %collective-permute-done.17.refs_4_ = bf16[32,4096]{1,0:T(8,128)(2,1)S(1)} collective-permute-done((bf16[32,4096]{1,0:T(8,128)(2,1)S(1)}, bf16[32,4096]{1,0:T(8,128)(2,1)S(1)}, u32[]{:S(2)}, u32[]{:S(2)}) %collective-permute-start.17) | collective-permute-done | bytes 262176 | tf_op jit(solution)/shard_map/ppermute | solution.py:552
  40.3 3.3 %select_docs.1 = (bf16[2,4,256,128]{3,2,1,0:T(8,128)(2,1)S(1)}, bf16[2,4,256,128]{3,2,1,0:T(8,128)(2,1)S(1)}, bf16[2,4,256,128]{3,2,1,0:T(8,128)(2,1)S(1)}, bf16...) custom-call(s32[4]{0:T(128)S(1)} %get-tuple-element.76.place_ref, ...), custom_call_target="tpu_custom_call" | custom-call | bytes 8388608 | tf_op jit(solution)/shard_map/select_docs/pallas_call | solution.py:215
  43.6 1.8 collective-permute-start.19
  45.4 1.6 collective-permute-start.13
  47.0 0.4 collective-permute-start.15
  47.5 0.5 collective-permute-start.4
  47.9 3.4 %collective-permute-done.18.refs_6_ = bf16[32,4096]{1,0:T(8,128)(2,1)S(1)} collective-permute-done((bf16[32,4096]{1,0:T(8,128)(2,1)S(1)}, bf16[32,4096]{1,0:T(8,128)(2,1)S(1)}, u32[]{:S(2)}, u32[]{:S(2)}) %collective-permute-start.18) | collective-permute-done | bytes 262176 | tf_op jit(solution)/shard_map/ppermute | solution.py:552
  51.3 1.6 collective-permute-start.5
  52.9 6.4 %project.2 = (f32[256,256]{1,0:T(8,128)S(1)}, f32[256,1024]{1,0:T(8,128)S(1)}) custom-call(s32[8]{0:T(128)S(1)} %dynamic-slice_bitcast_fusion.place_ref, bf16[32,4096]{1,0:T(8,128)(2,1)S(1)} %get-tuple-element.138.refs_0_, bf16[32,4096]{1,0:T(8,128)(2,1)S(1)} %collective-permute-done.refs_1_, bf16[32,4096]{1,0:T(8,128)(2,1)S(1)} %collective-permute-done.16.refs_2_, ...), custom_call_target="tpu_custom_call" | custom-call | flops 2684354560 | bytes 12582912 | tf_op jit(solution)/shard_map/project/pallas_call | solution.py:173
  59.3 7.2 %project.3 = (bf16[256,128]{1,0:T(8,128)(2,1)S(1)}, bf16[256,128]{1,0:T(8,128)(2,1)S(1)}, bf16[8,128,256]{2,1,0:T(8,128)(2,1)S(1)}) custom-call(s32[8]{0:T(128)S(1)} %dynamic-slice_bitcast_fusion.place_ref, bf16[32,4096]{1,0:T(8,128)(2,1)S(1)} %get-tuple-element.137.refs_0_, bf16[32,4096]{1,0:T(8,128)(2,1)S(1)} %collective-permute-done.9.refs_1_, ...), custom_call_target="tpu_custom_call" | custom-call | flops 2684354560 | bytes 12582912 | tf_op jit(solution)/shard_map/project/pallas_call | solution.py:173
  66.6 2.6 %collective-permute-start.20 = (bf16[8,128,256]{2,1,0:T(8,128)(2,1)S(1)}, bf16[8,128,256]{2,1,0:T(8,128)(2,1)S(1)}, u32[]{:S(2)}, u32[]{:S(2)}) collective-permute-start(bf16[8,128,256]{2,1,0:T(8,128)(2,1)S(1)} %get-tuple-element.108.refs_6_), channel_id=1, source_target_pairs={{0,4},{1,5},{2,6},{3,7},{4,0},{5,1},{6,2},{7,3},{8,12},{9,13},{10,... | collective-permute-start | bytes 1572872 | tf_op jit(solution)/shard_map/ppermute | solution.py:589
  69.1 2.8 %collective-permute-start.23 = (bf16[2,4,256,128]{3,2,1,0:T(8,128)(2,1)S(1)}, bf16[2,4,256,128]{3,2,1,0:T(8,128)(2,1)S(1)}, u32[]{:S(2)}, u32[]{:S(2)}) collective-permute-start(bf16[2,4,256,128]{3,2,1,0:T(8,128)(2,1)S(1)} %get-tuple-element.119), channel_id=1, source_target_pairs={{0,3},{1,2},{2,1},{3,0},{4,7},{5,6},{6,5},{7,4},{8,11},{9,10},{10,... | collective-permute-start | bytes 1572872 | tf_op jit(solution)/shard_map/ppermute | solution.py:605
  71.9 0.7 collective-permute-start.21
  72.6 3.2 %collective-permute-start.22 = (bf16[256,128]{1,0:T(8,128)(2,1)S(1)}, bf16[256,128]{1,0:T(8,128)(2,1)S(1)}, u32[]{:S(2)}, u32[]{:S(2)}) collective-permute-start(bf16[256,128]{1,0:T(8,128)(2,1)S(1)} %get-tuple-element.110), channel_id=1, source_target_pairs={{0,1},{1,3},{2,5},{3,7},{4,0},{5,2},{6,4},{7,6},{8,9},{9,11},{10,1... | collective-permute-start | bytes 196616 | tf_op jit(solution)/shard_map/ppermute | solution.py:594
  75.8 0.3 collective-permute-start.6
  76.2 18.7 %collective-permute-start.7 = (bf16[2,4,256,128]{3,2,1,0:T(8,128)(2,1)S(1)}, bf16[2,4,256,128]{3,2,1,0:T(8,128)(2,1)S(1)}, u32[]{:S(2)}, u32[]{:S(2)}) collective-permute-start(bf16[2,4,256,128]{3,2,1,0:T(8,128)(2,1)S(1)} %get-tuple-element.96), channel_id=1, source_target_pairs={{0,2},{1,3},{2,0},{3,1},{4,6},{5,7},{6,4},{7,5},{8,10},{9,11},{10,... | collective-permute-start | bytes 1572872 | tf_op jit(solution)/shard_map/ppermute | solution.py:605
  94.8 1.4 collective-permute-start.8
  96.2 9.9 %attend.5 = bf16[4,144,256]{2,1,0:T(8,128)(2,1)S(1)} custom-call(s32[16]{0:T(128)S(1)} %select_n.48.first_ref, s32[256]{0:T(256)S(1)} %bitcast.24, s32[1]{0:T(128)} %bitcast.6.odd_ref, bf16[2,4,256,128]{3,2,1,0:T(8,128)(2,1)S(1)} %get-tuple-element.116.refs_0_, bf16[2,4,256,128]{3,2,1,0:T(8,128)(2,1)S(1)} %collective-permute-done.4.refs_1_, ...), custom_call_target="tpu_custom_call" | custom-call | flops 1073741824 | tf_op jit(solution)/shard_map/attend/pallas_call | solution.py:384
  106.1 1.0 collective-permute-start.25
  107.1 4.7 %attend.4 = bf16[4,144,256]{2,1,0:T(8,128)(2,1)S(1)} custom-call(s32[16]{0:T(128)S(1)} %select_n.48.first_ref, s32[256]{0:T(256)S(1)} %bitcast.25, s32[1]{0:T(128)} %bitcast.6.odd_ref, bf16[2,4,256,128]{3,2,1,0:T(8,128)(2,1)S(1)} %get-tuple-element.116.refs_0_, bf16[2,4,256,128]{3,2,1,0:T(8,128)(2,1)S(1)} %collective-permute-done.4.refs_1_, ...), custom_call_target="tpu_custom_call" | custom-call | flops 1073741824 | tf_op jit(solution)/shard_map/attend/pallas_call | solution.py:384
  111.9 2.2 %collective-permute-start.24 = (bf16[4,144,256]{2,1,0:T(8,128)(2,1)S(1)}, bf16[4,144,256]{2,1,0:T(8,128)(2,1)S(1)}, u32[]{:S(2)}, u32[]{:S(2)}) collective-permute-start(bf16[4,144,256]{2,1,0:T(8,128)(2,1)S(1)} %attend.4), channel_id=1, source_target_pairs={{0,4},{1,5},{2,6},{3,7},{4,0},{5,1},{6,2},{7,3},{8,12},{9,13},{10,... | collective-permute-start | bytes 884744 | tf_op jit(solution)/shard_map/ppermute | solution.py:621
  114.0 1.9 %collective-permute-done.7.refs_2_ = bf16[2,4,256,128]{3,2,1,0:T(8,128)(2,1)S(1)} collective-permute-done((bf16[2,4,256,128]{3,2,1,0:T(8,128)(2,1)S(1)}, bf16[2,4,256,128]{3,2,1,0:T(8,128)(2,1)S(1)}, u32[]{:S(2)}, u32[]{:S(2)}) %collective-permute-start.7) | collective-permute-done | bytes 524320 | tf_op jit(solution)/shard_map/ppermute | solution.py:605
  116.0 7.5 %collective-permute-done.8.refs_3_ = bf16[2,4,256,128]{3,2,1,0:T(8,128)(2,1)S(1)} collective-permute-done((bf16[2,4,256,128]{3,2,1,0:T(8,128)(2,1)S(1)}, bf16[2,4,256,128]{3,2,1,0:T(8,128)(2,1)S(1)}, u32[]{:S(2)}, u32[]{:S(2)}) %collective-permute-start.8) | collective-permute-done | bytes 524320 | tf_op jit(solution)/shard_map/ppermute | solution.py:605
  123.4 15.7 %attend.3 = (f32[8,1,256]{2,1,0:T(1,128)S(1)}, f32[8,1,256]{2,1,0:T(1,128)S(1)}, f32[8,128,256]{2,1,0:T(8,128)S(1)}) custom-call(s32[16]{0:T(128)S(1)} %select_n.48.first_ref, s32[256]{0:T(256)S(1)} %bitcast.26, s32[1]{0:T(128)} %bitcast.6.odd_ref, bf16[2,4,256,128]{3,2,1,0:T(8,128)(2,1)S(1)} %get-tuple-element.94.refs_0_, ...), custom_call_target="tpu_custom_call" | custom-call | flops 1 | bytes 1 | tf_op jit(solution)/shard_map/attend/pallas_call | solution.py:384
  139.2 0.4 merge.1.x_ref
  139.6 5.1 %project_out.2 = (f32[32,4096]{1,0:T(8,128)S(1)}, f32[32,4096]{1,0:T(8,128)S(1)}, f32[32,4096]{1,0:T(8,128)S(1)}, f32[32,4096]{1,0:T(8,128)S(1)}, f32[32,4096]{1...) custom-call(s32[8]{0:T(128)S(1)} %dynamic-slice_bitcast_fusion.place_ref, ...), custom_call_target="tpu_custom_call" | custom-call | flops 2147483648 | bytes 13107200 | tf_op jit(solution)/shard_map/project_out/pallas_call | solution.py:469
  144.6 0.7 collective-permute-start.26
  145.4 2.0 %collective-permute-start.30 = (bf16[32,4096]{1,0:T(8,128)(2,1)S(1)}, bf16[32,4096]{1,0:T(8,128)(2,1)S(1)}, u32[]{:S(2)}, u32[]{:S(2)}) collective-permute-start(bf16[32,4096]{1,0:T(8,128)(2,1)S(1)} %convert_element_type.116), channel_id=1, source_target_pairs={{2,0},{4,2},{6,4},{7,6},{5,7},{3,5},{1,3},{0,1},{10,8},{12,10},{14... | collective-permute-start | bytes 786440 | tf_op jit(solution)/shard_map/ppermute | solution.py:641
  147.4 5.1 %project_out.3 = (f32[32,4096]{1,0:T(8,128)S(1)}, f32[32,4096]{1,0:T(8,128)S(1)}, f32[32,4096]{1,0:T(8,128)S(1)}, f32[32,4096]{1,0:T(8,128)S(1)}, f32[32,4096]{1...) custom-call(s32[8]{0:T(128)S(1)} %dynamic-slice_bitcast_fusion.place_ref, ...), custom_call_target="tpu_custom_call" | custom-call | flops 2147483648 | bytes 13107200 | tf_op jit(solution)/shard_map/project_out/pallas_call | solution.py:469
  152.7 2.0 %collective-permute-start.36 = (bf16[32,4096]{1,0:T(8,128)(2,1)S(1)}, bf16[32,4096]{1,0:T(8,128)(2,1)S(1)}, u32[]{:S(2)}, u32[]{:S(2)}) collective-permute-start(bf16[32,4096]{1,0:T(8,128)(2,1)S(1)} %get-tuple-element.136), channel_id=1, source_target_pairs={{2,0},{4,2},{6,4},{7,6},{5,7},{3,5},{1,3},{0,1},{10,8},{12,10},{14... | collective-permute-start | bytes 786440 | tf_op jit(solution)/shard_map/ppermute | solution.py:641
  154.9 2.1 %collective-permute-start.31 = (bf16[32,4096]{1,0:T(8,128)(2,1)S(1)}, bf16[32,4096]{1,0:T(8,128)(2,1)S(1)}, u32[]{:S(2)}, u32[]{:S(2)}) collective-permute-start(bf16[32,4096]{1,0:T(8,128)(2,1)S(1)} %add_convert_fusion.8), channel_id=1, source_target_pairs={{2,0},{4,2},{6,4},{7,6},{5,7},{3,5},{1,3},{0,1},{10,8},{12,10},{14... | collective-permute-start | bytes 786440 | tf_op jit(solution)/shard_map/ppermute | solution.py:641
  156.9 4.9 %collective-permute-done.33 = bf16[32,4096]{1,0:T(8,128)(2,1)S(1)} collective-permute-done((bf16[32,4096]{1,0:T(8,128)(2,1)S(1)}, bf16[32,4096]{1,0:T(8,128)(2,1)S(1)}, u32[]{:S(2)}, u32[]{:S(2)}) %collective-permute-start.33) | collective-permute-done | bytes 262176 | tf_op jit(solution)/shard_map/ppermute | solution.py:641
  162.1 2.0 %collective-permute-start.37 = (bf16[32,4096]{1,0:T(8,128)(2,1)S(1)}, bf16[32,4096]{1,0:T(8,128)(2,1)S(1)}, u32[]{:S(2)}, u32[]{:S(2)}) collective-permute-start(bf16[32,4096]{1,0:T(8,128)(2,1)S(1)} %add_convert_fusion.3), channel_id=1, source_target_pairs={{2,0},{4,2},{6,4},{7,6},{5,7},{3,5},{1,3},{0,1},{10,8},{12,10},{14... | collective-permute-start | bytes 786440 | tf_op jit(solution)/shard_map/ppermute | solution.py:641
  164.1 3.4 %collective-permute-done.27 = bf16[32,4096]{1,0:T(8,128)(2,1)S(1)} collective-permute-done((bf16[32,4096]{1,0:T(8,128)(2,1)S(1)}, bf16[32,4096]{1,0:T(8,128)(2,1)S(1)}, u32[]{:S(2)}, u32[]{:S(2)}) %collective-permute-start.27) | collective-permute-done | bytes 262176 | tf_op jit(solution)/shard_map/ppermute | solution.py:641
  167.7 2.0 %collective-permute-start.32 = (bf16[32,4096]{1,0:T(8,128)(2,1)S(1)}, bf16[32,4096]{1,0:T(8,128)(2,1)S(1)}, u32[]{:S(2)}, u32[]{:S(2)}) collective-permute-start(bf16[32,4096]{1,0:T(8,128)(2,1)S(1)} %add_convert_fusion.7), channel_id=1, source_target_pairs={{2,0},{4,2},{6,4},{7,6},{5,7},{3,5},{1,3},{0,1},{10,8},{12,10},{14... | collective-permute-start | bytes 786440 | tf_op jit(solution)/shard_map/ppermute | solution.py:641
  169.7 3.4 %collective-permute-done.34 = bf16[32,4096]{1,0:T(8,128)(2,1)S(1)} collective-permute-done((bf16[32,4096]{1,0:T(8,128)(2,1)S(1)}, bf16[32,4096]{1,0:T(8,128)(2,1)S(1)}, u32[]{:S(2)}, u32[]{:S(2)}) %collective-permute-start.34) | collective-permute-done | bytes 262176 | tf_op jit(solution)/shard_map/ppermute | solution.py:641
  173.3 2.0 %collective-permute-start.38 = (bf16[32,4096]{1,0:T(8,128)(2,1)S(1)}, bf16[32,4096]{1,0:T(8,128)(2,1)S(1)}, u32[]{:S(2)}, u32[]{:S(2)}) collective-permute-start(bf16[32,4096]{1,0:T(8,128)(2,1)S(1)} %add_convert_fusion.2), channel_id=1, source_target_pairs={{2,0},{4,2},{6,4},{7,6},{5,7},{3,5},{1,3},{0,1},{10,8},{12,10},{14... | collective-permute-start | bytes 786440 | tf_op jit(solution)/shard_map/ppermute | solution.py:641
  175.3 3.4 %collective-permute-done.28 = bf16[32,4096]{1,0:T(8,128)(2,1)S(1)} collective-permute-done((bf16[32,4096]{1,0:T(8,128)(2,1)S(1)}, bf16[32,4096]{1,0:T(8,128)(2,1)S(1)}, u32[]{:S(2)}, u32[]{:S(2)}) %collective-permute-start.28) | collective-permute-done | bytes 262176 | tf_op jit(solution)/shard_map/ppermute | solution.py:641
  178.9 2.6 %collective-permute-done.38 = bf16[32,4096]{1,0:T(8,128)(2,1)S(1)} collective-permute-done((bf16[32,4096]{1,0:T(8,128)(2,1)S(1)}, bf16[32,4096]{1,0:T(8,128)(2,1)S(1)}, u32[]{:S(2)}, u32[]{:S(2)}) %collective-permute-start.38) | collective-permute-done | bytes 262176 | tf_op jit(solution)/shard_map/ppermute | solution.py:641
  181.6 2.1 %collective-permute-start.39 = (bf16[32,4096]{1,0:T(8,128)(2,1)S(1)}, bf16[32,4096]{1,0:T(8,128)(2,1)S(1)}, u32[]{:S(2)}, u32[]{:S(2)}) collective-permute-start(bf16[32,4096]{1,0:T(8,128)(2,1)S(1)} %add_convert_fusion.1), channel_id=1, source_target_pairs={{2,0},{4,2},{6,4},{7,6},{5,7},{3,5},{1,3},{0,1},{10,8},{12,10},{14... | collective-permute-start | bytes 786440 | tf_op jit(solution)/shard_map/ppermute | solution.py:641
  183.6 2.8 %collective-permute-done.29 = bf16[32,4096]{1,0:T(8,128)(2,1)S(1)} collective-permute-done((bf16[32,4096]{1,0:T(8,128)(2,1)S(1)}, bf16[32,4096]{1,0:T(8,128)(2,1)S(1)}, u32[]{:S(2)}, u32[]{:S(2)}) %collective-permute-start.29) | collective-permute-done | bytes 262176 | tf_op jit(solution)/shard_map/ppermute | solution.py:641
  186.5 1.5 collective-permute-done.39
  188.1 0.8 pad_maximum_fusion
  (77 shorter events, 3.1 us)
Async XLA Ops:
  2.5 10.7 %copy-start = (s32[1,256]{1,0:T(1,128)S(1)}, s32[1,256]{1,0:T(1,128)}, u32[]{:S(2)}) copy-start(s32[1,256]{1,0:T(1,128)} %param.18) | copy-start | bytes 3076
  2.5 10.7 %copy-start.1 = (s32[1,4]{1,0:T(1,128)S(1)}, s32[1,4]{1,0:T(1,128)}, u32[]{:S(2)}) copy-start(s32[1,4]{1,0:T(1,128)} %param.17) | copy-start | bytes 52
  2.5 13.1 %copy-start.2 = (s32[4]{0:T(128)S(1)}, s32[4]{0:T(128)}, u32[]{:S(2)}) copy-start(s32[4]{0:T(128)} %param.16) | copy-start | bytes 52
  8.0 32.3 %collective-permute-start.3 = (bf16[4,2,256,1024]{3,2,1,0:T(8,128)(2,1)}, bf16[4,2,256,1024]{3,2,1,0:T(8,128)(2,1)}, u32[]{:S(2)}, u32[]{:S(2)}) collective-permute-start(bf16[4,2,256,1024]{3,2,1,0:T(8,128)(2,1)} %bitcast.21.refs_0_), channel_id=1, source_target_pairs={{8,0},{0,8},{9,1},{1,9},{10,2},{2,10},{11,3},{3,11},{12,4},{4,12},... | collective-permute-start | bytes 12582920 | tf_op jit(solution)/shard_map/ppermute | solution.py:559
  8.5 9.7 %collective-permute-start = (bf16[32,4096]{1,0:T(8,128)(2,1)S(1)}, bf16[32,4096]{1,0:T(8,128)(2,1)S(1)}, u32[]{:S(2)}, u32[]{:S(2)}) collective-permute-start(bf16[32,4096]{1,0:T(8,128)(2,1)S(1)} %get-tuple-element.138.refs_0_), channel_id=1, source_target_pairs={{0,2},{2,4},{4,6},{6,7},{7,5},{5,3},{3,1},{1,0},{8,10},{10,12},{12... | collective-permute-start | bytes 786440 | tf_op jit(solution)/shard_map/ppermute | solution.py:550
  11.1 15.9 %collective-permute-start.16 = (bf16[32,4096]{1,0:T(8,128)(2,1)S(1)}, bf16[32,4096]{1,0:T(8,128)(2,1)S(1)}, u32[]{:S(2)}, u32[]{:S(2)}) collective-permute-start(bf16[32,4096]{1,0:T(8,128)(2,1)S(1)} %get-tuple-element.138.refs_0_), channel_id=1, source_target_pairs={{2,0},{4,2},{6,4},{7,6},{5,7},{3,5},{1,3},{0,1},{10,8},{12,10},{14... | collective-permute-start | bytes 786440 | tf_op jit(solution)/shard_map/ppermute | solution.py:552
  11.2 14.0 %collective-permute-start.10 = (bf16[32,4096]{1,0:T(8,128)(2,1)S(1)}, bf16[32,4096]{1,0:T(8,128)(2,1)S(1)}, u32[]{:S(2)}, u32[]{:S(2)}) collective-permute-start(bf16[32,4096]{1,0:T(8,128)(2,1)S(1)} %get-tuple-element.137.refs_0_), channel_id=1, source_target_pairs={{2,0},{4,2},{6,4},{7,6},{5,7},{3,5},{1,3},{0,1},{10,8},{12,10},{14... | collective-permute-start | bytes 786440 | tf_op jit(solution)/shard_map/ppermute | solution.py:552
  13.1 18.6 %collective-permute-start.9 = (bf16[32,4096]{1,0:T(8,128)(2,1)S(1)}, bf16[32,4096]{1,0:T(8,128)(2,1)S(1)}, u32[]{:S(2)}, u32[]{:S(2)}) collective-permute-start(bf16[32,4096]{1,0:T(8,128)(2,1)S(1)} %get-tuple-element.137.refs_0_), channel_id=1, source_target_pairs={{0,2},{2,4},{4,6},{6,7},{7,5},{5,3},{3,1},{1,0},{8,10},{10,12},{12... | collective-permute-start | bytes 786440 | tf_op jit(solution)/shard_map/ppermute | solution.py:550
  18.3 11.1 %collective-permute-start.1 = (bf16[32,4096]{1,0:T(8,128)(2,1)S(1)}, bf16[32,4096]{1,0:T(8,128)(2,1)S(1)}, u32[]{:S(2)}, u32[]{:S(2)}) collective-permute-start(bf16[32,4096]{1,0:T(8,128)(2,1)S(1)} %collective-permute-done.refs_1_), channel_id=1, source_target_pairs={{0,2},{2,4},{4,6},{6,7},{7,5},{5,3},{3,1},{1,0},{8,10},{10,12},{12... | collective-permute-start | bytes 786440 | tf_op jit(solution)/shard_map/ppermute | solution.py:550
  25.2 9.2 %collective-permute-start.12 = (bf16[32,4096]{1,0:T(8,128)(2,1)S(1)}, bf16[32,4096]{1,0:T(8,128)(2,1)S(1)}, u32[]{:S(2)}, u32[]{:S(2)}) collective-permute-start(bf16[32,4096]{1,0:T(8,128)(2,1)S(1)} %collective-permute-done.10.refs_2_), channel_id=1, source_target_pairs={{2,0},{4,2},{6,4},{7,6},{5,7},{3,5},{1,3},{0,1},{10,8},{12,10},{14... | collective-permute-start | bytes 786440 | tf_op jit(solution)/shard_map/ppermute | solution.py:552
  27.0 13.0 %collective-permute-start.17 = (bf16[32,4096]{1,0:T(8,128)(2,1)S(1)}, bf16[32,4096]{1,0:T(8,128)(2,1)S(1)}, u32[]{:S(2)}, u32[]{:S(2)}) collective-permute-start(bf16[32,4096]{1,0:T(8,128)(2,1)S(1)} %collective-permute-done.16.refs_2_), channel_id=1, source_target_pairs={{2,0},{4,2},{6,4},{7,6},{5,7},{3,5},{1,3},{0,1},{10,8},{12,10},{14... | collective-permute-start | bytes 786440 | tf_op jit(solution)/shard_map/ppermute | solution.py:552
  29.9 13.7 %collective-permute-start.2 = (bf16[32,4096]{1,0:T(8,128)(2,1)S(1)}, bf16[32,4096]{1,0:T(8,128)(2,1)S(1)}, u32[]{:S(2)}, u32[]{:S(2)}) collective-permute-start(bf16[32,4096]{1,0:T(8,128)(2,1)S(1)} %collective-permute-done.1.refs_3_), channel_id=1, source_target_pairs={{0,2},{2,4},{4,6},{6,7},{7,5},{5,3},{3,1},{1,0},{8,10},{10,12},{12... | collective-permute-start | bytes 786440 | tf_op jit(solution)/shard_map/ppermute | solution.py:550
  31.8 13.7 %collective-permute-start.11 = (bf16[32,4096]{1,0:T(8,128)(2,1)S(1)}, bf16[32,4096]{1,0:T(8,128)(2,1)S(1)}, u32[]{:S(2)}, u32[]{:S(2)}) collective-permute-start(bf16[32,4096]{1,0:T(8,128)(2,1)S(1)} %collective-permute-done.9.refs_1_), channel_id=1, source_target_pairs={{0,2},{2,4},{4,6},{6,7},{7,5},{5,3},{3,1},{1,0},{8,10},{10,12},{12... | collective-permute-start | bytes 786440 | tf_op jit(solution)/shard_map/ppermute | solution.py:550
  34.4 12.6 %collective-permute-start.14 = (bf16[32,4096]{1,0:T(8,128)(2,1)S(1)}, bf16[32,4096]{1,0:T(8,128)(2,1)S(1)}, u32[]{:S(2)}, u32[]{:S(2)}) collective-permute-start(bf16[32,4096]{1,0:T(8,128)(2,1)S(1)} %collective-permute-done.12.refs_4_), channel_id=1, source_target_pairs={{2,0},{4,2},{6,4},{7,6},{5,7},{3,5},{1,3},{0,1},{10,8},{12,10},{14... | collective-permute-start | bytes 786440 | tf_op jit(solution)/shard_map/ppermute | solution.py:552
  40.1 11.2 %collective-permute-start.18 = (bf16[32,4096]{1,0:T(8,128)(2,1)S(1)}, bf16[32,4096]{1,0:T(8,128)(2,1)S(1)}, u32[]{:S(2)}, u32[]{:S(2)}) collective-permute-start(bf16[32,4096]{1,0:T(8,128)(2,1)S(1)} %collective-permute-done.17.refs_4_), channel_id=1, source_target_pairs={{2,0},{4,2},{6,4},{7,6},{5,7},{3,5},{1,3},{0,1},{10,8},{12,10},{14... | collective-permute-start | bytes 786440 | tf_op jit(solution)/shard_map/ppermute | solution.py:552
  43.6 9.3 %collective-permute-start.19 = (bf16[32,4096]{1,0:T(8,128)(2,1)S(1)}, bf16[32,4096]{1,0:T(8,128)(2,1)S(1)}, u32[]{:S(2)}, u32[]{:S(2)}) collective-permute-start(bf16[32,4096]{1,0:T(8,128)(2,1)S(1)} %collective-permute-done.2.refs_5_), channel_id=1, source_target_pairs={{0,2},{2,4},{4,6},{6,7},{7,5},{5,3},{3,1},{1,0},{8,10},{10,12},{12... | collective-permute-start | bytes 786440 | tf_op jit(solution)/shard_map/ppermute | solution.py:550
  45.4 13.9 %collective-permute-start.13 = (bf16[32,4096]{1,0:T(8,128)(2,1)S(1)}, bf16[32,4096]{1,0:T(8,128)(2,1)S(1)}, u32[]{:S(2)}, u32[]{:S(2)}) collective-permute-start(bf16[32,4096]{1,0:T(8,128)(2,1)S(1)} %collective-permute-done.11.refs_3_), channel_id=1, source_target_pairs={{0,2},{2,4},{4,6},{6,7},{7,5},{5,3},{3,1},{1,0},{8,10},{10,12},{12... | collective-permute-start | bytes 786440 | tf_op jit(solution)/shard_map/ppermute | solution.py:550
  47.0 12.3 %collective-permute-start.15 = (bf16[32,4096]{1,0:T(8,128)(2,1)S(1)}, bf16[32,4096]{1,0:T(8,128)(2,1)S(1)}, u32[]{:S(2)}, u32[]{:S(2)}) collective-permute-start(bf16[32,4096]{1,0:T(8,128)(2,1)S(1)} %collective-permute-done.14.refs_6_), channel_id=1, source_target_pairs={{2,0},{4,2},{6,4},{7,6},{5,7},{3,5},{1,3},{0,1},{10,8},{12,10},{14... | collective-permute-start | bytes 786440 | tf_op jit(solution)/shard_map/ppermute | solution.py:552
  47.5 25.1 %collective-permute-start.4 = (bf16[2,4,256,128]{3,2,1,0:T(8,128)(2,1)S(1)}, bf16[2,4,256,128]{3,2,1,0:T(8,128)(2,1)S(1)}, u32[]{:S(2)}, u32[]{:S(2)}) collective-permute-start(bf16[2,4,256,128]{3,2,1,0:T(8,128)(2,1)S(1)} %get-tuple-element.92), channel_id=1, source_target_pairs={{0,1},{1,0},{2,3},{3,2},{4,5},{5,4},{6,7},{7,6},{8,9},{9,8},{10,11... | collective-permute-start | bytes 1572872 | tf_op jit(solution)/shard_map/ppermute | solution.py:605
  51.3 24.5 %collective-permute-start.5 = (bf16[2,4,256,128]{3,2,1,0:T(8,128)(2,1)S(1)}, bf16[2,4,256,128]{3,2,1,0:T(8,128)(2,1)S(1)}, u32[]{:S(2)}, u32[]{:S(2)}) collective-permute-start(bf16[2,4,256,128]{3,2,1,0:T(8,128)(2,1)S(1)} %get-tuple-element.93), channel_id=1, source_target_pairs={{0,2},{1,3},{2,0},{3,1},{4,6},{5,7},{6,4},{7,5},{8,10},{9,11},{10,... | collective-permute-start | bytes 1572872 | tf_op jit(solution)/shard_map/ppermute | solution.py:605
  66.6 29.7 %collective-permute-start.20 = (bf16[8,128,256]{2,1,0:T(8,128)(2,1)S(1)}, bf16[8,128,256]{2,1,0:T(8,128)(2,1)S(1)}, u32[]{:S(2)}, u32[]{:S(2)}) collective-permute-start(bf16[8,128,256]{2,1,0:T(8,128)(2,1)S(1)} %get-tuple-element.108.refs_6_), channel_id=1, source_target_pairs={{0,4},{1,5},{2,6},{3,7},{4,0},{5,1},{6,2},{7,3},{8,12},{9,13},{10,... | collective-permute-start | bytes 1572872 | tf_op jit(solution)/shard_map/ppermute | solution.py:589
  69.1 27.1 %collective-permute-start.23 = (bf16[2,4,256,128]{3,2,1,0:T(8,128)(2,1)S(1)}, bf16[2,4,256,128]{3,2,1,0:T(8,128)(2,1)S(1)}, u32[]{:S(2)}, u32[]{:S(2)}) collective-permute-start(bf16[2,4,256,128]{3,2,1,0:T(8,128)(2,1)S(1)} %get-tuple-element.119), channel_id=1, source_target_pairs={{0,3},{1,2},{2,1},{3,0},{4,7},{5,6},{6,5},{7,4},{8,11},{9,10},{10,... | collective-permute-start | bytes 1572872 | tf_op jit(solution)/shard_map/ppermute | solution.py:605
  71.9 4.2 %collective-permute-start.21 = (bf16[256,128]{1,0:T(8,128)(2,1)S(1)}, bf16[256,128]{1,0:T(8,128)(2,1)S(1)}, u32[]{:S(2)}, u32[]{:S(2)}) collective-permute-start(bf16[256,128]{1,0:T(8,128)(2,1)S(1)} %get-tuple-element.109), channel_id=1, source_target_pairs={{0,0},{1,2},{2,4},{3,6},{4,1},{5,3},{6,5},{7,7},{8,8},{9,10},{10,1... | collective-permute-start | bytes 196616 | tf_op jit(solution)/shard_map/ppermute | solution.py:594
  72.6 22.2 %collective-permute-start.22 = (bf16[256,128]{1,0:T(8,128)(2,1)S(1)}, bf16[256,128]{1,0:T(8,128)(2,1)S(1)}, u32[]{:S(2)}, u32[]{:S(2)}) collective-permute-start(bf16[256,128]{1,0:T(8,128)(2,1)S(1)} %get-tuple-element.110), channel_id=1, source_target_pairs={{0,1},{1,3},{2,5},{3,7},{4,0},{5,2},{6,4},{7,6},{8,9},{9,11},{10,1... | collective-permute-start | bytes 196616 | tf_op jit(solution)/shard_map/ppermute | solution.py:594
  75.8 38.2 %collective-permute-start.6 = (bf16[2,4,256,128]{3,2,1,0:T(8,128)(2,1)S(1)}, bf16[2,4,256,128]{3,2,1,0:T(8,128)(2,1)S(1)}, u32[]{:S(2)}, u32[]{:S(2)}) collective-permute-start(bf16[2,4,256,128]{3,2,1,0:T(8,128)(2,1)S(1)} %get-tuple-element.95), channel_id=1, source_target_pairs={{0,1},{1,0},{2,3},{3,2},{4,5},{5,4},{6,7},{7,6},{8,9},{9,8},{10,11... | collective-permute-start | bytes 1572872 | tf_op jit(solution)/shard_map/ppermute | solution.py:605
  76.2 39.8 %collective-permute-start.7 = (bf16[2,4,256,128]{3,2,1,0:T(8,128)(2,1)S(1)}, bf16[2,4,256,128]{3,2,1,0:T(8,128)(2,1)S(1)}, u32[]{:S(2)}, u32[]{:S(2)}) collective-permute-start(bf16[2,4,256,128]{3,2,1,0:T(8,128)(2,1)S(1)} %get-tuple-element.96), channel_id=1, source_target_pairs={{0,2},{1,3},{2,0},{3,1},{4,6},{5,7},{6,4},{7,5},{8,10},{9,11},{10,... | collective-permute-start | bytes 1572872 | tf_op jit(solution)/shard_map/ppermute | solution.py:605
  94.8 28.6 %collective-permute-start.8 = (bf16[2,4,256,128]{3,2,1,0:T(8,128)(2,1)S(1)}, bf16[2,4,256,128]{3,2,1,0:T(8,128)(2,1)S(1)}, u32[]{:S(2)}, u32[]{:S(2)}) collective-permute-start(bf16[2,4,256,128]{3,2,1,0:T(8,128)(2,1)S(1)} %get-tuple-element.97), channel_id=1, source_target_pairs={{0,3},{1,2},{2,1},{3,0},{4,7},{5,6},{6,5},{7,4},{8,11},{9,10},{10,... | collective-permute-start | bytes 1572872 | tf_op jit(solution)/shard_map/ppermute | solution.py:605
  106.1 33.1 %collective-permute-start.25 = (bf16[4,144,256]{2,1,0:T(8,128)(2,1)S(1)}, bf16[4,144,256]{2,1,0:T(8,128)(2,1)S(1)}, u32[]{:S(2)}, u32[]{:S(2)}) collective-permute-start(bf16[4,144,256]{2,1,0:T(8,128)(2,1)S(1)} %attend.5), channel_id=1, source_target_pairs={{0,4},{1,5},{2,6},{3,7},{4,0},{5,1},{6,2},{7,3},{8,12},{9,13},{10,... | collective-permute-start | bytes 884744 | tf_op jit(solution)/shard_map/ppermute | solution.py:621
  111.9 27.3 %collective-permute-start.24 = (bf16[4,144,256]{2,1,0:T(8,128)(2,1)S(1)}, bf16[4,144,256]{2,1,0:T(8,128)(2,1)S(1)}, u32[]{:S(2)}, u32[]{:S(2)}) collective-permute-start(bf16[4,144,256]{2,1,0:T(8,128)(2,1)S(1)} %attend.4), channel_id=1, source_target_pairs={{0,4},{1,5},{2,6},{3,7},{4,0},{5,1},{6,2},{7,3},{8,12},{9,13},{10,... | collective-permute-start | bytes 884744 | tf_op jit(solution)/shard_map/ppermute | solution.py:621
  144.6 10.0 %collective-permute-start.26 = (bf16[32,4096]{1,0:T(8,128)(2,1)S(1)}, bf16[32,4096]{1,0:T(8,128)(2,1)S(1)}, u32[]{:S(2)}, u32[]{:S(2)}) collective-permute-start(bf16[32,4096]{1,0:T(8,128)(2,1)S(1)} %get-tuple-element.125), channel_id=1, source_target_pairs={{0,2},{2,4},{4,6},{6,7},{7,5},{5,3},{3,1},{1,0},{8,10},{10,12},{12... | collective-permute-start | bytes 786440 | tf_op jit(solution)/shard_map/ppermute | solution.py:641
  145.4 9.4 %collective-permute-start.30 = (bf16[32,4096]{1,0:T(8,128)(2,1)S(1)}, bf16[32,4096]{1,0:T(8,128)(2,1)S(1)}, u32[]{:S(2)}, u32[]{:S(2)}) collective-permute-start(bf16[32,4096]{1,0:T(8,128)(2,1)S(1)} %convert_element_type.116), channel_id=1, source_target_pairs={{2,0},{4,2},{6,4},{7,6},{5,7},{3,5},{1,3},{0,1},{10,8},{12,10},{14... | collective-permute-start | bytes 786440 | tf_op jit(solution)/shard_map/ppermute | solution.py:641
  152.5 9.3 %collective-permute-start.33 = (bf16[32,4096]{1,0:T(8,128)(2,1)S(1)}, bf16[32,4096]{1,0:T(8,128)(2,1)S(1)}, u32[]{:S(2)}, u32[]{:S(2)}) collective-permute-start(bf16[32,4096]{1,0:T(8,128)(2,1)S(1)} %convert_element_type.123), channel_id=1, source_target_pairs={{0,2},{2,4},{4,6},{6,7},{7,5},{5,3},{3,1},{1,0},{8,10},{10,12},{12... | collective-permute-start | bytes 786440 | tf_op jit(solution)/shard_map/ppermute | solution.py:641
  152.7 9.4 %collective-permute-start.36 = (bf16[32,4096]{1,0:T(8,128)(2,1)S(1)}, bf16[32,4096]{1,0:T(8,128)(2,1)S(1)}, u32[]{:S(2)}, u32[]{:S(2)}) collective-permute-start(bf16[32,4096]{1,0:T(8,128)(2,1)S(1)} %get-tuple-element.136), channel_id=1, source_target_pairs={{2,0},{4,2},{6,4},{7,6},{5,7},{3,5},{1,3},{0,1},{10,8},{12,10},{14... | collective-permute-start | bytes 786440 | tf_op jit(solution)/shard_map/ppermute | solution.py:641
  154.7 12.7 %collective-permute-start.27 = (bf16[32,4096]{1,0:T(8,128)(2,1)S(1)}, bf16[32,4096]{1,0:T(8,128)(2,1)S(1)}, u32[]{:S(2)}, u32[]{:S(2)}) collective-permute-start(bf16[32,4096]{1,0:T(8,128)(2,1)S(1)} %add_convert_fusion.11), channel_id=1, source_target_pairs={{0,2},{2,4},{4,6},{6,7},{7,5},{5,3},{3,1},{1,0},{8,10},{10,12},{12... | collective-permute-start | bytes 786440 | tf_op jit(solution)/shard_map/ppermute | solution.py:641
  154.9 12.8 %collective-permute-start.31 = (bf16[32,4096]{1,0:T(8,128)(2,1)S(1)}, bf16[32,4096]{1,0:T(8,128)(2,1)S(1)}, u32[]{:S(2)}, u32[]{:S(2)}) collective-permute-start(bf16[32,4096]{1,0:T(8,128)(2,1)S(1)} %add_convert_fusion.8), channel_id=1, source_target_pairs={{2,0},{4,2},{6,4},{7,6},{5,7},{3,5},{1,3},{0,1},{10,8},{12,10},{14... | collective-permute-start | bytes 786440 | tf_op jit(solution)/shard_map/ppermute | solution.py:641
  161.9 11.2 %collective-permute-start.34 = (bf16[32,4096]{1,0:T(8,128)(2,1)S(1)}, bf16[32,4096]{1,0:T(8,128)(2,1)S(1)}, u32[]{:S(2)}, u32[]{:S(2)}) collective-permute-start(bf16[32,4096]{1,0:T(8,128)(2,1)S(1)} %add_convert_fusion.5), channel_id=1, source_target_pairs={{0,2},{2,4},{4,6},{6,7},{7,5},{5,3},{3,1},{1,0},{8,10},{10,12},{12... | collective-permute-start | bytes 786440 | tf_op jit(solution)/shard_map/ppermute | solution.py:641
  162.1 11.2 %collective-permute-start.37 = (bf16[32,4096]{1,0:T(8,128)(2,1)S(1)}, bf16[32,4096]{1,0:T(8,128)(2,1)S(1)}, u32[]{:S(2)}, u32[]{:S(2)}) collective-permute-start(bf16[32,4096]{1,0:T(8,128)(2,1)S(1)} %add_convert_fusion.3), channel_id=1, source_target_pairs={{2,0},{4,2},{6,4},{7,6},{5,7},{3,5},{1,3},{0,1},{10,8},{12,10},{14... | collective-permute-start | bytes 786440 | tf_op jit(solution)/shard_map/ppermute | solution.py:641
  167.5 11.2 %collective-permute-start.28 = (bf16[32,4096]{1,0:T(8,128)(2,1)S(1)}, bf16[32,4096]{1,0:T(8,128)(2,1)S(1)}, u32[]{:S(2)}, u32[]{:S(2)}) collective-permute-start(bf16[32,4096]{1,0:T(8,128)(2,1)S(1)} %add_convert_fusion.10), channel_id=1, source_target_pairs={{0,2},{2,4},{4,6},{6,7},{7,5},{5,3},{3,1},{1,0},{8,10},{10,12},{12... | collective-permute-start | bytes 786440 | tf_op jit(solution)/shard_map/ppermute | solution.py:641
  167.7 15.9 %collective-permute-start.32 = (bf16[32,4096]{1,0:T(8,128)(2,1)S(1)}, bf16[32,4096]{1,0:T(8,128)(2,1)S(1)}, u32[]{:S(2)}, u32[]{:S(2)}) collective-permute-start(bf16[32,4096]{1,0:T(8,128)(2,1)S(1)} %add_convert_fusion.7), channel_id=1, source_target_pairs={{2,0},{4,2},{6,4},{7,6},{5,7},{3,5},{1,3},{0,1},{10,8},{12,10},{14... | collective-permute-start | bytes 786440 | tf_op jit(solution)/shard_map/ppermute | solution.py:641
  173.1 13.4 %collective-permute-start.35 = (bf16[32,4096]{1,0:T(8,128)(2,1)S(1)}, bf16[32,4096]{1,0:T(8,128)(2,1)S(1)}, u32[]{:S(2)}, u32[]{:S(2)}) collective-permute-start(bf16[32,4096]{1,0:T(8,128)(2,1)S(1)} %add_convert_fusion.4), channel_id=1, source_target_pairs={{0,2},{2,4},{4,6},{6,7},{7,5},{5,3},{3,1},{1,0},{8,10},{10,12},{12... | collective-permute-start | bytes 786440 | tf_op jit(solution)/shard_map/ppermute | solution.py:641
  173.3 8.2 %collective-permute-start.38 = (bf16[32,4096]{1,0:T(8,128)(2,1)S(1)}, bf16[32,4096]{1,0:T(8,128)(2,1)S(1)}, u32[]{:S(2)}, u32[]{:S(2)}) collective-permute-start(bf16[32,4096]{1,0:T(8,128)(2,1)S(1)} %add_convert_fusion.2), channel_id=1, source_target_pairs={{2,0},{4,2},{6,4},{7,6},{5,7},{3,5},{1,3},{0,1},{10,8},{12,10},{14... | collective-permute-start | bytes 786440 | tf_op jit(solution)/shard_map/ppermute | solution.py:641
  178.7 7.7 %collective-permute-start.29 = (bf16[32,4096]{1,0:T(8,128)(2,1)S(1)}, bf16[32,4096]{1,0:T(8,128)(2,1)S(1)}, u32[]{:S(2)}, u32[]{:S(2)}) collective-permute-start(bf16[32,4096]{1,0:T(8,128)(2,1)S(1)} %add_convert_fusion.9), channel_id=1, source_target_pairs={{0,2},{2,4},{4,6},{6,7},{7,5},{5,3},{3,1},{1,0},{8,10},{10,12},{12... | collective-permute-start | bytes 786440 | tf_op jit(solution)/shard_map/ppermute | solution.py:641
  181.6 6.4 %collective-permute-start.39 = (bf16[32,4096]{1,0:T(8,128)(2,1)S(1)}, bf16[32,4096]{1,0:T(8,128)(2,1)S(1)}, u32[]{:S(2)}, u32[]{:S(2)}) collective-permute-start(bf16[32,4096]{1,0:T(8,128)(2,1)S(1)} %add_convert_fusion.1), channel_id=1, source_target_pairs={{2,0},{4,2},{6,4},{7,6},{5,7},{3,5},{1,3},{0,1},{10,8},{12,10},{14... | collective-permute-start | bytes 786440 | tf_op jit(solution)/shard_map/ppermute | solution.py:641

commit v15 on v14

--- a/solution.py
+++ b/solution.py
@@ -232,20 +232,26 @@
     return pieces
 
 
-def attend_kernel(n_chunks, with_new, n_tiles, tile_q, first_tile, first_ref, pos_ref, odd_ref, *refs):
+def attend_kernel(
+    n_chunks, offset, packs, has_state, with_new, n_tiles, tile_q, first_tile, first_ref, pos_ref, odd_ref, *refs
+):
     refs = list(refs)
     take = lambda count: [refs.pop(0) for _ in range(count)]
     chunks = take(n_chunks)
     dead_ref, qpos_ref, queries = take(3)
+    if has_state:
+        old_top, old_total, old_summed = take(3)
     if with_new:
         cos_ref, sin_ref, new_a, new_b = take(4)
+    if packs:
+        (packed,) = take(1)
+    top, total, summed, values = take(4)
     if with_new:
-        top, total, summed, values, new_key, new_value = take(6)
-    else:
-        packed, top, total, summed, values = take(5)
+        new_key, new_value = take(2)
     together = min(PAIR, n_tiles)
     n_pairs = n_tiles // together
     tokens = chunks[0].shape[2]
+    all_chunks = dead_ref.shape[1] // tokens
     scale = math.log2(math.e) / math.sqrt(HD)
 
     for chunk in range(n_chunks):
@@ -289,9 +295,14 @@
     def _(pair):
         tiles = [pair * together + i for i in range(together)]
         for tile in tiles:
-            top[tile] = jnp.full(top.shape[1:], MASKED, jnp.float32)
-            total[tile] = jnp.zeros(total.shape[1:], jnp.float32)
-            summed[tile] = jnp.zeros(summed.shape[1:], jnp.float32)
+            if has_state:
+                top[tile] = old_top[tile]
+                total[tile] = old_total[tile]
+                summed[tile] = old_summed[tile]
+            else:
+                top[tile] = jnp.full(top.shape[1:], MASKED, jnp.float32)
+                total[tile] = jnp.zeros(total.shape[1:], jnp.float32)
+                summed[tile] = jnp.zeros(summed.shape[1:], jnp.float32)
         if with_new:
             fresh = []
             for tile in tiles:
@@ -306,7 +317,7 @@
 
         @pl.loop(0, DOCS)
         def _(doc):
-            firsts = [first_ref[doc * n_chunks + chunk] for chunk in range(n_chunks)]
+            firsts = [first_ref[doc * all_chunks + offset + chunk] for chunk in range(n_chunks)]
             lowest = functools.reduce(jnp.minimum, firsts)
             highest = functools.reduce(jnp.maximum, firsts)
             reach = highest + tokens - 1
@@ -318,8 +329,9 @@
                     parts = []
                     for chunk in members:
                         span = slice(chunk * tokens, (chunk + 1) * tokens)
+                        dead_span = slice((offset + chunk) * tokens, (offset + chunk + 1) * tokens)
                         keys = jnp.concatenate(
-                            [chunks[chunk][0, doc], dead_ref[doc, span, :]], axis=1
+                            [chunks[chunk][0, doc], dead_ref[doc, dead_span, :]], axis=1
                         )
                         scores = jnp.dot(keys, extended, preferred_element_type=jnp.float32)
                         if masked:
@@ -353,7 +365,7 @@
                 def _():
                     visit(True, [chunk])
 
-        if not with_new:
+        if packs:
             for tile in tiles:
                 extra = jnp.concatenate(
                     split_exact(top[tile])
@@ -364,33 +376,40 @@
                 packed[tile] = jnp.concatenate([summed[tile], extra], axis=0).astype(jnp.bfloat16)
 
 
-def attend(chunks, dead, first_pos, selected, q_pos, odd, queries, first_tile, n_tiles, fresh):
+def attend(chunks, offset, metadata, queries, first_tile, n_tiles, state=(), fresh=(), packs=False):
+    dead, first_pos, selected, q_pos, odd = metadata
     n_chunks = len(chunks)
     tokens = chunks[0].shape[2]
     tile_q = SEL // q_pos.shape[0]
     smem = pl.BlockSpec(memory_space=pltpu.SMEM)
     vmem = pl.BlockSpec(memory_space=pltpu.VMEM)
-    operands = [first_pos, selected, odd, *chunks, dead, q_pos, queries, *fresh]
-    state = [((n_tiles, 1, TILE_COLS), jnp.float32)] * 2
-    state += [((n_tiles, HD, TILE_COLS), jnp.float32)]
-    values = ((DOCS, HD, n_chunks * tokens), jnp.bfloat16)
+    operands = [first_pos, selected, odd, *chunks, dead, q_pos, queries, *state, *fresh]
+    outs = [((n_tiles, 1, TILE_COLS), jnp.float32)] * 2
+    outs += [((n_tiles, HD, TILE_COLS), jnp.float32)]
+    scratch = [((DOCS, HD, n_chunks * tokens), jnp.bfloat16)]
+    if packs:
+        outs, scratch = [((n_tiles, HD + STATS, TILE_COLS), jnp.bfloat16)], outs + scratch
     if fresh:
-        outs = state
-        scratch = [values, ((SEL, HD), jnp.bfloat16), ((HD, SEL), jnp.bfloat16)]
-    else:
-        outs = [((n_tiles, HD + STATS, TILE_COLS), jnp.bfloat16)]
-        scratch = state + [values]
+        scratch += [((SEL, HD), jnp.bfloat16), ((HD, SEL), jnp.bfloat16)]
     pairs = n_tiles * TILE_COLS * DOCS * n_chunks * tokens // 2
     return pl.pallas_call(
         functools.partial(
-            attend_kernel, n_chunks, bool(fresh), n_tiles, tile_q, first_tile
+            attend_kernel,
+            n_chunks,
+            offset,
+            packs,
+            bool(state),
+            bool(fresh),
+            n_tiles,
+            tile_q,
+            first_tile,
         ),
         in_specs=[smem] * 3 + [vmem] * (len(operands) - 3),
         out_specs=[vmem] * len(outs),
         out_shape=[jax.ShapeDtypeStruct(*s) for s in outs],
         scratch_shapes=[pltpu.VMEM(*s) for s in scratch],
         compiler_params=megabytes(16),
-        cost_estimate=cost(1, 1) if fresh else cost(4 * pairs * HD, 0, pairs),
+        cost_estimate=cost(4 * pairs * HD, 0, pairs) if packs else cost(1, 1),
         name="attend",
     )(*operands)
 
@@ -600,30 +619,28 @@
             for kind in range(2)
         ]
 
-    def exchange(kept):
-        got = {
-            j: lax.ppermute(kept[j], "tp", [(i, i ^ j) for i in range(tp_size)])
-            for j in range(1, middle)
-        }
-        return [kept[0]] + [got[j] for j in range(1, middle)]
-
-    kept = list(sent[middle:])
+    def exchange(keys, j):
+        return lax.ppermute(keys, "tp", [(i, i ^ j) for i in range(tp_size)])
+
+    n_tiles = queries.shape[0]
+    metadata = (dead, first_pos, selected, q_pos, odd)
+    own, kept = list(sent[:middle]), list(sent[middle:])
     kept[-1], queries = lax.optimization_barrier((kept[-1], queries))
-    own, partners = sent[:middle], exchange(kept)
-    own, *partners[1:-1] = lax.optimization_barrier((own, *partners[1:-1]))
-    chunks = [exchange(own), partners]
-    n_tiles = queries.shape[0]
-
-    metadata = (dead, first_pos, selected, q_pos, odd)
+    partners = [kept[0]] + [exchange(kept[j], j) for j in range(1, middle)]
+    near = attend([own[0], exchange(own[1], 1)], 0, metadata, queries, 0, n_tiles)
+    near, own, *partners[1:-1] = lax.optimization_barrier((near, own, *partners[1:-1]))
+    rest = [exchange(own[j], j) for j in range(2, middle)]
     their_queries, new = lax.optimization_barrier((their_queries, new))
     share = n_tiles // min(HALVES, n_tiles)
     theirs = [
         lax.ppermute(
-            attend(chunks[1], *metadata, their_queries, first, share, [])[0], "tp", across
+            attend(partners, 0, metadata, their_queries, first, share, packs=True)[0], "tp", across
         )
         for first in range(n_tiles - share, -1, -share)
     ][::-1]
-    mine = attend(chunks[0], *metadata, queries, 0, n_tiles, [cosine, sine_part, *new])
+    mine = attend(
+        rest, 2, metadata, queries, 0, n_tiles, near, (cosine, sine_part, *new)
+    )
     attention = merge(mine, theirs)
 
     finished = []

time: 191 us -> 189 us (0.990)
  starting transfers between devices: 67.4 us -> 46 us
  waiting for transfers between devices: 48.5 us -> 64.9 us
  Pallas kernels: 57.7 us -> 62 us
    ppermute x8, starting transfers between devices: 28.5 us -> 10 us  [the longest x6 7.93 us: exchange(): return lax.ppermute(keys, 'tp', [(i, i ^ j) for i in range(tp_size)])]
    ppermute x8, waiting for transfers between devices: 9.39 us -> 23 us  [the longest x6 23 us: exchange(): return lax.ppermute(keys, 'tp', [(i, i ^ j) for i in range(tp_size)])]
    pallas_call x3 -> x4, Pallas kernels: 30.3 us -> 34.6 us  [attend(): pl.pallas_call(functools.partial(attend_kernel, n_chunks, offset, packs,...]
    ppermute x1, starting transfers between devices: 3.21 us -> 0.35 us  [per_device(): lax.ppermute(second, 'tp', keys_to_odd)]
  transfers between devices with their start and end apart: 40 -> 40, of which waited for: 15 -> 16; matrix products, arithmetic and copies ran while one was open for 3% -> 3% of each run, Pallas kernels for 28% -> 30%
where the time goes in v15:
time: 189 us; the launch traced here: 188 us
  waiting for transfers between devices  64.9 us (34%)
  Pallas kernels  62 us (33%)
  starting transfers between devices  46 us (24%)
  local copies, waits for them, and re-layouts  7.6 us (4%)
  other arithmetic  7.25 us (4%)
    pallas_call x4, Pallas kernels, attend(): pl.pallas_call(functools.partial(attend_kernel, n_chunks, offset, packs,...  34.6 us
    ppermute x14, waiting for transfers between devices, per_device(): held = lax.ppermute(term.astype(jnp.bfloat16), 'tp', pairs)  23.4 us
    ppermute x6, waiting for transfers between devices, exchange(): return lax.ppermute(keys, 'tp', [(i, i ^ j) for i in range(tp_size)])  23 us
    ppermute x14, starting transfers between devices, per_device(): held = lax.ppermute(term.astype(jnp.bfloat16), 'tp', pairs)  15.4 us
    ppermute x7, waiting for transfers between devices, per_device(): held['behind'].append(lax.ppermute(held['behind'][-1], 'tp', back))  13.9 us
    pallas_call x2, Pallas kernels, project(): pl.pallas_call(functools.partial(project_kernel, len(blocks), chunk, is_l...  13.6 us
    ppermute x7, starting transfers between devices, per_device(): held['before'].append(lax.ppermute(held['before'][-1], 'tp', forth))  11.5 us
    pallas_call x2, Pallas kernels, project_out(): pl.pallas_call(functools.partial(out_kernel, n_blocks, chunk * width), in...  10.2 us
  transfers between devices with their start and end apart: 40, of which 16 were waited for; matrix products, arithmetic and copies ran while one was open for 3% of the time, Pallas kernels for 30%

profile of v15, /device:TPU:0, one launch (start us, length us, event | category | flops | bytes accessed | tf_op | source)
XLA Modules:
  0.0 188.2 jit_solution(6107385630074479432)
XLA Ops:
  0.0 1.2 fusion
  1.3 1.2 fusion.2
  2.5 5.5 %copy.16 = bf16[4,256,2,1024]{3,1,2,0:T(8,128)(2,1)} copy(bf16[4,256,2,1024]{3,2,1,0:T(2,128)(2,1)} %param.15) | data formatting | bytes 8388608 | tf_op jit(solution)/shard_map/optimization_barrier | solution.py:537
  8.5 2.6 %collective-permute-start = (bf16[32,4096]{1,0:T(8,128)(2,1)S(1)}, bf16[32,4096]{1,0:T(8,128)(2,1)S(1)}, u32[]{:S(2)}, u32[]{:S(2)}) collective-permute-start(bf16[32,4096]{1,0:T(8,128)(2,1)S(1)} %get-tuple-element.146.refs_0_), channel_id=1, source_target_pairs={{0,2},{2,4},{4,6},{6,7},{7,5},{5,3},{3,1},{1,0},{8,10},{10,12},{12... | collective-permute-start | bytes 786440 | tf_op jit(solution)/shard_map/ppermute | solution.py:569
  11.1 2.0 %collective-permute-start.6 = (bf16[32,4096]{1,0:T(8,128)(2,1)S(1)}, bf16[32,4096]{1,0:T(8,128)(2,1)S(1)}, u32[]{:S(2)}, u32[]{:S(2)}) collective-permute-start(bf16[32,4096]{1,0:T(8,128)(2,1)S(1)} %get-tuple-element.145.refs_0_), channel_id=1, source_target_pairs={{2,0},{4,2},{6,4},{7,6},{5,7},{3,5},{1,3},{0,1},{10,8},{12,10},{14... | collective-permute-start | bytes 786440 | tf_op jit(solution)/shard_map/ppermute | solution.py:571
  13.6 1.3 compare_reduce_fusion
  15.1 0.5 fusion.3
  15.6 2.6 %collective-permute-done.refs_1_ = bf16[32,4096]{1,0:T(8,128)(2,1)S(1)} collective-permute-done((bf16[32,4096]{1,0:T(8,128)(2,1)S(1)}, bf16[32,4096]{1,0:T(8,128)(2,1)S(1)}, u32[]{:S(2)}, u32[]{:S(2)}) %collective-permute-start) | collective-permute-done | bytes 262176 | tf_op jit(solution)/shard_map/ppermute | solution.py:569
  18.2 2.0 %collective-permute-start.1 = (bf16[32,4096]{1,0:T(8,128)(2,1)S(1)}, bf16[32,4096]{1,0:T(8,128)(2,1)S(1)}, u32[]{:S(2)}, u32[]{:S(2)}) collective-permute-start(bf16[32,4096]{1,0:T(8,128)(2,1)S(1)} %collective-permute-done.refs_1_), channel_id=1, source_target_pairs={{0,2},{2,4},{4,6},{6,7},{7,5},{5,3},{3,1},{1,0},{8,10},{10,12},{12... | collective-permute-start | bytes 786440 | tf_op jit(solution)/shard_map/ppermute | solution.py:569
  20.2 0.7 dynamic-slice_bitcast_fusion.place_ref
  21.1 4.1 %collective-permute-done.6.refs_2_ = bf16[32,4096]{1,0:T(8,128)(2,1)S(1)} collective-permute-done((bf16[32,4096]{1,0:T(8,128)(2,1)S(1)}, bf16[32,4096]{1,0:T(8,128)(2,1)S(1)}, u32[]{:S(2)}, u32[]{:S(2)}) %collective-permute-start.6) | collective-permute-done | bytes 262176 | tf_op jit(solution)/shard_map/ppermute | solution.py:571
  25.6 0.5 broadcast.179
  26.2 0.7 reduce.3
  27.0 1.7 collective-permute-start.13
  28.8 0.5 collective-permute-done.1.refs_3_
  29.3 0.6 broadcast_in_dim.23.refs_2_.refs_4_
  29.9 1.8 collective-permute-start.2
  31.8 1.6 collective-permute-start.7
  33.3 1.1 collective-permute-done.8.refs_4_
  34.7 5.4 %collective-permute-done.13.refs_4_ = bf16[32,4096]{1,0:T(8,128)(2,1)S(1)} collective-permute-done((bf16[32,4096]{1,0:T(8,128)(2,1)S(1)}, bf16[32,4096]{1,0:T(8,128)(2,1)S(1)}, u32[]{:S(2)}, u32[]{:S(2)}) %collective-permute-start.13) | collective-permute-done | bytes 262176 | tf_op jit(solution)/shard_map/ppermute | solution.py:571
  40.3 3.3 %select_docs.1 = (bf16[2,4,256,128]{3,2,1,0:T(8,128)(2,1)S(1)}, bf16[2,4,256,128]{3,2,1,0:T(8,128)(2,1)S(1)}, bf16[2,4,256,128]{3,2,1,0:T(8,128)(2,1)S(1)}, bf16...) custom-call(s32[4]{0:T(128)S(1)} %get-tuple-element.80.place_ref, ...), custom_call_target="tpu_custom_call" | custom-call | bytes 8388608 | tf_op jit(solution)/shard_map/select_docs/pallas_call | solution.py:215
  43.6 1.8 collective-permute-start.15
  45.4 1.6 collective-permute-start.9
  47.9 3.4 %collective-permute-done.14.refs_6_ = bf16[32,4096]{1,0:T(8,128)(2,1)S(1)} collective-permute-done((bf16[32,4096]{1,0:T(8,128)(2,1)S(1)}, bf16[32,4096]{1,0:T(8,128)(2,1)S(1)}, u32[]{:S(2)}, u32[]{:S(2)}) %collective-permute-start.14) | collective-permute-done | bytes 262176 | tf_op jit(solution)/shard_map/ppermute | solution.py:571
  51.5 1.3 collective-permute-done.15.refs_7_
  52.9 1.8 collective-permute-start.17
  54.7 6.4 %project.2 = (f32[256,256]{1,0:T(8,128)S(1)}, f32[256,1024]{1,0:T(8,128)S(1)}) custom-call(s32[8]{0:T(128)S(1)} %dynamic-slice_bitcast_fusion.place_ref, bf16[32,4096]{1,0:T(8,128)(2,1)S(1)} %get-tuple-element.146.refs_0_, bf16[32,4096]{1,0:T(8,128)(2,1)S(1)} %collective-permute-done.refs_1_, bf16[32,4096]{1,0:T(8,128)(2,1)S(1)} %collective-permute-done.12.refs_2_, ...), custom_call_target="tpu_custom_call" | custom-call | flops 2684354560 | bytes 12582912 | tf_op jit(solution)/shard_map/project/pallas_call | solution.py:173
  61.1 7.2 %project.3 = (bf16[256,128]{1,0:T(8,128)(2,1)S(1)}, bf16[256,128]{1,0:T(8,128)(2,1)S(1)}, bf16[8,128,256]{2,1,0:T(8,128)(2,1)S(1)}) custom-call(s32[8]{0:T(128)S(1)} %dynamic-slice_bitcast_fusion.place_ref, bf16[32,4096]{1,0:T(8,128)(2,1)S(1)} %get-tuple-element.145.refs_0_, bf16[32,4096]{1,0:T(8,128)(2,1)S(1)} %collective-permute-done.5.refs_1_, ...), custom_call_target="tpu_custom_call" | custom-call | flops 2684354560 | bytes 12582912 | tf_op jit(solution)/shard_map/project/pallas_call | solution.py:173
  68.3 2.7 %collective-permute-start.20 = (bf16[8,128,256]{2,1,0:T(8,128)(2,1)S(1)}, bf16[8,128,256]{2,1,0:T(8,128)(2,1)S(1)}, u32[]{:S(2)}, u32[]{:S(2)}) collective-permute-start(bf16[8,128,256]{2,1,0:T(8,128)(2,1)S(1)} %get-tuple-element.104.refs_4_), channel_id=1, source_target_pairs={{0,4},{1,5},{2,6},{3,7},{4,0},{5,1},{6,2},{7,3},{8,12},{9,13},{10,... | collective-permute-start | bytes 1572872 | tf_op jit(solution)/shard_map/ppermute | solution.py:608
  71.0 1.4 collective-permute-start.23
  72.4 0.7 collective-permute-start.21
  73.0 15.1 %collective-permute-done.16.refs_1_ = bf16[2,4,256,128]{3,2,1,0:T(8,128)(2,1)S(1)} collective-permute-done((bf16[2,4,256,128]{3,2,1,0:T(8,128)(2,1)S(1)}, bf16[2,4,256,128]{3,2,1,0:T(8,128)(2,1)S(1)}, u32[]{:S(2)}, u32[]{:S(2)}) %collective-permute-start.16) | collective-permute-done | bytes 524320 | tf_op jit(solution)/shard_map/ppermute | solution.py:623
  88.5 9.4 %attend.4 = (f32[8,1,256]{2,1,0:T(1,128)S(1)}, f32[8,1,256]{2,1,0:T(1,128)S(1)}, f32[8,128,256]{2,1,0:T(8,128)S(1)}) custom-call(s32[16]{0:T(128)S(1)} %select_n.48.first_ref, s32[256]{0:T(256)S(1)} %bitcast.24, s32[1]{0:T(128)} %bitcast.6.odd_ref, bf16[2,4,256,128]{3,2,1,0:T(8,128)(2,1)S(1)} %get-tuple-element.92.refs_0_, ...), custom_call_target="tpu_custom_call" | custom-call | flops 1 | bytes 1 | tf_op jit(solution)/shard_map/attend/pallas_call | solution.py:395
  98.0 4.0 %collective-permute-start.19 = (bf16[2,4,256,128]{3,2,1,0:T(8,128)(2,1)S(1)}, bf16[2,4,256,128]{3,2,1,0:T(8,128)(2,1)S(1)}, u32[]{:S(2)}, u32[]{:S(2)}) collective-permute-start(bf16[2,4,256,128]{3,2,1,0:T(8,128)(2,1)S(1)} %get-tuple-element.113), channel_id=1, source_target_pairs={{0,3},{1,2},{2,1},{3,0},{4,7},{5,6},{6,5},{7,4},{8,11},{9,10},{10,... | collective-permute-start | bytes 1572872 | tf_op jit(solution)/shard_map/ppermute | solution.py:623
  101.9 9.4 %attend.7 = bf16[4,144,256]{2,1,0:T(8,128)(2,1)S(1)} custom-call(s32[16]{0:T(128)S(1)} %select_n.48.first_ref, s32[256]{0:T(256)S(1)} %bitcast.25, s32[1]{0:T(128)} %bitcast.6.odd_ref, bf16[2,4,256,128]{3,2,1,0:T(8,128)(2,1)S(1)} %get-tuple-element.124.refs_0_, bf16[2,4,256,128]{3,2,1,0:T(8,128)(2,1)S(1)} %collective-permute-done.16.refs_1_, ...), custom_call_target="tpu_custom_call" | custom-call | flops 1073741824 | tf_op jit(solution)/shard_map/attend/pallas_call | solution.py:395
  111.3 1.1 collective-permute-start.25
  112.4 5.7 %attend.6 = bf16[4,144,256]{2,1,0:T(8,128)(2,1)S(1)} custom-call(s32[16]{0:T(128)S(1)} %select_n.48.first_ref, s32[256]{0:T(256)S(1)} %bitcast.26, s32[1]{0:T(128)} %bitcast.6.odd_ref, bf16[2,4,256,128]{3,2,1,0:T(8,128)(2,1)S(1)} %get-tuple-element.124.refs_0_, bf16[2,4,256,128]{3,2,1,0:T(8,128)(2,1)S(1)} %collective-permute-done.16.refs_1_, ...), custom_call_target="tpu_custom_call" | custom-call | flops 1073741824 | tf_op jit(solution)/shard_map/attend/pallas_call | solution.py:395
  118.1 1.0 collective-permute-start.24
  119.1 8.0 %collective-permute-done.19.refs_1_ = bf16[2,4,256,128]{3,2,1,0:T(8,128)(2,1)S(1)} collective-permute-done((bf16[2,4,256,128]{3,2,1,0:T(8,128)(2,1)S(1)}, bf16[2,4,256,128]{3,2,1,0:T(8,128)(2,1)S(1)}, u32[]{:S(2)}, u32[]{:S(2)}) %collective-permute-start.19) | collective-permute-done | bytes 524320 | tf_op jit(solution)/shard_map/ppermute | solution.py:623
  127.1 10.1 %attend.5 = (f32[8,1,256]{2,1,0:T(1,128)S(1)}, f32[8,1,256]{2,1,0:T(1,128)S(1)}, f32[8,128,256]{2,1,0:T(8,128)S(1)}) custom-call(s32[16]{0:T(128)S(1)} %select_n.48.first_ref, s32[256]{0:T(256)S(1)} %bitcast.27, s32[1]{0:T(128)} %bitcast.6.odd_ref, bf16[2,4,256,128]{3,2,1,0:T(8,128)(2,1)S(1)} %collective-permute-done.18.refs_0_, ...), custom_call_target="tpu_custom_call" | custom-call | flops 1 | bytes 1 | tf_op jit(solution)/shard_map/attend/pallas_call | solution.py:395
  137.6 5.1 %project_out.2 = (f32[32,4096]{1,0:T(8,128)S(1)}, f32[32,4096]{1,0:T(8,128)S(1)}, f32[32,4096]{1,0:T(8,128)S(1)}, f32[32,4096]{1,0:T(8,128)S(1)}, f32[32,4096]{1...) custom-call(s32[8]{0:T(128)S(1)} %dynamic-slice_bitcast_fusion.place_ref, ...), custom_call_target="tpu_custom_call" | custom-call | flops 2147483648 | bytes 13107200 | tf_op jit(solution)/shard_map/project_out/pallas_call | solution.py:488
  142.7 1.9 %collective-permute-start.26 = (bf16[32,4096]{1,0:T(8,128)(2,1)S(1)}, bf16[32,4096]{1,0:T(8,128)(2,1)S(1)}, u32[]{:S(2)}, u32[]{:S(2)}) collective-permute-start(bf16[32,4096]{1,0:T(8,128)(2,1)S(1)} %get-tuple-element.133), channel_id=1, source_target_pairs={{0,2},{2,4},{4,6},{6,7},{7,5},{5,3},{3,1},{1,0},{8,10},{10,12},{12... | collective-permute-start | bytes 786440 | tf_op jit(solution)/shard_map/ppermute | solution.py:658
  144.7 0.6 collective-permute-start.30
  145.3 5.1 %project_out.3 = (f32[32,4096]{1,0:T(8,128)S(1)}, f32[32,4096]{1,0:T(8,128)S(1)}, f32[32,4096]{1,0:T(8,128)S(1)}, f32[32,4096]{1,0:T(8,128)S(1)}, f32[32,4096]{1...) custom-call(s32[8]{0:T(128)S(1)} %dynamic-slice_bitcast_fusion.place_ref, ...), custom_call_target="tpu_custom_call" | custom-call | flops 2147483648 | bytes 13107200 | tf_op jit(solution)/shard_map/project_out/pallas_call | solution.py:488
  150.4 1.5 collective-permute-start.33
  151.9 0.6 collective-permute-start.36
  152.6 1.5 collective-permute-start.27
  154.1 0.6 collective-permute-start.31
  154.7 4.9 %collective-permute-done.33 = bf16[32,4096]{1,0:T(8,128)(2,1)S(1)} collective-permute-done((bf16[32,4096]{1,0:T(8,128)(2,1)S(1)}, bf16[32,4096]{1,0:T(8,128)(2,1)S(1)}, u32[]{:S(2)}, u32[]{:S(2)}) %collective-permute-start.33) | collective-permute-done | bytes 262176 | tf_op jit(solution)/shard_map/ppermute | solution.py:658
  159.7 1.5 collective-permute-start.34
  161.3 0.6 collective-permute-start.37
  161.9 3.4 %collective-permute-done.27 = bf16[32,4096]{1,0:T(8,128)(2,1)S(1)} collective-permute-done((bf16[32,4096]{1,0:T(8,128)(2,1)S(1)}, bf16[32,4096]{1,0:T(8,128)(2,1)S(1)}, u32[]{:S(2)}, u32[]{:S(2)}) %collective-permute-start.27) | collective-permute-done | bytes 262176 | tf_op jit(solution)/shard_map/ppermute | solution.py:658
  165.3 1.5 collective-permute-start.28
  166.9 0.6 collective-permute-start.32
  167.5 3.4 %collective-permute-done.34 = bf16[32,4096]{1,0:T(8,128)(2,1)S(1)} collective-permute-done((bf16[32,4096]{1,0:T(8,128)(2,1)S(1)}, bf16[32,4096]{1,0:T(8,128)(2,1)S(1)}, u32[]{:S(2)}, u32[]{:S(2)}) %collective-permute-start.34) | collective-permute-done | bytes 262176 | tf_op jit(solution)/shard_map/ppermute | solution.py:658
  171.0 1.5 collective-permute-start.35
  172.6 0.6 collective-permute-start.38
  173.2 3.4 %collective-permute-done.28 = bf16[32,4096]{1,0:T(8,128)(2,1)S(1)} collective-permute-done((bf16[32,4096]{1,0:T(8,128)(2,1)S(1)}, bf16[32,4096]{1,0:T(8,128)(2,1)S(1)}, u32[]{:S(2)}, u32[]{:S(2)}) %collective-permute-start.28) | collective-permute-done | bytes 262176 | tf_op jit(solution)/shard_map/ppermute | solution.py:658
  176.6 1.5 collective-permute-start.29
  178.1 2.6 %collective-permute-done.38 = bf16[32,4096]{1,0:T(8,128)(2,1)S(1)} collective-permute-done((bf16[32,4096]{1,0:T(8,128)(2,1)S(1)}, bf16[32,4096]{1,0:T(8,128)(2,1)S(1)}, u32[]{:S(2)}, u32[]{:S(2)}) %collective-permute-start.38) | collective-permute-done | bytes 262176 | tf_op jit(solution)/shard_map/ppermute | solution.py:658
  180.8 0.6 collective-permute-start.39
  181.4 1.8 collective-permute-done.29
  183.3 3.9 %collective-permute-done.39 = bf16[32,4096]{1,0:T(8,128)(2,1)S(1)} collective-permute-done((bf16[32,4096]{1,0:T(8,128)(2,1)S(1)}, bf16[32,4096]{1,0:T(8,128)(2,1)S(1)}, u32[]{:S(2)}, u32[]{:S(2)}) %collective-permute-start.39) | collective-permute-done | bytes 262176 | tf_op jit(solution)/shard_map/ppermute | solution.py:658
  187.3 0.8 pad_maximum_fusion
  (78 shorter events, 5.2 us)
Async XLA Ops:
  2.5 10.7 %copy-start = (s32[1,256]{1,0:T(1,128)S(1)}, s32[1,256]{1,0:T(1,128)}, u32[]{:S(2)}) copy-start(s32[1,256]{1,0:T(1,128)} %param.18) | copy-start | bytes 3076
  2.5 10.7 %copy-start.1 = (s32[1,4]{1,0:T(1,128)S(1)}, s32[1,4]{1,0:T(1,128)}, u32[]{:S(2)}) copy-start(s32[1,4]{1,0:T(1,128)} %param.17) | copy-start | bytes 52
  2.5 13.1 %copy-start.2 = (s32[4]{0:T(128)S(1)}, s32[4]{0:T(128)}, u32[]{:S(2)}) copy-start(s32[4]{0:T(128)} %param.16) | copy-start | bytes 52
  8.0 32.3 %collective-permute-start.3 = (bf16[4,2,256,1024]{3,2,1,0:T(8,128)(2,1)}, bf16[4,2,256,1024]{3,2,1,0:T(8,128)(2,1)}, u32[]{:S(2)}, u32[]{:S(2)}) collective-permute-start(bf16[4,2,256,1024]{3,2,1,0:T(8,128)(2,1)} %bitcast.21.refs_0_), channel_id=1, source_target_pairs={{8,0},{0,8},{9,1},{1,9},{10,2},{2,10},{11,3},{3,11},{12,4},{4,12},... | collective-permute-start | bytes 12582920 | tf_op jit(solution)/shard_map/ppermute | solution.py:578
  8.5 9.7 %collective-permute-start = (bf16[32,4096]{1,0:T(8,128)(2,1)S(1)}, bf16[32,4096]{1,0:T(8,128)(2,1)S(1)}, u32[]{:S(2)}, u32[]{:S(2)}) collective-permute-start(bf16[32,4096]{1,0:T(8,128)(2,1)S(1)} %get-tuple-element.146.refs_0_), channel_id=1, source_target_pairs={{0,2},{2,4},{4,6},{6,7},{7,5},{5,3},{3,1},{1,0},{8,10},{10,12},{12... | collective-permute-start | bytes 786440 | tf_op jit(solution)/shard_map/ppermute | solution.py:569
  11.1 15.9 %collective-permute-start.12 = (bf16[32,4096]{1,0:T(8,128)(2,1)S(1)}, bf16[32,4096]{1,0:T(8,128)(2,1)S(1)}, u32[]{:S(2)}, u32[]{:S(2)}) collective-permute-start(bf16[32,4096]{1,0:T(8,128)(2,1)S(1)} %get-tuple-element.146.refs_0_), channel_id=1, source_target_pairs={{2,0},{4,2},{6,4},{7,6},{5,7},{3,5},{1,3},{0,1},{10,8},{12,10},{14... | collective-permute-start | bytes 786440 | tf_op jit(solution)/shard_map/ppermute | solution.py:571
  11.1 14.0 %collective-permute-start.6 = (bf16[32,4096]{1,0:T(8,128)(2,1)S(1)}, bf16[32,4096]{1,0:T(8,128)(2,1)S(1)}, u32[]{:S(2)}, u32[]{:S(2)}) collective-permute-start(bf16[32,4096]{1,0:T(8,128)(2,1)S(1)} %get-tuple-element.145.refs_0_), channel_id=1, source_target_pairs={{2,0},{4,2},{6,4},{7,6},{5,7},{3,5},{1,3},{0,1},{10,8},{12,10},{14... | collective-permute-start | bytes 786440 | tf_op jit(solution)/shard_map/ppermute | solution.py:571
  13.1 18.6 %collective-permute-start.5 = (bf16[32,4096]{1,0:T(8,128)(2,1)S(1)}, bf16[32,4096]{1,0:T(8,128)(2,1)S(1)}, u32[]{:S(2)}, u32[]{:S(2)}) collective-permute-start(bf16[32,4096]{1,0:T(8,128)(2,1)S(1)} %get-tuple-element.145.refs_0_), channel_id=1, source_target_pairs={{0,2},{2,4},{4,6},{6,7},{7,5},{5,3},{3,1},{1,0},{8,10},{10,12},{12... | collective-permute-start | bytes 786440 | tf_op jit(solution)/shard_map/ppermute | solution.py:569
  18.2 11.1 %collective-permute-start.1 = (bf16[32,4096]{1,0:T(8,128)(2,1)S(1)}, bf16[32,4096]{1,0:T(8,128)(2,1)S(1)}, u32[]{:S(2)}, u32[]{:S(2)}) collective-permute-start(bf16[32,4096]{1,0:T(8,128)(2,1)S(1)} %collective-permute-done.refs_1_), channel_id=1, source_target_pairs={{0,2},{2,4},{4,6},{6,7},{7,5},{5,3},{3,1},{1,0},{8,10},{10,12},{12... | collective-permute-start | bytes 786440 | tf_op jit(solution)/shard_map/ppermute | solution.py:569
  25.2 9.2 %collective-permute-start.8 = (bf16[32,4096]{1,0:T(8,128)(2,1)S(1)}, bf16[32,4096]{1,0:T(8,128)(2,1)S(1)}, u32[]{:S(2)}, u32[]{:S(2)}) collective-permute-start(bf16[32,4096]{1,0:T(8,128)(2,1)S(1)} %collective-permute-done.6.refs_2_), channel_id=1, source_target_pairs={{2,0},{4,2},{6,4},{7,6},{5,7},{3,5},{1,3},{0,1},{10,8},{12,10},{14... | collective-permute-start | bytes 786440 | tf_op jit(solution)/shard_map/ppermute | solution.py:571
  27.0 13.0 %collective-permute-start.13 = (bf16[32,4096]{1,0:T(8,128)(2,1)S(1)}, bf16[32,4096]{1,0:T(8,128)(2,1)S(1)}, u32[]{:S(2)}, u32[]{:S(2)}) collective-permute-start(bf16[32,4096]{1,0:T(8,128)(2,1)S(1)} %collective-permute-done.12.refs_2_), channel_id=1, source_target_pairs={{2,0},{4,2},{6,4},{7,6},{5,7},{3,5},{1,3},{0,1},{10,8},{12,10},{14... | collective-permute-start | bytes 786440 | tf_op jit(solution)/shard_map/ppermute | solution.py:571
  29.9 13.7 %collective-permute-start.2 = (bf16[32,4096]{1,0:T(8,128)(2,1)S(1)}, bf16[32,4096]{1,0:T(8,128)(2,1)S(1)}, u32[]{:S(2)}, u32[]{:S(2)}) collective-permute-start(bf16[32,4096]{1,0:T(8,128)(2,1)S(1)} %collective-permute-done.1.refs_3_), channel_id=1, source_target_pairs={{0,2},{2,4},{4,6},{6,7},{7,5},{5,3},{3,1},{1,0},{8,10},{10,12},{12... | collective-permute-start | bytes 786440 | tf_op jit(solution)/shard_map/ppermute | solution.py:569
  31.8 13.7 %collective-permute-start.7 = (bf16[32,4096]{1,0:T(8,128)(2,1)S(1)}, bf16[32,4096]{1,0:T(8,128)(2,1)S(1)}, u32[]{:S(2)}, u32[]{:S(2)}) collective-permute-start(bf16[32,4096]{1,0:T(8,128)(2,1)S(1)} %collective-permute-done.5.refs_1_), channel_id=1, source_target_pairs={{0,2},{2,4},{4,6},{6,7},{7,5},{5,3},{3,1},{1,0},{8,10},{10,12},{12... | collective-permute-start | bytes 786440 | tf_op jit(solution)/shard_map/ppermute | solution.py:569
  34.4 12.6 %collective-permute-start.10 = (bf16[32,4096]{1,0:T(8,128)(2,1)S(1)}, bf16[32,4096]{1,0:T(8,128)(2,1)S(1)}, u32[]{:S(2)}, u32[]{:S(2)}) collective-permute-start(bf16[32,4096]{1,0:T(8,128)(2,1)S(1)} %collective-permute-done.8.refs_4_), channel_id=1, source_target_pairs={{2,0},{4,2},{6,4},{7,6},{5,7},{3,5},{1,3},{0,1},{10,8},{12,10},{14... | collective-permute-start | bytes 786440 | tf_op jit(solution)/shard_map/ppermute | solution.py:571
  40.1 11.2 %collective-permute-start.14 = (bf16[32,4096]{1,0:T(8,128)(2,1)S(1)}, bf16[32,4096]{1,0:T(8,128)(2,1)S(1)}, u32[]{:S(2)}, u32[]{:S(2)}) collective-permute-start(bf16[32,4096]{1,0:T(8,128)(2,1)S(1)} %collective-permute-done.13.refs_4_), channel_id=1, source_target_pairs={{2,0},{4,2},{6,4},{7,6},{5,7},{3,5},{1,3},{0,1},{10,8},{12,10},{14... | collective-permute-start | bytes 786440 | tf_op jit(solution)/shard_map/ppermute | solution.py:571
  43.6 9.3 %collective-permute-start.15 = (bf16[32,4096]{1,0:T(8,128)(2,1)S(1)}, bf16[32,4096]{1,0:T(8,128)(2,1)S(1)}, u32[]{:S(2)}, u32[]{:S(2)}) collective-permute-start(bf16[32,4096]{1,0:T(8,128)(2,1)S(1)} %collective-permute-done.2.refs_5_), channel_id=1, source_target_pairs={{0,2},{2,4},{4,6},{6,7},{7,5},{5,3},{3,1},{1,0},{8,10},{10,12},{12... | collective-permute-start | bytes 786440 | tf_op jit(solution)/shard_map/ppermute | solution.py:569
  45.4 15.6 %collective-permute-start.9 = (bf16[32,4096]{1,0:T(8,128)(2,1)S(1)}, bf16[32,4096]{1,0:T(8,128)(2,1)S(1)}, u32[]{:S(2)}, u32[]{:S(2)}) collective-permute-start(bf16[32,4096]{1,0:T(8,128)(2,1)S(1)} %collective-permute-done.7.refs_3_), channel_id=1, source_target_pairs={{0,2},{2,4},{4,6},{6,7},{7,5},{5,3},{3,1},{1,0},{8,10},{10,12},{12... | collective-permute-start | bytes 786440 | tf_op jit(solution)/shard_map/ppermute | solution.py:569
  47.0 14.1 %collective-permute-start.11 = (bf16[32,4096]{1,0:T(8,128)(2,1)S(1)}, bf16[32,4096]{1,0:T(8,128)(2,1)S(1)}, u32[]{:S(2)}, u32[]{:S(2)}) collective-permute-start(bf16[32,4096]{1,0:T(8,128)(2,1)S(1)} %collective-permute-done.10.refs_6_), channel_id=1, source_target_pairs={{2,0},{4,2},{6,4},{7,6},{5,7},{3,5},{1,3},{0,1},{10,8},{12,10},{14... | collective-permute-start | bytes 786440 | tf_op jit(solution)/shard_map/ppermute | solution.py:571
  47.5 24.9 %collective-permute-start.4 = (bf16[2,4,256,128]{3,2,1,0:T(8,128)(2,1)S(1)}, bf16[2,4,256,128]{3,2,1,0:T(8,128)(2,1)S(1)}, u32[]{:S(2)}, u32[]{:S(2)}) collective-permute-start(bf16[2,4,256,128]{3,2,1,0:T(8,128)(2,1)S(1)} %get-tuple-element.93), channel_id=1, source_target_pairs={{0,1},{1,0},{2,3},{3,2},{4,5},{5,4},{6,7},{7,6},{8,9},{9,8},{10,11... | collective-permute-start | bytes 1572872 | tf_op jit(solution)/shard_map/ppermute | solution.py:623
  51.3 36.8 %collective-permute-start.16 = (bf16[2,4,256,128]{3,2,1,0:T(8,128)(2,1)S(1)}, bf16[2,4,256,128]{3,2,1,0:T(8,128)(2,1)S(1)}, u32[]{:S(2)}, u32[]{:S(2)}) collective-permute-start(bf16[2,4,256,128]{3,2,1,0:T(8,128)(2,1)S(1)} %get-tuple-element.110), channel_id=1, source_target_pairs={{0,1},{1,0},{2,3},{3,2},{4,5},{5,4},{6,7},{7,6},{8,9},{9,8},{10,11... | collective-permute-start | bytes 1572872 | tf_op jit(solution)/shard_map/ppermute | solution.py:623
  52.9 45.0 %collective-permute-start.17 = (bf16[2,4,256,128]{3,2,1,0:T(8,128)(2,1)S(1)}, bf16[2,4,256,128]{3,2,1,0:T(8,128)(2,1)S(1)}, u32[]{:S(2)}, u32[]{:S(2)}) collective-permute-start(bf16[2,4,256,128]{3,2,1,0:T(8,128)(2,1)S(1)} %get-tuple-element.111), channel_id=1, source_target_pairs={{0,2},{1,3},{2,0},{3,1},{4,6},{5,7},{6,4},{7,5},{8,10},{9,11},{10,... | collective-permute-start | bytes 1572872 | tf_op jit(solution)/shard_map/ppermute | solution.py:623
  68.3 33.6 %collective-permute-start.20 = (bf16[8,128,256]{2,1,0:T(8,128)(2,1)S(1)}, bf16[8,128,256]{2,1,0:T(8,128)(2,1)S(1)}, u32[]{:S(2)}, u32[]{:S(2)}) collective-permute-start(bf16[8,128,256]{2,1,0:T(8,128)(2,1)S(1)} %get-tuple-element.104.refs_4_), channel_id=1, source_target_pairs={{0,4},{1,5},{2,6},{3,7},{4,0},{5,1},{6,2},{7,3},{8,12},{9,13},{10,... | collective-permute-start | bytes 1572872 | tf_op jit(solution)/shard_map/ppermute | solution.py:608
  71.0 31.0 %collective-permute-start.23 = (bf16[2,4,256,128]{3,2,1,0:T(8,128)(2,1)S(1)}, bf16[2,4,256,128]{3,2,1,0:T(8,128)(2,1)S(1)}, u32[]{:S(2)}, u32[]{:S(2)}) collective-permute-start(bf16[2,4,256,128]{3,2,1,0:T(8,128)(2,1)S(1)} %get-tuple-element.127), channel_id=1, source_target_pairs={{0,3},{1,2},{2,1},{3,0},{4,7},{5,6},{6,5},{7,4},{8,11},{9,10},{10,... | collective-permute-start | bytes 1572872 | tf_op jit(solution)/shard_map/ppermute | solution.py:623
  72.4 25.6 %collective-permute-start.21 = (bf16[256,128]{1,0:T(8,128)(2,1)S(1)}, bf16[256,128]{1,0:T(8,128)(2,1)S(1)}, u32[]{:S(2)}, u32[]{:S(2)}) collective-permute-start(bf16[256,128]{1,0:T(8,128)(2,1)S(1)} %get-tuple-element.117), channel_id=1, source_target_pairs={{0,0},{1,2},{2,4},{3,6},{4,1},{5,3},{6,5},{7,7},{8,8},{9,10},{10,1... | collective-permute-start | bytes 196616 | tf_op jit(solution)/shard_map/ppermute | solution.py:613
  88.1 13.8 %collective-permute-start.22 = (bf16[256,128]{1,0:T(8,128)(2,1)S(1)}, bf16[256,128]{1,0:T(8,128)(2,1)S(1)}, u32[]{:S(2)}, u32[]{:S(2)}) collective-permute-start(bf16[256,128]{1,0:T(8,128)(2,1)S(1)} %get-tuple-element.118), channel_id=1, source_target_pairs={{0,1},{1,3},{2,5},{3,7},{4,0},{5,2},{6,4},{7,6},{8,9},{9,11},{10,1... | collective-permute-start | bytes 196616 | tf_op jit(solution)/shard_map/ppermute | solution.py:613
  97.9 21.2 %collective-permute-start.18 = (bf16[2,4,256,128]{3,2,1,0:T(8,128)(2,1)S(1)}, bf16[2,4,256,128]{3,2,1,0:T(8,128)(2,1)S(1)}, u32[]{:S(2)}, u32[]{:S(2)}) collective-permute-start(bf16[2,4,256,128]{3,2,1,0:T(8,128)(2,1)S(1)} %get-tuple-element.112), channel_id=1, source_target_pairs={{0,2},{1,3},{2,0},{3,1},{4,6},{5,7},{6,4},{7,5},{8,10},{9,11},{10,... | collective-permute-start | bytes 1572872 | tf_op jit(solution)/shard_map/ppermute | solution.py:623
  98.0 29.1 %collective-permute-start.19 = (bf16[2,4,256,128]{3,2,1,0:T(8,128)(2,1)S(1)}, bf16[2,4,256,128]{3,2,1,0:T(8,128)(2,1)S(1)}, u32[]{:S(2)}, u32[]{:S(2)}) collective-permute-start(bf16[2,4,256,128]{3,2,1,0:T(8,128)(2,1)S(1)} %get-tuple-element.113), channel_id=1, source_target_pairs={{0,3},{1,2},{2,1},{3,0},{4,7},{5,6},{6,5},{7,4},{8,11},{9,10},{10,... | collective-permute-start | bytes 1572872 | tf_op jit(solution)/shard_map/ppermute | solution.py:623
  111.3 25.9 %collective-permute-start.25 = (bf16[4,144,256]{2,1,0:T(8,128)(2,1)S(1)}, bf16[4,144,256]{2,1,0:T(8,128)(2,1)S(1)}, u32[]{:S(2)}, u32[]{:S(2)}) collective-permute-start(bf16[4,144,256]{2,1,0:T(8,128)(2,1)S(1)} %attend.7), channel_id=1, source_target_pairs={{0,4},{1,5},{2,6},{3,7},{4,0},{5,1},{6,2},{7,3},{8,12},{9,13},{10,... | collective-permute-start | bytes 884744 | tf_op jit(solution)/shard_map/ppermute | solution.py:636
  118.1 19.1 %collective-permute-start.24 = (bf16[4,144,256]{2,1,0:T(8,128)(2,1)S(1)}, bf16[4,144,256]{2,1,0:T(8,128)(2,1)S(1)}, u32[]{:S(2)}, u32[]{:S(2)}) collective-permute-start(bf16[4,144,256]{2,1,0:T(8,128)(2,1)S(1)} %attend.6), channel_id=1, source_target_pairs={{0,4},{1,5},{2,6},{3,7},{4,0},{5,1},{6,2},{7,3},{8,12},{9,13},{10,... | collective-permute-start | bytes 884744 | tf_op jit(solution)/shard_map/ppermute | solution.py:636
  142.7 9.8 %collective-permute-start.26 = (bf16[32,4096]{1,0:T(8,128)(2,1)S(1)}, bf16[32,4096]{1,0:T(8,128)(2,1)S(1)}, u32[]{:S(2)}, u32[]{:S(2)}) collective-permute-start(bf16[32,4096]{1,0:T(8,128)(2,1)S(1)} %get-tuple-element.133), channel_id=1, source_target_pairs={{0,2},{2,4},{4,6},{6,7},{7,5},{5,3},{3,1},{1,0},{8,10},{10,12},{12... | collective-permute-start | bytes 786440 | tf_op jit(solution)/shard_map/ppermute | solution.py:658
  144.7 9.4 %collective-permute-start.30 = (bf16[32,4096]{1,0:T(8,128)(2,1)S(1)}, bf16[32,4096]{1,0:T(8,128)(2,1)S(1)}, u32[]{:S(2)}, u32[]{:S(2)}) collective-permute-start(bf16[32,4096]{1,0:T(8,128)(2,1)S(1)} %convert_element_type.116), channel_id=1, source_target_pairs={{2,0},{4,2},{6,4},{7,6},{5,7},{3,5},{1,3},{0,1},{10,8},{12,10},{14... | collective-permute-start | bytes 786440 | tf_op jit(solution)/shard_map/ppermute | solution.py:658
  150.4 9.3 %collective-permute-start.33 = (bf16[32,4096]{1,0:T(8,128)(2,1)S(1)}, bf16[32,4096]{1,0:T(8,128)(2,1)S(1)}, u32[]{:S(2)}, u32[]{:S(2)}) collective-permute-start(bf16[32,4096]{1,0:T(8,128)(2,1)S(1)} %convert_element_type.123), channel_id=1, source_target_pairs={{0,2},{2,4},{4,6},{6,7},{7,5},{5,3},{3,1},{1,0},{8,10},{10,12},{12... | collective-permute-start | bytes 786440 | tf_op jit(solution)/shard_map/ppermute | solution.py:658
  151.9 9.3 %collective-permute-start.36 = (bf16[32,4096]{1,0:T(8,128)(2,1)S(1)}, bf16[32,4096]{1,0:T(8,128)(2,1)S(1)}, u32[]{:S(2)}, u32[]{:S(2)}) collective-permute-start(bf16[32,4096]{1,0:T(8,128)(2,1)S(1)} %get-tuple-element.144), channel_id=1, source_target_pairs={{2,0},{4,2},{6,4},{7,6},{5,7},{3,5},{1,3},{0,1},{10,8},{12,10},{14... | collective-permute-start | bytes 786440 | tf_op jit(solution)/shard_map/ppermute | solution.py:658
  152.6 12.7 %collective-permute-start.27 = (bf16[32,4096]{1,0:T(8,128)(2,1)S(1)}, bf16[32,4096]{1,0:T(8,128)(2,1)S(1)}, u32[]{:S(2)}, u32[]{:S(2)}) collective-permute-start(bf16[32,4096]{1,0:T(8,128)(2,1)S(1)} %add_convert_fusion.11), channel_id=1, source_target_pairs={{0,2},{2,4},{4,6},{6,7},{7,5},{5,3},{3,1},{1,0},{8,10},{10,12},{12... | collective-permute-start | bytes 786440 | tf_op jit(solution)/shard_map/ppermute | solution.py:658
  154.1 12.8 %collective-permute-start.31 = (bf16[32,4096]{1,0:T(8,128)(2,1)S(1)}, bf16[32,4096]{1,0:T(8,128)(2,1)S(1)}, u32[]{:S(2)}, u32[]{:S(2)}) collective-permute-start(bf16[32,4096]{1,0:T(8,128)(2,1)S(1)} %add_convert_fusion.8), channel_id=1, source_target_pairs={{2,0},{4,2},{6,4},{7,6},{5,7},{3,5},{1,3},{0,1},{10,8},{12,10},{14... | collective-permute-start | bytes 786440 | tf_op jit(solution)/shard_map/ppermute | solution.py:658
  159.7 11.2 %collective-permute-start.34 = (bf16[32,4096]{1,0:T(8,128)(2,1)S(1)}, bf16[32,4096]{1,0:T(8,128)(2,1)S(1)}, u32[]{:S(2)}, u32[]{:S(2)}) collective-permute-start(bf16[32,4096]{1,0:T(8,128)(2,1)S(1)} %add_convert_fusion.5), channel_id=1, source_target_pairs={{0,2},{2,4},{4,6},{6,7},{7,5},{5,3},{3,1},{1,0},{8,10},{10,12},{12... | collective-permute-start | bytes 786440 | tf_op jit(solution)/shard_map/ppermute | solution.py:658
  161.3 11.2 %collective-permute-start.37 = (bf16[32,4096]{1,0:T(8,128)(2,1)S(1)}, bf16[32,4096]{1,0:T(8,128)(2,1)S(1)}, u32[]{:S(2)}, u32[]{:S(2)}) collective-permute-start(bf16[32,4096]{1,0:T(8,128)(2,1)S(1)} %add_convert_fusion.3), channel_id=1, source_target_pairs={{2,0},{4,2},{6,4},{7,6},{5,7},{3,5},{1,3},{0,1},{10,8},{12,10},{14... | collective-permute-start | bytes 786440 | tf_op jit(solution)/shard_map/ppermute | solution.py:658
  165.3 11.2 %collective-permute-start.28 = (bf16[32,4096]{1,0:T(8,128)(2,1)S(1)}, bf16[32,4096]{1,0:T(8,128)(2,1)S(1)}, u32[]{:S(2)}, u32[]{:S(2)}) collective-permute-start(bf16[32,4096]{1,0:T(8,128)(2,1)S(1)} %add_convert_fusion.10), channel_id=1, source_target_pairs={{0,2},{2,4},{4,6},{6,7},{7,5},{5,3},{3,1},{1,0},{8,10},{10,12},{12... | collective-permute-start | bytes 786440 | tf_op jit(solution)/shard_map/ppermute | solution.py:658
  166.9 14.5 %collective-permute-start.32 = (bf16[32,4096]{1,0:T(8,128)(2,1)S(1)}, bf16[32,4096]{1,0:T(8,128)(2,1)S(1)}, u32[]{:S(2)}, u32[]{:S(2)}) collective-permute-start(bf16[32,4096]{1,0:T(8,128)(2,1)S(1)} %add_convert_fusion.7), channel_id=1, source_target_pairs={{2,0},{4,2},{6,4},{7,6},{5,7},{3,5},{1,3},{0,1},{10,8},{12,10},{14... | collective-permute-start | bytes 786440 | tf_op jit(solution)/shard_map/ppermute | solution.py:658
  171.0 12.3 %collective-permute-start.35 = (bf16[32,4096]{1,0:T(8,128)(2,1)S(1)}, bf16[32,4096]{1,0:T(8,128)(2,1)S(1)}, u32[]{:S(2)}, u32[]{:S(2)}) collective-permute-start(bf16[32,4096]{1,0:T(8,128)(2,1)S(1)} %add_convert_fusion.4), channel_id=1, source_target_pairs={{0,2},{2,4},{4,6},{6,7},{7,5},{5,3},{3,1},{1,0},{8,10},{10,12},{12... | collective-permute-start | bytes 786440 | tf_op jit(solution)/shard_map/ppermute | solution.py:658
  172.6 8.2 %collective-permute-start.38 = (bf16[32,4096]{1,0:T(8,128)(2,1)S(1)}, bf16[32,4096]{1,0:T(8,128)(2,1)S(1)}, u32[]{:S(2)}, u32[]{:S(2)}) collective-permute-start(bf16[32,4096]{1,0:T(8,128)(2,1)S(1)} %add_convert_fusion.2), channel_id=1, source_target_pairs={{2,0},{4,2},{6,4},{7,6},{5,7},{3,5},{1,3},{0,1},{10,8},{12,10},{14... | collective-permute-start | bytes 786440 | tf_op jit(solution)/shard_map/ppermute | solution.py:658
  176.6 6.6 %collective-permute-start.29 = (bf16[32,4096]{1,0:T(8,128)(2,1)S(1)}, bf16[32,4096]{1,0:T(8,128)(2,1)S(1)}, u32[]{:S(2)}, u32[]{:S(2)}) collective-permute-start(bf16[32,4096]{1,0:T(8,128)(2,1)S(1)} %add_convert_fusion.9), channel_id=1, source_target_pairs={{0,2},{2,4},{4,6},{6,7},{7,5},{5,3},{3,1},{1,0},{8,10},{10,12},{12... | collective-permute-start | bytes 786440 | tf_op jit(solution)/shard_map/ppermute | solution.py:658
  180.8 6.4 %collective-permute-start.39 = (bf16[32,4096]{1,0:T(8,128)(2,1)S(1)}, bf16[32,4096]{1,0:T(8,128)(2,1)S(1)}, u32[]{:S(2)}, u32[]{:S(2)}) collective-permute-start(bf16[32,4096]{1,0:T(8,128)(2,1)S(1)} %add_convert_fusion.1), channel_id=1, source_target_pairs={{2,0},{4,2},{6,4},{7,6},{5,7},{3,5},{1,3},{0,1},{10,8},{12,10},{14... | collective-permute-start | bytes 786440 | tf_op jit(solution)/shard_map/ppermute | solution.py:658

commit v16 on v15

--- a/solution.py
+++ b/solution.py
@@ -627,20 +627,19 @@
     own, kept = list(sent[:middle]), list(sent[middle:])
     kept[-1], queries = lax.optimization_barrier((kept[-1], queries))
     partners = [kept[0]] + [exchange(kept[j], j) for j in range(1, middle)]
-    near = attend([own[0], exchange(own[1], 1)], 0, metadata, queries, 0, n_tiles)
-    near, own, *partners[1:-1] = lax.optimization_barrier((near, own, *partners[1:-1]))
-    rest = [exchange(own[j], j) for j in range(2, middle)]
+    own, *partners[1:-1] = lax.optimization_barrier((own, *partners[1:-1]))
+    own = [own[0]] + [exchange(own[j], j) for j in range(1, middle)]
     their_queries, new = lax.optimization_barrier((their_queries, new))
     share = n_tiles // min(HALVES, n_tiles)
-    theirs = [
-        lax.ppermute(
-            attend(partners, 0, metadata, their_queries, first, share, packs=True)[0], "tp", across
-        )
-        for first in range(n_tiles - share, -1, -share)
-    ][::-1]
-    mine = attend(
-        rest, 2, metadata, queries, 0, n_tiles, near, (cosine, sine_part, *new)
+    theirs = []
+    for first in range(n_tiles - share, -1, -share):
+        (packed,) = attend(partners, 0, metadata, their_queries, first, share, packs=True)
+        theirs.insert(0, lax.ppermute(packed, "tp", across))
+    queries, _ = lax.optimization_barrier((queries, packed))
+    near = attend(
+        own[:2], 0, metadata, queries, 0, n_tiles, fresh=(cosine, sine_part, *new)
     )
+    mine = attend(own[2:], 2, metadata, queries, 0, n_tiles, near)
     attention = merge(mine, theirs)
 
     finished = []

time: 189 us -> 183 us (0.968)
  waiting for transfers between devices: 64.9 us -> 42.3 us
  starting transfers between devices: 46 us -> 64.8 us
    ppermute x6, waiting for transfers between devices: 23 us -> 0.02 us  [exchange(): return lax.ppermute(keys, 'tp', [(i, i ^ j) for i in range(tp_size)])]
    ppermute x6, starting transfers between devices: 7.93 us -> 25.2 us  [exchange(): return lax.ppermute(keys, 'tp', [(i, i ^ j) for i in range(tp_size)])]
    ppermute x1, starting transfers between devices: 0.35 us -> 3.2 us  [per_device(): lax.ppermute(second, 'tp', keys_to_odd)]
  transfers between devices with their start and end apart: 40 -> 40, of which waited for: 16 -> 17; matrix products, arithmetic and copies ran while one was open for 3% -> 3% of each run, Pallas kernels for 30% -> 30%
where the time goes in v16:
time: 183 us
  starting transfers between devices  64.8 us (35%)
  Pallas kernels  60.8 us (33%)
  waiting for transfers between devices  42.3 us (23%)
  local copies, waits for them, and re-layouts  7.6 us (4%)
  other arithmetic  7.25 us (4%)
    pallas_call x4, Pallas kernels, attend(): pl.pallas_call(functools.partial(attend_kernel, n_chunks, offset, packs,...  33.4 us
    ppermute x6, starting transfers between devices, exchange(): return lax.ppermute(keys, 'tp', [(i, i ^ j) for i in range(tp_size)])  25.2 us
    ppermute x14, waiting for transfers between devices, per_device(): held = lax.ppermute(term.astype(jnp.bfloat16), 'tp', pairs)  24.9 us
    ppermute x7, waiting for transfers between devices, per_device(): held['behind'].append(lax.ppermute(held['behind'][-1], 'tp', back))  13.9 us
    pallas_call x2, Pallas kernels, project(): pl.pallas_call(functools.partial(project_kernel, len(blocks), chunk, is_l...  13.6 us
    ppermute x14, starting transfers between devices, per_device(): held = lax.ppermute(term.astype(jnp.bfloat16), 'tp', pairs)  13.6 us
    ppermute x7, starting transfers between devices, per_device(): held['before'].append(lax.ppermute(held['before'][-1], 'tp', forth))  11.5 us
    pallas_call x2, Pallas kernels, project_out(): pl.pallas_call(functools.partial(out_kernel, n_blocks, chunk * width), in...  10.2 us
  transfers between devices with their start and end apart: 40, of which 17 were waited for; matrix products, arithmetic and copies ran while one was open for 3% of the time, Pallas kernels for 30%

profile of v16, /device:TPU:0, one launch (start us, length us, event | category | flops | bytes accessed | tf_op | source)
XLA Modules:
  0.0 183.2 jit_solution(16303836031548558269)
XLA Ops:
  0.0 1.2 fusion
  1.3 1.2 fusion.2
  2.5 5.5 %copy.16 = bf16[4,256,2,1024]{3,1,2,0:T(8,128)(2,1)} copy(bf16[4,256,2,1024]{3,2,1,0:T(2,128)(2,1)} %param.15) | data formatting | bytes 8388608 | tf_op jit(solution)/shard_map/optimization_barrier | solution.py:537
  8.0 0.5 collective-permute-start.3
  8.5 2.6 %collective-permute-start = (bf16[32,4096]{1,0:T(8,128)(2,1)S(1)}, bf16[32,4096]{1,0:T(8,128)(2,1)S(1)}, u32[]{:S(2)}, u32[]{:S(2)}) collective-permute-start(bf16[32,4096]{1,0:T(8,128)(2,1)S(1)} %get-tuple-element.146.refs_0_), channel_id=1, source_target_pairs={{0,2},{2,4},{4,6},{6,7},{7,5},{5,3},{3,1},{1,0},{8,10},{10,12},{12... | collective-permute-start | bytes 786440 | tf_op jit(solution)/shard_map/ppermute | solution.py:569
  11.1 2.0 %collective-permute-start.9 = (bf16[32,4096]{1,0:T(8,128)(2,1)S(1)}, bf16[32,4096]{1,0:T(8,128)(2,1)S(1)}, u32[]{:S(2)}, u32[]{:S(2)}) collective-permute-start(bf16[32,4096]{1,0:T(8,128)(2,1)S(1)} %get-tuple-element.145.refs_0_), channel_id=1, source_target_pairs={{2,0},{4,2},{6,4},{7,6},{5,7},{3,5},{1,3},{0,1},{10,8},{12,10},{14... | collective-permute-start | bytes 786440 | tf_op jit(solution)/shard_map/ppermute | solution.py:571
  13.6 1.3 compare_reduce_fusion
  15.1 0.5 fusion.3
  15.6 2.6 %collective-permute-done.refs_1_ = bf16[32,4096]{1,0:T(8,128)(2,1)S(1)} collective-permute-done((bf16[32,4096]{1,0:T(8,128)(2,1)S(1)}, bf16[32,4096]{1,0:T(8,128)(2,1)S(1)}, u32[]{:S(2)}, u32[]{:S(2)}) %collective-permute-start) | collective-permute-done | bytes 262176 | tf_op jit(solution)/shard_map/ppermute | solution.py:569
  18.2 2.0 %collective-permute-start.1 = (bf16[32,4096]{1,0:T(8,128)(2,1)S(1)}, bf16[32,4096]{1,0:T(8,128)(2,1)S(1)}, u32[]{:S(2)}, u32[]{:S(2)}) collective-permute-start(bf16[32,4096]{1,0:T(8,128)(2,1)S(1)} %collective-permute-done.refs_1_), channel_id=1, source_target_pairs={{0,2},{2,4},{4,6},{6,7},{7,5},{5,3},{3,1},{1,0},{8,10},{10,12},{12... | collective-permute-start | bytes 786440 | tf_op jit(solution)/shard_map/ppermute | solution.py:569
  20.2 0.7 dynamic-slice_bitcast_fusion.place_ref
  21.1 4.1 %collective-permute-done.9.refs_2_ = bf16[32,4096]{1,0:T(8,128)(2,1)S(1)} collective-permute-done((bf16[32,4096]{1,0:T(8,128)(2,1)S(1)}, bf16[32,4096]{1,0:T(8,128)(2,1)S(1)}, u32[]{:S(2)}, u32[]{:S(2)}) %collective-permute-start.9) | collective-permute-done | bytes 262176 | tf_op jit(solution)/shard_map/ppermute | solution.py:571
  25.6 0.5 broadcast.179
  26.2 0.7 reduce.3
  27.0 1.7 collective-permute-start.16
  28.8 0.5 collective-permute-done.1.refs_3_
  29.3 0.6 broadcast_in_dim.23.refs_4_.refs_2_
  29.9 1.8 %collective-permute-start.2 = (bf16[32,4096]{1,0:T(8,128)(2,1)S(1)}, bf16[32,4096]{1,0:T(8,128)(2,1)S(1)}, u32[]{:S(2)}, u32[]{:S(2)}) collective-permute-start(bf16[32,4096]{1,0:T(8,128)(2,1)S(1)} %collective-permute-done.1.refs_3_), channel_id=1, source_target_pairs={{0,2},{2,4},{4,6},{6,7},{7,5},{5,3},{3,1},{1,0},{8,10},{10,12},{12... | collective-permute-start | bytes 786440 | tf_op jit(solution)/shard_map/ppermute | solution.py:569
  31.8 1.6 collective-permute-start.10
  33.3 1.1 collective-permute-done.11.refs_4_
  34.7 5.4 %collective-permute-done.16.refs_4_ = bf16[32,4096]{1,0:T(8,128)(2,1)S(1)} collective-permute-done((bf16[32,4096]{1,0:T(8,128)(2,1)S(1)}, bf16[32,4096]{1,0:T(8,128)(2,1)S(1)}, u32[]{:S(2)}, u32[]{:S(2)}) %collective-permute-start.16) | collective-permute-done | bytes 262176 | tf_op jit(solution)/shard_map/ppermute | solution.py:571
  40.3 3.3 %select_docs.1 = (bf16[2,4,256,128]{3,2,1,0:T(8,128)(2,1)S(1)}, bf16[2,4,256,128]{3,2,1,0:T(8,128)(2,1)S(1)}, bf16[2,4,256,128]{3,2,1,0:T(8,128)(2,1)S(1)}, bf16...) custom-call(s32[4]{0:T(128)S(1)} %get-tuple-element.80.place_ref, ...), custom_call_target="tpu_custom_call" | custom-call | bytes 8388608 | tf_op jit(solution)/shard_map/select_docs/pallas_call | solution.py:215
  43.6 1.8 collective-permute-start.18
  45.4 1.6 collective-permute-start.12
  47.4 0.5 collective-permute-start.4
  47.9 3.4 %collective-permute-done.17.refs_6_ = bf16[32,4096]{1,0:T(8,128)(2,1)S(1)} collective-permute-done((bf16[32,4096]{1,0:T(8,128)(2,1)S(1)}, bf16[32,4096]{1,0:T(8,128)(2,1)S(1)}, u32[]{:S(2)}, u32[]{:S(2)}) %collective-permute-start.17) | collective-permute-done | bytes 262176 | tf_op jit(solution)/shard_map/ppermute | solution.py:571
  51.3 1.6 collective-permute-start.5
  52.9 6.4 %project.2 = (f32[256,256]{1,0:T(8,128)S(1)}, f32[256,1024]{1,0:T(8,128)S(1)}) custom-call(s32[8]{0:T(128)S(1)} %dynamic-slice_bitcast_fusion.place_ref, bf16[32,4096]{1,0:T(8,128)(2,1)S(1)} %get-tuple-element.146.refs_0_, bf16[32,4096]{1,0:T(8,128)(2,1)S(1)} %collective-permute-done.refs_1_, bf16[32,4096]{1,0:T(8,128)(2,1)S(1)} %collective-permute-done.15.refs_2_, ...), custom_call_target="tpu_custom_call" | custom-call | flops 2684354560 | bytes 12582912 | tf_op jit(solution)/shard_map/project/pallas_call | solution.py:173
  59.3 7.2 %project.3 = (bf16[256,128]{1,0:T(8,128)(2,1)S(1)}, bf16[256,128]{1,0:T(8,128)(2,1)S(1)}, bf16[8,128,256]{2,1,0:T(8,128)(2,1)S(1)}) custom-call(s32[8]{0:T(128)S(1)} %dynamic-slice_bitcast_fusion.place_ref, bf16[32,4096]{1,0:T(8,128)(2,1)S(1)} %get-tuple-element.145.refs_0_, bf16[32,4096]{1,0:T(8,128)(2,1)S(1)} %collective-permute-done.8.refs_1_, ...), custom_call_target="tpu_custom_call" | custom-call | flops 2684354560 | bytes 12582912 | tf_op jit(solution)/shard_map/project/pallas_call | solution.py:173
  66.5 2.6 %collective-permute-start.20 = (bf16[8,128,256]{2,1,0:T(8,128)(2,1)S(1)}, bf16[8,128,256]{2,1,0:T(8,128)(2,1)S(1)}, u32[]{:S(2)}, u32[]{:S(2)}) collective-permute-start(bf16[8,128,256]{2,1,0:T(8,128)(2,1)S(1)} %get-tuple-element.118.refs_4_), channel_id=1, source_target_pairs={{0,4},{1,5},{2,6},{3,7},{4,0},{5,1},{6,2},{7,3},{8,12},{9,13},{10,... | collective-permute-start | bytes 1572872 | tf_op jit(solution)/shard_map/ppermute | solution.py:608
  69.1 2.8 %collective-permute-start.19 = (bf16[2,4,256,128]{3,2,1,0:T(8,128)(2,1)S(1)}, bf16[2,4,256,128]{3,2,1,0:T(8,128)(2,1)S(1)}, u32[]{:S(2)}, u32[]{:S(2)}) collective-permute-start(bf16[2,4,256,128]{3,2,1,0:T(8,128)(2,1)S(1)} %get-tuple-element.114), channel_id=1, source_target_pairs={{0,3},{1,2},{2,1},{3,0},{4,7},{5,6},{6,5},{7,4},{8,11},{9,10},{10,... | collective-permute-start | bytes 1572872 | tf_op jit(solution)/shard_map/ppermute | solution.py:623
  71.9 0.7 collective-permute-start.21
  72.6 3.2 %collective-permute-start.22 = (bf16[256,128]{1,0:T(8,128)(2,1)S(1)}, bf16[256,128]{1,0:T(8,128)(2,1)S(1)}, u32[]{:S(2)}, u32[]{:S(2)}) collective-permute-start(bf16[256,128]{1,0:T(8,128)(2,1)S(1)} %get-tuple-element.116), channel_id=1, source_target_pairs={{0,1},{1,3},{2,5},{3,7},{4,0},{5,2},{6,4},{7,6},{8,9},{9,11},{10,1... | collective-permute-start | bytes 196616 | tf_op jit(solution)/shard_map/ppermute | solution.py:613
  76.1 18.6 %collective-permute-start.6 = (bf16[2,4,256,128]{3,2,1,0:T(8,128)(2,1)S(1)}, bf16[2,4,256,128]{3,2,1,0:T(8,128)(2,1)S(1)}, u32[]{:S(2)}, u32[]{:S(2)}) collective-permute-start(bf16[2,4,256,128]{3,2,1,0:T(8,128)(2,1)S(1)} %get-tuple-element.98), channel_id=1, source_target_pairs={{0,2},{1,3},{2,0},{3,1},{4,6},{5,7},{6,4},{7,5},{8,10},{9,11},{10,... | collective-permute-start | bytes 1572872 | tf_op jit(solution)/shard_map/ppermute | solution.py:623
  94.8 1.4 collective-permute-start.7
  96.2 8.9 %attend.7 = bf16[4,144,256]{2,1,0:T(8,128)(2,1)S(1)} custom-call(s32[16]{0:T(128)S(1)} %select_n.48.first_ref, s32[256]{0:T(256)S(1)} %bitcast.24, s32[1]{0:T(128)} %bitcast.6.odd_ref, bf16[2,4,256,128]{3,2,1,0:T(8,128)(2,1)S(1)} %get-tuple-element.111.refs_0_, bf16[2,4,256,128]{3,2,1,0:T(8,128)(2,1)S(1)} %collective-permute-done.4.refs_1_, ...), custom_call_target="tpu_custom_call" | custom-call | flops 1073741824 | tf_op jit(solution)/shard_map/attend/pallas_call | solution.py:395
  105.1 2.5 %collective-permute-start.25 = (bf16[4,144,256]{2,1,0:T(8,128)(2,1)S(1)}, bf16[4,144,256]{2,1,0:T(8,128)(2,1)S(1)}, u32[]{:S(2)}, u32[]{:S(2)}) collective-permute-start(bf16[4,144,256]{2,1,0:T(8,128)(2,1)S(1)} %attend.7), channel_id=1, source_target_pairs={{0,4},{1,5},{2,6},{3,7},{4,0},{5,1},{6,2},{7,3},{8,12},{9,13},{10,... | collective-permute-start | bytes 884744 | tf_op jit(solution)/shard_map/ppermute | solution.py:637
  107.6 5.7 %attend.4 = bf16[4,144,256]{2,1,0:T(8,128)(2,1)S(1)} custom-call(s32[16]{0:T(128)S(1)} %select_n.48.first_ref, s32[256]{0:T(256)S(1)} %bitcast.25, s32[1]{0:T(128)} %bitcast.6.odd_ref, bf16[2,4,256,128]{3,2,1,0:T(8,128)(2,1)S(1)} %get-tuple-element.111.refs_0_, bf16[2,4,256,128]{3,2,1,0:T(8,128)(2,1)S(1)} %collective-permute-done.4.refs_1_, ...), custom_call_target="tpu_custom_call" | custom-call | flops 1073741824 | tf_op jit(solution)/shard_map/attend/pallas_call | solution.py:395
  113.4 10.8 %attend.5 = (f32[8,1,256]{2,1,0:T(1,128)S(1)}, f32[8,1,256]{2,1,0:T(1,128)S(1)}, f32[8,128,256]{2,1,0:T(8,128)S(1)}) custom-call(s32[16]{0:T(128)S(1)} %select_n.48.first_ref, s32[256]{0:T(256)S(1)} %bitcast.26, s32[1]{0:T(128)} %bitcast.6.odd_ref, bf16[2,4,256,128]{3,2,1,0:T(8,128)(2,1)S(1)} %get-tuple-element.119.refs_0_, ...), custom_call_target="tpu_custom_call" | custom-call | flops 1 | bytes 1 | tf_op jit(solution)/shard_map/attend/pallas_call | solution.py:395
  124.2 8.0 %attend.6 = (f32[8,1,256]{2,1,0:T(1,128)S(1)}, f32[8,1,256]{2,1,0:T(1,128)S(1)}, f32[8,128,256]{2,1,0:T(8,128)S(1)}) custom-call(s32[16]{0:T(128)S(1)} %select_n.48.first_ref, s32[256]{0:T(256)S(1)} %bitcast.27, s32[1]{0:T(128)} %bitcast.6.odd_ref, bf16[2,4,256,128]{3,2,1,0:T(8,128)(2,1)S(1)} %collective-permute-done.6.refs_0_, ...), custom_call_target="tpu_custom_call" | custom-call | flops 1 | bytes 1 | tf_op jit(solution)/shard_map/attend/pallas_call | solution.py:395
  132.9 5.1 %project_out.2 = (f32[32,4096]{1,0:T(8,128)S(1)}, f32[32,4096]{1,0:T(8,128)S(1)}, f32[32,4096]{1,0:T(8,128)S(1)}, f32[32,4096]{1,0:T(8,128)S(1)}, f32[32,4096]{1...) custom-call(s32[8]{0:T(128)S(1)} %dynamic-slice_bitcast_fusion.place_ref, ...), custom_call_target="tpu_custom_call" | custom-call | flops 2147483648 | bytes 13107200 | tf_op jit(solution)/shard_map/project_out/pallas_call | solution.py:488
  138.0 0.6 collective-permute-start.26
  138.7 1.5 collective-permute-start.30
  140.2 5.1 %project_out.3 = (f32[32,4096]{1,0:T(8,128)S(1)}, f32[32,4096]{1,0:T(8,128)S(1)}, f32[32,4096]{1,0:T(8,128)S(1)}, f32[32,4096]{1,0:T(8,128)S(1)}, f32[32,4096]{1...) custom-call(s32[8]{0:T(128)S(1)} %dynamic-slice_bitcast_fusion.place_ref, ...), custom_call_target="tpu_custom_call" | custom-call | flops 2147483648 | bytes 13107200 | tf_op jit(solution)/shard_map/project_out/pallas_call | solution.py:488
  145.3 0.6 collective-permute-start.33
  145.9 1.5 collective-permute-start.36
  147.4 1.0 collective-permute-start.27
  148.5 1.1 collective-permute-start.31
  149.6 5.0 %collective-permute-done.33 = bf16[32,4096]{1,0:T(8,128)(2,1)S(1)} collective-permute-done((bf16[32,4096]{1,0:T(8,128)(2,1)S(1)}, bf16[32,4096]{1,0:T(8,128)(2,1)S(1)}, u32[]{:S(2)}, u32[]{:S(2)}) %collective-permute-start.33) | collective-permute-done | bytes 262176 | tf_op jit(solution)/shard_map/ppermute | solution.py:657
  154.6 0.6 collective-permute-start.34
  155.6 1.2 collective-permute-start.37
  156.8 3.4 %collective-permute-done.27 = bf16[32,4096]{1,0:T(8,128)(2,1)S(1)} collective-permute-done((bf16[32,4096]{1,0:T(8,128)(2,1)S(1)}, bf16[32,4096]{1,0:T(8,128)(2,1)S(1)}, u32[]{:S(2)}, u32[]{:S(2)}) %collective-permute-start.27) | collective-permute-done | bytes 262176 | tf_op jit(solution)/shard_map/ppermute | solution.py:657
  160.2 0.6 collective-permute-start.28
  161.2 1.2 collective-permute-start.32
  162.4 3.4 %collective-permute-done.34 = bf16[32,4096]{1,0:T(8,128)(2,1)S(1)} collective-permute-done((bf16[32,4096]{1,0:T(8,128)(2,1)S(1)}, bf16[32,4096]{1,0:T(8,128)(2,1)S(1)}, u32[]{:S(2)}, u32[]{:S(2)}) %collective-permute-start.34) | collective-permute-done | bytes 262176 | tf_op jit(solution)/shard_map/ppermute | solution.py:657
  165.9 0.6 collective-permute-start.35
  166.8 1.2 collective-permute-start.38
  168.0 3.4 %collective-permute-done.28 = bf16[32,4096]{1,0:T(8,128)(2,1)S(1)} collective-permute-done((bf16[32,4096]{1,0:T(8,128)(2,1)S(1)}, bf16[32,4096]{1,0:T(8,128)(2,1)S(1)}, u32[]{:S(2)}, u32[]{:S(2)}) %collective-permute-start.28) | collective-permute-done | bytes 262176 | tf_op jit(solution)/shard_map/ppermute | solution.py:657
  171.5 0.6 collective-permute-start.29
  172.1 3.3 %collective-permute-done.38 = bf16[32,4096]{1,0:T(8,128)(2,1)S(1)} collective-permute-done((bf16[32,4096]{1,0:T(8,128)(2,1)S(1)}, bf16[32,4096]{1,0:T(8,128)(2,1)S(1)}, u32[]{:S(2)}, u32[]{:S(2)}) %collective-permute-start.38) | collective-permute-done | bytes 262176 | tf_op jit(solution)/shard_map/ppermute | solution.py:657
  175.5 1.0 collective-permute-start.39
  176.5 1.6 collective-permute-done.29
  178.2 4.0 %collective-permute-done.39 = bf16[32,4096]{1,0:T(8,128)(2,1)S(1)} collective-permute-done((bf16[32,4096]{1,0:T(8,128)(2,1)S(1)}, bf16[32,4096]{1,0:T(8,128)(2,1)S(1)}, u32[]{:S(2)}, u32[]{:S(2)}) %collective-permute-start.39) | collective-permute-done | bytes 262176 | tf_op jit(solution)/shard_map/ppermute | solution.py:657
  182.3 0.8 pad_maximum_fusion
  (78 shorter events, 5.1 us)
Async XLA Ops:
  2.5 10.7 %copy-start = (s32[1,256]{1,0:T(1,128)S(1)}, s32[1,256]{1,0:T(1,128)}, u32[]{:S(2)}) copy-start(s32[1,256]{1,0:T(1,128)} %param.18) | copy-start | bytes 3076
  2.5 10.7 %copy-start.1 = (s32[1,4]{1,0:T(1,128)S(1)}, s32[1,4]{1,0:T(1,128)}, u32[]{:S(2)}) copy-start(s32[1,4]{1,0:T(1,128)} %param.17) | copy-start | bytes 52
  2.5 13.1 %copy-start.2 = (s32[4]{0:T(128)S(1)}, s32[4]{0:T(128)}, u32[]{:S(2)}) copy-start(s32[4]{0:T(128)} %param.16) | copy-start | bytes 52
  8.0 32.3 %collective-permute-start.3 = (bf16[4,2,256,1024]{3,2,1,0:T(8,128)(2,1)}, bf16[4,2,256,1024]{3,2,1,0:T(8,128)(2,1)}, u32[]{:S(2)}, u32[]{:S(2)}) collective-permute-start(bf16[4,2,256,1024]{3,2,1,0:T(8,128)(2,1)} %bitcast.21.refs_0_), channel_id=1, source_target_pairs={{8,0},{0,8},{9,1},{1,9},{10,2},{2,10},{11,3},{3,11},{12,4},{4,12},... | collective-permute-start | bytes 12582920 | tf_op jit(solution)/shard_map/ppermute | solution.py:578
  8.5 9.7 %collective-permute-start = (bf16[32,4096]{1,0:T(8,128)(2,1)S(1)}, bf16[32,4096]{1,0:T(8,128)(2,1)S(1)}, u32[]{:S(2)}, u32[]{:S(2)}) collective-permute-start(bf16[32,4096]{1,0:T(8,128)(2,1)S(1)} %get-tuple-element.146.refs_0_), channel_id=1, source_target_pairs={{0,2},{2,4},{4,6},{6,7},{7,5},{5,3},{3,1},{1,0},{8,10},{10,12},{12... | collective-permute-start | bytes 786440 | tf_op jit(solution)/shard_map/ppermute | solution.py:569
  11.1 15.9 %collective-permute-start.15 = (bf16[32,4096]{1,0:T(8,128)(2,1)S(1)}, bf16[32,4096]{1,0:T(8,128)(2,1)S(1)}, u32[]{:S(2)}, u32[]{:S(2)}) collective-permute-start(bf16[32,4096]{1,0:T(8,128)(2,1)S(1)} %get-tuple-element.146.refs_0_), channel_id=1, source_target_pairs={{2,0},{4,2},{6,4},{7,6},{5,7},{3,5},{1,3},{0,1},{10,8},{12,10},{14... | collective-permute-start | bytes 786440 | tf_op jit(solution)/shard_map/ppermute | solution.py:571
  11.1 14.0 %collective-permute-start.9 = (bf16[32,4096]{1,0:T(8,128)(2,1)S(1)}, bf16[32,4096]{1,0:T(8,128)(2,1)S(1)}, u32[]{:S(2)}, u32[]{:S(2)}) collective-permute-start(bf16[32,4096]{1,0:T(8,128)(2,1)S(1)} %get-tuple-element.145.refs_0_), channel_id=1, source_target_pairs={{2,0},{4,2},{6,4},{7,6},{5,7},{3,5},{1,3},{0,1},{10,8},{12,10},{14... | collective-permute-start | bytes 786440 | tf_op jit(solution)/shard_map/ppermute | solution.py:571
  13.1 18.6 %collective-permute-start.8 = (bf16[32,4096]{1,0:T(8,128)(2,1)S(1)}, bf16[32,4096]{1,0:T(8,128)(2,1)S(1)}, u32[]{:S(2)}, u32[]{:S(2)}) collective-permute-start(bf16[32,4096]{1,0:T(8,128)(2,1)S(1)} %get-tuple-element.145.refs_0_), channel_id=1, source_target_pairs={{0,2},{2,4},{4,6},{6,7},{7,5},{5,3},{3,1},{1,0},{8,10},{10,12},{12... | collective-permute-start | bytes 786440 | tf_op jit(solution)/shard_map/ppermute | solution.py:569
  18.2 11.1 %collective-permute-start.1 = (bf16[32,4096]{1,0:T(8,128)(2,1)S(1)}, bf16[32,4096]{1,0:T(8,128)(2,1)S(1)}, u32[]{:S(2)}, u32[]{:S(2)}) collective-permute-start(bf16[32,4096]{1,0:T(8,128)(2,1)S(1)} %collective-permute-done.refs_1_), channel_id=1, source_target_pairs={{0,2},{2,4},{4,6},{6,7},{7,5},{5,3},{3,1},{1,0},{8,10},{10,12},{12... | collective-permute-start | bytes 786440 | tf_op jit(solution)/shard_map/ppermute | solution.py:569
  25.2 9.2 %collective-permute-start.11 = (bf16[32,4096]{1,0:T(8,128)(2,1)S(1)}, bf16[32,4096]{1,0:T(8,128)(2,1)S(1)}, u32[]{:S(2)}, u32[]{:S(2)}) collective-permute-start(bf16[32,4096]{1,0:T(8,128)(2,1)S(1)} %collective-permute-done.9.refs_2_), channel_id=1, source_target_pairs={{2,0},{4,2},{6,4},{7,6},{5,7},{3,5},{1,3},{0,1},{10,8},{12,10},{14... | collective-permute-start | bytes 786440 | tf_op jit(solution)/shard_map/ppermute | solution.py:571
  27.0 13.0 %collective-permute-start.16 = (bf16[32,4096]{1,0:T(8,128)(2,1)S(1)}, bf16[32,4096]{1,0:T(8,128)(2,1)S(1)}, u32[]{:S(2)}, u32[]{:S(2)}) collective-permute-start(bf16[32,4096]{1,0:T(8,128)(2,1)S(1)} %collective-permute-done.15.refs_2_), channel_id=1, source_target_pairs={{2,0},{4,2},{6,4},{7,6},{5,7},{3,5},{1,3},{0,1},{10,8},{12,10},{14... | collective-permute-start | bytes 786440 | tf_op jit(solution)/shard_map/ppermute | solution.py:571
  29.9 13.7 %collective-permute-start.2 = (bf16[32,4096]{1,0:T(8,128)(2,1)S(1)}, bf16[32,4096]{1,0:T(8,128)(2,1)S(1)}, u32[]{:S(2)}, u32[]{:S(2)}) collective-permute-start(bf16[32,4096]{1,0:T(8,128)(2,1)S(1)} %collective-permute-done.1.refs_3_), channel_id=1, source_target_pairs={{0,2},{2,4},{4,6},{6,7},{7,5},{5,3},{3,1},{1,0},{8,10},{10,12},{12... | collective-permute-start | bytes 786440 | tf_op jit(solution)/shard_map/ppermute | solution.py:569
  31.8 13.7 %collective-permute-start.10 = (bf16[32,4096]{1,0:T(8,128)(2,1)S(1)}, bf16[32,4096]{1,0:T(8,128)(2,1)S(1)}, u32[]{:S(2)}, u32[]{:S(2)}) collective-permute-start(bf16[32,4096]{1,0:T(8,128)(2,1)S(1)} %collective-permute-done.8.refs_1_), channel_id=1, source_target_pairs={{0,2},{2,4},{4,6},{6,7},{7,5},{5,3},{3,1},{1,0},{8,10},{10,12},{12... | collective-permute-start | bytes 786440 | tf_op jit(solution)/shard_map/ppermute | solution.py:569
  34.4 12.6 %collective-permute-start.13 = (bf16[32,4096]{1,0:T(8,128)(2,1)S(1)}, bf16[32,4096]{1,0:T(8,128)(2,1)S(1)}, u32[]{:S(2)}, u32[]{:S(2)}) collective-permute-start(bf16[32,4096]{1,0:T(8,128)(2,1)S(1)} %collective-permute-done.11.refs_4_), channel_id=1, source_target_pairs={{2,0},{4,2},{6,4},{7,6},{5,7},{3,5},{1,3},{0,1},{10,8},{12,10},{14... | collective-permute-start | bytes 786440 | tf_op jit(solution)/shard_map/ppermute | solution.py:571
  40.1 11.2 %collective-permute-start.17 = (bf16[32,4096]{1,0:T(8,128)(2,1)S(1)}, bf16[32,4096]{1,0:T(8,128)(2,1)S(1)}, u32[]{:S(2)}, u32[]{:S(2)}) collective-permute-start(bf16[32,4096]{1,0:T(8,128)(2,1)S(1)} %collective-permute-done.16.refs_4_), channel_id=1, source_target_pairs={{2,0},{4,2},{6,4},{7,6},{5,7},{3,5},{1,3},{0,1},{10,8},{12,10},{14... | collective-permute-start | bytes 786440 | tf_op jit(solution)/shard_map/ppermute | solution.py:571
  43.6 9.3 %collective-permute-start.18 = (bf16[32,4096]{1,0:T(8,128)(2,1)S(1)}, bf16[32,4096]{1,0:T(8,128)(2,1)S(1)}, u32[]{:S(2)}, u32[]{:S(2)}) collective-permute-start(bf16[32,4096]{1,0:T(8,128)(2,1)S(1)} %collective-permute-done.2.refs_5_), channel_id=1, source_target_pairs={{0,2},{2,4},{4,6},{6,7},{7,5},{5,3},{3,1},{1,0},{8,10},{10,12},{12... | collective-permute-start | bytes 786440 | tf_op jit(solution)/shard_map/ppermute | solution.py:569
  45.4 13.9 %collective-permute-start.12 = (bf16[32,4096]{1,0:T(8,128)(2,1)S(1)}, bf16[32,4096]{1,0:T(8,128)(2,1)S(1)}, u32[]{:S(2)}, u32[]{:S(2)}) collective-permute-start(bf16[32,4096]{1,0:T(8,128)(2,1)S(1)} %collective-permute-done.10.refs_3_), channel_id=1, source_target_pairs={{0,2},{2,4},{4,6},{6,7},{7,5},{5,3},{3,1},{1,0},{8,10},{10,12},{12... | collective-permute-start | bytes 786440 | tf_op jit(solution)/shard_map/ppermute | solution.py:569
  47.0 12.3 %collective-permute-start.14 = (bf16[32,4096]{1,0:T(8,128)(2,1)S(1)}, bf16[32,4096]{1,0:T(8,128)(2,1)S(1)}, u32[]{:S(2)}, u32[]{:S(2)}) collective-permute-start(bf16[32,4096]{1,0:T(8,128)(2,1)S(1)} %collective-permute-done.13.refs_6_), channel_id=1, source_target_pairs={{2,0},{4,2},{6,4},{7,6},{5,7},{3,5},{1,3},{0,1},{10,8},{12,10},{14... | collective-permute-start | bytes 786440 | tf_op jit(solution)/shard_map/ppermute | solution.py:571
  47.4 25.1 %collective-permute-start.4 = (bf16[2,4,256,128]{3,2,1,0:T(8,128)(2,1)S(1)}, bf16[2,4,256,128]{3,2,1,0:T(8,128)(2,1)S(1)}, u32[]{:S(2)}, u32[]{:S(2)}) collective-permute-start(bf16[2,4,256,128]{3,2,1,0:T(8,128)(2,1)S(1)} %get-tuple-element.96), channel_id=1, source_target_pairs={{0,1},{1,0},{2,3},{3,2},{4,5},{5,4},{6,7},{7,6},{8,9},{9,8},{10,11... | collective-permute-start | bytes 1572872 | tf_op jit(solution)/shard_map/ppermute | solution.py:623
  51.3 24.5 %collective-permute-start.5 = (bf16[2,4,256,128]{3,2,1,0:T(8,128)(2,1)S(1)}, bf16[2,4,256,128]{3,2,1,0:T(8,128)(2,1)S(1)}, u32[]{:S(2)}, u32[]{:S(2)}) collective-permute-start(bf16[2,4,256,128]{3,2,1,0:T(8,128)(2,1)S(1)} %get-tuple-element.97), channel_id=1, source_target_pairs={{0,2},{1,3},{2,0},{3,1},{4,6},{5,7},{6,4},{7,5},{8,10},{9,11},{10,... | collective-permute-start | bytes 1572872 | tf_op jit(solution)/shard_map/ppermute | solution.py:623
  66.5 29.7 %collective-permute-start.20 = (bf16[8,128,256]{2,1,0:T(8,128)(2,1)S(1)}, bf16[8,128,256]{2,1,0:T(8,128)(2,1)S(1)}, u32[]{:S(2)}, u32[]{:S(2)}) collective-permute-start(bf16[8,128,256]{2,1,0:T(8,128)(2,1)S(1)} %get-tuple-element.118.refs_4_), channel_id=1, source_target_pairs={{0,4},{1,5},{2,6},{3,7},{4,0},{5,1},{6,2},{7,3},{8,12},{9,13},{10,... | collective-permute-start | bytes 1572872 | tf_op jit(solution)/shard_map/ppermute | solution.py:608
  69.1 27.1 %collective-permute-start.19 = (bf16[2,4,256,128]{3,2,1,0:T(8,128)(2,1)S(1)}, bf16[2,4,256,128]{3,2,1,0:T(8,128)(2,1)S(1)}, u32[]{:S(2)}, u32[]{:S(2)}) collective-permute-start(bf16[2,4,256,128]{3,2,1,0:T(8,128)(2,1)S(1)} %get-tuple-element.114), channel_id=1, source_target_pairs={{0,3},{1,2},{2,1},{3,0},{4,7},{5,6},{6,5},{7,4},{8,11},{9,10},{10,... | collective-permute-start | bytes 1572872 | tf_op jit(solution)/shard_map/ppermute | solution.py:623
  71.9 4.2 %collective-permute-start.21 = (bf16[256,128]{1,0:T(8,128)(2,1)S(1)}, bf16[256,128]{1,0:T(8,128)(2,1)S(1)}, u32[]{:S(2)}, u32[]{:S(2)}) collective-permute-start(bf16[256,128]{1,0:T(8,128)(2,1)S(1)} %get-tuple-element.115), channel_id=1, source_target_pairs={{0,0},{1,2},{2,4},{3,6},{4,1},{5,3},{6,5},{7,7},{8,8},{9,10},{10,1... | collective-permute-start | bytes 196616 | tf_op jit(solution)/shard_map/ppermute | solution.py:613
  72.6 22.2 %collective-permute-start.22 = (bf16[256,128]{1,0:T(8,128)(2,1)S(1)}, bf16[256,128]{1,0:T(8,128)(2,1)S(1)}, u32[]{:S(2)}, u32[]{:S(2)}) collective-permute-start(bf16[256,128]{1,0:T(8,128)(2,1)S(1)} %get-tuple-element.116), channel_id=1, source_target_pairs={{0,1},{1,3},{2,5},{3,7},{4,0},{5,2},{6,4},{7,6},{8,9},{9,11},{10,1... | collective-permute-start | bytes 196616 | tf_op jit(solution)/shard_map/ppermute | solution.py:613
  75.8 37.6 %collective-permute-start.23 = (bf16[2,4,256,128]{3,2,1,0:T(8,128)(2,1)S(1)}, bf16[2,4,256,128]{3,2,1,0:T(8,128)(2,1)S(1)}, u32[]{:S(2)}, u32[]{:S(2)}) collective-permute-start(bf16[2,4,256,128]{3,2,1,0:T(8,128)(2,1)S(1)} %get-tuple-element.120), channel_id=1, source_target_pairs={{0,1},{1,0},{2,3},{3,2},{4,5},{5,4},{6,7},{7,6},{8,9},{9,8},{10,11... | collective-permute-start | bytes 1572872 | tf_op jit(solution)/shard_map/ppermute | solution.py:623
  76.1 48.1 %collective-permute-start.6 = (bf16[2,4,256,128]{3,2,1,0:T(8,128)(2,1)S(1)}, bf16[2,4,256,128]{3,2,1,0:T(8,128)(2,1)S(1)}, u32[]{:S(2)}, u32[]{:S(2)}) collective-permute-start(bf16[2,4,256,128]{3,2,1,0:T(8,128)(2,1)S(1)} %get-tuple-element.98), channel_id=1, source_target_pairs={{0,2},{1,3},{2,0},{3,1},{4,6},{5,7},{6,4},{7,5},{8,10},{9,11},{10,... | collective-permute-start | bytes 1572872 | tf_op jit(solution)/shard_map/ppermute | solution.py:623
  94.8 29.4 %collective-permute-start.7 = (bf16[2,4,256,128]{3,2,1,0:T(8,128)(2,1)S(1)}, bf16[2,4,256,128]{3,2,1,0:T(8,128)(2,1)S(1)}, u32[]{:S(2)}, u32[]{:S(2)}) collective-permute-start(bf16[2,4,256,128]{3,2,1,0:T(8,128)(2,1)S(1)} %get-tuple-element.99), channel_id=1, source_target_pairs={{0,3},{1,2},{2,1},{3,0},{4,7},{5,6},{6,5},{7,4},{8,11},{9,10},{10,... | collective-permute-start | bytes 1572872 | tf_op jit(solution)/shard_map/ppermute | solution.py:623
  105.1 27.2 %collective-permute-start.25 = (bf16[4,144,256]{2,1,0:T(8,128)(2,1)S(1)}, bf16[4,144,256]{2,1,0:T(8,128)(2,1)S(1)}, u32[]{:S(2)}, u32[]{:S(2)}) collective-permute-start(bf16[4,144,256]{2,1,0:T(8,128)(2,1)S(1)} %attend.7), channel_id=1, source_target_pairs={{0,4},{1,5},{2,6},{3,7},{4,0},{5,1},{6,2},{7,3},{8,12},{9,13},{10,... | collective-permute-start | bytes 884744 | tf_op jit(solution)/shard_map/ppermute | solution.py:637
  113.3 19.2 %collective-permute-start.24 = (bf16[4,144,256]{2,1,0:T(8,128)(2,1)S(1)}, bf16[4,144,256]{2,1,0:T(8,128)(2,1)S(1)}, u32[]{:S(2)}, u32[]{:S(2)}) collective-permute-start(bf16[4,144,256]{2,1,0:T(8,128)(2,1)S(1)} %attend.4), channel_id=1, source_target_pairs={{0,4},{1,5},{2,6},{3,7},{4,0},{5,1},{6,2},{7,3},{8,12},{9,13},{10,... | collective-permute-start | bytes 884744 | tf_op jit(solution)/shard_map/ppermute | solution.py:637
  138.0 9.4 %collective-permute-start.26 = (bf16[32,4096]{1,0:T(8,128)(2,1)S(1)}, bf16[32,4096]{1,0:T(8,128)(2,1)S(1)}, u32[]{:S(2)}, u32[]{:S(2)}) collective-permute-start(bf16[32,4096]{1,0:T(8,128)(2,1)S(1)} %get-tuple-element.133), channel_id=1, source_target_pairs={{0,2},{2,4},{4,6},{6,7},{7,5},{5,3},{3,1},{1,0},{8,10},{10,12},{12... | collective-permute-start | bytes 786440 | tf_op jit(solution)/shard_map/ppermute | solution.py:657
  138.7 9.8 %collective-permute-start.30 = (bf16[32,4096]{1,0:T(8,128)(2,1)S(1)}, bf16[32,4096]{1,0:T(8,128)(2,1)S(1)}, u32[]{:S(2)}, u32[]{:S(2)}) collective-permute-start(bf16[32,4096]{1,0:T(8,128)(2,1)S(1)} %convert_element_type.116), channel_id=1, source_target_pairs={{2,0},{4,2},{6,4},{7,6},{5,7},{3,5},{1,3},{0,1},{10,8},{12,10},{14... | collective-permute-start | bytes 786440 | tf_op jit(solution)/shard_map/ppermute | solution.py:657
  145.3 9.3 %collective-permute-start.33 = (bf16[32,4096]{1,0:T(8,128)(2,1)S(1)}, bf16[32,4096]{1,0:T(8,128)(2,1)S(1)}, u32[]{:S(2)}, u32[]{:S(2)}) collective-permute-start(bf16[32,4096]{1,0:T(8,128)(2,1)S(1)} %convert_element_type.123), channel_id=1, source_target_pairs={{0,2},{2,4},{4,6},{6,7},{7,5},{5,3},{3,1},{1,0},{8,10},{10,12},{12... | collective-permute-start | bytes 786440 | tf_op jit(solution)/shard_map/ppermute | solution.py:657
  145.9 9.6 %collective-permute-start.36 = (bf16[32,4096]{1,0:T(8,128)(2,1)S(1)}, bf16[32,4096]{1,0:T(8,128)(2,1)S(1)}, u32[]{:S(2)}, u32[]{:S(2)}) collective-permute-start(bf16[32,4096]{1,0:T(8,128)(2,1)S(1)} %get-tuple-element.144), channel_id=1, source_target_pairs={{2,0},{4,2},{6,4},{7,6},{5,7},{3,5},{1,3},{0,1},{10,8},{12,10},{14... | collective-permute-start | bytes 786440 | tf_op jit(solution)/shard_map/ppermute | solution.py:657
  147.4 12.8 %collective-permute-start.27 = (bf16[32,4096]{1,0:T(8,128)(2,1)S(1)}, bf16[32,4096]{1,0:T(8,128)(2,1)S(1)}, u32[]{:S(2)}, u32[]{:S(2)}) collective-permute-start(bf16[32,4096]{1,0:T(8,128)(2,1)S(1)} %add_convert_fusion.11), channel_id=1, source_target_pairs={{0,2},{2,4},{4,6},{6,7},{7,5},{5,3},{3,1},{1,0},{8,10},{10,12},{12... | collective-permute-start | bytes 786440 | tf_op jit(solution)/shard_map/ppermute | solution.py:657
  148.5 12.7 %collective-permute-start.31 = (bf16[32,4096]{1,0:T(8,128)(2,1)S(1)}, bf16[32,4096]{1,0:T(8,128)(2,1)S(1)}, u32[]{:S(2)}, u32[]{:S(2)}) collective-permute-start(bf16[32,4096]{1,0:T(8,128)(2,1)S(1)} %add_convert_fusion.8), channel_id=1, source_target_pairs={{2,0},{4,2},{6,4},{7,6},{5,7},{3,5},{1,3},{0,1},{10,8},{12,10},{14... | collective-permute-start | bytes 786440 | tf_op jit(solution)/shard_map/ppermute | solution.py:657
  154.6 11.2 %collective-permute-start.34 = (bf16[32,4096]{1,0:T(8,128)(2,1)S(1)}, bf16[32,4096]{1,0:T(8,128)(2,1)S(1)}, u32[]{:S(2)}, u32[]{:S(2)}) collective-permute-start(bf16[32,4096]{1,0:T(8,128)(2,1)S(1)} %add_convert_fusion.5), channel_id=1, source_target_pairs={{0,2},{2,4},{4,6},{6,7},{7,5},{5,3},{3,1},{1,0},{8,10},{10,12},{12... | collective-permute-start | bytes 786440 | tf_op jit(solution)/shard_map/ppermute | solution.py:657
  155.6 11.2 %collective-permute-start.37 = (bf16[32,4096]{1,0:T(8,128)(2,1)S(1)}, bf16[32,4096]{1,0:T(8,128)(2,1)S(1)}, u32[]{:S(2)}, u32[]{:S(2)}) collective-permute-start(bf16[32,4096]{1,0:T(8,128)(2,1)S(1)} %add_convert_fusion.3), channel_id=1, source_target_pairs={{2,0},{4,2},{6,4},{7,6},{5,7},{3,5},{1,3},{0,1},{10,8},{12,10},{14... | collective-permute-start | bytes 786440 | tf_op jit(solution)/shard_map/ppermute | solution.py:657
  160.2 11.2 %collective-permute-start.28 = (bf16[32,4096]{1,0:T(8,128)(2,1)S(1)}, bf16[32,4096]{1,0:T(8,128)(2,1)S(1)}, u32[]{:S(2)}, u32[]{:S(2)}) collective-permute-start(bf16[32,4096]{1,0:T(8,128)(2,1)S(1)} %add_convert_fusion.10), channel_id=1, source_target_pairs={{0,2},{2,4},{4,6},{6,7},{7,5},{5,3},{3,1},{1,0},{8,10},{10,12},{12... | collective-permute-start | bytes 786440 | tf_op jit(solution)/shard_map/ppermute | solution.py:657
  161.2 15.3 %collective-permute-start.32 = (bf16[32,4096]{1,0:T(8,128)(2,1)S(1)}, bf16[32,4096]{1,0:T(8,128)(2,1)S(1)}, u32[]{:S(2)}, u32[]{:S(2)}) collective-permute-start(bf16[32,4096]{1,0:T(8,128)(2,1)S(1)} %add_convert_fusion.7), channel_id=1, source_target_pairs={{2,0},{4,2},{6,4},{7,6},{5,7},{3,5},{1,3},{0,1},{10,8},{12,10},{14... | collective-permute-start | bytes 786440 | tf_op jit(solution)/shard_map/ppermute | solution.py:657
  165.9 12.4 %collective-permute-start.35 = (bf16[32,4096]{1,0:T(8,128)(2,1)S(1)}, bf16[32,4096]{1,0:T(8,128)(2,1)S(1)}, u32[]{:S(2)}, u32[]{:S(2)}) collective-permute-start(bf16[32,4096]{1,0:T(8,128)(2,1)S(1)} %add_convert_fusion.4), channel_id=1, source_target_pairs={{0,2},{2,4},{4,6},{6,7},{7,5},{5,3},{3,1},{1,0},{8,10},{10,12},{12... | collective-permute-start | bytes 786440 | tf_op jit(solution)/shard_map/ppermute | solution.py:657
  166.8 8.6 %collective-permute-start.38 = (bf16[32,4096]{1,0:T(8,128)(2,1)S(1)}, bf16[32,4096]{1,0:T(8,128)(2,1)S(1)}, u32[]{:S(2)}, u32[]{:S(2)}) collective-permute-start(bf16[32,4096]{1,0:T(8,128)(2,1)S(1)} %add_convert_fusion.2), channel_id=1, source_target_pairs={{2,0},{4,2},{6,4},{7,6},{5,7},{3,5},{1,3},{0,1},{10,8},{12,10},{14... | collective-permute-start | bytes 786440 | tf_op jit(solution)/shard_map/ppermute | solution.py:657
  171.5 6.6 %collective-permute-start.29 = (bf16[32,4096]{1,0:T(8,128)(2,1)S(1)}, bf16[32,4096]{1,0:T(8,128)(2,1)S(1)}, u32[]{:S(2)}, u32[]{:S(2)}) collective-permute-start(bf16[32,4096]{1,0:T(8,128)(2,1)S(1)} %add_convert_fusion.9), channel_id=1, source_target_pairs={{0,2},{2,4},{4,6},{6,7},{7,5},{5,3},{3,1},{1,0},{8,10},{10,12},{12... | collective-permute-start | bytes 786440 | tf_op jit(solution)/shard_map/ppermute | solution.py:657
  175.5 6.7 %collective-permute-start.39 = (bf16[32,4096]{1,0:T(8,128)(2,1)S(1)}, bf16[32,4096]{1,0:T(8,128)(2,1)S(1)}, u32[]{:S(2)}, u32[]{:S(2)}) collective-permute-start(bf16[32,4096]{1,0:T(8,128)(2,1)S(1)} %add_convert_fusion.1), channel_id=1, source_target_pairs={{2,0},{4,2},{6,4},{7,6},{5,7},{3,5},{1,3},{0,1},{10,8},{12,10},{14... | collective-permute-start | bytes 786440 | tf_op jit(solution)/shard_map/ppermute | solution.py:657

commit v17 on v16

--- a/solution.py
+++ b/solution.py
@@ -35,6 +35,26 @@
     return pl.CostEstimate(
         flops=int(flops), bytes_accessed=int(bytes_accessed), transcendentals=int(transcendentals)
     )
+
+
+def norm_kernel(rows_ref, gain_ref, *outs):
+    widened = rows_ref[...].astype(jnp.float32)
+    mean = jnp.mean(widened * widened, axis=-1, keepdims=True)
+    normed = (widened * lax.rsqrt(mean + EPSILON) * gain_ref[...]).astype(jnp.bfloat16)
+    part = outs[0].shape[1]
+    for index, out in enumerate(outs):
+        out[...] = normed[:, index * part : (index + 1) * part]
+
+
+def norm(rows, gain):
+    height, width = rows.shape
+    return pl.pallas_call(
+        norm_kernel,
+        out_shape=[jax.ShapeDtypeStruct((height, width // CHUNKS), jnp.bfloat16)] * CHUNKS,
+        compiler_params=megabytes(8),
+        cost_estimate=cost(4 * height * width, 4 * height * width),
+        name="norm",
+    )(rows, gain[None, :])
 
 
 def rotation_tables(positions):
@@ -528,13 +548,8 @@
     table = [[ring[(ring.index(i) + s) % tp_size] for s in steps] for i in range(tp_size)]
     place = jnp.array(table, jnp.int32)[me]
 
-    widened = hidden_in.astype(jnp.float32)
-    normed = (
-        widened
-        * lax.rsqrt(jnp.mean(widened * widened, axis=-1, keepdims=True) + EPSILON)
-        * norm_gain
-    ).astype(jnp.bfloat16)
-    normed, pool_cache = lax.optimization_barrier((normed, pool_cache))
+    normed = norm(hidden_in, norm_gain)
+    *normed, pool_cache = lax.optimization_barrier((*normed, pool_cache))
     w_query, w_keyval, w_out = (
         pltpu.with_memory_space_constraint(w, pltpu.HBM) for w in (w_query, w_keyval, w_out)
     )
@@ -558,10 +573,9 @@
     q_pos = jnp.tile(selected.reshape(SEL // tile_q, tile_q), (1, heads_here))
     q_pos = q_pos.reshape(SEL // tile_q, 1, TILE_COLS)
 
-    part = width // CHUNKS
     streams = []
     for chunk in range(CHUNKS):
-        own = normed[:, chunk * part : (chunk + 1) * part]
+        own = normed[chunk]
         streams.append({"before": [own], "behind": [own]})
     for k in range(1, far + 1):
         for chunk, held in enumerate(streams):
@@ -588,8 +602,9 @@
                     + (place, side, odd)
                 )
             )
+            sent = select_docs(sources, holder, slot, takers, tp_size)
+            first[-1], *sent = lax.optimization_barrier((first[-1], *sent))
         if k == far - 1:
-            sent = select_docs(sources, holder, slot, takers, tp_size)
             first[-1], *sent = lax.optimization_barrier((first[-1], *sent))
     weights = [w_keyval, w_query]
     sums = []

time: 183 us -> 187 us (1.022)
  starting transfers between devices: 64.8 us -> 68.6 us
  other arithmetic: 7.25 us -> 4.75 us
  waiting for transfers between devices: 42.3 us -> 40.2 us
  Pallas kernels: 60.8 us -> 62.7 us
    ppermute x7, waiting for transfers between devices: 13.9 us -> 5.5 us  [per_device(): held['behind'].append(lax.ppermute(held['behind'][-1], 'tp', back))]
    ppermute x7, waiting for transfers between devices: 3.17 us -> 10.4 us  [per_device(): held['before'].append(lax.ppermute(held['before'][-1], 'tp', forth))]
    ppermute x14, starting transfers between devices: 13.6 us -> 15.7 us  [per_device(): held = lax.ppermute(term.astype(jnp.bfloat16), 'tp', pairs)]
  transfers between devices with their start and end apart: 40 -> 40, of which waited for: 17 -> 15; matrix products, arithmetic and copies ran while one was open for 3% -> 3% of each run, Pallas kernels for 30% -> 31%
where the time goes in v17:
time: 187 us; the launch traced here: 186 us
  starting transfers between devices  68.6 us (37%)
  Pallas kernels  62.7 us (34%)
  waiting for transfers between devices  40.2 us (21%)
  local copies, waits for them, and re-layouts  9.38 us (5%)
  other arithmetic  4.75 us (3%)
    pallas_call x4, Pallas kernels, attend(): pl.pallas_call(functools.partial(attend_kernel, n_chunks, offset, packs,...  35 us
    ppermute x6, starting transfers between devices, exchange(): return lax.ppermute(keys, 'tp', [(i, i ^ j) for i in range(tp_size)])  26.1 us
    ppermute x14, waiting for transfers between devices, per_device(): held = lax.ppermute(term.astype(jnp.bfloat16), 'tp', pairs)  23.4 us
    ppermute x14, starting transfers between devices, per_device(): held = lax.ppermute(term.astype(jnp.bfloat16), 'tp', pairs)  15.7 us
    pallas_call x2, Pallas kernels, project(): pl.pallas_call(functools.partial(project_kernel, len(blocks), chunk, is_l...  13.6 us
    ppermute x7, starting transfers between devices, per_device(): held['before'].append(lax.ppermute(held['before'][-1], 'tp', forth))  11.8 us
    ppermute x7, waiting for transfers between devices, per_device(): held['before'].append(lax.ppermute(held['before'][-1], 'tp', forth))  10.4 us
    pallas_call x2, Pallas kernels, project_out(): pl.pallas_call(functools.partial(out_kernel, n_blocks, chunk * width), in...  10.2 us
  transfers between devices with their start and end apart: 40, of which 15 were waited for; matrix products, arithmetic and copies ran while one was open for 3% of the time, Pallas kernels for 31%

profile of v17, /device:TPU:0, one launch (start us, length us, event | category | flops | bytes accessed | tf_op | source)
XLA Modules:
  0.0 186.1 jit_solution(1518692067064115202)
XLA Ops:
  0.0 1.0 copy-done
  1.0 0.8 copy-done.2
  2.2 5.5 %copy.16 = bf16[4,256,2,1024]{3,1,2,0:T(8,128)(2,1)} copy(bf16[4,256,2,1024]{3,2,1,0:T(2,128)(2,1)} %param.15) | data formatting | bytes 8388608 | tf_op jit(solution)/shard_map/optimization_barrier | solution.py:552
  8.1 2.6 %collective-permute-start = (bf16[32,4096]{1,0:T(8,128)(2,1)S(1)}, bf16[32,4096]{1,0:T(8,128)(2,1)S(1)}, u32[]{:S(2)}, u32[]{:S(2)}) collective-permute-start(bf16[32,4096]{1,0:T(8,128)(2,1)S(1)} %get-tuple-element.89.refs_0_), channel_id=1, source_target_pairs={{0,2},{2,4},{4,6},{6,7},{7,5},{5,3},{3,1},{1,0},{8,10},{10,12},{12... | collective-permute-start | bytes 786440 | tf_op jit(solution)/shard_map/ppermute | solution.py:583
  10.7 2.0 %collective-permute-start.9 = (bf16[32,4096]{1,0:T(8,128)(2,1)S(1)}, bf16[32,4096]{1,0:T(8,128)(2,1)S(1)}, u32[]{:S(2)}, u32[]{:S(2)}) collective-permute-start(bf16[32,4096]{1,0:T(8,128)(2,1)S(1)} %get-tuple-element.126.refs_0_), channel_id=1, source_target_pairs={{2,0},{4,2},{6,4},{7,6},{5,7},{3,5},{1,3},{0,1},{10,8},{12,10},{14... | collective-permute-start | bytes 786440 | tf_op jit(solution)/shard_map/ppermute | solution.py:585
  13.1 1.3 compare_reduce_fusion
  14.6 0.5 fusion
  15.2 2.6 %collective-permute-done.refs_1_ = bf16[32,4096]{1,0:T(8,128)(2,1)S(1)} collective-permute-done((bf16[32,4096]{1,0:T(8,128)(2,1)S(1)}, bf16[32,4096]{1,0:T(8,128)(2,1)S(1)}, u32[]{:S(2)}, u32[]{:S(2)}) %collective-permute-start) | collective-permute-done | bytes 262176 | tf_op jit(solution)/shard_map/ppermute | solution.py:583
  17.8 2.0 %collective-permute-start.1 = (bf16[32,4096]{1,0:T(8,128)(2,1)S(1)}, bf16[32,4096]{1,0:T(8,128)(2,1)S(1)}, u32[]{:S(2)}, u32[]{:S(2)}) collective-permute-start(bf16[32,4096]{1,0:T(8,128)(2,1)S(1)} %collective-permute-done.refs_1_), channel_id=1, source_target_pairs={{0,2},{2,4},{4,6},{6,7},{7,5},{5,3},{3,1},{1,0},{8,10},{10,12},{12... | collective-permute-start | bytes 786440 | tf_op jit(solution)/shard_map/ppermute | solution.py:583
  19.8 0.7 dynamic-slice_bitcast_fusion.place_ref
  20.6 4.1 %collective-permute-done.9.refs_2_ = bf16[32,4096]{1,0:T(8,128)(2,1)S(1)} collective-permute-done((bf16[32,4096]{1,0:T(8,128)(2,1)S(1)}, bf16[32,4096]{1,0:T(8,128)(2,1)S(1)}, u32[]{:S(2)}, u32[]{:S(2)}) %collective-permute-start.9) | collective-permute-done | bytes 262176 | tf_op jit(solution)/shard_map/ppermute | solution.py:585
  25.2 0.5 broadcast.167
  25.7 0.7 reduce.3
  26.6 1.7 collective-permute-start.16
  28.3 0.5 collective-permute-done.1.refs_3_
  28.8 0.6 broadcast_in_dim.46.refs_4_.refs_2_
  29.5 3.3 %select_docs.1 = (bf16[2,4,256,128]{3,2,1,0:T(8,128)(2,1)S(1)}, bf16[2,4,256,128]{3,2,1,0:T(8,128)(2,1)S(1)}, bf16[2,4,256,128]{3,2,1,0:T(8,128)(2,1)S(1)}, bf16...) custom-call(s32[4]{0:T(128)S(1)} %get-tuple-element.94.place_ref, ...), custom_call_target="tpu_custom_call" | custom-call | bytes 8388608 | tf_op jit(solution)/shard_map/select_docs/pallas_call | solution.py:235
  32.7 1.9 collective-permute-start.3
  34.6 1.6 collective-permute-start.10
  36.6 1.4 collective-permute-done.16.refs_4_
  38.0 0.7 collective-permute-start.17
  38.7 3.3 %collective-permute-done.3.refs_5_ = bf16[32,4096]{1,0:T(8,128)(2,1)S(1)} collective-permute-done((bf16[32,4096]{1,0:T(8,128)(2,1)S(1)}, bf16[32,4096]{1,0:T(8,128)(2,1)S(1)}, u32[]{:S(2)}, u32[]{:S(2)}) %collective-permute-start.3) | collective-permute-done | bytes 262176 | tf_op jit(solution)/shard_map/ppermute | solution.py:583
  42.0 1.8 collective-permute-start.18
  43.8 3.8 %collective-permute-done.10.refs_3_ = bf16[32,4096]{1,0:T(8,128)(2,1)S(1)} collective-permute-done((bf16[32,4096]{1,0:T(8,128)(2,1)S(1)}, bf16[32,4096]{1,0:T(8,128)(2,1)S(1)}, u32[]{:S(2)}, u32[]{:S(2)}) %collective-permute-start.10) | collective-permute-done | bytes 262176 | tf_op jit(solution)/shard_map/ppermute | solution.py:583
  47.6 1.8 collective-permute-start.12
  49.6 1.8 collective-permute-start.4
  51.4 1.6 collective-permute-start.5
  53.2 6.4 %project.2 = (f32[256,256]{1,0:T(8,128)S(1)}, f32[256,1024]{1,0:T(8,128)S(1)}) custom-call(s32[8]{0:T(128)S(1)} %dynamic-slice_bitcast_fusion.place_ref, bf16[32,4096]{1,0:T(8,128)(2,1)S(1)} %get-tuple-element.89.refs_0_, bf16[32,4096]{1,0:T(8,128)(2,1)S(1)} %collective-permute-done.refs_1_, bf16[32,4096]{1,0:T(8,128)(2,1)S(1)} %collective-permute-done.15.refs_2_, ...), custom_call_target="tpu_custom_call" | custom-call | flops 2684354560 | bytes 12582912 | tf_op jit(solution)/shard_map/project/pallas_call | solution.py:193
  59.6 7.2 %project.3 = (bf16[256,128]{1,0:T(8,128)(2,1)S(1)}, bf16[256,128]{1,0:T(8,128)(2,1)S(1)}, bf16[8,128,256]{2,1,0:T(8,128)(2,1)S(1)}) custom-call(s32[8]{0:T(128)S(1)} %dynamic-slice_bitcast_fusion.place_ref, bf16[32,4096]{1,0:T(8,128)(2,1)S(1)} %get-tuple-element.126.refs_0_, bf16[32,4096]{1,0:T(8,128)(2,1)S(1)} %collective-permute-done.8.refs_1_, ...), custom_call_target="tpu_custom_call" | custom-call | flops 2684354560 | bytes 12582912 | tf_op jit(solution)/shard_map/project/pallas_call | solution.py:193
  66.9 2.9 %collective-permute-start.20 = (bf16[8,128,256]{2,1,0:T(8,128)(2,1)S(1)}, bf16[8,128,256]{2,1,0:T(8,128)(2,1)S(1)}, u32[]{:S(2)}, u32[]{:S(2)}) collective-permute-start(bf16[8,128,256]{2,1,0:T(8,128)(2,1)S(1)} %get-tuple-element.142.refs_4_), channel_id=1, source_target_pairs={{0,4},{1,5},{2,6},{3,7},{4,0},{5,1},{6,2},{7,3},{8,12},{9,13},{10,... | collective-permute-start | bytes 1572872 | tf_op jit(solution)/shard_map/ppermute | solution.py:623
  69.8 2.5 %collective-permute-start.19 = (bf16[2,4,256,128]{3,2,1,0:T(8,128)(2,1)S(1)}, bf16[2,4,256,128]{3,2,1,0:T(8,128)(2,1)S(1)}, u32[]{:S(2)}, u32[]{:S(2)}) collective-permute-start(bf16[2,4,256,128]{3,2,1,0:T(8,128)(2,1)S(1)} %get-tuple-element.138), channel_id=1, source_target_pairs={{0,3},{1,2},{2,1},{3,0},{4,7},{5,6},{6,5},{7,4},{8,11},{9,10},{10,... | collective-permute-start | bytes 1572872 | tf_op jit(solution)/shard_map/ppermute | solution.py:638
  72.3 0.7 collective-permute-start.21
  73.0 3.2 %collective-permute-start.22 = (bf16[256,128]{1,0:T(8,128)(2,1)S(1)}, bf16[256,128]{1,0:T(8,128)(2,1)S(1)}, u32[]{:S(2)}, u32[]{:S(2)}) collective-permute-start(bf16[256,128]{1,0:T(8,128)(2,1)S(1)} %get-tuple-element.140), channel_id=1, source_target_pairs={{0,1},{1,3},{2,5},{3,7},{4,0},{5,2},{6,4},{7,6},{8,9},{9,11},{10,1... | collective-permute-start | bytes 196616 | tf_op jit(solution)/shard_map/ppermute | solution.py:628
  76.5 19.8 %collective-permute-start.6 = (bf16[2,4,256,128]{3,2,1,0:T(8,128)(2,1)S(1)}, bf16[2,4,256,128]{3,2,1,0:T(8,128)(2,1)S(1)}, u32[]{:S(2)}, u32[]{:S(2)}) collective-permute-start(bf16[2,4,256,128]{3,2,1,0:T(8,128)(2,1)S(1)} %get-tuple-element.121), channel_id=1, source_target_pairs={{0,2},{1,3},{2,0},{3,1},{4,6},{5,7},{6,4},{7,5},{8,10},{9,11},{10,... | collective-permute-start | bytes 1572872 | tf_op jit(solution)/shard_map/ppermute | solution.py:638
  96.4 8.9 %attend.7 = bf16[4,144,256]{2,1,0:T(8,128)(2,1)S(1)} custom-call(s32[16]{0:T(128)S(1)} %select_n.48.first_ref, s32[256]{0:T(256)S(1)} %bitcast.25, s32[1]{0:T(128)} %bitcast.7.odd_ref, bf16[2,4,256,128]{3,2,1,0:T(8,128)(2,1)S(1)} %get-tuple-element.135.refs_0_, bf16[2,4,256,128]{3,2,1,0:T(8,128)(2,1)S(1)} %collective-permute-done.4.refs_1_, ...), custom_call_target="tpu_custom_call" | custom-call | flops 1073741824 | tf_op jit(solution)/shard_map/attend/pallas_call | solution.py:415
  105.3 2.5 %collective-permute-start.25 = (bf16[4,144,256]{2,1,0:T(8,128)(2,1)S(1)}, bf16[4,144,256]{2,1,0:T(8,128)(2,1)S(1)}, u32[]{:S(2)}, u32[]{:S(2)}) collective-permute-start(bf16[4,144,256]{2,1,0:T(8,128)(2,1)S(1)} %attend.7), channel_id=1, source_target_pairs={{0,4},{1,5},{2,6},{3,7},{4,0},{5,1},{6,2},{7,3},{8,12},{9,13},{10,... | collective-permute-start | bytes 884744 | tf_op jit(solution)/shard_map/ppermute | solution.py:652
  107.8 6.6 %attend.4 = bf16[4,144,256]{2,1,0:T(8,128)(2,1)S(1)} custom-call(s32[16]{0:T(128)S(1)} %select_n.48.first_ref, s32[256]{0:T(256)S(1)} %bitcast.26, s32[1]{0:T(128)} %bitcast.7.odd_ref, bf16[2,4,256,128]{3,2,1,0:T(8,128)(2,1)S(1)} %get-tuple-element.135.refs_0_, bf16[2,4,256,128]{3,2,1,0:T(8,128)(2,1)S(1)} %collective-permute-done.4.refs_1_, ...), custom_call_target="tpu_custom_call" | custom-call | flops 1073741824 | tf_op jit(solution)/shard_map/attend/pallas_call | solution.py:415
  114.5 11.5 %attend.5 = (f32[8,1,256]{2,1,0:T(1,128)S(1)}, f32[8,1,256]{2,1,0:T(1,128)S(1)}, f32[8,128,256]{2,1,0:T(8,128)S(1)}) custom-call(s32[16]{0:T(128)S(1)} %select_n.48.first_ref, s32[256]{0:T(256)S(1)} %bitcast.27, s32[1]{0:T(128)} %bitcast.7.odd_ref, bf16[2,4,256,128]{3,2,1,0:T(8,128)(2,1)S(1)} %get-tuple-element.143.refs_0_, ...), custom_call_target="tpu_custom_call" | custom-call | flops 1 | bytes 1 | tf_op jit(solution)/shard_map/attend/pallas_call | solution.py:415
  126.0 0.9 collective-permute-done.7.refs_1_
  126.9 8.0 %attend.6 = (f32[8,1,256]{2,1,0:T(1,128)S(1)}, f32[8,1,256]{2,1,0:T(1,128)S(1)}, f32[8,128,256]{2,1,0:T(8,128)S(1)}) custom-call(s32[16]{0:T(128)S(1)} %select_n.48.first_ref, s32[256]{0:T(256)S(1)} %bitcast.28, s32[1]{0:T(128)} %bitcast.7.odd_ref, bf16[2,4,256,128]{3,2,1,0:T(8,128)(2,1)S(1)} %collective-permute-done.6.refs_0_, ...), custom_call_target="tpu_custom_call" | custom-call | flops 1 | bytes 1 | tf_op jit(solution)/shard_map/attend/pallas_call | solution.py:415
  135.3 5.1 %project_out.2 = (f32[32,4096]{1,0:T(8,128)S(1)}, f32[32,4096]{1,0:T(8,128)S(1)}, f32[32,4096]{1,0:T(8,128)S(1)}, f32[32,4096]{1,0:T(8,128)S(1)}, f32[32,4096]{1...) custom-call(s32[8]{0:T(128)S(1)} %dynamic-slice_bitcast_fusion.place_ref, ...), custom_call_target="tpu_custom_call" | custom-call | flops 2147483648 | bytes 13107200 | tf_op jit(solution)/shard_map/project_out/pallas_call | solution.py:508
  140.4 2.2 %collective-permute-start.26 = (bf16[32,4096]{1,0:T(8,128)(2,1)S(1)}, bf16[32,4096]{1,0:T(8,128)(2,1)S(1)}, u32[]{:S(2)}, u32[]{:S(2)}) collective-permute-start(bf16[32,4096]{1,0:T(8,128)(2,1)S(1)} %get-tuple-element.157), channel_id=1, source_target_pairs={{0,2},{2,4},{4,6},{6,7},{7,5},{5,3},{3,1},{1,0},{8,10},{10,12},{12... | collective-permute-start | bytes 786440 | tf_op jit(solution)/shard_map/ppermute | solution.py:672
  142.6 0.6 collective-permute-start.30
  143.2 5.1 %project_out.3 = (f32[32,4096]{1,0:T(8,128)S(1)}, f32[32,4096]{1,0:T(8,128)S(1)}, f32[32,4096]{1,0:T(8,128)S(1)}, f32[32,4096]{1,0:T(8,128)S(1)}, f32[32,4096]{1...) custom-call(s32[8]{0:T(128)S(1)} %dynamic-slice_bitcast_fusion.place_ref, ...), custom_call_target="tpu_custom_call" | custom-call | flops 2147483648 | bytes 13107200 | tf_op jit(solution)/shard_map/project_out/pallas_call | solution.py:508
  148.4 1.5 collective-permute-start.33
  149.9 0.6 collective-permute-start.36
  150.5 1.5 collective-permute-start.27
  152.1 0.6 collective-permute-start.31
  152.7 4.9 %collective-permute-done.33 = bf16[32,4096]{1,0:T(8,128)(2,1)S(1)} collective-permute-done((bf16[32,4096]{1,0:T(8,128)(2,1)S(1)}, bf16[32,4096]{1,0:T(8,128)(2,1)S(1)}, u32[]{:S(2)}, u32[]{:S(2)}) %collective-permute-start.33) | collective-permute-done | bytes 262176 | tf_op jit(solution)/shard_map/ppermute | solution.py:672
  157.7 1.5 collective-permute-start.34
  159.3 0.6 collective-permute-start.37
  159.9 3.4 %collective-permute-done.27 = bf16[32,4096]{1,0:T(8,128)(2,1)S(1)} collective-permute-done((bf16[32,4096]{1,0:T(8,128)(2,1)S(1)}, bf16[32,4096]{1,0:T(8,128)(2,1)S(1)}, u32[]{:S(2)}, u32[]{:S(2)}) %collective-permute-start.27) | collective-permute-done | bytes 262176 | tf_op jit(solution)/shard_map/ppermute | solution.py:672
  163.3 1.5 collective-permute-start.28
  164.9 0.6 collective-permute-start.32
  165.5 3.4 %collective-permute-done.34 = bf16[32,4096]{1,0:T(8,128)(2,1)S(1)} collective-permute-done((bf16[32,4096]{1,0:T(8,128)(2,1)S(1)}, bf16[32,4096]{1,0:T(8,128)(2,1)S(1)}, u32[]{:S(2)}, u32[]{:S(2)}) %collective-permute-start.34) | collective-permute-done | bytes 262176 | tf_op jit(solution)/shard_map/ppermute | solution.py:672
  169.0 1.5 collective-permute-start.35
  170.5 0.6 collective-permute-start.38
  171.1 3.4 %collective-permute-done.28 = bf16[32,4096]{1,0:T(8,128)(2,1)S(1)} collective-permute-done((bf16[32,4096]{1,0:T(8,128)(2,1)S(1)}, bf16[32,4096]{1,0:T(8,128)(2,1)S(1)}, u32[]{:S(2)}, u32[]{:S(2)}) %collective-permute-start.28) | collective-permute-done | bytes 262176 | tf_op jit(solution)/shard_map/ppermute | solution.py:672
  174.6 1.5 collective-permute-start.29
  176.1 2.6 %collective-permute-done.38 = bf16[32,4096]{1,0:T(8,128)(2,1)S(1)} collective-permute-done((bf16[32,4096]{1,0:T(8,128)(2,1)S(1)}, bf16[32,4096]{1,0:T(8,128)(2,1)S(1)}, u32[]{:S(2)}, u32[]{:S(2)}) %collective-permute-start.38) | collective-permute-done | bytes 262176 | tf_op jit(solution)/shard_map/ppermute | solution.py:672
  178.8 0.6 collective-permute-start.39
  179.4 1.8 collective-permute-done.29
  181.3 3.9 %collective-permute-done.39 = bf16[32,4096]{1,0:T(8,128)(2,1)S(1)} collective-permute-done((bf16[32,4096]{1,0:T(8,128)(2,1)S(1)}, bf16[32,4096]{1,0:T(8,128)(2,1)S(1)}, u32[]{:S(2)}, u32[]{:S(2)}) %collective-permute-start.39) | collective-permute-done | bytes 262176 | tf_op jit(solution)/shard_map/ppermute | solution.py:672
  185.3 0.8 pad_maximum_fusion
  (79 shorter events, 4.7 us)
Async XLA Ops:
  0.0 1.0 copy-start
  1.0 0.8 copy-start.2
  2.1 10.6 %copy-start.1 = (s32[1,256]{1,0:T(1,128)S(1)}, s32[1,256]{1,0:T(1,128)}, u32[]{:S(2)}) copy-start(s32[1,256]{1,0:T(1,128)} %param.18) | copy-start | bytes 3076
  2.1 10.6 %copy-start.3 = (s32[1,4]{1,0:T(1,128)S(1)}, s32[1,4]{1,0:T(1,128)}, u32[]{:S(2)}) copy-start(s32[1,4]{1,0:T(1,128)} %param.17) | copy-start | bytes 52
  2.2 13.0 %copy-start.4 = (s32[4]{0:T(128)S(1)}, s32[4]{0:T(128)}, u32[]{:S(2)}) copy-start(s32[4]{0:T(128)} %param.16) | copy-start | bytes 52
  7.7 21.8 %collective-permute-start.2 = (bf16[4,2,256,1024]{3,2,1,0:T(8,128)(2,1)}, bf16[4,2,256,1024]{3,2,1,0:T(8,128)(2,1)}, u32[]{:S(2)}, u32[]{:S(2)}) collective-permute-start(bf16[4,2,256,1024]{3,2,1,0:T(8,128)(2,1)} %bitcast.22.refs_0_), channel_id=1, source_target_pairs={{8,0},{0,8},{9,1},{1,9},{10,2},{2,10},{11,3},{3,11},{12,4},{4,12},... | collective-permute-start | bytes 12582920 | tf_op jit(solution)/shard_map/ppermute | solution.py:592
  8.1 9.7 %collective-permute-start = (bf16[32,4096]{1,0:T(8,128)(2,1)S(1)}, bf16[32,4096]{1,0:T(8,128)(2,1)S(1)}, u32[]{:S(2)}, u32[]{:S(2)}) collective-permute-start(bf16[32,4096]{1,0:T(8,128)(2,1)S(1)} %get-tuple-element.89.refs_0_), channel_id=1, source_target_pairs={{0,2},{2,4},{4,6},{6,7},{7,5},{5,3},{3,1},{1,0},{8,10},{10,12},{12... | collective-permute-start | bytes 786440 | tf_op jit(solution)/shard_map/ppermute | solution.py:583
  10.7 15.9 %collective-permute-start.15 = (bf16[32,4096]{1,0:T(8,128)(2,1)S(1)}, bf16[32,4096]{1,0:T(8,128)(2,1)S(1)}, u32[]{:S(2)}, u32[]{:S(2)}) collective-permute-start(bf16[32,4096]{1,0:T(8,128)(2,1)S(1)} %get-tuple-element.89.refs_0_), channel_id=1, source_target_pairs={{2,0},{4,2},{6,4},{7,6},{5,7},{3,5},{1,3},{0,1},{10,8},{12,10},{14... | collective-permute-start | bytes 786440 | tf_op jit(solution)/shard_map/ppermute | solution.py:585
  10.7 14.1 %collective-permute-start.9 = (bf16[32,4096]{1,0:T(8,128)(2,1)S(1)}, bf16[32,4096]{1,0:T(8,128)(2,1)S(1)}, u32[]{:S(2)}, u32[]{:S(2)}) collective-permute-start(bf16[32,4096]{1,0:T(8,128)(2,1)S(1)} %get-tuple-element.126.refs_0_), channel_id=1, source_target_pairs={{2,0},{4,2},{6,4},{7,6},{5,7},{3,5},{1,3},{0,1},{10,8},{12,10},{14... | collective-permute-start | bytes 786440 | tf_op jit(solution)/shard_map/ppermute | solution.py:585
  12.7 21.9 %collective-permute-start.8 = (bf16[32,4096]{1,0:T(8,128)(2,1)S(1)}, bf16[32,4096]{1,0:T(8,128)(2,1)S(1)}, u32[]{:S(2)}, u32[]{:S(2)}) collective-permute-start(bf16[32,4096]{1,0:T(8,128)(2,1)S(1)} %get-tuple-element.126.refs_0_), channel_id=1, source_target_pairs={{0,2},{2,4},{4,6},{6,7},{7,5},{5,3},{3,1},{1,0},{8,10},{10,12},{12... | collective-permute-start | bytes 786440 | tf_op jit(solution)/shard_map/ppermute | solution.py:583
  17.8 11.1 %collective-permute-start.1 = (bf16[32,4096]{1,0:T(8,128)(2,1)S(1)}, bf16[32,4096]{1,0:T(8,128)(2,1)S(1)}, u32[]{:S(2)}, u32[]{:S(2)}) collective-permute-start(bf16[32,4096]{1,0:T(8,128)(2,1)S(1)} %collective-permute-done.refs_1_), channel_id=1, source_target_pairs={{0,2},{2,4},{4,6},{6,7},{7,5},{5,3},{3,1},{1,0},{8,10},{10,12},{12... | collective-permute-start | bytes 786440 | tf_op jit(solution)/shard_map/ppermute | solution.py:583
  24.7 11.4 %collective-permute-start.11 = (bf16[32,4096]{1,0:T(8,128)(2,1)S(1)}, bf16[32,4096]{1,0:T(8,128)(2,1)S(1)}, u32[]{:S(2)}, u32[]{:S(2)}) collective-permute-start(bf16[32,4096]{1,0:T(8,128)(2,1)S(1)} %collective-permute-done.9.refs_2_), channel_id=1, source_target_pairs={{2,0},{4,2},{6,4},{7,6},{5,7},{3,5},{1,3},{0,1},{10,8},{12,10},{14... | collective-permute-start | bytes 786440 | tf_op jit(solution)/shard_map/ppermute | solution.py:585
  26.6 11.4 %collective-permute-start.16 = (bf16[32,4096]{1,0:T(8,128)(2,1)S(1)}, bf16[32,4096]{1,0:T(8,128)(2,1)S(1)}, u32[]{:S(2)}, u32[]{:S(2)}) collective-permute-start(bf16[32,4096]{1,0:T(8,128)(2,1)S(1)} %collective-permute-done.15.refs_2_), channel_id=1, source_target_pairs={{2,0},{4,2},{6,4},{7,6},{5,7},{3,5},{1,3},{0,1},{10,8},{12,10},{14... | collective-permute-start | bytes 786440 | tf_op jit(solution)/shard_map/ppermute | solution.py:585
  32.7 9.2 %collective-permute-start.3 = (bf16[32,4096]{1,0:T(8,128)(2,1)S(1)}, bf16[32,4096]{1,0:T(8,128)(2,1)S(1)}, u32[]{:S(2)}, u32[]{:S(2)}) collective-permute-start(bf16[32,4096]{1,0:T(8,128)(2,1)S(1)} %collective-permute-done.1.refs_3_), channel_id=1, source_target_pairs={{0,2},{2,4},{4,6},{6,7},{7,5},{5,3},{3,1},{1,0},{8,10},{10,12},{12... | collective-permute-start | bytes 786440 | tf_op jit(solution)/shard_map/ppermute | solution.py:583
  34.6 13.0 %collective-permute-start.10 = (bf16[32,4096]{1,0:T(8,128)(2,1)S(1)}, bf16[32,4096]{1,0:T(8,128)(2,1)S(1)}, u32[]{:S(2)}, u32[]{:S(2)}) collective-permute-start(bf16[32,4096]{1,0:T(8,128)(2,1)S(1)} %collective-permute-done.8.refs_1_), channel_id=1, source_target_pairs={{0,2},{2,4},{4,6},{6,7},{7,5},{5,3},{3,1},{1,0},{8,10},{10,12},{12... | collective-permute-start | bytes 786440 | tf_op jit(solution)/shard_map/ppermute | solution.py:583
  36.2 13.2 %collective-permute-start.13 = (bf16[32,4096]{1,0:T(8,128)(2,1)S(1)}, bf16[32,4096]{1,0:T(8,128)(2,1)S(1)}, u32[]{:S(2)}, u32[]{:S(2)}) collective-permute-start(bf16[32,4096]{1,0:T(8,128)(2,1)S(1)} %collective-permute-done.11.refs_4_), channel_id=1, source_target_pairs={{2,0},{4,2},{6,4},{7,6},{5,7},{3,5},{1,3},{0,1},{10,8},{12,10},{14... | collective-permute-start | bytes 786440 | tf_op jit(solution)/shard_map/ppermute | solution.py:585
  38.0 13.4 %collective-permute-start.17 = (bf16[32,4096]{1,0:T(8,128)(2,1)S(1)}, bf16[32,4096]{1,0:T(8,128)(2,1)S(1)}, u32[]{:S(2)}, u32[]{:S(2)}) collective-permute-start(bf16[32,4096]{1,0:T(8,128)(2,1)S(1)} %collective-permute-done.16.refs_4_), channel_id=1, source_target_pairs={{2,0},{4,2},{6,4},{7,6},{5,7},{3,5},{1,3},{0,1},{10,8},{12,10},{14... | collective-permute-start | bytes 786440 | tf_op jit(solution)/shard_map/ppermute | solution.py:585
  42.0 11.2 %collective-permute-start.18 = (bf16[32,4096]{1,0:T(8,128)(2,1)S(1)}, bf16[32,4096]{1,0:T(8,128)(2,1)S(1)}, u32[]{:S(2)}, u32[]{:S(2)}) collective-permute-start(bf16[32,4096]{1,0:T(8,128)(2,1)S(1)} %collective-permute-done.3.refs_5_), channel_id=1, source_target_pairs={{0,2},{2,4},{4,6},{6,7},{7,5},{5,3},{3,1},{1,0},{8,10},{10,12},{12... | collective-permute-start | bytes 786440 | tf_op jit(solution)/shard_map/ppermute | solution.py:583
  47.6 12.0 %collective-permute-start.12 = (bf16[32,4096]{1,0:T(8,128)(2,1)S(1)}, bf16[32,4096]{1,0:T(8,128)(2,1)S(1)}, u32[]{:S(2)}, u32[]{:S(2)}) collective-permute-start(bf16[32,4096]{1,0:T(8,128)(2,1)S(1)} %collective-permute-done.10.refs_3_), channel_id=1, source_target_pairs={{0,2},{2,4},{4,6},{6,7},{7,5},{5,3},{3,1},{1,0},{8,10},{10,12},{12... | collective-permute-start | bytes 786440 | tf_op jit(solution)/shard_map/ppermute | solution.py:583
  49.4 10.2 %collective-permute-start.14 = (bf16[32,4096]{1,0:T(8,128)(2,1)S(1)}, bf16[32,4096]{1,0:T(8,128)(2,1)S(1)}, u32[]{:S(2)}, u32[]{:S(2)}) collective-permute-start(bf16[32,4096]{1,0:T(8,128)(2,1)S(1)} %collective-permute-done.13.refs_6_), channel_id=1, source_target_pairs={{2,0},{4,2},{6,4},{7,6},{5,7},{3,5},{1,3},{0,1},{10,8},{12,10},{14... | collective-permute-start | bytes 786440 | tf_op jit(solution)/shard_map/ppermute | solution.py:585
  49.6 23.4 %collective-permute-start.4 = (bf16[2,4,256,128]{3,2,1,0:T(8,128)(2,1)S(1)}, bf16[2,4,256,128]{3,2,1,0:T(8,128)(2,1)S(1)}, u32[]{:S(2)}, u32[]{:S(2)}) collective-permute-start(bf16[2,4,256,128]{3,2,1,0:T(8,128)(2,1)S(1)} %get-tuple-element.119), channel_id=1, source_target_pairs={{0,1},{1,0},{2,3},{3,2},{4,5},{5,4},{6,7},{7,6},{8,9},{9,8},{10,11... | collective-permute-start | bytes 1572872 | tf_op jit(solution)/shard_map/ppermute | solution.py:638
  51.4 24.8 %collective-permute-start.5 = (bf16[2,4,256,128]{3,2,1,0:T(8,128)(2,1)S(1)}, bf16[2,4,256,128]{3,2,1,0:T(8,128)(2,1)S(1)}, u32[]{:S(2)}, u32[]{:S(2)}) collective-permute-start(bf16[2,4,256,128]{3,2,1,0:T(8,128)(2,1)S(1)} %get-tuple-element.120), channel_id=1, source_target_pairs={{0,2},{1,3},{2,0},{3,1},{4,6},{5,7},{6,4},{7,5},{8,10},{9,11},{10,... | collective-permute-start | bytes 1572872 | tf_op jit(solution)/shard_map/ppermute | solution.py:638
  66.9 29.6 %collective-permute-start.20 = (bf16[8,128,256]{2,1,0:T(8,128)(2,1)S(1)}, bf16[8,128,256]{2,1,0:T(8,128)(2,1)S(1)}, u32[]{:S(2)}, u32[]{:S(2)}) collective-permute-start(bf16[8,128,256]{2,1,0:T(8,128)(2,1)S(1)} %get-tuple-element.142.refs_4_), channel_id=1, source_target_pairs={{0,4},{1,5},{2,6},{3,7},{4,0},{5,1},{6,2},{7,3},{8,12},{9,13},{10,... | collective-permute-start | bytes 1572872 | tf_op jit(solution)/shard_map/ppermute | solution.py:623
  69.8 26.7 %collective-permute-start.19 = (bf16[2,4,256,128]{3,2,1,0:T(8,128)(2,1)S(1)}, bf16[2,4,256,128]{3,2,1,0:T(8,128)(2,1)S(1)}, u32[]{:S(2)}, u32[]{:S(2)}) collective-permute-start(bf16[2,4,256,128]{3,2,1,0:T(8,128)(2,1)S(1)} %get-tuple-element.138), channel_id=1, source_target_pairs={{0,3},{1,2},{2,1},{3,0},{4,7},{5,6},{6,5},{7,4},{8,11},{9,10},{10,... | collective-permute-start | bytes 1572872 | tf_op jit(solution)/shard_map/ppermute | solution.py:638
  72.3 4.2 %collective-permute-start.21 = (bf16[256,128]{1,0:T(8,128)(2,1)S(1)}, bf16[256,128]{1,0:T(8,128)(2,1)S(1)}, u32[]{:S(2)}, u32[]{:S(2)}) collective-permute-start(bf16[256,128]{1,0:T(8,128)(2,1)S(1)} %get-tuple-element.139), channel_id=1, source_target_pairs={{0,0},{1,2},{2,4},{3,6},{4,1},{5,3},{6,5},{7,7},{8,8},{9,10},{10,1... | collective-permute-start | bytes 196616 | tf_op jit(solution)/shard_map/ppermute | solution.py:628
  73.0 23.4 %collective-permute-start.22 = (bf16[256,128]{1,0:T(8,128)(2,1)S(1)}, bf16[256,128]{1,0:T(8,128)(2,1)S(1)}, u32[]{:S(2)}, u32[]{:S(2)}) collective-permute-start(bf16[256,128]{1,0:T(8,128)(2,1)S(1)} %get-tuple-element.140), channel_id=1, source_target_pairs={{0,1},{1,3},{2,5},{3,7},{4,0},{5,2},{6,4},{7,6},{8,9},{9,11},{10,1... | collective-permute-start | bytes 196616 | tf_op jit(solution)/shard_map/ppermute | solution.py:628
  76.2 38.3 %collective-permute-start.23 = (bf16[2,4,256,128]{3,2,1,0:T(8,128)(2,1)S(1)}, bf16[2,4,256,128]{3,2,1,0:T(8,128)(2,1)S(1)}, u32[]{:S(2)}, u32[]{:S(2)}) collective-permute-start(bf16[2,4,256,128]{3,2,1,0:T(8,128)(2,1)S(1)} %get-tuple-element.144), channel_id=1, source_target_pairs={{0,1},{1,0},{2,3},{3,2},{4,5},{5,4},{6,7},{7,6},{8,9},{9,8},{10,11... | collective-permute-start | bytes 1572872 | tf_op jit(solution)/shard_map/ppermute | solution.py:638
  76.5 49.5 %collective-permute-start.6 = (bf16[2,4,256,128]{3,2,1,0:T(8,128)(2,1)S(1)}, bf16[2,4,256,128]{3,2,1,0:T(8,128)(2,1)S(1)}, u32[]{:S(2)}, u32[]{:S(2)}) collective-permute-start(bf16[2,4,256,128]{3,2,1,0:T(8,128)(2,1)S(1)} %get-tuple-element.121), channel_id=1, source_target_pairs={{0,2},{1,3},{2,0},{3,1},{4,6},{5,7},{6,4},{7,5},{8,10},{9,11},{10,... | collective-permute-start | bytes 1572872 | tf_op jit(solution)/shard_map/ppermute | solution.py:638
  96.3 30.6 %collective-permute-start.7 = (bf16[2,4,256,128]{3,2,1,0:T(8,128)(2,1)S(1)}, bf16[2,4,256,128]{3,2,1,0:T(8,128)(2,1)S(1)}, u32[]{:S(2)}, u32[]{:S(2)}) collective-permute-start(bf16[2,4,256,128]{3,2,1,0:T(8,128)(2,1)S(1)} %get-tuple-element.122), channel_id=1, source_target_pairs={{0,3},{1,2},{2,1},{3,0},{4,7},{5,6},{6,5},{7,4},{8,11},{9,10},{10,... | collective-permute-start | bytes 1572872 | tf_op jit(solution)/shard_map/ppermute | solution.py:638
  105.3 29.6 %collective-permute-start.25 = (bf16[4,144,256]{2,1,0:T(8,128)(2,1)S(1)}, bf16[4,144,256]{2,1,0:T(8,128)(2,1)S(1)}, u32[]{:S(2)}, u32[]{:S(2)}) collective-permute-start(bf16[4,144,256]{2,1,0:T(8,128)(2,1)S(1)} %attend.7), channel_id=1, source_target_pairs={{0,4},{1,5},{2,6},{3,7},{4,0},{5,1},{6,2},{7,3},{8,12},{9,13},{10,... | collective-permute-start | bytes 884744 | tf_op jit(solution)/shard_map/ppermute | solution.py:652
  114.4 20.5 %collective-permute-start.24 = (bf16[4,144,256]{2,1,0:T(8,128)(2,1)S(1)}, bf16[4,144,256]{2,1,0:T(8,128)(2,1)S(1)}, u32[]{:S(2)}, u32[]{:S(2)}) collective-permute-start(bf16[4,144,256]{2,1,0:T(8,128)(2,1)S(1)} %attend.4), channel_id=1, source_target_pairs={{0,4},{1,5},{2,6},{3,7},{4,0},{5,1},{6,2},{7,3},{8,12},{9,13},{10,... | collective-permute-start | bytes 884744 | tf_op jit(solution)/shard_map/ppermute | solution.py:652
  140.4 10.1 %collective-permute-start.26 = (bf16[32,4096]{1,0:T(8,128)(2,1)S(1)}, bf16[32,4096]{1,0:T(8,128)(2,1)S(1)}, u32[]{:S(2)}, u32[]{:S(2)}) collective-permute-start(bf16[32,4096]{1,0:T(8,128)(2,1)S(1)} %get-tuple-element.157), channel_id=1, source_target_pairs={{0,2},{2,4},{4,6},{6,7},{7,5},{5,3},{3,1},{1,0},{8,10},{10,12},{12... | collective-permute-start | bytes 786440 | tf_op jit(solution)/shard_map/ppermute | solution.py:672
  142.6 9.4 %collective-permute-start.30 = (bf16[32,4096]{1,0:T(8,128)(2,1)S(1)}, bf16[32,4096]{1,0:T(8,128)(2,1)S(1)}, u32[]{:S(2)}, u32[]{:S(2)}) collective-permute-start(bf16[32,4096]{1,0:T(8,128)(2,1)S(1)} %convert_element_type.108), channel_id=1, source_target_pairs={{2,0},{4,2},{6,4},{7,6},{5,7},{3,5},{1,3},{0,1},{10,8},{12,10},{14... | collective-permute-start | bytes 786440 | tf_op jit(solution)/shard_map/ppermute | solution.py:672
  148.4 9.3 %collective-permute-start.33 = (bf16[32,4096]{1,0:T(8,128)(2,1)S(1)}, bf16[32,4096]{1,0:T(8,128)(2,1)S(1)}, u32[]{:S(2)}, u32[]{:S(2)}) collective-permute-start(bf16[32,4096]{1,0:T(8,128)(2,1)S(1)} %convert_element_type.115), channel_id=1, source_target_pairs={{0,2},{2,4},{4,6},{6,7},{7,5},{5,3},{3,1},{1,0},{8,10},{10,12},{12... | collective-permute-start | bytes 786440 | tf_op jit(solution)/shard_map/ppermute | solution.py:672
  149.9 9.3 %collective-permute-start.36 = (bf16[32,4096]{1,0:T(8,128)(2,1)S(1)}, bf16[32,4096]{1,0:T(8,128)(2,1)S(1)}, u32[]{:S(2)}, u32[]{:S(2)}) collective-permute-start(bf16[32,4096]{1,0:T(8,128)(2,1)S(1)} %get-tuple-element.168), channel_id=1, source_target_pairs={{2,0},{4,2},{6,4},{7,6},{5,7},{3,5},{1,3},{0,1},{10,8},{12,10},{14... | collective-permute-start | bytes 786440 | tf_op jit(solution)/shard_map/ppermute | solution.py:672
  150.5 12.7 %collective-permute-start.27 = (bf16[32,4096]{1,0:T(8,128)(2,1)S(1)}, bf16[32,4096]{1,0:T(8,128)(2,1)S(1)}, u32[]{:S(2)}, u32[]{:S(2)}) collective-permute-start(bf16[32,4096]{1,0:T(8,128)(2,1)S(1)} %add_convert_fusion.11), channel_id=1, source_target_pairs={{0,2},{2,4},{4,6},{6,7},{7,5},{5,3},{3,1},{1,0},{8,10},{10,12},{12... | collective-permute-start | bytes 786440 | tf_op jit(solution)/shard_map/ppermute | solution.py:672
  152.1 12.8 %collective-permute-start.31 = (bf16[32,4096]{1,0:T(8,128)(2,1)S(1)}, bf16[32,4096]{1,0:T(8,128)(2,1)S(1)}, u32[]{:S(2)}, u32[]{:S(2)}) collective-permute-start(bf16[32,4096]{1,0:T(8,128)(2,1)S(1)} %add_convert_fusion.8), channel_id=1, source_target_pairs={{2,0},{4,2},{6,4},{7,6},{5,7},{3,5},{1,3},{0,1},{10,8},{12,10},{14... | collective-permute-start | bytes 786440 | tf_op jit(solution)/shard_map/ppermute | solution.py:672
  157.7 11.2 %collective-permute-start.34 = (bf16[32,4096]{1,0:T(8,128)(2,1)S(1)}, bf16[32,4096]{1,0:T(8,128)(2,1)S(1)}, u32[]{:S(2)}, u32[]{:S(2)}) collective-permute-start(bf16[32,4096]{1,0:T(8,128)(2,1)S(1)} %add_convert_fusion.5), channel_id=1, source_target_pairs={{0,2},{2,4},{4,6},{6,7},{7,5},{5,3},{3,1},{1,0},{8,10},{10,12},{12... | collective-permute-start | bytes 786440 | tf_op jit(solution)/shard_map/ppermute | solution.py:672
  159.3 11.2 %collective-permute-start.37 = (bf16[32,4096]{1,0:T(8,128)(2,1)S(1)}, bf16[32,4096]{1,0:T(8,128)(2,1)S(1)}, u32[]{:S(2)}, u32[]{:S(2)}) collective-permute-start(bf16[32,4096]{1,0:T(8,128)(2,1)S(1)} %add_convert_fusion.3), channel_id=1, source_target_pairs={{2,0},{4,2},{6,4},{7,6},{5,7},{3,5},{1,3},{0,1},{10,8},{12,10},{14... | collective-permute-start | bytes 786440 | tf_op jit(solution)/shard_map/ppermute | solution.py:672
  163.3 11.2 %collective-permute-start.28 = (bf16[32,4096]{1,0:T(8,128)(2,1)S(1)}, bf16[32,4096]{1,0:T(8,128)(2,1)S(1)}, u32[]{:S(2)}, u32[]{:S(2)}) collective-permute-start(bf16[32,4096]{1,0:T(8,128)(2,1)S(1)} %add_convert_fusion.10), channel_id=1, source_target_pairs={{0,2},{2,4},{4,6},{6,7},{7,5},{5,3},{3,1},{1,0},{8,10},{10,12},{12... | collective-permute-start | bytes 786440 | tf_op jit(solution)/shard_map/ppermute | solution.py:672
  164.9 14.5 %collective-permute-start.32 = (bf16[32,4096]{1,0:T(8,128)(2,1)S(1)}, bf16[32,4096]{1,0:T(8,128)(2,1)S(1)}, u32[]{:S(2)}, u32[]{:S(2)}) collective-permute-start(bf16[32,4096]{1,0:T(8,128)(2,1)S(1)} %add_convert_fusion.7), channel_id=1, source_target_pairs={{2,0},{4,2},{6,4},{7,6},{5,7},{3,5},{1,3},{0,1},{10,8},{12,10},{14... | collective-permute-start | bytes 786440 | tf_op jit(solution)/shard_map/ppermute | solution.py:672
  169.0 12.3 %collective-permute-start.35 = (bf16[32,4096]{1,0:T(8,128)(2,1)S(1)}, bf16[32,4096]{1,0:T(8,128)(2,1)S(1)}, u32[]{:S(2)}, u32[]{:S(2)}) collective-permute-start(bf16[32,4096]{1,0:T(8,128)(2,1)S(1)} %add_convert_fusion.4), channel_id=1, source_target_pairs={{0,2},{2,4},{4,6},{6,7},{7,5},{5,3},{3,1},{1,0},{8,10},{10,12},{12... | collective-permute-start | bytes 786440 | tf_op jit(solution)/shard_map/ppermute | solution.py:672
  170.5 8.2 %collective-permute-start.38 = (bf16[32,4096]{1,0:T(8,128)(2,1)S(1)}, bf16[32,4096]{1,0:T(8,128)(2,1)S(1)}, u32[]{:S(2)}, u32[]{:S(2)}) collective-permute-start(bf16[32,4096]{1,0:T(8,128)(2,1)S(1)} %add_convert_fusion.2), channel_id=1, source_target_pairs={{2,0},{4,2},{6,4},{7,6},{5,7},{3,5},{1,3},{0,1},{10,8},{12,10},{14... | collective-permute-start | bytes 786440 | tf_op jit(solution)/shard_map/ppermute | solution.py:672
  174.6 6.6 %collective-permute-start.29 = (bf16[32,4096]{1,0:T(8,128)(2,1)S(1)}, bf16[32,4096]{1,0:T(8,128)(2,1)S(1)}, u32[]{:S(2)}, u32[]{:S(2)}) collective-permute-start(bf16[32,4096]{1,0:T(8,128)(2,1)S(1)} %add_convert_fusion.9), channel_id=1, source_target_pairs={{0,2},{2,4},{4,6},{6,7},{7,5},{5,3},{3,1},{1,0},{8,10},{10,12},{12... | collective-permute-start | bytes 786440 | tf_op jit(solution)/shard_map/ppermute | solution.py:672
  178.8 6.4 %collective-permute-start.39 = (bf16[32,4096]{1,0:T(8,128)(2,1)S(1)}, bf16[32,4096]{1,0:T(8,128)(2,1)S(1)}, u32[]{:S(2)}, u32[]{:S(2)}) collective-permute-start(bf16[32,4096]{1,0:T(8,128)(2,1)S(1)} %add_convert_fusion.1), channel_id=1, source_target_pairs={{2,0},{4,2},{6,4},{7,6},{5,7},{3,5},{1,3},{0,1},{10,8},{12,10},{14... | collective-permute-start | bytes 786440 | tf_op jit(solution)/shard_map/ppermute | solution.py:672
